TPU v7x, 32 devices: a whole 2x2x4 slice. The times are simulated.
32 devices in a mesh: groups: 2 (over y), tensor: 4 (over z), seq: 2 (over x), sub: 2 (over core).
Axes of the slice: x: 2, y: 2, z: 4, core: 2. Of those that a mesh axis runs over, the one named last changes fastest.
Arguments:
- hidden: bfloat16 [512, 53248], P(('groups', 'seq'), ('tensor', 'sub')), parts along dimension 0, may hold values from -6 to 6
- down_weight: bfloat16 [53248, 8192], P(('tensor', 'sub'), 'seq'), may hold values from -0.02734375 to 0.02734375
- sign_bits: int32 [8192], P('seq'), may hold values from 0 to 1
Outputs:
- sum_codes: bfloat16 [512, 8192], P(('groups', 'sub'), 'seq'), parts along dimension 0
- sum_scales: bfloat16 [512, 64], P(('groups', 'sub'), 'seq'), parts along dimension 0
There are 2 independent parts, one for each index of `groups`. A program takes and returns all parts, laid end to end along the dimension named above; an argument that names none is the same for every part. Nothing has to cross between parts.
All inputs are finite; a program needn't handle non-finite values. Where the computation divides by a largest or mean magnitude, that divisor is 1e-20 or more.
Results may differ from a plain program's by a relative error of at most 0.014.
Values may be sent and summed in bfloat16 or wider, within the bound.
No kernel may reach another device: no remote copies, remote signals or barrier semaphores. Data moves between devices by JAX's collectives and lax.ppermute only.
A program may use at most 192 MiB of HBM per device.

v0:
```python
import math

import jax
import jax.numpy as jnp
from jax import lax
from jax.sharding import PartitionSpec as P

BLOCK = 128


epsilon = 1e-06


def hadamard(order):
    indices = jnp.arange(order, dtype=jnp.int32)
    parity = jnp.zeros((order, order), jnp.int32)
    for position in range(order.bit_length() - 1):
        parity = parity + (indices[:, None] >> position & 1) * (indices[None, :] >> position & 1)
    return (1 - 2 * (parity % 2)).astype(jnp.float32) / math.sqrt(order)


def rotate_blocks(values, flips):
    blocks = (values * flips[None, :]).reshape(values.shape[0], -1, BLOCK)
    rotated = jnp.einsum("tnb,bc->tnc", blocks, hadamard(BLOCK), precision=lax.Precision.HIGHEST)
    return rotated.reshape(values.shape)


def encode_blocks(values):
    blocks = values.reshape(values.shape[:-1] + (-1, BLOCK))
    scales = (jnp.max(jnp.abs(blocks), axis=-1) + epsilon).astype(jnp.bfloat16)
    encoded = (blocks / scales.astype(jnp.float32)[..., None]).astype(jnp.bfloat16)
    return (encoded.reshape(values.shape), scales)


def decode_blocks(encoded, scales):
    blocks = encoded.astype(jnp.float32).reshape(encoded.shape[:-1] + (-1, BLOCK))
    return (blocks * scales.astype(jnp.float32)[..., None]).reshape(encoded.shape)


def shards(hidden, down_weight, sign_bits):
    tensor_count = lax.axis_size("tensor")
    sub_count = lax.axis_size("sub")
    sources = tensor_count * sub_count
    gathered = lax.all_gather(hidden, "seq", axis=0, tiled=True)
    token_count = gathered.shape[0]
    block_rows = token_count // sources
    ordered = (
        gathered.reshape(sub_count, tensor_count, block_rows, -1)
        .transpose(1, 0, 2, 3)
        .reshape(token_count, -1)
    )
    partial_value = jnp.dot(ordered, down_weight, preferred_element_type=jnp.float32)
    flips = (2 * sign_bits - 1).astype(jnp.float32)
    encoded, scales = encode_blocks(rotate_blocks(partial_value, flips))
    recv_codes, recv_scales = (
        lax.all_to_all(
            encoded.reshape(sources, block_rows, -1),
            ("tensor", "sub"),
            split_axis=0,
            concat_axis=0,
            tiled=True,
        ),
        lax.all_to_all(
            scales.reshape(sources, block_rows, -1),
            ("tensor", "sub"),
            split_axis=0,
            concat_axis=0,
            tiled=True,
        ),
    )
    summed = jnp.sum(decode_blocks(recv_codes, recv_scales), axis=0)
    sum_codes, sum_scales = encode_blocks(summed)
    full_codes, full_scales = (
        lax.all_gather(sum_codes, "tensor", axis=0, tiled=True),
        lax.all_gather(sum_scales, "tensor", axis=0, tiled=True),
    )
    return (full_codes, full_scales)


def solution(mesh):
    return jax.shard_map(
        shards,
        mesh=mesh,
        in_specs=(P(("groups", "seq"), ("tensor", "sub")), P(("tensor", "sub"), "seq"), P("seq")),
        out_specs=(P(("groups", "sub"), "seq"), P(("groups", "sub"), "seq")),
        check_vma=False,
    )
```

profile of v0, /device:TPU:0, one launch (start us, length us, event | category | flops | bytes accessed | tf_op | source)
XLA Modules:
  0.0 201.8 jit_solution(13769460751998523420)
XLA Ops:
  7.2 0.0 all-gather.3.cloned.1.call-start
  7.2 0.7 all-gather.3.cloned.1.call-update
  7.9 0.7 add_convert_fusion.2
  8.7 51.5 %all-gather.3.cloned.1.call-done = bf16[256,6656]{1,0:T(8,128)(2,1)} async-done(((bf16[128,6656]{1,0:T(8,128)(2,1)}), bf16[256,6656]{1,0:T(8,128)(2,1)}) %all-gather.3.cloned.1.call-update) | async-done | bytes 3407888 | tf_op jit(solution)/shard_map/all_gather | solution.py:44
  60.2 3.9 %copy.21 = bf16[4,2,32,6656]{3,2,1,0:T(8,128)(2,1)} copy(bf16[4,2,32,6656]{3,2,0,1:T(8,128)(2,1)} %bitcast.34) | data formatting | bytes 6815744 | tf_op jit(solution)/shard_map/transpose | solution.py:49
  64.1 22.3 %fusion.3 = f32[32,32,8,128]{3,2,1,0:T(8,128)S(1)} fusion(bf16[256,6656]{1,0:T(8,128)(2,1)} %bitcast.35, bf16[6656,4096]{1,0:T(8,128)(2,1)} %param.4, f32[4096]{0:T(1024)S(1)} %add_convert_fusion.2), kind=kOutput, calls=%fused_computation.7 | convolution fusion | flops 13959692288 | bytes 62144512 | tf_op jit(solution)/shard_map/dot_general | solution.py:52
  86.4 6.0 %abs_reduce_fusion = (f32[256,32]{0,1:T(8,128)S(1)}, f32[256,32,128]{0,2,1:T(8,128)}) fusion(s32[128]{0:T(128)S(1)} %get-tuple-element.10, s32[128]{0:T(128)S(1)} %get-tuple-element.11, s32[128]{0:T(128)S(1)} %get-tuple-element.12, s32[128]{0:T(128)S(1)} %get-tuple-element.13, s32[128]{0:T(128)S(1)} %get-tuple-element.14, s32[128]{0:T(128)S(1)} %get-tuple-element.15, ...), kind=kOutput, calls=%fused_computation.6 | convolution fusion | flops 1613160448 | bytes 8424960 | tf_op jit(solution)/shard_map/tnb,bc->tnc/dot_general | solution.py:24
  92.4 0.1 convert_element_type.57
  92.5 0.7 reshape.139
  93.2 4.6 %all-to-all-start.1 = ((bf16[8,2,512]{2,1,0:T(2,128)(2,1)}), bf16[8,2,512]{2,1,0:T(2,128)(2,1)S(1)}, u32[]{:S(2)}, u32[]{:S(2)}) async-start(bf16[8,2,512]{2,1,0:T(2,128)(2,1)} %reshape.139), calls=%async_computation.1 | async-start | bytes 32768 | tf_op jit(solution)/shard_map/all_to_all | solution.py:63
  97.8 2.7 %divide_convert_fusion = bf16[256,32,128]{0,2,1:T(8,128)(2,1)S(1)} fusion(f32[256,32,128]{0,2,1:T(8,128)} %get-tuple-element.9, f32[256,32]{0,1:T(8,128)S(1)} %get-tuple-element.6), kind=kLoop, calls=%fused_computation.5 | loop fusion | flops 2097152 | bytes 6324224 | tf_op jit(solution)/shard_map/convert_element_type | solution.py:31
  100.6 3.1 %copy.23 = bf16[256,32,128]{2,1,0:T(8,128)(2,1)} copy(bf16[256,32,128]{0,2,1:T(8,128)(2,1)S(1)} %divide_convert_fusion) | data formatting | bytes 4194304 | tf_op jit(solution)/shard_map/convert_element_type | solution.py:31
  103.7 4.2 %reshape_reshape.3 = bf16[8,32,4096]{2,1,0:T(8,128)(2,1)} reshape(bf16[256,32,128]{2,1,0:T(8,128)(2,1)} %copy.23) | data formatting | bytes 4194304 | tf_op jit(solution)/shard_map/reshape;reshape | solution.py:57
  107.9 0.0 all-to-all-done.1
  107.9 5.1 %all-to-all-start = ((bf16[8,32,4096]{2,1,0:T(8,128)(2,1)}), bf16[8,32,4096]{2,1,0:T(8,128)(2,1)S(1)}, u32[]{:S(2)}, u32[]{:S(2)}) async-start(bf16[8,32,4096]{2,1,0:T(8,128)(2,1)} %reshape_reshape.3), calls=%async_computation | async-start | bytes 4194304 | tf_op jit(solution)/shard_map/all_to_all | solution.py:56
  113.0 0.0 all-gather.5.cloned.1.call-start
  113.0 0.1 reshape.140
  113.1 0.1 copy.25
  113.2 2.6 %mul.146 = f32[8,32,32,128]{3,2,1,0:T(8,128)} broadcast(f32[8,32,32]{2,1,0:T(8,128)S(1)} %copy.25), dimensions={0,1,2} | broadcast | bytes 4227072 | tf_op jit(solution)/shard_map/mul | solution.py:37
  115.8 4.9 %mul.147 = f32[8,32,4096]{2,1,0:T(8,128)} reshape(f32[8,32,32,128]{3,2,1,0:T(8,128)} %mul.146) | data formatting | bytes 8388608 | tf_op jit(solution)/shard_map/mul | solution.py:37
  120.7 41.3 %all-to-all-done = bf16[8,32,4096]{2,1,0:T(8,128)(2,1)S(1)} async-done(((bf16[8,32,4096]{2,1,0:T(8,128)(2,1)}), bf16[8,32,4096]{2,1,0:T(8,128)(2,1)S(1)}, u32[]{:S(2)}, u32[]{:S(2)}) %all-to-all-start) | async-done | bytes 2097184 | tf_op jit(solution)/shard_map/all_to_all | solution.py:56
  162.0 2.8 %multiply_reduce_fusion = f32[32,4096]{1,0:T(8,128)S(1)} fusion(f32[8,32,4096]{2,1,0:T(8,128)} %mul.147, bf16[8,32,4096]{2,1,0:T(8,128)(2,1)S(1)} %all-to-all-done), kind=kLoop, calls=%fused_computation.4 | loop fusion | flops 3014656 | bytes 6815744 | tf_op jit(solution)/shard_map/reduce_sum | solution.py:71
  164.8 0.1 copy.28
  164.9 0.2 reduce_max.19
  165.2 0.2 div.29
  165.4 1.0 fusion.4
  166.4 0.0 all-gather.5.cloned.1.call-update
  166.4 13.2 %all_gather.11 = bf16[128,32]{1,0:T(8,128)(2,1)S(1)} all-gather(bf16[32,32]{1,0:T(8,128)(2,1)S(1)} %add_convert_fusion.1), channel_id=1, replica_groups=mesh['groups'=2,'tensor'=4,'seq'=2,'sub'=2] {'tensor'}, dimensions={0}, use_global_device_ids=true | all-gather | bytes 10240 | tf_op jit(solution)/shard_map/all_gather | solution.py:75
  179.7 0.7 copy.26
  180.3 12.3 %all-gather.5.cloned.1.call-done = bf16[128,4096]{1,0:T(8,128)(2,1)} async-done(((bf16[32,4096]{1,0:T(8,128)(2,1)}), bf16[128,4096]{1,0:T(8,128)(2,1)}) %all-gather.5.cloned.1.call-update) | async-done | bytes 1048592 | tf_op jit(solution)/shard_map/all_gather | solution.py:74
  192.6 2.3 %copy.40 = bf16[128,4096]{1,0:T(8,128)(2,1)} copy(bf16[128,4096]{1,0:T(8,128)(2,1)} %all-gather.5.cloned.1.call-done) | data formatting | bytes 2097152
  (8 shorter events, 0.1 us)
Async XLA Ops:
  7.2 53.0 %all-gather.3.cloned.1.call-start = ((), (), s32[]{:S(2)}) async-start(), calls=%async_computation.2 | async-start | bytes 5111808 | tf_op jit(solution)/shard_map/all_gather | solution.py:44
  93.2 14.6 %all-to-all-start.1 = ((bf16[8,2,512]{2,1,0:T(2,128)(2,1)}), bf16[8,2,512]{2,1,0:T(2,128)(2,1)S(1)}, u32[]{:S(2)}, u32[]{:S(2)}) async-start(bf16[8,2,512]{2,1,0:T(2,128)(2,1)} %reshape.139), calls=%async_computation.1 | async-start | bytes 32768 | tf_op jit(solution)/shard_map/all_to_all | solution.py:63
  107.9 54.2 %all-to-all-start = ((bf16[8,32,4096]{2,1,0:T(8,128)(2,1)}), bf16[8,32,4096]{2,1,0:T(8,128)(2,1)S(1)}, u32[]{:S(2)}, u32[]{:S(2)}) async-start(bf16[8,32,4096]{2,1,0:T(8,128)(2,1)} %reshape_reshape.3), calls=%async_computation | async-start | bytes 4194304 | tf_op jit(solution)/shard_map/all_to_all | solution.py:56
  113.0 79.7 %all-gather.5.cloned.1.call-start = ((), (), s32[]{:S(2)}) async-start(), calls=%async_computation.3 | async-start | bytes 1310720 | tf_op jit(solution)/shard_map/all_gather | solution.py:74
Sparse Core Ops, SparseCore 0:
  9.5 50.5 all-gather.2
  166.6 26.0 all-gather.4
where the time goes:
time: 202 us
  waiting for transfers between devices  106 us (52%)
  matrix products  28.3 us (14%)
  local copies, waits for them, and re-layouts  23.1 us (11%)
  between operations  14.1 us (7%)
  blocking collectives  13.2 us (7%)
  starting transfers between devices  9.78 us (5%)
  other arithmetic  7.51 us (4%)
    all_gather x1, waiting for transfers between devices, shards(): gathered = lax.all_gather(hidden, 'seq', axis=0, tiled=True)  51.5 us
    all_to_all x1, waiting for transfers between devices, shards(): lax.all_to_all(encoded.reshape(sources, block_rows, -1), ('tensor', 'sub'...  41.3 us
    dot_general x1, matrix products, shards(): jnp.dot(ordered, down_weight, preferred_element_type=jnp.float32)  22.3 us
    all_gather x1, blocking collectives, shards(): lax.all_gather(sum_scales, 'tensor', axis=0, tiled=True)  13.2 us
    all_gather x1, waiting for transfers between devices, shards(): lax.all_gather(sum_codes, 'tensor', axis=0, tiled=True)  12.3 us
    mul x2, local copies, waits for them, and re-layouts, decode_blocks(): blocks * scales.astype(jnp.float32)[..., None]  7.54 us
    dot_general x1, matrix products, rotate_blocks(): jnp.einsum('tnb,bc->tnc', blocks, hadamard(BLOCK), precision=lax.Precisio...  5.95 us
    all_to_all x1, starting transfers between devices, shards(): lax.all_to_all(encoded.reshape(sources, block_rows, -1), ('tensor', 'sub'...  5.1 us
  transfers between devices with their start and end apart: 4, of which 3 were waited for; matrix products, arithmetic and copies ran while one was open for 9% of the time, Pallas kernels for 0%

commit v1 on v0

v1 whole, which is shorter than its diff:
```python
import math

import jax
import jax.numpy as jnp
from jax import lax
from jax.sharding import PartitionSpec as P

BLOCK = 128
AXES = ("tensor", "seq", "sub")
epsilon = 1e-06


def hadamard(order):
    indices = jnp.arange(order, dtype=jnp.int32)
    parity = jnp.zeros((order, order), jnp.int32)
    for position in range(order.bit_length() - 1):
        parity = parity + (indices[:, None] >> position & 1) * (indices[None, :] >> position & 1)
    return (1 - 2 * (parity % 2)).astype(jnp.float32) / math.sqrt(order)


def rotate_blocks(values, flips):
    blocks = (values * flips[None, :]).reshape(values.shape[0], -1, BLOCK)
    rotated = jnp.einsum("tnb,bc->tnc", blocks, hadamard(BLOCK), precision=lax.Precision.HIGHEST)
    return rotated.reshape(values.shape)


def encode_blocks(values):
    blocks = values.reshape(values.shape[:-1] + (-1, BLOCK))
    scales = (jnp.max(jnp.abs(blocks), axis=-1) + epsilon).astype(jnp.bfloat16)
    encoded = (blocks / scales.astype(jnp.float32)[..., None]).astype(jnp.bfloat16)
    return (encoded.reshape(values.shape), scales)


def shards(hidden, down_weight, sign_bits):
    tensor_count = lax.axis_size("tensor")
    seq_count = lax.axis_size("seq")
    sub_count = lax.axis_size("sub")
    tensor_at = lax.axis_index("tensor")
    seq_at = lax.axis_index("seq")
    sub_at = lax.axis_index("sub")
    rows, depth = hidden.shape
    per_sub = seq_count // sub_count
    piece = rows // tensor_count
    chunks = 4
    width = depth // chunks
    flips = (2 * sign_bits - 1).astype(jnp.float32)

    def linear(tensor, seq, sub):
        return (tensor * seq_count + seq) * sub_count + sub

    def owner(seq, shift):
        return (seq - shift) % seq_count // per_sub

    def chip_sum(partial_value, shift):
        total = partial_value
        for step in range(1, sub_count):
            pairs = [
                (linear(t, s, (owner(s, shift) + step) % sub_count), linear(t, s, owner(s, shift)))
                for t in range(tensor_count)
                for s in range(seq_count)
            ]
            total = total + lax.ppermute(partial_value.astype(jnp.bfloat16), AXES, pairs).astype(jnp.float32)
        return total

    def along_tensor(values, step, shift):
        pairs = [
            (linear(t, s, owner(s, shift)), linear((t + step) % tensor_count, s, owner(s, shift)))
            for t in range(tensor_count)
            for s in range(seq_count)
        ]
        return lax.ppermute(values, AXES, pairs)

    def finish(partial_value, shift):
        total = chip_sum(partial_value, shift)
        summed = lax.dynamic_slice_in_dim(total, tensor_at * piece, piece, 0)
        narrow = total.astype(jnp.bfloat16)
        for step in range(1, tensor_count):
            target = (tensor_at + step) % tensor_count
            sent = lax.dynamic_slice_in_dim(narrow, target * piece, piece, 0)
            summed = summed + along_tensor(sent, step, shift).astype(jnp.float32)
        codes, scales = encode_blocks(rotate_blocks(summed, flips))
        full_codes = jnp.zeros((rows, codes.shape[1]), jnp.bfloat16)
        full_scales = jnp.zeros((rows, scales.shape[1]), jnp.bfloat16)
        for step in range(tensor_count):
            at = (tensor_at - step) % tensor_count * piece
            held = (codes, scales)
            if step:
                held = (along_tensor(codes, step, shift), along_tensor(scales, step, shift))
            full_codes = lax.dynamic_update_slice_in_dim(full_codes, held[0], at, 0)
            full_scales = lax.dynamic_update_slice_in_dim(full_scales, held[1], at, 0)
        return full_codes, full_scales

    def from_seq(values, shift):
        return lax.ppermute(values, "seq", [(s, (s + shift) % seq_count) for s in range(seq_count)])

    results = []
    for shift in range(seq_count):
        if shift == 0:
            partial_value = jnp.dot(hidden, down_weight, preferred_element_type=jnp.float32)
        else:
            partial_value = jnp.zeros((rows, down_weight.shape[1]), jnp.float32)
            for chunk in range(chunks):
                part = slice(chunk * width, (chunk + 1) * width)
                arrived = from_seq(hidden[:, part], shift)
                partial_value = partial_value + jnp.dot(
                    arrived, down_weight[part], preferred_element_type=jnp.float32
                )
        results.append(finish(partial_value, shift))

    out = []
    for at in range(2):
        stacked = jnp.stack([result[at] for result in results])
        held = []
        for place in range(per_sub):
            shift = (seq_at - (sub_at * per_sub + place)) % seq_count
            held.append(lax.dynamic_index_in_dim(stacked, shift, 0, keepdims=False))
        out.append(jnp.concatenate(held))
    return tuple(out)


def solution(mesh):
    return jax.shard_map(
        shards,
        mesh=mesh,
        in_specs=(P(("groups", "seq"), ("tensor", "sub")), P(("tensor", "sub"), "seq"), P("seq")),
        out_specs=(P(("groups", "sub"), "seq"), P(("groups", "sub"), "seq")),
        check_vma=False,
    )
```

time: 202 us -> 135 us (0.67)
  waiting for transfers between devices: 106 us -> 17.7 us
  starting transfers between devices: 9.78 us -> 53.8 us
  matrix products: 28.3 us -> 45.4 us
  local copies, waits for them, and re-layouts: 23.1 us -> 8 us
  blocking collectives: 13.2 us -> 0 us
  between operations: 14.1 us -> 1.23 us
    all_gather x2 -> x0, waiting for transfers between devices: 63.8 us -> none  [the longest x1 51.5 us: shards(): gathered = lax.all_gather(hidden, 'seq', axis=0, tiled=True)]
    ppermute x0 -> x24, starting transfers between devices: none -> 53.8 us  [the longest x18 43.5 us: along_tensor(): return lax.ppermute(values, AXES, pairs)]
    all_to_all x2 -> x0, waiting for transfers between devices: 41.3 us -> none  [the longest x1 41.3 us: shards(): lax.all_to_all(encoded.reshape(sources, block_rows, -1), ('tensor', 'sub'...]
    dot_general x1 -> x5, matrix products: 22.3 us -> 43.7 us  [the longest x4 24.9 us: shards(): jnp.dot(arrived, down_weight[part], preferred_element_type=jnp.float32)]
    ppermute x0 -> x24, waiting for transfers between devices: none -> 17.7 us  [the longest x18 17.7 us: along_tensor(): return lax.ppermute(values, AXES, pairs)]
    all_gather x1 -> x0, blocking collectives: 13.2 us -> none  [shards(): lax.all_gather(sum_scales, 'tensor', axis=0, tiled=True)]
    all_to_all x2 -> x0, starting transfers between devices: 9.7 us -> none  [the longest x1 5.1 us: shards(): lax.all_to_all(encoded.reshape(sources, block_rows, -1), ('tensor', 'sub'...]
    mul x2 -> x0, local copies, waits for them, and re-layouts: 7.54 us -> none  [decode_blocks(): blocks * scales.astype(jnp.float32)[..., None]]
  transfers between devices with their start and end apart: 4 -> 24, of which waited for: 3 -> 4; matrix products, arithmetic and copies ran while one was open for 9% -> 40% of each run, Pallas kernels for 0% -> 0%
where the time goes in v1:
time: 135 us; the launch traced here: 133 us
  starting transfers between devices  53.8 us (40%)
  matrix products  45.4 us (34%)
  waiting for transfers between devices  17.7 us (13%)
  local copies, waits for them, and re-layouts  8 us (6%)
  other arithmetic  7.35 us (5%)
    ppermute x18, starting transfers between devices, along_tensor(): return lax.ppermute(values, AXES, pairs)  43.5 us
    dot_general x4, matrix products, shards(): jnp.dot(arrived, down_weight[part], preferred_element_type=jnp.float32)  24.9 us
    dot_general x1, matrix products, shards(): jnp.dot(hidden, down_weight, preferred_element_type=jnp.float32)  18.9 us
    ppermute x18, waiting for transfers between devices, along_tensor(): return lax.ppermute(values, AXES, pairs)  17.7 us
    ppermute x2, starting transfers between devices, chip_sum(): lax.ppermute(partial_value.astype(jnp.bfloat16), AXES, pairs)  5.36 us
    ppermute x4, starting transfers between devices, from_seq(): lax.ppermute(values, 'seq', [(s, (s + shift) % seq_count) for s in range(...  5.01 us
    convert_element_type x2, other arithmetic, finish(): narrow = total.astype(jnp.bfloat16)  3.15 us
    slice x1, local copies, waits for them, and re-layouts, shards(): arrived = from_seq(hidden[:, part], shift)  2.75 us
  transfers between devices with their start and end apart: 24, of which 4 were waited for; matrix products, arithmetic and copies ran while one was open for 40% of the time, Pallas kernels for 0%

profile of v1, /device:TPU:0, one launch (start us, length us, event | category | flops | bytes accessed | tf_op | source)
XLA Modules:
  0.0 133.5 jit_solution(3194951619062457990)
XLA Ops:
  0.6 2.8 %fusion.73 = (bf16[128,1664]{1,0:T(8,128)(2,1)}, bf16[128,1664]{1,0:T(8,128)(2,1)}, bf16[128,1664]{1,0:T(8,128)(2,1)}, bf16[128,1664]{1,0:T(8,128)(2,1)}) fusion(bf16[128,6656]{1,0:T(8,128)(2,1)} %param.3), kind=kLoop, calls=%fused_computation.106 | loop fusion | bytes 3407872 | tf_op jit(solution)/shard_map/slice | solution.py:104
  3.4 2.9 %collective-permute-start.10 = (bf16[128,1664]{1,0:T(8,128)(2,1)}, bf16[128,1664]{1,0:T(8,128)(2,1)}, u32[]{:S(2)}, u32[]{:S(2)}) collective-permute-start(bf16[128,1664]{1,0:T(8,128)(2,1)} %get-tuple-element.12), channel_id=1, source_target_pairs={{0,2},{2,0},{1,3},{3,1},{4,6},{6,4},{5,7},{7,5},{8,10},{10,8},{9,1... | collective-permute-start | bytes 1277960 | tf_op jit(solution)/shard_map/ppermute | solution.py:94
  6.4 2.0 %collective-permute-start.8 = (bf16[128,1664]{1,0:T(8,128)(2,1)}, bf16[128,1664]{1,0:T(8,128)(2,1)}, u32[]{:S(2)}, u32[]{:S(2)}) collective-permute-start(bf16[128,1664]{1,0:T(8,128)(2,1)} %get-tuple-element.11), channel_id=1, source_target_pairs={{0,2},{2,0},{1,3},{3,1},{4,6},{6,4},{5,7},{7,5},{8,10},{10,8},{9,1... | collective-permute-start | bytes 1277960 | tf_op jit(solution)/shard_map/ppermute | solution.py:94
  8.4 18.9 %fusion.75 = (bf16[128,4096]{1,0:T(8,128)(2,1)S(1)}, f32[128,4096]{1,0:T(8,128)S(1)}) fusion(bf16[128,6656]{1,0:T(8,128)(2,1)S(1)} %copy-done, bf16[6656,4096]{1,0:T(8,128)(2,1)} %param.4), kind=kOutput, calls=%fused_computation.108 | convolution fusion | flops 6979846144 | bytes 59375616 | tf_op jit(solution)/shard_map/dot_general | solution.py:99
  27.3 1.3 collective-permute-start
  28.7 6.2 %fusion = f32[128,4096]{1,0:T(8,128)S(1)} fusion(bf16[128,1664]{1,0:T(8,128)(2,1)} %collective-permute-done.10, bf16[6656,4096]{1,0:T(8,128)(2,1)} %param.4), kind=kOutput, calls=%fused_computation | convolution fusion | flops 1744830464 | bytes 16154624 | tf_op jit(solution)/shard_map/dot_general | solution.py:105
  34.9 6.2 %fusion.2 = f32[128,4096]{1,0:T(8,128)S(1)} fusion(bf16[128,1664]{1,0:T(8,128)(2,1)} %collective-permute-done.9, bf16[6656,4096]{1,0:T(8,128)(2,1)} %param.4), kind=kOutput, calls=%fused_computation.2 | convolution fusion | flops 1744830464 | bytes 16154624 | tf_op jit(solution)/shard_map/dot_general | solution.py:105
  41.0 6.2 %fusion.4 = f32[128,4096]{1,0:T(8,128)S(1)} fusion(bf16[128,1664]{1,0:T(8,128)(2,1)} %collective-permute-done.8, bf16[6656,4096]{1,0:T(8,128)(2,1)} %param.4), kind=kOutput, calls=%fused_computation.4 | convolution fusion | flops 1744830464 | bytes 16154624 | tf_op jit(solution)/shard_map/dot_general | solution.py:105
  47.2 6.4 %fusion.74 = (bf16[128,4096]{1,0:T(8,128)(2,1)S(1)}, f32[128,4096]{1,0:T(8,128)S(1)}) fusion(f32[128,4096]{1,0:T(8,128)S(1)} %fusion, f32[128,4096]{1,0:T(8,128)S(1)} %fusion.2, f32[128,4096]{1,0:T(8,128)S(1)} %fusion.4, bf16[128,1664]{1,0:T(8,128)(2,1)} %collective-permute-done.7, bf16[6656,4096]{1,0:T(8,128)(2,1)} %param.4), kind=kOutput, calls=%fused_computation.107 | convolution fusion | flops 1746927616 | bytes 23494656 | tf_op jit(solution)/shard_map/dot_general | solution.py:105
  53.6 4.1 %collective-permute-start.11 = (bf16[128,4096]{1,0:T(8,128)(2,1)S(1)}, bf16[128,4096]{1,0:T(8,128)(2,1)S(1)}, u32[]{:S(2)}, u32[]{:S(2)}) collective-permute-start(bf16[128,4096]{1,0:T(8,128)(2,1)S(1)} %get-tuple-element.22), channel_id=1, source_target_pairs={{0,1},{3,2},{4,5},{7,6},{8,9},{11,10},{12,13},{15,14},{16,17},{19,... | collective-permute-start | bytes 3145736 | tf_op jit(solution)/shard_map/ppermute | solution.py:62
  57.7 2.8 %fusion.72 = (bf16[128,4096]{1,0:T(8,128)(2,1)S(1)}, f32[128,4096]{1,0:T(8,128)}) fusion(f32[128,4096]{1,0:T(8,128)S(1)} %get-tuple-element.25, bf16[128,4096]{1,0:T(8,128)(2,1)} %collective-permute-done), kind=kLoop, calls=%fused_computation.105 | loop fusion | flops 1572864 | bytes 6291456 | tf_op jit(solution)/shard_map/convert_element_type | solution.py:76
  60.6 4.0 %collective-permute-start.1 = (bf16[32,4096]{1,0:T(8,128)(2,1)S(1)}, bf16[32,4096]{1,0:T(8,128)(2,1)S(1)}, u32[]{:S(2)}, u32[]{:S(2)}) collective-permute-start(bf16[32,4096]{1,0:T(8,128)(2,1)S(1)} %get-tuple-element.17), channel_id=1, source_target_pairs={{0,4},{3,7},{4,8},{7,11},{8,12},{11,15},{12,0},{15,3},{16,20},{19,... | collective-permute-start | bytes 786440 | tf_op jit(solution)/shard_map/ppermute | solution.py:71
  64.6 4.5 %collective-permute-start.2 = (bf16[32,4096]{1,0:T(8,128)(2,1)S(1)}, bf16[32,4096]{1,0:T(8,128)(2,1)}, u32[]{:S(2)}, u32[]{:S(2)}) collective-permute-start(bf16[32,4096]{1,0:T(8,128)(2,1)S(1)} %get-tuple-element.19), channel_id=1, source_target_pairs={{0,8},{3,11},{4,12},{7,15},{8,0},{11,3},{12,4},{15,7},{16,24},{19,... | collective-permute-start | bytes 786440 | tf_op jit(solution)/shard_map/ppermute | solution.py:71
  69.1 3.3 %collective-permute-start.3 = (bf16[32,4096]{1,0:T(8,128)(2,1)S(1)}, bf16[32,4096]{1,0:T(8,128)(2,1)}, u32[]{:S(2)}, u32[]{:S(2)}) collective-permute-start(bf16[32,4096]{1,0:T(8,128)(2,1)S(1)} %get-tuple-element.18), channel_id=1, source_target_pairs={{0,12},{3,15},{4,0},{7,3},{8,4},{11,7},{12,8},{15,11},{16,28},{19,... | collective-permute-start | bytes 786440 | tf_op jit(solution)/shard_map/ppermute | solution.py:71
  72.4 0.3 fusion.70
  72.8 1.4 %collective-permute-start.12 = (bf16[32,4096]{1,0:T(8,128)(2,1)S(1)}, bf16[32,4096]{1,0:T(8,128)(2,1)}, u32[]{:S(2)}, u32[]{:S(2)}) collective-permute-start(bf16[32,4096]{1,0:T(8,128)(2,1)S(1)} %get-tuple-element.14), channel_id=1, source_target_pairs={{1,5},{2,6},{5,9},{6,10},{9,13},{10,14},{13,1},{14,2},{17,21},{18,... | collective-permute-start | bytes 786440 | tf_op jit(solution)/shard_map/ppermute | solution.py:71
  74.1 1.4 %collective-permute-start.13 = (bf16[32,4096]{1,0:T(8,128)(2,1)S(1)}, bf16[32,4096]{1,0:T(8,128)(2,1)}, u32[]{:S(2)}, u32[]{:S(2)}) collective-permute-start(bf16[32,4096]{1,0:T(8,128)(2,1)S(1)} %get-tuple-element.16), channel_id=1, source_target_pairs={{1,9},{2,10},{5,13},{6,14},{9,1},{10,2},{13,5},{14,6},{17,25},{18,... | collective-permute-start | bytes 786440 | tf_op jit(solution)/shard_map/ppermute | solution.py:71
  75.5 1.4 %collective-permute-start.14 = (bf16[32,4096]{1,0:T(8,128)(2,1)S(1)}, bf16[32,4096]{1,0:T(8,128)(2,1)}, u32[]{:S(2)}, u32[]{:S(2)}) collective-permute-start(bf16[32,4096]{1,0:T(8,128)(2,1)S(1)} %get-tuple-element.15), channel_id=1, source_target_pairs={{1,13},{2,14},{5,1},{6,2},{9,5},{10,6},{13,9},{14,10},{17,29},{18,... | collective-permute-start | bytes 786440 | tf_op jit(solution)/shard_map/ppermute | solution.py:71
  76.9 8.2 %collective-permute-done.2 = bf16[32,4096]{1,0:T(8,128)(2,1)} collective-permute-done((bf16[32,4096]{1,0:T(8,128)(2,1)S(1)}, bf16[32,4096]{1,0:T(8,128)(2,1)}, u32[]{:S(2)}, u32[]{:S(2)}) %collective-permute-start.2) | collective-permute-done | bytes 262176 | tf_op jit(solution)/shard_map/ppermute | solution.py:71
  85.1 1.8 %multiply_bitcast_fusion = (f32[4,8,32,128]{3,1,2,0:T(8,128)S(1)}, f32[4,8,32,128]{3,1,2,0:T(8,128)S(1)}) fusion(bf16[32,4096]{1,0:T(8,128)(2,1)} %collective-permute-done.14, bf16[32,4096]{1,0:T(8,128)(2,1)} %collective-permute-done.13, bf16[32,4096]{1,0:T(8,128)(2,1)} %collective-permute-done.12, f32[128,4096]{1,0:T(8,128)S(1)} %get-tuple-element.5, ...), kind=kLoop, calls=%fused_computation.19 | loop fusion | flops 1835008 | bytes 3686404
  87.0 0.8 abs_reduce_fusion
  87.8 0.7 collective-permute-start.21
  88.5 0.7 collective-permute-start.22
  89.2 0.7 collective-permute-start.23
  89.9 0.8 abs_reduce_fusion.1
  90.8 8.0 %collective-permute-start.18 = (bf16[32,32]{1,0:T(8,128)(2,1)S(1)}, bf16[32,32]{1,0:T(8,128)(2,1)S(1)}, u32[]{:S(2)}, u32[]{:S(2)}) collective-permute-start(bf16[32,32]{1,0:T(8,128)(2,1)S(1)} %get-tuple-element.7), channel_id=1, source_target_pairs={{0,4},{3,7},{4,8},{7,11},{8,12},{11,15},{12,0},{15,3},{16,20},{19,... | collective-permute-start | bytes 6152 | tf_op jit(solution)/shard_map/ppermute | solution.py:71
  98.8 1.9 %collective-permute-start.19 = (bf16[32,32]{1,0:T(8,128)(2,1)S(1)}, bf16[32,32]{1,0:T(8,128)(2,1)S(1)}, u32[]{:S(2)}, u32[]{:S(2)}) collective-permute-start(bf16[32,32]{1,0:T(8,128)(2,1)S(1)} %get-tuple-element.7), channel_id=1, source_target_pairs={{0,8},{3,11},{4,12},{7,15},{8,0},{11,3},{12,4},{15,7},{16,24},{19,... | collective-permute-start | bytes 6152 | tf_op jit(solution)/shard_map/ppermute | solution.py:71
  100.8 0.2 divide_convert_fusion
  101.4 0.8 copy.19
  102.4 4.3 %collective-permute-start.20 = (bf16[32,32]{1,0:T(8,128)(2,1)S(1)}, bf16[32,32]{1,0:T(8,128)(2,1)S(1)}, u32[]{:S(2)}, u32[]{:S(2)}) collective-permute-start(bf16[32,32]{1,0:T(8,128)(2,1)S(1)} %get-tuple-element.7), channel_id=1, source_target_pairs={{0,12},{3,15},{4,0},{7,3},{8,4},{11,7},{12,8},{15,11},{16,28},{19,... | collective-permute-start | bytes 6152 | tf_op jit(solution)/shard_map/ppermute | solution.py:71
  106.7 0.9 collective-permute-start.15
  107.8 0.8 copy.20
  109.1 0.7 collective-permute-start.16
  109.9 0.7 collective-permute-start.17
  110.7 1.9 %collective-permute-start.4 = (bf16[32,4096]{1,0:T(8,128)(2,1)}, bf16[32,4096]{1,0:T(8,128)(2,1)S(1)}, u32[]{:S(2)}, u32[]{:S(2)}) collective-permute-start(bf16[32,4096]{1,0:T(8,128)(2,1)} %bitcast.53), channel_id=1, source_target_pairs={{0,4},{3,7},{4,8},{7,11},{8,12},{11,15},{12,0},{15,3},{16,20},{19,... | collective-permute-start | bytes 786440 | tf_op jit(solution)/shard_map/ppermute | solution.py:71
  112.7 4.8 %collective-permute-start.5 = (bf16[32,4096]{1,0:T(8,128)(2,1)}, bf16[32,4096]{1,0:T(8,128)(2,1)S(1)}, u32[]{:S(2)}, u32[]{:S(2)}) collective-permute-start(bf16[32,4096]{1,0:T(8,128)(2,1)} %bitcast.53), channel_id=1, source_target_pairs={{0,8},{3,11},{4,12},{7,15},{8,0},{11,3},{12,4},{15,7},{16,24},{19,... | collective-permute-start | bytes 786440 | tf_op jit(solution)/shard_map/ppermute | solution.py:71
  117.5 0.3 dynamic_update_slice.77
  117.8 0.3 dynamic_update_slice.73
  118.1 0.3 dynamic_update_slice.78
  118.4 0.3 dynamic_update_slice.74
  118.7 0.3 dynamic_update_slice.79
  119.0 0.3 dynamic_update_slice.75
  119.3 0.6 fusion.60
  120.0 2.6 %collective-permute-start.6 = (bf16[32,4096]{1,0:T(8,128)(2,1)}, bf16[32,4096]{1,0:T(8,128)(2,1)S(1)}, u32[]{:S(2)}, u32[]{:S(2)}) collective-permute-start(bf16[32,4096]{1,0:T(8,128)(2,1)} %bitcast.53), channel_id=1, source_target_pairs={{0,12},{3,15},{4,0},{7,3},{8,4},{11,7},{12,8},{15,11},{16,28},{19,... | collective-permute-start | bytes 786440 | tf_op jit(solution)/shard_map/ppermute | solution.py:71
  122.7 1.2 collective-permute-done.4
  123.9 7.1 %collective-permute-done.5 = bf16[32,4096]{1,0:T(8,128)(2,1)S(1)} collective-permute-done((bf16[32,4096]{1,0:T(8,128)(2,1)}, bf16[32,4096]{1,0:T(8,128)(2,1)S(1)}, u32[]{:S(2)}, u32[]{:S(2)}) %collective-permute-start.5) | collective-permute-done | bytes 262176 | tf_op jit(solution)/shard_map/ppermute | solution.py:71
  131.0 1.1 collective-permute-done.6
  132.1 1.4 %fusion.18 = bf16[128,4096]{1,0:T(8,128)(2,1)} fusion(s32[]{:T(128)S(6)} %select_n.124, bf16[1,128,4096]{2,1,0:T(8,128)(2,1)S(1)} %bitcast_dynamic-update-slice_fusion.3, bf16[1,128,4096]{2,1,0:T(8,128)(2,1)S(1)} %bitcast_dynamic-update-slice_fusion), kind=kLoop, calls=%fused_computation.16 | loop fusion | flops 524288 | bytes 3145732 | tf_op jit(solution)/shard_map/jit(dynamic_index_in_dim)/squeeze | solution.py:116
  (64 shorter events, 2.3 us)
Async XLA Ops:
  0.6 7.8 %copy-start = (bf16[128,6656]{1,0:T(8,128)(2,1)S(1)}, bf16[128,6656]{1,0:T(8,128)(2,1)}, u32[]{:S(2)}) copy-start(bf16[128,6656]{1,0:T(8,128)(2,1)} %param.3) | copy-start | bytes 5111812
  3.4 25.3 %collective-permute-start.10 = (bf16[128,1664]{1,0:T(8,128)(2,1)}, bf16[128,1664]{1,0:T(8,128)(2,1)}, u32[]{:S(2)}, u32[]{:S(2)}) collective-permute-start(bf16[128,1664]{1,0:T(8,128)(2,1)} %get-tuple-element.12), channel_id=1, source_target_pairs={{0,2},{2,0},{1,3},{3,1},{4,6},{6,4},{5,7},{7,5},{8,10},{10,8},{9,1... | collective-permute-start | bytes 1277960 | tf_op jit(solution)/shard_map/ppermute | solution.py:94
  6.3 28.5 %collective-permute-start.9 = (bf16[128,1664]{1,0:T(8,128)(2,1)}, bf16[128,1664]{1,0:T(8,128)(2,1)}, u32[]{:S(2)}, u32[]{:S(2)}) collective-permute-start(bf16[128,1664]{1,0:T(8,128)(2,1)} %get-tuple-element.13), channel_id=1, source_target_pairs={{0,2},{2,0},{1,3},{3,1},{4,6},{6,4},{5,7},{7,5},{8,10},{10,8},{9,1... | collective-permute-start | bytes 1277960 | tf_op jit(solution)/shard_map/ppermute | solution.py:94
  6.4 34.7 %collective-permute-start.8 = (bf16[128,1664]{1,0:T(8,128)(2,1)}, bf16[128,1664]{1,0:T(8,128)(2,1)}, u32[]{:S(2)}, u32[]{:S(2)}) collective-permute-start(bf16[128,1664]{1,0:T(8,128)(2,1)} %get-tuple-element.11), channel_id=1, source_target_pairs={{0,2},{2,0},{1,3},{3,1},{4,6},{6,4},{5,7},{7,5},{8,10},{10,8},{9,1... | collective-permute-start | bytes 1277960 | tf_op jit(solution)/shard_map/ppermute | solution.py:94
  8.4 38.8 %collective-permute-start.7 = (bf16[128,1664]{1,0:T(8,128)(2,1)}, bf16[128,1664]{1,0:T(8,128)(2,1)}, u32[]{:S(2)}, u32[]{:S(2)}) collective-permute-start(bf16[128,1664]{1,0:T(8,128)(2,1)} %get-tuple-element.10), channel_id=1, source_target_pairs={{0,2},{2,0},{1,3},{3,1},{4,6},{6,4},{5,7},{7,5},{8,10},{10,8},{9,1... | collective-permute-start | bytes 1277960 | tf_op jit(solution)/shard_map/ppermute | solution.py:94
  27.3 30.4 %collective-permute-start = (bf16[128,4096]{1,0:T(8,128)(2,1)S(1)}, bf16[128,4096]{1,0:T(8,128)(2,1)}, u32[]{:S(2)}, u32[]{:S(2)}) collective-permute-start(bf16[128,4096]{1,0:T(8,128)(2,1)S(1)} %get-tuple-element.24), channel_id=1, source_target_pairs={{1,0},{2,3},{5,4},{6,7},{9,8},{10,11},{13,12},{14,15},{17,16},{18,... | collective-permute-start | bytes 3145736 | tf_op jit(solution)/shard_map/ppermute | solution.py:62
  53.6 18.7 %collective-permute-start.11 = (bf16[128,4096]{1,0:T(8,128)(2,1)S(1)}, bf16[128,4096]{1,0:T(8,128)(2,1)S(1)}, u32[]{:S(2)}, u32[]{:S(2)}) collective-permute-start(bf16[128,4096]{1,0:T(8,128)(2,1)S(1)} %get-tuple-element.22), channel_id=1, source_target_pairs={{0,1},{3,2},{4,5},{7,6},{8,9},{11,10},{12,13},{15,14},{16,17},{19,... | collective-permute-start | bytes 3145736 | tf_op jit(solution)/shard_map/ppermute | solution.py:62
  60.6 14.9 %collective-permute-start.1 = (bf16[32,4096]{1,0:T(8,128)(2,1)S(1)}, bf16[32,4096]{1,0:T(8,128)(2,1)S(1)}, u32[]{:S(2)}, u32[]{:S(2)}) collective-permute-start(bf16[32,4096]{1,0:T(8,128)(2,1)S(1)} %get-tuple-element.17), channel_id=1, source_target_pairs={{0,4},{3,7},{4,8},{7,11},{8,12},{11,15},{12,0},{15,3},{16,20},{19,... | collective-permute-start | bytes 786440 | tf_op jit(solution)/shard_map/ppermute | solution.py:71
  64.6 20.5 %collective-permute-start.2 = (bf16[32,4096]{1,0:T(8,128)(2,1)S(1)}, bf16[32,4096]{1,0:T(8,128)(2,1)}, u32[]{:S(2)}, u32[]{:S(2)}) collective-permute-start(bf16[32,4096]{1,0:T(8,128)(2,1)S(1)} %get-tuple-element.19), channel_id=1, source_target_pairs={{0,8},{3,11},{4,12},{7,15},{8,0},{11,3},{12,4},{15,7},{16,24},{19,... | collective-permute-start | bytes 786440 | tf_op jit(solution)/shard_map/ppermute | solution.py:71
  69.1 16.0 %collective-permute-start.3 = (bf16[32,4096]{1,0:T(8,128)(2,1)S(1)}, bf16[32,4096]{1,0:T(8,128)(2,1)}, u32[]{:S(2)}, u32[]{:S(2)}) collective-permute-start(bf16[32,4096]{1,0:T(8,128)(2,1)S(1)} %get-tuple-element.18), channel_id=1, source_target_pairs={{0,12},{3,15},{4,0},{7,3},{8,4},{11,7},{12,8},{15,11},{16,28},{19,... | collective-permute-start | bytes 786440 | tf_op jit(solution)/shard_map/ppermute | solution.py:71
  72.4 4.5 %copy-start.2 = (s32[4096]{0:T(1024)S(1)}, s32[4096]{0:T(1024)}, u32[]{:S(2)}) copy-start(s32[4096]{0:T(1024)} %param.5) | copy-start | bytes 49156
  72.8 12.3 %collective-permute-start.12 = (bf16[32,4096]{1,0:T(8,128)(2,1)S(1)}, bf16[32,4096]{1,0:T(8,128)(2,1)}, u32[]{:S(2)}, u32[]{:S(2)}) collective-permute-start(bf16[32,4096]{1,0:T(8,128)(2,1)S(1)} %get-tuple-element.14), channel_id=1, source_target_pairs={{1,5},{2,6},{5,9},{6,10},{9,13},{10,14},{13,1},{14,2},{17,21},{18,... | collective-permute-start | bytes 786440 | tf_op jit(solution)/shard_map/ppermute | solution.py:71
  74.1 11.0 %collective-permute-start.13 = (bf16[32,4096]{1,0:T(8,128)(2,1)S(1)}, bf16[32,4096]{1,0:T(8,128)(2,1)}, u32[]{:S(2)}, u32[]{:S(2)}) collective-permute-start(bf16[32,4096]{1,0:T(8,128)(2,1)S(1)} %get-tuple-element.16), channel_id=1, source_target_pairs={{1,9},{2,10},{5,13},{6,14},{9,1},{10,2},{13,5},{14,6},{17,25},{18,... | collective-permute-start | bytes 786440 | tf_op jit(solution)/shard_map/ppermute | solution.py:71
  75.5 1.4 %copy-start.1 = (bf16[32,4096]{1,0:T(8,128)(2,1)}, bf16[32,4096]{1,0:T(8,128)(2,1)S(1)}, u32[]{:S(2)}) copy-start(bf16[32,4096]{1,0:T(8,128)(2,1)S(1)} %collective-permute-done.1) | copy-start | bytes 786436
  75.5 9.6 %collective-permute-start.14 = (bf16[32,4096]{1,0:T(8,128)(2,1)S(1)}, bf16[32,4096]{1,0:T(8,128)(2,1)}, u32[]{:S(2)}, u32[]{:S(2)}) collective-permute-start(bf16[32,4096]{1,0:T(8,128)(2,1)S(1)} %get-tuple-element.15), channel_id=1, source_target_pairs={{1,13},{2,14},{5,1},{6,2},{9,5},{10,6},{13,9},{14,10},{17,29},{18,... | collective-permute-start | bytes 786440 | tf_op jit(solution)/shard_map/ppermute | solution.py:71
  87.8 14.5 %collective-permute-start.21 = (bf16[32,32]{1,0:T(8,128)(2,1)S(1)}, bf16[32,32]{1,0:T(8,128)(2,1)S(1)}, u32[]{:S(2)}, u32[]{:S(2)}) collective-permute-start(bf16[32,32]{1,0:T(8,128)(2,1)S(1)} %get-tuple-element.3), channel_id=1, source_target_pairs={{1,5},{2,6},{5,9},{6,10},{9,13},{10,14},{13,1},{14,2},{17,21},{18,... | collective-permute-start | bytes 6152 | tf_op jit(solution)/shard_map/ppermute | solution.py:71
  88.5 18.1 %collective-permute-start.22 = (bf16[32,32]{1,0:T(8,128)(2,1)S(1)}, bf16[32,32]{1,0:T(8,128)(2,1)S(1)}, u32[]{:S(2)}, u32[]{:S(2)}) collective-permute-start(bf16[32,32]{1,0:T(8,128)(2,1)S(1)} %get-tuple-element.3), channel_id=1, source_target_pairs={{1,9},{2,10},{5,13},{6,14},{9,1},{10,2},{13,5},{14,6},{17,25},{18,... | collective-permute-start | bytes 6152 | tf_op jit(solution)/shard_map/ppermute | solution.py:71
  89.2 19.9 %collective-permute-start.23 = (bf16[32,32]{1,0:T(8,128)(2,1)S(1)}, bf16[32,32]{1,0:T(8,128)(2,1)S(1)}, u32[]{:S(2)}, u32[]{:S(2)}) collective-permute-start(bf16[32,32]{1,0:T(8,128)(2,1)S(1)} %get-tuple-element.3), channel_id=1, source_target_pairs={{1,13},{2,14},{5,1},{6,2},{9,5},{10,6},{13,9},{14,10},{17,29},{18,... | collective-permute-start | bytes 6152 | tf_op jit(solution)/shard_map/ppermute | solution.py:71
  90.8 19.1 %collective-permute-start.18 = (bf16[32,32]{1,0:T(8,128)(2,1)S(1)}, bf16[32,32]{1,0:T(8,128)(2,1)S(1)}, u32[]{:S(2)}, u32[]{:S(2)}) collective-permute-start(bf16[32,32]{1,0:T(8,128)(2,1)S(1)} %get-tuple-element.7), channel_id=1, source_target_pairs={{0,4},{3,7},{4,8},{7,11},{8,12},{11,15},{12,0},{15,3},{16,20},{19,... | collective-permute-start | bytes 6152 | tf_op jit(solution)/shard_map/ppermute | solution.py:71
  98.8 11.8 %collective-permute-start.19 = (bf16[32,32]{1,0:T(8,128)(2,1)S(1)}, bf16[32,32]{1,0:T(8,128)(2,1)S(1)}, u32[]{:S(2)}, u32[]{:S(2)}) collective-permute-start(bf16[32,32]{1,0:T(8,128)(2,1)S(1)} %get-tuple-element.7), channel_id=1, source_target_pairs={{0,8},{3,11},{4,12},{7,15},{8,0},{11,3},{12,4},{15,7},{16,24},{19,... | collective-permute-start | bytes 6152 | tf_op jit(solution)/shard_map/ppermute | solution.py:71
  102.4 10.3 %collective-permute-start.20 = (bf16[32,32]{1,0:T(8,128)(2,1)S(1)}, bf16[32,32]{1,0:T(8,128)(2,1)S(1)}, u32[]{:S(2)}, u32[]{:S(2)}) collective-permute-start(bf16[32,32]{1,0:T(8,128)(2,1)S(1)} %get-tuple-element.7), channel_id=1, source_target_pairs={{0,12},{3,15},{4,0},{7,3},{8,4},{11,7},{12,8},{15,11},{16,28},{19,... | collective-permute-start | bytes 6152 | tf_op jit(solution)/shard_map/ppermute | solution.py:71
  106.7 13.3 %collective-permute-start.15 = (bf16[32,4096]{1,0:T(8,128)(2,1)}, bf16[32,4096]{1,0:T(8,128)(2,1)S(1)}, u32[]{:S(2)}, u32[]{:S(2)}) collective-permute-start(bf16[32,4096]{1,0:T(8,128)(2,1)} %bitcast.52), channel_id=1, source_target_pairs={{1,5},{2,6},{5,9},{6,10},{9,13},{10,14},{13,1},{14,2},{17,21},{18,... | collective-permute-start | bytes 786440 | tf_op jit(solution)/shard_map/ppermute | solution.py:71
  109.1 13.5 %collective-permute-start.16 = (bf16[32,4096]{1,0:T(8,128)(2,1)}, bf16[32,4096]{1,0:T(8,128)(2,1)S(1)}, u32[]{:S(2)}, u32[]{:S(2)}) collective-permute-start(bf16[32,4096]{1,0:T(8,128)(2,1)} %bitcast.52), channel_id=1, source_target_pairs={{1,9},{2,10},{5,13},{6,14},{9,1},{10,2},{13,5},{14,6},{17,25},{18,... | collective-permute-start | bytes 786440 | tf_op jit(solution)/shard_map/ppermute | solution.py:71
  109.9 12.7 %collective-permute-start.17 = (bf16[32,4096]{1,0:T(8,128)(2,1)}, bf16[32,4096]{1,0:T(8,128)(2,1)S(1)}, u32[]{:S(2)}, u32[]{:S(2)}) collective-permute-start(bf16[32,4096]{1,0:T(8,128)(2,1)} %bitcast.52), channel_id=1, source_target_pairs={{1,13},{2,14},{5,1},{6,2},{9,5},{10,6},{13,9},{14,10},{17,29},{18,... | collective-permute-start | bytes 786440 | tf_op jit(solution)/shard_map/ppermute | solution.py:71
  110.7 13.2 %collective-permute-start.4 = (bf16[32,4096]{1,0:T(8,128)(2,1)}, bf16[32,4096]{1,0:T(8,128)(2,1)S(1)}, u32[]{:S(2)}, u32[]{:S(2)}) collective-permute-start(bf16[32,4096]{1,0:T(8,128)(2,1)} %bitcast.53), channel_id=1, source_target_pairs={{0,4},{3,7},{4,8},{7,11},{8,12},{11,15},{12,0},{15,3},{16,20},{19,... | collective-permute-start | bytes 786440 | tf_op jit(solution)/shard_map/ppermute | solution.py:71
  112.7 18.3 %collective-permute-start.5 = (bf16[32,4096]{1,0:T(8,128)(2,1)}, bf16[32,4096]{1,0:T(8,128)(2,1)S(1)}, u32[]{:S(2)}, u32[]{:S(2)}) collective-permute-start(bf16[32,4096]{1,0:T(8,128)(2,1)} %bitcast.53), channel_id=1, source_target_pairs={{0,8},{3,11},{4,12},{7,15},{8,0},{11,3},{12,4},{15,7},{16,24},{19,... | collective-permute-start | bytes 786440 | tf_op jit(solution)/shard_map/ppermute | solution.py:71
  120.0 12.1 %collective-permute-start.6 = (bf16[32,4096]{1,0:T(8,128)(2,1)}, bf16[32,4096]{1,0:T(8,128)(2,1)S(1)}, u32[]{:S(2)}, u32[]{:S(2)}) collective-permute-start(bf16[32,4096]{1,0:T(8,128)(2,1)} %bitcast.53), channel_id=1, source_target_pairs={{0,12},{3,15},{4,0},{7,3},{8,4},{11,7},{12,8},{15,11},{16,28},{19,... | collective-permute-start | bytes 786440 | tf_op jit(solution)/shard_map/ppermute | solution.py:71

commit v2 on v1

v2 whole, which is shorter than its diff:
```python
import math

import jax
import jax.numpy as jnp
from jax import lax
from jax.sharding import PartitionSpec as P

BLOCK = 128
epsilon = 1e-06


def hadamard(order):
    indices = jnp.arange(order, dtype=jnp.int32)
    parity = jnp.zeros((order, order), jnp.int32)
    for position in range(order.bit_length() - 1):
        parity = parity + (indices[:, None] >> position & 1) * (indices[None, :] >> position & 1)
    return (1 - 2 * (parity % 2)).astype(jnp.float32) / math.sqrt(order)


def rotate_blocks(values, flips):
    blocks = (values * flips[None, :]).reshape(values.shape[0], -1, BLOCK)
    rotated = jnp.einsum("tnb,bc->tnc", blocks, hadamard(BLOCK), precision=lax.Precision.HIGHEST)
    return rotated.reshape(values.shape)


def encode_blocks(values):
    blocks = values.reshape(values.shape[:-1] + (-1, BLOCK))
    scales = (jnp.max(jnp.abs(blocks), axis=-1) + epsilon).astype(jnp.bfloat16)
    encoded = (blocks / scales.astype(jnp.float32)[..., None]).astype(jnp.bfloat16)
    return (encoded.reshape(values.shape), scales)


def shards(hidden, down_weight, sign_bits):
    seq_count = lax.axis_size("seq")
    sub_count = lax.axis_size("sub")
    seq_at = lax.axis_index("seq")
    sub_at = lax.axis_index("sub")
    rows, depth = hidden.shape
    per_sub = seq_count // sub_count
    chunks = 4
    width = depth // chunks
    flips = (2 * sign_bits - 1).astype(jnp.float32)

    def finish(partial_value):
        summed = lax.psum_scatter(
            partial_value.astype(jnp.bfloat16), ("tensor", "sub"), scatter_dimension=0, tiled=True
        ).astype(jnp.float32)
        codes, scales = encode_blocks(rotate_blocks(summed, flips))
        padding = jnp.zeros((codes.shape[0], -scales.shape[1] % BLOCK), jnp.bfloat16)
        packed = jnp.concatenate([codes, scales, padding], axis=1)
        full = lax.all_gather(packed, ("tensor", "sub"), axis=0, tiled=True)
        return full[:, : codes.shape[1]], full[:, codes.shape[1] : codes.shape[1] + scales.shape[1]]

    def from_seq(values, shift):
        return lax.ppermute(values, "seq", [(s, (s + shift) % seq_count) for s in range(seq_count)])

    results = []
    for shift in range(seq_count):
        if shift == 0:
            partial_value = jnp.dot(hidden, down_weight, preferred_element_type=jnp.float32)
        else:
            partial_value = jnp.zeros((rows, down_weight.shape[1]), jnp.float32)
            for chunk in range(chunks):
                part = slice(chunk * width, (chunk + 1) * width)
                arrived = from_seq(hidden[:, part], shift)
                partial_value = partial_value + jnp.dot(
                    arrived, down_weight[part], preferred_element_type=jnp.float32
                )
        results.append(finish(partial_value))

    out = []
    for at in range(2):
        stacked = jnp.stack([result[at] for result in results])
        held = []
        for place in range(per_sub):
            shift = (seq_at - (sub_at * per_sub + place)) % seq_count
            held.append(lax.dynamic_index_in_dim(stacked, shift, 0, keepdims=False))
        out.append(jnp.concatenate(held))
    return tuple(out)


def solution(mesh):
    return jax.shard_map(
        shards,
        mesh=mesh,
        in_specs=(P(("groups", "seq"), ("tensor", "sub")), P(("tensor", "sub"), "seq"), P("seq")),
        out_specs=(P(("groups", "sub"), "seq"), P(("groups", "sub"), "seq")),
        check_vma=False,
    )
```

time: 135 us -> 161 us (1.19)
  waiting for transfers between devices: 17.7 us -> 82.5 us
  starting transfers between devices: 53.8 us -> 5.27 us
  between operations: 1.23 us -> 14 us
  other arithmetic: 7.35 us -> 3.31 us
  matrix products: 45.4 us -> 48.7 us
    ppermute x20 -> x0, starting transfers between devices: 48.8 us -> none  [the longest x18 43.5 us: along_tensor(): return lax.ppermute(values, AXES, pairs)]
    all_gather x0 -> x2, waiting for transfers between devices: none -> 42.3 us  [finish(): full = lax.all_gather(packed, ('tensor', 'sub'), axis=0, tiled=True)]
    reduce_scatter x0 -> x2, waiting for transfers between devices: none -> 40.1 us  [finish(): lax.psum_scatter(partial_value.astype(jnp.bfloat16), ('tensor', 'sub'), s...]
    ppermute x20 -> x0, waiting for transfers between devices: 17.7 us -> none  [the longest x18 17.7 us: along_tensor(): return lax.ppermute(values, AXES, pairs)]
    convert_element_type x2 -> x0, other arithmetic: 3.15 us -> none  [finish(): narrow = total.astype(jnp.bfloat16)]
    dot_general x4, matrix products: 24.9 us -> 27.4 us  [shards(): jnp.dot(arrived, down_weight[part], preferred_element_type=jnp.float32)]
    another operation x12 -> x6, local copies, waits for them, and re-layouts: 0.94 us -> 3.15 us  [shards(): stacked = jnp.stack([result[at] for result in results])]
    dynamic_update_slice x16 -> x0, local copies, waits for them, and re-layouts: 2.21 us -> none  [the longest x8 2.02 us: finish(): full_scales = lax.dynamic_update_slice_in_dim(full_scales, held[1], at, 0)]
  transfers between devices with their start and end apart: 24 -> 8, of which waited for: 4 -> 4; matrix products, arithmetic and copies ran while one was open for 40% -> 31% of each run, Pallas kernels for 0% -> 0%
where the time goes in v2:
time: 161 us; the launch traced here: 160 us
  waiting for transfers between devices  82.5 us (51%)
  matrix products  48.7 us (30%)
  between operations  14 us (9%)
  local copies, waits for them, and re-layouts  6.5 us (4%)
  starting transfers between devices  5.27 us (3%)
  other arithmetic  3.31 us (2%)
    all_gather x2, waiting for transfers between devices, finish(): full = lax.all_gather(packed, ('tensor', 'sub'), axis=0, tiled=True)  42.3 us
    reduce_scatter x2, waiting for transfers between devices, finish(): lax.psum_scatter(partial_value.astype(jnp.bfloat16), ('tensor', 'sub'), s...  40.1 us
    dot_general x4, matrix products, shards(): jnp.dot(arrived, down_weight[part], preferred_element_type=jnp.float32)  27.4 us
    dot_general x1, matrix products, shards(): jnp.dot(hidden, down_weight, preferred_element_type=jnp.float32)  20.1 us
    ppermute x4, starting transfers between devices, from_seq(): lax.ppermute(values, 'seq', [(s, (s + shift) % seq_count) for s in range(...  5.11 us
  transfers between devices with their start and end apart: 8, of which 4 were waited for; matrix products, arithmetic and copies ran while one was open for 31% of the time, Pallas kernels for 0%

profile of v2, /device:TPU:0, one launch (start us, length us, event | category | flops | bytes accessed | tf_op | source)
XLA Modules:
  0.0 160.3 jit_solution(5719814123137795505)
XLA Ops:
  7.2 0.0 copy-start
  7.2 0.0 reduce-scatter.3.cloned.1.call-start
  7.2 1.6 %fusion.74 = (bf16[128,1664]{1,0:T(8,128)(2,1)S(1)}, bf16[128,1664]{1,0:T(8,128)(2,1)S(1)}, bf16[128,1664]{1,0:T(8,128)(2,1)S(1)}, bf16[128,1664]{1,0:T(8,128)(2,1)S(1)}) fusion(bf16[128,6656]{1,0:T(8,128)(2,1)} %param.3), kind=kLoop, calls=%fused_computation.94 | loop fusion | bytes 3407872 | tf_op jit(solution)/shard_map/slice | solution.py:65
  8.9 3.0 %collective-permute-start.3 = (bf16[128,1664]{1,0:T(8,128)(2,1)S(1)}, bf16[128,1664]{1,0:T(8,128)(2,1)}, u32[]{:S(2)}, u32[]{:S(2)}) collective-permute-start(bf16[128,1664]{1,0:T(8,128)(2,1)S(1)} %get-tuple-element.8), channel_id=1, source_target_pairs={{0,2},{2,0},{1,3},{3,1},{4,6},{6,4},{5,7},{7,5},{8,10},{10,8},{9,1... | collective-permute-start | bytes 1277960 | tf_op jit(solution)/shard_map/ppermute | solution.py:55
  11.9 0.1 collective-permute-start.2
  11.9 1.9 %collective-permute-start.1 = (bf16[128,1664]{1,0:T(8,128)(2,1)S(1)}, bf16[128,1664]{1,0:T(8,128)(2,1)}, u32[]{:S(2)}, u32[]{:S(2)}) collective-permute-start(bf16[128,1664]{1,0:T(8,128)(2,1)S(1)} %get-tuple-element.7), channel_id=1, source_target_pairs={{0,2},{2,0},{1,3},{3,1},{4,6},{6,4},{5,7},{7,5},{8,10},{10,8},{9,1... | collective-permute-start | bytes 1277960 | tf_op jit(solution)/shard_map/ppermute | solution.py:55
  13.9 0.1 collective-permute-start
  14.0 20.1 %convolution_convert_fusion = bf16[128,4096]{1,0:T(8,128)(2,1)} fusion(bf16[128,6656]{1,0:T(8,128)(2,1)S(1)} %copy-done, bf16[6656,4096]{1,0:T(8,128)(2,1)} %param.4), kind=kOutput, calls=%fused_computation.11 | convolution fusion | flops 6979846144 | bytes 57278464 | tf_op jit(solution)/shard_map/dot_general | solution.py:60
  34.1 0.0 reduce-scatter.3.cloned.1.call-update
  34.1 0.0 reduce-scatter.5.cloned.1.call-start
  34.2 0.0 collective-permute-done.3
  34.2 6.2 %fusion = f32[128,4096]{1,0:T(8,128)S(1)} fusion(bf16[128,1664]{1,0:T(8,128)(2,1)} %collective-permute-done.3, bf16[6656,4096]{1,0:T(8,128)(2,1)} %param.4), kind=kOutput, calls=%fused_computation | convolution fusion | flops 1744830464 | bytes 16154624 | tf_op jit(solution)/shard_map/dot_general | solution.py:66
  40.3 0.0 collective-permute-done.2
  40.3 6.3 %fusion.2 = f32[128,4096]{1,0:T(8,128)S(1)} fusion(bf16[128,1664]{1,0:T(8,128)(2,1)} %collective-permute-done.2, bf16[6656,4096]{1,0:T(8,128)(2,1)} %param.4), kind=kOutput, calls=%fused_computation.2 | convolution fusion | flops 1744830464 | bytes 16154624 | tf_op jit(solution)/shard_map/dot_general | solution.py:66
  46.6 0.0 collective-permute-done.1
  46.6 6.2 %fusion.4 = f32[128,4096]{1,0:T(8,128)S(1)} fusion(bf16[128,1664]{1,0:T(8,128)(2,1)} %collective-permute-done.1, bf16[6656,4096]{1,0:T(8,128)(2,1)} %param.4), kind=kOutput, calls=%fused_computation.4 | convolution fusion | flops 1744830464 | bytes 16154624 | tf_op jit(solution)/shard_map/dot_general | solution.py:66
  52.9 0.0 copy-start.2
  52.9 0.0 collective-permute-done
  52.9 8.7 %fusion.17 = bf16[128,4096]{1,0:T(8,128)(2,1)} fusion(f32[128,4096]{1,0:T(8,128)S(1)} %fusion, f32[128,4096]{1,0:T(8,128)S(1)} %fusion.2, f32[128,4096]{1,0:T(8,128)S(1)} %fusion.4, bf16[128,1664]{1,0:T(8,128)(2,1)} %collective-permute-done, bf16[6656,4096]{1,0:T(8,128)(2,1)} %param.4), kind=kOutput, calls=%fused_computation.12 | convolution fusion | flops 1746927616 | bytes 21397504 | tf_op jit(solution)/shard_map/dot_general | solution.py:66
  61.6 0.0 reduce-scatter.5.cloned.1.call-update
  61.6 0.0 all-gather.5.cloned.1.call-start
  61.7 0.0 copy-done.2
  61.7 6.6 %reduce-scatter.3.cloned.1.call-done = bf16[16,4096]{1,0:T(8,128)(2,1)} async-done(((bf16[128,4096]{1,0:T(8,128)(2,1)}), bf16[16,4096]{1,0:T(8,128)(2,1)}) %reduce-scatter.3.cloned.1.call-update) | async-done | bytes 131088 | tf_op jit(solution)/shard_map/reduce_scatter | solution.py:45
  68.3 33.6 %reduce-scatter.5.cloned.1.call-done = bf16[16,4096]{1,0:T(8,128)(2,1)} async-done(((bf16[128,4096]{1,0:T(8,128)(2,1)}), bf16[16,4096]{1,0:T(8,128)(2,1)}) %reduce-scatter.5.cloned.1.call-update) | async-done | bytes 131088 | tf_op jit(solution)/shard_map/reduce_scatter | solution.py:45
  101.9 1.0 multiply_bitcast_fusion
  102.9 0.1 copy.14
  103.0 0.6 abs_reduce_fusion
  103.6 0.1 divide_convert_fusion
  103.7 0.1 copy.18
  103.8 0.7 concatenate.7
  104.5 0.0 all-gather.5.cloned.1.call-update
  104.6 0.0 all-gather.3.cloned.1.call-start
  104.6 0.1 copy.12
  104.7 0.6 abs_reduce_fusion.1
  105.3 0.1 divide_convert_fusion.1
  105.5 0.1 copy.19
  105.5 0.7 concatenate.6
  106.3 0.0 all-gather.3.cloned.1.call-update
  106.3 19.0 %all-gather.5.cloned.1.call-done = bf16[128,4224]{1,0:T(8,128)(2,1)} async-done(((bf16[16,4224]{1,0:T(8,128)(2,1)}), bf16[128,4224]{1,0:T(8,128)(2,1)}) %all-gather.5.cloned.1.call-update) | async-done | bytes 1081360 | tf_op jit(solution)/shard_map/all_gather | solution.py:51
  125.4 0.8 slice_bitcast_fusion.2
  126.1 0.1 copy.11
  126.2 23.2 %all-gather.3.cloned.1.call-done = bf16[128,4224]{1,0:T(8,128)(2,1)} async-done(((bf16[16,4224]{1,0:T(8,128)(2,1)}), bf16[128,4224]{1,0:T(8,128)(2,1)}) %all-gather.3.cloned.1.call-update) | async-done | bytes 1081360 | tf_op jit(solution)/shard_map/all_gather | solution.py:51
  149.4 0.9 slice_bitcast_fusion.3
  150.3 0.1 copy.10
  150.4 0.6 fusion.63
  151.0 1.3 slice_bitcast_fusion
  152.3 0.1 slice_bitcast_fusion.1
  152.4 1.4 fusion.21
  (11 shorter events, 0.0 us)
Async XLA Ops:
  7.2 6.8 %copy-start = (bf16[128,6656]{1,0:T(8,128)(2,1)S(1)}, bf16[128,6656]{1,0:T(8,128)(2,1)}, u32[]{:S(2)}) copy-start(bf16[128,6656]{1,0:T(8,128)(2,1)} %param.3) | copy-start | bytes 5111812
  7.2 61.1 %reduce-scatter.3.cloned.1.call-start = ((), (), s32[]{:S(2)}) async-start(), calls=%async_computation.2 | async-start | bytes 1179648 | tf_op jit(solution)/shard_map/reduce_scatter | solution.py:45
  8.9 25.3 %collective-permute-start.3 = (bf16[128,1664]{1,0:T(8,128)(2,1)S(1)}, bf16[128,1664]{1,0:T(8,128)(2,1)}, u32[]{:S(2)}, u32[]{:S(2)}) collective-permute-start(bf16[128,1664]{1,0:T(8,128)(2,1)S(1)} %get-tuple-element.8), channel_id=1, source_target_pairs={{0,2},{2,0},{1,3},{3,1},{4,6},{6,4},{5,7},{7,5},{8,10},{10,8},{9,1... | collective-permute-start | bytes 1277960 | tf_op jit(solution)/shard_map/ppermute | solution.py:55
  11.9 28.5 %collective-permute-start.2 = (bf16[128,1664]{1,0:T(8,128)(2,1)S(1)}, bf16[128,1664]{1,0:T(8,128)(2,1)}, u32[]{:S(2)}, u32[]{:S(2)}) collective-permute-start(bf16[128,1664]{1,0:T(8,128)(2,1)S(1)} %get-tuple-element.9), channel_id=1, source_target_pairs={{0,2},{2,0},{1,3},{3,1},{4,6},{6,4},{5,7},{7,5},{8,10},{10,8},{9,1... | collective-permute-start | bytes 1277960 | tf_op jit(solution)/shard_map/ppermute | solution.py:55
  11.9 34.7 %collective-permute-start.1 = (bf16[128,1664]{1,0:T(8,128)(2,1)S(1)}, bf16[128,1664]{1,0:T(8,128)(2,1)}, u32[]{:S(2)}, u32[]{:S(2)}) collective-permute-start(bf16[128,1664]{1,0:T(8,128)(2,1)S(1)} %get-tuple-element.7), channel_id=1, source_target_pairs={{0,2},{2,0},{1,3},{3,1},{4,6},{6,4},{5,7},{7,5},{8,10},{10,8},{9,1... | collective-permute-start | bytes 1277960 | tf_op jit(solution)/shard_map/ppermute | solution.py:55
  13.9 39.0 %collective-permute-start = (bf16[128,1664]{1,0:T(8,128)(2,1)S(1)}, bf16[128,1664]{1,0:T(8,128)(2,1)}, u32[]{:S(2)}, u32[]{:S(2)}) collective-permute-start(bf16[128,1664]{1,0:T(8,128)(2,1)S(1)} %get-tuple-element.6), channel_id=1, source_target_pairs={{0,2},{2,0},{1,3},{3,1},{4,6},{6,4},{5,7},{7,5},{8,10},{10,8},{9,1... | collective-permute-start | bytes 1277960 | tf_op jit(solution)/shard_map/ppermute | solution.py:55
  34.1 67.8 %reduce-scatter.5.cloned.1.call-start = ((), (), s32[]{:S(2)}) async-start(), calls=%async_computation.4 | async-start | bytes 1179648 | tf_op jit(solution)/shard_map/reduce_scatter | solution.py:45
  52.9 8.8 %copy-start.2 = (s32[4096]{0:T(1024)S(1)}, s32[4096]{0:T(1024)}, u32[]{:S(2)}) copy-start(s32[4096]{0:T(1024)} %param.5) | copy-start | bytes 49156
  61.6 63.8 %all-gather.5.cloned.1.call-start = ((), (), s32[]{:S(2)}) async-start(), calls=%async_computation.5 | async-start | bytes 1216512 | tf_op jit(solution)/shard_map/all_gather | solution.py:51
  104.6 44.9 %all-gather.3.cloned.1.call-start = ((), (), s32[]{:S(2)}) async-start(), calls=%async_computation.3 | async-start | bytes 1216512 | tf_op jit(solution)/shard_map/all_gather | solution.py:51
  149.4 2.9 %copy-start.1 = (bf16[128,4224]{1,0:T(8,128)(2,1)S(1)}, bf16[128,4224]{1,0:T(8,128)(2,1)}, u32[]{:S(2)}) copy-start(bf16[128,4224]{1,0:T(8,128)(2,1)} %all-gather.3.cloned.1.call-done) | copy-start | bytes 3244036
Sparse Core Ops, SparseCore 0:
  34.2 34.0 reduce-scatter.2
  71.2 30.6 reduce-scatter.4
  104.7 20.6 all-gather.4
  127.4 21.9 all-gather.2

commit v3 on v2

v3 whole, which is shorter than its diff:
```python
import functools
import math

import jax
import jax.numpy as jnp
import numpy as np
from jax import lax
from jax.experimental import pallas as pl
from jax.experimental.pallas import tpu as pltpu
from jax.sharding import PartitionSpec as P

BLOCK = 128
UNIT = 512
VMEM_LIMIT = 48 * 2**20
epsilon = 1e-06


def hadamard(order):
    indices = np.arange(order)
    parity = np.zeros((order, order), np.int64)
    for position in range(order.bit_length() - 1):
        parity = parity + (indices[:, None] >> position & 1) * (indices[None, :] >> position & 1)
    return ((1 - 2 * (parity % 2)) / math.sqrt(order)).astype(np.float32)


def multiply_body(has_total, start_ref, x_ref, w_ref, *rest):
    product = jnp.dot(x_ref[...], w_ref[...], preferred_element_type=jnp.float32)
    if has_total:
        product = product + rest[0][...]
    out_ref = rest[-1]
    out_ref[...] = product.astype(out_ref.dtype)


def multiply(x, w, row, start, columns, wide, total=None, tokens=(), dtype=jnp.float32):
    rows, depth = x.shape
    steps = columns // wide
    in_specs = [
        pl.BlockSpec((rows, depth), lambda n, s: (0, 0)),
        pl.BlockSpec((pl.Element(depth), pl.Element(wide)), lambda n, s: (row, (s[0] * steps + n) * wide)),
    ]
    operands = [x, w]
    if total is not None:
        in_specs.append(pl.BlockSpec((rows, wide), lambda n, s: (0, s[0] * steps + n)))
        operands.append(total)
    for token in tokens:
        in_specs.append(pl.BlockSpec(memory_space=pl.ANY))
        operands.append(token)
    return pl.pallas_call(
        functools.partial(multiply_body, total is not None),
        out_shape=jax.ShapeDtypeStruct((rows, columns), dtype),
        grid_spec=pltpu.PrefetchScalarGridSpec(
            num_scalar_prefetch=1,
            grid=(steps,),
            in_specs=in_specs,
            out_specs=pl.BlockSpec((rows, wide), lambda n, s: (0, n)),
        ),
        compiler_params=pltpu.CompilerParams(vmem_limit_bytes=VMEM_LIMIT),
        cost_estimate=pl.CostEstimate(
            flops=2 * rows * depth * columns, bytes_accessed=2 * depth * columns, transcendentals=0
        ),
    )(start, *operands)


def encode_body(parts_ref, flips_ref, rotation_ref, out_ref):
    count, rows, columns = parts_ref.shape
    blocks = columns // BLOCK
    held = []
    for block in range(blocks):
        at = slice(block * BLOCK, (block + 1) * BLOCK)
        total = parts_ref[0, :, at].astype(jnp.float32)
        for part in range(1, count):
            total = total + parts_ref[part, :, at].astype(jnp.float32)
        held.append(total * flips_ref[:, at])
    rotation = rotation_ref[...]
    lane = lax.broadcasted_iota(jnp.int32, (rows, BLOCK), 1)
    scales = jnp.zeros((rows, BLOCK), jnp.float32)
    for block in range(blocks):
        at = slice(block * BLOCK, (block + 1) * BLOCK)
        rotated = jnp.dot(
            held[block], rotation, precision=lax.Precision.HIGHEST, preferred_element_type=jnp.float32
        )
        largest = jnp.max(jnp.abs(rotated), axis=1, keepdims=True)
        scale = (largest + epsilon).astype(jnp.bfloat16).astype(jnp.float32)
        codes = (rotated / scale).astype(jnp.bfloat16)
        scales = jnp.where(lane == block, scale, scales)
        for part in range(count):
            out_ref[part, :, at] = codes
    for part in range(count):
        out_ref[part, :, columns:] = scales.astype(jnp.bfloat16)


def encode(parts, flips):
    count, rows, columns = parts.shape
    return pl.pallas_call(
        encode_body,
        out_shape=jax.ShapeDtypeStruct((count, rows, columns + BLOCK), jnp.bfloat16),
        compiler_params=pltpu.CompilerParams(vmem_limit_bytes=VMEM_LIMIT),
        cost_estimate=pl.CostEstimate(
            flops=12 * rows * columns * BLOCK, bytes_accessed=4 * count * rows * columns, transcendentals=0
        ),
    )(parts, flips, hadamard(BLOCK))


def choose_body(places, chosen_ref, *refs):
    out_ref = refs[-1]
    rows = refs[0].shape[0]
    for place in range(places):
        for index, ref in enumerate(refs[:-1]):

            @pl.when(chosen_ref[place] == index)
            def _():
                out_ref[place * rows : (place + 1) * rows] = ref[...]


def choose(results, chosen):
    rows, columns = results[0].shape
    vmem = pl.BlockSpec(memory_space=pltpu.VMEM)
    return pl.pallas_call(
        functools.partial(choose_body, chosen.shape[0]),
        out_shape=jax.ShapeDtypeStruct((chosen.shape[0] * rows, columns), jnp.bfloat16),
        in_specs=[pl.BlockSpec(memory_space=pltpu.SMEM)] + [vmem] * len(results),
        out_specs=vmem,
        compiler_params=pltpu.CompilerParams(vmem_limit_bytes=VMEM_LIMIT),
    )(chosen, *results)


def assemble_body(places, half, chosen_ref, here_ref, other_ref, *refs):
    codes_ref, scales_ref = refs[-2:]
    rows = refs[0].shape[0]
    scales = half // BLOCK

    def put(core, mine_ref, place):
        at = slice(place * rows, (place + 1) * rows)
        columns = slice(core * half, (core + 1) * half)
        rest = slice((1 - core) * half, (2 - core) * half)
        codes_ref[at, columns] = mine_ref[:, :half]
        codes_ref[at, rest] = other_ref[at, :half]
        pair = [mine_ref[:, half : half + scales], other_ref[at, half : half + scales]]
        scales_ref[at] = jnp.concatenate(pair if core == 0 else pair[::-1], axis=1)

    for place in range(places):
        for core in range(2):
            for index, ref in enumerate(refs[:-2]):
                pl.when((chosen_ref[place] == index) & (here_ref[0] == core))(
                    functools.partial(put, core, ref, place)
                )


def assemble(results, chosen, here, other, half):
    rows = other.shape[0]
    vmem = pl.BlockSpec(memory_space=pltpu.VMEM)
    smem = pl.BlockSpec(memory_space=pltpu.SMEM)
    return pl.pallas_call(
        functools.partial(assemble_body, chosen.shape[0], half),
        out_shape=(
            jax.ShapeDtypeStruct((rows, 2 * half), jnp.bfloat16),
            jax.ShapeDtypeStruct((rows, 2 * half // BLOCK), jnp.bfloat16),
        ),
        in_specs=[smem, smem, vmem] + [vmem] * len(results),
        out_specs=(vmem, vmem),
        compiler_params=pltpu.CompilerParams(vmem_limit_bytes=VMEM_LIMIT),
    )(chosen, here, other, *results)


def cut(depth):
    if depth % UNIT or depth < 8 * UNIT:
        return [depth]
    units = depth // UNIT
    sizes = []
    for share in (0.31, 0.31, 0.23):
        sizes.append(max(1, round(units * share)))
    sizes.append(units - sum(sizes))
    return [size * UNIT for size in sizes]


def shards(hidden, down_weight, sign_bits):
    tensor_count = lax.axis_size("tensor")
    seq_count = lax.axis_size("seq")
    sub_count = lax.axis_size("sub")
    seq_at = lax.axis_index("seq")
    sub_at = lax.axis_index("sub")
    rows, depth = hidden.shape
    half = down_weight.shape[1] // sub_count
    per_sub = seq_count // sub_count
    piece = rows // tensor_count
    wide = min(256, half)
    wide_chunk = min(512, half)
    flips = (2 * sign_bits - 1).astype(jnp.float32)[None, :]
    own_flips = lax.dynamic_slice_in_dim(flips, sub_at * half, half, 1)
    whole = jnp.zeros((1,), jnp.int32)
    here = jnp.reshape(sub_at, (1,)).astype(jnp.int32)
    there = 1 - here

    def swap(values):
        return lax.ppermute(values, "sub", [(0, 1), (1, 0)])

    def scatter(sent, kept):
        total = (kept.astype(jnp.float32) + swap(sent).astype(jnp.float32)).astype(jnp.bfloat16)
        return [total], lax.all_to_all(
            total.reshape(tensor_count, piece, half), "tensor", split_axis=0, concat_axis=0, tiled=True
        )

    def gather(parts):
        packed = encode(parts, own_flips)
        full = lax.all_to_all(packed, "tensor", split_axis=0, concat_axis=0, tiled=True)
        return [packed], full.reshape(rows, half + BLOCK)

    sizes = cut(depth)
    places = [sum(sizes[:index]) for index in range(len(sizes))]
    slices = [hidden[:, at : at + size] for at, size in zip(places, sizes)]
    arrivals = []
    for shift in range(1, seq_count):
        pairs = [(s, (s + shift) % seq_count) for s in range(seq_count)]
        arrivals.append([lax.ppermute(part, "seq", pairs) for part in slices])

    sent = multiply(hidden, down_weight, 0, there, half, wide, tokens=slices, dtype=jnp.bfloat16)
    kept = multiply(hidden, down_weight, 0, here, half, wide, tokens=[sent], dtype=jnp.bfloat16)
    tokens, parts = scatter(sent, kept)
    results = []
    for arrived in arrivals:
        total = None
        for index, (at, size) in enumerate(zip(places, sizes)):
            if index == len(sizes) // 2:
                tokens, full = gather(parts)
                results.append(full)
            if index < len(sizes) - 1:
                total = multiply(
                    arrived[index], down_weight, at, whole, sub_count * half, wide_chunk, total=total, tokens=tokens
                )
                tokens = []
            else:
                last = functools.partial(multiply, arrived[index], down_weight, at, total=total, dtype=jnp.bfloat16)
                sent = last(there, half, wide_chunk, tokens=tokens)
                kept = last(here, half, wide_chunk, tokens=[sent])
        tokens, parts = scatter(sent, kept)
    results.append(gather(parts)[1])

    def of_sub(sub):
        return jnp.stack([(seq_at - (sub * per_sub + place)) % seq_count for place in range(per_sub)])

    other = swap(choose(results, of_sub(1 - sub_at)))
    return assemble(results, of_sub(sub_at), here, other, half)


def solution(mesh):
    return jax.shard_map(
        shards,
        mesh=mesh,
        in_specs=(P(("groups", "seq"), ("tensor", "sub")), P(("tensor", "sub"), "seq"), P("seq")),
        out_specs=(P(("groups", "sub"), "seq"), P(("groups", "sub"), "seq")),
        check_vma=False,
    )
```

time: 161 us -> 142 us (0.88)
  Pallas kernels: 0 us -> 63.7 us
  waiting for transfers between devices: 82.5 us -> 32.3 us
  matrix products: 48.7 us -> 0 us
  blocking collectives: 0 us -> 20 us
  between operations: 14 us -> 0.85 us
  starting transfers between devices: 5.27 us -> 17.6 us
  other arithmetic: 3.31 us -> 1.05 us
    pallas_call x0 -> x11, Pallas kernels: none -> 63.7 us  [the longest x7 58.9 us: multiply(): pl.pallas_call(functools.partial(multiply_body, total is not None), out_s...]
    dot_general x7 -> x0, matrix products: 48.7 us -> none  [the longest x4 27.4 us: shards(): jnp.dot(arrived, down_weight[part], preferred_element_type=jnp.float32)]
    all_gather x2 -> x0, waiting for transfers between devices: 42.3 us -> none  [finish(): full = lax.all_gather(packed, ('tensor', 'sub'), axis=0, tiled=True)]
    reduce_scatter x2 -> x0, waiting for transfers between devices: 40.1 us -> none  [finish(): lax.psum_scatter(partial_value.astype(jnp.bfloat16), ('tensor', 'sub'), s...]
    all_to_all x0 -> x3, waiting for transfers between devices: none -> 27.7 us  [the longest x2 27.7 us: gather(): lax.all_to_all(packed, 'tensor', split_axis=0, concat_axis=0, tiled=True)]
    all_to_all x0 -> x1, blocking collectives: none -> 20 us  [scatter(): lax.all_to_all(total.reshape(tensor_count, piece, half), 'tensor', split_...]
    all_to_all x0 -> x3, starting transfers between devices: none -> 11.8 us  [the longest x2 6.95 us: gather(): lax.all_to_all(packed, 'tensor', split_axis=0, concat_axis=0, tiled=True)]
    ppermute x4 -> x7, waiting for transfers between devices: 0.01 us -> 4.57 us  [the longest x4 2.64 us: shards(): arrivals.append([lax.ppermute(part, 'seq', pairs) for part in slices])]
  transfers between devices with their start and end apart: 8 -> 10, of which waited for: 4 -> 4; matrix products, arithmetic and copies ran while one was open for 31% -> 1% of each run, Pallas kernels for 0% -> 33%
where the time goes in v3:
time: 142 us; the launch traced here: 141 us
  Pallas kernels  63.7 us (45%)
  waiting for transfers between devices  32.3 us (23%)
  blocking collectives  20 us (14%)
  starting transfers between devices  17.6 us (12%)
  local copies, waits for them, and re-layouts  5.79 us (4%)
    pallas_call x7, Pallas kernels, multiply(): pl.pallas_call(functools.partial(multiply_body, total is not None), out_s...  58.9 us
    all_to_all x2, waiting for transfers between devices, gather(): lax.all_to_all(packed, 'tensor', split_axis=0, concat_axis=0, tiled=True)  27.7 us
    all_to_all x1, blocking collectives, scatter(): lax.all_to_all(total.reshape(tensor_count, piece, half), 'tensor', split_...  20 us
    all_to_all x2, starting transfers between devices, gather(): lax.all_to_all(packed, 'tensor', split_axis=0, concat_axis=0, tiled=True)  6.95 us
    ppermute x4, starting transfers between devices, shards(): arrivals.append([lax.ppermute(part, 'seq', pairs) for part in slices])  5.12 us
    all_to_all x1, starting transfers between devices, scatter(): lax.all_to_all(total.reshape(tensor_count, piece, half), 'tensor', split_...  4.87 us
    pallas_call x2, Pallas kernels, encode(): pl.pallas_call(encode_body, out_shape=jax.ShapeDtypeStruct((count, rows,...  3.67 us
    slice x3, local copies, waits for them, and re-layouts, shards(): slices = [hidden[:, at:at + size] for at, size in zip(places, sizes)]  2.9 us
  transfers between devices with their start and end apart: 10, of which 4 were waited for; matrix products, arithmetic and copies ran while one was open for 1% of the time, Pallas kernels for 33%

profile of v3, /device:TPU:0, one launch (start us, length us, event | category | flops | bytes accessed | tf_op | source)
XLA Modules:
  0.0 141.3 jit_solution(4408481196948117783)
XLA Ops:
  0.6 0.0 copy-start
  0.6 1.4 fusion.2
  2.0 0.4 copy-done
  2.4 0.8 slice.14.rest_2_
  3.2 0.7 slice.15.rest_3_
  3.9 12.1 %shard_map.68.rest_0_ = bf16[128,2048]{1,0:T(8,128)(2,1)S(1)} custom-call(s32[1]{0:T(128)S(6)} %sub.19.start_ref, bf16[128,6656]{1,0:T(8,128)(2,1)S(1)} %copy-done, bf16[6656,4096]{1,0:T(8,128)(2,1)} %w_ref.13, bf16[128,2048]{1,0:T(8,128)(2,1)S(1)} %get-tuple-element.5.rest_0_, bf16[128,2048]{1,0:T(8,128)(2,1)S(1)} %get-tuple-element.4.rest_1_, ...), custom_call_target="tpu_custom_call" | custom-call | flops 3489660928 | bytes 27262976 | tf_op jit(solution)/shard_map/pallas_call | solution.py:48
  16.0 0.5 collective-permute-start
  16.6 2.6 %collective-permute-start.4 = (bf16[128,2048]{1,0:T(8,128)(2,1)S(1)}, bf16[128,2048]{1,0:T(8,128)(2,1)}, u32[]{:S(2)}, u32[]{:S(2)}) collective-permute-start(bf16[128,2048]{1,0:T(8,128)(2,1)S(1)} %get-tuple-element.5.rest_0_), channel_id=1, source_target_pairs={{0,2},{2,0},{1,3},{3,1},{4,6},{6,4},{5,7},{7,5},{8,10},{10,8},{9,1... | collective-permute-start | bytes 1572872 | tf_op jit(solution)/shard_map/ppermute | solution.py:214
  19.1 12.1 %shard_map.69 = bf16[128,2048]{1,0:T(8,128)(2,1)S(1)} custom-call(s32[1]{0:T(128)} %bitcast.1.start_ref.here_ref, bf16[128,6656]{1,0:T(8,128)(2,1)S(1)} %copy-done, bf16[6656,4096]{1,0:T(8,128)(2,1)} %w_ref.13, bf16[128,2048]{1,0:T(8,128)(2,1)S(1)} %shard_map.68.rest_0_), custom_call_target="tpu_custom_call" | custom-call | flops 3489660928 | bytes 27262976 | tf_op jit(solution)/shard_map/pallas_call | solution.py:48
  31.3 0.0 copy-start.4
  31.3 0.0 collective-permute-done
  31.3 0.9 add_convert_fusion.1.rest_0_
  32.2 4.9 %all-to-all-start = ((bf16[4,32,2048]{2,1,0:T(8,128)(2,1)}), bf16[4,32,2048]{2,1,0:T(8,128)(2,1)S(1)}, u32[]{:S(2)}, u32[]{:S(2)}) async-start(bf16[4,32,2048]{2,1,0:T(8,128)(2,1)} %bitcast.3), calls=%async_computation | async-start | bytes 1048576 | tf_op jit(solution)/shard_map/all_to_all | solution.py:199
  37.1 0.5 collective-permute-start.3
  37.6 1.5 %collective-permute-start.2 = (bf16[128,1536]{1,0:T(8,128)(2,1)}, bf16[128,1536]{1,0:T(8,128)(2,1)}, u32[]{:S(2)}, u32[]{:S(2)}) collective-permute-start(bf16[128,1536]{1,0:T(8,128)(2,1)} %slice.14.rest_2_), channel_id=1, source_target_pairs={{0,2},{2,0},{1,3},{3,1},{4,6},{6,4},{5,7},{7,5},{8,10},{10,8},{9,1... | collective-permute-start | bytes 1179656 | tf_op jit(solution)/shard_map/ppermute | solution.py:214
  39.1 0.5 collective-permute-start.1
  39.6 0.0 copy-done.4
  39.7 0.0 collective-permute-done.4.x_ref
  39.7 9.6 %shard_map.71.rest_0_ = f32[128,4096]{1,0:T(8,128)S(1)} custom-call(s32[1]{0:T(128)} %constant.38.clone.1.start_ref, bf16[128,2048]{1,0:T(8,128)(2,1)} %collective-permute-done.4.x_ref, bf16[6656,4096]{1,0:T(8,128)(2,1)} %w_ref.13, bf16[128,2048]{1,0:T(8,128)(2,1)} %add_convert_fusion.1.rest_0_), custom_call_target="tpu_custom_call" | custom-call | flops 2147483648 | bytes 16777216 | tf_op jit(solution)/shard_map/pallas_call | solution.py:48
  49.3 2.6 %collective-permute-done.3.x_ref = bf16[128,2048]{1,0:T(8,128)(2,1)S(1)} collective-permute-done((bf16[128,2048]{1,0:T(8,128)(2,1)S(1)}, bf16[128,2048]{1,0:T(8,128)(2,1)S(1)}, u32[]{:S(2)}, u32[]{:S(2)}) %collective-permute-start.3) | collective-permute-done | bytes 524320 | tf_op jit(solution)/shard_map/ppermute | solution.py:214
  51.9 0.0 copy-start.1
  51.9 0.8 copy-done.1
  52.7 0.0 copy-start.2
  52.7 1.0 copy-done.2
  53.7 0.0 copy-start.3
  53.7 9.5 %shard_map.72.rest_0_ = f32[128,4096]{1,0:T(8,128)S(1)} custom-call(s32[1]{0:T(128)} %constant.38.clone.1.start_ref, bf16[128,2048]{1,0:T(8,128)(2,1)S(1)} %copy-done.2, bf16[6656,4096]{1,0:T(8,128)(2,1)} %w_ref.13, f32[128,4096]{1,0:T(8,128)S(1)} %shard_map.71.rest_0_), custom_call_target="tpu_custom_call" | custom-call | flops 2147483648 | bytes 16777216 | tf_op jit(solution)/shard_map/pallas_call | solution.py:48
  63.2 0.0 all-to-all-done.parts_ref
  63.2 0.0 copy-done.3
  63.2 1.8 %shard_map.70.rest_1_ = bf16[4,32,2176]{2,1,0:T(8,128)(2,1)} custom-call(bf16[4,32,2048]{2,1,0:T(8,128)(2,1)S(1)} %all-to-all-done.parts_ref, f32[1,2048]{1,0:T(1,128)S(1)} %bitcast.12, f32[128,128]{1,0:T(8,128)S(1)} %copy-done.3), custom_call_target="tpu_custom_call" | custom-call | flops 100663296 | bytes 1048576 | tf_op jit(solution)/shard_map/pallas_call | solution.py:94
  65.1 0.0 collective-permute-done.2.x_ref
  65.1 8.3 %shard_map.73.rest_0_ = f32[128,4096]{1,0:T(8,128)S(1)} custom-call(s32[1]{0:T(128)} %constant.38.clone.1.start_ref, bf16[128,1536]{1,0:T(8,128)(2,1)} %collective-permute-done.2.x_ref, bf16[6656,4096]{1,0:T(8,128)(2,1)} %w_ref.13, f32[128,4096]{1,0:T(8,128)S(1)} %shard_map.72.rest_0_, bf16[4,32,2176]{2,1,0:T(8,128)(2,1)} %shard_map.70.rest_1_), custom_call_target="tpu_custom_call" | custom-call | flops 1610612736 | bytes 12582912 | tf_op jit(solution)/shard_map/pallas_call | solution.py:48
  73.4 0.0 collective-permute-done.1.x_ref
  73.4 3.6 %shard_map.74.rest_1_ = bf16[128,2048]{1,0:T(8,128)(2,1)S(1)} custom-call(s32[1]{0:T(128)S(6)} %sub.19.start_ref, bf16[128,1024]{1,0:T(8,128)(2,1)S(1)} %collective-permute-done.1.x_ref, bf16[6656,4096]{1,0:T(8,128)(2,1)} %w_ref.13, f32[128,4096]{1,0:T(8,128)S(1)} %shard_map.73.rest_0_), custom_call_target="tpu_custom_call" | custom-call | flops 536870912 | bytes 4194304 | tf_op jit(solution)/shard_map/pallas_call | solution.py:48
  77.0 0.1 collective-permute-start.5
  77.1 3.6 %shard_map.75 = bf16[128,2048]{1,0:T(8,128)(2,1)S(1)} custom-call(s32[1]{0:T(128)} %bitcast.1.start_ref.here_ref, bf16[128,1024]{1,0:T(8,128)(2,1)S(1)} %collective-permute-done.1.x_ref, bf16[6656,4096]{1,0:T(8,128)(2,1)} %w_ref.13, f32[128,4096]{1,0:T(8,128)S(1)} %shard_map.73.rest_0_, bf16[128,2048]{1,0:T(8,128)(2,1)S(1)} %shard_map.74.rest_1_), custom_call_target="tpu_custom_call" | custom-call | flops 536870912 | bytes 4194304 | tf_op jit(solution)/shard_map/pallas_call | solution.py:48
  80.7 0.0 collective-permute-done.5
  80.7 0.1 add_convert_fusion
  80.9 20.0 %all_to_all.20.parts_ref = bf16[4,32,2048]{2,1,0:T(8,128)(2,1)S(1)} all-to-all(bf16[4,32,2048]{2,1,0:T(8,128)(2,1)S(1)} %bitcast.14), channel_id=1, replica_groups=mesh['groups'=2,'tensor'=4,'seq'=2,'sub'=2] {'tensor'}, dimensions={0} | all-to-all | bytes 1048576 | tf_op jit(solution)/shard_map/all_to_all | solution.py:199
  100.9 3.5 %all-to-all-start.1 = ((bf16[4,32,2176]{2,1,0:T(8,128)(2,1)}), bf16[4,32,2176]{2,1,0:T(8,128)(2,1)S(1)}, u32[]{:S(2)}, u32[]{:S(2)}) async-start(bf16[4,32,2176]{2,1,0:T(8,128)(2,1)} %shard_map.70.rest_1_), calls=%async_computation.1 | async-start | bytes 1114112 | tf_op jit(solution)/shard_map/all_to_all | solution.py:205
  104.4 1.8 %shard_map.76 = bf16[4,32,2176]{2,1,0:T(8,128)(2,1)} custom-call(bf16[4,32,2048]{2,1,0:T(8,128)(2,1)S(1)} %all_to_all.20.parts_ref, f32[1,2048]{1,0:T(1,128)S(1)} %bitcast.13, f32[128,128]{1,0:T(8,128)S(1)} %copy-done.3), custom_call_target="tpu_custom_call" | custom-call | flops 100663296 | bytes 1048576 | tf_op jit(solution)/shard_map/pallas_call | solution.py:94
  106.2 13.1 %all-to-all-done.1 = bf16[4,32,2176]{2,1,0:T(8,128)(2,1)S(1)} async-done(((bf16[4,32,2176]{2,1,0:T(8,128)(2,1)}), bf16[4,32,2176]{2,1,0:T(8,128)(2,1)S(1)}, u32[]{:S(2)}, u32[]{:S(2)}) %all-to-all-start.1) | async-done | bytes 557088 | tf_op jit(solution)/shard_map/all_to_all | solution.py:205
  119.3 3.5 %all-to-all-start.3 = ((bf16[4,32,2176]{2,1,0:T(8,128)(2,1)}), bf16[4,32,2176]{2,1,0:T(8,128)(2,1)S(1)}, u32[]{:S(2)}, u32[]{:S(2)}) async-start(bf16[4,32,2176]{2,1,0:T(8,128)(2,1)} %shard_map.76), calls=%async_computation.3 | async-start | bytes 1114112 | tf_op jit(solution)/shard_map/all_to_all | solution.py:205
  122.8 14.6 %all-to-all-done.3 = bf16[4,32,2176]{2,1,0:T(8,128)(2,1)S(1)} async-done(((bf16[4,32,2176]{2,1,0:T(8,128)(2,1)}), bf16[4,32,2176]{2,1,0:T(8,128)(2,1)S(1)}, u32[]{:S(2)}, u32[]{:S(2)}) %all-to-all-start.3) | async-done | bytes 557088 | tf_op jit(solution)/shard_map/all_to_all | solution.py:205
  137.5 0.1 collective-permute-start.6
  137.6 1.9 %collective-permute-done.6.other_ref = bf16[128,2176]{1,0:T(8,128)(2,1)S(1)} collective-permute-done((bf16[128,2176]{1,0:T(8,128)(2,1)S(1)}, bf16[128,2176]{1,0:T(8,128)(2,1)S(1)}, u32[]{:S(2)}, u32[]{:S(2)}) %collective-permute-start.6) | collective-permute-done | bytes 557088 | tf_op jit(solution)/shard_map/ppermute | solution.py:195
  139.5 1.1 shard_map.78
  140.6 0.7 copy.7
  (2 shorter events, 0.0 us)
Async XLA Ops:
  0.6 1.8 %copy-start = (bf16[128,6656]{1,0:T(8,128)(2,1)S(1)}, bf16[128,6656]{1,0:T(8,128)(2,1)}, u32[]{:S(2)}) copy-start(bf16[128,6656]{1,0:T(8,128)(2,1)} %x_ref.3) | copy-start | bytes 5111812
  16.0 15.2 %collective-permute-start = (bf16[128,2048]{1,0:T(8,128)(2,1)S(1)}, bf16[128,2048]{1,0:T(8,128)(2,1)S(1)}, u32[]{:S(2)}, u32[]{:S(2)}) collective-permute-start(bf16[128,2048]{1,0:T(8,128)(2,1)S(1)} %shard_map.68.rest_0_), channel_id=1, source_target_pairs={{0,1},{1,0},{2,3},{3,2},{4,5},{5,4},{6,7},{7,6},{8,9},{9,8},{10,11... | collective-permute-start | bytes 1572872 | tf_op jit(solution)/shard_map/ppermute | solution.py:195
  16.6 23.1 %collective-permute-start.4 = (bf16[128,2048]{1,0:T(8,128)(2,1)S(1)}, bf16[128,2048]{1,0:T(8,128)(2,1)}, u32[]{:S(2)}, u32[]{:S(2)}) collective-permute-start(bf16[128,2048]{1,0:T(8,128)(2,1)S(1)} %get-tuple-element.5.rest_0_), channel_id=1, source_target_pairs={{0,2},{2,0},{1,3},{3,1},{4,6},{6,4},{5,7},{7,5},{8,10},{10,8},{9,1... | collective-permute-start | bytes 1572872 | tf_op jit(solution)/shard_map/ppermute | solution.py:214
  31.3 8.4 %copy-start.4 = (s32[4096]{0:T(1024)S(1)}, s32[4096]{0:T(1024)}, u32[]{:S(2)}) copy-start(s32[4096]{0:T(1024)} %param.7) | copy-start | bytes 49156
  32.2 31.0 %all-to-all-start = ((bf16[4,32,2048]{2,1,0:T(8,128)(2,1)}), bf16[4,32,2048]{2,1,0:T(8,128)(2,1)S(1)}, u32[]{:S(2)}, u32[]{:S(2)}) async-start(bf16[4,32,2048]{2,1,0:T(8,128)(2,1)} %bitcast.3), calls=%async_computation | async-start | bytes 1048576 | tf_op jit(solution)/shard_map/all_to_all | solution.py:199
  37.1 14.8 %collective-permute-start.3 = (bf16[128,2048]{1,0:T(8,128)(2,1)S(1)}, bf16[128,2048]{1,0:T(8,128)(2,1)S(1)}, u32[]{:S(2)}, u32[]{:S(2)}) collective-permute-start(bf16[128,2048]{1,0:T(8,128)(2,1)S(1)} %get-tuple-element.4.rest_1_), channel_id=1, source_target_pairs={{0,2},{2,0},{1,3},{3,1},{4,6},{6,4},{5,7},{7,5},{8,10},{10,8},{9,1... | collective-permute-start | bytes 1572872 | tf_op jit(solution)/shard_map/ppermute | solution.py:214
  37.6 27.4 %collective-permute-start.2 = (bf16[128,1536]{1,0:T(8,128)(2,1)}, bf16[128,1536]{1,0:T(8,128)(2,1)}, u32[]{:S(2)}, u32[]{:S(2)}) collective-permute-start(bf16[128,1536]{1,0:T(8,128)(2,1)} %slice.14.rest_2_), channel_id=1, source_target_pairs={{0,2},{2,0},{1,3},{3,1},{4,6},{6,4},{5,7},{7,5},{8,10},{10,8},{9,1... | collective-permute-start | bytes 1179656 | tf_op jit(solution)/shard_map/ppermute | solution.py:214
  39.1 34.2 %collective-permute-start.1 = (bf16[128,1024]{1,0:T(8,128)(2,1)}, bf16[128,1024]{1,0:T(8,128)(2,1)S(1)}, u32[]{:S(2)}, u32[]{:S(2)}) collective-permute-start(bf16[128,1024]{1,0:T(8,128)(2,1)} %slice.15.rest_3_), channel_id=1, source_target_pairs={{0,2},{2,0},{1,3},{3,1},{4,6},{6,4},{5,7},{7,5},{8,10},{10,8},{9,1... | collective-permute-start | bytes 786440 | tf_op jit(solution)/shard_map/ppermute | solution.py:214
  51.9 0.8 copy-start.1
  52.7 1.0 copy-start.2
  53.7 9.5 %copy-start.3 = (f32[128,128]{1,0:T(8,128)S(1)}, f32[128,128]{1,0:T(8,128)}, u32[]{:S(2)}) copy-start(f32[128,128]{1,0:T(8,128)} %constant.39.clone.rotation_ref) | copy-start | bytes 196612
  77.0 3.7 %collective-permute-start.5 = (bf16[128,2048]{1,0:T(8,128)(2,1)S(1)}, bf16[128,2048]{1,0:T(8,128)(2,1)S(1)}, u32[]{:S(2)}, u32[]{:S(2)}) collective-permute-start(bf16[128,2048]{1,0:T(8,128)(2,1)S(1)} %shard_map.74.rest_1_), channel_id=1, source_target_pairs={{0,1},{1,0},{2,3},{3,2},{4,5},{5,4},{6,7},{7,6},{8,9},{9,8},{10,11... | collective-permute-start | bytes 1572872 | tf_op jit(solution)/shard_map/ppermute | solution.py:195
  100.9 18.4 %all-to-all-start.1 = ((bf16[4,32,2176]{2,1,0:T(8,128)(2,1)}), bf16[4,32,2176]{2,1,0:T(8,128)(2,1)S(1)}, u32[]{:S(2)}, u32[]{:S(2)}) async-start(bf16[4,32,2176]{2,1,0:T(8,128)(2,1)} %shard_map.70.rest_1_), calls=%async_computation.1 | async-start | bytes 1114112 | tf_op jit(solution)/shard_map/all_to_all | solution.py:205
  119.3 18.1 %all-to-all-start.3 = ((bf16[4,32,2176]{2,1,0:T(8,128)(2,1)}), bf16[4,32,2176]{2,1,0:T(8,128)(2,1)S(1)}, u32[]{:S(2)}, u32[]{:S(2)}) async-start(bf16[4,32,2176]{2,1,0:T(8,128)(2,1)} %shard_map.76), calls=%async_computation.3 | async-start | bytes 1114112 | tf_op jit(solution)/shard_map/all_to_all | solution.py:205
  137.5 2.0 %collective-permute-start.6 = (bf16[128,2176]{1,0:T(8,128)(2,1)S(1)}, bf16[128,2176]{1,0:T(8,128)(2,1)S(1)}, u32[]{:S(2)}, u32[]{:S(2)}) collective-permute-start(bf16[128,2176]{1,0:T(8,128)(2,1)S(1)} %shard_map.77), channel_id=1, source_target_pairs={{0,1},{1,0},{2,3},{3,2},{4,5},{5,4},{6,7},{7,6},{8,9},{9,8},{10,11... | collective-permute-start | bytes 1671176 | tf_op jit(solution)/shard_map/ppermute | solution.py:195

commit v4 on v2

v4 whole, which is shorter than its diff:
```python
import functools
import math

import jax
import jax.numpy as jnp
import numpy as np
from jax import lax
from jax.experimental import pallas as pl
from jax.experimental.pallas import tpu as pltpu
from jax.sharding import PartitionSpec as P

BLOCK = 128
UNIT = 512
GROUPS = 2
BUFFERS = 4
VMEM_LIMIT = 40 * 2**20
epsilon = 1e-06

SMALL = pl.CostEstimate(flops=1, bytes_accessed=1, transcendentals=0)
PARAMS = pltpu.CompilerParams(vmem_limit_bytes=VMEM_LIMIT)
VMEM = pl.BlockSpec(memory_space=pltpu.VMEM)
SMEM = pl.BlockSpec(memory_space=pltpu.SMEM)
ANY = pl.BlockSpec(memory_space=pl.ANY)


def hadamard(order):
    indices = np.arange(order)
    parity = np.zeros((order, order), np.int64)
    for position in range(order.bit_length() - 1):
        parity = parity + (indices[:, None] >> position & 1) * (indices[None, :] >> position & 1)
    return ((1 - 2 * (parity % 2)) / math.sqrt(order)).astype(np.float32)


def slice_body(places, in_ref, *out_refs):
    for (at, size), out_ref in zip(places, out_refs):
        out_ref[...] = in_ref[:, at : at + size]


def slices_of(values, places):
    return pl.pallas_call(
        functools.partial(slice_body, places),
        out_shape=[jax.ShapeDtypeStruct((values.shape[0], size), values.dtype) for _, size in places],
        in_specs=[VMEM],
        out_specs=[VMEM] * len(places),
        compiler_params=PARAMS,
        cost_estimate=SMALL,
    )(values)


def multiply_body(offsets, has_totals, splits, row, first, number, here_ref, *refs):
    lefts = len(offsets)
    left_refs, refs = refs[:lefts], refs[lefts:]
    w_ref, refs = refs[0], refs[1:]
    total_refs, refs = list(refs[: sum(has_totals)]), refs[sum(has_totals) :]
    buffer, arrived = refs[-2:]
    out_count = sum(2 if split else 1 for split in splits)
    out_refs = refs[-2 - out_count : -2]
    buffers, depth, wide = buffer.shape
    rows = left_refs[0].shape[0]
    in_half = w_ref.shape[1] // wide // 2
    steps = 2 * first if any(splits) else 2 * in_half

    def column(n):
        if not any(splits):
            return n
        side = jnp.where(n < first, 1 - here_ref[0], here_ref[0])
        return side * in_half + number * first + n - jnp.where(n < first, 0, first)

    def at(block):
        return pl.ds(pl.multiple_of(block * wide, wide), wide)

    def copy(n):
        slot = lax.rem(n, buffers)
        return pltpu.make_async_copy(
            w_ref.at[pl.ds(row, depth), at(column(n))], buffer.at[slot], arrived.at[slot]
        )

    def step(n, second):
        copy(n).wait()

        @pl.when(n + buffers - 1 < steps)
        def _():
            copy(n + buffers - 1).start()

        parts = [ref[:, offset : offset + depth] for ref, offset in zip(left_refs, offsets)]
        left = parts[0] if lefts == 1 else jnp.concatenate(parts, axis=0)
        product = jnp.dot(left, buffer[lax.rem(n, buffers)], preferred_element_type=jnp.float32)
        totals, outs = list(total_refs), list(out_refs)
        for index in range(lefts):
            value = product[index * rows : (index + 1) * rows]
            if has_totals[index]:
                value = value + totals.pop(0)[:, at(column(n))]
            if splits[index]:
                sent_ref, kept_ref = outs.pop(0), outs.pop(0)
                if second:
                    kept_ref[:, at(n - first)] = value
                else:
                    sent_ref[:, at(n)] = value.astype(sent_ref.dtype)
            else:
                outs.pop(0)[:, at(column(n))] = value

    for n in range(min(buffers - 1, steps)):
        copy(jnp.int32(n)).start()
    pl.loop(0, first)(functools.partial(step, second=False))
    pl.loop(first, steps)(functools.partial(step, second=True))


def multiply(lefts, weight, row, depth, here, totals, splits, wide, group=None, tokens=()):
    rows = lefts[0][0].shape[0]
    columns = weight.shape[1]
    number, count = group or (0, 1)
    first = columns // wide // 2 // count
    held = [total for total in totals if total is not None]
    out_shape = []
    for split in splits:
        if split:
            out_shape += [
                jax.ShapeDtypeStruct((rows, first * wide), jnp.bfloat16),
                jax.ShapeDtypeStruct((rows, first * wide), jnp.float32),
            ]
        else:
            out_shape.append(jax.ShapeDtypeStruct((rows, columns), jnp.float32))
    body = functools.partial(
        multiply_body,
        [offset for _, offset in lefts],
        [total is not None for total in totals],
        splits,
        row,
        first,
        number,
    )
    return pl.pallas_call(
        body,
        out_shape=out_shape,
        in_specs=[SMEM]
        + [VMEM] * len(lefts)
        + [ANY]
        + [VMEM] * len(held)
        + [ANY] * len(tokens),
        out_specs=[VMEM] * len(out_shape),
        scratch_shapes=[
            pltpu.VMEM((BUFFERS, depth, wide), weight.dtype),
            pltpu.SemaphoreType.DMA((BUFFERS,)),
        ],
        compiler_params=PARAMS,
        cost_estimate=SMALL,
    )(here, *[left for left, _ in lefts], weight, *held, *tokens)


def halve_body(bit_ref, kept_ref, came_ref, sent_out, kept_out):
    half = sent_out.shape[0]

    def put(bit):
        mine, other = slice(bit * half, (bit + 1) * half), slice((1 - bit) * half, (2 - bit) * half)
        kept_out[...] = kept_ref[mine] + came_ref[mine].astype(jnp.float32)
        sent_out[...] = (kept_ref[other] + came_ref[other].astype(jnp.float32)).astype(jnp.bfloat16)

    for bit in range(2):
        pl.when(bit_ref[0] == bit)(functools.partial(put, bit))


def halve(kept, came, bit):
    rows, columns = kept.shape
    half = rows // 2
    if half % 16:
        total = kept + came.astype(jnp.float32)
        sent = lax.dynamic_slice_in_dim(total, (1 - bit) * half, half, 0).astype(jnp.bfloat16)
        return sent, lax.dynamic_slice_in_dim(total, bit * half, half, 0)
    return pl.pallas_call(
        halve_body,
        out_shape=[
            jax.ShapeDtypeStruct((half, columns), jnp.bfloat16),
            jax.ShapeDtypeStruct((half, columns), jnp.float32),
        ],
        in_specs=[SMEM, VMEM, VMEM],
        out_specs=[VMEM, VMEM],
        compiler_params=PARAMS,
        cost_estimate=SMALL,
    )(jnp.reshape(bit, (1,)), kept, came)


def encode_body(kept_ref, came_ref, flips_ref, rotation_ref, out_ref):
    rows, columns = kept_ref.shape
    rotation = rotation_ref[...]
    lane = lax.broadcasted_iota(jnp.int32, (rows, BLOCK), 1)
    scales = jnp.zeros((rows, BLOCK), jnp.float32)
    for block in range(columns // BLOCK):
        at = slice(block * BLOCK, (block + 1) * BLOCK)
        total = (kept_ref[:, at] + came_ref[:, at].astype(jnp.float32)) * flips_ref[:, at]
        rotated = jnp.dot(
            total, rotation, precision=lax.Precision.HIGHEST, preferred_element_type=jnp.float32
        )
        largest = jnp.max(jnp.abs(rotated), axis=1, keepdims=True)
        scale = (largest + epsilon).astype(jnp.bfloat16).astype(jnp.float32)
        out_ref[:, at] = (rotated / scale).astype(jnp.bfloat16)
        scales = jnp.where(lane == block, scale, scales)
    out_ref[:, columns:] = scales.astype(jnp.bfloat16)


def encode(kept, came, flips):
    rows, columns = kept.shape
    return pl.pallas_call(
        encode_body,
        out_shape=jax.ShapeDtypeStruct((rows, columns + BLOCK), jnp.bfloat16),
        in_specs=[VMEM] * 4,
        out_specs=VMEM,
        compiler_params=PARAMS,
        cost_estimate=SMALL,
    )(kept, came, flips, hadamard(BLOCK))


def choose_body(blocks, pieces, width, at, rank_ref, chosen_ref, *refs):
    out_ref = refs[-1]
    rows = refs[0].shape[0]
    scales = width // BLOCK

    def put(block, place):
        begin, scale_at = at[block]
        for piece in range(pieces):
            ref = refs[block * pieces + piece]
            row = (place * pieces + rank_ref[piece]) * rows
            here = pl.ds(pl.multiple_of(row, rows), rows)
            out_ref[here, :width] = ref[:, begin : begin + width]
            out_ref[here, width : width + scales] = ref[:, scale_at : scale_at + scales]

    for place in range(chosen_ref.shape[0]):
        for block in range(blocks):
            pl.when(chosen_ref[place] == block)(functools.partial(put, block, place))


def choose(results, group, width, rank, chosen):
    picked, at = [], []
    for result in results:
        if len(result) == 1:
            pieces, begin = result[0], group * width
            at.append((begin, pieces[0].shape[1] - BLOCK + begin // BLOCK))
        else:
            pieces = result[group]
            at.append((0, width))
        picked.append(pieces)
    rows = picked[0][0].shape[0]
    count = len(picked[0])
    if rows % 16:
        blocks = []
        for pieces, (begin, scale_at) in zip(picked, at):
            block = jnp.zeros((count * rows, width + BLOCK), jnp.bfloat16)
            for index, piece in enumerate(pieces):
                scale = jnp.pad(piece[:, scale_at : scale_at + width // BLOCK], ((0, 0), (0, BLOCK - width // BLOCK)))
                part = jnp.concatenate([piece[:, begin : begin + width], scale], axis=1)
                block = lax.dynamic_update_slice_in_dim(block, part, rank[index] * rows, 0)
            blocks.append(block)
        stacked = jnp.stack(blocks)
        return jnp.concatenate([stacked[chosen[place]] for place in range(chosen.shape[0])])
    return pl.pallas_call(
        functools.partial(choose_body, len(picked), count, width, at),
        out_shape=jax.ShapeDtypeStruct((chosen.shape[0] * count * rows, width + BLOCK), jnp.bfloat16),
        in_specs=[SMEM, SMEM] + [VMEM] * (len(picked) * count),
        out_specs=VMEM,
        compiler_params=PARAMS,
        cost_estimate=SMALL,
    )(rank, chosen, *[piece for pieces in picked for piece in pieces])


def assemble_body(groups, half, here_ref, *refs):
    mine, other = refs[:groups], refs[groups : 2 * groups]
    codes_ref, scales_ref = refs[2 * groups :]
    width = half // groups
    scales = width // BLOCK

    def put(core):
        held = []
        for side, side_refs in ((core, mine), (1 - core, other)):
            for group, ref in enumerate(side_refs):
                begin = side * half + group * width
                codes_ref[:, begin : begin + width] = ref[:, :width]
                held.append((begin, ref[:, width : width + scales].astype(jnp.float32)))
        held = jnp.concatenate([value for _, value in sorted(held, key=lambda pair: pair[0])], axis=1)
        scales_ref[...] = held.T.astype(jnp.bfloat16)

    for core in range(2):
        pl.when(here_ref[0] == core)(functools.partial(put, core))


def assemble(mine, other, here, half):
    rows = mine[0].shape[0]
    codes, scales = pl.pallas_call(
        functools.partial(assemble_body, len(mine), half),
        out_shape=(
            jax.ShapeDtypeStruct((rows, 2 * half), jnp.bfloat16),
            jax.ShapeDtypeStruct((2 * half // BLOCK, rows), jnp.bfloat16),
        ),
        in_specs=[SMEM] + [VMEM] * (2 * len(mine)),
        out_specs=(VMEM, VMEM),
        compiler_params=PARAMS,
        cost_estimate=SMALL,
    )(here, *mine, *other)
    return codes, scales.T


def cut(depth):
    if depth % UNIT or depth < 8 * UNIT:
        return [depth]
    units = depth // UNIT
    sizes = []
    for share in (0.31, 0.31, 0.23):
        sizes.append(max(1, round(units * share)))
    sizes.append(units - sum(sizes))
    return [size * UNIT for size in sizes]


def shards(hidden, down_weight, sign_bits):
    tensor_count = lax.axis_size("tensor")
    seq_count = lax.axis_size("seq")
    sub_count = lax.axis_size("sub")
    tensor_at = lax.axis_index("tensor")
    seq_at = lax.axis_index("seq")
    sub_at = lax.axis_index("sub")
    rows, depth = hidden.shape
    half = down_weight.shape[1] // sub_count
    per_sub = seq_count // sub_count
    levels = tensor_count.bit_length() - 1
    bits = [tensor_at >> level & 1 for level in range(levels)]
    wide, wide_chunk = min(256, half // GROUPS), min(512, half // GROUPS)
    flips = (2 * sign_bits - 1).astype(jnp.float32)[None, :]
    own_flips = lax.dynamic_slice_in_dim(flips, sub_at * half, half, 1)
    here = jnp.reshape(sub_at, (1,)).astype(jnp.int32)

    def swap(values):
        return lax.ppermute(values, "sub", [(0, 1), (1, 0)])

    def exchange(values, level):
        return lax.ppermute(values, "tensor", [(t, t ^ 1 << level) for t in range(tensor_count)])

    def reduce(sent, kept, begin):
        came = swap(sent)
        tokens = []
        for level in range(levels):
            sent, kept = halve(kept, came, bits[level])
            tokens.append(sent)
            came = exchange(sent, level)
        packed = encode(kept, came, own_flips[:, begin : begin + kept.shape[1]])
        return tokens, packed

    def spread(packed):
        pieces = {0: packed}
        for level in reversed(range(levels)):
            for index in list(pieces):
                pieces[index ^ 1 << level] = exchange(pieces[index], level)
        return [pieces[index] for index in range(tensor_count)]

    def rank_of(index):
        return sum((index >> level & 1) << (levels - 1 - level) for level in range(levels))

    sizes = cut(depth)
    places = [(sum(sizes[:index]), size) for index, size in enumerate(sizes)]
    parts = slices_of(hidden, places)
    arrivals = []
    for shift in range(1, seq_count):
        pairs = [(s, (s + shift) % seq_count) for s in range(seq_count)]
        arrivals.append([lax.ppermute(part, "seq", pairs) for part in parts])

    single = len(sizes) == 1
    own = None
    if not single:
        rest = sizes[0]
        (own,) = multiply(
            [(hidden, rest)], down_weight, rest, depth - rest, here, [None], [False], wide, tokens=parts
        )
    outs = multiply(
        [(hidden, 0), (arrivals[0][0], 0)], down_weight, 0, sizes[0], here, [own, None], [True, single], wide_chunk
    )
    (sent, kept), first = outs[:2], outs[2:]
    own_tokens, own_packed = reduce(sent, kept, 0)
    results = [[spread(own_packed)]]
    for shift, arrived in enumerate(arrivals):
        groups = 1 if single else GROUPS
        reduced = []
        if single:
            if shift:
                first = multiply([(arrived[0], 0)], down_weight, 0, depth, here, [None], [True], wide_chunk)
            reduced.append(reduce(*first, 0)[1])
        else:
            total = first[0] if shift == 0 else None
            for index, (at, size) in enumerate(places):
                if index == 0 and shift == 0:
                    continue
                if index == len(places) - 1:
                    break
                tokens = own_tokens[index - 1 : index] if shift == 0 else ()
                (total,) = multiply(
                    [(arrived[index], 0)], down_weight, at, size, here, [total], [False], wide_chunk, tokens=tokens
                )
            tokens = [own_packed] if shift == 0 else ()
            for group in range(groups):
                sent, kept = multiply(
                    [(arrived[index], 0)], down_weight, at, size, here, [total], [True], wide_chunk,
                    group=(group, groups), tokens=tokens,
                )
                tokens = [sent]
                reduced.append(reduce(sent, kept, group * half // groups)[1])
        results.append([spread(packed) for packed in reduced])

    def of_sub(sub):
        return jnp.stack([(seq_at - (sub * per_sub + place)) % seq_count for place in range(per_sub)])

    rank = jnp.stack([rank_of(tensor_at ^ index) for index in range(tensor_count)])
    groups = max(len(result) for result in results)
    width = half // groups
    other = [swap(choose(results, group, width, rank, of_sub(1 - sub_at))) for group in range(groups)]
    mine = [choose(results, group, width, rank, of_sub(sub_at)) for group in range(groups)]
    return assemble(mine, other, here, half)


def solution(mesh):
    return jax.shard_map(
        shards,
        mesh=mesh,
        in_specs=(P(("groups", "seq"), ("tensor", "sub")), P(("tensor", "sub"), "seq"), P("seq")),
        out_specs=(P(("groups", "sub"), "seq"), P(("groups", "sub"), "seq")),
        check_vma=False,
    )
```

time: 161 us -> 109 us (0.68)
  waiting for transfers between devices: 82.5 us -> 26.3 us
  Pallas kernels: 0 us -> 49.6 us
  matrix products: 48.7 us -> 0 us
  starting transfers between devices: 5.27 us -> 23.7 us
  between operations: 14 us -> 0.95 us
  other arithmetic: 3.31 us -> 0.08 us
  local copies, waits for them, and re-layouts: 6.5 us -> 8.14 us
    pallas_call x0 -> x21, Pallas kernels: none -> 49.6 us  [the longest x6 40 us: multiply(): pl.pallas_call(body, out_shape=out_shape, in_specs=[SMEM] + [VMEM] * len(...]
    dot_general x7 -> x0, matrix products: 48.7 us -> none  [the longest x4 27.4 us: shards(): jnp.dot(arrived, down_weight[part], preferred_element_type=jnp.float32)]
    all_gather x2 -> x0, waiting for transfers between devices: 42.3 us -> none  [finish(): full = lax.all_gather(packed, ('tensor', 'sub'), axis=0, tiled=True)]
    reduce_scatter x2 -> x0, waiting for transfers between devices: 40.1 us -> none  [finish(): lax.psum_scatter(partial_value.astype(jnp.bfloat16), ('tensor', 'sub'), s...]
    ppermute x4 -> x24, waiting for transfers between devices: 0.01 us -> 26.3 us  [the longest x15 23.8 us: exchange(): lax.ppermute(values, 'tensor', [(t, t ^ 1 << level) for t in range(tensor...]
    ppermute x4 -> x24, starting transfers between devices: 5.11 us -> 23.7 us  [the longest x15 16.9 us: exchange(): lax.ppermute(values, 'tensor', [(t, t ^ 1 << level) for t in range(tensor...]
    unnamed x10 -> x26, local copies, waits for them, and re-layouts: 0.23 us -> 8.14 us
    another operation x7 -> x0, local copies, waits for them, and re-layouts: 3.15 us -> none  [the longest x6 3.15 us: shards(): stacked = jnp.stack([result[at] for result in results])]
  transfers between devices with their start and end apart: 8 -> 24, of which waited for: 4 -> 11; matrix products, arithmetic and copies ran while one was open for 31% -> 0% of each run, Pallas kernels for 0% -> 31%
where the time goes in v4:
time: 109 us
  Pallas kernels  49.6 us (46%)
  waiting for transfers between devices  26.3 us (24%)
  starting transfers between devices  23.7 us (22%)
  local copies, waits for them, and re-layouts  8.14 us (7%)
    pallas_call x6, Pallas kernels, multiply(): pl.pallas_call(body, out_shape=out_shape, in_specs=[SMEM] + [VMEM] * len(...  40 us
    ppermute x15, waiting for transfers between devices, exchange(): lax.ppermute(values, 'tensor', [(t, t ^ 1 << level) for t in range(tensor...  23.8 us
    ppermute x15, starting transfers between devices, exchange(): lax.ppermute(values, 'tensor', [(t, t ^ 1 << level) for t in range(tensor...  16.9 us
    unnamed x26, local copies, waits for them, and re-layouts  8.14 us
    ppermute x4, starting transfers between devices, shards(): arrivals.append([lax.ppermute(part, 'seq', pairs) for part in parts])  5.79 us
    pallas_call x3, Pallas kernels, encode(): pl.pallas_call(encode_body, out_shape=jax.ShapeDtypeStruct((rows, columns...  3.15 us
    ppermute x5, waiting for transfers between devices, swap(): return lax.ppermute(values, 'sub', [(0, 1), (1, 0)])  2.46 us
    pallas_call x4, Pallas kernels, choose(): pl.pallas_call(functools.partial(choose_body, len(picked), count, width,...  2.38 us
  transfers between devices with their start and end apart: 24, of which 11 were waited for; matrix products, arithmetic and copies ran while one was open for 0% of the time, Pallas kernels for 31%

profile of v4, /device:TPU:0, one launch (start us, length us, event | category | flops | bytes accessed | tf_op | source)
XLA Modules:
  0.0 108.8 jit_solution(1831683218079557066)
XLA Ops:
  0.6 1.4 %copy-done = bf16[128,6656]{1,0:T(8,128)(2,1)S(1)} copy-done((bf16[128,6656]{1,0:T(8,128)(2,1)S(1)}, bf16[128,6656]{1,0:T(8,128)(2,1)}, u32[]{:S(2)}) %copy-start) | copy-done | bytes 1703960
  2.1 0.9 shard_map.77
  3.0 2.9 %collective-permute-start = (bf16[128,2048]{1,0:T(8,128)(2,1)S(1)}, bf16[128,2048]{1,0:T(8,128)(2,1)S(1)}, u32[]{:S(2)}, u32[]{:S(2)}) collective-permute-start(bf16[128,2048]{1,0:T(8,128)(2,1)S(1)} %get-tuple-element.27.refs_2_), channel_id=1, source_target_pairs={{0,2},{2,0},{1,3},{3,1},{4,6},{6,4},{5,7},{7,5},{8,10},{10,8},{9,1... | collective-permute-start | bytes 1572872 | tf_op jit(solution)/shard_map/ppermute | solution.py:360
  5.9 12.8 %shard_map.78.refs_3_ = f32[128,4096]{1,0:T(8,128)S(1)} custom-call(s32[1]{0:T(128)} %bitcast.here_ref, bf16[128,6656]{1,0:T(8,128)(2,1)S(1)} %copy-done.1, bf16[6656,4096]{1,0:T(8,128)(2,1)} %refs_1_.9, bf16[128,2048]{1,0:T(8,128)(2,1)S(1)} %get-tuple-element.27.refs_2_, bf16[128,2048]{1,0:T(8,128)(2,1)} %get-tuple-element.28.refs_3_, ...), custom_call_target="tpu_custom_call" | custom-call | flops 1 | bytes 1 | tf_op jit(solution)/shard_map/pallas_call | solution.py:132
  18.8 0.8 copy-done.5
  19.6 1.0 copy-done.6
  20.6 7.9 %shard_map.79 = (bf16[128,2048]{1,0:T(8,128)(2,1)}, f32[128,2048]{1,0:T(8,128)S(1)}, f32[128,4096]{1,0:T(8,128)S(1)}) custom-call(s32[1]{0:T(128)} %bitcast.here_ref, bf16[128,6656]{1,0:T(8,128)(2,1)S(1)} %copy-done.1, bf16[128,2048]{1,0:T(8,128)(2,1)S(1)} %copy-done.6, bf16[6656,4096]{1,0:T(8,128)(2,1)} %refs_1_.9, f32[128,4096]{1,0:T(8,128)S(1)} %shard_map.78.refs_3_), custom_call_target="tpu_custom_call" | custom-call | flops 1 | bytes 1 | tf_op jit(solution)/shard_map/pallas_call | solution.py:132
  28.6 1.3 %copy-done.2 = f32[128,4096]{1,0:T(8,128)} copy-done((f32[128,4096]{1,0:T(8,128)}, f32[128,4096]{1,0:T(8,128)S(1)}, u32[]{:S(2)}) %copy-start.2) | copy-done | bytes 2097176
  29.9 0.8 collective-permute-start.9
  30.7 1.4 %collective-permute-done.1.came_ref = bf16[128,2048]{1,0:T(8,128)(2,1)} collective-permute-done((bf16[128,2048]{1,0:T(8,128)(2,1)}, bf16[128,2048]{1,0:T(8,128)(2,1)}, u32[]{:S(2)}, u32[]{:S(2)}) %collective-permute-start.1) | collective-permute-done | bytes 524320 | tf_op jit(solution)/shard_map/ppermute | solution.py:329
  32.2 1.8 %shard_map.80 = (bf16[64,2048]{1,0:T(8,128)(2,1)}, f32[64,2048]{1,0:T(8,128)S(1)}) custom-call(s32[1]{0:T(128)} %bitcast.7.bit_ref, f32[128,2048]{1,0:T(8,128)S(1)} %get-tuple-element.31.kept_ref, bf16[128,2048]{1,0:T(8,128)(2,1)} %collective-permute-done.1.came_ref), custom_call_target="tpu_custom_call" | custom-call | flops 1 | bytes 1 | tf_op jit(solution)/shard_map/pallas_call | solution.py:169
  34.0 0.8 copy-done.7
  34.8 1.6 %collective-permute-start.2 = (bf16[64,2048]{1,0:T(8,128)(2,1)}, bf16[64,2048]{1,0:T(8,128)(2,1)S(1)}, u32[]{:S(2)}, u32[]{:S(2)}) collective-permute-start(bf16[64,2048]{1,0:T(8,128)(2,1)} %get-tuple-element.34.refs_3_), channel_id=1, source_target_pairs={{0,4},{4,0},{8,12},{12,8},{1,5},{5,1},{9,13},{13,9},{2,6},{6,2},{1... | collective-permute-start | bytes 786440 | tf_op jit(solution)/shard_map/ppermute | solution.py:332
  36.4 0.8 collective-permute-start.8
  37.2 1.2 %collective-permute-start.7 = (bf16[128,1024]{1,0:T(8,128)(2,1)}, bf16[128,1024]{1,0:T(8,128)(2,1)S(1)}, u32[]{:S(2)}, u32[]{:S(2)}) collective-permute-start(bf16[128,1024]{1,0:T(8,128)(2,1)} %copy-done.9), channel_id=1, source_target_pairs={{0,2},{2,0},{1,3},{3,1},{4,6},{6,4},{5,7},{7,5},{8,10},{10,8},{9,1... | collective-permute-start | bytes 786440 | tf_op jit(solution)/shard_map/ppermute | solution.py:360
  38.4 5.0 %collective-permute-done.2.came_ref = bf16[64,2048]{1,0:T(8,128)(2,1)S(1)} collective-permute-done((bf16[64,2048]{1,0:T(8,128)(2,1)}, bf16[64,2048]{1,0:T(8,128)(2,1)S(1)}, u32[]{:S(2)}, u32[]{:S(2)}) %collective-permute-start.2) | collective-permute-done | bytes 262176 | tf_op jit(solution)/shard_map/ppermute | solution.py:332
  43.3 0.7 copy-done.10
  44.1 1.0 copy-done.8
  45.1 0.9 copy-done.11
  46.1 2.6 %collective-permute-start.3 = (bf16[32,2048]{1,0:T(8,128)(2,1)S(1)}, bf16[32,2048]{1,0:T(8,128)(2,1)}, u32[]{:S(2)}, u32[]{:S(2)}) collective-permute-start(bf16[32,2048]{1,0:T(8,128)(2,1)S(1)} %get-tuple-element.36.refs_3_), channel_id=1, source_target_pairs={{0,8},{4,12},{8,0},{12,4},{1,9},{5,13},{9,1},{13,5},{2,10},{6,14},... | collective-permute-start | bytes 393224 | tf_op jit(solution)/shard_map/ppermute | solution.py:332
  48.8 7.7 %shard_map.83.refs_2_ = f32[128,4096]{1,0:T(8,128)S(1)} custom-call(s32[1]{0:T(128)} %bitcast.here_ref, bf16[128,2048]{1,0:T(8,128)(2,1)} %collective-permute-done.9.refs_0_, bf16[6656,4096]{1,0:T(8,128)(2,1)} %refs_1_.9, f32[128,4096]{1,0:T(8,128)S(1)} %copy-done.3, bf16[64,2048]{1,0:T(8,128)(2,1)} %get-tuple-element.34.refs_3_), custom_call_target="tpu_custom_call" | custom-call | flops 1 | bytes 1 | tf_op jit(solution)/shard_map/pallas_call | solution.py:132
  56.6 5.6 %shard_map.84.refs_2_ = f32[128,4096]{1,0:T(8,128)S(1)} custom-call(s32[1]{0:T(128)} %bitcast.here_ref, bf16[128,1536]{1,0:T(8,128)(2,1)S(1)} %collective-permute-done.8.refs_0_, bf16[6656,4096]{1,0:T(8,128)(2,1)} %refs_1_.9, f32[128,4096]{1,0:T(8,128)S(1)} %shard_map.83.refs_2_, bf16[32,2048]{1,0:T(8,128)(2,1)S(1)} %get-tuple-element.36.refs_3_), custom_call_target="tpu_custom_call" | custom-call | flops 1 | bytes 1 | tf_op jit(solution)/shard_map/pallas_call | solution.py:132
  62.2 1.9 %shard_map.82.refs_3_.refs_0_ = bf16[32,2176]{1,0:T(8,128)(2,1)S(1)} custom-call(f32[32,2048]{1,0:T(8,128)S(1)} %get-tuple-element.35.kept_ref, bf16[32,2048]{1,0:T(8,128)(2,1)} %collective-permute-done.3.came_ref, f32[1,2048]{1,0:T(1,128)S(1)} %bitcast.11, f32[128,128]{1,0:T(8,128)S(1)} %copy-done.4), custom_call_target="tpu_custom_call" | custom-call | flops 1 | bytes 1 | tf_op jit(solution)/shard_map/pallas_call | solution.py:202
  64.1 3.0 %shard_map.85 = (bf16[128,1024]{1,0:T(8,128)(2,1)S(1)}, f32[128,1024]{1,0:T(8,128)S(1)}) custom-call(s32[1]{0:T(128)} %bitcast.here_ref, bf16[128,1024]{1,0:T(8,128)(2,1)S(1)} %collective-permute-done.7.refs_0_, bf16[6656,4096]{1,0:T(8,128)(2,1)} %refs_1_.9, f32[128,4096]{1,0:T(8,128)S(1)} %shard_map.84.refs_2_, bf16[32,2176]{1,0:T(8,128)(2,1)S(1)} %shard_map.82.refs_3_.refs_0_), custom_call_target="tpu_custom_call" | custom-call | flops 1 | bytes 1 | tf_op jit(solution)/shard_map/pallas_call | solution.py:132
  67.1 3.0 %shard_map.90 = (bf16[128,1024]{1,0:T(8,128)(2,1)S(1)}, f32[128,1024]{1,0:T(8,128)S(1)}) custom-call(s32[1]{0:T(128)} %bitcast.here_ref, bf16[128,1024]{1,0:T(8,128)(2,1)S(1)} %collective-permute-done.7.refs_0_, bf16[6656,4096]{1,0:T(8,128)(2,1)} %refs_1_.9, f32[128,4096]{1,0:T(8,128)S(1)} %shard_map.84.refs_2_, bf16[128,1024]{1,0:T(8,128)(2,1)S(1)} %get-tuple-element.39.refs_3_), custom_call_target="tpu_custom_call" | custom-call | flops 1 | bytes 1 | tf_op jit(solution)/shard_map/pallas_call | solution.py:132
  70.7 1.0 collective-permute-done.16.came_ref
  71.7 1.6 %collective-permute-start.17 = (bf16[64,1024]{1,0:T(8,128)(2,1)S(1)}, bf16[64,1024]{1,0:T(8,128)(2,1)S(1)}, u32[]{:S(2)}, u32[]{:S(2)}) collective-permute-start(bf16[64,1024]{1,0:T(8,128)(2,1)S(1)} %get-tuple-element.47), channel_id=1, source_target_pairs={{0,4},{4,0},{8,12},{12,8},{1,5},{5,1},{9,13},{13,9},{2,6},{6,2},{1... | collective-permute-start | bytes 393224 | tf_op jit(solution)/shard_map/ppermute | solution.py:332
  74.3 1.6 %collective-permute-start.4 = (bf16[32,2176]{1,0:T(8,128)(2,1)S(1)}, bf16[32,2176]{1,0:T(8,128)(2,1)S(1)}, u32[]{:S(2)}, u32[]{:S(2)}) collective-permute-start(bf16[32,2176]{1,0:T(8,128)(2,1)S(1)} %shard_map.82.refs_3_.refs_0_), channel_id=1, source_target_pairs={{0,4},{4,0},{8,12},{12,8},{1,5},{5,1},{9,13},{13,9},{2,6},{6,2},{1... | collective-permute-start | bytes 417800 | tf_op jit(solution)/shard_map/ppermute | solution.py:332
  75.9 5.2 %collective-permute-done.17.came_ref = bf16[64,1024]{1,0:T(8,128)(2,1)S(1)} collective-permute-done((bf16[64,1024]{1,0:T(8,128)(2,1)S(1)}, bf16[64,1024]{1,0:T(8,128)(2,1)S(1)}, u32[]{:S(2)}, u32[]{:S(2)}) %collective-permute-start.17) | collective-permute-done | bytes 131104 | tf_op jit(solution)/shard_map/ppermute | solution.py:332
  81.3 3.3 %collective-permute-done.11.came_ref = bf16[64,1024]{1,0:T(8,128)(2,1)S(1)} collective-permute-done((bf16[64,1024]{1,0:T(8,128)(2,1)S(1)}, bf16[64,1024]{1,0:T(8,128)(2,1)S(1)}, u32[]{:S(2)}, u32[]{:S(2)}) %collective-permute-start.11) | collective-permute-done | bytes 131104 | tf_op jit(solution)/shard_map/ppermute | solution.py:332
  84.8 4.6 %collective-permute-done.18.came_ref = bf16[32,1024]{1,0:T(8,128)(2,1)S(1)} collective-permute-done((bf16[32,1024]{1,0:T(8,128)(2,1)S(1)}, bf16[32,1024]{1,0:T(8,128)(2,1)S(1)}, u32[]{:S(2)}, u32[]{:S(2)}) %collective-permute-start.18) | collective-permute-done | bytes 65568 | tf_op jit(solution)/shard_map/ppermute | solution.py:332
  89.4 0.6 shard_map.93.refs_4_
  90.0 1.3 %collective-permute-start.20 = (bf16[32,1152]{1,0:T(8,128)(2,1)S(1)}, bf16[32,1152]{1,0:T(8,128)(2,1)S(1)}, u32[]{:S(2)}, u32[]{:S(2)}) collective-permute-start(bf16[32,1152]{1,0:T(8,128)(2,1)S(1)} %shard_map.93.refs_4_), channel_id=1, source_target_pairs={{0,8},{4,12},{8,0},{12,4},{1,9},{5,13},{9,1},{13,5},{2,10},{6,14},... | collective-permute-start | bytes 221192 | tf_op jit(solution)/shard_map/ppermute | solution.py:332
  91.4 0.6 shard_map.88.refs_4_
  92.0 1.7 %collective-permute-start.14 = (bf16[32,1152]{1,0:T(8,128)(2,1)S(1)}, bf16[32,1152]{1,0:T(8,128)(2,1)S(1)}, u32[]{:S(2)}, u32[]{:S(2)}) collective-permute-start(bf16[32,1152]{1,0:T(8,128)(2,1)S(1)} %shard_map.88.refs_4_), channel_id=1, source_target_pairs={{0,8},{4,12},{8,0},{12,4},{1,9},{5,13},{9,1},{13,5},{2,10},{6,14},... | collective-permute-start | bytes 221192 | tf_op jit(solution)/shard_map/ppermute | solution.py:332
  93.7 1.2 %collective-permute-start.6 = (bf16[32,2176]{1,0:T(8,128)(2,1)S(1)}, bf16[32,2176]{1,0:T(8,128)(2,1)S(1)}, u32[]{:S(2)}, u32[]{:S(2)}) collective-permute-start(bf16[32,2176]{1,0:T(8,128)(2,1)S(1)} %collective-permute-done.5.refs_2_), channel_id=1, source_target_pairs={{0,4},{4,0},{8,12},{12,8},{1,5},{5,1},{9,13},{13,9},{2,6},{6,2},{1... | collective-permute-start | bytes 417800 | tf_op jit(solution)/shard_map/ppermute | solution.py:332
  94.9 0.8 collective-permute-start.19
  95.7 1.2 %collective-permute-start.13 = (bf16[32,1152]{1,0:T(8,128)(2,1)S(1)}, bf16[32,1152]{1,0:T(8,128)(2,1)S(1)}, u32[]{:S(2)}, u32[]{:S(2)}) collective-permute-start(bf16[32,1152]{1,0:T(8,128)(2,1)S(1)} %shard_map.88.refs_4_), channel_id=1, source_target_pairs={{0,4},{4,0},{8,12},{12,8},{1,5},{5,1},{9,13},{13,9},{2,6},{6,2},{1... | collective-permute-start | bytes 221192 | tf_op jit(solution)/shard_map/ppermute | solution.py:332
  97.0 0.8 collective-permute-start.21
  97.9 1.1 %collective-permute-start.15 = (bf16[32,1152]{1,0:T(8,128)(2,1)S(1)}, bf16[32,1152]{1,0:T(8,128)(2,1)S(1)}, u32[]{:S(2)}, u32[]{:S(2)}) collective-permute-start(bf16[32,1152]{1,0:T(8,128)(2,1)S(1)} %collective-permute-done.14.refs_6_), channel_id=1, source_target_pairs={{0,4},{4,0},{8,12},{12,8},{1,5},{5,1},{9,13},{13,9},{2,6},{6,2},{1... | collective-permute-start | bytes 221192 | tf_op jit(solution)/shard_map/ppermute | solution.py:332
  99.1 1.7 %collective-permute-done.6.refs_3_ = bf16[32,2176]{1,0:T(8,128)(2,1)S(1)} collective-permute-done((bf16[32,2176]{1,0:T(8,128)(2,1)S(1)}, bf16[32,2176]{1,0:T(8,128)(2,1)S(1)}, u32[]{:S(2)}, u32[]{:S(2)}) %collective-permute-start.6) | collective-permute-done | bytes 139296 | tf_op jit(solution)/shard_map/ppermute | solution.py:332
  100.7 1.6 %collective-permute-done.19.refs_5_ = bf16[32,1152]{1,0:T(8,128)(2,1)S(1)} collective-permute-done((bf16[32,1152]{1,0:T(8,128)(2,1)S(1)}, bf16[32,1152]{1,0:T(8,128)(2,1)S(1)}, u32[]{:S(2)}, u32[]{:S(2)}) %collective-permute-start.19) | collective-permute-done | bytes 73760 | tf_op jit(solution)/shard_map/ppermute | solution.py:332
  102.3 2.3 %collective-permute-done.21.refs_7_ = bf16[32,1152]{1,0:T(8,128)(2,1)S(1)} collective-permute-done((bf16[32,1152]{1,0:T(8,128)(2,1)S(1)}, bf16[32,1152]{1,0:T(8,128)(2,1)S(1)}, u32[]{:S(2)}, u32[]{:S(2)}) %collective-permute-start.21) | collective-permute-done | bytes 73760 | tf_op jit(solution)/shard_map/ppermute | solution.py:332
  104.6 0.6 shard_map.96
  105.4 0.6 shard_map.95
  106.4 0.6 shard_map.94.refs_1_
  107.0 0.6 shard_map.89.refs_0_
  107.7 1.1 %shard_map.97 = (bf16[128,4096]{1,0:T(8,128)(2,1)}, bf16[32,128]{1,0:T(8,128)(2,1)}) custom-call(s32[1]{0:T(128)} %bitcast.here_ref, bf16[128,1152]{1,0:T(8,128)(2,1)S(1)} %shard_map.89.refs_0_, bf16[128,1152]{1,0:T(8,128)(2,1)S(1)} %shard_map.94.refs_1_, bf16[128,1152]{1,0:T(8,128)(2,1)S(1)} %collective-permute-done.22.refs_2_, ...), custom_call_target="tpu_custom_call" | custom-call | flops 1 | bytes 1 | tf_op jit(solution)/shard_map/pallas_call | solution.py:286
  (50 shorter events, 2.9 us)
Async XLA Ops:
  0.6 1.5 %copy-start = (bf16[128,6656]{1,0:T(8,128)(2,1)S(1)}, bf16[128,6656]{1,0:T(8,128)(2,1)}, u32[]{:S(2)}) copy-start(bf16[128,6656]{1,0:T(8,128)(2,1)} %refs_0_.3) | copy-start | bytes 5111812
  2.1 3.8 %copy-start.1 = (bf16[128,6656]{1,0:T(8,128)(2,1)S(1)}, bf16[128,6656]{1,0:T(8,128)(2,1)}, u32[]{:S(2)}) copy-start(bf16[128,6656]{1,0:T(8,128)(2,1)} %refs_0_.3) | copy-start | bytes 5111812
  3.0 15.8 %copy-start.9 = (bf16[128,1024]{1,0:T(8,128)(2,1)}, bf16[128,1024]{1,0:T(8,128)(2,1)S(1)}, u32[]{:S(2)}) copy-start(bf16[128,1024]{1,0:T(8,128)(2,1)S(1)} %get-tuple-element.30.refs_5_) | copy-start | bytes 786436
  3.0 15.8 %collective-permute-start = (bf16[128,2048]{1,0:T(8,128)(2,1)S(1)}, bf16[128,2048]{1,0:T(8,128)(2,1)S(1)}, u32[]{:S(2)}, u32[]{:S(2)}) collective-permute-start(bf16[128,2048]{1,0:T(8,128)(2,1)S(1)} %get-tuple-element.27.refs_2_), channel_id=1, source_target_pairs={{0,2},{2,0},{1,3},{3,1},{4,6},{6,4},{5,7},{7,5},{8,10},{10,8},{9,1... | collective-permute-start | bytes 1572872 | tf_op jit(solution)/shard_map/ppermute | solution.py:360
  18.8 0.8 copy-start.5
  19.6 1.0 copy-start.6
  20.6 28.1 %copy-start.12 = (s32[4096]{0:T(1024)S(1)}, s32[4096]{0:T(1024)}, u32[]{:S(2)}) copy-start(s32[4096]{0:T(1024)} %param.8) | copy-start | bytes 49156
  28.6 1.3 %copy-start.2 = (f32[128,4096]{1,0:T(8,128)}, f32[128,4096]{1,0:T(8,128)S(1)}, u32[]{:S(2)}) copy-start(f32[128,4096]{1,0:T(8,128)S(1)} %get-tuple-element.37.refs_2_) | copy-start | bytes 6291460
  29.9 18.9 %copy-start.3 = (f32[128,4096]{1,0:T(8,128)S(1)}, f32[128,4096]{1,0:T(8,128)}, u32[]{:S(2)}) copy-start(f32[128,4096]{1,0:T(8,128)} %copy-done.2) | copy-start | bytes 6291460
  29.9 2.3 %collective-permute-start.1 = (bf16[128,2048]{1,0:T(8,128)(2,1)}, bf16[128,2048]{1,0:T(8,128)(2,1)}, u32[]{:S(2)}, u32[]{:S(2)}) collective-permute-start(bf16[128,2048]{1,0:T(8,128)(2,1)} %get-tuple-element.32), channel_id=1, source_target_pairs={{0,1},{1,0},{2,3},{3,2},{4,5},{5,4},{6,7},{7,6},{8,9},{9,8},{10,11... | collective-permute-start | bytes 1572872 | tf_op jit(solution)/shard_map/ppermute | solution.py:329
  29.9 18.9 %collective-permute-start.9 = (bf16[128,2048]{1,0:T(8,128)(2,1)}, bf16[128,2048]{1,0:T(8,128)(2,1)}, u32[]{:S(2)}, u32[]{:S(2)}) collective-permute-start(bf16[128,2048]{1,0:T(8,128)(2,1)} %get-tuple-element.28.refs_3_), channel_id=1, source_target_pairs={{0,2},{2,0},{1,3},{3,1},{4,6},{6,4},{5,7},{7,5},{8,10},{10,8},{9,1... | collective-permute-start | bytes 1572872 | tf_op jit(solution)/shard_map/ppermute | solution.py:360
  34.0 0.8 copy-start.7
  34.8 8.6 %collective-permute-start.2 = (bf16[64,2048]{1,0:T(8,128)(2,1)}, bf16[64,2048]{1,0:T(8,128)(2,1)S(1)}, u32[]{:S(2)}, u32[]{:S(2)}) collective-permute-start(bf16[64,2048]{1,0:T(8,128)(2,1)} %get-tuple-element.34.refs_3_), channel_id=1, source_target_pairs={{0,4},{4,0},{8,12},{12,8},{1,5},{5,1},{9,13},{13,9},{2,6},{6,2},{1... | collective-permute-start | bytes 786440 | tf_op jit(solution)/shard_map/ppermute | solution.py:332
  36.4 20.2 %collective-permute-start.8 = (bf16[128,1536]{1,0:T(8,128)(2,1)S(1)}, bf16[128,1536]{1,0:T(8,128)(2,1)S(1)}, u32[]{:S(2)}, u32[]{:S(2)}) collective-permute-start(bf16[128,1536]{1,0:T(8,128)(2,1)S(1)} %get-tuple-element.29.refs_4_), channel_id=1, source_target_pairs={{0,2},{2,0},{1,3},{3,1},{4,6},{6,4},{5,7},{7,5},{8,10},{10,8},{9,1... | collective-permute-start | bytes 1179656 | tf_op jit(solution)/shard_map/ppermute | solution.py:360
  37.2 26.9 %collective-permute-start.7 = (bf16[128,1024]{1,0:T(8,128)(2,1)}, bf16[128,1024]{1,0:T(8,128)(2,1)S(1)}, u32[]{:S(2)}, u32[]{:S(2)}) collective-permute-start(bf16[128,1024]{1,0:T(8,128)(2,1)} %copy-done.9), channel_id=1, source_target_pairs={{0,2},{2,0},{1,3},{3,1},{4,6},{6,4},{5,7},{7,5},{8,10},{10,8},{9,1... | collective-permute-start | bytes 786440 | tf_op jit(solution)/shard_map/ppermute | solution.py:360
  43.3 0.7 copy-start.10
  44.1 1.0 copy-start.8
  45.1 0.9 copy-start.11
  46.1 16.1 %collective-permute-start.3 = (bf16[32,2048]{1,0:T(8,128)(2,1)S(1)}, bf16[32,2048]{1,0:T(8,128)(2,1)}, u32[]{:S(2)}, u32[]{:S(2)}) collective-permute-start(bf16[32,2048]{1,0:T(8,128)(2,1)S(1)} %get-tuple-element.36.refs_3_), channel_id=1, source_target_pairs={{0,8},{4,12},{8,0},{12,4},{1,9},{5,13},{9,1},{13,5},{2,10},{6,14},... | collective-permute-start | bytes 393224 | tf_op jit(solution)/shard_map/ppermute | solution.py:332
  56.5 5.6 %copy-start.4 = (f32[128,128]{1,0:T(8,128)S(1)}, f32[128,128]{1,0:T(8,128)}, u32[]{:S(2)}) copy-start(f32[128,128]{1,0:T(8,128)} %constant.46.clone.rotation_ref) | copy-start | bytes 196612
  70.1 1.6 %collective-permute-start.16 = (bf16[128,1024]{1,0:T(8,128)(2,1)S(1)}, bf16[128,1024]{1,0:T(8,128)(2,1)S(1)}, u32[]{:S(2)}, u32[]{:S(2)}) collective-permute-start(bf16[128,1024]{1,0:T(8,128)(2,1)S(1)} %get-tuple-element.45), channel_id=1, source_target_pairs={{0,1},{1,0},{2,3},{3,2},{4,5},{5,4},{6,7},{7,6},{8,9},{9,8},{10,11... | collective-permute-start | bytes 786440 | tf_op jit(solution)/shard_map/ppermute | solution.py:329
  70.2 3.2 %collective-permute-start.10 = (bf16[128,1024]{1,0:T(8,128)(2,1)S(1)}, bf16[128,1024]{1,0:T(8,128)(2,1)S(1)}, u32[]{:S(2)}, u32[]{:S(2)}) collective-permute-start(bf16[128,1024]{1,0:T(8,128)(2,1)S(1)} %get-tuple-element.39.refs_3_), channel_id=1, source_target_pairs={{0,1},{1,0},{2,3},{3,2},{4,5},{5,4},{6,7},{7,6},{8,9},{9,8},{10,11... | collective-permute-start | bytes 786440 | tf_op jit(solution)/shard_map/ppermute | solution.py:329
  71.7 9.3 %collective-permute-start.17 = (bf16[64,1024]{1,0:T(8,128)(2,1)S(1)}, bf16[64,1024]{1,0:T(8,128)(2,1)S(1)}, u32[]{:S(2)}, u32[]{:S(2)}) collective-permute-start(bf16[64,1024]{1,0:T(8,128)(2,1)S(1)} %get-tuple-element.47), channel_id=1, source_target_pairs={{0,4},{4,0},{8,12},{12,8},{1,5},{5,1},{9,13},{13,9},{2,6},{6,2},{1... | collective-permute-start | bytes 393224 | tf_op jit(solution)/shard_map/ppermute | solution.py:332
  73.4 11.2 %collective-permute-start.11 = (bf16[64,1024]{1,0:T(8,128)(2,1)S(1)}, bf16[64,1024]{1,0:T(8,128)(2,1)S(1)}, u32[]{:S(2)}, u32[]{:S(2)}) collective-permute-start(bf16[64,1024]{1,0:T(8,128)(2,1)S(1)} %get-tuple-element.41), channel_id=1, source_target_pairs={{0,4},{4,0},{8,12},{12,8},{1,5},{5,1},{9,13},{13,9},{2,6},{6,2},{1... | collective-permute-start | bytes 393224 | tf_op jit(solution)/shard_map/ppermute | solution.py:332
  73.9 19.8 %collective-permute-start.5 = (bf16[32,2176]{1,0:T(8,128)(2,1)S(1)}, bf16[32,2176]{1,0:T(8,128)(2,1)S(1)}, u32[]{:S(2)}, u32[]{:S(2)}) collective-permute-start(bf16[32,2176]{1,0:T(8,128)(2,1)S(1)} %shard_map.82.refs_3_.refs_0_), channel_id=1, source_target_pairs={{0,8},{4,12},{8,0},{12,4},{1,9},{5,13},{9,1},{13,5},{2,10},{6,14},... | collective-permute-start | bytes 417800 | tf_op jit(solution)/shard_map/ppermute | solution.py:332
  74.3 21.5 %collective-permute-start.4 = (bf16[32,2176]{1,0:T(8,128)(2,1)S(1)}, bf16[32,2176]{1,0:T(8,128)(2,1)S(1)}, u32[]{:S(2)}, u32[]{:S(2)}) collective-permute-start(bf16[32,2176]{1,0:T(8,128)(2,1)S(1)} %shard_map.82.refs_3_.refs_0_), channel_id=1, source_target_pairs={{0,4},{4,0},{8,12},{12,8},{1,5},{5,1},{9,13},{13,9},{2,6},{6,2},{1... | collective-permute-start | bytes 417800 | tf_op jit(solution)/shard_map/ppermute | solution.py:332
  81.1 8.3 %collective-permute-start.18 = (bf16[32,1024]{1,0:T(8,128)(2,1)S(1)}, bf16[32,1024]{1,0:T(8,128)(2,1)S(1)}, u32[]{:S(2)}, u32[]{:S(2)}) collective-permute-start(bf16[32,1024]{1,0:T(8,128)(2,1)S(1)} %get-tuple-element.49), channel_id=1, source_target_pairs={{0,8},{4,12},{8,0},{12,4},{1,9},{5,13},{9,1},{13,5},{2,10},{6,14},... | collective-permute-start | bytes 196616 | tf_op jit(solution)/shard_map/ppermute | solution.py:332
  84.7 6.7 %collective-permute-start.12 = (bf16[32,1024]{1,0:T(8,128)(2,1)S(1)}, bf16[32,1024]{1,0:T(8,128)(2,1)S(1)}, u32[]{:S(2)}, u32[]{:S(2)}) collective-permute-start(bf16[32,1024]{1,0:T(8,128)(2,1)S(1)} %get-tuple-element.43), channel_id=1, source_target_pairs={{0,8},{4,12},{8,0},{12,4},{1,9},{5,13},{9,1},{13,5},{2,10},{6,14},... | collective-permute-start | bytes 196616 | tf_op jit(solution)/shard_map/ppermute | solution.py:332
  90.0 6.9 %collective-permute-start.20 = (bf16[32,1152]{1,0:T(8,128)(2,1)S(1)}, bf16[32,1152]{1,0:T(8,128)(2,1)S(1)}, u32[]{:S(2)}, u32[]{:S(2)}) collective-permute-start(bf16[32,1152]{1,0:T(8,128)(2,1)S(1)} %shard_map.93.refs_4_), channel_id=1, source_target_pairs={{0,8},{4,12},{8,0},{12,4},{1,9},{5,13},{9,1},{13,5},{2,10},{6,14},... | collective-permute-start | bytes 221192 | tf_op jit(solution)/shard_map/ppermute | solution.py:332
  92.0 5.9 %collective-permute-start.14 = (bf16[32,1152]{1,0:T(8,128)(2,1)S(1)}, bf16[32,1152]{1,0:T(8,128)(2,1)S(1)}, u32[]{:S(2)}, u32[]{:S(2)}) collective-permute-start(bf16[32,1152]{1,0:T(8,128)(2,1)S(1)} %shard_map.88.refs_4_), channel_id=1, source_target_pairs={{0,8},{4,12},{8,0},{12,4},{1,9},{5,13},{9,1},{13,5},{2,10},{6,14},... | collective-permute-start | bytes 221192 | tf_op jit(solution)/shard_map/ppermute | solution.py:332
  93.7 7.0 %collective-permute-start.6 = (bf16[32,2176]{1,0:T(8,128)(2,1)S(1)}, bf16[32,2176]{1,0:T(8,128)(2,1)S(1)}, u32[]{:S(2)}, u32[]{:S(2)}) collective-permute-start(bf16[32,2176]{1,0:T(8,128)(2,1)S(1)} %collective-permute-done.5.refs_2_), channel_id=1, source_target_pairs={{0,4},{4,0},{8,12},{12,8},{1,5},{5,1},{9,13},{13,9},{2,6},{6,2},{1... | collective-permute-start | bytes 417800 | tf_op jit(solution)/shard_map/ppermute | solution.py:332
  94.9 7.4 %collective-permute-start.19 = (bf16[32,1152]{1,0:T(8,128)(2,1)S(1)}, bf16[32,1152]{1,0:T(8,128)(2,1)S(1)}, u32[]{:S(2)}, u32[]{:S(2)}) collective-permute-start(bf16[32,1152]{1,0:T(8,128)(2,1)S(1)} %shard_map.93.refs_4_), channel_id=1, source_target_pairs={{0,4},{4,0},{8,12},{12,8},{1,5},{5,1},{9,13},{13,9},{2,6},{6,2},{1... | collective-permute-start | bytes 221192 | tf_op jit(solution)/shard_map/ppermute | solution.py:332
  95.7 9.5 %collective-permute-start.13 = (bf16[32,1152]{1,0:T(8,128)(2,1)S(1)}, bf16[32,1152]{1,0:T(8,128)(2,1)S(1)}, u32[]{:S(2)}, u32[]{:S(2)}) collective-permute-start(bf16[32,1152]{1,0:T(8,128)(2,1)S(1)} %shard_map.88.refs_4_), channel_id=1, source_target_pairs={{0,4},{4,0},{8,12},{12,8},{1,5},{5,1},{9,13},{13,9},{2,6},{6,2},{1... | collective-permute-start | bytes 221192 | tf_op jit(solution)/shard_map/ppermute | solution.py:332
  97.0 7.6 %collective-permute-start.21 = (bf16[32,1152]{1,0:T(8,128)(2,1)S(1)}, bf16[32,1152]{1,0:T(8,128)(2,1)S(1)}, u32[]{:S(2)}, u32[]{:S(2)}) collective-permute-start(bf16[32,1152]{1,0:T(8,128)(2,1)S(1)} %collective-permute-done.20.refs_6_), channel_id=1, source_target_pairs={{0,4},{4,0},{8,12},{12,8},{1,5},{5,1},{9,13},{13,9},{2,6},{6,2},{1... | collective-permute-start | bytes 221192 | tf_op jit(solution)/shard_map/ppermute | solution.py:332
  97.9 7.5 %collective-permute-start.15 = (bf16[32,1152]{1,0:T(8,128)(2,1)S(1)}, bf16[32,1152]{1,0:T(8,128)(2,1)S(1)}, u32[]{:S(2)}, u32[]{:S(2)}) collective-permute-start(bf16[32,1152]{1,0:T(8,128)(2,1)S(1)} %collective-permute-done.14.refs_6_), channel_id=1, source_target_pairs={{0,4},{4,0},{8,12},{12,8},{1,5},{5,1},{9,13},{13,9},{2,6},{6,2},{1... | collective-permute-start | bytes 221192 | tf_op jit(solution)/shard_map/ppermute | solution.py:332
  105.2 2.5 %collective-permute-start.23 = (bf16[128,1152]{1,0:T(8,128)(2,1)S(1)}, bf16[128,1152]{1,0:T(8,128)(2,1)S(1)}, u32[]{:S(2)}, u32[]{:S(2)}) collective-permute-start(bf16[128,1152]{1,0:T(8,128)(2,1)S(1)} %shard_map.96), channel_id=1, source_target_pairs={{0,1},{1,0},{2,3},{3,2},{4,5},{5,4},{6,7},{7,6},{8,9},{9,8},{10,11... | collective-permute-start | bytes 884744 | tf_op jit(solution)/shard_map/ppermute | solution.py:329
  106.0 1.7 %collective-permute-start.22 = (bf16[128,1152]{1,0:T(8,128)(2,1)S(1)}, bf16[128,1152]{1,0:T(8,128)(2,1)S(1)}, u32[]{:S(2)}, u32[]{:S(2)}) collective-permute-start(bf16[128,1152]{1,0:T(8,128)(2,1)S(1)} %shard_map.95), channel_id=1, source_target_pairs={{0,1},{1,0},{2,3},{3,2},{4,5},{5,4},{6,7},{7,6},{8,9},{9,8},{10,11... | collective-permute-start | bytes 884744 | tf_op jit(solution)/shard_map/ppermute | solution.py:329

commit v5 on v4

--- a/solution.py
+++ b/solution.py
@@ -13,7 +13,8 @@
 UNIT = 512
 GROUPS = 2
 BUFFERS = 4
-VMEM_LIMIT = 40 * 2**20
+VMEM_LIMIT = 6 * 2**20
+SHARES = (3, 3, 3, 2)
 epsilon = 1e-06
 
 SMALL = pl.CostEstimate(flops=1, bytes_accessed=1, transcendentals=0)
@@ -21,6 +22,7 @@
 VMEM = pl.BlockSpec(memory_space=pltpu.VMEM)
 SMEM = pl.BlockSpec(memory_space=pltpu.SMEM)
 ANY = pl.BlockSpec(memory_space=pl.ANY)
+HBM = pl.BlockSpec(memory_space=pltpu.HBM)
 
 
 def hadamard(order):
@@ -31,20 +33,123 @@
     return ((1 - 2 * (parity % 2)) / math.sqrt(order)).astype(np.float32)
 
 
-def slice_body(places, in_ref, *out_refs):
-    for (at, size), out_ref in zip(places, out_refs):
-        out_ref[...] = in_ref[:, at : at + size]
+def slice_body(places, in_ref, *refs):
+    out_refs, arrived = refs[:-1], refs[-1]
+    copies = [
+        pltpu.make_async_copy(in_ref.at[:, at : at + size], out_ref, arrived.at[index])
+        for index, ((at, size), out_ref) in enumerate(zip(places, out_refs))
+    ]
+    for copy in copies:
+        copy.start()
+    for copy in copies:
+        copy.wait()
 
 
 def slices_of(values, places):
     return pl.pallas_call(
         functools.partial(slice_body, places),
         out_shape=[jax.ShapeDtypeStruct((values.shape[0], size), values.dtype) for _, size in places],
-        in_specs=[VMEM],
+        in_specs=[HBM],
         out_specs=[VMEM] * len(places),
+        scratch_shapes=[pltpu.SemaphoreType.DMA((len(places),))],
         compiler_params=PARAMS,
         cost_estimate=SMALL,
     )(values)
+
+
+def resident_body(sizes, row, lead, *refs):
+    left_refs, w_ref, refs = refs[: len(sizes)], refs[len(sizes)], refs[len(sizes) + 1 :]
+    out_ref, held_ref, sems = refs[lead:]
+    columns = w_ref.shape[1]
+    steps, wide = sems.shape[0], columns // sems.shape[0]
+
+    def at(n):
+        return pl.ds(pl.multiple_of(n * wide, wide), wide)
+
+    def copy(n):
+        return pltpu.make_async_copy(w_ref.at[pl.ds(row, sum(sizes)), at(n)], held_ref.at[:, at(n)], sems.at[n])
+
+    for n in range(steps):
+        copy(n).start()
+
+    def step(n):
+        copy(n).wait()
+        total, begin = None, 0
+        for left_ref, size in zip(left_refs, sizes):
+            product = jnp.dot(
+                left_ref[...], held_ref[begin : begin + size, at(n)], preferred_element_type=jnp.float32
+            )
+            total = product if total is None else total + product
+            begin += size
+        out_ref[:, at(n)] = total
+
+    pl.loop(0, steps)(step)
+
+
+def multiply_resident(lefts, weight, row, wide, tokens=()):
+    rows, columns = lefts[0].shape[0], weight.shape[1]
+    sizes = [left.shape[1] for left in lefts]
+    return pl.pallas_call(
+        functools.partial(resident_body, sizes, row, len(tokens)),
+        out_shape=[
+            jax.ShapeDtypeStruct((rows, columns), jnp.float32),
+            jax.ShapeDtypeStruct((sum(sizes), columns), weight.dtype),
+        ],
+        in_specs=[VMEM] * len(lefts) + [HBM] + [ANY] * len(tokens),
+        out_specs=[VMEM, VMEM],
+        scratch_shapes=[pltpu.SemaphoreType.DMA((columns // wide,))],
+        compiler_params=PARAMS,
+        cost_estimate=SMALL,
+    )(*lefts, weight, *tokens)
+
+
+def held_body(row, has_total, split, first, number, wide, here_ref, left_ref, w_ref, *refs):
+    total_refs, out_refs = refs[:has_total], refs[len(refs) - 1 - split :]
+    in_half = w_ref.shape[1] // wide // 2
+    steps = 2 * first if split else 2 * in_half
+
+    def at(block):
+        return pl.ds(pl.multiple_of(block * wide, wide), wide)
+
+    def step(n, second):
+        block = n
+        if split:
+            block = (here_ref[0] if second else 1 - here_ref[0]) * in_half + number * first + n
+            block = block - (first if second else 0)
+        value = jnp.dot(left_ref[...], w_ref[row : row + left_ref.shape[1], at(block)], preferred_element_type=jnp.float32)
+        if has_total:
+            value = value + total_refs[0][:, at(block)]
+        if second:
+            out_refs[1][:, at(n - first)] = value
+        else:
+            out_refs[0][:, at(n)] = value.astype(out_refs[0].dtype)
+
+    if split:
+        pl.loop(0, first)(functools.partial(step, second=False))
+        pl.loop(first, steps)(functools.partial(step, second=True))
+    else:
+        pl.loop(0, steps)(functools.partial(step, second=False))
+
+
+def multiply_held(left, weight, row, facts, total, split, wide, group=(0, 1), tokens=()):
+    rows, columns = left.shape[0], weight.shape[1]
+    number, count = group
+    first = columns // wide // 2 // count
+    out_shape = [jax.ShapeDtypeStruct((rows, columns), jnp.float32)]
+    if split:
+        out_shape = [
+            jax.ShapeDtypeStruct((rows, first * wide), jnp.bfloat16),
+            jax.ShapeDtypeStruct((rows, first * wide), jnp.float32),
+        ]
+    held = [] if total is None else [total]
+    return pl.pallas_call(
+        functools.partial(held_body, row, len(held), split, first, number, wide),
+        out_shape=out_shape,
+        in_specs=[SMEM, VMEM, VMEM] + [VMEM] * len(held) + [ANY] * len(tokens),
+        out_specs=[VMEM] * len(out_shape),
+        compiler_params=PARAMS,
+        cost_estimate=SMALL,
+    )(facts, left, weight, *held, *tokens)
 
 
 def multiply_body(offsets, has_totals, splits, row, first, number, here_ref, *refs):
@@ -105,7 +210,7 @@
     pl.loop(first, steps)(functools.partial(step, second=True))
 
 
-def multiply(lefts, weight, row, depth, here, totals, splits, wide, group=None, tokens=()):
+def multiply(lefts, weight, row, depth, facts, totals, splits, wide, group=None, tokens=()):
     rows = lefts[0][0].shape[0]
     columns = weight.shape[1]
     number, count = group or (0, 1)
@@ -134,7 +239,7 @@
         out_shape=out_shape,
         in_specs=[SMEM]
         + [VMEM] * len(lefts)
-        + [ANY]
+        + [HBM]
         + [VMEM] * len(held)
         + [ANY] * len(tokens),
         out_specs=[VMEM] * len(out_shape),
@@ -144,10 +249,11 @@
         ],
         compiler_params=PARAMS,
         cost_estimate=SMALL,
-    )(here, *[left for left, _ in lefts], weight, *held, *tokens)
-
-
-def halve_body(bit_ref, kept_ref, came_ref, sent_out, kept_out):
+    )(facts, *[left for left, _ in lefts], weight, *held, *tokens)
+
+
+def halve_body(level, facts_ref, kept_ref, came_ref, *refs):
+    sent_out, kept_out = refs[-2:]
     half = sent_out.shape[0]
 
     def put(bit):
@@ -156,37 +262,40 @@
         sent_out[...] = (kept_ref[other] + came_ref[other].astype(jnp.float32)).astype(jnp.bfloat16)
 
     for bit in range(2):
-        pl.when(bit_ref[0] == bit)(functools.partial(put, bit))
-
-
-def halve(kept, came, bit):
+        pl.when(facts_ref[1 + level] == bit)(functools.partial(put, bit))
+
+
+def halve(kept, came, level, facts, tokens=()):
     rows, columns = kept.shape
     half = rows // 2
     if half % 16:
-        total = kept + came.astype(jnp.float32)
+        total, bit = kept + came.astype(jnp.float32), facts[1 + level]
         sent = lax.dynamic_slice_in_dim(total, (1 - bit) * half, half, 0).astype(jnp.bfloat16)
         return sent, lax.dynamic_slice_in_dim(total, bit * half, half, 0)
     return pl.pallas_call(
-        halve_body,
+        functools.partial(halve_body, level),
         out_shape=[
             jax.ShapeDtypeStruct((half, columns), jnp.bfloat16),
             jax.ShapeDtypeStruct((half, columns), jnp.float32),
         ],
-        in_specs=[SMEM, VMEM, VMEM],
+        in_specs=[SMEM, VMEM, VMEM] + [ANY] * len(tokens),
         out_specs=[VMEM, VMEM],
         compiler_params=PARAMS,
         cost_estimate=SMALL,
-    )(jnp.reshape(bit, (1,)), kept, came)
-
-
-def encode_body(kept_ref, came_ref, flips_ref, rotation_ref, out_ref):
+    )(facts, kept, came, *tokens)
+
+
+def encode_body(begin, facts_ref, kept_ref, came_ref, flips_ref, rotation_ref, *refs):
+    out_ref = refs[-1]
     rows, columns = kept_ref.shape
+    half = flips_ref.shape[1] // 2
     rotation = rotation_ref[...]
     lane = lax.broadcasted_iota(jnp.int32, (rows, BLOCK), 1)
     scales = jnp.zeros((rows, BLOCK), jnp.float32)
     for block in range(columns // BLOCK):
         at = slice(block * BLOCK, (block + 1) * BLOCK)
-        total = (kept_ref[:, at] + came_ref[:, at].astype(jnp.float32)) * flips_ref[:, at]
+        flips = flips_ref[:, pl.ds(pl.multiple_of(facts_ref[0] * half + begin + block * BLOCK, BLOCK), BLOCK)]
+        total = (kept_ref[:, at] + came_ref[:, at].astype(jnp.float32)) * flips
         rotated = jnp.dot(
             total, rotation, precision=lax.Precision.HIGHEST, preferred_element_type=jnp.float32
         )
@@ -197,19 +306,19 @@
     out_ref[:, columns:] = scales.astype(jnp.bfloat16)
 
 
-def encode(kept, came, flips):
+def encode(kept, came, begin, facts, flips, rotation, tokens=()):
     rows, columns = kept.shape
     return pl.pallas_call(
-        encode_body,
+        functools.partial(encode_body, begin),
         out_shape=jax.ShapeDtypeStruct((rows, columns + BLOCK), jnp.bfloat16),
-        in_specs=[VMEM] * 4,
+        in_specs=[SMEM] + [VMEM] * 4 + [ANY] * len(tokens),
         out_specs=VMEM,
         compiler_params=PARAMS,
         cost_estimate=SMALL,
-    )(kept, came, flips, hadamard(BLOCK))
-
-
-def choose_body(blocks, pieces, width, at, rank_ref, chosen_ref, *refs):
+    )(facts, kept, came, flips, rotation, *tokens)
+
+
+def choose_body(blocks, pieces, width, at, rank, chosen, places, facts_ref, *refs):
     out_ref = refs[-1]
     rows = refs[0].shape[0]
     scales = width // BLOCK
@@ -218,17 +327,17 @@
         begin, scale_at = at[block]
         for piece in range(pieces):
             ref = refs[block * pieces + piece]
-            row = (place * pieces + rank_ref[piece]) * rows
+            row = (place * pieces + facts_ref[rank + piece]) * rows
             here = pl.ds(pl.multiple_of(row, rows), rows)
             out_ref[here, :width] = ref[:, begin : begin + width]
             out_ref[here, width : width + scales] = ref[:, scale_at : scale_at + scales]
 
-    for place in range(chosen_ref.shape[0]):
+    for place in range(places):
         for block in range(blocks):
-            pl.when(chosen_ref[place] == block)(functools.partial(put, block, place))
-
-
-def choose(results, group, width, rank, chosen):
+            pl.when(facts_ref[chosen + place] == block)(functools.partial(put, block, place))
+
+
+def choose(results, group, width, rank, chosen, places, facts):
     picked, at = [], []
     for result in results:
         if len(result) == 1:
@@ -247,18 +356,18 @@
             for index, piece in enumerate(pieces):
                 scale = jnp.pad(piece[:, scale_at : scale_at + width // BLOCK], ((0, 0), (0, BLOCK - width // BLOCK)))
                 part = jnp.concatenate([piece[:, begin : begin + width], scale], axis=1)
-                block = lax.dynamic_update_slice_in_dim(block, part, rank[index] * rows, 0)
+                block = lax.dynamic_update_slice_in_dim(block, part, facts[rank + index] * rows, 0)
             blocks.append(block)
         stacked = jnp.stack(blocks)
-        return jnp.concatenate([stacked[chosen[place]] for place in range(chosen.shape[0])])
-    return pl.pallas_call(
-        functools.partial(choose_body, len(picked), count, width, at),
-        out_shape=jax.ShapeDtypeStruct((chosen.shape[0] * count * rows, width + BLOCK), jnp.bfloat16),
-        in_specs=[SMEM, SMEM] + [VMEM] * (len(picked) * count),
+        return jnp.concatenate([stacked[facts[chosen + place]] for place in range(places)])
+    return pl.pallas_call(
+        functools.partial(choose_body, len(picked), count, width, at, rank, chosen, places),
+        out_shape=jax.ShapeDtypeStruct((places * count * rows, width + BLOCK), jnp.bfloat16),
+        in_specs=[SMEM] + [VMEM] * (len(picked) * count),
         out_specs=VMEM,
         compiler_params=PARAMS,
         cost_estimate=SMALL,
-    )(rank, chosen, *[piece for pieces in picked for piece in pieces])
+    )(facts, *[piece for pieces in picked for piece in pieces])
 
 
 def assemble_body(groups, half, here_ref, *refs):
@@ -281,7 +390,7 @@
         pl.when(here_ref[0] == core)(functools.partial(put, core))
 
 
-def assemble(mine, other, here, half):
+def assemble(mine, other, facts, half):
     rows = mine[0].shape[0]
     codes, scales = pl.pallas_call(
         functools.partial(assemble_body, len(mine), half),
@@ -293,7 +402,7 @@
         out_specs=(VMEM, VMEM),
         compiler_params=PARAMS,
         cost_estimate=SMALL,
-    )(here, *mine, *other)
+    )(facts, *mine, *other)
     return codes, scales.T
 
 
@@ -301,11 +410,8 @@
     if depth % UNIT or depth < 8 * UNIT:
         return [depth]
     units = depth // UNIT
-    sizes = []
-    for share in (0.31, 0.31, 0.23):
-        sizes.append(max(1, round(units * share)))
-    sizes.append(units - sum(sizes))
-    return [size * UNIT for size in sizes]
+    sizes = [max(1, units * share // 13) for share in SHARES]
+    return [size * UNIT for size in sizes + [units - sum(sizes)]]
 
 
 def shards(hidden, down_weight, sign_bits):
@@ -319,11 +425,24 @@
     half = down_weight.shape[1] // sub_count
     per_sub = seq_count // sub_count
     levels = tensor_count.bit_length() - 1
-    bits = [tensor_at >> level & 1 for level in range(levels)]
     wide, wide_chunk = min(256, half // GROUPS), min(512, half // GROUPS)
     flips = (2 * sign_bits - 1).astype(jnp.float32)[None, :]
-    own_flips = lax.dynamic_slice_in_dim(flips, sub_at * half, half, 1)
-    here = jnp.reshape(sub_at, (1,)).astype(jnp.int32)
+    rotation = jnp.asarray(hadamard(BLOCK))
+
+    def rank_of(index):
+        return sum((index >> level & 1) << (levels - 1 - level) for level in range(levels))
+
+    def of_sub(sub):
+        return [lax.rem(seq_at - (sub * per_sub + place) + seq_count, seq_count) for place in range(per_sub)]
+
+    facts = [sub_at] + [tensor_at >> level & 1 for level in range(levels)]
+    ranks = len(facts)
+    facts += [rank_of(tensor_at ^ index) for index in range(tensor_count)]
+    own_choice = len(facts)
+    facts += of_sub(sub_at)
+    other_choice = len(facts)
+    facts += of_sub(1 - sub_at)
+    facts = jnp.stack(facts).astype(jnp.int32)
 
     def swap(values):
         return lax.ppermute(values, "sub", [(0, 1), (1, 0)])
@@ -332,14 +451,13 @@
         return lax.ppermute(values, "tensor", [(t, t ^ 1 << level) for t in range(tensor_count)])
 
     def reduce(sent, kept, begin):
+        tokens = (yield None) or []
         came = swap(sent)
-        tokens = []
         for level in range(levels):
-            sent, kept = halve(kept, came, bits[level])
-            tokens.append(sent)
+            sent, kept = halve(kept, came, level, facts, tokens)
+            tokens = (yield sent) or []
             came = exchange(sent, level)
-        packed = encode(kept, came, own_flips[:, begin : begin + kept.shape[1]])
-        return tokens, packed
+        yield encode(kept, came, begin, facts, flips, rotation, tokens)
 
     def spread(packed):
         pieces = {0: packed}
@@ -347,9 +465,6 @@
             for index in list(pieces):
                 pieces[index ^ 1 << level] = exchange(pieces[index], level)
         return [pieces[index] for index in range(tensor_count)]
-
-    def rank_of(index):
-        return sum((index >> level & 1) << (levels - 1 - level) for level in range(levels))
 
     sizes = cut(depth)
     places = [(sum(sizes[:index]), size) for index, size in enumerate(sizes)]
@@ -359,56 +474,58 @@
         pairs = [(s, (s + shift) % seq_count) for s in range(seq_count)]
         arrivals.append([lax.ppermute(part, "seq", pairs) for part in parts])
 
-    single = len(sizes) == 1
-    own = None
-    if not single:
-        rest = sizes[0]
-        (own,) = multiply(
-            [(hidden, rest)], down_weight, rest, depth - rest, here, [None], [False], wide, tokens=parts
+    if len(sizes) == 1:
+        outs = multiply(
+            [(parts[0], 0), (arrivals[0][0], 0)], down_weight, 0, depth, facts, [None, None], [True, True], wide_chunk
         )
-    outs = multiply(
-        [(hidden, 0), (arrivals[0][0], 0)], down_weight, 0, sizes[0], here, [own, None], [True, single], wide_chunk
-    )
-    (sent, kept), first = outs[:2], outs[2:]
-    own_tokens, own_packed = reduce(sent, kept, 0)
-    results = [[spread(own_packed)]]
-    for shift, arrived in enumerate(arrivals):
-        groups = 1 if single else GROUPS
-        reduced = []
-        if single:
+        reduced = [list(reduce(*outs[:2], 0))[-1], list(reduce(*outs[2:], 0))[-1]]
+        for arrived in arrivals[1:]:
+            outs = multiply([(arrived[0], 0)], down_weight, 0, depth, facts, [None], [True], wide_chunk)
+            reduced.append(list(reduce(*outs, 0))[-1])
+        results = [[spread(packed)] for packed in reduced]
+    else:
+        own, held = multiply_resident(
+            parts[1:], down_weight, sizes[0], wide, tokens=[parts[0], facts, flips, rotation]
+        )
+        sent, kept, total = multiply(
+            [(parts[0], 0), (arrivals[0][0], 0)], down_weight, 0, sizes[0], facts, [own, None], [True, False], wide
+        )
+        own_steps = reduce(sent, kept, 0)
+        next(own_steps)
+        own_packed, tokens = None, []
+        results = []
+        for shift, arrived in enumerate(arrivals):
             if shift:
-                first = multiply([(arrived[0], 0)], down_weight, 0, depth, here, [None], [True], wide_chunk)
-            reduced.append(reduce(*first, 0)[1])
-        else:
-            total = first[0] if shift == 0 else None
-            for index, (at, size) in enumerate(places):
-                if index == 0 and shift == 0:
-                    continue
-                if index == len(places) - 1:
-                    break
-                tokens = own_tokens[index - 1 : index] if shift == 0 else ()
-                (total,) = multiply(
-                    [(arrived[index], 0)], down_weight, at, size, here, [total], [False], wide_chunk, tokens=tokens
+                (total,) = multiply([(arrived[0], 0)], down_weight, 0, sizes[0], facts, [None], [False], wide)
+            for index in range(1, len(sizes) - 1):
+                (total,) = multiply_held(
+                    arrived[index], held, places[index][0] - sizes[0], facts, total, False, wide_chunk, tokens=tokens
                 )
-            tokens = [own_packed] if shift == 0 else ()
-            for group in range(groups):
-                sent, kept = multiply(
-                    [(arrived[index], 0)], down_weight, at, size, here, [total], [True], wide_chunk,
-                    group=(group, groups), tokens=tokens,
+                if own_packed is None:
+                    step = own_steps.send([total])
+                    tokens = [step]
+                    if step.shape[1] > half:
+                        own_packed = step
+            remote_steps = []
+            for group in range(GROUPS):
+                sent, kept = multiply_held(
+                    arrived[-1], held, places[-1][0] - sizes[0], facts, total, True, wide_chunk,
+                    group=(group, GROUPS), tokens=tokens,
                 )
                 tokens = [sent]
-                reduced.append(reduce(sent, kept, group * half // groups)[1])
-        results.append([spread(packed) for packed in reduced])
-
-    def of_sub(sub):
-        return jnp.stack([(seq_at - (sub * per_sub + place)) % seq_count for place in range(per_sub)])
-
-    rank = jnp.stack([rank_of(tensor_at ^ index) for index in range(tensor_count)])
+                remote_steps.append(reduce(sent, kept, group * half // GROUPS))
+            if own_packed is None:
+                own_packed = list(own_steps)[-1]
+            if not results:
+                results.append([spread(own_packed)])
+            results.append([spread(list(steps)[-1]) for steps in remote_steps])
+            tokens = []
+
     groups = max(len(result) for result in results)
     width = half // groups
-    other = [swap(choose(results, group, width, rank, of_sub(1 - sub_at))) for group in range(groups)]
-    mine = [choose(results, group, width, rank, of_sub(sub_at)) for group in range(groups)]
-    return assemble(mine, other, here, half)
+    other = [swap(choose(results, group, width, ranks, other_choice, per_sub, facts)) for group in range(groups)]
+    mine = [choose(results, group, width, ranks, own_choice, per_sub, facts) for group in range(groups)]
+    return assemble(mine, other, facts, half)
 
 
 def solution(mesh):

time: 109 us -> 171 us (1.57)
  local copies, waits for them, and re-layouts: 8.14 us -> 68.2 us
    unnamed x26 -> x16, local copies, waits for them, and re-layouts: 8.14 us -> 68.1 us
    pallas_call x6 -> x1, Pallas kernels: 40 us -> 8.34 us  [multiply(): pl.pallas_call(body, out_shape=out_shape, in_specs=[SMEM] + [VMEM] * len(...]
    pallas_call x9 -> x15, Pallas kernels: 5.19 us -> 35.6 us  [the longest x5 14.1 us: multiply_held(): pl.pallas_call(functools.partial(held_body, row, len(held), split, first,...]
    ppermute x4 -> x5, waiting for transfers between devices: 0.01 us -> 9.9 us  [shards(): arrivals.append([lax.ppermute(part, 'seq', pairs) for part in parts])]
    ppermute x15, waiting for transfers between devices: 23.8 us -> 16.5 us  [exchange(): lax.ppermute(values, 'tensor', [(t, t ^ 1 << level) for t in range(tensor...]
    ppermute x4 -> x5, starting transfers between devices: 5.79 us -> 7.12 us  [shards(): arrivals.append([lax.ppermute(part, 'seq', pairs) for part in parts])]
  transfers between devices with their start and end apart: 24 -> 25, of which waited for: 11 -> 13; matrix products, arithmetic and copies ran while one was open for 0% -> 0% of each run, Pallas kernels for 31% -> 20%
where the time goes in v5:
time: 171 us; the launch traced here: 170 us
  local copies, waits for them, and re-layouts  68.2 us (40%)
  Pallas kernels  48.1 us (28%)
  waiting for transfers between devices  27.7 us (16%)
  starting transfers between devices  24.6 us (14%)
    unnamed x16, local copies, waits for them, and re-layouts  68.1 us
    ppermute x15, starting transfers between devices, exchange(): lax.ppermute(values, 'tensor', [(t, t ^ 1 << level) for t in range(tensor...  16.7 us
    ppermute x15, waiting for transfers between devices, exchange(): lax.ppermute(values, 'tensor', [(t, t ^ 1 << level) for t in range(tensor...  16.5 us
    pallas_call x5, Pallas kernels, multiply_held(): pl.pallas_call(functools.partial(held_body, row, len(held), split, first,...  14.1 us
    pallas_call x1, Pallas kernels, multiply_resident(): pl.pallas_call(functools.partial(resident_body, sizes, row, len(tokens)),...  14 us
    ppermute x5, waiting for transfers between devices, shards(): arrivals.append([lax.ppermute(part, 'seq', pairs) for part in parts])  9.9 us
    pallas_call x1, Pallas kernels, multiply(): pl.pallas_call(body, out_shape=out_shape, in_specs=[SMEM] + [VMEM] * len(...  8.34 us
    ppermute x5, starting transfers between devices, shards(): arrivals.append([lax.ppermute(part, 'seq', pairs) for part in parts])  7.12 us
  transfers between devices with their start and end apart: 25, of which 13 were waited for; matrix products, arithmetic and copies ran while one was open for 0% of the time, Pallas kernels for 20%

profile of v5, /device:TPU:0, one launch (start us, length us, event | category | flops | bytes accessed | tf_op | source)
XLA Modules:
  0.0 170.4 jit_solution(912284100672710781)
XLA Ops:
  0.6 1.4 copy-done.5
  2.3 3.0 %collective-permute-start = (bf16[128,1536]{1,0:T(8,128)(2,1)S(1)}, bf16[128,1536]{1,0:T(8,128)(2,1)S(1)}, u32[]{:S(2)}, u32[]{:S(2)}) collective-permute-start(bf16[128,1536]{1,0:T(8,128)(2,1)S(1)} %get-tuple-element.30.refs_5_.refs_0_), channel_id=1, source_target_pairs={{0,2},{2,0},{1,3},{3,1},{4,6},{6,4},{5,7},{7,5},{8,10},{10,8},{9,1... | collective-permute-start | bytes 1179656 | tf_op jit(solution)/shard_map/ppermute | solution.py:475
  5.4 0.7 add_convert_fusion
  6.1 0.8 copy-done.6
  6.9 14.0 %shard_map.60 = (f32[128,4096]{1,0:T(8,128)S(1)}, bf16[5120,4096]{1,0:T(8,128)(2,1)S(1)}) custom-call(bf16[128,1536]{1,0:T(8,128)(2,1)S(1)} %get-tuple-element.31.refs_0_, bf16[128,1536]{1,0:T(8,128)(2,1)S(1)} %get-tuple-element.32.refs_1_, bf16[128,1024]{1,0:T(8,128)(2,1)S(1)} %get-tuple-element.33.refs_2_, ...), custom_call_target="tpu_custom_call" | custom-call | flops 1 | bytes 1 | tf_op jit(solution)/shard_map/pallas_call | solution.py:92
  20.9 13.8 %copy-done = bf16[5120,4096]{1,0:T(8,128)(2,1)} copy-done((bf16[5120,4096]{1,0:T(8,128)(2,1)}, bf16[5120,4096]{1,0:T(8,128)(2,1)S(1)}, u32[]{:S(2)}) %copy-start) | copy-done | bytes 41943064
  34.7 8.3 %shard_map.61 = (bf16[128,2048]{1,0:T(8,128)(2,1)S(1)}, f32[128,2048]{1,0:T(8,128)S(1)}, f32[128,4096]{1,0:T(8,128)S(1)}) custom-call(s32[9]{0:T(128)S(1)} %stack.39.refs_6_.here_ref.facts_ref, bf16[128,1536]{1,0:T(8,128)(2,1)S(1)} %get-tuple-element.30.refs_5_.refs_0_, bf16[128,1536]{1,0:T(8,128)(2,1)S(1)} %collective-permute-done.refs_1_, ...), custom_call_target="tpu_custom_call" | custom-call | flops 1 | bytes 1 | tf_op jit(solution)/shard_map/pallas_call | solution.py:237
  43.2 2.0 %collective-permute-start.4 = (bf16[128,1536]{1,0:T(8,128)(2,1)S(1)}, bf16[128,1536]{1,0:T(8,128)(2,1)S(1)}, u32[]{:S(2)}, u32[]{:S(2)}) collective-permute-start(bf16[128,1536]{1,0:T(8,128)(2,1)S(1)} %get-tuple-element.32.refs_1_), channel_id=1, source_target_pairs={{0,2},{2,0},{1,3},{3,1},{4,6},{6,4},{5,7},{7,5},{8,10},{10,8},{9,1... | collective-permute-start | bytes 1179656 | tf_op jit(solution)/shard_map/ppermute | solution.py:475
  45.2 9.9 %collective-permute-done.2.left_ref = bf16[128,1536]{1,0:T(8,128)(2,1)S(1)} collective-permute-done((bf16[128,1536]{1,0:T(8,128)(2,1)S(1)}, bf16[128,1536]{1,0:T(8,128)(2,1)S(1)}, u32[]{:S(2)}, u32[]{:S(2)}) %collective-permute-start.2) | collective-permute-done | bytes 393248 | tf_op jit(solution)/shard_map/ppermute | solution.py:475
  55.1 13.0 %copy-done.1 = bf16[5120,4096]{1,0:T(8,128)(2,1)S(1)} copy-done((bf16[5120,4096]{1,0:T(8,128)(2,1)S(1)}, bf16[5120,4096]{1,0:T(8,128)(2,1)}, u32[]{:S(2)}) %copy-start.1) | copy-done | bytes 41943064
  68.1 3.6 %shard_map.62.refs_0_ = f32[128,4096]{1,0:T(8,128)S(1)} custom-call(s32[9]{0:T(128)S(1)} %stack.39.refs_6_.here_ref.facts_ref, bf16[128,1536]{1,0:T(8,128)(2,1)S(1)} %collective-permute-done.2.left_ref, bf16[5120,4096]{1,0:T(8,128)(2,1)S(1)} %copy-done.1, f32[128,4096]{1,0:T(8,128)S(1)} %get-tuple-element.39.refs_0_), custom_call_target="tpu_custom_call" | custom-call | flops 1 | bytes 1 | tf_op jit(solution)/shard_map/pallas_call | solution.py:145
  71.8 0.6 shard_map.63
  72.4 1.6 collective-permute-start.3
  74.6 1.5 collective-permute-start.10
  76.1 13.0 %copy-done.2 = bf16[5120,4096]{1,0:T(8,128)(2,1)S(1)} copy-done((bf16[5120,4096]{1,0:T(8,128)(2,1)S(1)}, bf16[5120,4096]{1,0:T(8,128)(2,1)}, u32[]{:S(2)}) %copy-start.2) | copy-done | bytes 41943064
  89.1 3.7 %shard_map.64.refs_0_ = f32[128,4096]{1,0:T(8,128)S(1)} custom-call(s32[9]{0:T(128)S(1)} %stack.39.refs_6_.here_ref.facts_ref, bf16[128,1536]{1,0:T(8,128)(2,1)S(1)} %collective-permute-done.4.left_ref, bf16[5120,4096]{1,0:T(8,128)(2,1)S(1)} %copy-done.2, f32[128,4096]{1,0:T(8,128)S(1)} %shard_map.62.refs_0_, bf16[64,2048]{1,0:T(8,128)(2,1)S(1)} %get-tuple-element.41.refs_1_), custom_call_target="tpu_custom_call" | custom-call | flops 1 | bytes 1 | tf_op jit(solution)/shard_map/pallas_call | solution.py:145
  92.8 0.6 shard_map.65
  93.4 2.7 %collective-permute-start.5 = (bf16[32,2048]{1,0:T(8,128)(2,1)S(1)}, bf16[32,2048]{1,0:T(8,128)(2,1)S(1)}, u32[]{:S(2)}, u32[]{:S(2)}) collective-permute-start(bf16[32,2048]{1,0:T(8,128)(2,1)S(1)} %get-tuple-element.43.refs_1_), channel_id=1, source_target_pairs={{0,8},{4,12},{8,0},{12,4},{1,9},{5,13},{9,1},{13,5},{2,10},{6,14},... | collective-permute-start | bytes 393224 | tf_op jit(solution)/shard_map/ppermute | solution.py:451
  96.1 13.0 %copy-done.3 = bf16[5120,4096]{1,0:T(8,128)(2,1)S(1)} copy-done((bf16[5120,4096]{1,0:T(8,128)(2,1)S(1)}, bf16[5120,4096]{1,0:T(8,128)(2,1)}, u32[]{:S(2)}) %copy-start.3) | copy-done | bytes 41943064
  109.1 3.1 %shard_map.66.refs_0_ = f32[128,4096]{1,0:T(8,128)S(1)} custom-call(s32[9]{0:T(128)S(1)} %stack.39.refs_6_.here_ref.facts_ref, bf16[128,1024]{1,0:T(8,128)(2,1)S(1)} %collective-permute-done.6.left_ref, bf16[5120,4096]{1,0:T(8,128)(2,1)S(1)} %copy-done.3, f32[128,4096]{1,0:T(8,128)S(1)} %shard_map.64.refs_0_, bf16[32,2048]{1,0:T(8,128)(2,1)S(1)} %get-tuple-element.43.refs_1_), custom_call_target="tpu_custom_call" | custom-call | flops 1 | bytes 1 | tf_op jit(solution)/shard_map/pallas_call | solution.py:145
  112.3 1.6 shard_map.67.refs_1_.refs_0_
  113.9 13.0 %copy-done.4 = bf16[5120,4096]{1,0:T(8,128)(2,1)S(1)} copy-done((bf16[5120,4096]{1,0:T(8,128)(2,1)S(1)}, bf16[5120,4096]{1,0:T(8,128)(2,1)}, u32[]{:S(2)}) %copy-start.4) | copy-done | bytes 41943064
  126.9 1.8 %shard_map.68 = (bf16[128,1024]{1,0:T(8,128)(2,1)S(1)}, f32[128,1024]{1,0:T(8,128)S(1)}) custom-call(s32[9]{0:T(128)S(1)} %stack.39.refs_6_.here_ref.facts_ref, bf16[128,1024]{1,0:T(8,128)(2,1)S(1)} %collective-permute-done.10.left_ref, bf16[5120,4096]{1,0:T(8,128)(2,1)S(1)} %copy-done.4, f32[128,4096]{1,0:T(8,128)S(1)} %shard_map.66.refs_0_, ...), custom_call_target="tpu_custom_call" | custom-call | flops 1 | bytes 1 | tf_op jit(solution)/shard_map/pallas_call | solution.py:145
  128.7 1.8 %shard_map.73 = (bf16[128,1024]{1,0:T(8,128)(2,1)S(1)}, f32[128,1024]{1,0:T(8,128)S(1)}) custom-call(s32[9]{0:T(128)S(1)} %stack.39.refs_6_.here_ref.facts_ref, bf16[128,1024]{1,0:T(8,128)(2,1)S(1)} %collective-permute-done.10.left_ref, bf16[5120,4096]{1,0:T(8,128)(2,1)S(1)} %copy-done.4, f32[128,4096]{1,0:T(8,128)S(1)} %shard_map.66.refs_0_, ...), custom_call_target="tpu_custom_call" | custom-call | flops 1 | bytes 1 | tf_op jit(solution)/shard_map/pallas_call | solution.py:145
  131.1 1.0 collective-permute-done.17.came_ref
  132.1 0.6 shard_map.74
  133.2 0.6 shard_map.69
  133.9 1.7 collective-permute-start.12
  135.8 5.3 %collective-permute-done.18.came_ref = bf16[64,1024]{1,0:T(8,128)(2,1)S(1)} collective-permute-done((bf16[64,1024]{1,0:T(8,128)(2,1)S(1)}, bf16[64,1024]{1,0:T(8,128)(2,1)S(1)}, u32[]{:S(2)}, u32[]{:S(2)}) %collective-permute-start.18) | collective-permute-done | bytes 131104 | tf_op jit(solution)/shard_map/ppermute | solution.py:451
  141.8 1.7 %collective-permute-done.12.came_ref = bf16[64,1024]{1,0:T(8,128)(2,1)S(1)} collective-permute-done((bf16[64,1024]{1,0:T(8,128)(2,1)S(1)}, bf16[64,1024]{1,0:T(8,128)(2,1)S(1)}, u32[]{:S(2)}, u32[]{:S(2)}) %collective-permute-start.12) | collective-permute-done | bytes 131104 | tf_op jit(solution)/shard_map/ppermute | solution.py:451
  143.5 0.6 shard_map.70
  144.1 1.2 collective-permute-start.13
  145.3 0.9 collective-permute-start.7
  146.2 2.6 %collective-permute-done.19.came_ref = bf16[32,1024]{1,0:T(8,128)(2,1)S(1)} collective-permute-done((bf16[32,1024]{1,0:T(8,128)(2,1)S(1)}, bf16[32,1024]{1,0:T(8,128)(2,1)S(1)}, u32[]{:S(2)}, u32[]{:S(2)}) %collective-permute-start.19) | collective-permute-done | bytes 65568 | tf_op jit(solution)/shard_map/ppermute | solution.py:451
  148.8 1.2 shard_map.76.refs_4_
  150.3 1.2 shard_map.71.refs_4_
  151.5 2.7 %collective-permute-start.15 = (bf16[32,1152]{1,0:T(8,128)(2,1)S(1)}, bf16[32,1152]{1,0:T(8,128)(2,1)S(1)}, u32[]{:S(2)}, u32[]{:S(2)}) collective-permute-start(bf16[32,1152]{1,0:T(8,128)(2,1)S(1)} %shard_map.71.refs_4_), channel_id=1, source_target_pairs={{0,8},{4,12},{8,0},{12,4},{1,9},{5,13},{9,1},{13,5},{2,10},{6,14},... | collective-permute-start | bytes 221192 | tf_op jit(solution)/shard_map/ppermute | solution.py:451
  154.2 2.0 %collective-permute-start.20 = (bf16[32,1152]{1,0:T(8,128)(2,1)S(1)}, bf16[32,1152]{1,0:T(8,128)(2,1)S(1)}, u32[]{:S(2)}, u32[]{:S(2)}) collective-permute-start(bf16[32,1152]{1,0:T(8,128)(2,1)S(1)} %shard_map.76.refs_4_), channel_id=1, source_target_pairs={{0,4},{4,0},{8,12},{12,8},{1,5},{5,1},{9,13},{13,9},{2,6},{6,2},{1... | collective-permute-start | bytes 221192 | tf_op jit(solution)/shard_map/ppermute | solution.py:451
  156.3 2.0 %collective-permute-start.14 = (bf16[32,1152]{1,0:T(8,128)(2,1)S(1)}, bf16[32,1152]{1,0:T(8,128)(2,1)S(1)}, u32[]{:S(2)}, u32[]{:S(2)}) collective-permute-start(bf16[32,1152]{1,0:T(8,128)(2,1)S(1)} %shard_map.71.refs_4_), channel_id=1, source_target_pairs={{0,4},{4,0},{8,12},{12,8},{1,5},{5,1},{9,13},{13,9},{2,6},{6,2},{1... | collective-permute-start | bytes 221192 | tf_op jit(solution)/shard_map/ppermute | solution.py:451
  158.3 0.9 collective-permute-start.16
  159.3 1.6 collective-permute-done.9.refs_3_
  160.8 1.6 collective-permute-done.20.refs_5_
  162.4 1.6 collective-permute-done.22.refs_7_
  164.7 0.9 collective-permute-done.14.refs_5_
  165.6 0.9 collective-permute-done.16.refs_7_
  167.1 0.6 shard_map.72.refs_0_
  167.7 0.6 shard_map.77.refs_1_
  168.7 1.7 shard_map.80
  (42 shorter events, 5.0 us)
Async XLA Ops:
  0.6 1.5 copy-start.5
  2.3 32.4 %collective-permute-start = (bf16[128,1536]{1,0:T(8,128)(2,1)S(1)}, bf16[128,1536]{1,0:T(8,128)(2,1)S(1)}, u32[]{:S(2)}, u32[]{:S(2)}) collective-permute-start(bf16[128,1536]{1,0:T(8,128)(2,1)S(1)} %get-tuple-element.30.refs_5_.refs_0_), channel_id=1, source_target_pairs={{0,2},{2,0},{1,3},{3,1},{4,6},{6,4},{5,7},{7,5},{8,10},{10,8},{9,1... | collective-permute-start | bytes 1179656 | tf_op jit(solution)/shard_map/ppermute | solution.py:475
  6.1 0.8 copy-start.6
  20.9 13.8 %copy-start = (bf16[5120,4096]{1,0:T(8,128)(2,1)}, bf16[5120,4096]{1,0:T(8,128)(2,1)S(1)}, u32[]{:S(2)}) copy-start(bf16[5120,4096]{1,0:T(8,128)(2,1)S(1)} %get-tuple-element.38.w_ref) | copy-start | bytes 125829120
  43.1 28.7 %collective-permute-start.1 = (bf16[128,2048]{1,0:T(8,128)(2,1)S(1)}, bf16[128,2048]{1,0:T(8,128)(2,1)S(1)}, u32[]{:S(2)}, u32[]{:S(2)}) collective-permute-start(bf16[128,2048]{1,0:T(8,128)(2,1)S(1)} %get-tuple-element.37), channel_id=1, source_target_pairs={{0,1},{1,0},{2,3},{3,2},{4,5},{5,4},{6,7},{7,6},{8,9},{9,8},{10,11... | collective-permute-start | bytes 1572872 | tf_op jit(solution)/shard_map/ppermute | solution.py:448
  43.1 12.0 %collective-permute-start.2 = (bf16[128,1536]{1,0:T(8,128)(2,1)S(1)}, bf16[128,1536]{1,0:T(8,128)(2,1)S(1)}, u32[]{:S(2)}, u32[]{:S(2)}) collective-permute-start(bf16[128,1536]{1,0:T(8,128)(2,1)S(1)} %get-tuple-element.31.refs_0_), channel_id=1, source_target_pairs={{0,2},{2,0},{1,3},{3,1},{4,6},{6,4},{5,7},{7,5},{8,10},{10,8},{9,1... | collective-permute-start | bytes 1179656 | tf_op jit(solution)/shard_map/ppermute | solution.py:475
  43.2 32.9 %collective-permute-start.4 = (bf16[128,1536]{1,0:T(8,128)(2,1)S(1)}, bf16[128,1536]{1,0:T(8,128)(2,1)S(1)}, u32[]{:S(2)}, u32[]{:S(2)}) collective-permute-start(bf16[128,1536]{1,0:T(8,128)(2,1)S(1)} %get-tuple-element.32.refs_1_), channel_id=1, source_target_pairs={{0,2},{2,0},{1,3},{3,1},{4,6},{6,4},{5,7},{7,5},{8,10},{10,8},{9,1... | collective-permute-start | bytes 1179656 | tf_op jit(solution)/shard_map/ppermute | solution.py:475
  55.1 13.0 %copy-start.1 = (bf16[5120,4096]{1,0:T(8,128)(2,1)S(1)}, bf16[5120,4096]{1,0:T(8,128)(2,1)}, u32[]{:S(2)}) copy-start(bf16[5120,4096]{1,0:T(8,128)(2,1)} %copy-done) | copy-start | bytes 125829120
  72.4 20.4 %collective-permute-start.3 = (bf16[64,2048]{1,0:T(8,128)(2,1)S(1)}, bf16[64,2048]{1,0:T(8,128)(2,1)S(1)}, u32[]{:S(2)}, u32[]{:S(2)}) collective-permute-start(bf16[64,2048]{1,0:T(8,128)(2,1)S(1)} %get-tuple-element.41.refs_1_), channel_id=1, source_target_pairs={{0,4},{4,0},{8,12},{12,8},{1,5},{5,1},{9,13},{13,9},{2,6},{6,2},{1... | collective-permute-start | bytes 786440 | tf_op jit(solution)/shard_map/ppermute | solution.py:451
  74.1 22.0 %collective-permute-start.6 = (bf16[128,1024]{1,0:T(8,128)(2,1)S(1)}, bf16[128,1024]{1,0:T(8,128)(2,1)S(1)}, u32[]{:S(2)}, u32[]{:S(2)}) collective-permute-start(bf16[128,1024]{1,0:T(8,128)(2,1)S(1)} %get-tuple-element.33.refs_2_), channel_id=1, source_target_pairs={{0,2},{2,0},{1,3},{3,1},{4,6},{6,4},{5,7},{7,5},{8,10},{10,8},{9,1... | collective-permute-start | bytes 786440 | tf_op jit(solution)/shard_map/ppermute | solution.py:475
  74.6 39.2 %collective-permute-start.10 = (bf16[128,1024]{1,0:T(8,128)(2,1)S(1)}, bf16[128,1024]{1,0:T(8,128)(2,1)S(1)}, u32[]{:S(2)}, u32[]{:S(2)}) collective-permute-start(bf16[128,1024]{1,0:T(8,128)(2,1)S(1)} %get-tuple-element.34.refs_3_), channel_id=1, source_target_pairs={{0,2},{2,0},{1,3},{3,1},{4,6},{6,4},{5,7},{7,5},{8,10},{10,8},{9,1... | collective-permute-start | bytes 786440 | tf_op jit(solution)/shard_map/ppermute | solution.py:475
  76.1 13.0 %copy-start.2 = (bf16[5120,4096]{1,0:T(8,128)(2,1)S(1)}, bf16[5120,4096]{1,0:T(8,128)(2,1)}, u32[]{:S(2)}) copy-start(bf16[5120,4096]{1,0:T(8,128)(2,1)} %copy-done) | copy-start | bytes 125829120
  93.4 18.8 %collective-permute-start.5 = (bf16[32,2048]{1,0:T(8,128)(2,1)S(1)}, bf16[32,2048]{1,0:T(8,128)(2,1)S(1)}, u32[]{:S(2)}, u32[]{:S(2)}) collective-permute-start(bf16[32,2048]{1,0:T(8,128)(2,1)S(1)} %get-tuple-element.43.refs_1_), channel_id=1, source_target_pairs={{0,8},{4,12},{8,0},{12,4},{1,9},{5,13},{9,1},{13,5},{2,10},{6,14},... | collective-permute-start | bytes 393224 | tf_op jit(solution)/shard_map/ppermute | solution.py:451
  96.1 13.0 %copy-start.3 = (bf16[5120,4096]{1,0:T(8,128)(2,1)S(1)}, bf16[5120,4096]{1,0:T(8,128)(2,1)}, u32[]{:S(2)}) copy-start(bf16[5120,4096]{1,0:T(8,128)(2,1)} %copy-done) | copy-start | bytes 125829120
  109.1 3.1 %copy-start.7 = (f32[128,128]{1,0:T(8,128)S(1)}, f32[128,128]{1,0:T(8,128)}, u32[]{:S(2)}) copy-start(f32[128,128]{1,0:T(8,128)} %constant.29.clone.refs_8_.rotation_ref) | copy-start | bytes 196612
  113.9 13.0 %copy-start.4 = (bf16[5120,4096]{1,0:T(8,128)(2,1)S(1)}, bf16[5120,4096]{1,0:T(8,128)(2,1)}, u32[]{:S(2)}) copy-start(bf16[5120,4096]{1,0:T(8,128)(2,1)} %copy-done) | copy-start | bytes 125829120
  130.5 1.6 collective-permute-start.17
  130.6 2.6 %collective-permute-start.11 = (bf16[128,1024]{1,0:T(8,128)(2,1)S(1)}, bf16[128,1024]{1,0:T(8,128)(2,1)S(1)}, u32[]{:S(2)}, u32[]{:S(2)}) collective-permute-start(bf16[128,1024]{1,0:T(8,128)(2,1)S(1)} %get-tuple-element.45.refs_1_), channel_id=1, source_target_pairs={{0,1},{1,0},{2,3},{3,2},{4,5},{5,4},{6,7},{7,6},{8,9},{9,8},{10,11... | collective-permute-start | bytes 786440 | tf_op jit(solution)/shard_map/ppermute | solution.py:448
  132.8 8.3 %collective-permute-start.18 = (bf16[64,1024]{1,0:T(8,128)(2,1)S(1)}, bf16[64,1024]{1,0:T(8,128)(2,1)S(1)}, u32[]{:S(2)}, u32[]{:S(2)}) collective-permute-start(bf16[64,1024]{1,0:T(8,128)(2,1)S(1)} %get-tuple-element.53), channel_id=1, source_target_pairs={{0,4},{4,0},{8,12},{12,8},{1,5},{5,1},{9,13},{13,9},{2,6},{6,2},{1... | collective-permute-start | bytes 393224 | tf_op jit(solution)/shard_map/ppermute | solution.py:451
  133.9 9.7 %collective-permute-start.12 = (bf16[64,1024]{1,0:T(8,128)(2,1)S(1)}, bf16[64,1024]{1,0:T(8,128)(2,1)S(1)}, u32[]{:S(2)}, u32[]{:S(2)}) collective-permute-start(bf16[64,1024]{1,0:T(8,128)(2,1)S(1)} %get-tuple-element.47), channel_id=1, source_target_pairs={{0,4},{4,0},{8,12},{12,8},{1,5},{5,1},{9,13},{13,9},{2,6},{6,2},{1... | collective-permute-start | bytes 393224 | tf_op jit(solution)/shard_map/ppermute | solution.py:451
  135.6 18.7 %collective-permute-start.8 = (bf16[32,2176]{1,0:T(8,128)(2,1)S(1)}, bf16[32,2176]{1,0:T(8,128)(2,1)S(1)}, u32[]{:S(2)}, u32[]{:S(2)}) collective-permute-start(bf16[32,2176]{1,0:T(8,128)(2,1)S(1)} %shard_map.67.refs_1_.refs_0_), channel_id=1, source_target_pairs={{0,8},{4,12},{8,0},{12,4},{1,9},{5,13},{9,1},{13,5},{2,10},{6,14},... | collective-permute-start | bytes 417800 | tf_op jit(solution)/shard_map/ppermute | solution.py:451
  141.7 7.1 %collective-permute-start.19 = (bf16[32,1024]{1,0:T(8,128)(2,1)S(1)}, bf16[32,1024]{1,0:T(8,128)(2,1)S(1)}, u32[]{:S(2)}, u32[]{:S(2)}) collective-permute-start(bf16[32,1024]{1,0:T(8,128)(2,1)S(1)} %get-tuple-element.55), channel_id=1, source_target_pairs={{0,8},{4,12},{8,0},{12,4},{1,9},{5,13},{9,1},{13,5},{2,10},{6,14},... | collective-permute-start | bytes 196616 | tf_op jit(solution)/shard_map/ppermute | solution.py:451
  144.1 6.2 %collective-permute-start.13 = (bf16[32,1024]{1,0:T(8,128)(2,1)S(1)}, bf16[32,1024]{1,0:T(8,128)(2,1)S(1)}, u32[]{:S(2)}, u32[]{:S(2)}) collective-permute-start(bf16[32,1024]{1,0:T(8,128)(2,1)S(1)} %get-tuple-element.49), channel_id=1, source_target_pairs={{0,8},{4,12},{8,0},{12,4},{1,9},{5,13},{9,1},{13,5},{2,10},{6,14},... | collective-permute-start | bytes 196616 | tf_op jit(solution)/shard_map/ppermute | solution.py:451
  145.3 11.0 %collective-permute-start.7 = (bf16[32,2176]{1,0:T(8,128)(2,1)S(1)}, bf16[32,2176]{1,0:T(8,128)(2,1)S(1)}, u32[]{:S(2)}, u32[]{:S(2)}) collective-permute-start(bf16[32,2176]{1,0:T(8,128)(2,1)S(1)} %shard_map.67.refs_1_.refs_0_), channel_id=1, source_target_pairs={{0,4},{4,0},{8,12},{12,8},{1,5},{5,1},{9,13},{13,9},{2,6},{6,2},{1... | collective-permute-start | bytes 417800 | tf_op jit(solution)/shard_map/ppermute | solution.py:451
  150.0 6.3 %collective-permute-start.21 = (bf16[32,1152]{1,0:T(8,128)(2,1)S(1)}, bf16[32,1152]{1,0:T(8,128)(2,1)S(1)}, u32[]{:S(2)}, u32[]{:S(2)}) collective-permute-start(bf16[32,1152]{1,0:T(8,128)(2,1)S(1)} %shard_map.76.refs_4_), channel_id=1, source_target_pairs={{0,8},{4,12},{8,0},{12,4},{1,9},{5,13},{9,1},{13,5},{2,10},{6,14},... | collective-permute-start | bytes 221192 | tf_op jit(solution)/shard_map/ppermute | solution.py:451
  151.5 6.9 %collective-permute-start.15 = (bf16[32,1152]{1,0:T(8,128)(2,1)S(1)}, bf16[32,1152]{1,0:T(8,128)(2,1)S(1)}, u32[]{:S(2)}, u32[]{:S(2)}) collective-permute-start(bf16[32,1152]{1,0:T(8,128)(2,1)S(1)} %shard_map.71.refs_4_), channel_id=1, source_target_pairs={{0,8},{4,12},{8,0},{12,4},{1,9},{5,13},{9,1},{13,5},{2,10},{6,14},... | collective-permute-start | bytes 221192 | tf_op jit(solution)/shard_map/ppermute | solution.py:451
  154.2 6.6 %collective-permute-start.9 = (bf16[32,2176]{1,0:T(8,128)(2,1)S(1)}, bf16[32,2176]{1,0:T(8,128)(2,1)S(1)}, u32[]{:S(2)}, u32[]{:S(2)}) collective-permute-start(bf16[32,2176]{1,0:T(8,128)(2,1)S(1)} %collective-permute-done.8.refs_2_), channel_id=1, source_target_pairs={{0,4},{4,0},{8,12},{12,8},{1,5},{5,1},{9,13},{13,9},{2,6},{6,2},{1... | collective-permute-start | bytes 417800 | tf_op jit(solution)/shard_map/ppermute | solution.py:451
  154.2 8.2 %collective-permute-start.20 = (bf16[32,1152]{1,0:T(8,128)(2,1)S(1)}, bf16[32,1152]{1,0:T(8,128)(2,1)S(1)}, u32[]{:S(2)}, u32[]{:S(2)}) collective-permute-start(bf16[32,1152]{1,0:T(8,128)(2,1)S(1)} %shard_map.76.refs_4_), channel_id=1, source_target_pairs={{0,4},{4,0},{8,12},{12,8},{1,5},{5,1},{9,13},{13,9},{2,6},{6,2},{1... | collective-permute-start | bytes 221192 | tf_op jit(solution)/shard_map/ppermute | solution.py:451
  156.3 7.7 %collective-permute-start.22 = (bf16[32,1152]{1,0:T(8,128)(2,1)S(1)}, bf16[32,1152]{1,0:T(8,128)(2,1)S(1)}, u32[]{:S(2)}, u32[]{:S(2)}) collective-permute-start(bf16[32,1152]{1,0:T(8,128)(2,1)S(1)} %collective-permute-done.21.refs_6_), channel_id=1, source_target_pairs={{0,4},{4,0},{8,12},{12,8},{1,5},{5,1},{9,13},{13,9},{2,6},{6,2},{1... | collective-permute-start | bytes 221192 | tf_op jit(solution)/shard_map/ppermute | solution.py:451
  156.3 9.2 %collective-permute-start.14 = (bf16[32,1152]{1,0:T(8,128)(2,1)S(1)}, bf16[32,1152]{1,0:T(8,128)(2,1)S(1)}, u32[]{:S(2)}, u32[]{:S(2)}) collective-permute-start(bf16[32,1152]{1,0:T(8,128)(2,1)S(1)} %shard_map.71.refs_4_), channel_id=1, source_target_pairs={{0,4},{4,0},{8,12},{12,8},{1,5},{5,1},{9,13},{13,9},{2,6},{6,2},{1... | collective-permute-start | bytes 221192 | tf_op jit(solution)/shard_map/ppermute | solution.py:451
  158.3 8.1 %collective-permute-start.16 = (bf16[32,1152]{1,0:T(8,128)(2,1)S(1)}, bf16[32,1152]{1,0:T(8,128)(2,1)S(1)}, u32[]{:S(2)}, u32[]{:S(2)}) collective-permute-start(bf16[32,1152]{1,0:T(8,128)(2,1)S(1)} %collective-permute-done.15.refs_6_), channel_id=1, source_target_pairs={{0,4},{4,0},{8,12},{12,8},{1,5},{5,1},{9,13},{13,9},{2,6},{6,2},{1... | collective-permute-start | bytes 221192 | tf_op jit(solution)/shard_map/ppermute | solution.py:451
  164.6 3.8 %collective-permute-start.24 = (bf16[128,1152]{1,0:T(8,128)(2,1)S(1)}, bf16[128,1152]{1,0:T(8,128)(2,1)S(1)}, u32[]{:S(2)}, u32[]{:S(2)}) collective-permute-start(bf16[128,1152]{1,0:T(8,128)(2,1)S(1)} %shard_map.79), channel_id=1, source_target_pairs={{0,1},{1,0},{2,3},{3,2},{4,5},{5,4},{6,7},{7,6},{8,9},{9,8},{10,11... | collective-permute-start | bytes 884744 | tf_op jit(solution)/shard_map/ppermute | solution.py:448
  167.0 1.6 collective-permute-start.23

commit v6 on v5

--- a/solution.py
+++ b/solution.py
@@ -12,9 +12,8 @@
 BLOCK = 128
 UNIT = 512
 GROUPS = 2
-BUFFERS = 4
 VMEM_LIMIT = 6 * 2**20
-SHARES = (3, 3, 3, 2)
+SHARES = (4, 4, 3)
 epsilon = 1e-06
 
 SMALL = pl.CostEstimate(flops=1, bytes_accessed=1, transcendentals=0)
@@ -57,141 +56,42 @@
     )(values)
 
 
-def resident_body(sizes, row, lead, *refs):
-    left_refs, w_ref, refs = refs[: len(sizes)], refs[len(sizes)], refs[len(sizes) + 1 :]
-    out_ref, held_ref, sems = refs[lead:]
-    columns = w_ref.shape[1]
-    steps, wide = sems.shape[0], columns // sems.shape[0]
-
-    def at(n):
-        return pl.ds(pl.multiple_of(n * wide, wide), wide)
-
-    def copy(n):
-        return pltpu.make_async_copy(w_ref.at[pl.ds(row, sum(sizes)), at(n)], held_ref.at[:, at(n)], sems.at[n])
-
-    for n in range(steps):
-        copy(n).start()
-
-    def step(n):
-        copy(n).wait()
-        total, begin = None, 0
-        for left_ref, size in zip(left_refs, sizes):
-            product = jnp.dot(
-                left_ref[...], held_ref[begin : begin + size, at(n)], preferred_element_type=jnp.float32
-            )
-            total = product if total is None else total + product
-            begin += size
-        out_ref[:, at(n)] = total
-
-    pl.loop(0, steps)(step)
-
-
-def multiply_resident(lefts, weight, row, wide, tokens=()):
-    rows, columns = lefts[0].shape[0], weight.shape[1]
-    sizes = [left.shape[1] for left in lefts]
-    return pl.pallas_call(
-        functools.partial(resident_body, sizes, row, len(tokens)),
-        out_shape=[
-            jax.ShapeDtypeStruct((rows, columns), jnp.float32),
-            jax.ShapeDtypeStruct((sum(sizes), columns), weight.dtype),
-        ],
-        in_specs=[VMEM] * len(lefts) + [HBM] + [ANY] * len(tokens),
-        out_specs=[VMEM, VMEM],
-        scratch_shapes=[pltpu.SemaphoreType.DMA((columns // wide,))],
-        compiler_params=PARAMS,
-        cost_estimate=SMALL,
-    )(*lefts, weight, *tokens)
-
-
-def held_body(row, has_total, split, first, number, wide, here_ref, left_ref, w_ref, *refs):
-    total_refs, out_refs = refs[:has_total], refs[len(refs) - 1 - split :]
-    in_half = w_ref.shape[1] // wide // 2
-    steps = 2 * first if split else 2 * in_half
-
-    def at(block):
-        return pl.ds(pl.multiple_of(block * wide, wide), wide)
-
-    def step(n, second):
-        block = n
-        if split:
-            block = (here_ref[0] if second else 1 - here_ref[0]) * in_half + number * first + n
-            block = block - (first if second else 0)
-        value = jnp.dot(left_ref[...], w_ref[row : row + left_ref.shape[1], at(block)], preferred_element_type=jnp.float32)
-        if has_total:
-            value = value + total_refs[0][:, at(block)]
-        if second:
-            out_refs[1][:, at(n - first)] = value
-        else:
-            out_refs[0][:, at(n)] = value.astype(out_refs[0].dtype)
-
-    if split:
-        pl.loop(0, first)(functools.partial(step, second=False))
-        pl.loop(first, steps)(functools.partial(step, second=True))
-    else:
-        pl.loop(0, steps)(functools.partial(step, second=False))
-
-
-def multiply_held(left, weight, row, facts, total, split, wide, group=(0, 1), tokens=()):
-    rows, columns = left.shape[0], weight.shape[1]
-    number, count = group
-    first = columns // wide // 2 // count
-    out_shape = [jax.ShapeDtypeStruct((rows, columns), jnp.float32)]
-    if split:
-        out_shape = [
-            jax.ShapeDtypeStruct((rows, first * wide), jnp.bfloat16),
-            jax.ShapeDtypeStruct((rows, first * wide), jnp.float32),
-        ]
-    held = [] if total is None else [total]
-    return pl.pallas_call(
-        functools.partial(held_body, row, len(held), split, first, number, wide),
-        out_shape=out_shape,
-        in_specs=[SMEM, VMEM, VMEM] + [VMEM] * len(held) + [ANY] * len(tokens),
-        out_specs=[VMEM] * len(out_shape),
-        compiler_params=PARAMS,
-        cost_estimate=SMALL,
-    )(facts, left, weight, *held, *tokens)
-
-
-def multiply_body(offsets, has_totals, splits, row, first, number, here_ref, *refs):
-    lefts = len(offsets)
-    left_refs, refs = refs[:lefts], refs[lefts:]
+def multiply_body(spans, has_totals, splits, row, first, number, facts_ref, *refs):
+    lefts = [refs[begin:end] for begin, end in spans]
+    refs = refs[spans[-1][1] :]
     w_ref, refs = refs[0], refs[1:]
     total_refs, refs = list(refs[: sum(has_totals)]), refs[sum(has_totals) :]
     buffer, arrived = refs[-2:]
     out_count = sum(2 if split else 1 for split in splits)
     out_refs = refs[-2 - out_count : -2]
-    buffers, depth, wide = buffer.shape
-    rows = left_refs[0].shape[0]
+    steps, depth, wide = buffer.shape
+    rows = lefts[0][0].shape[0]
     in_half = w_ref.shape[1] // wide // 2
-    steps = 2 * first if any(splits) else 2 * in_half
 
     def column(n):
         if not any(splits):
             return n
-        side = jnp.where(n < first, 1 - here_ref[0], here_ref[0])
+        side = jnp.where(n < first, 1 - facts_ref[0], facts_ref[0])
         return side * in_half + number * first + n - jnp.where(n < first, 0, first)
 
     def at(block):
         return pl.ds(pl.multiple_of(block * wide, wide), wide)
 
     def copy(n):
-        slot = lax.rem(n, buffers)
-        return pltpu.make_async_copy(
-            w_ref.at[pl.ds(row, depth), at(column(n))], buffer.at[slot], arrived.at[slot]
-        )
+        return pltpu.make_async_copy(w_ref.at[pl.ds(row, depth), at(column(n))], buffer.at[n], arrived.at[n])
 
     def step(n, second):
         copy(n).wait()
-
-        @pl.when(n + buffers - 1 < steps)
-        def _():
-            copy(n + buffers - 1).start()
-
-        parts = [ref[:, offset : offset + depth] for ref, offset in zip(left_refs, offsets)]
-        left = parts[0] if lefts == 1 else jnp.concatenate(parts, axis=0)
-        product = jnp.dot(left, buffer[lax.rem(n, buffers)], preferred_element_type=jnp.float32)
+        product, begin = None, 0
+        for index in range(len(lefts[0])):
+            parts = [left[index][...] for left in lefts]
+            left = parts[0] if len(parts) == 1 else jnp.concatenate(parts, axis=0)
+            end = begin + left.shape[1]
+            part = jnp.dot(left, buffer[n, begin:end], preferred_element_type=jnp.float32)
+            product = part if product is None else product + part
+            begin = end
         totals, outs = list(total_refs), list(out_refs)
-        for index in range(lefts):
+        for index in range(len(lefts)):
             value = product[index * rows : (index + 1) * rows]
             if has_totals[index]:
                 value = value + totals.pop(0)[:, at(column(n))]
@@ -204,17 +104,20 @@
             else:
                 outs.pop(0)[:, at(column(n))] = value
 
-    for n in range(min(buffers - 1, steps)):
-        copy(jnp.int32(n)).start()
+    for n in range(steps):
+        copy(n).start()
     pl.loop(0, first)(functools.partial(step, second=False))
     pl.loop(first, steps)(functools.partial(step, second=True))
 
 
-def multiply(lefts, weight, row, depth, facts, totals, splits, wide, group=None, tokens=()):
+def multiply(lefts, weight, row, facts, totals, splits, wide, group=(0, 1), tokens=()):
     rows = lefts[0][0].shape[0]
+    depth = sum(part.shape[1] for part in lefts[0])
     columns = weight.shape[1]
-    number, count = group or (0, 1)
+    number, count = group
     first = columns // wide // 2 // count
+    steps = 2 * first if any(splits) else columns // wide
+    spans = [(index * len(left), (index + 1) * len(left)) for index, left in enumerate(lefts)]
     held = [total for total in totals if total is not None]
     out_shape = []
     for split in splits:
@@ -226,30 +129,26 @@
         else:
             out_shape.append(jax.ShapeDtypeStruct((rows, columns), jnp.float32))
     body = functools.partial(
-        multiply_body,
-        [offset for _, offset in lefts],
-        [total is not None for total in totals],
-        splits,
-        row,
-        first,
-        number,
+        multiply_body, spans, [total is not None for total in totals], splits, row, first, number
     )
     return pl.pallas_call(
         body,
         out_shape=out_shape,
         in_specs=[SMEM]
-        + [VMEM] * len(lefts)
+        + [VMEM] * spans[-1][1]
         + [HBM]
         + [VMEM] * len(held)
         + [ANY] * len(tokens),
         out_specs=[VMEM] * len(out_shape),
         scratch_shapes=[
-            pltpu.VMEM((BUFFERS, depth, wide), weight.dtype),
-            pltpu.SemaphoreType.DMA((BUFFERS,)),
+            pltpu.VMEM((steps, depth, wide), weight.dtype),
+            pltpu.SemaphoreType.DMA((steps,)),
         ],
-        compiler_params=PARAMS,
-        cost_estimate=SMALL,
-    )(facts, *[left for left, _ in lefts], weight, *held, *tokens)
+        compiler_params=pltpu.CompilerParams(
+            vmem_limit_bytes=2 * steps * depth * wide + VMEM_LIMIT
+        ),
+        cost_estimate=SMALL,
+    )(facts, *[part for left in lefts for part in left], weight, *held, *tokens)
 
 
 def halve_body(level, facts_ref, kept_ref, came_ref, *refs):
@@ -476,19 +375,20 @@
 
     if len(sizes) == 1:
         outs = multiply(
-            [(parts[0], 0), (arrivals[0][0], 0)], down_weight, 0, depth, facts, [None, None], [True, True], wide_chunk
+            [[parts[0]], [arrivals[0][0]]], down_weight, 0, facts, [None, None], [True, True], wide_chunk
         )
         reduced = [list(reduce(*outs[:2], 0))[-1], list(reduce(*outs[2:], 0))[-1]]
         for arrived in arrivals[1:]:
-            outs = multiply([(arrived[0], 0)], down_weight, 0, depth, facts, [None], [True], wide_chunk)
+            outs = multiply([[arrived[0]]], down_weight, 0, facts, [None], [True], wide_chunk)
             reduced.append(list(reduce(*outs, 0))[-1])
         results = [[spread(packed)] for packed in reduced]
     else:
-        own, held = multiply_resident(
-            parts[1:], down_weight, sizes[0], wide, tokens=[parts[0], facts, flips, rotation]
+        (own,) = multiply(
+            [parts[1:]], down_weight, sizes[0], facts, [None], [False], wide,
+            tokens=[parts[0], flips, rotation],
         )
         sent, kept, total = multiply(
-            [(parts[0], 0), (arrivals[0][0], 0)], down_weight, 0, sizes[0], facts, [own, None], [True, False], wide
+            [[parts[0]], [arrivals[0][0]]], down_weight, 0, facts, [own, None], [True, False], wide_chunk
         )
         own_steps = reduce(sent, kept, 0)
         next(own_steps)
@@ -496,10 +396,10 @@
         results = []
         for shift, arrived in enumerate(arrivals):
             if shift:
-                (total,) = multiply([(arrived[0], 0)], down_weight, 0, sizes[0], facts, [None], [False], wide)
+                (total,) = multiply([[arrived[0]]], down_weight, 0, facts, [None], [False], wide_chunk)
             for index in range(1, len(sizes) - 1):
-                (total,) = multiply_held(
-                    arrived[index], held, places[index][0] - sizes[0], facts, total, False, wide_chunk, tokens=tokens
+                (total,) = multiply(
+                    [[arrived[index]]], down_weight, places[index][0], facts, [total], [False], wide_chunk, tokens=tokens
                 )
                 if own_packed is None:
                     step = own_steps.send([total])
@@ -508,14 +408,15 @@
                         own_packed = step
             remote_steps = []
             for group in range(GROUPS):
-                sent, kept = multiply_held(
-                    arrived[-1], held, places[-1][0] - sizes[0], facts, total, True, wide_chunk,
+                sent, kept = multiply(
+                    [[arrived[-1]]], down_weight, places[-1][0], facts, [total], [True], wide_chunk,
                     group=(group, GROUPS), tokens=tokens,
                 )
                 tokens = [sent]
                 remote_steps.append(reduce(sent, kept, group * half // GROUPS))
-            if own_packed is None:
-                own_packed = list(own_steps)[-1]
+                if own_packed is None:
+                    own_packed = own_steps.send(tokens)
+                    tokens = [own_packed]
             if not results:
                 results.append([spread(own_packed)])
             results.append([spread(list(steps)[-1]) for steps in remote_steps])

time: 171 us -> 98.8 us (0.58)
  local copies, waits for them, and re-layouts: 68.2 us -> 2.37 us
  waiting for transfers between devices: 27.7 us -> 13.9 us
  starting transfers between devices: 24.6 us -> 29 us
  Pallas kernels: 48.1 us -> 51.7 us
    unnamed x16 -> x4, local copies, waits for them, and re-layouts: 68.1 us -> 2.29 us
    ppermute x5 -> x4, waiting for transfers between devices: 9.9 us -> 0.01 us  [shards(): arrivals.append([lax.ppermute(part, 'seq', pairs) for part in parts])]
    ppermute x15, starting transfers between devices: 16.7 us -> 23 us  [exchange(): lax.ppermute(values, 'tensor', [(t, t ^ 1 << level) for t in range(tensor...]
    pallas_call x7 -> x6, Pallas kernels: 36.4 us -> 40 us  [multiply(): pl.pallas_call(body, out_shape=out_shape, in_specs=[SMEM] + [VMEM] * span...]
    ppermute x15, waiting for transfers between devices: 16.5 us -> 13.3 us  [exchange(): lax.ppermute(values, 'tensor', [(t, t ^ 1 << level) for t in range(tensor...]
    ppermute x5 -> x4, starting transfers between devices: 7.12 us -> 5.63 us  [shards(): arrivals.append([lax.ppermute(part, 'seq', pairs) for part in parts])]
  transfers between devices with their start and end apart: 25 -> 24, of which waited for: 13 -> 13; matrix products, arithmetic and copies ran while one was open for 0% -> 1% of each run, Pallas kernels for 20% -> 51%
where the time goes in v6:
time: 98.8 us; the launch traced here: 98.5 us
  Pallas kernels  51.7 us (52%)
  starting transfers between devices  29 us (29%)
  waiting for transfers between devices  13.9 us (14%)
  local copies, waits for them, and re-layouts  2.37 us (2%)
    pallas_call x6, Pallas kernels, multiply(): pl.pallas_call(body, out_shape=out_shape, in_specs=[SMEM] + [VMEM] * span...  40 us
    ppermute x15, starting transfers between devices, exchange(): lax.ppermute(values, 'tensor', [(t, t ^ 1 << level) for t in range(tensor...  23 us
    ppermute x15, waiting for transfers between devices, exchange(): lax.ppermute(values, 'tensor', [(t, t ^ 1 << level) for t in range(tensor...  13.3 us
    ppermute x4, starting transfers between devices, shards(): arrivals.append([lax.ppermute(part, 'seq', pairs) for part in parts])  5.63 us
    pallas_call x3, Pallas kernels, encode(): pl.pallas_call(functools.partial(encode_body, begin), out_shape=jax.Shape...  3.86 us
    pallas_call x6, Pallas kernels, halve(): pl.pallas_call(functools.partial(halve_body, level), out_shape=[jax.Shape...  3.59 us
    pallas_call x4, Pallas kernels, choose(): pl.pallas_call(functools.partial(choose_body, len(picked), count, width,...  2.38 us
    unnamed x4, local copies, waits for them, and re-layouts  2.29 us
  transfers between devices with their start and end apart: 24, of which 13 were waited for; matrix products, arithmetic and copies ran while one was open for 1% of the time, Pallas kernels for 51%

profile of v6, /device:TPU:0, one launch (start us, length us, event | category | flops | bytes accessed | tf_op | source)
XLA Modules:
  0.0 98.5 jit_solution(7957329922642798676)
XLA Ops:
  0.6 1.4 %copy-done = bf16[128,6656]{1,0:T(8,128)(2,1)S(1)} copy-done((bf16[128,6656]{1,0:T(8,128)(2,1)S(1)}, bf16[128,6656]{1,0:T(8,128)(2,1)}, u32[]{:S(2)}) %copy-start) | copy-done | bytes 1703960
  2.2 3.0 %collective-permute-start = (bf16[128,2048]{1,0:T(8,128)(2,1)S(1)}, bf16[128,2048]{1,0:T(8,128)(2,1)S(1)}, u32[]{:S(2)}, u32[]{:S(2)}) collective-permute-start(bf16[128,2048]{1,0:T(8,128)(2,1)S(1)} %get-tuple-element.27.refs_4_.refs_0_), channel_id=1, source_target_pairs={{0,2},{2,0},{1,3},{3,1},{4,6},{6,4},{5,7},{7,5},{8,10},{10,8},{9,1... | collective-permute-start | bytes 1572872 | tf_op jit(solution)/shard_map/ppermute | solution.py:374
  5.4 0.7 add_convert_fusion
  6.1 0.8 copy-done.1
  7.0 13.2 %shard_map.60.refs_3_ = f32[128,4096]{1,0:T(8,128)S(1)} custom-call(s32[9]{0:T(128)S(1)} %stack.39.facts_ref.here_ref, bf16[128,2048]{1,0:T(8,128)(2,1)S(1)} %get-tuple-element.28.refs_0_, bf16[128,1536]{1,0:T(8,128)(2,1)S(1)} %get-tuple-element.29.refs_1_, bf16[128,1024]{1,0:T(8,128)(2,1)S(1)} %get-tuple-element.30.refs_2_, bf16[6656,4096]{1,0:T(8,128)(2,1)} %refs_1_.7, ...), custom_call_target="tpu_custom_call" | custom-call | flops 1 | bytes 1 | tf_op jit(solution)/shard_map/pallas_call | solution.py:134
  20.2 7.9 %shard_map.61 = (bf16[128,2048]{1,0:T(8,128)(2,1)S(1)}, f32[128,2048]{1,0:T(8,128)S(1)}, f32[128,4096]{1,0:T(8,128)S(1)}) custom-call(s32[9]{0:T(128)S(1)} %stack.39.facts_ref.here_ref, bf16[128,2048]{1,0:T(8,128)(2,1)S(1)} %get-tuple-element.27.refs_4_.refs_0_, bf16[128,2048]{1,0:T(8,128)(2,1)S(1)} %collective-permute-done.refs_1_, ...), custom_call_target="tpu_custom_call" | custom-call | flops 1 | bytes 1 | tf_op jit(solution)/shard_map/pallas_call | solution.py:134
  28.2 2.0 %collective-permute-start.4 = (bf16[128,1536]{1,0:T(8,128)(2,1)S(1)}, bf16[128,1536]{1,0:T(8,128)(2,1)S(1)}, u32[]{:S(2)}, u32[]{:S(2)}) collective-permute-start(bf16[128,1536]{1,0:T(8,128)(2,1)S(1)} %get-tuple-element.29.refs_1_), channel_id=1, source_target_pairs={{0,2},{2,0},{1,3},{3,1},{4,6},{6,4},{5,7},{7,5},{8,10},{10,8},{9,1... | collective-permute-start | bytes 1179656 | tf_op jit(solution)/shard_map/ppermute | solution.py:374
  30.2 7.0 %shard_map.62.refs_0_.refs_2_ = f32[128,4096]{1,0:T(8,128)S(1)} custom-call(s32[9]{0:T(128)S(1)} %stack.39.facts_ref.here_ref, bf16[128,2048]{1,0:T(8,128)(2,1)S(1)} %collective-permute-done.2.refs_0_, bf16[6656,4096]{1,0:T(8,128)(2,1)} %refs_1_.7, f32[128,4096]{1,0:T(8,128)S(1)} %get-tuple-element.33.refs_2_), custom_call_target="tpu_custom_call" | custom-call | flops 1 | bytes 1 | tf_op jit(solution)/shard_map/pallas_call | solution.py:134
  37.2 0.6 shard_map.63
  37.9 1.6 %collective-permute-start.3 = (bf16[64,2048]{1,0:T(8,128)(2,1)S(1)}, bf16[64,2048]{1,0:T(8,128)(2,1)S(1)}, u32[]{:S(2)}, u32[]{:S(2)}) collective-permute-start(bf16[64,2048]{1,0:T(8,128)(2,1)S(1)} %get-tuple-element.35.refs_3_), channel_id=1, source_target_pairs={{0,4},{4,0},{8,12},{12,8},{1,5},{5,1},{9,13},{13,9},{2,6},{6,2},{1... | collective-permute-start | bytes 786440 | tf_op jit(solution)/shard_map/ppermute | solution.py:350
  39.5 0.5 collective-permute-start.6
  40.1 5.7 %shard_map.64.refs_0_.refs_2_ = f32[128,4096]{1,0:T(8,128)S(1)} custom-call(s32[9]{0:T(128)S(1)} %stack.39.facts_ref.here_ref, bf16[128,1536]{1,0:T(8,128)(2,1)S(1)} %collective-permute-done.4.refs_0_, bf16[6656,4096]{1,0:T(8,128)(2,1)} %refs_1_.7, f32[128,4096]{1,0:T(8,128)S(1)} %shard_map.62.refs_0_.refs_2_, bf16[64,2048]{1,0:T(8,128)(2,1)S(1)} %get-tuple-element.35.refs_3_), custom_call_target="tpu_custom_call" | custom-call | flops 1 | bytes 1 | tf_op jit(solution)/shard_map/pallas_call | solution.py:134
  45.8 0.6 collective-permute-done.3.came_ref
  46.3 0.6 shard_map.65
  47.0 2.7 %collective-permute-start.5 = (bf16[32,2048]{1,0:T(8,128)(2,1)S(1)}, bf16[32,2048]{1,0:T(8,128)(2,1)S(1)}, u32[]{:S(2)}, u32[]{:S(2)}) collective-permute-start(bf16[32,2048]{1,0:T(8,128)(2,1)S(1)} %get-tuple-element.37.refs_3_), channel_id=1, source_target_pairs={{0,8},{4,12},{8,0},{12,4},{1,9},{5,13},{9,1},{13,5},{2,10},{6,14},... | collective-permute-start | bytes 393224 | tf_op jit(solution)/shard_map/ppermute | solution.py:350
  49.6 3.1 %shard_map.66 = (bf16[128,1024]{1,0:T(8,128)(2,1)S(1)}, f32[128,1024]{1,0:T(8,128)S(1)}) custom-call(s32[9]{0:T(128)S(1)} %stack.39.facts_ref.here_ref, bf16[128,1024]{1,0:T(8,128)(2,1)S(1)} %collective-permute-done.6.refs_0_, bf16[6656,4096]{1,0:T(8,128)(2,1)} %refs_1_.7, f32[128,4096]{1,0:T(8,128)S(1)} %shard_map.64.refs_0_.refs_2_, ...), custom_call_target="tpu_custom_call" | custom-call | flops 1 | bytes 1 | tf_op jit(solution)/shard_map/pallas_call | solution.py:134
  52.8 2.7 %collective-permute-done.5.came_ref = bf16[32,2048]{1,0:T(8,128)(2,1)S(1)} collective-permute-done((bf16[32,2048]{1,0:T(8,128)(2,1)S(1)}, bf16[32,2048]{1,0:T(8,128)(2,1)S(1)}, u32[]{:S(2)}, u32[]{:S(2)}) %collective-permute-start.5) | collective-permute-done | bytes 131104 | tf_op jit(solution)/shard_map/ppermute | solution.py:350
  55.5 1.6 %shard_map.67.refs_0_.refs_3_ = bf16[32,2176]{1,0:T(8,128)(2,1)S(1)} custom-call(s32[9]{0:T(128)S(1)} %stack.39.facts_ref.here_ref, f32[32,2048]{1,0:T(8,128)S(1)} %get-tuple-element.36.kept_ref, bf16[32,2048]{1,0:T(8,128)(2,1)S(1)} %collective-permute-done.5.came_ref, f32[1,4096]{1,0:T(1,128)S(1)} %bitcast.12, f32[128,128]{1,0:T(8,128)S(1)} %copy-done.1, ...), custom_call_target="tpu_custom_call" | custom-call | flops 1 | bytes 1 | tf_op jit(solution)/shard_map/pallas_call | solution.py:210
  57.0 3.1 %shard_map.72 = (bf16[128,1024]{1,0:T(8,128)(2,1)S(1)}, f32[128,1024]{1,0:T(8,128)S(1)}) custom-call(s32[9]{0:T(128)S(1)} %stack.39.facts_ref.here_ref, bf16[128,1024]{1,0:T(8,128)(2,1)S(1)} %collective-permute-done.6.refs_0_, bf16[6656,4096]{1,0:T(8,128)(2,1)} %refs_1_.7, f32[128,4096]{1,0:T(8,128)S(1)} %shard_map.64.refs_0_.refs_2_, ...), custom_call_target="tpu_custom_call" | custom-call | flops 1 | bytes 1 | tf_op jit(solution)/shard_map/pallas_call | solution.py:134
  60.2 0.6 shard_map.68
  60.8 0.7 collective-permute-start.11
  61.8 0.6 shard_map.73
  62.4 1.3 %collective-permute-start.17 = (bf16[64,1024]{1,0:T(8,128)(2,1)S(1)}, bf16[64,1024]{1,0:T(8,128)(2,1)S(1)}, u32[]{:S(2)}, u32[]{:S(2)}) collective-permute-start(bf16[64,1024]{1,0:T(8,128)(2,1)S(1)} %get-tuple-element.47), channel_id=1, source_target_pairs={{0,4},{4,0},{8,12},{12,8},{1,5},{5,1},{9,13},{13,9},{2,6},{6,2},{1... | collective-permute-start | bytes 393224 | tf_op jit(solution)/shard_map/ppermute | solution.py:350
  63.6 2.8 %collective-permute-start.8 = (bf16[32,2176]{1,0:T(8,128)(2,1)S(1)}, bf16[32,2176]{1,0:T(8,128)(2,1)S(1)}, u32[]{:S(2)}, u32[]{:S(2)}) collective-permute-start(bf16[32,2176]{1,0:T(8,128)(2,1)S(1)} %shard_map.67.refs_0_.refs_3_), channel_id=1, source_target_pairs={{0,8},{4,12},{8,0},{12,4},{1,9},{5,13},{9,1},{13,5},{2,10},{6,14},... | collective-permute-start | bytes 417800 | tf_op jit(solution)/shard_map/ppermute | solution.py:350
  66.5 0.8 collective-permute-done.11.came_ref
  67.2 0.6 shard_map.69
  67.8 2.1 %collective-permute-start.12 = (bf16[32,1024]{1,0:T(8,128)(2,1)S(1)}, bf16[32,1024]{1,0:T(8,128)(2,1)S(1)}, u32[]{:S(2)}, u32[]{:S(2)}) collective-permute-start(bf16[32,1024]{1,0:T(8,128)(2,1)S(1)} %get-tuple-element.43), channel_id=1, source_target_pairs={{0,8},{4,12},{8,0},{12,4},{1,9},{5,13},{9,1},{13,5},{2,10},{6,14},... | collective-permute-start | bytes 196616 | tf_op jit(solution)/shard_map/ppermute | solution.py:350
  70.0 3.4 %collective-permute-done.17.came_ref = bf16[64,1024]{1,0:T(8,128)(2,1)S(1)} collective-permute-done((bf16[64,1024]{1,0:T(8,128)(2,1)S(1)}, bf16[64,1024]{1,0:T(8,128)(2,1)S(1)}, u32[]{:S(2)}, u32[]{:S(2)}) %collective-permute-start.17) | collective-permute-done | bytes 131104 | tf_op jit(solution)/shard_map/ppermute | solution.py:350
  73.4 0.6 shard_map.74
  74.1 1.9 %collective-permute-start.7 = (bf16[32,2176]{1,0:T(8,128)(2,1)S(1)}, bf16[32,2176]{1,0:T(8,128)(2,1)S(1)}, u32[]{:S(2)}, u32[]{:S(2)}) collective-permute-start(bf16[32,2176]{1,0:T(8,128)(2,1)S(1)} %shard_map.67.refs_0_.refs_3_), channel_id=1, source_target_pairs={{0,4},{4,0},{8,12},{12,8},{1,5},{5,1},{9,13},{13,9},{2,6},{6,2},{1... | collective-permute-start | bytes 417800 | tf_op jit(solution)/shard_map/ppermute | solution.py:350
  75.9 1.3 %collective-permute-done.12.came_ref = bf16[32,1024]{1,0:T(8,128)(2,1)S(1)} collective-permute-done((bf16[32,1024]{1,0:T(8,128)(2,1)S(1)}, bf16[32,1024]{1,0:T(8,128)(2,1)S(1)}, u32[]{:S(2)}, u32[]{:S(2)}) %collective-permute-start.12) | collective-permute-done | bytes 65568 | tf_op jit(solution)/shard_map/ppermute | solution.py:350
  77.3 1.2 %shard_map.70.refs_4_ = bf16[32,1152]{1,0:T(8,128)(2,1)S(1)} custom-call(s32[9]{0:T(128)S(1)} %stack.39.facts_ref.here_ref, f32[32,1024]{1,0:T(8,128)S(1)} %get-tuple-element.42.kept_ref, bf16[32,1024]{1,0:T(8,128)(2,1)S(1)} %collective-permute-done.12.came_ref, f32[1,4096]{1,0:T(1,128)S(1)} %bitcast.13, f32[128,128]{1,0:T(8,128)S(1)} %copy-done.1), custom_call_target="tpu_custom_call" | custom-call | flops 1 | bytes 1 | tf_op jit(solution)/shard_map/pallas_call | solution.py:210
  78.5 0.9 collective-permute-done.18.came_ref
  79.4 1.2 %shard_map.75.refs_4_ = bf16[32,1152]{1,0:T(8,128)(2,1)S(1)} custom-call(s32[9]{0:T(128)S(1)} %stack.39.facts_ref.here_ref, f32[32,1024]{1,0:T(8,128)S(1)} %get-tuple-element.48.kept_ref, bf16[32,1024]{1,0:T(8,128)(2,1)S(1)} %collective-permute-done.18.came_ref, f32[1,4096]{1,0:T(1,128)S(1)} %bitcast.14, f32[128,128]{1,0:T(8,128)S(1)} %copy-done.1), custom_call_target="tpu_custom_call" | custom-call | flops 1 | bytes 1 | tf_op jit(solution)/shard_map/pallas_call | solution.py:210
  80.6 2.1 %collective-permute-start.20 = (bf16[32,1152]{1,0:T(8,128)(2,1)S(1)}, bf16[32,1152]{1,0:T(8,128)(2,1)S(1)}, u32[]{:S(2)}, u32[]{:S(2)}) collective-permute-start(bf16[32,1152]{1,0:T(8,128)(2,1)S(1)} %shard_map.75.refs_4_), channel_id=1, source_target_pairs={{0,8},{4,12},{8,0},{12,4},{1,9},{5,13},{9,1},{13,5},{2,10},{6,14},... | collective-permute-start | bytes 221192 | tf_op jit(solution)/shard_map/ppermute | solution.py:350
  82.6 2.0 %collective-permute-start.9 = (bf16[32,2176]{1,0:T(8,128)(2,1)S(1)}, bf16[32,2176]{1,0:T(8,128)(2,1)S(1)}, u32[]{:S(2)}, u32[]{:S(2)}) collective-permute-start(bf16[32,2176]{1,0:T(8,128)(2,1)S(1)} %collective-permute-done.8.refs_2_), channel_id=1, source_target_pairs={{0,4},{4,0},{8,12},{12,8},{1,5},{5,1},{9,13},{13,9},{2,6},{6,2},{1... | collective-permute-start | bytes 417800 | tf_op jit(solution)/shard_map/ppermute | solution.py:350
  84.7 1.9 %collective-permute-start.15 = (bf16[32,1152]{1,0:T(8,128)(2,1)S(1)}, bf16[32,1152]{1,0:T(8,128)(2,1)S(1)}, u32[]{:S(2)}, u32[]{:S(2)}) collective-permute-start(bf16[32,1152]{1,0:T(8,128)(2,1)S(1)} %collective-permute-done.14.refs_6_), channel_id=1, source_target_pairs={{0,4},{4,0},{8,12},{12,8},{1,5},{5,1},{9,13},{13,9},{2,6},{6,2},{1... | collective-permute-start | bytes 221192 | tf_op jit(solution)/shard_map/ppermute | solution.py:350
  86.7 0.3 collective-permute-done.20.refs_6_
  87.0 3.6 %collective-permute-start.21 = (bf16[32,1152]{1,0:T(8,128)(2,1)S(1)}, bf16[32,1152]{1,0:T(8,128)(2,1)S(1)}, u32[]{:S(2)}, u32[]{:S(2)}) collective-permute-start(bf16[32,1152]{1,0:T(8,128)(2,1)S(1)} %collective-permute-done.20.refs_6_), channel_id=1, source_target_pairs={{0,4},{4,0},{8,12},{12,8},{1,5},{5,1},{9,13},{13,9},{2,6},{6,2},{1... | collective-permute-start | bytes 221192 | tf_op jit(solution)/shard_map/ppermute | solution.py:350
  90.6 1.0 %collective-permute-done.13.refs_5_ = bf16[32,1152]{1,0:T(8,128)(2,1)S(1)} collective-permute-done((bf16[32,1152]{1,0:T(8,128)(2,1)S(1)}, bf16[32,1152]{1,0:T(8,128)(2,1)S(1)}, u32[]{:S(2)}, u32[]{:S(2)}) %collective-permute-start.13) | collective-permute-done | bytes 73760 | tf_op jit(solution)/shard_map/ppermute | solution.py:350
  91.6 1.4 %collective-permute-done.15.refs_7_ = bf16[32,1152]{1,0:T(8,128)(2,1)S(1)} collective-permute-done((bf16[32,1152]{1,0:T(8,128)(2,1)S(1)}, bf16[32,1152]{1,0:T(8,128)(2,1)S(1)}, u32[]{:S(2)}, u32[]{:S(2)}) %collective-permute-start.15) | collective-permute-done | bytes 73760 | tf_op jit(solution)/shard_map/ppermute | solution.py:350
  93.0 0.6 shard_map.77
  93.8 0.8 collective-permute-done.21.refs_7_
  94.6 0.6 shard_map.78
  95.3 0.6 shard_map.71.refs_0_
  95.9 0.6 shard_map.76.refs_1_
  96.5 0.3 collective-permute-done.23.refs_3_
  96.9 1.7 %shard_map.79 = (bf16[128,4096]{1,0:T(8,128)(2,1)}, bf16[32,128]{1,0:T(8,128)(2,1)}) custom-call(s32[9]{0:T(128)S(1)} %stack.39.facts_ref.here_ref, bf16[128,1152]{1,0:T(8,128)(2,1)S(1)} %shard_map.71.refs_0_, bf16[128,1152]{1,0:T(8,128)(2,1)S(1)} %shard_map.76.refs_1_, bf16[128,1152]{1,0:T(8,128)(2,1)S(1)} %collective-permute-done.22.refs_2_, ...), custom_call_target="tpu_custom_call" | custom-call | flops 1 | bytes 1 | tf_op jit(solution)/shard_map/pallas_call | solution.py:294
  (27 shorter events, 1.3 us)
Async XLA Ops:
  0.6 1.5 %copy-start = (bf16[128,6656]{1,0:T(8,128)(2,1)S(1)}, bf16[128,6656]{1,0:T(8,128)(2,1)}, u32[]{:S(2)}) copy-start(bf16[128,6656]{1,0:T(8,128)(2,1)} %in_ref.1) | copy-start | bytes 5111812
  2.2 18.0 %collective-permute-start = (bf16[128,2048]{1,0:T(8,128)(2,1)S(1)}, bf16[128,2048]{1,0:T(8,128)(2,1)S(1)}, u32[]{:S(2)}, u32[]{:S(2)}) collective-permute-start(bf16[128,2048]{1,0:T(8,128)(2,1)S(1)} %get-tuple-element.27.refs_4_.refs_0_), channel_id=1, source_target_pairs={{0,2},{2,0},{1,3},{3,1},{4,6},{6,4},{5,7},{7,5},{8,10},{10,8},{9,1... | collective-permute-start | bytes 1572872 | tf_op jit(solution)/shard_map/ppermute | solution.py:374
  5.3 25.0 %collective-permute-start.2 = (bf16[128,2048]{1,0:T(8,128)(2,1)S(1)}, bf16[128,2048]{1,0:T(8,128)(2,1)S(1)}, u32[]{:S(2)}, u32[]{:S(2)}) collective-permute-start(bf16[128,2048]{1,0:T(8,128)(2,1)S(1)} %get-tuple-element.28.refs_0_), channel_id=1, source_target_pairs={{0,2},{2,0},{1,3},{3,1},{4,6},{6,4},{5,7},{7,5},{8,10},{10,8},{9,1... | collective-permute-start | bytes 1572872 | tf_op jit(solution)/shard_map/ppermute | solution.py:374
  6.1 0.8 copy-start.1
  28.1 9.1 %collective-permute-start.1 = (bf16[128,2048]{1,0:T(8,128)(2,1)S(1)}, bf16[128,2048]{1,0:T(8,128)(2,1)S(1)}, u32[]{:S(2)}, u32[]{:S(2)}) collective-permute-start(bf16[128,2048]{1,0:T(8,128)(2,1)S(1)} %get-tuple-element.32), channel_id=1, source_target_pairs={{0,1},{1,0},{2,3},{3,2},{4,5},{5,4},{6,7},{7,6},{8,9},{9,8},{10,11... | collective-permute-start | bytes 1572872 | tf_op jit(solution)/shard_map/ppermute | solution.py:347
  28.2 11.9 %collective-permute-start.4 = (bf16[128,1536]{1,0:T(8,128)(2,1)S(1)}, bf16[128,1536]{1,0:T(8,128)(2,1)S(1)}, u32[]{:S(2)}, u32[]{:S(2)}) collective-permute-start(bf16[128,1536]{1,0:T(8,128)(2,1)S(1)} %get-tuple-element.29.refs_1_), channel_id=1, source_target_pairs={{0,2},{2,0},{1,3},{3,1},{4,6},{6,4},{5,7},{7,5},{8,10},{10,8},{9,1... | collective-permute-start | bytes 1179656 | tf_op jit(solution)/shard_map/ppermute | solution.py:374
  37.9 8.4 %collective-permute-start.3 = (bf16[64,2048]{1,0:T(8,128)(2,1)S(1)}, bf16[64,2048]{1,0:T(8,128)(2,1)S(1)}, u32[]{:S(2)}, u32[]{:S(2)}) collective-permute-start(bf16[64,2048]{1,0:T(8,128)(2,1)S(1)} %get-tuple-element.35.refs_3_), channel_id=1, source_target_pairs={{0,4},{4,0},{8,12},{12,8},{1,5},{5,1},{9,13},{13,9},{2,6},{6,2},{1... | collective-permute-start | bytes 786440 | tf_op jit(solution)/shard_map/ppermute | solution.py:350
  39.5 10.1 %collective-permute-start.6 = (bf16[128,1024]{1,0:T(8,128)(2,1)S(1)}, bf16[128,1024]{1,0:T(8,128)(2,1)S(1)}, u32[]{:S(2)}, u32[]{:S(2)}) collective-permute-start(bf16[128,1024]{1,0:T(8,128)(2,1)S(1)} %get-tuple-element.30.refs_2_), channel_id=1, source_target_pairs={{0,2},{2,0},{1,3},{3,1},{4,6},{6,4},{5,7},{7,5},{8,10},{10,8},{9,1... | collective-permute-start | bytes 786440 | tf_op jit(solution)/shard_map/ppermute | solution.py:374
  47.0 8.5 %collective-permute-start.5 = (bf16[32,2048]{1,0:T(8,128)(2,1)S(1)}, bf16[32,2048]{1,0:T(8,128)(2,1)S(1)}, u32[]{:S(2)}, u32[]{:S(2)}) collective-permute-start(bf16[32,2048]{1,0:T(8,128)(2,1)S(1)} %get-tuple-element.37.refs_3_), channel_id=1, source_target_pairs={{0,8},{4,12},{8,0},{12,4},{1,9},{5,13},{9,1},{13,5},{2,10},{6,14},... | collective-permute-start | bytes 393224 | tf_op jit(solution)/shard_map/ppermute | solution.py:350
  52.7 7.5 %collective-permute-start.10 = (bf16[128,1024]{1,0:T(8,128)(2,1)S(1)}, bf16[128,1024]{1,0:T(8,128)(2,1)S(1)}, u32[]{:S(2)}, u32[]{:S(2)}) collective-permute-start(bf16[128,1024]{1,0:T(8,128)(2,1)S(1)} %get-tuple-element.38.refs_0_), channel_id=1, source_target_pairs={{0,1},{1,0},{2,3},{3,2},{4,5},{5,4},{6,7},{7,6},{8,9},{9,8},{10,11... | collective-permute-start | bytes 786440 | tf_op jit(solution)/shard_map/ppermute | solution.py:347
  60.2 1.6 %collective-permute-start.16 = (bf16[128,1024]{1,0:T(8,128)(2,1)S(1)}, bf16[128,1024]{1,0:T(8,128)(2,1)S(1)}, u32[]{:S(2)}, u32[]{:S(2)}) collective-permute-start(bf16[128,1024]{1,0:T(8,128)(2,1)S(1)} %get-tuple-element.45), channel_id=1, source_target_pairs={{0,1},{1,0},{2,3},{3,2},{4,5},{5,4},{6,7},{7,6},{8,9},{9,8},{10,11... | collective-permute-start | bytes 786440 | tf_op jit(solution)/shard_map/ppermute | solution.py:347
  60.8 6.4 %collective-permute-start.11 = (bf16[64,1024]{1,0:T(8,128)(2,1)S(1)}, bf16[64,1024]{1,0:T(8,128)(2,1)S(1)}, u32[]{:S(2)}, u32[]{:S(2)}) collective-permute-start(bf16[64,1024]{1,0:T(8,128)(2,1)S(1)} %get-tuple-element.41), channel_id=1, source_target_pairs={{0,4},{4,0},{8,12},{12,8},{1,5},{5,1},{9,13},{13,9},{2,6},{6,2},{1... | collective-permute-start | bytes 393224 | tf_op jit(solution)/shard_map/ppermute | solution.py:350
  62.4 11.0 %collective-permute-start.17 = (bf16[64,1024]{1,0:T(8,128)(2,1)S(1)}, bf16[64,1024]{1,0:T(8,128)(2,1)S(1)}, u32[]{:S(2)}, u32[]{:S(2)}) collective-permute-start(bf16[64,1024]{1,0:T(8,128)(2,1)S(1)} %get-tuple-element.47), channel_id=1, source_target_pairs={{0,4},{4,0},{8,12},{12,8},{1,5},{5,1},{9,13},{13,9},{2,6},{6,2},{1... | collective-permute-start | bytes 393224 | tf_op jit(solution)/shard_map/ppermute | solution.py:350
  63.6 19.0 %collective-permute-start.8 = (bf16[32,2176]{1,0:T(8,128)(2,1)S(1)}, bf16[32,2176]{1,0:T(8,128)(2,1)S(1)}, u32[]{:S(2)}, u32[]{:S(2)}) collective-permute-start(bf16[32,2176]{1,0:T(8,128)(2,1)S(1)} %shard_map.67.refs_0_.refs_3_), channel_id=1, source_target_pairs={{0,8},{4,12},{8,0},{12,4},{1,9},{5,13},{9,1},{13,5},{2,10},{6,14},... | collective-permute-start | bytes 417800 | tf_op jit(solution)/shard_map/ppermute | solution.py:350
  67.8 9.5 %collective-permute-start.12 = (bf16[32,1024]{1,0:T(8,128)(2,1)S(1)}, bf16[32,1024]{1,0:T(8,128)(2,1)S(1)}, u32[]{:S(2)}, u32[]{:S(2)}) collective-permute-start(bf16[32,1024]{1,0:T(8,128)(2,1)S(1)} %get-tuple-element.43), channel_id=1, source_target_pairs={{0,8},{4,12},{8,0},{12,4},{1,9},{5,13},{9,1},{13,5},{2,10},{6,14},... | collective-permute-start | bytes 196616 | tf_op jit(solution)/shard_map/ppermute | solution.py:350
  74.0 5.4 %collective-permute-start.18 = (bf16[32,1024]{1,0:T(8,128)(2,1)S(1)}, bf16[32,1024]{1,0:T(8,128)(2,1)S(1)}, u32[]{:S(2)}, u32[]{:S(2)}) collective-permute-start(bf16[32,1024]{1,0:T(8,128)(2,1)S(1)} %get-tuple-element.49), channel_id=1, source_target_pairs={{0,8},{4,12},{8,0},{12,4},{1,9},{5,13},{9,1},{13,5},{2,10},{6,14},... | collective-permute-start | bytes 196616 | tf_op jit(solution)/shard_map/ppermute | solution.py:350
  74.1 12.6 %collective-permute-start.7 = (bf16[32,2176]{1,0:T(8,128)(2,1)S(1)}, bf16[32,2176]{1,0:T(8,128)(2,1)S(1)}, u32[]{:S(2)}, u32[]{:S(2)}) collective-permute-start(bf16[32,2176]{1,0:T(8,128)(2,1)S(1)} %shard_map.67.refs_0_.refs_3_), channel_id=1, source_target_pairs={{0,4},{4,0},{8,12},{12,8},{1,5},{5,1},{9,13},{13,9},{2,6},{6,2},{1... | collective-permute-start | bytes 417800 | tf_op jit(solution)/shard_map/ppermute | solution.py:350
  78.4 6.3 %collective-permute-start.14 = (bf16[32,1152]{1,0:T(8,128)(2,1)S(1)}, bf16[32,1152]{1,0:T(8,128)(2,1)S(1)}, u32[]{:S(2)}, u32[]{:S(2)}) collective-permute-start(bf16[32,1152]{1,0:T(8,128)(2,1)S(1)} %shard_map.70.refs_4_), channel_id=1, source_target_pairs={{0,8},{4,12},{8,0},{12,4},{1,9},{5,13},{9,1},{13,5},{2,10},{6,14},... | collective-permute-start | bytes 221192 | tf_op jit(solution)/shard_map/ppermute | solution.py:350
  80.6 6.4 %collective-permute-start.20 = (bf16[32,1152]{1,0:T(8,128)(2,1)S(1)}, bf16[32,1152]{1,0:T(8,128)(2,1)S(1)}, u32[]{:S(2)}, u32[]{:S(2)}) collective-permute-start(bf16[32,1152]{1,0:T(8,128)(2,1)S(1)} %shard_map.75.refs_4_), channel_id=1, source_target_pairs={{0,8},{4,12},{8,0},{12,4},{1,9},{5,13},{9,1},{13,5},{2,10},{6,14},... | collective-permute-start | bytes 221192 | tf_op jit(solution)/shard_map/ppermute | solution.py:350
  82.6 8.0 %collective-permute-start.9 = (bf16[32,2176]{1,0:T(8,128)(2,1)S(1)}, bf16[32,2176]{1,0:T(8,128)(2,1)S(1)}, u32[]{:S(2)}, u32[]{:S(2)}) collective-permute-start(bf16[32,2176]{1,0:T(8,128)(2,1)S(1)} %collective-permute-done.8.refs_2_), channel_id=1, source_target_pairs={{0,4},{4,0},{8,12},{12,8},{1,5},{5,1},{9,13},{13,9},{2,6},{6,2},{1... | collective-permute-start | bytes 417800 | tf_op jit(solution)/shard_map/ppermute | solution.py:350
  84.6 7.0 %collective-permute-start.13 = (bf16[32,1152]{1,0:T(8,128)(2,1)S(1)}, bf16[32,1152]{1,0:T(8,128)(2,1)S(1)}, u32[]{:S(2)}, u32[]{:S(2)}) collective-permute-start(bf16[32,1152]{1,0:T(8,128)(2,1)S(1)} %shard_map.70.refs_4_), channel_id=1, source_target_pairs={{0,4},{4,0},{8,12},{12,8},{1,5},{5,1},{9,13},{13,9},{2,6},{6,2},{1... | collective-permute-start | bytes 221192 | tf_op jit(solution)/shard_map/ppermute | solution.py:350
  84.7 8.4 %collective-permute-start.15 = (bf16[32,1152]{1,0:T(8,128)(2,1)S(1)}, bf16[32,1152]{1,0:T(8,128)(2,1)S(1)}, u32[]{:S(2)}, u32[]{:S(2)}) collective-permute-start(bf16[32,1152]{1,0:T(8,128)(2,1)S(1)} %collective-permute-done.14.refs_6_), channel_id=1, source_target_pairs={{0,4},{4,0},{8,12},{12,8},{1,5},{5,1},{9,13},{13,9},{2,6},{6,2},{1... | collective-permute-start | bytes 221192 | tf_op jit(solution)/shard_map/ppermute | solution.py:350
  86.6 7.2 %collective-permute-start.19 = (bf16[32,1152]{1,0:T(8,128)(2,1)S(1)}, bf16[32,1152]{1,0:T(8,128)(2,1)S(1)}, u32[]{:S(2)}, u32[]{:S(2)}) collective-permute-start(bf16[32,1152]{1,0:T(8,128)(2,1)S(1)} %shard_map.75.refs_4_), channel_id=1, source_target_pairs={{0,4},{4,0},{8,12},{12,8},{1,5},{5,1},{9,13},{13,9},{2,6},{6,2},{1... | collective-permute-start | bytes 221192 | tf_op jit(solution)/shard_map/ppermute | solution.py:350
  87.0 7.6 %collective-permute-start.21 = (bf16[32,1152]{1,0:T(8,128)(2,1)S(1)}, bf16[32,1152]{1,0:T(8,128)(2,1)S(1)}, u32[]{:S(2)}, u32[]{:S(2)}) collective-permute-start(bf16[32,1152]{1,0:T(8,128)(2,1)S(1)} %collective-permute-done.20.refs_6_), channel_id=1, source_target_pairs={{0,4},{4,0},{8,12},{12,8},{1,5},{5,1},{9,13},{13,9},{2,6},{6,2},{1... | collective-permute-start | bytes 221192 | tf_op jit(solution)/shard_map/ppermute | solution.py:350
  93.6 2.9 %collective-permute-start.22 = (bf16[128,1152]{1,0:T(8,128)(2,1)S(1)}, bf16[128,1152]{1,0:T(8,128)(2,1)S(1)}, u32[]{:S(2)}, u32[]{:S(2)}) collective-permute-start(bf16[128,1152]{1,0:T(8,128)(2,1)S(1)} %shard_map.77), channel_id=1, source_target_pairs={{0,1},{1,0},{2,3},{3,2},{4,5},{5,4},{6,7},{7,6},{8,9},{9,8},{10,11... | collective-permute-start | bytes 884744 | tf_op jit(solution)/shard_map/ppermute | solution.py:347
  95.2 1.6 %collective-permute-start.23 = (bf16[128,1152]{1,0:T(8,128)(2,1)S(1)}, bf16[128,1152]{1,0:T(8,128)(2,1)S(1)}, u32[]{:S(2)}, u32[]{:S(2)}) collective-permute-start(bf16[128,1152]{1,0:T(8,128)(2,1)S(1)} %shard_map.78), channel_id=1, source_target_pairs={{0,1},{1,0},{2,3},{3,2},{4,5},{5,4},{6,7},{7,6},{8,9},{9,8},{10,11... | collective-permute-start | bytes 884744 | tf_op jit(solution)/shard_map/ppermute | solution.py:347

commit v7 on v6

v7 whole, which is shorter than its diff:
```python
import functools
import math

import jax
import jax.numpy as jnp
import numpy as np
from jax import lax
from jax.experimental import pallas as pl
from jax.experimental.pallas import tpu as pltpu
from jax.sharding import PartitionSpec as P

BLOCK = 128
UNIT = 512
GROUPS = 2
VMEM_LIMIT = 6 * 2**20
SHARES = (4, 5, 2)
epsilon = 1e-06

SMALL = pl.CostEstimate(flops=1, bytes_accessed=1, transcendentals=0)
PARAMS = pltpu.CompilerParams(vmem_limit_bytes=VMEM_LIMIT)
VMEM = pl.BlockSpec(memory_space=pltpu.VMEM)
ANY = pl.BlockSpec(memory_space=pl.ANY)
HBM = pl.BlockSpec(memory_space=pltpu.HBM)


def hadamard(order):
    indices = np.arange(order)
    parity = np.zeros((order, order), np.int64)
    for position in range(order.bit_length() - 1):
        parity = parity + (indices[:, None] >> position & 1) * (indices[None, :] >> position & 1)
    return ((1 - 2 * (parity % 2)) / math.sqrt(order)).astype(np.float32)


def slice_body(places, in_ref, *refs):
    out_refs, arrived = refs[:-1], refs[-1]
    copies = [
        pltpu.make_async_copy(in_ref.at[:, at : at + size], out_ref, arrived.at[index])
        for index, ((at, size), out_ref) in enumerate(zip(places, out_refs))
    ]
    for copy in copies:
        copy.start()
    for copy in copies:
        copy.wait()


def slices_of(values, places):
    return pl.pallas_call(
        functools.partial(slice_body, places),
        out_shape=[jax.ShapeDtypeStruct((values.shape[0], size), values.dtype) for _, size in places],
        in_specs=[HBM],
        out_specs=[VMEM] * len(places),
        scratch_shapes=[pltpu.SemaphoreType.DMA((len(places),))],
        compiler_params=PARAMS,
        cost_estimate=SMALL,
    )(values)


def multiply_body(spans, has_totals, splits, row, groups, *refs):
    lefts = [refs[begin:end] for begin, end in spans]
    refs = refs[spans[-1][1] :]
    w_ref, refs = refs[0], refs[1:]
    total_refs, refs = list(refs[: sum(has_totals)]), refs[sum(has_totals) :]
    buffer, arrived = refs[-2:]
    out_count = sum(2 * groups if split else 1 for split in splits)
    out_refs = refs[-2 - out_count : -2]
    steps, depth, wide = buffer.shape
    rows = lefts[0][0].shape[0]
    first = steps // 2 // groups
    here = lax.axis_index("sub")

    def column(n):
        if not any(splits):
            return n
        group, place = n // (2 * first), n % (2 * first)
        side, place = (here, place - first) if place >= first else (1 - here, place)
        return side * (steps // 2) + group * first + place

    def at(block):
        return pl.ds(pl.multiple_of(block * wide, wide), wide)

    def copy(n):
        return pltpu.make_async_copy(w_ref.at[pl.ds(row, depth), at(column(n))], buffer.at[n], arrived.at[n])

    def step(n):
        copy(n).wait()
        product, begin = None, 0
        for index in range(len(lefts[0])):
            parts = [left[index][...] for left in lefts]
            left = parts[0] if len(parts) == 1 else jnp.concatenate(parts, axis=0)
            end = begin + left.shape[1]
            part = jnp.dot(left, buffer[n, begin:end], preferred_element_type=jnp.float32)
            product = part if product is None else product + part
            begin = end
        totals, outs = list(total_refs), list(out_refs)
        for index in range(len(lefts)):
            value = product[index * rows : (index + 1) * rows]
            if has_totals[index]:
                value = value + totals.pop(0)[:, at(column(n))]
            if splits[index]:
                group, place = n // (2 * first), n % (2 * first)
                out_ref = outs[2 * group + place // first]
                begin = place % first * wide
                out_ref[:, begin : begin + wide] = value.astype(out_ref.dtype)
                outs = outs[2 * groups :]
            else:
                outs.pop(0)[:, at(column(n))] = value

    for n in range(steps):
        copy(n).start()
    if any(splits):
        for n in range(steps):
            step(n)
    else:
        pl.loop(0, steps)(step)


def multiply(lefts, weight, row, totals, splits, wide, groups=1, tokens=()):
    rows = lefts[0][0].shape[0]
    depth = sum(part.shape[1] for part in lefts[0])
    columns = weight.shape[1]
    steps = columns // wide
    spans = [(index * len(left), (index + 1) * len(left)) for index, left in enumerate(lefts)]
    held = [total for total in totals if total is not None]
    out_shape = []
    for split in splits:
        if split:
            out_shape += [
                jax.ShapeDtypeStruct((rows, columns // 2 // groups), jnp.bfloat16),
                jax.ShapeDtypeStruct((rows, columns // 2 // groups), jnp.float32),
            ] * groups
        else:
            out_shape.append(jax.ShapeDtypeStruct((rows, columns), jnp.float32))
    body = functools.partial(
        multiply_body, spans, [total is not None for total in totals], splits, row, groups
    )
    return pl.pallas_call(
        body,
        out_shape=out_shape,
        in_specs=[VMEM] * spans[-1][1] + [HBM] + [VMEM] * len(held) + [ANY] * len(tokens),
        out_specs=[VMEM] * len(out_shape),
        scratch_shapes=[
            pltpu.VMEM((steps, depth, wide), weight.dtype),
            pltpu.SemaphoreType.DMA((steps,)),
        ],
        compiler_params=pltpu.CompilerParams(
            vmem_limit_bytes=2 * steps * depth * wide + VMEM_LIMIT
        ),
        cost_estimate=SMALL,
    )(*[part for left in lefts for part in left], weight, *held, *tokens)


def gate(values, tokens):
    return pl.pallas_call(
        lambda *refs: None,
        out_shape=jax.ShapeDtypeStruct(values.shape, values.dtype),
        in_specs=[ANY] * (1 + len(tokens)),
        out_specs=ANY,
        input_output_aliases={0: 0},
        compiler_params=PARAMS,
        cost_estimate=SMALL,
    )(values, *tokens)


def halve_body(level, kept_ref, came_ref, *refs):
    sent_out, kept_out = refs[-2:]
    half = sent_out.shape[0]

    def put(bit):
        mine, other = slice(bit * half, (bit + 1) * half), slice((1 - bit) * half, (2 - bit) * half)
        kept_out[...] = kept_ref[mine] + came_ref[mine].astype(jnp.float32)
        sent_out[...] = (kept_ref[other] + came_ref[other].astype(jnp.float32)).astype(jnp.bfloat16)

    for bit in range(2):
        pl.when(lax.axis_index("tensor") >> level & 1 == bit)(functools.partial(put, bit))


def halve(kept, came, level, tokens=()):
    rows, columns = kept.shape
    half = rows // 2
    if half % 16:
        total, bit = kept + came.astype(jnp.float32), lax.axis_index("tensor") >> level & 1
        sent = lax.dynamic_slice_in_dim(total, (1 - bit) * half, half, 0).astype(jnp.bfloat16)
        return sent, lax.dynamic_slice_in_dim(total, bit * half, half, 0)
    return pl.pallas_call(
        functools.partial(halve_body, level),
        out_shape=[
            jax.ShapeDtypeStruct((half, columns), jnp.bfloat16),
            jax.ShapeDtypeStruct((half, columns), jnp.float32),
        ],
        in_specs=[VMEM, VMEM] + [ANY] * len(tokens),
        out_specs=[VMEM, VMEM],
        compiler_params=PARAMS,
        cost_estimate=SMALL,
    )(kept, came, *tokens)


def encode_body(begin, kept_ref, came_ref, flips_ref, rotation_ref, *refs):
    out_ref = refs[-1]
    rows, columns = kept_ref.shape
    half = flips_ref.shape[1] // 2
    rotation = rotation_ref[...]
    lane = lax.broadcasted_iota(jnp.int32, (rows, BLOCK), 1)
    scales = jnp.zeros((rows, BLOCK), jnp.float32)
    for block in range(columns // BLOCK):
        at = slice(block * BLOCK, (block + 1) * BLOCK)
        flips = flips_ref[:, pl.ds(pl.multiple_of(lax.axis_index("sub") * half + begin + block * BLOCK, BLOCK), BLOCK)]
        total = (kept_ref[:, at] + came_ref[:, at].astype(jnp.float32)) * flips
        rotated = jnp.dot(
            total, rotation, precision=lax.Precision.HIGHEST, preferred_element_type=jnp.float32
        )
        largest = jnp.max(jnp.abs(rotated), axis=1, keepdims=True)
        scale = (largest + epsilon).astype(jnp.bfloat16).astype(jnp.float32)
        out_ref[:, at] = (rotated / scale).astype(jnp.bfloat16)
        scales = jnp.where(lane == block, scale, scales)
    out_ref[:, columns:] = scales.astype(jnp.bfloat16)


def encode(kept, came, begin, flips, rotation, tokens=()):
    rows, columns = kept.shape
    return pl.pallas_call(
        functools.partial(encode_body, begin),
        out_shape=jax.ShapeDtypeStruct((rows, columns + BLOCK), jnp.bfloat16),
        in_specs=[VMEM] * 4 + [ANY] * len(tokens),
        out_specs=VMEM,
        compiler_params=PARAMS,
        cost_estimate=SMALL,
    )(kept, came, flips, rotation, *tokens)


def rank_of(index, count):
    levels = count.bit_length() - 1
    return sum((index >> level & 1) << (levels - 1 - level) for level in range(levels))


def block_of(other, place, places, blocks):
    sub = lax.axis_index("sub")
    sub = 1 - sub if other else sub
    return lax.rem(lax.axis_index("seq") - (sub * places + place) + blocks, blocks)


def choose_body(blocks, pieces, width, at, other, places, *refs):
    out_ref = refs[-1]
    rows = refs[0].shape[0]
    scales = width // BLOCK

    def put(block, place):
        begin, scale_at = at[block]
        for piece in range(pieces):
            ref = refs[block * pieces + piece]
            row = (place * pieces + rank_of(lax.axis_index("tensor") ^ piece, pieces)) * rows
            here = pl.ds(pl.multiple_of(row, rows), rows)
            out_ref[here, :width] = ref[:, begin : begin + width]
            out_ref[here, width : width + scales] = ref[:, scale_at : scale_at + scales]

    for place in range(places):
        for block in range(blocks):
            pl.when(block_of(other, place, places, blocks) == block)(functools.partial(put, block, place))


def choose(results, group, width, other, places):
    picked, at = [], []
    for result in results:
        if len(result) == 1:
            pieces, begin = result[0], group * width
            at.append((begin, pieces[0].shape[1] - BLOCK + begin // BLOCK))
        else:
            pieces = result[group]
            at.append((0, width))
        picked.append(pieces)
    rows = picked[0][0].shape[0]
    count = len(picked[0])
    if rows % 16:
        blocks = []
        for pieces, (begin, scale_at) in zip(picked, at):
            block = jnp.zeros((count * rows, width + BLOCK), jnp.bfloat16)
            for index, piece in enumerate(pieces):
                scale = jnp.pad(piece[:, scale_at : scale_at + width // BLOCK], ((0, 0), (0, BLOCK - width // BLOCK)))
                part = jnp.concatenate([piece[:, begin : begin + width], scale], axis=1)
                block = lax.dynamic_update_slice_in_dim(block, part, rank_of(lax.axis_index("tensor") ^ index, count) * rows, 0)
            blocks.append(block)
        stacked = jnp.stack(blocks)
        return jnp.concatenate([stacked[block_of(other, place, places, len(blocks))] for place in range(places)])
    return pl.pallas_call(
        functools.partial(choose_body, len(picked), count, width, at, other, places),
        out_shape=jax.ShapeDtypeStruct((places * count * rows, width + BLOCK), jnp.bfloat16),
        in_specs=[VMEM] * (len(picked) * count),
        out_specs=VMEM,
        compiler_params=PARAMS,
        cost_estimate=SMALL,
    )(*[piece for pieces in picked for piece in pieces])


def assemble_body(groups, half, *refs):
    mine, other = refs[:groups], refs[groups : 2 * groups]
    codes_ref, scales_ref = refs[2 * groups :]
    width = half // groups
    scales = width // BLOCK

    def put(core):
        held = []
        for side, side_refs in ((core, mine), (1 - core, other)):
            for group, ref in enumerate(side_refs):
                begin = side * half + group * width
                codes_ref[:, begin : begin + width] = ref[:, :width]
                held.append((begin, ref[:, width : width + scales].astype(jnp.float32)))
        held = jnp.concatenate([value for _, value in sorted(held, key=lambda pair: pair[0])], axis=1)
        scales_ref[...] = held.T.astype(jnp.bfloat16)

    for core in range(2):
        pl.when(lax.axis_index("sub") == core)(functools.partial(put, core))


def assemble(mine, other, half):
    rows = mine[0].shape[0]
    codes, scales = pl.pallas_call(
        functools.partial(assemble_body, len(mine), half),
        out_shape=(
            jax.ShapeDtypeStruct((rows, 2 * half), jnp.bfloat16),
            jax.ShapeDtypeStruct((2 * half // BLOCK, rows), jnp.bfloat16),
        ),
        in_specs=[VMEM] * (2 * len(mine)),
        out_specs=(VMEM, VMEM),
        compiler_params=PARAMS,
        cost_estimate=SMALL,
    )(*mine, *other)
    return codes, scales.T


def cut(depth):
    if depth % UNIT or depth < 8 * UNIT:
        return [depth]
    units = depth // UNIT
    sizes = [max(1, units * share // 13) for share in SHARES]
    return [size * UNIT for size in sizes + [units - sum(sizes)]]


def shards(hidden, down_weight, sign_bits):
    tensor_count = lax.axis_size("tensor")
    seq_count = lax.axis_size("seq")
    sub_count = lax.axis_size("sub")
    depth = hidden.shape[1]
    half = down_weight.shape[1] // sub_count
    per_sub = seq_count // sub_count
    levels = tensor_count.bit_length() - 1
    wide, wide_chunk = min(256, half // GROUPS), min(512, half // GROUPS)
    flips = (2 * sign_bits - 1).astype(jnp.float32)[None, :]
    rotation = jnp.asarray(hadamard(BLOCK))

    def swap(values):
        return lax.ppermute(values, "sub", [(0, 1), (1, 0)])

    def exchange(values, level):
        return lax.ppermute(values, "tensor", [(t, t ^ 1 << level) for t in range(tensor_count)])

    def reduce(sent, kept, begin):
        tokens = (yield None) or []
        came = swap(sent)
        for level in range(levels):
            sent, kept = halve(kept, came, level, tokens)
            tokens = (yield sent) or []
            came = exchange(sent, level)
        yield encode(kept, came, begin, flips, rotation, tokens)

    def spread(packed):
        pieces = {0: packed}
        for level in reversed(range(levels)):
            for index in list(pieces):
                pieces[index ^ 1 << level] = exchange(pieces[index], level)
        return [pieces[index] for index in range(tensor_count)]

    sizes = cut(depth)
    places = [sum(sizes[:index]) for index in range(len(sizes))]
    parts = slices_of(hidden, list(zip(places, sizes)))
    arrivals = []
    for shift in range(1, seq_count):
        pairs = [(s, (s + shift) % seq_count) for s in range(seq_count)]
        arrivals.append([lax.ppermute(part, "seq", pairs) for part in parts])

    if len(sizes) == 1:
        outs = multiply([[parts[0]], [arrivals[0][0]]], down_weight, 0, [None, None], [True, True], wide_chunk)
        reduced = [list(reduce(*outs[:2], 0))[-1], list(reduce(*outs[2:], 0))[-1]]
        for arrived in arrivals[1:]:
            outs = multiply([[arrived[0]]], down_weight, 0, [None], [True], wide_chunk)
            reduced.append(list(reduce(*outs, 0))[-1])
        results = [[spread(packed)] for packed in reduced]
    else:
        (own,) = multiply([parts[1:]], down_weight, sizes[0], [None], [False], wide, tokens=parts[:1])
        sent, kept, total = multiply(
            [[parts[0]], [arrivals[0][0]]], down_weight, 0, [own, None], [True, False], wide_chunk
        )
        own_steps = reduce(sent, kept, 0)
        next(own_steps)
        tokens = [own_steps.send([arrivals[0][1]])]
        results = []
        for shift, arrived in enumerate(arrivals):
            if shift:
                (total,) = multiply([[arrived[0]]], down_weight, 0, [None], [False], wide_chunk)
            for index in range(1, len(sizes) - 1):
                (total,) = multiply(
                    [[arrived[index]]], down_weight, places[index], [total], [False], wide_chunk, tokens=tokens
                )
                if not results:
                    step = own_steps.send([total])
                    tokens = [step]
                    if step.shape[1] > half:
                        results.append([spread(step)])
            if not results:
                results.append([spread(list(own_steps)[-1])])
            outs = multiply(
                [[arrived[-1]]], down_weight, places[-1], [total], [True], wide_chunk, groups=GROUPS, tokens=tokens
            )
            remote = []
            for group in range(GROUPS):
                sent, kept = outs[2 * group : 2 * group + 2]
                if group == GROUPS - 1 and shift == 0 and levels > 1:
                    sent = gate(sent, [results[0][0][1], results[0][0][1 << levels - 1]])
                steps = reduce(sent, kept, group * half // GROUPS)
                next(steps)
                wait = []
                for level in range(levels + 1):
                    packed = steps.send(wait)
                    wait = results[0][0][1:] if group == 0 and shift == 0 and level == 0 else []
                remote.append(spread(packed))
            results.append(remote)
            tokens = []

    groups = max(len(result) for result in results)
    width = half // groups
    other = [swap(choose(results, group, width, True, per_sub)) for group in range(groups)]
    mine = [choose(results, group, width, False, per_sub) for group in range(groups)]
    return assemble(mine, other, half)


def solution(mesh):
    return jax.shard_map(
        shards,
        mesh=mesh,
        in_specs=(P(("groups", "seq"), ("tensor", "sub")), P(("tensor", "sub"), "seq"), P("seq")),
        out_specs=(P(("groups", "sub"), "seq"), P(("groups", "sub"), "seq")),
        check_vma=False,
    )
```

time: 98.8 us -> 92.5 us (0.936)
  waiting for transfers between devices: 13.9 us -> 28.3 us
  Pallas kernels: 51.7 us -> 39.6 us
  starting transfers between devices: 29 us -> 22.1 us
    ppermute x15, waiting for transfers between devices: 13.3 us -> 21.1 us  [exchange(): lax.ppermute(values, 'tensor', [(t, t ^ 1 << level) for t in range(tensor...]
    ppermute x15, starting transfers between devices: 23 us -> 16.7 us  [exchange(): lax.ppermute(values, 'tensor', [(t, t ^ 1 << level) for t in range(tensor...]
    ppermute x4, waiting for transfers between devices: 0.01 us -> 5.77 us  [shards(): arrivals.append([lax.ppermute(part, 'seq', pairs) for part in parts])]
    pallas_call x6, Pallas kernels: 40 us -> 35.5 us  [the longest x5 35.5 us: multiply(): pl.pallas_call(body, out_shape=out_shape, in_specs=[VMEM] * spans[-1][1]...]
    pallas_call x6, Pallas kernels: 3.59 us -> 0.36 us  [halve(): pl.pallas_call(functools.partial(halve_body, level), out_shape=[jax.Shape...]
    pallas_call x4, Pallas kernels: 2.38 us -> 0.22 us  [choose(): pl.pallas_call(functools.partial(choose_body, len(picked), count, width,...]
    pallas_call x3, Pallas kernels: 3.86 us -> 2.24 us  [encode(): pl.pallas_call(functools.partial(encode_body, begin), out_shape=jax.Shape...]
    unnamed x4 -> x6, local copies, waits for them, and re-layouts: 2.29 us -> 1.46 us
  transfers between devices with their start and end apart: 24 -> 24, of which waited for: 13 -> 15; matrix products, arithmetic and copies ran while one was open for 1% -> 0% of each run, Pallas kernels for 51% -> 41%
where the time goes in v7:
time: 92.5 us; the launch traced here: 92.4 us
  Pallas kernels  39.6 us (43%)
  waiting for transfers between devices  28.3 us (31%)
  starting transfers between devices  22.1 us (24%)
  local copies, waits for them, and re-layouts  1.46 us (2%)
    pallas_call x5, Pallas kernels, multiply(): pl.pallas_call(body, out_shape=out_shape, in_specs=[VMEM] * spans[-1][1]...  35.5 us
    ppermute x15, waiting for transfers between devices, exchange(): lax.ppermute(values, 'tensor', [(t, t ^ 1 << level) for t in range(tensor...  21.1 us
    ppermute x15, starting transfers between devices, exchange(): lax.ppermute(values, 'tensor', [(t, t ^ 1 << level) for t in range(tensor...  16.7 us
    ppermute x4, waiting for transfers between devices, shards(): arrivals.append([lax.ppermute(part, 'seq', pairs) for part in parts])  5.77 us
    ppermute x4, starting transfers between devices, shards(): arrivals.append([lax.ppermute(part, 'seq', pairs) for part in parts])  5.11 us
    pallas_call x3, Pallas kernels, encode(): pl.pallas_call(functools.partial(encode_body, begin), out_shape=jax.Shape...  2.24 us
  transfers between devices with their start and end apart: 24, of which 15 were waited for; matrix products, arithmetic and copies ran while one was open for 0% of the time, Pallas kernels for 41%

profile of v7, /device:TPU:0, one launch (start us, length us, event | category | flops | bytes accessed | tf_op | source)
XLA Modules:
  0.0 92.4 jit_solution(17942479539247441702)
XLA Ops:
  0.6 1.4 %copy-done = bf16[128,6656]{1,0:T(8,128)(2,1)S(1)} copy-done((bf16[128,6656]{1,0:T(8,128)(2,1)S(1)}, bf16[128,6656]{1,0:T(8,128)(2,1)}, u32[]{:S(2)}) %copy-start) | copy-done | bytes 1703960
  2.1 0.2 shard_map.59
  2.2 3.0 %collective-permute-start = (bf16[128,2048]{1,0:T(8,128)(2,1)S(1)}, bf16[128,2048]{1,0:T(8,128)(2,1)S(1)}, u32[]{:S(2)}, u32[]{:S(2)}) collective-permute-start(bf16[128,2048]{1,0:T(8,128)(2,1)S(1)} %get-tuple-element.27.refs_4_.refs_0_), channel_id=1, source_target_pairs={{0,2},{2,0},{1,3},{3,1},{4,6},{6,4},{5,7},{7,5},{8,10},{10,8},{9,1... | collective-permute-start | bytes 1572872 | tf_op jit(solution)/shard_map/ppermute | solution.py:377
  5.3 0.1 collective-permute-start.2
  5.3 12.7 %shard_map.60.refs_3_ = f32[128,4096]{1,0:T(8,128)S(1)} custom-call(bf16[128,2560]{1,0:T(8,128)(2,1)S(1)} %get-tuple-element.28.refs_0_, bf16[128,1024]{1,0:T(8,128)(2,1)S(1)} %get-tuple-element.29.refs_1_, bf16[128,1024]{1,0:T(8,128)(2,1)S(1)} %get-tuple-element.30.refs_2_, bf16[6656,4096]{1,0:T(8,128)(2,1)} %refs_1_.5, ...), custom_call_target="tpu_custom_call" | custom-call | flops 1 | bytes 1 | tf_op jit(solution)/shard_map/pallas_call | solution.py:136
  18.0 7.3 %shard_map.61 = (bf16[128,2048]{1,0:T(8,128)(2,1)S(1)}, f32[128,2048]{1,0:T(8,128)S(1)}, f32[128,4096]{1,0:T(8,128)S(1)}) custom-call(bf16[128,2048]{1,0:T(8,128)(2,1)S(1)} %get-tuple-element.27.refs_4_.refs_0_, bf16[128,2048]{1,0:T(8,128)(2,1)S(1)} %collective-permute-done.refs_1_, bf16[6656,4096]{1,0:T(8,128)(2,1)} %refs_1_.5, ...), custom_call_target="tpu_custom_call" | custom-call | flops 1 | bytes 1 | tf_op jit(solution)/shard_map/pallas_call | solution.py:136
  25.4 0.1 collective-permute-start.1
  25.5 5.8 %collective-permute-done.2.refs_0_ = bf16[128,2560]{1,0:T(8,128)(2,1)S(1)} collective-permute-done((bf16[128,2560]{1,0:T(8,128)(2,1)S(1)}, bf16[128,2560]{1,0:T(8,128)(2,1)S(1)}, u32[]{:S(2)}, u32[]{:S(2)}) %collective-permute-start.2) | collective-permute-done | bytes 655392 | tf_op jit(solution)/shard_map/ppermute | solution.py:377
  31.2 0.1 shard_map.62
  31.3 1.9 %collective-permute-start.3 = (bf16[64,2048]{1,0:T(8,128)(2,1)S(1)}, bf16[64,2048]{1,0:T(8,128)(2,1)S(1)}, u32[]{:S(2)}, u32[]{:S(2)}) collective-permute-start(bf16[64,2048]{1,0:T(8,128)(2,1)S(1)} %get-tuple-element.34.refs_3_), channel_id=1, source_target_pairs={{0,4},{4,0},{8,12},{12,8},{1,5},{5,1},{9,13},{13,9},{2,6},{6,2},{1... | collective-permute-start | bytes 786440 | tf_op jit(solution)/shard_map/ppermute | solution.py:353
  33.2 1.5 %collective-permute-start.5 = (bf16[128,1024]{1,0:T(8,128)(2,1)S(1)}, bf16[128,1024]{1,0:T(8,128)(2,1)S(1)}, u32[]{:S(2)}, u32[]{:S(2)}) collective-permute-start(bf16[128,1024]{1,0:T(8,128)(2,1)S(1)} %get-tuple-element.29.refs_1_), channel_id=1, source_target_pairs={{0,2},{2,0},{1,3},{3,1},{4,6},{6,4},{5,7},{7,5},{8,10},{10,8},{9,1... | collective-permute-start | bytes 786440 | tf_op jit(solution)/shard_map/ppermute | solution.py:377
  34.7 0.5 collective-permute-start.9
  35.2 7.7 %shard_map.63.refs_0_.refs_2_ = f32[128,4096]{1,0:T(8,128)S(1)} custom-call(bf16[128,2560]{1,0:T(8,128)(2,1)S(1)} %collective-permute-done.2.refs_0_, bf16[6656,4096]{1,0:T(8,128)(2,1)} %refs_1_.5, f32[128,4096]{1,0:T(8,128)S(1)} %get-tuple-element.35.refs_2_, bf16[64,2048]{1,0:T(8,128)(2,1)S(1)} %get-tuple-element.34.refs_3_), custom_call_target="tpu_custom_call" | custom-call | flops 1 | bytes 1 | tf_op jit(solution)/shard_map/pallas_call | solution.py:136
  43.1 2.7 %collective-permute-start.4 = (bf16[32,2048]{1,0:T(8,128)(2,1)S(1)}, bf16[32,2048]{1,0:T(8,128)(2,1)S(1)}, u32[]{:S(2)}, u32[]{:S(2)}) collective-permute-start(bf16[32,2048]{1,0:T(8,128)(2,1)S(1)} %get-tuple-element.37.refs_3_), channel_id=1, source_target_pairs={{0,8},{4,12},{8,0},{12,4},{1,9},{5,13},{9,1},{13,5},{2,10},{6,14},... | collective-permute-start | bytes 393224 | tf_op jit(solution)/shard_map/ppermute | solution.py:353
  45.8 3.9 %shard_map.65.refs_0_.refs_2_ = f32[128,4096]{1,0:T(8,128)S(1)} custom-call(bf16[128,1024]{1,0:T(8,128)(2,1)S(1)} %collective-permute-done.5.refs_0_, bf16[6656,4096]{1,0:T(8,128)(2,1)} %refs_1_.5, f32[128,4096]{1,0:T(8,128)S(1)} %shard_map.63.refs_0_.refs_2_, bf16[32,2048]{1,0:T(8,128)(2,1)S(1)} %get-tuple-element.37.refs_3_), custom_call_target="tpu_custom_call" | custom-call | flops 1 | bytes 1 | tf_op jit(solution)/shard_map/pallas_call | solution.py:136
  49.7 0.7 collective-permute-done.4.came_ref
  50.3 1.0 %shard_map.66.refs_3_.refs_0_ = bf16[32,2176]{1,0:T(8,128)(2,1)S(1)} custom-call(f32[32,2048]{1,0:T(8,128)S(1)} %get-tuple-element.36.kept_ref, bf16[32,2048]{1,0:T(8,128)(2,1)S(1)} %collective-permute-done.4.came_ref, f32[1,4096]{1,0:T(1,128)S(1)} %bitcast.2, f32[128,128]{1,0:T(8,128)S(1)} %copy-done.1, f32[128,4096]{1,0:T(8,128)S(1)} %shard_map.65.refs_0_.refs_2_), custom_call_target="tpu_custom_call" | custom-call | flops 1 | bytes 1 | tf_op jit(solution)/shard_map/pallas_call | solution.py:220
  51.4 0.1 collective-permute-start.6
  51.4 3.1 %collective-permute-start.7 = (bf16[32,2176]{1,0:T(8,128)(2,1)S(1)}, bf16[32,2176]{1,0:T(8,128)(2,1)S(1)}, u32[]{:S(2)}, u32[]{:S(2)}) collective-permute-start(bf16[32,2176]{1,0:T(8,128)(2,1)S(1)} %shard_map.66.refs_3_.refs_0_), channel_id=1, source_target_pairs={{0,8},{4,12},{8,0},{12,4},{1,9},{5,13},{9,1},{13,5},{2,10},{6,14},... | collective-permute-start | bytes 417800 | tf_op jit(solution)/shard_map/ppermute | solution.py:353
  54.6 3.9 %shard_map.67 = (bf16[128,1024]{1,0:T(8,128)(2,1)S(1)}, f32[128,1024]{1,0:T(8,128)S(1)}, bf16[128,1024]{1,0:T(8,128)(2,1)S(1)}, f32[128,1024]{1,0:T(8,128)S(1)}) custom-call(bf16[128,1024]{1,0:T(8,128)(2,1)S(1)} %collective-permute-done.9.refs_0_, bf16[6656,4096]{1,0:T(8,128)(2,1)} %refs_1_.5, f32[128,4096]{1,0:T(8,128)S(1)} %shard_map.65.refs_0_.refs_2_, ...), custom_call_target="tpu_custom_call" | custom-call | flops 1 | bytes 1 | tf_op jit(solution)/shard_map/pallas_call | solution.py:136
  58.5 1.3 %collective-permute-done.7.refs_1_.refs_2_ = bf16[32,2176]{1,0:T(8,128)(2,1)S(1)} collective-permute-done((bf16[32,2176]{1,0:T(8,128)(2,1)S(1)}, bf16[32,2176]{1,0:T(8,128)(2,1)S(1)}, u32[]{:S(2)}, u32[]{:S(2)}) %collective-permute-start.7) | collective-permute-done | bytes 139296 | tf_op jit(solution)/shard_map/ppermute | solution.py:353
  59.8 0.2 collective-permute-start.8
  60.2 1.9 %collective-permute-start.11 = (bf16[64,1024]{1,0:T(8,128)(2,1)S(1)}, bf16[64,1024]{1,0:T(8,128)(2,1)S(1)}, u32[]{:S(2)}, u32[]{:S(2)}) collective-permute-start(bf16[64,1024]{1,0:T(8,128)(2,1)S(1)} %get-tuple-element.41), channel_id=1, source_target_pairs={{0,4},{4,0},{8,12},{12,8},{1,5},{5,1},{9,13},{13,9},{2,6},{6,2},{1... | collective-permute-start | bytes 393224 | tf_op jit(solution)/shard_map/ppermute | solution.py:353
  62.1 0.3 collective-permute-start.17
  62.4 3.9 %collective-permute-done.8.refs_2_.refs_3_ = bf16[32,2176]{1,0:T(8,128)(2,1)S(1)} collective-permute-done((bf16[32,2176]{1,0:T(8,128)(2,1)S(1)}, bf16[32,2176]{1,0:T(8,128)(2,1)S(1)}, u32[]{:S(2)}, u32[]{:S(2)}) %collective-permute-start.8) | collective-permute-done | bytes 139296 | tf_op jit(solution)/shard_map/ppermute | solution.py:353
  66.3 2.8 %collective-permute-done.11.came_ref = bf16[64,1024]{1,0:T(8,128)(2,1)S(1)} collective-permute-done((bf16[64,1024]{1,0:T(8,128)(2,1)S(1)}, bf16[64,1024]{1,0:T(8,128)(2,1)S(1)}, u32[]{:S(2)}, u32[]{:S(2)}) %collective-permute-start.11) | collective-permute-done | bytes 131104 | tf_op jit(solution)/shard_map/ppermute | solution.py:353
  69.2 0.8 collective-permute-start.12
  70.0 1.6 %collective-permute-done.17.came_ref = bf16[64,1024]{1,0:T(8,128)(2,1)S(1)} collective-permute-done((bf16[64,1024]{1,0:T(8,128)(2,1)S(1)}, bf16[64,1024]{1,0:T(8,128)(2,1)S(1)}, u32[]{:S(2)}, u32[]{:S(2)}) %collective-permute-start.17) | collective-permute-done | bytes 131104 | tf_op jit(solution)/shard_map/ppermute | solution.py:353
  71.6 0.9 collective-permute-start.18
  72.5 3.0 %collective-permute-done.12.came_ref = bf16[32,1024]{1,0:T(8,128)(2,1)S(1)} collective-permute-done((bf16[32,1024]{1,0:T(8,128)(2,1)S(1)}, bf16[32,1024]{1,0:T(8,128)(2,1)S(1)}, u32[]{:S(2)}, u32[]{:S(2)}) %collective-permute-start.12) | collective-permute-done | bytes 65568 | tf_op jit(solution)/shard_map/ppermute | solution.py:353
  75.5 0.6 shard_map.70.refs_4_
  76.1 0.1 collective-permute-start.14
  76.2 2.5 %collective-permute-done.18.came_ref = bf16[32,1024]{1,0:T(8,128)(2,1)S(1)} collective-permute-done((bf16[32,1024]{1,0:T(8,128)(2,1)S(1)}, bf16[32,1024]{1,0:T(8,128)(2,1)S(1)}, u32[]{:S(2)}, u32[]{:S(2)}) %collective-permute-start.18) | collective-permute-done | bytes 65568 | tf_op jit(solution)/shard_map/ppermute | solution.py:353
  78.7 0.6 shard_map.75.refs_4_
  79.3 0.5 collective-permute-start.20
  79.8 2.2 %collective-permute-start.13 = (bf16[32,1152]{1,0:T(8,128)(2,1)S(1)}, bf16[32,1152]{1,0:T(8,128)(2,1)S(1)}, u32[]{:S(2)}, u32[]{:S(2)}) collective-permute-start(bf16[32,1152]{1,0:T(8,128)(2,1)S(1)} %shard_map.70.refs_4_), channel_id=1, source_target_pairs={{0,4},{4,0},{8,12},{12,8},{1,5},{5,1},{9,13},{13,9},{2,6},{6,2},{1... | collective-permute-start | bytes 221192 | tf_op jit(solution)/shard_map/ppermute | solution.py:353
  82.0 0.8 collective-permute-done.14.refs_6_
  82.8 2.0 %collective-permute-start.19 = (bf16[32,1152]{1,0:T(8,128)(2,1)S(1)}, bf16[32,1152]{1,0:T(8,128)(2,1)S(1)}, u32[]{:S(2)}, u32[]{:S(2)}) collective-permute-start(bf16[32,1152]{1,0:T(8,128)(2,1)S(1)} %shard_map.75.refs_4_), channel_id=1, source_target_pairs={{0,4},{4,0},{8,12},{12,8},{1,5},{5,1},{9,13},{13,9},{2,6},{6,2},{1... | collective-permute-start | bytes 221192 | tf_op jit(solution)/shard_map/ppermute | solution.py:353
  84.8 0.4 collective-permute-done.20.refs_6_
  85.2 0.2 collective-permute-start.21
  85.4 0.5 collective-permute-done.13.refs_5_
  85.9 2.0 %collective-permute-done.15.refs_7_ = bf16[32,1152]{1,0:T(8,128)(2,1)S(1)} collective-permute-done((bf16[32,1152]{1,0:T(8,128)(2,1)S(1)}, bf16[32,1152]{1,0:T(8,128)(2,1)S(1)}, u32[]{:S(2)}, u32[]{:S(2)}) %collective-permute-start.15) | collective-permute-done | bytes 73760 | tf_op jit(solution)/shard_map/ppermute | solution.py:353
  87.9 0.1 collective-permute-start.22
  88.0 0.7 collective-permute-done.19.refs_5_
  88.7 0.9 collective-permute-done.21.refs_7_
  89.8 0.1 shard_map.76.refs_1_
  89.9 1.4 %collective-permute-done.23.refs_3_ = bf16[128,1152]{1,0:T(8,128)(2,1)S(1)} collective-permute-done((bf16[128,1152]{1,0:T(8,128)(2,1)S(1)}, bf16[128,1152]{1,0:T(8,128)(2,1)S(1)}, u32[]{:S(2)}, u32[]{:S(2)}) %collective-permute-start.23) | collective-permute-done | bytes 294944 | tf_op jit(solution)/shard_map/ppermute | solution.py:350
  91.3 1.1 %shard_map.79 = (bf16[128,4096]{1,0:T(8,128)(2,1)}, bf16[32,128]{1,0:T(8,128)(2,1)}) custom-call(bf16[128,1152]{1,0:T(8,128)(2,1)S(1)} %shard_map.71.refs_0_, bf16[128,1152]{1,0:T(8,128)(2,1)S(1)} %shard_map.76.refs_1_, bf16[128,1152]{1,0:T(8,128)(2,1)S(1)} %collective-permute-done.22.refs_2_, bf16[128,1152]{1,0:T(8,128)(2,1)S(1)} %collective-permute-done.23.refs_3_), custom_call_target="tpu_custom_call" | custom-call | flops 1 | bytes 1 | tf_op jit(solution)/shard_map/pallas_call | solution.py:315
  (28 shorter events, 0.6 us)
Async XLA Ops:
  0.6 1.5 %copy-start = (bf16[128,6656]{1,0:T(8,128)(2,1)S(1)}, bf16[128,6656]{1,0:T(8,128)(2,1)}, u32[]{:S(2)}) copy-start(bf16[128,6656]{1,0:T(8,128)(2,1)} %in_ref.1) | copy-start | bytes 5111812
  2.2 15.8 %collective-permute-start = (bf16[128,2048]{1,0:T(8,128)(2,1)S(1)}, bf16[128,2048]{1,0:T(8,128)(2,1)S(1)}, u32[]{:S(2)}, u32[]{:S(2)}) collective-permute-start(bf16[128,2048]{1,0:T(8,128)(2,1)S(1)} %get-tuple-element.27.refs_4_.refs_0_), channel_id=1, source_target_pairs={{0,2},{2,0},{1,3},{3,1},{4,6},{6,4},{5,7},{7,5},{8,10},{10,8},{9,1... | collective-permute-start | bytes 1572872 | tf_op jit(solution)/shard_map/ppermute | solution.py:377
  5.3 26.0 %collective-permute-start.2 = (bf16[128,2560]{1,0:T(8,128)(2,1)S(1)}, bf16[128,2560]{1,0:T(8,128)(2,1)S(1)}, u32[]{:S(2)}, u32[]{:S(2)}) collective-permute-start(bf16[128,2560]{1,0:T(8,128)(2,1)S(1)} %get-tuple-element.28.refs_0_), channel_id=1, source_target_pairs={{0,2},{2,0},{1,3},{3,1},{4,6},{6,4},{5,7},{7,5},{8,10},{10,8},{9,1... | collective-permute-start | bytes 1966088 | tf_op jit(solution)/shard_map/ppermute | solution.py:377
  25.4 5.8 %collective-permute-start.1 = (bf16[128,2048]{1,0:T(8,128)(2,1)S(1)}, bf16[128,2048]{1,0:T(8,128)(2,1)S(1)}, u32[]{:S(2)}, u32[]{:S(2)}) collective-permute-start(bf16[128,2048]{1,0:T(8,128)(2,1)S(1)} %get-tuple-element.32), channel_id=1, source_target_pairs={{0,1},{1,0},{2,3},{3,2},{4,5},{5,4},{6,7},{7,6},{8,9},{9,8},{10,11... | collective-permute-start | bytes 1572872 | tf_op jit(solution)/shard_map/ppermute | solution.py:350
  31.3 11.7 %collective-permute-start.3 = (bf16[64,2048]{1,0:T(8,128)(2,1)S(1)}, bf16[64,2048]{1,0:T(8,128)(2,1)S(1)}, u32[]{:S(2)}, u32[]{:S(2)}) collective-permute-start(bf16[64,2048]{1,0:T(8,128)(2,1)S(1)} %get-tuple-element.34.refs_3_), channel_id=1, source_target_pairs={{0,4},{4,0},{8,12},{12,8},{1,5},{5,1},{9,13},{13,9},{2,6},{6,2},{1... | collective-permute-start | bytes 786440 | tf_op jit(solution)/shard_map/ppermute | solution.py:353
  33.2 12.5 %collective-permute-start.5 = (bf16[128,1024]{1,0:T(8,128)(2,1)S(1)}, bf16[128,1024]{1,0:T(8,128)(2,1)S(1)}, u32[]{:S(2)}, u32[]{:S(2)}) collective-permute-start(bf16[128,1024]{1,0:T(8,128)(2,1)S(1)} %get-tuple-element.29.refs_1_), channel_id=1, source_target_pairs={{0,2},{2,0},{1,3},{3,1},{4,6},{6,4},{5,7},{7,5},{8,10},{10,8},{9,1... | collective-permute-start | bytes 786440 | tf_op jit(solution)/shard_map/ppermute | solution.py:377
  34.7 19.9 %collective-permute-start.9 = (bf16[128,1024]{1,0:T(8,128)(2,1)S(1)}, bf16[128,1024]{1,0:T(8,128)(2,1)S(1)}, u32[]{:S(2)}, u32[]{:S(2)}) collective-permute-start(bf16[128,1024]{1,0:T(8,128)(2,1)S(1)} %get-tuple-element.30.refs_2_), channel_id=1, source_target_pairs={{0,2},{2,0},{1,3},{3,1},{4,6},{6,4},{5,7},{7,5},{8,10},{10,8},{9,1... | collective-permute-start | bytes 786440 | tf_op jit(solution)/shard_map/ppermute | solution.py:377
  43.0 2.8 %copy-start.2 = (s32[4096]{0:T(1024)S(1)}, s32[4096]{0:T(1024)}, u32[]{:S(2)}) copy-start(s32[4096]{0:T(1024)} %param.6) | copy-start | bytes 49156
  43.1 7.3 %collective-permute-start.4 = (bf16[32,2048]{1,0:T(8,128)(2,1)S(1)}, bf16[32,2048]{1,0:T(8,128)(2,1)S(1)}, u32[]{:S(2)}, u32[]{:S(2)}) collective-permute-start(bf16[32,2048]{1,0:T(8,128)(2,1)S(1)} %get-tuple-element.37.refs_3_), channel_id=1, source_target_pairs={{0,8},{4,12},{8,0},{12,4},{1,9},{5,13},{9,1},{13,5},{2,10},{6,14},... | collective-permute-start | bytes 393224 | tf_op jit(solution)/shard_map/ppermute | solution.py:353
  45.7 4.6 %copy-start.1 = (f32[128,128]{1,0:T(8,128)S(1)}, f32[128,128]{1,0:T(8,128)}, u32[]{:S(2)}) copy-start(f32[128,128]{1,0:T(8,128)} %constant.7.clone.rotation_ref) | copy-start | bytes 196612
  51.4 7.1 %collective-permute-start.6 = (bf16[32,2176]{1,0:T(8,128)(2,1)S(1)}, bf16[32,2176]{1,0:T(8,128)(2,1)S(1)}, u32[]{:S(2)}, u32[]{:S(2)}) collective-permute-start(bf16[32,2176]{1,0:T(8,128)(2,1)S(1)} %shard_map.66.refs_3_.refs_0_), channel_id=1, source_target_pairs={{0,4},{4,0},{8,12},{12,8},{1,5},{5,1},{9,13},{13,9},{2,6},{6,2},{1... | collective-permute-start | bytes 417800 | tf_op jit(solution)/shard_map/ppermute | solution.py:353
  51.4 8.4 %collective-permute-start.7 = (bf16[32,2176]{1,0:T(8,128)(2,1)S(1)}, bf16[32,2176]{1,0:T(8,128)(2,1)S(1)}, u32[]{:S(2)}, u32[]{:S(2)}) collective-permute-start(bf16[32,2176]{1,0:T(8,128)(2,1)S(1)} %shard_map.66.refs_3_.refs_0_), channel_id=1, source_target_pairs={{0,8},{4,12},{8,0},{12,4},{1,9},{5,13},{9,1},{13,5},{2,10},{6,14},... | collective-permute-start | bytes 417800 | tf_op jit(solution)/shard_map/ppermute | solution.py:353
  58.4 1.7 %collective-permute-start.10 = (bf16[128,1024]{1,0:T(8,128)(2,1)S(1)}, bf16[128,1024]{1,0:T(8,128)(2,1)S(1)}, u32[]{:S(2)}, u32[]{:S(2)}) collective-permute-start(bf16[128,1024]{1,0:T(8,128)(2,1)S(1)} %get-tuple-element.39), channel_id=1, source_target_pairs={{0,1},{1,0},{2,3},{3,2},{4,5},{5,4},{6,7},{7,6},{8,9},{9,8},{10,11... | collective-permute-start | bytes 786440 | tf_op jit(solution)/shard_map/ppermute | solution.py:350
  59.8 2.2 %collective-permute-start.16 = (bf16[128,1024]{1,0:T(8,128)(2,1)S(1)}, bf16[128,1024]{1,0:T(8,128)(2,1)S(1)}, u32[]{:S(2)}, u32[]{:S(2)}) collective-permute-start(bf16[128,1024]{1,0:T(8,128)(2,1)S(1)} %shard_map.72), channel_id=1, source_target_pairs={{0,1},{1,0},{2,3},{3,2},{4,5},{5,4},{6,7},{7,6},{8,9},{9,8},{10,11... | collective-permute-start | bytes 786440 | tf_op jit(solution)/shard_map/ppermute | solution.py:350
  59.8 6.5 %collective-permute-start.8 = (bf16[32,2176]{1,0:T(8,128)(2,1)S(1)}, bf16[32,2176]{1,0:T(8,128)(2,1)S(1)}, u32[]{:S(2)}, u32[]{:S(2)}) collective-permute-start(bf16[32,2176]{1,0:T(8,128)(2,1)S(1)} %collective-permute-done.7.refs_1_.refs_2_), channel_id=1, source_target_pairs={{0,4},{4,0},{8,12},{12,8},{1,5},{5,1},{9,13},{13,9},{2,6},{6,2},{1... | collective-permute-start | bytes 417800 | tf_op jit(solution)/shard_map/ppermute | solution.py:353
  60.2 9.0 %collective-permute-start.11 = (bf16[64,1024]{1,0:T(8,128)(2,1)S(1)}, bf16[64,1024]{1,0:T(8,128)(2,1)S(1)}, u32[]{:S(2)}, u32[]{:S(2)}) collective-permute-start(bf16[64,1024]{1,0:T(8,128)(2,1)S(1)} %get-tuple-element.41), channel_id=1, source_target_pairs={{0,4},{4,0},{8,12},{12,8},{1,5},{5,1},{9,13},{13,9},{2,6},{6,2},{1... | collective-permute-start | bytes 393224 | tf_op jit(solution)/shard_map/ppermute | solution.py:353
  62.1 9.5 %collective-permute-start.17 = (bf16[64,1024]{1,0:T(8,128)(2,1)S(1)}, bf16[64,1024]{1,0:T(8,128)(2,1)S(1)}, u32[]{:S(2)}, u32[]{:S(2)}) collective-permute-start(bf16[64,1024]{1,0:T(8,128)(2,1)S(1)} %get-tuple-element.47), channel_id=1, source_target_pairs={{0,4},{4,0},{8,12},{12,8},{1,5},{5,1},{9,13},{13,9},{2,6},{6,2},{1... | collective-permute-start | bytes 393224 | tf_op jit(solution)/shard_map/ppermute | solution.py:353
  69.2 6.3 %collective-permute-start.12 = (bf16[32,1024]{1,0:T(8,128)(2,1)S(1)}, bf16[32,1024]{1,0:T(8,128)(2,1)S(1)}, u32[]{:S(2)}, u32[]{:S(2)}) collective-permute-start(bf16[32,1024]{1,0:T(8,128)(2,1)S(1)} %get-tuple-element.43), channel_id=1, source_target_pairs={{0,8},{4,12},{8,0},{12,4},{1,9},{5,13},{9,1},{13,5},{2,10},{6,14},... | collective-permute-start | bytes 196616 | tf_op jit(solution)/shard_map/ppermute | solution.py:353
  71.6 7.1 %collective-permute-start.18 = (bf16[32,1024]{1,0:T(8,128)(2,1)S(1)}, bf16[32,1024]{1,0:T(8,128)(2,1)S(1)}, u32[]{:S(2)}, u32[]{:S(2)}) collective-permute-start(bf16[32,1024]{1,0:T(8,128)(2,1)S(1)} %get-tuple-element.49), channel_id=1, source_target_pairs={{0,8},{4,12},{8,0},{12,4},{1,9},{5,13},{9,1},{13,5},{2,10},{6,14},... | collective-permute-start | bytes 196616 | tf_op jit(solution)/shard_map/ppermute | solution.py:353
  76.1 6.7 %collective-permute-start.14 = (bf16[32,1152]{1,0:T(8,128)(2,1)S(1)}, bf16[32,1152]{1,0:T(8,128)(2,1)S(1)}, u32[]{:S(2)}, u32[]{:S(2)}) collective-permute-start(bf16[32,1152]{1,0:T(8,128)(2,1)S(1)} %shard_map.70.refs_4_), channel_id=1, source_target_pairs={{0,8},{4,12},{8,0},{12,4},{1,9},{5,13},{9,1},{13,5},{2,10},{6,14},... | collective-permute-start | bytes 221192 | tf_op jit(solution)/shard_map/ppermute | solution.py:353
  79.3 5.9 %collective-permute-start.20 = (bf16[32,1152]{1,0:T(8,128)(2,1)S(1)}, bf16[32,1152]{1,0:T(8,128)(2,1)S(1)}, u32[]{:S(2)}, u32[]{:S(2)}) collective-permute-start(bf16[32,1152]{1,0:T(8,128)(2,1)S(1)} %shard_map.75.refs_4_), channel_id=1, source_target_pairs={{0,8},{4,12},{8,0},{12,4},{1,9},{5,13},{9,1},{13,5},{2,10},{6,14},... | collective-permute-start | bytes 221192 | tf_op jit(solution)/shard_map/ppermute | solution.py:353
  79.8 6.2 %collective-permute-start.13 = (bf16[32,1152]{1,0:T(8,128)(2,1)S(1)}, bf16[32,1152]{1,0:T(8,128)(2,1)S(1)}, u32[]{:S(2)}, u32[]{:S(2)}) collective-permute-start(bf16[32,1152]{1,0:T(8,128)(2,1)S(1)} %shard_map.70.refs_4_), channel_id=1, source_target_pairs={{0,4},{4,0},{8,12},{12,8},{1,5},{5,1},{9,13},{13,9},{2,6},{6,2},{1... | collective-permute-start | bytes 221192 | tf_op jit(solution)/shard_map/ppermute | solution.py:353
  82.8 5.1 %collective-permute-start.15 = (bf16[32,1152]{1,0:T(8,128)(2,1)S(1)}, bf16[32,1152]{1,0:T(8,128)(2,1)S(1)}, u32[]{:S(2)}, u32[]{:S(2)}) collective-permute-start(bf16[32,1152]{1,0:T(8,128)(2,1)S(1)} %collective-permute-done.14.refs_6_), channel_id=1, source_target_pairs={{0,4},{4,0},{8,12},{12,8},{1,5},{5,1},{9,13},{13,9},{2,6},{6,2},{1... | collective-permute-start | bytes 221192 | tf_op jit(solution)/shard_map/ppermute | solution.py:353
  82.8 5.9 %collective-permute-start.19 = (bf16[32,1152]{1,0:T(8,128)(2,1)S(1)}, bf16[32,1152]{1,0:T(8,128)(2,1)S(1)}, u32[]{:S(2)}, u32[]{:S(2)}) collective-permute-start(bf16[32,1152]{1,0:T(8,128)(2,1)S(1)} %shard_map.75.refs_4_), channel_id=1, source_target_pairs={{0,4},{4,0},{8,12},{12,8},{1,5},{5,1},{9,13},{13,9},{2,6},{6,2},{1... | collective-permute-start | bytes 221192 | tf_op jit(solution)/shard_map/ppermute | solution.py:353
  85.2 4.4 %collective-permute-start.21 = (bf16[32,1152]{1,0:T(8,128)(2,1)S(1)}, bf16[32,1152]{1,0:T(8,128)(2,1)S(1)}, u32[]{:S(2)}, u32[]{:S(2)}) collective-permute-start(bf16[32,1152]{1,0:T(8,128)(2,1)S(1)} %collective-permute-done.20.refs_6_), channel_id=1, source_target_pairs={{0,4},{4,0},{8,12},{12,8},{1,5},{5,1},{9,13},{13,9},{2,6},{6,2},{1... | collective-permute-start | bytes 221192 | tf_op jit(solution)/shard_map/ppermute | solution.py:353
  87.9 1.9 %collective-permute-start.22 = (bf16[128,1152]{1,0:T(8,128)(2,1)S(1)}, bf16[128,1152]{1,0:T(8,128)(2,1)S(1)}, u32[]{:S(2)}, u32[]{:S(2)}) collective-permute-start(bf16[128,1152]{1,0:T(8,128)(2,1)S(1)} %shard_map.77), channel_id=1, source_target_pairs={{0,1},{1,0},{2,3},{3,2},{4,5},{5,4},{6,7},{7,6},{8,9},{9,8},{10,11... | collective-permute-start | bytes 884744 | tf_op jit(solution)/shard_map/ppermute | solution.py:350
  89.6 1.6 %collective-permute-start.23 = (bf16[128,1152]{1,0:T(8,128)(2,1)S(1)}, bf16[128,1152]{1,0:T(8,128)(2,1)S(1)}, u32[]{:S(2)}, u32[]{:S(2)}) collective-permute-start(bf16[128,1152]{1,0:T(8,128)(2,1)S(1)} %shard_map.78), channel_id=1, source_target_pairs={{0,1},{1,0},{2,3},{3,2},{4,5},{5,4},{6,7},{7,6},{8,9},{9,8},{10,11... | collective-permute-start | bytes 884744 | tf_op jit(solution)/shard_map/ppermute | solution.py:350

commit v8 on v7

--- a/solution.py
+++ b/solution.py
@@ -13,7 +13,7 @@
 UNIT = 512
 GROUPS = 2
 VMEM_LIMIT = 6 * 2**20
-SHARES = (4, 5, 2)
+SHARES = (4, 3, 3)
 epsilon = 1e-06
 
 SMALL = pl.CostEstimate(flops=1, bytes_accessed=1, transcendentals=0)
@@ -161,37 +161,41 @@
     )(values, *tokens)
 
 
-def halve_body(level, kept_ref, came_ref, *refs):
-    sent_out, kept_out = refs[-2:]
-    half = sent_out.shape[0]
+def halve_body(level, count, *refs):
+    kept_refs, came_refs, (sent_out, kept_out) = refs[:count], refs[count : 2 * count], refs[-2:]
+    half, columns = sent_out.shape
+    width = columns // count
 
     def put(bit):
         mine, other = slice(bit * half, (bit + 1) * half), slice((1 - bit) * half, (2 - bit) * half)
-        kept_out[...] = kept_ref[mine] + came_ref[mine].astype(jnp.float32)
-        sent_out[...] = (kept_ref[other] + came_ref[other].astype(jnp.float32)).astype(jnp.bfloat16)
+        for index, (kept_ref, came_ref) in enumerate(zip(kept_refs, came_refs)):
+            at = slice(index * width, (index + 1) * width)
+            kept_out[:, at] = kept_ref[mine] + came_ref[mine].astype(jnp.float32)
+            sent_out[:, at] = (kept_ref[other] + came_ref[other].astype(jnp.float32)).astype(jnp.bfloat16)
 
     for bit in range(2):
         pl.when(lax.axis_index("tensor") >> level & 1 == bit)(functools.partial(put, bit))
 
 
 def halve(kept, came, level, tokens=()):
-    rows, columns = kept.shape
-    half = rows // 2
+    rows, columns = kept[0].shape
+    half, columns = rows // 2, columns * len(kept)
     if half % 16:
-        total, bit = kept + came.astype(jnp.float32), lax.axis_index("tensor") >> level & 1
+        total = jnp.concatenate(kept, axis=1) + jnp.concatenate(came, axis=1).astype(jnp.float32)
+        bit = lax.axis_index("tensor") >> level & 1
         sent = lax.dynamic_slice_in_dim(total, (1 - bit) * half, half, 0).astype(jnp.bfloat16)
         return sent, lax.dynamic_slice_in_dim(total, bit * half, half, 0)
     return pl.pallas_call(
-        functools.partial(halve_body, level),
+        functools.partial(halve_body, level, len(kept)),
         out_shape=[
             jax.ShapeDtypeStruct((half, columns), jnp.bfloat16),
             jax.ShapeDtypeStruct((half, columns), jnp.float32),
         ],
-        in_specs=[VMEM, VMEM] + [ANY] * len(tokens),
+        in_specs=[VMEM] * (2 * len(kept)) + [ANY] * len(tokens),
         out_specs=[VMEM, VMEM],
         compiler_params=PARAMS,
         cost_estimate=SMALL,
-    )(kept, came, *tokens)
+    )(*kept, *came, *tokens)
 
 
 def encode_body(begin, kept_ref, came_ref, flips_ref, rotation_ref, *refs):
@@ -352,14 +356,14 @@
     def exchange(values, level):
         return lax.ppermute(values, "tensor", [(t, t ^ 1 << level) for t in range(tensor_count)])
 
-    def reduce(sent, kept, begin):
+    def reduce(halves, begin):
         tokens = (yield None) or []
-        came = swap(sent)
+        kept, came = halves[1::2], [swap(sent) for sent in halves[::2]]
         for level in range(levels):
-            sent, kept = halve(kept, came, level, tokens)
+            sent, held = halve(kept, came, level, tokens)
             tokens = (yield sent) or []
-            came = exchange(sent, level)
-        yield encode(kept, came, begin, flips, rotation, tokens)
+            kept, came = [held], [exchange(sent, level)]
+        yield encode(kept[0], came[0], begin, flips, rotation, tokens)
 
     def spread(packed):
         pieces = {0: packed}
@@ -378,17 +382,17 @@
 
     if len(sizes) == 1:
         outs = multiply([[parts[0]], [arrivals[0][0]]], down_weight, 0, [None, None], [True, True], wide_chunk)
-        reduced = [list(reduce(*outs[:2], 0))[-1], list(reduce(*outs[2:], 0))[-1]]
+        reduced = [list(reduce(outs[:2], 0))[-1], list(reduce(outs[2:], 0))[-1]]
         for arrived in arrivals[1:]:
             outs = multiply([[arrived[0]]], down_weight, 0, [None], [True], wide_chunk)
-            reduced.append(list(reduce(*outs, 0))[-1])
+            reduced.append(list(reduce(outs, 0))[-1])
         results = [[spread(packed)] for packed in reduced]
     else:
         (own,) = multiply([parts[1:]], down_weight, sizes[0], [None], [False], wide, tokens=parts[:1])
-        sent, kept, total = multiply(
-            [[parts[0]], [arrivals[0][0]]], down_weight, 0, [own, None], [True, False], wide_chunk
+        *halves, total = multiply(
+            [[parts[0]], [arrivals[0][0]]], down_weight, 0, [own, None], [True, False], wide_chunk, groups=GROUPS
         )
-        own_steps = reduce(sent, kept, 0)
+        own_steps = reduce(halves, 0)
         next(own_steps)
         tokens = [own_steps.send([arrivals[0][1]])]
         results = []
@@ -409,18 +413,25 @@
             outs = multiply(
                 [[arrived[-1]]], down_weight, places[-1], [total], [True], wide_chunk, groups=GROUPS, tokens=tokens
             )
-            remote = []
+            remote, all_steps = [], []
             for group in range(GROUPS):
                 sent, kept = outs[2 * group : 2 * group + 2]
                 if group == GROUPS - 1 and shift == 0 and levels > 1:
                     sent = gate(sent, [results[0][0][1], results[0][0][1 << levels - 1]])
-                steps = reduce(sent, kept, group * half // GROUPS)
-                next(steps)
-                wait = []
-                for level in range(levels + 1):
-                    packed = steps.send(wait)
-                    wait = results[0][0][1:] if group == 0 and shift == 0 and level == 0 else []
-                remote.append(spread(packed))
+                all_steps.append(reduce([sent, kept], group * half // GROUPS))
+                next(all_steps[-1])
+            last = []
+            for level in range(levels + 1):
+                for group, steps in enumerate(all_steps):
+                    wait = list(last) if group == 0 else []
+                    if group == 0 and level == 1 and shift == 0:
+                        wait += results[0][0][1:]
+                    if remote:
+                        wait.append(remote[-1][1])
+                    step = steps.send(wait)
+                    if level == levels:
+                        remote.append(spread(step))
+                last = [step]
             results.append(remote)
             tokens = []
 

time: 92.5 us -> 95.5 us (1.032)
  starting transfers between devices: 22.1 us -> 25.9 us
    ppermute x4, waiting for transfers between devices: 5.77 us -> 2.04 us  [shards(): arrivals.append([lax.ppermute(part, 'seq', pairs) for part in parts])]
    ppermute x15, starting transfers between devices: 16.7 us -> 19.5 us  [exchange(): lax.ppermute(values, 'tensor', [(t, t ^ 1 << level) for t in range(tensor...]
    ppermute x15, waiting for transfers between devices: 21.1 us -> 22.6 us  [exchange(): lax.ppermute(values, 'tensor', [(t, t ^ 1 << level) for t in range(tensor...]
    ppermute x5 -> x6, waiting for transfers between devices: 1.41 us -> 2.8 us  [swap(): return lax.ppermute(values, 'sub', [(0, 1), (1, 0)])]
    ppermute x5 -> x6, starting transfers between devices: 0.29 us -> 1.26 us  [swap(): return lax.ppermute(values, 'sub', [(0, 1), (1, 0)])]
  transfers between devices with their start and end apart: 24 -> 25, of which waited for: 15 -> 14; matrix products, arithmetic and copies ran while one was open for 0% -> 0% of each run, Pallas kernels for 41% -> 39%
where the time goes in v8:
time: 95.5 us; the launch traced here: 95.3 us
  Pallas kernels  39.6 us (41%)
  waiting for transfers between devices  27.5 us (29%)
  starting transfers between devices  25.9 us (27%)
  local copies, waits for them, and re-layouts  1.46 us (2%)
    pallas_call x5, Pallas kernels, multiply(): pl.pallas_call(body, out_shape=out_shape, in_specs=[VMEM] * spans[-1][1]...  35.5 us
    ppermute x15, waiting for transfers between devices, exchange(): lax.ppermute(values, 'tensor', [(t, t ^ 1 << level) for t in range(tensor...  22.6 us
    ppermute x15, starting transfers between devices, exchange(): lax.ppermute(values, 'tensor', [(t, t ^ 1 << level) for t in range(tensor...  19.5 us
    ppermute x4, starting transfers between devices, shards(): arrivals.append([lax.ppermute(part, 'seq', pairs) for part in parts])  5.11 us
    ppermute x6, waiting for transfers between devices, swap(): return lax.ppermute(values, 'sub', [(0, 1), (1, 0)])  2.8 us
    pallas_call x3, Pallas kernels, encode(): pl.pallas_call(functools.partial(encode_body, begin), out_shape=jax.Shape...  2.25 us
    ppermute x4, waiting for transfers between devices, shards(): arrivals.append([lax.ppermute(part, 'seq', pairs) for part in parts])  2.04 us
  transfers between devices with their start and end apart: 25, of which 14 were waited for; matrix products, arithmetic and copies ran while one was open for 0% of the time, Pallas kernels for 39%

profile of v8, /device:TPU:0, one launch (start us, length us, event | category | flops | bytes accessed | tf_op | source)
XLA Modules:
  0.0 95.3 jit_solution(15445689922049370382)
XLA Ops:
  0.6 1.4 %copy-done = bf16[128,6656]{1,0:T(8,128)(2,1)S(1)} copy-done((bf16[128,6656]{1,0:T(8,128)(2,1)S(1)}, bf16[128,6656]{1,0:T(8,128)(2,1)}, u32[]{:S(2)}) %copy-start) | copy-done | bytes 1703960
  2.1 0.2 shard_map.59
  2.3 3.0 %collective-permute-start = (bf16[128,2048]{1,0:T(8,128)(2,1)S(1)}, bf16[128,2048]{1,0:T(8,128)(2,1)S(1)}, u32[]{:S(2)}, u32[]{:S(2)}) collective-permute-start(bf16[128,2048]{1,0:T(8,128)(2,1)S(1)} %get-tuple-element.29.refs_4_.refs_0_), channel_id=1, source_target_pairs={{0,2},{2,0},{1,3},{3,1},{4,6},{6,4},{5,7},{7,5},{8,10},{10,8},{9,1... | collective-permute-start | bytes 1572872 | tf_op jit(solution)/shard_map/ppermute | solution.py:381
  5.3 0.1 collective-permute-start.3
  5.3 12.7 %shard_map.60.refs_3_ = f32[128,4096]{1,0:T(8,128)S(1)} custom-call(bf16[128,1536]{1,0:T(8,128)(2,1)S(1)} %get-tuple-element.30.refs_0_, bf16[128,1536]{1,0:T(8,128)(2,1)S(1)} %get-tuple-element.31.refs_1_, bf16[128,1536]{1,0:T(8,128)(2,1)S(1)} %get-tuple-element.32.refs_2_, bf16[6656,4096]{1,0:T(8,128)(2,1)} %refs_1_.5, ...), custom_call_target="tpu_custom_call" | custom-call | flops 1 | bytes 1 | tf_op jit(solution)/shard_map/pallas_call | solution.py:136
  18.0 7.3 %shard_map.61 = (bf16[128,1024]{1,0:T(8,128)(2,1)S(1)}, f32[128,1024]{1,0:T(8,128)S(1)}, bf16[128,1024]{1,0:T(8,128)(2,1)S(1)}, f32[128,1024]{1,0:T(8,128)S(1)}, f32[128,4096]{1,0:T(8,128)S(1)}) custom-call(bf16[128,2048]{1,0:T(8,128)(2,1)S(1)} %get-tuple-element.29.refs_4_.refs_0_, bf16[128,2048]{1,0:T(8,128)(2,1)S(1)} %collective-permute-done.refs_1_, ...), custom_call_target="tpu_custom_call" | custom-call | flops 1 | bytes 1 | tf_op jit(solution)/shard_map/pallas_call | solution.py:136
  25.4 0.1 collective-permute-start.1
  25.5 0.5 collective-permute-start.2
  26.0 1.0 %collective-permute-done.1.refs_2_ = bf16[128,1024]{1,0:T(8,128)(2,1)S(1)} collective-permute-done((bf16[128,1024]{1,0:T(8,128)(2,1)S(1)}, bf16[128,1024]{1,0:T(8,128)(2,1)S(1)}, u32[]{:S(2)}, u32[]{:S(2)}) %collective-permute-start.1) | collective-permute-done | bytes 262176 | tf_op jit(solution)/shard_map/ppermute | solution.py:354
  27.0 0.4 collective-permute-done.2.refs_3_
  27.4 0.1 shard_map.62
  27.4 2.2 %collective-permute-start.4 = (bf16[64,2048]{1,0:T(8,128)(2,1)S(1)}, bf16[64,2048]{1,0:T(8,128)(2,1)S(1)}, u32[]{:S(2)}, u32[]{:S(2)}) collective-permute-start(bf16[64,2048]{1,0:T(8,128)(2,1)S(1)} %get-tuple-element.38.refs_3_), channel_id=1, source_target_pairs={{0,4},{4,0},{8,12},{12,8},{1,5},{5,1},{9,13},{13,9},{2,6},{6,2},{1... | collective-permute-start | bytes 786440 | tf_op jit(solution)/shard_map/ppermute | solution.py:357
  29.6 1.5 %collective-permute-start.6 = (bf16[128,1536]{1,0:T(8,128)(2,1)S(1)}, bf16[128,1536]{1,0:T(8,128)(2,1)S(1)}, u32[]{:S(2)}, u32[]{:S(2)}) collective-permute-start(bf16[128,1536]{1,0:T(8,128)(2,1)S(1)} %get-tuple-element.31.refs_1_), channel_id=1, source_target_pairs={{0,2},{2,0},{1,3},{3,1},{4,6},{6,4},{5,7},{7,5},{8,10},{10,8},{9,1... | collective-permute-start | bytes 1179656 | tf_op jit(solution)/shard_map/ppermute | solution.py:381
  31.1 0.5 collective-permute-start.10
  31.6 5.2 %shard_map.63.refs_2_ = f32[128,4096]{1,0:T(8,128)S(1)} custom-call(bf16[128,1536]{1,0:T(8,128)(2,1)S(1)} %collective-permute-done.3.refs_4_.refs_0_, bf16[6656,4096]{1,0:T(8,128)(2,1)} %refs_1_.5, f32[128,4096]{1,0:T(8,128)S(1)} %get-tuple-element.39.refs_2_, bf16[64,2048]{1,0:T(8,128)(2,1)S(1)} %get-tuple-element.38.refs_3_), custom_call_target="tpu_custom_call" | custom-call | flops 1 | bytes 1 | tf_op jit(solution)/shard_map/pallas_call | solution.py:136
  36.9 2.7 %collective-permute-start.5 = (bf16[32,2048]{1,0:T(8,128)(2,1)S(1)}, bf16[32,2048]{1,0:T(8,128)(2,1)S(1)}, u32[]{:S(2)}, u32[]{:S(2)}) collective-permute-start(bf16[32,2048]{1,0:T(8,128)(2,1)S(1)} %get-tuple-element.41.refs_3_), channel_id=1, source_target_pairs={{0,8},{4,12},{8,0},{12,4},{1,9},{5,13},{9,1},{13,5},{2,10},{6,14},... | collective-permute-start | bytes 393224 | tf_op jit(solution)/shard_map/ppermute | solution.py:357
  39.6 2.0 %collective-permute-done.6.refs_0_ = bf16[128,1536]{1,0:T(8,128)(2,1)S(1)} collective-permute-done((bf16[128,1536]{1,0:T(8,128)(2,1)S(1)}, bf16[128,1536]{1,0:T(8,128)(2,1)S(1)}, u32[]{:S(2)}, u32[]{:S(2)}) %collective-permute-start.6) | collective-permute-done | bytes 393248 | tf_op jit(solution)/shard_map/ppermute | solution.py:381
  41.6 5.2 %shard_map.65.refs_0_.refs_2_ = f32[128,4096]{1,0:T(8,128)S(1)} custom-call(bf16[128,1536]{1,0:T(8,128)(2,1)S(1)} %collective-permute-done.6.refs_0_, bf16[6656,4096]{1,0:T(8,128)(2,1)} %refs_1_.5, f32[128,4096]{1,0:T(8,128)S(1)} %shard_map.63.refs_2_, bf16[32,2048]{1,0:T(8,128)(2,1)S(1)} %get-tuple-element.41.refs_3_), custom_call_target="tpu_custom_call" | custom-call | flops 1 | bytes 1 | tf_op jit(solution)/shard_map/pallas_call | solution.py:136
  46.8 1.0 %shard_map.66.refs_3_.refs_0_ = bf16[32,2176]{1,0:T(8,128)(2,1)S(1)} custom-call(f32[32,2048]{1,0:T(8,128)S(1)} %get-tuple-element.40.kept_ref, bf16[32,2048]{1,0:T(8,128)(2,1)S(1)} %collective-permute-done.5.came_ref, f32[1,4096]{1,0:T(1,128)S(1)} %bitcast.2, f32[128,128]{1,0:T(8,128)S(1)} %copy-done.1, f32[128,4096]{1,0:T(8,128)S(1)} %shard_map.65.refs_0_.refs_2_), custom_call_target="tpu_custom_call" | custom-call | flops 1 | bytes 1 | tf_op jit(solution)/shard_map/pallas_call | solution.py:224
  47.8 0.1 collective-permute-start.7
  47.9 3.0 %collective-permute-start.8 = (bf16[32,2176]{1,0:T(8,128)(2,1)S(1)}, bf16[32,2176]{1,0:T(8,128)(2,1)S(1)}, u32[]{:S(2)}, u32[]{:S(2)}) collective-permute-start(bf16[32,2176]{1,0:T(8,128)(2,1)S(1)} %shard_map.66.refs_3_.refs_0_), channel_id=1, source_target_pairs={{0,8},{4,12},{8,0},{12,4},{1,9},{5,13},{9,1},{13,5},{2,10},{6,14},... | collective-permute-start | bytes 417800 | tf_op jit(solution)/shard_map/ppermute | solution.py:357
  50.9 5.2 %shard_map.67 = (bf16[128,1024]{1,0:T(8,128)(2,1)S(1)}, f32[128,1024]{1,0:T(8,128)S(1)}, bf16[128,1024]{1,0:T(8,128)(2,1)S(1)}, f32[128,1024]{1,0:T(8,128)S(1)}) custom-call(bf16[128,1536]{1,0:T(8,128)(2,1)S(1)} %collective-permute-done.10.refs_0_, bf16[6656,4096]{1,0:T(8,128)(2,1)} %refs_1_.5, f32[128,4096]{1,0:T(8,128)S(1)} %shard_map.65.refs_0_.refs_2_, ...), custom_call_target="tpu_custom_call" | custom-call | flops 1 | bytes 1 | tf_op jit(solution)/shard_map/pallas_call | solution.py:136
  56.1 0.1 collective-permute-start.11
  56.2 0.5 collective-permute-start.13
  56.7 1.6 %collective-permute-start.9 = (bf16[32,2176]{1,0:T(8,128)(2,1)S(1)}, bf16[32,2176]{1,0:T(8,128)(2,1)S(1)}, u32[]{:S(2)}, u32[]{:S(2)}) collective-permute-start(bf16[32,2176]{1,0:T(8,128)(2,1)S(1)} %collective-permute-done.8.refs_2_.refs_4_), channel_id=1, source_target_pairs={{0,4},{4,0},{8,12},{12,8},{1,5},{5,1},{9,13},{13,9},{2,6},{6,2},{1... | collective-permute-start | bytes 417800 | tf_op jit(solution)/shard_map/ppermute | solution.py:357
  58.4 1.1 %collective-permute-start.12 = (bf16[64,1024]{1,0:T(8,128)(2,1)S(1)}, bf16[64,1024]{1,0:T(8,128)(2,1)S(1)}, u32[]{:S(2)}, u32[]{:S(2)}) collective-permute-start(bf16[64,1024]{1,0:T(8,128)(2,1)S(1)} %get-tuple-element.45), channel_id=1, source_target_pairs={{0,4},{4,0},{8,12},{12,8},{1,5},{5,1},{9,13},{13,9},{2,6},{6,2},{1... | collective-permute-start | bytes 393224 | tf_op jit(solution)/shard_map/ppermute | solution.py:357
  59.5 1.1 %collective-permute-start.15 = (bf16[64,1024]{1,0:T(8,128)(2,1)S(1)}, bf16[64,1024]{1,0:T(8,128)(2,1)S(1)}, u32[]{:S(2)}, u32[]{:S(2)}) collective-permute-start(bf16[64,1024]{1,0:T(8,128)(2,1)S(1)} %get-tuple-element.48.refs_2_), channel_id=1, source_target_pairs={{0,4},{4,0},{8,12},{12,8},{1,5},{5,1},{9,13},{13,9},{2,6},{6,2},{1... | collective-permute-start | bytes 393224 | tf_op jit(solution)/shard_map/ppermute | solution.py:357
  60.6 2.6 %collective-permute-done.9.refs_5_.refs_3_ = bf16[32,2176]{1,0:T(8,128)(2,1)S(1)} collective-permute-done((bf16[32,2176]{1,0:T(8,128)(2,1)S(1)}, bf16[32,2176]{1,0:T(8,128)(2,1)S(1)}, u32[]{:S(2)}, u32[]{:S(2)}) %collective-permute-start.9) | collective-permute-done | bytes 139296 | tf_op jit(solution)/shard_map/ppermute | solution.py:357
  63.2 2.8 %collective-permute-done.12.refs_1_ = bf16[64,1024]{1,0:T(8,128)(2,1)S(1)} collective-permute-done((bf16[64,1024]{1,0:T(8,128)(2,1)S(1)}, bf16[64,1024]{1,0:T(8,128)(2,1)S(1)}, u32[]{:S(2)}, u32[]{:S(2)}) %collective-permute-start.12) | collective-permute-done | bytes 131104 | tf_op jit(solution)/shard_map/ppermute | solution.py:357
  66.1 1.2 %collective-permute-start.14 = (bf16[32,1024]{1,0:T(8,128)(2,1)S(1)}, bf16[32,1024]{1,0:T(8,128)(2,1)S(1)}, u32[]{:S(2)}, u32[]{:S(2)}) collective-permute-start(bf16[32,1024]{1,0:T(8,128)(2,1)S(1)} %get-tuple-element.50), channel_id=1, source_target_pairs={{0,8},{4,12},{8,0},{12,4},{1,9},{5,13},{9,1},{13,5},{2,10},{6,14},... | collective-permute-start | bytes 196616 | tf_op jit(solution)/shard_map/ppermute | solution.py:357
  67.3 0.7 collective-permute-done.15.refs_1_
  68.0 3.3 %collective-permute-done.14.came_ref = bf16[32,1024]{1,0:T(8,128)(2,1)S(1)} collective-permute-done((bf16[32,1024]{1,0:T(8,128)(2,1)S(1)}, bf16[32,1024]{1,0:T(8,128)(2,1)S(1)}, u32[]{:S(2)}, u32[]{:S(2)}) %collective-permute-start.14) | collective-permute-done | bytes 65568 | tf_op jit(solution)/shard_map/ppermute | solution.py:357
  71.3 0.6 shard_map.73.refs_4_
  71.9 1.6 %collective-permute-start.16 = (bf16[32,1152]{1,0:T(8,128)(2,1)S(1)}, bf16[32,1152]{1,0:T(8,128)(2,1)S(1)}, u32[]{:S(2)}, u32[]{:S(2)}) collective-permute-start(bf16[32,1152]{1,0:T(8,128)(2,1)S(1)} %shard_map.73.refs_4_), channel_id=1, source_target_pairs={{0,4},{4,0},{8,12},{12,8},{1,5},{5,1},{9,13},{13,9},{2,6},{6,2},{1... | collective-permute-start | bytes 221192 | tf_op jit(solution)/shard_map/ppermute | solution.py:357
  73.6 1.9 %collective-permute-start.19 = (bf16[32,1024]{1,0:T(8,128)(2,1)S(1)}, bf16[32,1024]{1,0:T(8,128)(2,1)S(1)}, u32[]{:S(2)}, u32[]{:S(2)}) collective-permute-start(bf16[32,1024]{1,0:T(8,128)(2,1)S(1)} %get-tuple-element.52.refs_0_), channel_id=1, source_target_pairs={{0,8},{4,12},{8,0},{12,4},{1,9},{5,13},{9,1},{13,5},{2,10},{6,14},... | collective-permute-start | bytes 196616 | tf_op jit(solution)/shard_map/ppermute | solution.py:357
  75.5 1.0 %collective-permute-start.17 = (bf16[32,1152]{1,0:T(8,128)(2,1)S(1)}, bf16[32,1152]{1,0:T(8,128)(2,1)S(1)}, u32[]{:S(2)}, u32[]{:S(2)}) collective-permute-start(bf16[32,1152]{1,0:T(8,128)(2,1)S(1)} %shard_map.73.refs_4_), channel_id=1, source_target_pairs={{0,8},{4,12},{8,0},{12,4},{1,9},{5,13},{9,1},{13,5},{2,10},{6,14},... | collective-permute-start | bytes 221192 | tf_op jit(solution)/shard_map/ppermute | solution.py:357
  76.5 5.6 %collective-permute-done.19.came_ref = bf16[32,1024]{1,0:T(8,128)(2,1)S(1)} collective-permute-done((bf16[32,1024]{1,0:T(8,128)(2,1)S(1)}, bf16[32,1024]{1,0:T(8,128)(2,1)S(1)}, u32[]{:S(2)}, u32[]{:S(2)}) %collective-permute-start.19) | collective-permute-done | bytes 65568 | tf_op jit(solution)/shard_map/ppermute | solution.py:357
  82.1 0.6 shard_map.75.refs_4_
  82.8 0.9 collective-permute-done.17.refs_6_
  83.7 0.9 collective-permute-start.18
  84.6 1.1 %collective-permute-start.20 = (bf16[32,1152]{1,0:T(8,128)(2,1)S(1)}, bf16[32,1152]{1,0:T(8,128)(2,1)S(1)}, u32[]{:S(2)}, u32[]{:S(2)}) collective-permute-start(bf16[32,1152]{1,0:T(8,128)(2,1)S(1)} %shard_map.75.refs_4_), channel_id=1, source_target_pairs={{0,4},{4,0},{8,12},{12,8},{1,5},{5,1},{9,13},{13,9},{2,6},{6,2},{1... | collective-permute-start | bytes 221192 | tf_op jit(solution)/shard_map/ppermute | solution.py:357
  85.7 2.4 %collective-permute-done.21.refs_6_ = bf16[32,1152]{1,0:T(8,128)(2,1)S(1)} collective-permute-done((bf16[32,1152]{1,0:T(8,128)(2,1)S(1)}, bf16[32,1152]{1,0:T(8,128)(2,1)S(1)}, u32[]{:S(2)}, u32[]{:S(2)}) %collective-permute-start.21) | collective-permute-done | bytes 73760 | tf_op jit(solution)/shard_map/ppermute | solution.py:357
  88.2 0.8 collective-permute-done.18.refs_7_
  89.0 0.7 collective-permute-done.20.refs_5_
  89.7 2.8 %collective-permute-done.22.refs_7_ = bf16[32,1152]{1,0:T(8,128)(2,1)S(1)} collective-permute-done((bf16[32,1152]{1,0:T(8,128)(2,1)S(1)}, bf16[32,1152]{1,0:T(8,128)(2,1)S(1)}, u32[]{:S(2)}, u32[]{:S(2)}) %collective-permute-start.22) | collective-permute-done | bytes 73760 | tf_op jit(solution)/shard_map/ppermute | solution.py:357
  92.7 0.1 shard_map.76.refs_1_
  92.8 1.4 %collective-permute-done.24.refs_3_ = bf16[128,1152]{1,0:T(8,128)(2,1)S(1)} collective-permute-done((bf16[128,1152]{1,0:T(8,128)(2,1)S(1)}, bf16[128,1152]{1,0:T(8,128)(2,1)S(1)}, u32[]{:S(2)}, u32[]{:S(2)}) %collective-permute-start.24) | collective-permute-done | bytes 294944 | tf_op jit(solution)/shard_map/ppermute | solution.py:354
  94.2 1.1 %shard_map.79 = (bf16[128,4096]{1,0:T(8,128)(2,1)}, bf16[32,128]{1,0:T(8,128)(2,1)}) custom-call(bf16[128,1152]{1,0:T(8,128)(2,1)S(1)} %shard_map.74.refs_0_, bf16[128,1152]{1,0:T(8,128)(2,1)S(1)} %shard_map.76.refs_1_, bf16[128,1152]{1,0:T(8,128)(2,1)S(1)} %collective-permute-done.23.refs_2_, bf16[128,1152]{1,0:T(8,128)(2,1)S(1)} %collective-permute-done.24.refs_3_), custom_call_target="tpu_custom_call" | custom-call | flops 1 | bytes 1 | tf_op jit(solution)/shard_map/pallas_call | solution.py:319
  (30 shorter events, 0.6 us)
Async XLA Ops:
  0.6 1.5 %copy-start = (bf16[128,6656]{1,0:T(8,128)(2,1)S(1)}, bf16[128,6656]{1,0:T(8,128)(2,1)}, u32[]{:S(2)}) copy-start(bf16[128,6656]{1,0:T(8,128)(2,1)} %in_ref.1) | copy-start | bytes 5111812
  2.3 15.8 %collective-permute-start = (bf16[128,2048]{1,0:T(8,128)(2,1)S(1)}, bf16[128,2048]{1,0:T(8,128)(2,1)S(1)}, u32[]{:S(2)}, u32[]{:S(2)}) collective-permute-start(bf16[128,2048]{1,0:T(8,128)(2,1)S(1)} %get-tuple-element.29.refs_4_.refs_0_), channel_id=1, source_target_pairs={{0,2},{2,0},{1,3},{3,1},{4,6},{6,4},{5,7},{7,5},{8,10},{10,8},{9,1... | collective-permute-start | bytes 1572872 | tf_op jit(solution)/shard_map/ppermute | solution.py:381
  5.3 20.7 %collective-permute-start.3 = (bf16[128,1536]{1,0:T(8,128)(2,1)S(1)}, bf16[128,1536]{1,0:T(8,128)(2,1)S(1)}, u32[]{:S(2)}, u32[]{:S(2)}) collective-permute-start(bf16[128,1536]{1,0:T(8,128)(2,1)S(1)} %get-tuple-element.30.refs_0_), channel_id=1, source_target_pairs={{0,2},{2,0},{1,3},{3,1},{4,6},{6,4},{5,7},{7,5},{8,10},{10,8},{9,1... | collective-permute-start | bytes 1179656 | tf_op jit(solution)/shard_map/ppermute | solution.py:381
  25.4 1.6 %collective-permute-start.1 = (bf16[128,1024]{1,0:T(8,128)(2,1)S(1)}, bf16[128,1024]{1,0:T(8,128)(2,1)S(1)}, u32[]{:S(2)}, u32[]{:S(2)}) collective-permute-start(bf16[128,1024]{1,0:T(8,128)(2,1)S(1)} %get-tuple-element.35), channel_id=1, source_target_pairs={{0,1},{1,0},{2,3},{3,2},{4,5},{5,4},{6,7},{7,6},{8,9},{9,8},{10,11... | collective-permute-start | bytes 786440 | tf_op jit(solution)/shard_map/ppermute | solution.py:354
  25.5 1.9 %collective-permute-start.2 = (bf16[128,1024]{1,0:T(8,128)(2,1)S(1)}, bf16[128,1024]{1,0:T(8,128)(2,1)S(1)}, u32[]{:S(2)}, u32[]{:S(2)}) collective-permute-start(bf16[128,1024]{1,0:T(8,128)(2,1)S(1)} %get-tuple-element.36), channel_id=1, source_target_pairs={{0,1},{1,0},{2,3},{3,2},{4,5},{5,4},{6,7},{7,6},{8,9},{9,8},{10,11... | collective-permute-start | bytes 786440 | tf_op jit(solution)/shard_map/ppermute | solution.py:354
  27.4 9.4 %collective-permute-start.4 = (bf16[64,2048]{1,0:T(8,128)(2,1)S(1)}, bf16[64,2048]{1,0:T(8,128)(2,1)S(1)}, u32[]{:S(2)}, u32[]{:S(2)}) collective-permute-start(bf16[64,2048]{1,0:T(8,128)(2,1)S(1)} %get-tuple-element.38.refs_3_), channel_id=1, source_target_pairs={{0,4},{4,0},{8,12},{12,8},{1,5},{5,1},{9,13},{13,9},{2,6},{6,2},{1... | collective-permute-start | bytes 786440 | tf_op jit(solution)/shard_map/ppermute | solution.py:357
  29.6 12.0 %collective-permute-start.6 = (bf16[128,1536]{1,0:T(8,128)(2,1)S(1)}, bf16[128,1536]{1,0:T(8,128)(2,1)S(1)}, u32[]{:S(2)}, u32[]{:S(2)}) collective-permute-start(bf16[128,1536]{1,0:T(8,128)(2,1)S(1)} %get-tuple-element.31.refs_1_), channel_id=1, source_target_pairs={{0,2},{2,0},{1,3},{3,1},{4,6},{6,4},{5,7},{7,5},{8,10},{10,8},{9,1... | collective-permute-start | bytes 1179656 | tf_op jit(solution)/shard_map/ppermute | solution.py:381
  31.1 19.8 %collective-permute-start.10 = (bf16[128,1536]{1,0:T(8,128)(2,1)S(1)}, bf16[128,1536]{1,0:T(8,128)(2,1)S(1)}, u32[]{:S(2)}, u32[]{:S(2)}) collective-permute-start(bf16[128,1536]{1,0:T(8,128)(2,1)S(1)} %get-tuple-element.32.refs_2_), channel_id=1, source_target_pairs={{0,2},{2,0},{1,3},{3,1},{4,6},{6,4},{5,7},{7,5},{8,10},{10,8},{9,1... | collective-permute-start | bytes 1179656 | tf_op jit(solution)/shard_map/ppermute | solution.py:381
  36.8 2.8 %copy-start.2 = (s32[4096]{0:T(1024)S(1)}, s32[4096]{0:T(1024)}, u32[]{:S(2)}) copy-start(s32[4096]{0:T(1024)} %param.6) | copy-start | bytes 49156
  36.9 9.9 %collective-permute-start.5 = (bf16[32,2048]{1,0:T(8,128)(2,1)S(1)}, bf16[32,2048]{1,0:T(8,128)(2,1)S(1)}, u32[]{:S(2)}, u32[]{:S(2)}) collective-permute-start(bf16[32,2048]{1,0:T(8,128)(2,1)S(1)} %get-tuple-element.41.refs_3_), channel_id=1, source_target_pairs={{0,8},{4,12},{8,0},{12,4},{1,9},{5,13},{9,1},{13,5},{2,10},{6,14},... | collective-permute-start | bytes 393224 | tf_op jit(solution)/shard_map/ppermute | solution.py:357
  39.6 7.2 %copy-start.1 = (f32[128,128]{1,0:T(8,128)S(1)}, f32[128,128]{1,0:T(8,128)}, u32[]{:S(2)}) copy-start(f32[128,128]{1,0:T(8,128)} %constant.7.clone.rotation_ref) | copy-start | bytes 196612
  47.8 8.4 %collective-permute-start.7 = (bf16[32,2176]{1,0:T(8,128)(2,1)S(1)}, bf16[32,2176]{1,0:T(8,128)(2,1)S(1)}, u32[]{:S(2)}, u32[]{:S(2)}) collective-permute-start(bf16[32,2176]{1,0:T(8,128)(2,1)S(1)} %shard_map.66.refs_3_.refs_0_), channel_id=1, source_target_pairs={{0,4},{4,0},{8,12},{12,8},{1,5},{5,1},{9,13},{13,9},{2,6},{6,2},{1... | collective-permute-start | bytes 417800 | tf_op jit(solution)/shard_map/ppermute | solution.py:357
  47.9 8.3 %collective-permute-start.8 = (bf16[32,2176]{1,0:T(8,128)(2,1)S(1)}, bf16[32,2176]{1,0:T(8,128)(2,1)S(1)}, u32[]{:S(2)}, u32[]{:S(2)}) collective-permute-start(bf16[32,2176]{1,0:T(8,128)(2,1)S(1)} %shard_map.66.refs_3_.refs_0_), channel_id=1, source_target_pairs={{0,8},{4,12},{8,0},{12,4},{1,9},{5,13},{9,1},{13,5},{2,10},{6,14},... | collective-permute-start | bytes 417800 | tf_op jit(solution)/shard_map/ppermute | solution.py:357
  56.1 2.2 %collective-permute-start.11 = (bf16[128,1024]{1,0:T(8,128)(2,1)S(1)}, bf16[128,1024]{1,0:T(8,128)(2,1)S(1)}, u32[]{:S(2)}, u32[]{:S(2)}) collective-permute-start(bf16[128,1024]{1,0:T(8,128)(2,1)S(1)} %get-tuple-element.43), channel_id=1, source_target_pairs={{0,1},{1,0},{2,3},{3,2},{4,5},{5,4},{6,7},{7,6},{8,9},{9,8},{10,11... | collective-permute-start | bytes 786440 | tf_op jit(solution)/shard_map/ppermute | solution.py:354
  56.2 3.2 %collective-permute-start.13 = (bf16[128,1024]{1,0:T(8,128)(2,1)S(1)}, bf16[128,1024]{1,0:T(8,128)(2,1)S(1)}, u32[]{:S(2)}, u32[]{:S(2)}) collective-permute-start(bf16[128,1024]{1,0:T(8,128)(2,1)S(1)} %shard_map.69), channel_id=1, source_target_pairs={{0,1},{1,0},{2,3},{3,2},{4,5},{5,4},{6,7},{7,6},{8,9},{9,8},{10,11... | collective-permute-start | bytes 786440 | tf_op jit(solution)/shard_map/ppermute | solution.py:354
  56.7 6.5 %collective-permute-start.9 = (bf16[32,2176]{1,0:T(8,128)(2,1)S(1)}, bf16[32,2176]{1,0:T(8,128)(2,1)S(1)}, u32[]{:S(2)}, u32[]{:S(2)}) collective-permute-start(bf16[32,2176]{1,0:T(8,128)(2,1)S(1)} %collective-permute-done.8.refs_2_.refs_4_), channel_id=1, source_target_pairs={{0,4},{4,0},{8,12},{12,8},{1,5},{5,1},{9,13},{13,9},{2,6},{6,2},{1... | collective-permute-start | bytes 417800 | tf_op jit(solution)/shard_map/ppermute | solution.py:357
  58.4 7.7 %collective-permute-start.12 = (bf16[64,1024]{1,0:T(8,128)(2,1)S(1)}, bf16[64,1024]{1,0:T(8,128)(2,1)S(1)}, u32[]{:S(2)}, u32[]{:S(2)}) collective-permute-start(bf16[64,1024]{1,0:T(8,128)(2,1)S(1)} %get-tuple-element.45), channel_id=1, source_target_pairs={{0,4},{4,0},{8,12},{12,8},{1,5},{5,1},{9,13},{13,9},{2,6},{6,2},{1... | collective-permute-start | bytes 393224 | tf_op jit(solution)/shard_map/ppermute | solution.py:357
  59.5 8.5 %collective-permute-start.15 = (bf16[64,1024]{1,0:T(8,128)(2,1)S(1)}, bf16[64,1024]{1,0:T(8,128)(2,1)S(1)}, u32[]{:S(2)}, u32[]{:S(2)}) collective-permute-start(bf16[64,1024]{1,0:T(8,128)(2,1)S(1)} %get-tuple-element.48.refs_2_), channel_id=1, source_target_pairs={{0,4},{4,0},{8,12},{12,8},{1,5},{5,1},{9,13},{13,9},{2,6},{6,2},{1... | collective-permute-start | bytes 393224 | tf_op jit(solution)/shard_map/ppermute | solution.py:357
  66.1 5.2 %collective-permute-start.14 = (bf16[32,1024]{1,0:T(8,128)(2,1)S(1)}, bf16[32,1024]{1,0:T(8,128)(2,1)S(1)}, u32[]{:S(2)}, u32[]{:S(2)}) collective-permute-start(bf16[32,1024]{1,0:T(8,128)(2,1)S(1)} %get-tuple-element.50), channel_id=1, source_target_pairs={{0,8},{4,12},{8,0},{12,4},{1,9},{5,13},{9,1},{13,5},{2,10},{6,14},... | collective-permute-start | bytes 196616 | tf_op jit(solution)/shard_map/ppermute | solution.py:357
  71.9 10.2 %collective-permute-start.16 = (bf16[32,1152]{1,0:T(8,128)(2,1)S(1)}, bf16[32,1152]{1,0:T(8,128)(2,1)S(1)}, u32[]{:S(2)}, u32[]{:S(2)}) collective-permute-start(bf16[32,1152]{1,0:T(8,128)(2,1)S(1)} %shard_map.73.refs_4_), channel_id=1, source_target_pairs={{0,4},{4,0},{8,12},{12,8},{1,5},{5,1},{9,13},{13,9},{2,6},{6,2},{1... | collective-permute-start | bytes 221192 | tf_op jit(solution)/shard_map/ppermute | solution.py:357
  73.6 8.6 %collective-permute-start.19 = (bf16[32,1024]{1,0:T(8,128)(2,1)S(1)}, bf16[32,1024]{1,0:T(8,128)(2,1)S(1)}, u32[]{:S(2)}, u32[]{:S(2)}) collective-permute-start(bf16[32,1024]{1,0:T(8,128)(2,1)S(1)} %get-tuple-element.52.refs_0_), channel_id=1, source_target_pairs={{0,8},{4,12},{8,0},{12,4},{1,9},{5,13},{9,1},{13,5},{2,10},{6,14},... | collective-permute-start | bytes 196616 | tf_op jit(solution)/shard_map/ppermute | solution.py:357
  75.5 8.2 %collective-permute-start.17 = (bf16[32,1152]{1,0:T(8,128)(2,1)S(1)}, bf16[32,1152]{1,0:T(8,128)(2,1)S(1)}, u32[]{:S(2)}, u32[]{:S(2)}) collective-permute-start(bf16[32,1152]{1,0:T(8,128)(2,1)S(1)} %shard_map.73.refs_4_), channel_id=1, source_target_pairs={{0,8},{4,12},{8,0},{12,4},{1,9},{5,13},{9,1},{13,5},{2,10},{6,14},... | collective-permute-start | bytes 221192 | tf_op jit(solution)/shard_map/ppermute | solution.py:357
  82.7 5.4 %collective-permute-start.21 = (bf16[32,1152]{1,0:T(8,128)(2,1)S(1)}, bf16[32,1152]{1,0:T(8,128)(2,1)S(1)}, u32[]{:S(2)}, u32[]{:S(2)}) collective-permute-start(bf16[32,1152]{1,0:T(8,128)(2,1)S(1)} %shard_map.75.refs_4_), channel_id=1, source_target_pairs={{0,8},{4,12},{8,0},{12,4},{1,9},{5,13},{9,1},{13,5},{2,10},{6,14},... | collective-permute-start | bytes 221192 | tf_op jit(solution)/shard_map/ppermute | solution.py:357
  83.7 5.2 %collective-permute-start.18 = (bf16[32,1152]{1,0:T(8,128)(2,1)S(1)}, bf16[32,1152]{1,0:T(8,128)(2,1)S(1)}, u32[]{:S(2)}, u32[]{:S(2)}) collective-permute-start(bf16[32,1152]{1,0:T(8,128)(2,1)S(1)} %collective-permute-done.17.refs_6_), channel_id=1, source_target_pairs={{0,4},{4,0},{8,12},{12,8},{1,5},{5,1},{9,13},{13,9},{2,6},{6,2},{1... | collective-permute-start | bytes 221192 | tf_op jit(solution)/shard_map/ppermute | solution.py:357
  84.6 5.1 %collective-permute-start.20 = (bf16[32,1152]{1,0:T(8,128)(2,1)S(1)}, bf16[32,1152]{1,0:T(8,128)(2,1)S(1)}, u32[]{:S(2)}, u32[]{:S(2)}) collective-permute-start(bf16[32,1152]{1,0:T(8,128)(2,1)S(1)} %shard_map.75.refs_4_), channel_id=1, source_target_pairs={{0,4},{4,0},{8,12},{12,8},{1,5},{5,1},{9,13},{13,9},{2,6},{6,2},{1... | collective-permute-start | bytes 221192 | tf_op jit(solution)/shard_map/ppermute | solution.py:357
  88.2 4.4 %collective-permute-start.22 = (bf16[32,1152]{1,0:T(8,128)(2,1)S(1)}, bf16[32,1152]{1,0:T(8,128)(2,1)S(1)}, u32[]{:S(2)}, u32[]{:S(2)}) collective-permute-start(bf16[32,1152]{1,0:T(8,128)(2,1)S(1)} %collective-permute-done.21.refs_6_), channel_id=1, source_target_pairs={{0,4},{4,0},{8,12},{12,8},{1,5},{5,1},{9,13},{13,9},{2,6},{6,2},{1... | collective-permute-start | bytes 221192 | tf_op jit(solution)/shard_map/ppermute | solution.py:357
  89.0 3.8 %collective-permute-start.23 = (bf16[128,1152]{1,0:T(8,128)(2,1)S(1)}, bf16[128,1152]{1,0:T(8,128)(2,1)S(1)}, u32[]{:S(2)}, u32[]{:S(2)}) collective-permute-start(bf16[128,1152]{1,0:T(8,128)(2,1)S(1)} %shard_map.77), channel_id=1, source_target_pairs={{0,1},{1,0},{2,3},{3,2},{4,5},{5,4},{6,7},{7,6},{8,9},{9,8},{10,11... | collective-permute-start | bytes 884744 | tf_op jit(solution)/shard_map/ppermute | solution.py:354
  92.6 1.6 %collective-permute-start.24 = (bf16[128,1152]{1,0:T(8,128)(2,1)S(1)}, bf16[128,1152]{1,0:T(8,128)(2,1)S(1)}, u32[]{:S(2)}, u32[]{:S(2)}) collective-permute-start(bf16[128,1152]{1,0:T(8,128)(2,1)S(1)} %shard_map.78), channel_id=1, source_target_pairs={{0,1},{1,0},{2,3},{3,2},{4,5},{5,4},{6,7},{7,6},{8,9},{9,8},{10,11... | collective-permute-start | bytes 884744 | tf_op jit(solution)/shard_map/ppermute | solution.py:354

commit v9 on v8

--- a/solution.py
+++ b/solution.py
@@ -13,7 +13,7 @@
 UNIT = 512
 GROUPS = 2
 VMEM_LIMIT = 6 * 2**20
-SHARES = (4, 3, 3)
+SHARES = (4, 4, 3)
 epsilon = 1e-06
 
 SMALL = pl.CostEstimate(flops=1, bytes_accessed=1, transcendentals=0)
@@ -426,8 +426,6 @@
                     wait = list(last) if group == 0 else []
                     if group == 0 and level == 1 and shift == 0:
                         wait += results[0][0][1:]
-                    if remote:
-                        wait.append(remote[-1][1])
                     step = steps.send(wait)
                     if level == levels:
                         remote.append(spread(step))

time: 95.5 us -> 90.1 us (0.943)
  waiting for transfers between devices: 27.5 us -> 16 us
  starting transfers between devices: 25.9 us -> 31.9 us
    ppermute x15, waiting for transfers between devices: 22.6 us -> 11.4 us  [exchange(): lax.ppermute(values, 'tensor', [(t, t ^ 1 << level) for t in range(tensor...]
    ppermute x15, starting transfers between devices: 19.5 us -> 25.5 us  [exchange(): lax.ppermute(values, 'tensor', [(t, t ^ 1 << level) for t in range(tensor...]
    ppermute x6, waiting for transfers between devices: 2.8 us -> 1.41 us  [swap(): return lax.ppermute(values, 'sub', [(0, 1), (1, 0)])]
    ppermute x4, waiting for transfers between devices: 2.04 us -> 3.22 us  [shards(): arrivals.append([lax.ppermute(part, 'seq', pairs) for part in parts])]
  transfers between devices with their start and end apart: 25 -> 25, of which waited for: 14 -> 11; matrix products, arithmetic and copies ran while one was open for 0% -> 0% of each run, Pallas kernels for 39% -> 43%
where the time goes in v9:
time: 90.1 us; the launch traced here: 89.9 us
  Pallas kernels  39.6 us (44%)
  starting transfers between devices  31.9 us (35%)
  waiting for transfers between devices  16 us (18%)
  local copies, waits for them, and re-layouts  1.46 us (2%)
    pallas_call x5, Pallas kernels, multiply(): pl.pallas_call(body, out_shape=out_shape, in_specs=[VMEM] * spans[-1][1]...  35.5 us
    ppermute x15, starting transfers between devices, exchange(): lax.ppermute(values, 'tensor', [(t, t ^ 1 << level) for t in range(tensor...  25.5 us
    ppermute x15, waiting for transfers between devices, exchange(): lax.ppermute(values, 'tensor', [(t, t ^ 1 << level) for t in range(tensor...  11.4 us
    ppermute x4, starting transfers between devices, shards(): arrivals.append([lax.ppermute(part, 'seq', pairs) for part in parts])  5.11 us
    ppermute x4, waiting for transfers between devices, shards(): arrivals.append([lax.ppermute(part, 'seq', pairs) for part in parts])  3.22 us
    pallas_call x3, Pallas kernels, encode(): pl.pallas_call(functools.partial(encode_body, begin), out_shape=jax.Shape...  2.24 us
  transfers between devices with their start and end apart: 25, of which 11 were waited for; matrix products, arithmetic and copies ran while one was open for 0% of the time, Pallas kernels for 43%

profile of v9, /device:TPU:0, one launch (start us, length us, event | category | flops | bytes accessed | tf_op | source)
XLA Modules:
  0.0 89.9 jit_solution(3533004147062060645)
XLA Ops:
  0.6 1.4 %copy-done = bf16[128,6656]{1,0:T(8,128)(2,1)S(1)} copy-done((bf16[128,6656]{1,0:T(8,128)(2,1)S(1)}, bf16[128,6656]{1,0:T(8,128)(2,1)}, u32[]{:S(2)}) %copy-start) | copy-done | bytes 1703960
  2.1 0.2 shard_map.59
  2.2 3.0 %collective-permute-start = (bf16[128,2048]{1,0:T(8,128)(2,1)S(1)}, bf16[128,2048]{1,0:T(8,128)(2,1)S(1)}, u32[]{:S(2)}, u32[]{:S(2)}) collective-permute-start(bf16[128,2048]{1,0:T(8,128)(2,1)S(1)} %get-tuple-element.29.refs_4_.refs_0_), channel_id=1, source_target_pairs={{0,2},{2,0},{1,3},{3,1},{4,6},{6,4},{5,7},{7,5},{8,10},{10,8},{9,1... | collective-permute-start | bytes 1572872 | tf_op jit(solution)/shard_map/ppermute | solution.py:381
  5.3 0.1 collective-permute-start.3
  5.3 12.7 %shard_map.60.refs_3_ = f32[128,4096]{1,0:T(8,128)S(1)} custom-call(bf16[128,2048]{1,0:T(8,128)(2,1)S(1)} %get-tuple-element.30.refs_0_, bf16[128,1536]{1,0:T(8,128)(2,1)S(1)} %get-tuple-element.31.refs_1_, bf16[128,1024]{1,0:T(8,128)(2,1)S(1)} %get-tuple-element.32.refs_2_, bf16[6656,4096]{1,0:T(8,128)(2,1)} %refs_1_.5, ...), custom_call_target="tpu_custom_call" | custom-call | flops 1 | bytes 1 | tf_op jit(solution)/shard_map/pallas_call | solution.py:136
  18.0 7.3 %shard_map.61 = (bf16[128,1024]{1,0:T(8,128)(2,1)S(1)}, f32[128,1024]{1,0:T(8,128)S(1)}, bf16[128,1024]{1,0:T(8,128)(2,1)S(1)}, f32[128,1024]{1,0:T(8,128)S(1)}, f32[128,4096]{1,0:T(8,128)S(1)}) custom-call(bf16[128,2048]{1,0:T(8,128)(2,1)S(1)} %get-tuple-element.29.refs_4_.refs_0_, bf16[128,2048]{1,0:T(8,128)(2,1)S(1)} %collective-permute-done.refs_1_, ...), custom_call_target="tpu_custom_call" | custom-call | flops 1 | bytes 1 | tf_op jit(solution)/shard_map/pallas_call | solution.py:136
  25.4 0.1 collective-permute-start.1
  25.5 0.5 collective-permute-start.2
  26.0 2.5 %collective-permute-done.3.refs_4_.refs_0_ = bf16[128,2048]{1,0:T(8,128)(2,1)S(1)} collective-permute-done((bf16[128,2048]{1,0:T(8,128)(2,1)S(1)}, bf16[128,2048]{1,0:T(8,128)(2,1)S(1)}, u32[]{:S(2)}, u32[]{:S(2)}) %collective-permute-start.3) | collective-permute-done | bytes 524320 | tf_op jit(solution)/shard_map/ppermute | solution.py:381
  28.4 0.1 shard_map.62
  28.5 1.9 %collective-permute-start.4 = (bf16[64,2048]{1,0:T(8,128)(2,1)S(1)}, bf16[64,2048]{1,0:T(8,128)(2,1)S(1)}, u32[]{:S(2)}, u32[]{:S(2)}) collective-permute-start(bf16[64,2048]{1,0:T(8,128)(2,1)S(1)} %get-tuple-element.38.refs_3_), channel_id=1, source_target_pairs={{0,4},{4,0},{8,12},{12,8},{1,5},{5,1},{9,13},{13,9},{2,6},{6,2},{1... | collective-permute-start | bytes 786440 | tf_op jit(solution)/shard_map/ppermute | solution.py:357
  30.4 1.5 %collective-permute-start.6 = (bf16[128,1536]{1,0:T(8,128)(2,1)S(1)}, bf16[128,1536]{1,0:T(8,128)(2,1)S(1)}, u32[]{:S(2)}, u32[]{:S(2)}) collective-permute-start(bf16[128,1536]{1,0:T(8,128)(2,1)S(1)} %get-tuple-element.31.refs_1_), channel_id=1, source_target_pairs={{0,2},{2,0},{1,3},{3,1},{4,6},{6,4},{5,7},{7,5},{8,10},{10,8},{9,1... | collective-permute-start | bytes 1179656 | tf_op jit(solution)/shard_map/ppermute | solution.py:381
  31.9 0.5 collective-permute-start.10
  32.4 6.5 %shard_map.63.refs_2_ = f32[128,4096]{1,0:T(8,128)S(1)} custom-call(bf16[128,2048]{1,0:T(8,128)(2,1)S(1)} %collective-permute-done.3.refs_4_.refs_0_, bf16[6656,4096]{1,0:T(8,128)(2,1)} %refs_1_.5, f32[128,4096]{1,0:T(8,128)S(1)} %get-tuple-element.39.refs_2_, bf16[64,2048]{1,0:T(8,128)(2,1)S(1)} %get-tuple-element.38.refs_3_), custom_call_target="tpu_custom_call" | custom-call | flops 1 | bytes 1 | tf_op jit(solution)/shard_map/pallas_call | solution.py:136
  39.0 2.7 %collective-permute-start.5 = (bf16[32,2048]{1,0:T(8,128)(2,1)S(1)}, bf16[32,2048]{1,0:T(8,128)(2,1)S(1)}, u32[]{:S(2)}, u32[]{:S(2)}) collective-permute-start(bf16[32,2048]{1,0:T(8,128)(2,1)S(1)} %get-tuple-element.41.refs_3_), channel_id=1, source_target_pairs={{0,8},{4,12},{8,0},{12,4},{1,9},{5,13},{9,1},{13,5},{2,10},{6,14},... | collective-permute-start | bytes 393224 | tf_op jit(solution)/shard_map/ppermute | solution.py:357
  41.7 0.8 collective-permute-done.6.refs_0_
  42.5 5.2 %shard_map.65.refs_0_.refs_2_ = f32[128,4096]{1,0:T(8,128)S(1)} custom-call(bf16[128,1536]{1,0:T(8,128)(2,1)S(1)} %collective-permute-done.6.refs_0_, bf16[6656,4096]{1,0:T(8,128)(2,1)} %refs_1_.5, f32[128,4096]{1,0:T(8,128)S(1)} %shard_map.63.refs_2_, bf16[32,2048]{1,0:T(8,128)(2,1)S(1)} %get-tuple-element.41.refs_3_), custom_call_target="tpu_custom_call" | custom-call | flops 1 | bytes 1 | tf_op jit(solution)/shard_map/pallas_call | solution.py:136
  47.6 1.0 %shard_map.66.refs_3_.refs_0_ = bf16[32,2176]{1,0:T(8,128)(2,1)S(1)} custom-call(f32[32,2048]{1,0:T(8,128)S(1)} %get-tuple-element.40.kept_ref, bf16[32,2048]{1,0:T(8,128)(2,1)S(1)} %collective-permute-done.5.came_ref, f32[1,4096]{1,0:T(1,128)S(1)} %bitcast.2, f32[128,128]{1,0:T(8,128)S(1)} %copy-done.1, f32[128,4096]{1,0:T(8,128)S(1)} %shard_map.65.refs_0_.refs_2_), custom_call_target="tpu_custom_call" | custom-call | flops 1 | bytes 1 | tf_op jit(solution)/shard_map/pallas_call | solution.py:224
  48.7 0.3 collective-permute-start.7
  48.9 2.8 %collective-permute-start.8 = (bf16[32,2176]{1,0:T(8,128)(2,1)S(1)}, bf16[32,2176]{1,0:T(8,128)(2,1)S(1)}, u32[]{:S(2)}, u32[]{:S(2)}) collective-permute-start(bf16[32,2176]{1,0:T(8,128)(2,1)S(1)} %shard_map.66.refs_3_.refs_0_), channel_id=1, source_target_pairs={{0,8},{4,12},{8,0},{12,4},{1,9},{5,13},{9,1},{13,5},{2,10},{6,14},... | collective-permute-start | bytes 417800 | tf_op jit(solution)/shard_map/ppermute | solution.py:357
  51.8 3.9 %shard_map.67 = (bf16[128,1024]{1,0:T(8,128)(2,1)S(1)}, f32[128,1024]{1,0:T(8,128)S(1)}, bf16[128,1024]{1,0:T(8,128)(2,1)S(1)}, f32[128,1024]{1,0:T(8,128)S(1)}) custom-call(bf16[128,1024]{1,0:T(8,128)(2,1)S(1)} %collective-permute-done.10.refs_0_, bf16[6656,4096]{1,0:T(8,128)(2,1)} %refs_1_.5, f32[128,4096]{1,0:T(8,128)S(1)} %shard_map.65.refs_0_.refs_2_, ...), custom_call_target="tpu_custom_call" | custom-call | flops 1 | bytes 1 | tf_op jit(solution)/shard_map/pallas_call | solution.py:136
  55.6 0.1 collective-permute-start.11
  55.8 0.5 collective-permute-start.13
  56.2 1.6 %collective-permute-start.9 = (bf16[32,2176]{1,0:T(8,128)(2,1)S(1)}, bf16[32,2176]{1,0:T(8,128)(2,1)S(1)}, u32[]{:S(2)}, u32[]{:S(2)}) collective-permute-start(bf16[32,2176]{1,0:T(8,128)(2,1)S(1)} %collective-permute-done.8.refs_2_.refs_4_), channel_id=1, source_target_pairs={{0,4},{4,0},{8,12},{12,8},{1,5},{5,1},{9,13},{13,9},{2,6},{6,2},{1... | collective-permute-start | bytes 417800 | tf_op jit(solution)/shard_map/ppermute | solution.py:357
  58.0 1.0 %collective-permute-start.12 = (bf16[64,1024]{1,0:T(8,128)(2,1)S(1)}, bf16[64,1024]{1,0:T(8,128)(2,1)S(1)}, u32[]{:S(2)}, u32[]{:S(2)}) collective-permute-start(bf16[64,1024]{1,0:T(8,128)(2,1)S(1)} %get-tuple-element.45), channel_id=1, source_target_pairs={{0,4},{4,0},{8,12},{12,8},{1,5},{5,1},{9,13},{13,9},{2,6},{6,2},{1... | collective-permute-start | bytes 393224 | tf_op jit(solution)/shard_map/ppermute | solution.py:357
  59.0 1.1 %collective-permute-start.15 = (bf16[64,1024]{1,0:T(8,128)(2,1)S(1)}, bf16[64,1024]{1,0:T(8,128)(2,1)S(1)}, u32[]{:S(2)}, u32[]{:S(2)}) collective-permute-start(bf16[64,1024]{1,0:T(8,128)(2,1)S(1)} %get-tuple-element.48.refs_2_), channel_id=1, source_target_pairs={{0,4},{4,0},{8,12},{12,8},{1,5},{5,1},{9,13},{13,9},{2,6},{6,2},{1... | collective-permute-start | bytes 393224 | tf_op jit(solution)/shard_map/ppermute | solution.py:357
  60.2 2.5 %collective-permute-done.9.refs_5_.refs_3_ = bf16[32,2176]{1,0:T(8,128)(2,1)S(1)} collective-permute-done((bf16[32,2176]{1,0:T(8,128)(2,1)S(1)}, bf16[32,2176]{1,0:T(8,128)(2,1)S(1)}, u32[]{:S(2)}, u32[]{:S(2)}) %collective-permute-start.9) | collective-permute-done | bytes 139296 | tf_op jit(solution)/shard_map/ppermute | solution.py:357
  62.7 2.8 %collective-permute-done.12.refs_1_ = bf16[64,1024]{1,0:T(8,128)(2,1)S(1)} collective-permute-done((bf16[64,1024]{1,0:T(8,128)(2,1)S(1)}, bf16[64,1024]{1,0:T(8,128)(2,1)S(1)}, u32[]{:S(2)}, u32[]{:S(2)}) %collective-permute-start.12) | collective-permute-done | bytes 131104 | tf_op jit(solution)/shard_map/ppermute | solution.py:357
  65.6 2.6 %collective-permute-start.14 = (bf16[32,1024]{1,0:T(8,128)(2,1)S(1)}, bf16[32,1024]{1,0:T(8,128)(2,1)S(1)}, u32[]{:S(2)}, u32[]{:S(2)}) collective-permute-start(bf16[32,1024]{1,0:T(8,128)(2,1)S(1)} %get-tuple-element.50), channel_id=1, source_target_pairs={{0,8},{4,12},{8,0},{12,4},{1,9},{5,13},{9,1},{13,5},{2,10},{6,14},... | collective-permute-start | bytes 196616 | tf_op jit(solution)/shard_map/ppermute | solution.py:357
  68.2 2.8 %collective-permute-start.19 = (bf16[32,1024]{1,0:T(8,128)(2,1)S(1)}, bf16[32,1024]{1,0:T(8,128)(2,1)S(1)}, u32[]{:S(2)}, u32[]{:S(2)}) collective-permute-start(bf16[32,1024]{1,0:T(8,128)(2,1)S(1)} %get-tuple-element.52.refs_0_), channel_id=1, source_target_pairs={{0,8},{4,12},{8,0},{12,4},{1,9},{5,13},{9,1},{13,5},{2,10},{6,14},... | collective-permute-start | bytes 196616 | tf_op jit(solution)/shard_map/ppermute | solution.py:357
  70.9 1.3 %collective-permute-done.14.came_ref = bf16[32,1024]{1,0:T(8,128)(2,1)S(1)} collective-permute-done((bf16[32,1024]{1,0:T(8,128)(2,1)S(1)}, bf16[32,1024]{1,0:T(8,128)(2,1)S(1)}, u32[]{:S(2)}, u32[]{:S(2)}) %collective-permute-start.14) | collective-permute-done | bytes 65568 | tf_op jit(solution)/shard_map/ppermute | solution.py:357
  72.3 0.6 shard_map.73.refs_4_
  72.9 1.2 %collective-permute-start.17 = (bf16[32,1152]{1,0:T(8,128)(2,1)S(1)}, bf16[32,1152]{1,0:T(8,128)(2,1)S(1)}, u32[]{:S(2)}, u32[]{:S(2)}) collective-permute-start(bf16[32,1152]{1,0:T(8,128)(2,1)S(1)} %shard_map.73.refs_4_), channel_id=1, source_target_pairs={{0,8},{4,12},{8,0},{12,4},{1,9},{5,13},{9,1},{13,5},{2,10},{6,14},... | collective-permute-start | bytes 221192 | tf_op jit(solution)/shard_map/ppermute | solution.py:357
  74.1 0.8 collective-permute-done.19.came_ref
  74.9 0.6 shard_map.75.refs_4_
  75.5 1.4 %collective-permute-start.21 = (bf16[32,1152]{1,0:T(8,128)(2,1)S(1)}, bf16[32,1152]{1,0:T(8,128)(2,1)S(1)}, u32[]{:S(2)}, u32[]{:S(2)}) collective-permute-start(bf16[32,1152]{1,0:T(8,128)(2,1)S(1)} %shard_map.75.refs_4_), channel_id=1, source_target_pairs={{0,8},{4,12},{8,0},{12,4},{1,9},{5,13},{9,1},{13,5},{2,10},{6,14},... | collective-permute-start | bytes 221192 | tf_op jit(solution)/shard_map/ppermute | solution.py:357
  76.9 3.0 %collective-permute-start.16 = (bf16[32,1152]{1,0:T(8,128)(2,1)S(1)}, bf16[32,1152]{1,0:T(8,128)(2,1)S(1)}, u32[]{:S(2)}, u32[]{:S(2)}) collective-permute-start(bf16[32,1152]{1,0:T(8,128)(2,1)S(1)} %shard_map.73.refs_4_), channel_id=1, source_target_pairs={{0,4},{4,0},{8,12},{12,8},{1,5},{5,1},{9,13},{13,9},{2,6},{6,2},{1... | collective-permute-start | bytes 221192 | tf_op jit(solution)/shard_map/ppermute | solution.py:357
  80.0 2.0 %collective-permute-start.20 = (bf16[32,1152]{1,0:T(8,128)(2,1)S(1)}, bf16[32,1152]{1,0:T(8,128)(2,1)S(1)}, u32[]{:S(2)}, u32[]{:S(2)}) collective-permute-start(bf16[32,1152]{1,0:T(8,128)(2,1)S(1)} %shard_map.75.refs_4_), channel_id=1, source_target_pairs={{0,4},{4,0},{8,12},{12,8},{1,5},{5,1},{9,13},{13,9},{2,6},{6,2},{1... | collective-permute-start | bytes 221192 | tf_op jit(solution)/shard_map/ppermute | solution.py:357
  82.0 1.1 %collective-permute-start.22 = (bf16[32,1152]{1,0:T(8,128)(2,1)S(1)}, bf16[32,1152]{1,0:T(8,128)(2,1)S(1)}, u32[]{:S(2)}, u32[]{:S(2)}) collective-permute-start(bf16[32,1152]{1,0:T(8,128)(2,1)S(1)} %collective-permute-done.21.refs_6_), channel_id=1, source_target_pairs={{0,4},{4,0},{8,12},{12,8},{1,5},{5,1},{9,13},{13,9},{2,6},{6,2},{1... | collective-permute-start | bytes 221192 | tf_op jit(solution)/shard_map/ppermute | solution.py:357
  83.1 0.1 collective-permute-done.16.refs_5_
  83.2 2.0 %collective-permute-done.18.refs_7_ = bf16[32,1152]{1,0:T(8,128)(2,1)S(1)} collective-permute-done((bf16[32,1152]{1,0:T(8,128)(2,1)S(1)}, bf16[32,1152]{1,0:T(8,128)(2,1)S(1)}, u32[]{:S(2)}, u32[]{:S(2)}) %collective-permute-start.18) | collective-permute-done | bytes 73760 | tf_op jit(solution)/shard_map/ppermute | solution.py:357
  85.2 0.1 collective-permute-start.23
  85.3 1.0 %collective-permute-done.20.refs_5_ = bf16[32,1152]{1,0:T(8,128)(2,1)S(1)} collective-permute-done((bf16[32,1152]{1,0:T(8,128)(2,1)S(1)}, bf16[32,1152]{1,0:T(8,128)(2,1)S(1)}, u32[]{:S(2)}, u32[]{:S(2)}) %collective-permute-start.20) | collective-permute-done | bytes 73760 | tf_op jit(solution)/shard_map/ppermute | solution.py:357
  86.3 0.8 collective-permute-done.22.refs_7_
  87.1 0.1 collective-permute-start.24
  87.3 0.1 shard_map.76.refs_1_
  87.4 1.4 %collective-permute-done.24.refs_3_ = bf16[128,1152]{1,0:T(8,128)(2,1)S(1)} collective-permute-done((bf16[128,1152]{1,0:T(8,128)(2,1)S(1)}, bf16[128,1152]{1,0:T(8,128)(2,1)S(1)}, u32[]{:S(2)}, u32[]{:S(2)}) %collective-permute-start.24) | collective-permute-done | bytes 294944 | tf_op jit(solution)/shard_map/ppermute | solution.py:354
  88.8 1.1 %shard_map.79 = (bf16[128,4096]{1,0:T(8,128)(2,1)}, bf16[32,128]{1,0:T(8,128)(2,1)}) custom-call(bf16[128,1152]{1,0:T(8,128)(2,1)S(1)} %shard_map.74.refs_0_, bf16[128,1152]{1,0:T(8,128)(2,1)S(1)} %shard_map.76.refs_1_, bf16[128,1152]{1,0:T(8,128)(2,1)S(1)} %collective-permute-done.23.refs_2_, bf16[128,1152]{1,0:T(8,128)(2,1)S(1)} %collective-permute-done.24.refs_3_), custom_call_target="tpu_custom_call" | custom-call | flops 1 | bytes 1 | tf_op jit(solution)/shard_map/pallas_call | solution.py:319
  (30 shorter events, 0.5 us)
Async XLA Ops:
  0.6 1.5 %copy-start = (bf16[128,6656]{1,0:T(8,128)(2,1)S(1)}, bf16[128,6656]{1,0:T(8,128)(2,1)}, u32[]{:S(2)}) copy-start(bf16[128,6656]{1,0:T(8,128)(2,1)} %in_ref.1) | copy-start | bytes 5111812
  2.2 15.8 %collective-permute-start = (bf16[128,2048]{1,0:T(8,128)(2,1)S(1)}, bf16[128,2048]{1,0:T(8,128)(2,1)S(1)}, u32[]{:S(2)}, u32[]{:S(2)}) collective-permute-start(bf16[128,2048]{1,0:T(8,128)(2,1)S(1)} %get-tuple-element.29.refs_4_.refs_0_), channel_id=1, source_target_pairs={{0,2},{2,0},{1,3},{3,1},{4,6},{6,4},{5,7},{7,5},{8,10},{10,8},{9,1... | collective-permute-start | bytes 1572872 | tf_op jit(solution)/shard_map/ppermute | solution.py:381
  5.3 23.2 %collective-permute-start.3 = (bf16[128,2048]{1,0:T(8,128)(2,1)S(1)}, bf16[128,2048]{1,0:T(8,128)(2,1)S(1)}, u32[]{:S(2)}, u32[]{:S(2)}) collective-permute-start(bf16[128,2048]{1,0:T(8,128)(2,1)S(1)} %get-tuple-element.30.refs_0_), channel_id=1, source_target_pairs={{0,2},{2,0},{1,3},{3,1},{4,6},{6,4},{5,7},{7,5},{8,10},{10,8},{9,1... | collective-permute-start | bytes 1572872 | tf_op jit(solution)/shard_map/ppermute | solution.py:381
  25.4 3.0 %collective-permute-start.1 = (bf16[128,1024]{1,0:T(8,128)(2,1)S(1)}, bf16[128,1024]{1,0:T(8,128)(2,1)S(1)}, u32[]{:S(2)}, u32[]{:S(2)}) collective-permute-start(bf16[128,1024]{1,0:T(8,128)(2,1)S(1)} %get-tuple-element.35), channel_id=1, source_target_pairs={{0,1},{1,0},{2,3},{3,2},{4,5},{5,4},{6,7},{7,6},{8,9},{9,8},{10,11... | collective-permute-start | bytes 786440 | tf_op jit(solution)/shard_map/ppermute | solution.py:354
  25.5 3.0 %collective-permute-start.2 = (bf16[128,1024]{1,0:T(8,128)(2,1)S(1)}, bf16[128,1024]{1,0:T(8,128)(2,1)S(1)}, u32[]{:S(2)}, u32[]{:S(2)}) collective-permute-start(bf16[128,1024]{1,0:T(8,128)(2,1)S(1)} %get-tuple-element.36), channel_id=1, source_target_pairs={{0,1},{1,0},{2,3},{3,2},{4,5},{5,4},{6,7},{7,6},{8,9},{9,8},{10,11... | collective-permute-start | bytes 786440 | tf_op jit(solution)/shard_map/ppermute | solution.py:354
  28.5 10.4 %collective-permute-start.4 = (bf16[64,2048]{1,0:T(8,128)(2,1)S(1)}, bf16[64,2048]{1,0:T(8,128)(2,1)S(1)}, u32[]{:S(2)}, u32[]{:S(2)}) collective-permute-start(bf16[64,2048]{1,0:T(8,128)(2,1)S(1)} %get-tuple-element.38.refs_3_), channel_id=1, source_target_pairs={{0,4},{4,0},{8,12},{12,8},{1,5},{5,1},{9,13},{13,9},{2,6},{6,2},{1... | collective-permute-start | bytes 786440 | tf_op jit(solution)/shard_map/ppermute | solution.py:357
  30.4 12.1 %collective-permute-start.6 = (bf16[128,1536]{1,0:T(8,128)(2,1)S(1)}, bf16[128,1536]{1,0:T(8,128)(2,1)S(1)}, u32[]{:S(2)}, u32[]{:S(2)}) collective-permute-start(bf16[128,1536]{1,0:T(8,128)(2,1)S(1)} %get-tuple-element.31.refs_1_), channel_id=1, source_target_pairs={{0,2},{2,0},{1,3},{3,1},{4,6},{6,4},{5,7},{7,5},{8,10},{10,8},{9,1... | collective-permute-start | bytes 1179656 | tf_op jit(solution)/shard_map/ppermute | solution.py:381
  31.9 19.9 %collective-permute-start.10 = (bf16[128,1024]{1,0:T(8,128)(2,1)S(1)}, bf16[128,1024]{1,0:T(8,128)(2,1)S(1)}, u32[]{:S(2)}, u32[]{:S(2)}) collective-permute-start(bf16[128,1024]{1,0:T(8,128)(2,1)S(1)} %get-tuple-element.32.refs_2_), channel_id=1, source_target_pairs={{0,2},{2,0},{1,3},{3,1},{4,6},{6,4},{5,7},{7,5},{8,10},{10,8},{9,1... | collective-permute-start | bytes 786440 | tf_op jit(solution)/shard_map/ppermute | solution.py:381
  38.9 2.7 %copy-start.2 = (s32[4096]{0:T(1024)S(1)}, s32[4096]{0:T(1024)}, u32[]{:S(2)}) copy-start(s32[4096]{0:T(1024)} %param.6) | copy-start | bytes 49156
  39.0 8.6 %collective-permute-start.5 = (bf16[32,2048]{1,0:T(8,128)(2,1)S(1)}, bf16[32,2048]{1,0:T(8,128)(2,1)S(1)}, u32[]{:S(2)}, u32[]{:S(2)}) collective-permute-start(bf16[32,2048]{1,0:T(8,128)(2,1)S(1)} %get-tuple-element.41.refs_3_), channel_id=1, source_target_pairs={{0,8},{4,12},{8,0},{12,4},{1,9},{5,13},{9,1},{13,5},{2,10},{6,14},... | collective-permute-start | bytes 393224 | tf_op jit(solution)/shard_map/ppermute | solution.py:357
  41.7 5.9 %copy-start.1 = (f32[128,128]{1,0:T(8,128)S(1)}, f32[128,128]{1,0:T(8,128)}, u32[]{:S(2)}) copy-start(f32[128,128]{1,0:T(8,128)} %constant.7.clone.rotation_ref) | copy-start | bytes 196612
  48.7 7.1 %collective-permute-start.7 = (bf16[32,2176]{1,0:T(8,128)(2,1)S(1)}, bf16[32,2176]{1,0:T(8,128)(2,1)S(1)}, u32[]{:S(2)}, u32[]{:S(2)}) collective-permute-start(bf16[32,2176]{1,0:T(8,128)(2,1)S(1)} %shard_map.66.refs_3_.refs_0_), channel_id=1, source_target_pairs={{0,4},{4,0},{8,12},{12,8},{1,5},{5,1},{9,13},{13,9},{2,6},{6,2},{1... | collective-permute-start | bytes 417800 | tf_op jit(solution)/shard_map/ppermute | solution.py:357
  48.9 6.8 %collective-permute-start.8 = (bf16[32,2176]{1,0:T(8,128)(2,1)S(1)}, bf16[32,2176]{1,0:T(8,128)(2,1)S(1)}, u32[]{:S(2)}, u32[]{:S(2)}) collective-permute-start(bf16[32,2176]{1,0:T(8,128)(2,1)S(1)} %shard_map.66.refs_3_.refs_0_), channel_id=1, source_target_pairs={{0,8},{4,12},{8,0},{12,4},{1,9},{5,13},{9,1},{13,5},{2,10},{6,14},... | collective-permute-start | bytes 417800 | tf_op jit(solution)/shard_map/ppermute | solution.py:357
  55.6 2.2 %collective-permute-start.11 = (bf16[128,1024]{1,0:T(8,128)(2,1)S(1)}, bf16[128,1024]{1,0:T(8,128)(2,1)S(1)}, u32[]{:S(2)}, u32[]{:S(2)}) collective-permute-start(bf16[128,1024]{1,0:T(8,128)(2,1)S(1)} %get-tuple-element.43), channel_id=1, source_target_pairs={{0,1},{1,0},{2,3},{3,2},{4,5},{5,4},{6,7},{7,6},{8,9},{9,8},{10,11... | collective-permute-start | bytes 786440 | tf_op jit(solution)/shard_map/ppermute | solution.py:354
  55.8 3.2 %collective-permute-start.13 = (bf16[128,1024]{1,0:T(8,128)(2,1)S(1)}, bf16[128,1024]{1,0:T(8,128)(2,1)S(1)}, u32[]{:S(2)}, u32[]{:S(2)}) collective-permute-start(bf16[128,1024]{1,0:T(8,128)(2,1)S(1)} %shard_map.69), channel_id=1, source_target_pairs={{0,1},{1,0},{2,3},{3,2},{4,5},{5,4},{6,7},{7,6},{8,9},{9,8},{10,11... | collective-permute-start | bytes 786440 | tf_op jit(solution)/shard_map/ppermute | solution.py:354
  56.2 6.5 %collective-permute-start.9 = (bf16[32,2176]{1,0:T(8,128)(2,1)S(1)}, bf16[32,2176]{1,0:T(8,128)(2,1)S(1)}, u32[]{:S(2)}, u32[]{:S(2)}) collective-permute-start(bf16[32,2176]{1,0:T(8,128)(2,1)S(1)} %collective-permute-done.8.refs_2_.refs_4_), channel_id=1, source_target_pairs={{0,4},{4,0},{8,12},{12,8},{1,5},{5,1},{9,13},{13,9},{2,6},{6,2},{1... | collective-permute-start | bytes 417800 | tf_op jit(solution)/shard_map/ppermute | solution.py:357
  58.0 7.6 %collective-permute-start.12 = (bf16[64,1024]{1,0:T(8,128)(2,1)S(1)}, bf16[64,1024]{1,0:T(8,128)(2,1)S(1)}, u32[]{:S(2)}, u32[]{:S(2)}) collective-permute-start(bf16[64,1024]{1,0:T(8,128)(2,1)S(1)} %get-tuple-element.45), channel_id=1, source_target_pairs={{0,4},{4,0},{8,12},{12,8},{1,5},{5,1},{9,13},{13,9},{2,6},{6,2},{1... | collective-permute-start | bytes 393224 | tf_op jit(solution)/shard_map/ppermute | solution.py:357
  59.0 9.1 %collective-permute-start.15 = (bf16[64,1024]{1,0:T(8,128)(2,1)S(1)}, bf16[64,1024]{1,0:T(8,128)(2,1)S(1)}, u32[]{:S(2)}, u32[]{:S(2)}) collective-permute-start(bf16[64,1024]{1,0:T(8,128)(2,1)S(1)} %get-tuple-element.48.refs_2_), channel_id=1, source_target_pairs={{0,4},{4,0},{8,12},{12,8},{1,5},{5,1},{9,13},{13,9},{2,6},{6,2},{1... | collective-permute-start | bytes 393224 | tf_op jit(solution)/shard_map/ppermute | solution.py:357
  65.6 6.7 %collective-permute-start.14 = (bf16[32,1024]{1,0:T(8,128)(2,1)S(1)}, bf16[32,1024]{1,0:T(8,128)(2,1)S(1)}, u32[]{:S(2)}, u32[]{:S(2)}) collective-permute-start(bf16[32,1024]{1,0:T(8,128)(2,1)S(1)} %get-tuple-element.50), channel_id=1, source_target_pairs={{0,8},{4,12},{8,0},{12,4},{1,9},{5,13},{9,1},{13,5},{2,10},{6,14},... | collective-permute-start | bytes 196616 | tf_op jit(solution)/shard_map/ppermute | solution.py:357
  68.2 6.7 %collective-permute-start.19 = (bf16[32,1024]{1,0:T(8,128)(2,1)S(1)}, bf16[32,1024]{1,0:T(8,128)(2,1)S(1)}, u32[]{:S(2)}, u32[]{:S(2)}) collective-permute-start(bf16[32,1024]{1,0:T(8,128)(2,1)S(1)} %get-tuple-element.52.refs_0_), channel_id=1, source_target_pairs={{0,8},{4,12},{8,0},{12,4},{1,9},{5,13},{9,1},{13,5},{2,10},{6,14},... | collective-permute-start | bytes 196616 | tf_op jit(solution)/shard_map/ppermute | solution.py:357
  72.9 7.0 %collective-permute-start.17 = (bf16[32,1152]{1,0:T(8,128)(2,1)S(1)}, bf16[32,1152]{1,0:T(8,128)(2,1)S(1)}, u32[]{:S(2)}, u32[]{:S(2)}) collective-permute-start(bf16[32,1152]{1,0:T(8,128)(2,1)S(1)} %shard_map.73.refs_4_), channel_id=1, source_target_pairs={{0,8},{4,12},{8,0},{12,4},{1,9},{5,13},{9,1},{13,5},{2,10},{6,14},... | collective-permute-start | bytes 221192 | tf_op jit(solution)/shard_map/ppermute | solution.py:357
  75.5 6.4 %collective-permute-start.21 = (bf16[32,1152]{1,0:T(8,128)(2,1)S(1)}, bf16[32,1152]{1,0:T(8,128)(2,1)S(1)}, u32[]{:S(2)}, u32[]{:S(2)}) collective-permute-start(bf16[32,1152]{1,0:T(8,128)(2,1)S(1)} %shard_map.75.refs_4_), channel_id=1, source_target_pairs={{0,8},{4,12},{8,0},{12,4},{1,9},{5,13},{9,1},{13,5},{2,10},{6,14},... | collective-permute-start | bytes 221192 | tf_op jit(solution)/shard_map/ppermute | solution.py:357
  76.9 6.3 %collective-permute-start.16 = (bf16[32,1152]{1,0:T(8,128)(2,1)S(1)}, bf16[32,1152]{1,0:T(8,128)(2,1)S(1)}, u32[]{:S(2)}, u32[]{:S(2)}) collective-permute-start(bf16[32,1152]{1,0:T(8,128)(2,1)S(1)} %shard_map.73.refs_4_), channel_id=1, source_target_pairs={{0,4},{4,0},{8,12},{12,8},{1,5},{5,1},{9,13},{13,9},{2,6},{6,2},{1... | collective-permute-start | bytes 221192 | tf_op jit(solution)/shard_map/ppermute | solution.py:357
  79.9 5.2 %collective-permute-start.18 = (bf16[32,1152]{1,0:T(8,128)(2,1)S(1)}, bf16[32,1152]{1,0:T(8,128)(2,1)S(1)}, u32[]{:S(2)}, u32[]{:S(2)}) collective-permute-start(bf16[32,1152]{1,0:T(8,128)(2,1)S(1)} %collective-permute-done.17.refs_6_), channel_id=1, source_target_pairs={{0,4},{4,0},{8,12},{12,8},{1,5},{5,1},{9,13},{13,9},{2,6},{6,2},{1... | collective-permute-start | bytes 221192 | tf_op jit(solution)/shard_map/ppermute | solution.py:357
  80.0 6.3 %collective-permute-start.20 = (bf16[32,1152]{1,0:T(8,128)(2,1)S(1)}, bf16[32,1152]{1,0:T(8,128)(2,1)S(1)}, u32[]{:S(2)}, u32[]{:S(2)}) collective-permute-start(bf16[32,1152]{1,0:T(8,128)(2,1)S(1)} %shard_map.75.refs_4_), channel_id=1, source_target_pairs={{0,4},{4,0},{8,12},{12,8},{1,5},{5,1},{9,13},{13,9},{2,6},{6,2},{1... | collective-permute-start | bytes 221192 | tf_op jit(solution)/shard_map/ppermute | solution.py:357
  82.0 5.1 %collective-permute-start.22 = (bf16[32,1152]{1,0:T(8,128)(2,1)S(1)}, bf16[32,1152]{1,0:T(8,128)(2,1)S(1)}, u32[]{:S(2)}, u32[]{:S(2)}) collective-permute-start(bf16[32,1152]{1,0:T(8,128)(2,1)S(1)} %collective-permute-done.21.refs_6_), channel_id=1, source_target_pairs={{0,4},{4,0},{8,12},{12,8},{1,5},{5,1},{9,13},{13,9},{2,6},{6,2},{1... | collective-permute-start | bytes 221192 | tf_op jit(solution)/shard_map/ppermute | solution.py:357
  85.2 2.2 %collective-permute-start.23 = (bf16[128,1152]{1,0:T(8,128)(2,1)S(1)}, bf16[128,1152]{1,0:T(8,128)(2,1)S(1)}, u32[]{:S(2)}, u32[]{:S(2)}) collective-permute-start(bf16[128,1152]{1,0:T(8,128)(2,1)S(1)} %shard_map.77), channel_id=1, source_target_pairs={{0,1},{1,0},{2,3},{3,2},{4,5},{5,4},{6,7},{7,6},{8,9},{9,8},{10,11... | collective-permute-start | bytes 884744 | tf_op jit(solution)/shard_map/ppermute | solution.py:354
  87.1 1.6 %collective-permute-start.24 = (bf16[128,1152]{1,0:T(8,128)(2,1)S(1)}, bf16[128,1152]{1,0:T(8,128)(2,1)S(1)}, u32[]{:S(2)}, u32[]{:S(2)}) collective-permute-start(bf16[128,1152]{1,0:T(8,128)(2,1)S(1)} %shard_map.78), channel_id=1, source_target_pairs={{0,1},{1,0},{2,3},{3,2},{4,5},{5,4},{6,7},{7,6},{8,9},{9,8},{10,11... | collective-permute-start | bytes 884744 | tf_op jit(solution)/shard_map/ppermute | solution.py:354

commit v10 on v9

--- a/solution.py
+++ b/solution.py
@@ -13,7 +13,7 @@
 UNIT = 512
 GROUPS = 2
 VMEM_LIMIT = 6 * 2**20
-SHARES = (4, 4, 3)
+SHARES = (4, 3, 4)
 epsilon = 1e-06
 
 SMALL = pl.CostEstimate(flops=1, bytes_accessed=1, transcendentals=0)
@@ -55,25 +55,28 @@
     )(values)
 
 
-def multiply_body(spans, has_totals, splits, row, groups, *refs):
+def multiply_body(spans, has_totals, splits, row, groups, only, *refs):
     lefts = [refs[begin:end] for begin, end in spans]
     refs = refs[spans[-1][1] :]
     w_ref, refs = refs[0], refs[1:]
     total_refs, refs = list(refs[: sum(has_totals)]), refs[sum(has_totals) :]
     buffer, arrived = refs[-2:]
-    out_count = sum(2 * groups if split else 1 for split in splits)
+    outs_of_split = 2 if only is not None else 2 * groups
+    out_count = sum(outs_of_split if split else 1 for split in splits)
     out_refs = refs[-2 - out_count : -2]
     steps, depth, wide = buffer.shape
     rows = lefts[0][0].shape[0]
-    first = steps // 2 // groups
+    in_half = w_ref.shape[1] // wide // 2
+    first = in_half // groups
     here = lax.axis_index("sub")
 
     def column(n):
         if not any(splits):
             return n
         group, place = n // (2 * first), n % (2 * first)
+        group = group if only is None else only
         side, place = (here, place - first) if place >= first else (1 - here, place)
-        return side * (steps // 2) + group * first + place
+        return side * in_half + group * first + place
 
     def at(block):
         return pl.ds(pl.multiple_of(block * wide, wide), wide)
@@ -101,7 +104,7 @@
                 out_ref = outs[2 * group + place // first]
                 begin = place % first * wide
                 out_ref[:, begin : begin + wide] = value.astype(out_ref.dtype)
-                outs = outs[2 * groups :]
+                outs = outs[outs_of_split:]
             else:
                 outs.pop(0)[:, at(column(n))] = value
 
@@ -114,11 +117,11 @@
         pl.loop(0, steps)(step)
 
 
-def multiply(lefts, weight, row, totals, splits, wide, groups=1, tokens=()):
+def multiply(lefts, weight, row, totals, splits, wide, groups=1, only=None, tokens=()):
     rows = lefts[0][0].shape[0]
     depth = sum(part.shape[1] for part in lefts[0])
     columns = weight.shape[1]
-    steps = columns // wide
+    steps = columns // wide // (1 if only is None else groups)
     spans = [(index * len(left), (index + 1) * len(left)) for index, left in enumerate(lefts)]
     held = [total for total in totals if total is not None]
     out_shape = []
@@ -127,11 +130,11 @@
             out_shape += [
                 jax.ShapeDtypeStruct((rows, columns // 2 // groups), jnp.bfloat16),
                 jax.ShapeDtypeStruct((rows, columns // 2 // groups), jnp.float32),
-            ] * groups
+            ] * (groups if only is None else 1)
         else:
             out_shape.append(jax.ShapeDtypeStruct((rows, columns), jnp.float32))
     body = functools.partial(
-        multiply_body, spans, [total is not None for total in totals], splits, row, groups
+        multiply_body, spans, [total is not None for total in totals], splits, row, groups, only
     )
     return pl.pallas_call(
         body,
@@ -410,12 +413,13 @@
                         results.append([spread(step)])
             if not results:
                 results.append([spread(list(own_steps)[-1])])
-            outs = multiply(
-                [[arrived[-1]]], down_weight, places[-1], [total], [True], wide_chunk, groups=GROUPS, tokens=tokens
-            )
             remote, all_steps = [], []
             for group in range(GROUPS):
-                sent, kept = outs[2 * group : 2 * group + 2]
+                sent, kept = multiply(
+                    [[arrived[-1]]], down_weight, places[-1], [total], [True], wide_chunk,
+                    groups=GROUPS, only=group, tokens=tokens,
+                )
+                tokens = [sent]
                 if group == GROUPS - 1 and shift == 0 and levels > 1:
                     sent = gate(sent, [results[0][0][1], results[0][0][1 << levels - 1]])
                 all_steps.append(reduce([sent, kept], group * half // GROUPS))
@@ -424,7 +428,7 @@
             for level in range(levels + 1):
                 for group, steps in enumerate(all_steps):
                     wait = list(last) if group == 0 else []
-                    if group == 0 and level == 1 and shift == 0:
+                    if group == 0 and level == levels and shift == 0:
                         wait += results[0][0][1:]
                     step = steps.send(wait)
                     if level == levels:

time: 90.1 us -> 91 us (level)
  starting transfers between devices: 31.9 us -> 24.8 us
  waiting for transfers between devices: 16 us -> 22.8 us
  Pallas kernels: 39.6 us -> 40.9 us
    ppermute x15, starting transfers between devices: 25.5 us -> 17 us  [exchange(): lax.ppermute(values, 'tensor', [(t, t ^ 1 << level) for t in range(tensor...]
    ppermute x15, waiting for transfers between devices: 11.4 us -> 19.3 us  [exchange(): lax.ppermute(values, 'tensor', [(t, t ^ 1 << level) for t in range(tensor...]
    ppermute x4, waiting for transfers between devices: 3.22 us -> 1.59 us  [shards(): arrivals.append([lax.ppermute(part, 'seq', pairs) for part in parts])]
    ppermute x4, starting transfers between devices: 5.11 us -> 6.46 us  [shards(): arrivals.append([lax.ppermute(part, 'seq', pairs) for part in parts])]
    pallas_call x5 -> x6, Pallas kernels: 35.5 us -> 36.8 us  [multiply(): pl.pallas_call(body, out_shape=out_shape, in_specs=[VMEM] * spans[-1][1]...]
  transfers between devices with their start and end apart: 25 -> 25, of which waited for: 11 -> 13; matrix products, arithmetic and copies ran while one was open for 0% -> 0% of each run, Pallas kernels for 43% -> 44%
where the time goes in v10:
time: 91 us; the launch traced here: 90.9 us
  Pallas kernels  40.9 us (45%)
  starting transfers between devices  24.8 us (27%)
  waiting for transfers between devices  22.8 us (25%)
  local copies, waits for them, and re-layouts  1.46 us (2%)
  between operations  0.93 us (1%)
    pallas_call x6, Pallas kernels, multiply(): pl.pallas_call(body, out_shape=out_shape, in_specs=[VMEM] * spans[-1][1]...  36.8 us
    ppermute x15, waiting for transfers between devices, exchange(): lax.ppermute(values, 'tensor', [(t, t ^ 1 << level) for t in range(tensor...  19.3 us
    ppermute x15, starting transfers between devices, exchange(): lax.ppermute(values, 'tensor', [(t, t ^ 1 << level) for t in range(tensor...  17 us
    ppermute x4, starting transfers between devices, shards(): arrivals.append([lax.ppermute(part, 'seq', pairs) for part in parts])  6.46 us
    pallas_call x3, Pallas kernels, encode(): pl.pallas_call(functools.partial(encode_body, begin), out_shape=jax.Shape...  2.24 us
    ppermute x6, waiting for transfers between devices, swap(): return lax.ppermute(values, 'sub', [(0, 1), (1, 0)])  1.97 us
  transfers between devices with their start and end apart: 25, of which 13 were waited for; matrix products, arithmetic and copies ran while one was open for 0% of the time, Pallas kernels for 44%

profile of v10, /device:TPU:0, one launch (start us, length us, event | category | flops | bytes accessed | tf_op | source)
XLA Modules:
  0.0 90.9 jit_solution(17802818552074400274)
XLA Ops:
  0.6 1.4 %copy-done = bf16[128,6656]{1,0:T(8,128)(2,1)S(1)} copy-done((bf16[128,6656]{1,0:T(8,128)(2,1)S(1)}, bf16[128,6656]{1,0:T(8,128)(2,1)}, u32[]{:S(2)}) %copy-start) | copy-done | bytes 1703960
  2.1 0.2 shard_map.59
  2.2 3.0 %collective-permute-start = (bf16[128,2048]{1,0:T(8,128)(2,1)S(1)}, bf16[128,2048]{1,0:T(8,128)(2,1)S(1)}, u32[]{:S(2)}, u32[]{:S(2)}) collective-permute-start(bf16[128,2048]{1,0:T(8,128)(2,1)S(1)} %get-tuple-element.29.refs_4_.refs_0_), channel_id=1, source_target_pairs={{0,2},{2,0},{1,3},{3,1},{4,6},{6,4},{5,7},{7,5},{8,10},{10,8},{9,1... | collective-permute-start | bytes 1572872 | tf_op jit(solution)/shard_map/ppermute | solution.py:384
  5.3 0.1 collective-permute-start.3
  5.3 12.7 %shard_map.60.refs_3_ = f32[128,4096]{1,0:T(8,128)S(1)} custom-call(bf16[128,1536]{1,0:T(8,128)(2,1)S(1)} %get-tuple-element.30.refs_0_, bf16[128,2048]{1,0:T(8,128)(2,1)S(1)} %get-tuple-element.31.refs_1_, bf16[128,1024]{1,0:T(8,128)(2,1)S(1)} %get-tuple-element.32.refs_2_, bf16[6656,4096]{1,0:T(8,128)(2,1)} %refs_1_.7, ...), custom_call_target="tpu_custom_call" | custom-call | flops 1 | bytes 1 | tf_op jit(solution)/shard_map/pallas_call | solution.py:139
  18.0 7.3 %shard_map.61 = (bf16[128,1024]{1,0:T(8,128)(2,1)S(1)}, f32[128,1024]{1,0:T(8,128)S(1)}, bf16[128,1024]{1,0:T(8,128)(2,1)S(1)}, f32[128,1024]{1,0:T(8,128)S(1)}, f32[128,4096]{1,0:T(8,128)S(1)}) custom-call(bf16[128,2048]{1,0:T(8,128)(2,1)S(1)} %get-tuple-element.29.refs_4_.refs_0_, bf16[128,2048]{1,0:T(8,128)(2,1)S(1)} %collective-permute-done.refs_1_, ...), custom_call_target="tpu_custom_call" | custom-call | flops 1 | bytes 1 | tf_op jit(solution)/shard_map/pallas_call | solution.py:139
  25.4 0.1 collective-permute-start.1
  25.5 0.5 collective-permute-start.2
  26.0 2.0 %collective-permute-start.6 = (bf16[128,2048]{1,0:T(8,128)(2,1)S(1)}, bf16[128,2048]{1,0:T(8,128)(2,1)S(1)}, u32[]{:S(2)}, u32[]{:S(2)}) collective-permute-start(bf16[128,2048]{1,0:T(8,128)(2,1)S(1)} %get-tuple-element.31.refs_1_), channel_id=1, source_target_pairs={{0,2},{2,0},{1,3},{3,1},{4,6},{6,4},{5,7},{7,5},{8,10},{10,8},{9,1... | collective-permute-start | bytes 1572872 | tf_op jit(solution)/shard_map/ppermute | solution.py:384
  28.0 0.1 shard_map.62
  28.1 1.6 %collective-permute-start.4 = (bf16[64,2048]{1,0:T(8,128)(2,1)S(1)}, bf16[64,2048]{1,0:T(8,128)(2,1)S(1)}, u32[]{:S(2)}, u32[]{:S(2)}) collective-permute-start(bf16[64,2048]{1,0:T(8,128)(2,1)S(1)} %get-tuple-element.38.refs_3_), channel_id=1, source_target_pairs={{0,4},{4,0},{8,12},{12,8},{1,5},{5,1},{9,13},{13,9},{2,6},{6,2},{1... | collective-permute-start | bytes 786440 | tf_op jit(solution)/shard_map/ppermute | solution.py:360
  29.7 1.4 %collective-permute-start.10 = (bf16[128,1024]{1,0:T(8,128)(2,1)S(1)}, bf16[128,1024]{1,0:T(8,128)(2,1)S(1)}, u32[]{:S(2)}, u32[]{:S(2)}) collective-permute-start(bf16[128,1024]{1,0:T(8,128)(2,1)S(1)} %get-tuple-element.32.refs_2_), channel_id=1, source_target_pairs={{0,2},{2,0},{1,3},{3,1},{4,6},{6,4},{5,7},{7,5},{8,10},{10,8},{9,1... | collective-permute-start | bytes 786440 | tf_op jit(solution)/shard_map/ppermute | solution.py:384
  31.1 5.2 %shard_map.63.refs_2_ = f32[128,4096]{1,0:T(8,128)S(1)} custom-call(bf16[128,1536]{1,0:T(8,128)(2,1)S(1)} %collective-permute-done.3.refs_4_.refs_0_, bf16[6656,4096]{1,0:T(8,128)(2,1)} %refs_1_.7, f32[128,4096]{1,0:T(8,128)S(1)} %get-tuple-element.39.refs_2_, bf16[64,2048]{1,0:T(8,128)(2,1)S(1)} %get-tuple-element.38.refs_3_), custom_call_target="tpu_custom_call" | custom-call | flops 1 | bytes 1 | tf_op jit(solution)/shard_map/pallas_call | solution.py:139
  36.4 2.7 %collective-permute-start.5 = (bf16[32,2048]{1,0:T(8,128)(2,1)S(1)}, bf16[32,2048]{1,0:T(8,128)(2,1)S(1)}, u32[]{:S(2)}, u32[]{:S(2)}) collective-permute-start(bf16[32,2048]{1,0:T(8,128)(2,1)S(1)} %get-tuple-element.41.refs_3_), channel_id=1, source_target_pairs={{0,8},{4,12},{8,0},{12,4},{1,9},{5,13},{9,1},{13,5},{2,10},{6,14},... | collective-permute-start | bytes 393224 | tf_op jit(solution)/shard_map/ppermute | solution.py:360
  39.1 1.6 %collective-permute-done.6.refs_0_ = bf16[128,2048]{1,0:T(8,128)(2,1)S(1)} collective-permute-done((bf16[128,2048]{1,0:T(8,128)(2,1)S(1)}, bf16[128,2048]{1,0:T(8,128)(2,1)S(1)}, u32[]{:S(2)}, u32[]{:S(2)}) %collective-permute-start.6) | collective-permute-done | bytes 524320 | tf_op jit(solution)/shard_map/ppermute | solution.py:384
  40.7 6.5 %shard_map.65.refs_0_.refs_2_ = f32[128,4096]{1,0:T(8,128)S(1)} custom-call(bf16[128,2048]{1,0:T(8,128)(2,1)S(1)} %collective-permute-done.6.refs_0_, bf16[6656,4096]{1,0:T(8,128)(2,1)} %refs_1_.7, f32[128,4096]{1,0:T(8,128)S(1)} %shard_map.63.refs_2_, bf16[32,2048]{1,0:T(8,128)(2,1)S(1)} %get-tuple-element.41.refs_3_), custom_call_target="tpu_custom_call" | custom-call | flops 1 | bytes 1 | tf_op jit(solution)/shard_map/pallas_call | solution.py:139
  47.2 1.0 %shard_map.66.refs_3_.refs_0_ = bf16[32,2176]{1,0:T(8,128)(2,1)S(1)} custom-call(f32[32,2048]{1,0:T(8,128)S(1)} %get-tuple-element.40.kept_ref, bf16[32,2048]{1,0:T(8,128)(2,1)S(1)} %collective-permute-done.5.came_ref, f32[1,4096]{1,0:T(1,128)S(1)} %bitcast.2, f32[128,128]{1,0:T(8,128)S(1)} %copy-done.1, f32[128,4096]{1,0:T(8,128)S(1)} %shard_map.65.refs_0_.refs_2_), custom_call_target="tpu_custom_call" | custom-call | flops 1 | bytes 1 | tf_op jit(solution)/shard_map/pallas_call | solution.py:227
  48.2 2.2 %collective-permute-start.7 = (bf16[32,2176]{1,0:T(8,128)(2,1)S(1)}, bf16[32,2176]{1,0:T(8,128)(2,1)S(1)}, u32[]{:S(2)}, u32[]{:S(2)}) collective-permute-start(bf16[32,2176]{1,0:T(8,128)(2,1)S(1)} %shard_map.66.refs_3_.refs_0_), channel_id=1, source_target_pairs={{0,4},{4,0},{8,12},{12,8},{1,5},{5,1},{9,13},{13,9},{2,6},{6,2},{1... | collective-permute-start | bytes 417800 | tf_op jit(solution)/shard_map/ppermute | solution.py:360
  50.4 2.6 %collective-permute-start.8 = (bf16[32,2176]{1,0:T(8,128)(2,1)S(1)}, bf16[32,2176]{1,0:T(8,128)(2,1)S(1)}, u32[]{:S(2)}, u32[]{:S(2)}) collective-permute-start(bf16[32,2176]{1,0:T(8,128)(2,1)S(1)} %shard_map.66.refs_3_.refs_0_), channel_id=1, source_target_pairs={{0,8},{4,12},{8,0},{12,4},{1,9},{5,13},{9,1},{13,5},{2,10},{6,14},... | collective-permute-start | bytes 417800 | tf_op jit(solution)/shard_map/ppermute | solution.py:360
  53.0 2.5 %shard_map.67 = (bf16[128,1024]{1,0:T(8,128)(2,1)S(1)}, f32[128,1024]{1,0:T(8,128)S(1)}) custom-call(bf16[128,1024]{1,0:T(8,128)(2,1)S(1)} %collective-permute-done.10.refs_0_, bf16[6656,4096]{1,0:T(8,128)(2,1)} %refs_1_.7, f32[128,4096]{1,0:T(8,128)S(1)} %shard_map.65.refs_0_.refs_2_, bf16[32,2176]{1,0:T(8,128)(2,1)S(1)} %shard_map.66.refs_3_.refs_0_), custom_call_target="tpu_custom_call" | custom-call | flops 1 | bytes 1 | tf_op jit(solution)/shard_map/pallas_call | solution.py:139
  55.6 0.1 collective-permute-start.11
  55.7 2.6 %shard_map.69 = (bf16[128,1024]{1,0:T(8,128)(2,1)S(1)}, f32[128,1024]{1,0:T(8,128)S(1)}) custom-call(bf16[128,1024]{1,0:T(8,128)(2,1)S(1)} %collective-permute-done.10.refs_0_, bf16[6656,4096]{1,0:T(8,128)(2,1)} %refs_1_.7, f32[128,4096]{1,0:T(8,128)S(1)} %shard_map.65.refs_0_.refs_2_, bf16[128,1024]{1,0:T(8,128)(2,1)S(1)} %get-tuple-element.43.refs_3_), custom_call_target="tpu_custom_call" | custom-call | flops 1 | bytes 1 | tf_op jit(solution)/shard_map/pallas_call | solution.py:139
  58.3 0.5 collective-permute-start.13
  58.9 0.5 collective-permute-start.12
  59.4 0.6 collective-permute-done.13.refs_1_
  60.0 1.1 %collective-permute-start.15 = (bf16[64,1024]{1,0:T(8,128)(2,1)S(1)}, bf16[64,1024]{1,0:T(8,128)(2,1)S(1)}, u32[]{:S(2)}, u32[]{:S(2)}) collective-permute-start(bf16[64,1024]{1,0:T(8,128)(2,1)S(1)} %get-tuple-element.48.refs_2_), channel_id=1, source_target_pairs={{0,4},{4,0},{8,12},{12,8},{1,5},{5,1},{9,13},{13,9},{2,6},{6,2},{1... | collective-permute-start | bytes 393224 | tf_op jit(solution)/shard_map/ppermute | solution.py:360
  61.1 1.0 %collective-permute-start.9 = (bf16[32,2176]{1,0:T(8,128)(2,1)S(1)}, bf16[32,2176]{1,0:T(8,128)(2,1)S(1)}, u32[]{:S(2)}, u32[]{:S(2)}) collective-permute-start(bf16[32,2176]{1,0:T(8,128)(2,1)S(1)} %collective-permute-done.8.refs_2_), channel_id=1, source_target_pairs={{0,4},{4,0},{8,12},{12,8},{1,5},{5,1},{9,13},{13,9},{2,6},{6,2},{1... | collective-permute-start | bytes 417800 | tf_op jit(solution)/shard_map/ppermute | solution.py:360
  62.1 3.2 %collective-permute-done.12.refs_1_ = bf16[64,1024]{1,0:T(8,128)(2,1)S(1)} collective-permute-done((bf16[64,1024]{1,0:T(8,128)(2,1)S(1)}, bf16[64,1024]{1,0:T(8,128)(2,1)S(1)}, u32[]{:S(2)}, u32[]{:S(2)}) %collective-permute-start.12) | collective-permute-done | bytes 131104 | tf_op jit(solution)/shard_map/ppermute | solution.py:360
  65.3 0.6 collective-permute-start.14
  65.9 2.9 %collective-permute-done.15.refs_1_ = bf16[64,1024]{1,0:T(8,128)(2,1)S(1)} collective-permute-done((bf16[64,1024]{1,0:T(8,128)(2,1)S(1)}, bf16[64,1024]{1,0:T(8,128)(2,1)S(1)}, u32[]{:S(2)}, u32[]{:S(2)}) %collective-permute-start.15) | collective-permute-done | bytes 131104 | tf_op jit(solution)/shard_map/ppermute | solution.py:360
  68.9 0.1 collective-permute-start.19
  68.9 3.0 %collective-permute-done.9.refs_3_ = bf16[32,2176]{1,0:T(8,128)(2,1)S(1)} collective-permute-done((bf16[32,2176]{1,0:T(8,128)(2,1)S(1)}, bf16[32,2176]{1,0:T(8,128)(2,1)S(1)}, u32[]{:S(2)}, u32[]{:S(2)}) %collective-permute-start.9) | collective-permute-done | bytes 139296 | tf_op jit(solution)/shard_map/ppermute | solution.py:360
  72.0 2.0 %collective-permute-done.14.came_ref = bf16[32,1024]{1,0:T(8,128)(2,1)S(1)} collective-permute-done((bf16[32,1024]{1,0:T(8,128)(2,1)S(1)}, bf16[32,1024]{1,0:T(8,128)(2,1)S(1)}, u32[]{:S(2)}, u32[]{:S(2)}) %collective-permute-start.14) | collective-permute-done | bytes 65568 | tf_op jit(solution)/shard_map/ppermute | solution.py:360
  74.0 0.6 shard_map.74.refs_4_
  74.6 0.1 collective-permute-start.17
  74.7 0.6 collective-permute-done.19.came_ref
  75.3 0.6 shard_map.76.refs_4_
  75.9 2.4 %collective-permute-start.21 = (bf16[32,1152]{1,0:T(8,128)(2,1)S(1)}, bf16[32,1152]{1,0:T(8,128)(2,1)S(1)}, u32[]{:S(2)}, u32[]{:S(2)}) collective-permute-start(bf16[32,1152]{1,0:T(8,128)(2,1)S(1)} %shard_map.76.refs_4_), channel_id=1, source_target_pairs={{0,8},{4,12},{8,0},{12,4},{1,9},{5,13},{9,1},{13,5},{2,10},{6,14},... | collective-permute-start | bytes 221192 | tf_op jit(solution)/shard_map/ppermute | solution.py:360
  78.3 3.4 %collective-permute-done.17.refs_6_ = bf16[32,1152]{1,0:T(8,128)(2,1)S(1)} collective-permute-done((bf16[32,1152]{1,0:T(8,128)(2,1)S(1)}, bf16[32,1152]{1,0:T(8,128)(2,1)S(1)}, u32[]{:S(2)}, u32[]{:S(2)}) %collective-permute-start.17) | collective-permute-done | bytes 73760 | tf_op jit(solution)/shard_map/ppermute | solution.py:360
  81.7 2.0 %collective-permute-start.20 = (bf16[32,1152]{1,0:T(8,128)(2,1)S(1)}, bf16[32,1152]{1,0:T(8,128)(2,1)S(1)}, u32[]{:S(2)}, u32[]{:S(2)}) collective-permute-start(bf16[32,1152]{1,0:T(8,128)(2,1)S(1)} %shard_map.76.refs_4_), channel_id=1, source_target_pairs={{0,4},{4,0},{8,12},{12,8},{1,5},{5,1},{9,13},{13,9},{2,6},{6,2},{1... | collective-permute-start | bytes 221192 | tf_op jit(solution)/shard_map/ppermute | solution.py:360
  83.8 0.3 collective-permute-done.16.refs_5_
  84.0 2.0 %collective-permute-done.18.refs_7_ = bf16[32,1152]{1,0:T(8,128)(2,1)S(1)} collective-permute-done((bf16[32,1152]{1,0:T(8,128)(2,1)S(1)}, bf16[32,1152]{1,0:T(8,128)(2,1)S(1)}, u32[]{:S(2)}, u32[]{:S(2)}) %collective-permute-start.18) | collective-permute-done | bytes 73760 | tf_op jit(solution)/shard_map/ppermute | solution.py:360
  86.1 0.1 collective-permute-start.23
  86.2 0.7 collective-permute-done.20.refs_5_
  86.8 1.2 %collective-permute-done.22.refs_7_ = bf16[32,1152]{1,0:T(8,128)(2,1)S(1)} collective-permute-done((bf16[32,1152]{1,0:T(8,128)(2,1)S(1)}, bf16[32,1152]{1,0:T(8,128)(2,1)S(1)}, u32[]{:S(2)}, u32[]{:S(2)}) %collective-permute-start.22) | collective-permute-done | bytes 73760 | tf_op jit(solution)/shard_map/ppermute | solution.py:360
  88.2 0.1 shard_map.77.refs_1_
  88.4 1.4 %collective-permute-done.24.refs_3_ = bf16[128,1152]{1,0:T(8,128)(2,1)S(1)} collective-permute-done((bf16[128,1152]{1,0:T(8,128)(2,1)S(1)}, bf16[128,1152]{1,0:T(8,128)(2,1)S(1)}, u32[]{:S(2)}, u32[]{:S(2)}) %collective-permute-start.24) | collective-permute-done | bytes 294944 | tf_op jit(solution)/shard_map/ppermute | solution.py:357
  89.8 1.1 %shard_map.80 = (bf16[128,4096]{1,0:T(8,128)(2,1)}, bf16[32,128]{1,0:T(8,128)(2,1)}) custom-call(bf16[128,1152]{1,0:T(8,128)(2,1)S(1)} %shard_map.75.refs_0_, bf16[128,1152]{1,0:T(8,128)(2,1)S(1)} %shard_map.77.refs_1_, bf16[128,1152]{1,0:T(8,128)(2,1)S(1)} %collective-permute-done.23.refs_2_, bf16[128,1152]{1,0:T(8,128)(2,1)S(1)} %collective-permute-done.24.refs_3_), custom_call_target="tpu_custom_call" | custom-call | flops 1 | bytes 1 | tf_op jit(solution)/shard_map/pallas_call | solution.py:322
  (31 shorter events, 0.6 us)
Async XLA Ops:
  0.6 1.5 %copy-start = (bf16[128,6656]{1,0:T(8,128)(2,1)S(1)}, bf16[128,6656]{1,0:T(8,128)(2,1)}, u32[]{:S(2)}) copy-start(bf16[128,6656]{1,0:T(8,128)(2,1)} %in_ref.1) | copy-start | bytes 5111812
  2.2 15.8 %collective-permute-start = (bf16[128,2048]{1,0:T(8,128)(2,1)S(1)}, bf16[128,2048]{1,0:T(8,128)(2,1)S(1)}, u32[]{:S(2)}, u32[]{:S(2)}) collective-permute-start(bf16[128,2048]{1,0:T(8,128)(2,1)S(1)} %get-tuple-element.29.refs_4_.refs_0_), channel_id=1, source_target_pairs={{0,2},{2,0},{1,3},{3,1},{4,6},{6,4},{5,7},{7,5},{8,10},{10,8},{9,1... | collective-permute-start | bytes 1572872 | tf_op jit(solution)/shard_map/ppermute | solution.py:384
  5.3 22.7 %collective-permute-start.3 = (bf16[128,1536]{1,0:T(8,128)(2,1)S(1)}, bf16[128,1536]{1,0:T(8,128)(2,1)S(1)}, u32[]{:S(2)}, u32[]{:S(2)}) collective-permute-start(bf16[128,1536]{1,0:T(8,128)(2,1)S(1)} %get-tuple-element.30.refs_0_), channel_id=1, source_target_pairs={{0,2},{2,0},{1,3},{3,1},{4,6},{6,4},{5,7},{7,5},{8,10},{10,8},{9,1... | collective-permute-start | bytes 1179656 | tf_op jit(solution)/shard_map/ppermute | solution.py:384
  25.4 2.6 %collective-permute-start.1 = (bf16[128,1024]{1,0:T(8,128)(2,1)S(1)}, bf16[128,1024]{1,0:T(8,128)(2,1)S(1)}, u32[]{:S(2)}, u32[]{:S(2)}) collective-permute-start(bf16[128,1024]{1,0:T(8,128)(2,1)S(1)} %get-tuple-element.35), channel_id=1, source_target_pairs={{0,1},{1,0},{2,3},{3,2},{4,5},{5,4},{6,7},{7,6},{8,9},{9,8},{10,11... | collective-permute-start | bytes 786440 | tf_op jit(solution)/shard_map/ppermute | solution.py:357
  25.5 2.5 %collective-permute-start.2 = (bf16[128,1024]{1,0:T(8,128)(2,1)S(1)}, bf16[128,1024]{1,0:T(8,128)(2,1)S(1)}, u32[]{:S(2)}, u32[]{:S(2)}) collective-permute-start(bf16[128,1024]{1,0:T(8,128)(2,1)S(1)} %get-tuple-element.36), channel_id=1, source_target_pairs={{0,1},{1,0},{2,3},{3,2},{4,5},{5,4},{6,7},{7,6},{8,9},{9,8},{10,11... | collective-permute-start | bytes 786440 | tf_op jit(solution)/shard_map/ppermute | solution.py:357
  26.0 14.7 %collective-permute-start.6 = (bf16[128,2048]{1,0:T(8,128)(2,1)S(1)}, bf16[128,2048]{1,0:T(8,128)(2,1)S(1)}, u32[]{:S(2)}, u32[]{:S(2)}) collective-permute-start(bf16[128,2048]{1,0:T(8,128)(2,1)S(1)} %get-tuple-element.31.refs_1_), channel_id=1, source_target_pairs={{0,2},{2,0},{1,3},{3,1},{4,6},{6,4},{5,7},{7,5},{8,10},{10,8},{9,1... | collective-permute-start | bytes 1572872 | tf_op jit(solution)/shard_map/ppermute | solution.py:384
  28.1 8.2 %collective-permute-start.4 = (bf16[64,2048]{1,0:T(8,128)(2,1)S(1)}, bf16[64,2048]{1,0:T(8,128)(2,1)S(1)}, u32[]{:S(2)}, u32[]{:S(2)}) collective-permute-start(bf16[64,2048]{1,0:T(8,128)(2,1)S(1)} %get-tuple-element.38.refs_3_), channel_id=1, source_target_pairs={{0,4},{4,0},{8,12},{12,8},{1,5},{5,1},{9,13},{13,9},{2,6},{6,2},{1... | collective-permute-start | bytes 786440 | tf_op jit(solution)/shard_map/ppermute | solution.py:360
  29.7 23.3 %collective-permute-start.10 = (bf16[128,1024]{1,0:T(8,128)(2,1)S(1)}, bf16[128,1024]{1,0:T(8,128)(2,1)S(1)}, u32[]{:S(2)}, u32[]{:S(2)}) collective-permute-start(bf16[128,1024]{1,0:T(8,128)(2,1)S(1)} %get-tuple-element.32.refs_2_), channel_id=1, source_target_pairs={{0,2},{2,0},{1,3},{3,1},{4,6},{6,4},{5,7},{7,5},{8,10},{10,8},{9,1... | collective-permute-start | bytes 786440 | tf_op jit(solution)/shard_map/ppermute | solution.py:384
  36.3 2.8 %copy-start.2 = (s32[4096]{0:T(1024)S(1)}, s32[4096]{0:T(1024)}, u32[]{:S(2)}) copy-start(s32[4096]{0:T(1024)} %param.6) | copy-start | bytes 49156
  36.4 10.8 %collective-permute-start.5 = (bf16[32,2048]{1,0:T(8,128)(2,1)S(1)}, bf16[32,2048]{1,0:T(8,128)(2,1)S(1)}, u32[]{:S(2)}, u32[]{:S(2)}) collective-permute-start(bf16[32,2048]{1,0:T(8,128)(2,1)S(1)} %get-tuple-element.41.refs_3_), channel_id=1, source_target_pairs={{0,8},{4,12},{8,0},{12,4},{1,9},{5,13},{9,1},{13,5},{2,10},{6,14},... | collective-permute-start | bytes 393224 | tf_op jit(solution)/shard_map/ppermute | solution.py:360
  39.1 8.1 %copy-start.1 = (f32[128,128]{1,0:T(8,128)S(1)}, f32[128,128]{1,0:T(8,128)}, u32[]{:S(2)}) copy-start(f32[128,128]{1,0:T(8,128)} %constant.7.clone.rotation_ref) | copy-start | bytes 196612
  48.2 10.0 %collective-permute-start.7 = (bf16[32,2176]{1,0:T(8,128)(2,1)S(1)}, bf16[32,2176]{1,0:T(8,128)(2,1)S(1)}, u32[]{:S(2)}, u32[]{:S(2)}) collective-permute-start(bf16[32,2176]{1,0:T(8,128)(2,1)S(1)} %shard_map.66.refs_3_.refs_0_), channel_id=1, source_target_pairs={{0,4},{4,0},{8,12},{12,8},{1,5},{5,1},{9,13},{13,9},{2,6},{6,2},{1... | collective-permute-start | bytes 417800 | tf_op jit(solution)/shard_map/ppermute | solution.py:360
  50.4 7.8 %collective-permute-start.8 = (bf16[32,2176]{1,0:T(8,128)(2,1)S(1)}, bf16[32,2176]{1,0:T(8,128)(2,1)S(1)}, u32[]{:S(2)}, u32[]{:S(2)}) collective-permute-start(bf16[32,2176]{1,0:T(8,128)(2,1)S(1)} %shard_map.66.refs_3_.refs_0_), channel_id=1, source_target_pairs={{0,8},{4,12},{8,0},{12,4},{1,9},{5,13},{9,1},{13,5},{2,10},{6,14},... | collective-permute-start | bytes 417800 | tf_op jit(solution)/shard_map/ppermute | solution.py:360
  55.6 3.2 %collective-permute-start.11 = (bf16[128,1024]{1,0:T(8,128)(2,1)S(1)}, bf16[128,1024]{1,0:T(8,128)(2,1)S(1)}, u32[]{:S(2)}, u32[]{:S(2)}) collective-permute-start(bf16[128,1024]{1,0:T(8,128)(2,1)S(1)} %get-tuple-element.43.refs_3_), channel_id=1, source_target_pairs={{0,1},{1,0},{2,3},{3,2},{4,5},{5,4},{6,7},{7,6},{8,9},{9,8},{10,11... | collective-permute-start | bytes 786440 | tf_op jit(solution)/shard_map/ppermute | solution.py:357
  58.3 1.7 %collective-permute-start.13 = (bf16[128,1024]{1,0:T(8,128)(2,1)S(1)}, bf16[128,1024]{1,0:T(8,128)(2,1)S(1)}, u32[]{:S(2)}, u32[]{:S(2)}) collective-permute-start(bf16[128,1024]{1,0:T(8,128)(2,1)S(1)} %shard_map.70), channel_id=1, source_target_pairs={{0,1},{1,0},{2,3},{3,2},{4,5},{5,4},{6,7},{7,6},{8,9},{9,8},{10,11... | collective-permute-start | bytes 786440 | tf_op jit(solution)/shard_map/ppermute | solution.py:357
  58.9 6.4 %collective-permute-start.12 = (bf16[64,1024]{1,0:T(8,128)(2,1)S(1)}, bf16[64,1024]{1,0:T(8,128)(2,1)S(1)}, u32[]{:S(2)}, u32[]{:S(2)}) collective-permute-start(bf16[64,1024]{1,0:T(8,128)(2,1)S(1)} %get-tuple-element.45), channel_id=1, source_target_pairs={{0,4},{4,0},{8,12},{12,8},{1,5},{5,1},{9,13},{13,9},{2,6},{6,2},{1... | collective-permute-start | bytes 393224 | tf_op jit(solution)/shard_map/ppermute | solution.py:360
  60.0 8.8 %collective-permute-start.15 = (bf16[64,1024]{1,0:T(8,128)(2,1)S(1)}, bf16[64,1024]{1,0:T(8,128)(2,1)S(1)}, u32[]{:S(2)}, u32[]{:S(2)}) collective-permute-start(bf16[64,1024]{1,0:T(8,128)(2,1)S(1)} %get-tuple-element.48.refs_2_), channel_id=1, source_target_pairs={{0,4},{4,0},{8,12},{12,8},{1,5},{5,1},{9,13},{13,9},{2,6},{6,2},{1... | collective-permute-start | bytes 393224 | tf_op jit(solution)/shard_map/ppermute | solution.py:360
  61.1 10.9 %collective-permute-start.9 = (bf16[32,2176]{1,0:T(8,128)(2,1)S(1)}, bf16[32,2176]{1,0:T(8,128)(2,1)S(1)}, u32[]{:S(2)}, u32[]{:S(2)}) collective-permute-start(bf16[32,2176]{1,0:T(8,128)(2,1)S(1)} %collective-permute-done.8.refs_2_), channel_id=1, source_target_pairs={{0,4},{4,0},{8,12},{12,8},{1,5},{5,1},{9,13},{13,9},{2,6},{6,2},{1... | collective-permute-start | bytes 417800 | tf_op jit(solution)/shard_map/ppermute | solution.py:360
  65.3 8.6 %collective-permute-start.14 = (bf16[32,1024]{1,0:T(8,128)(2,1)S(1)}, bf16[32,1024]{1,0:T(8,128)(2,1)S(1)}, u32[]{:S(2)}, u32[]{:S(2)}) collective-permute-start(bf16[32,1024]{1,0:T(8,128)(2,1)S(1)} %get-tuple-element.50), channel_id=1, source_target_pairs={{0,8},{4,12},{8,0},{12,4},{1,9},{5,13},{9,1},{13,5},{2,10},{6,14},... | collective-permute-start | bytes 196616 | tf_op jit(solution)/shard_map/ppermute | solution.py:360
  68.9 6.4 %collective-permute-start.19 = (bf16[32,1024]{1,0:T(8,128)(2,1)S(1)}, bf16[32,1024]{1,0:T(8,128)(2,1)S(1)}, u32[]{:S(2)}, u32[]{:S(2)}) collective-permute-start(bf16[32,1024]{1,0:T(8,128)(2,1)S(1)} %get-tuple-element.52.refs_0_), channel_id=1, source_target_pairs={{0,8},{4,12},{8,0},{12,4},{1,9},{5,13},{9,1},{13,5},{2,10},{6,14},... | collective-permute-start | bytes 196616 | tf_op jit(solution)/shard_map/ppermute | solution.py:360
  74.6 7.1 %collective-permute-start.17 = (bf16[32,1152]{1,0:T(8,128)(2,1)S(1)}, bf16[32,1152]{1,0:T(8,128)(2,1)S(1)}, u32[]{:S(2)}, u32[]{:S(2)}) collective-permute-start(bf16[32,1152]{1,0:T(8,128)(2,1)S(1)} %shard_map.74.refs_4_), channel_id=1, source_target_pairs={{0,8},{4,12},{8,0},{12,4},{1,9},{5,13},{9,1},{13,5},{2,10},{6,14},... | collective-permute-start | bytes 221192 | tf_op jit(solution)/shard_map/ppermute | solution.py:360
  75.9 7.8 %collective-permute-start.21 = (bf16[32,1152]{1,0:T(8,128)(2,1)S(1)}, bf16[32,1152]{1,0:T(8,128)(2,1)S(1)}, u32[]{:S(2)}, u32[]{:S(2)}) collective-permute-start(bf16[32,1152]{1,0:T(8,128)(2,1)S(1)} %shard_map.76.refs_4_), channel_id=1, source_target_pairs={{0,8},{4,12},{8,0},{12,4},{1,9},{5,13},{9,1},{13,5},{2,10},{6,14},... | collective-permute-start | bytes 221192 | tf_op jit(solution)/shard_map/ppermute | solution.py:360
  78.3 5.8 %collective-permute-start.16 = (bf16[32,1152]{1,0:T(8,128)(2,1)S(1)}, bf16[32,1152]{1,0:T(8,128)(2,1)S(1)}, u32[]{:S(2)}, u32[]{:S(2)}) collective-permute-start(bf16[32,1152]{1,0:T(8,128)(2,1)S(1)} %shard_map.74.refs_4_), channel_id=1, source_target_pairs={{0,4},{4,0},{8,12},{12,8},{1,5},{5,1},{9,13},{13,9},{2,6},{6,2},{1... | collective-permute-start | bytes 221192 | tf_op jit(solution)/shard_map/ppermute | solution.py:360
  81.7 4.4 %collective-permute-start.18 = (bf16[32,1152]{1,0:T(8,128)(2,1)S(1)}, bf16[32,1152]{1,0:T(8,128)(2,1)S(1)}, u32[]{:S(2)}, u32[]{:S(2)}) collective-permute-start(bf16[32,1152]{1,0:T(8,128)(2,1)S(1)} %collective-permute-done.17.refs_6_), channel_id=1, source_target_pairs={{0,4},{4,0},{8,12},{12,8},{1,5},{5,1},{9,13},{13,9},{2,6},{6,2},{1... | collective-permute-start | bytes 221192 | tf_op jit(solution)/shard_map/ppermute | solution.py:360
  81.7 5.1 %collective-permute-start.20 = (bf16[32,1152]{1,0:T(8,128)(2,1)S(1)}, bf16[32,1152]{1,0:T(8,128)(2,1)S(1)}, u32[]{:S(2)}, u32[]{:S(2)}) collective-permute-start(bf16[32,1152]{1,0:T(8,128)(2,1)S(1)} %shard_map.76.refs_4_), channel_id=1, source_target_pairs={{0,4},{4,0},{8,12},{12,8},{1,5},{5,1},{9,13},{13,9},{2,6},{6,2},{1... | collective-permute-start | bytes 221192 | tf_op jit(solution)/shard_map/ppermute | solution.py:360
  83.7 4.4 %collective-permute-start.22 = (bf16[32,1152]{1,0:T(8,128)(2,1)S(1)}, bf16[32,1152]{1,0:T(8,128)(2,1)S(1)}, u32[]{:S(2)}, u32[]{:S(2)}) collective-permute-start(bf16[32,1152]{1,0:T(8,128)(2,1)S(1)} %collective-permute-done.21.refs_6_), channel_id=1, source_target_pairs={{0,4},{4,0},{8,12},{12,8},{1,5},{5,1},{9,13},{13,9},{2,6},{6,2},{1... | collective-permute-start | bytes 221192 | tf_op jit(solution)/shard_map/ppermute | solution.py:360
  86.1 2.3 %collective-permute-start.23 = (bf16[128,1152]{1,0:T(8,128)(2,1)S(1)}, bf16[128,1152]{1,0:T(8,128)(2,1)S(1)}, u32[]{:S(2)}, u32[]{:S(2)}) collective-permute-start(bf16[128,1152]{1,0:T(8,128)(2,1)S(1)} %shard_map.78), channel_id=1, source_target_pairs={{0,1},{1,0},{2,3},{3,2},{4,5},{5,4},{6,7},{7,6},{8,9},{9,8},{10,11... | collective-permute-start | bytes 884744 | tf_op jit(solution)/shard_map/ppermute | solution.py:357
  88.1 1.6 %collective-permute-start.24 = (bf16[128,1152]{1,0:T(8,128)(2,1)S(1)}, bf16[128,1152]{1,0:T(8,128)(2,1)S(1)}, u32[]{:S(2)}, u32[]{:S(2)}) collective-permute-start(bf16[128,1152]{1,0:T(8,128)(2,1)S(1)} %shard_map.79), channel_id=1, source_target_pairs={{0,1},{1,0},{2,3},{3,2},{4,5},{5,4},{6,7},{7,6},{8,9},{9,8},{10,11... | collective-permute-start | bytes 884744 | tf_op jit(solution)/shard_map/ppermute | solution.py:357

commit v11 on v10

--- a/solution.py
+++ b/solution.py
@@ -13,7 +13,7 @@
 UNIT = 512
 GROUPS = 2
 VMEM_LIMIT = 6 * 2**20
-SHARES = (4, 3, 4)
+SHARES = (4, 4, 3)
 epsilon = 1e-06
 
 SMALL = pl.CostEstimate(flops=1, bytes_accessed=1, transcendentals=0)
@@ -201,37 +201,47 @@
     )(*kept, *came, *tokens)
 
 
-def encode_body(begin, kept_ref, came_ref, flips_ref, rotation_ref, *refs):
-    out_ref = refs[-1]
+def encode_body(begin, lane, last, kept_ref, came_ref, scales_ref, flips_ref, rotation_ref, *refs):
     rows, columns = kept_ref.shape
     half = flips_ref.shape[1] // 2
     rotation = rotation_ref[...]
-    lane = lax.broadcasted_iota(jnp.int32, (rows, BLOCK), 1)
-    scales = jnp.zeros((rows, BLOCK), jnp.float32)
+    lanes = lax.broadcasted_iota(jnp.int32, (rows, BLOCK), 1)
+    scales = scales_ref[...]
     for block in range(columns // BLOCK):
         at = slice(block * BLOCK, (block + 1) * BLOCK)
-        flips = flips_ref[:, pl.ds(pl.multiple_of(lax.axis_index("sub") * half + begin + block * BLOCK, BLOCK), BLOCK)]
+        place = lax.axis_index("sub") * half + begin + block * BLOCK
+        flips = flips_ref[:, pl.ds(pl.multiple_of(place, BLOCK), BLOCK)]
         total = (kept_ref[:, at] + came_ref[:, at].astype(jnp.float32)) * flips
         rotated = jnp.dot(
             total, rotation, precision=lax.Precision.HIGHEST, preferred_element_type=jnp.float32
         )
         largest = jnp.max(jnp.abs(rotated), axis=1, keepdims=True)
         scale = (largest + epsilon).astype(jnp.bfloat16).astype(jnp.float32)
-        out_ref[:, at] = (rotated / scale).astype(jnp.bfloat16)
-        scales = jnp.where(lane == block, scale, scales)
-    out_ref[:, columns:] = scales.astype(jnp.bfloat16)
-
-
-def encode(kept, came, begin, flips, rotation, tokens=()):
+        refs[-1 if last else -2][:, at] = (rotated / scale).astype(jnp.bfloat16)
+        scales = jnp.where(lanes == lane + block, scale, scales)
+    if last:
+        refs[-1][:, columns:] = scales.astype(jnp.bfloat16)
+    else:
+        refs[-1][...] = scales
+
+
+def encode(kept, came, begin, scales, lane, last, flips, rotation, tokens=()):
     rows, columns = kept.shape
-    return pl.pallas_call(
-        functools.partial(encode_body, begin),
-        out_shape=jax.ShapeDtypeStruct((rows, columns + BLOCK), jnp.bfloat16),
-        in_specs=[VMEM] * 4 + [ANY] * len(tokens),
-        out_specs=VMEM,
-        compiler_params=PARAMS,
-        cost_estimate=SMALL,
-    )(kept, came, flips, rotation, *tokens)
+    if last:
+        out_shape = [jax.ShapeDtypeStruct((rows, columns + BLOCK), jnp.bfloat16)]
+    else:
+        out_shape = [
+            jax.ShapeDtypeStruct((rows, columns), jnp.bfloat16),
+            jax.ShapeDtypeStruct((rows, BLOCK), jnp.float32),
+        ]
+    return pl.pallas_call(
+        functools.partial(encode_body, begin, lane, last),
+        out_shape=out_shape,
+        in_specs=[VMEM] * 5 + [ANY] * len(tokens),
+        out_specs=[VMEM] * len(out_shape),
+        compiler_params=PARAMS,
+        cost_estimate=SMALL,
+    )(kept, came, scales, flips, rotation, *tokens)
 
 
 def rank_of(index, count):
@@ -245,92 +255,107 @@
     return lax.rem(lax.axis_index("seq") - (sub * places + place) + blocks, blocks)
 
 
-def choose_body(blocks, pieces, width, at, other, places, *refs):
+def choose_body(blocks, count, width, begins, other, places, scales, *refs):
     out_ref = refs[-1]
     rows = refs[0].shape[0]
-    scales = width // BLOCK
 
     def put(block, place):
-        begin, scale_at = at[block]
-        for piece in range(pieces):
-            ref = refs[block * pieces + piece]
-            row = (place * pieces + rank_of(lax.axis_index("tensor") ^ piece, pieces)) * rows
+        for piece in range(count):
+            row = (place * count + rank_of(lax.axis_index("tensor") ^ piece, count)) * rows
             here = pl.ds(pl.multiple_of(row, rows), rows)
-            out_ref[here, :width] = ref[:, begin : begin + width]
-            out_ref[here, width : width + scales] = ref[:, scale_at : scale_at + scales]
+            begin = begins[block]
+            out_ref[here, :width] = refs[block * count + piece][:, begin : begin + width]
+            if scales:
+                ref = refs[blocks * count + piece]
+                at = ref.shape[1] - BLOCK + block * scales
+                out_ref[here, width : width + scales] = ref[:, at : at + scales]
 
     for place in range(places):
         for block in range(blocks):
             pl.when(block_of(other, place, places, blocks) == block)(functools.partial(put, block, place))
 
 
-def choose(results, group, width, other, places):
-    picked, at = [], []
-    for result in results:
-        if len(result) == 1:
-            pieces, begin = result[0], group * width
-            at.append((begin, pieces[0].shape[1] - BLOCK + begin // BLOCK))
-        else:
-            pieces = result[group]
-            at.append((0, width))
-        picked.append(pieces)
-    rows = picked[0][0].shape[0]
-    count = len(picked[0])
+def choose(results, group, width, other, places, scales, tokens):
+    picked = [result[0] if len(result) == 1 else result[group] for result in results]
+    begins = [group * width if len(result) == 1 else 0 for result in results]
+    last = results[-1][-1] if scales else []
+    rows, count = picked[0][0].shape[0], len(picked[0])
+    columns = width + (BLOCK if scales else 0)
     if rows % 16:
         blocks = []
-        for pieces, (begin, scale_at) in zip(picked, at):
-            block = jnp.zeros((count * rows, width + BLOCK), jnp.bfloat16)
+        for block, (pieces, begin) in enumerate(zip(picked, begins)):
+            held = jnp.zeros((count * rows, columns), jnp.bfloat16)
             for index, piece in enumerate(pieces):
-                scale = jnp.pad(piece[:, scale_at : scale_at + width // BLOCK], ((0, 0), (0, BLOCK - width // BLOCK)))
-                part = jnp.concatenate([piece[:, begin : begin + width], scale], axis=1)
-                block = lax.dynamic_update_slice_in_dim(block, part, rank_of(lax.axis_index("tensor") ^ index, count) * rows, 0)
-            blocks.append(block)
+                part = piece[:, begin : begin + width]
+                if scales:
+                    at = last[index].shape[1] - BLOCK + block * scales
+                    scale = jnp.pad(last[index][:, at : at + scales], ((0, 0), (0, BLOCK - scales)))
+                    part = jnp.concatenate([part, scale], axis=1)
+                row = rank_of(lax.axis_index("tensor") ^ index, count) * rows
+                held = lax.dynamic_update_slice_in_dim(held, part, row, 0)
+            blocks.append(held)
         stacked = jnp.stack(blocks)
         return jnp.concatenate([stacked[block_of(other, place, places, len(blocks))] for place in range(places)])
-    return pl.pallas_call(
-        functools.partial(choose_body, len(picked), count, width, at, other, places),
-        out_shape=jax.ShapeDtypeStruct((places * count * rows, width + BLOCK), jnp.bfloat16),
-        in_specs=[VMEM] * (len(picked) * count),
+    operands = [piece for pieces in picked for piece in pieces] + last
+    return pl.pallas_call(
+        functools.partial(choose_body, len(picked), count, width, begins, other, places, scales),
+        out_shape=jax.ShapeDtypeStruct((places * count * rows, columns), jnp.bfloat16),
+        in_specs=[VMEM] * len(operands) + [ANY] * len(tokens),
         out_specs=VMEM,
         compiler_params=PARAMS,
         cost_estimate=SMALL,
-    )(*[piece for pieces in picked for piece in pieces])
-
-
-def assemble_body(groups, half, *refs):
-    mine, other = refs[:groups], refs[groups : 2 * groups]
-    codes_ref, scales_ref = refs[2 * groups :]
-    width = half // groups
-    scales = width // BLOCK
+    )(*operands, *tokens)
+
+
+def place_body(mine, half, widths, groups, scales, held, *refs):
+    refs = refs[held:]
+    codes_ref, sems = refs[-3] if scales else refs[-2], refs[-1]
+    sub = lax.axis_index("sub")
+    side = sub if mine else 1 - sub
+
+    def copies(core):
+        return [
+            pltpu.make_async_copy(
+                ref.at[:, :width], codes_ref.at[:, pl.ds(core * half + group * width, width)], sems.at[index]
+            )
+            for index, (ref, width, group) in enumerate(zip(refs, widths, groups))
+        ]
 
     def put(core):
-        held = []
-        for side, side_refs in ((core, mine), (1 - core, other)):
-            for group, ref in enumerate(side_refs):
-                begin = side * half + group * width
-                codes_ref[:, begin : begin + width] = ref[:, :width]
-                held.append((begin, ref[:, width : width + scales].astype(jnp.float32)))
-        held = jnp.concatenate([value for _, value in sorted(held, key=lambda pair: pair[0])], axis=1)
-        scales_ref[...] = held.T.astype(jnp.bfloat16)
+        for copy in copies(core):
+            copy.start()
+        if scales:
+            pair = [ref[:, width : width + scales] for ref, width in ((refs[len(widths)], widths[-1]), (refs[len(widths) - 1], widths[-1]))]
+            pair = pair if core == 1 else pair[::-1]
+            held = jnp.concatenate([value.astype(jnp.float32) for value in pair], axis=1)
+            refs[-2][...] = held.T.astype(jnp.bfloat16)
+        for copy in copies(core):
+            copy.wait()
 
     for core in range(2):
-        pl.when(lax.axis_index("sub") == core)(functools.partial(put, core))
-
-
-def assemble(mine, other, half):
-    rows = mine[0].shape[0]
-    codes, scales = pl.pallas_call(
-        functools.partial(assemble_body, len(mine), half),
-        out_shape=(
-            jax.ShapeDtypeStruct((rows, 2 * half), jnp.bfloat16),
-            jax.ShapeDtypeStruct((2 * half // BLOCK, rows), jnp.bfloat16),
-        ),
-        in_specs=[VMEM] * (2 * len(mine)),
-        out_specs=(VMEM, VMEM),
-        compiler_params=PARAMS,
-        cost_estimate=SMALL,
-    )(*mine, *other)
-    return codes, scales.T
+        pl.when(side == core)(functools.partial(put, core))
+
+
+def put_codes(arrays, groups, width, half, mine, codes=None, scales_of=None):
+    rows = arrays[0].shape[0]
+    scales = half // BLOCK if scales_of is not None else 0
+    operands = list(arrays) + ([scales_of] if scales else [])
+    out_shape = [jax.ShapeDtypeStruct((rows, 2 * half), jnp.bfloat16)]
+    out_specs = [HBM]
+    if scales:
+        out_shape.append(jax.ShapeDtypeStruct((2 * scales, rows), jnp.bfloat16))
+        out_specs.append(VMEM)
+    held = [] if codes is None else [codes]
+    return pl.pallas_call(
+        functools.partial(place_body, mine, half, [width] * len(arrays), groups, scales, len(held)),
+        out_shape=out_shape,
+        in_specs=[HBM] * len(held) + [VMEM] * len(operands),
+        out_specs=out_specs,
+        input_output_aliases={0: 0} if held else {},
+        scratch_shapes=[pltpu.SemaphoreType.DMA((len(arrays),))],
+        compiler_params=PARAMS,
+        cost_estimate=SMALL,
+    )(*held, *operands)
 
 
 def cut(depth):
@@ -359,14 +384,18 @@
     def exchange(values, level):
         return lax.ppermute(values, "tensor", [(t, t ^ 1 << level) for t in range(tensor_count)])
 
-    def reduce(halves, begin):
+    def reduce(halves, begin, block, last):
         tokens = (yield None) or []
         kept, came = halves[1::2], [swap(sent) for sent in halves[::2]]
         for level in range(levels):
             sent, held = halve(kept, came, level, tokens)
             tokens = (yield sent) or []
             kept, came = [held], [exchange(sent, level)]
-        yield encode(kept[0], came[0], begin, flips, rotation, tokens)
+        packed, *rest = encode(
+            kept[0], came[0], begin, scales[-1], (block * half + begin) // BLOCK, last, flips, rotation, tokens
+        )
+        scales.extend(rest)
+        yield packed
 
     def spread(packed):
         pieces = {0: packed}
@@ -375,6 +404,7 @@
                 pieces[index ^ 1 << level] = exchange(pieces[index], level)
         return [pieces[index] for index in range(tensor_count)]
 
+    scales = [jnp.zeros((hidden.shape[0] // tensor_count, BLOCK), jnp.float32)]
     sizes = cut(depth)
     places = [sum(sizes[:index]) for index in range(len(sizes))]
     parts = slices_of(hidden, list(zip(places, sizes)))
@@ -385,17 +415,17 @@
 
     if len(sizes) == 1:
         outs = multiply([[parts[0]], [arrivals[0][0]]], down_weight, 0, [None, None], [True, True], wide_chunk)
-        reduced = [list(reduce(outs[:2], 0))[-1], list(reduce(outs[2:], 0))[-1]]
-        for arrived in arrivals[1:]:
+        reduced = [list(reduce(outs[:2], 0, 0, False))[-1], list(reduce(outs[2:], 0, 1, seq_count == 2))[-1]]
+        for block, arrived in enumerate(arrivals[1:], 2):
             outs = multiply([[arrived[0]]], down_weight, 0, [None], [True], wide_chunk)
-            reduced.append(list(reduce(outs, 0))[-1])
+            reduced.append(list(reduce(outs, 0, block, block == seq_count - 1))[-1])
         results = [[spread(packed)] for packed in reduced]
     else:
         (own,) = multiply([parts[1:]], down_weight, sizes[0], [None], [False], wide, tokens=parts[:1])
         *halves, total = multiply(
             [[parts[0]], [arrivals[0][0]]], down_weight, 0, [own, None], [True, False], wide_chunk, groups=GROUPS
         )
-        own_steps = reduce(halves, 0)
+        own_steps = reduce(halves, 0, 0, False)
         next(own_steps)
         tokens = [own_steps.send([arrivals[0][1]])]
         results = []
@@ -409,7 +439,7 @@
                 if not results:
                     step = own_steps.send([total])
                     tokens = [step]
-                    if step.shape[1] > half:
+                    if step.shape[0] * tensor_count == hidden.shape[0] and len(scales) > 1:
                         results.append([spread(step)])
             if not results:
                 results.append([spread(list(own_steps)[-1])])
@@ -422,16 +452,18 @@
                 tokens = [sent]
                 if group == GROUPS - 1 and shift == 0 and levels > 1:
                     sent = gate(sent, [results[0][0][1], results[0][0][1 << levels - 1]])
-                all_steps.append(reduce([sent, kept], group * half // GROUPS))
+                all_steps.append(reduce([sent, kept], group * half // GROUPS, shift + 1, shift == seq_count - 2 and group == GROUPS - 1))
                 next(all_steps[-1])
             last = []
             for level in range(levels + 1):
                 for group, steps in enumerate(all_steps):
                     wait = list(last) if group == 0 else []
-                    if group == 0 and level == levels and shift == 0:
+                    if group == GROUPS - 1 and level == levels and shift == 0:
                         wait += results[0][0][1:]
                     step = steps.send(wait)
                     if level == levels:
+                        if remote and levels > 1:
+                            step = gate(step, [remote[-1][1], remote[-1][1 << levels - 1]])
                         remote.append(spread(step))
                 last = [step]
             results.append(remote)
@@ -439,9 +471,20 @@
 
     groups = max(len(result) for result in results)
     width = half // groups
-    other = [swap(choose(results, group, width, True, per_sub)) for group in range(groups)]
-    mine = [choose(results, group, width, False, per_sub) for group in range(groups)]
-    return assemble(mine, other, half)
+    last = groups - 1
+
+    def chosen(group, other, tokens):
+        return choose(results, group, width, other, per_sub, half // BLOCK if group == last else 0, tokens)
+
+    came = []
+    for group in range(groups):
+        came.append(swap(chosen(group, True, came[-1:])))
+    mine = [chosen(group, False, []) for group in range(groups)]
+    (codes,) = put_codes(mine, list(range(groups)), width, half, True)
+    if last:
+        (codes,) = put_codes(came[:last], list(range(last)), width, half, False, codes)
+    codes, flat = put_codes(came[last:], [last], width, half, False, codes, mine[last])
+    return codes, flat.T
 
 
 def solution(mesh):

time: 91 us -> 101 us (1.11)
  starting transfers between devices: 24.8 us -> 29.6 us
  waiting for transfers between devices: 22.8 us -> 26.6 us
  Pallas kernels: 40.9 us -> 42.6 us
    ppermute x15, starting transfers between devices: 17 us -> 23.2 us  [exchange(): lax.ppermute(values, 'tensor', [(t, t ^ 1 << level) for t in range(tensor...]
    ppermute x15, waiting for transfers between devices: 19.3 us -> 23.3 us  [exchange(): lax.ppermute(values, 'tensor', [(t, t ^ 1 << level) for t in range(tensor...]
    ppermute x6, waiting for transfers between devices: 1.97 us -> 0.02 us  [swap(): return lax.ppermute(values, 'sub', [(0, 1), (1, 0)])]
    pallas_call x4 -> x6, Pallas kernels: 3.37 us -> 5.13 us  [the longest x3 2.88 us: put_codes(): pl.pallas_call(functools.partial(place_body, mine, half, [width] * len(ar...]
    ppermute x4, waiting for transfers between devices: 1.59 us -> 3.22 us  [shards(): arrivals.append([lax.ppermute(part, 'seq', pairs) for part in parts])]
    ppermute x4, starting transfers between devices: 6.46 us -> 5.11 us  [shards(): arrivals.append([lax.ppermute(part, 'seq', pairs) for part in parts])]
  transfers between devices with their start and end apart: 25 -> 25, of which waited for: 13 -> 10; matrix products, arithmetic and copies ran while one was open for 0% -> 0% of each run, Pallas kernels for 44% -> 40%
where the time goes in v11:
time: 101 us
  Pallas kernels  42.6 us (42%)
  starting transfers between devices  29.6 us (29%)
  waiting for transfers between devices  26.6 us (26%)
  local copies, waits for them, and re-layouts  1.46 us (1%)
    pallas_call x6, Pallas kernels, multiply(): pl.pallas_call(body, out_shape=out_shape, in_specs=[VMEM] * spans[-1][1]...  36.8 us
    ppermute x15, waiting for transfers between devices, exchange(): lax.ppermute(values, 'tensor', [(t, t ^ 1 << level) for t in range(tensor...  23.3 us
    ppermute x15, starting transfers between devices, exchange(): lax.ppermute(values, 'tensor', [(t, t ^ 1 << level) for t in range(tensor...  23.2 us
    ppermute x4, starting transfers between devices, shards(): arrivals.append([lax.ppermute(part, 'seq', pairs) for part in parts])  5.11 us
    ppermute x4, waiting for transfers between devices, shards(): arrivals.append([lax.ppermute(part, 'seq', pairs) for part in parts])  3.22 us
    pallas_call x3, Pallas kernels, put_codes(): pl.pallas_call(functools.partial(place_body, mine, half, [width] * len(ar...  2.88 us
    pallas_call x3, Pallas kernels, encode(): pl.pallas_call(functools.partial(encode_body, begin, lane, last), out_sha...  2.25 us
  transfers between devices with their start and end apart: 25, of which 10 were waited for; matrix products, arithmetic and copies ran while one was open for 0% of the time, Pallas kernels for 40%

profile of v11, /device:TPU:0, one launch (start us, length us, event | category | flops | bytes accessed | tf_op | source)
XLA Modules:
  0.0 101.2 jit_solution(5067701165614933473)
XLA Ops:
  0.6 1.4 %copy-done = bf16[128,6656]{1,0:T(8,128)(2,1)S(1)} copy-done((bf16[128,6656]{1,0:T(8,128)(2,1)S(1)}, bf16[128,6656]{1,0:T(8,128)(2,1)}, u32[]{:S(2)}) %copy-start) | copy-done | bytes 1703960
  2.1 0.2 shard_map.59
  2.2 3.0 %collective-permute-start = (bf16[128,2048]{1,0:T(8,128)(2,1)S(1)}, bf16[128,2048]{1,0:T(8,128)(2,1)S(1)}, u32[]{:S(2)}, u32[]{:S(2)}) collective-permute-start(bf16[128,2048]{1,0:T(8,128)(2,1)S(1)} %get-tuple-element.33.refs_4_.refs_0_), channel_id=1, source_target_pairs={{0,2},{2,0},{1,3},{3,1},{4,6},{6,4},{5,7},{7,5},{8,10},{10,8},{9,1... | collective-permute-start | bytes 1572872 | tf_op jit(solution)/shard_map/ppermute | solution.py:414
  5.3 0.1 collective-permute-start.3
  5.3 12.7 %shard_map.60.refs_3_ = f32[128,4096]{1,0:T(8,128)S(1)} custom-call(bf16[128,2048]{1,0:T(8,128)(2,1)S(1)} %get-tuple-element.34.refs_0_, bf16[128,1536]{1,0:T(8,128)(2,1)S(1)} %get-tuple-element.35.refs_1_, bf16[128,1024]{1,0:T(8,128)(2,1)S(1)} %get-tuple-element.36.refs_2_, bf16[6656,4096]{1,0:T(8,128)(2,1)} %refs_1_.7, ...), custom_call_target="tpu_custom_call" | custom-call | flops 1 | bytes 1 | tf_op jit(solution)/shard_map/pallas_call | solution.py:139
  18.0 7.3 %shard_map.61 = (bf16[128,1024]{1,0:T(8,128)(2,1)S(1)}, f32[128,1024]{1,0:T(8,128)S(1)}, bf16[128,1024]{1,0:T(8,128)(2,1)S(1)}, f32[128,1024]{1,0:T(8,128)S(1)}, f32[128,4096]{1,0:T(8,128)S(1)}) custom-call(bf16[128,2048]{1,0:T(8,128)(2,1)S(1)} %get-tuple-element.33.refs_4_.refs_0_, bf16[128,2048]{1,0:T(8,128)(2,1)S(1)} %collective-permute-done.refs_1_, ...), custom_call_target="tpu_custom_call" | custom-call | flops 1 | bytes 1 | tf_op jit(solution)/shard_map/pallas_call | solution.py:139
  25.4 0.1 collective-permute-start.1
  25.5 0.5 collective-permute-start.2
  26.0 2.5 %collective-permute-done.3.refs_4_.refs_0_ = bf16[128,2048]{1,0:T(8,128)(2,1)S(1)} collective-permute-done((bf16[128,2048]{1,0:T(8,128)(2,1)S(1)}, bf16[128,2048]{1,0:T(8,128)(2,1)S(1)}, u32[]{:S(2)}, u32[]{:S(2)}) %collective-permute-start.3) | collective-permute-done | bytes 524320 | tf_op jit(solution)/shard_map/ppermute | solution.py:414
  28.4 0.1 shard_map.62
  28.5 1.9 %collective-permute-start.4 = (bf16[64,2048]{1,0:T(8,128)(2,1)S(1)}, bf16[64,2048]{1,0:T(8,128)(2,1)S(1)}, u32[]{:S(2)}, u32[]{:S(2)}) collective-permute-start(bf16[64,2048]{1,0:T(8,128)(2,1)S(1)} %get-tuple-element.42.refs_3_), channel_id=1, source_target_pairs={{0,4},{4,0},{8,12},{12,8},{1,5},{5,1},{9,13},{13,9},{2,6},{6,2},{1... | collective-permute-start | bytes 786440 | tf_op jit(solution)/shard_map/ppermute | solution.py:385
  30.4 1.5 %collective-permute-start.6 = (bf16[128,1536]{1,0:T(8,128)(2,1)S(1)}, bf16[128,1536]{1,0:T(8,128)(2,1)S(1)}, u32[]{:S(2)}, u32[]{:S(2)}) collective-permute-start(bf16[128,1536]{1,0:T(8,128)(2,1)S(1)} %get-tuple-element.35.refs_1_), channel_id=1, source_target_pairs={{0,2},{2,0},{1,3},{3,1},{4,6},{6,4},{5,7},{7,5},{8,10},{10,8},{9,1... | collective-permute-start | bytes 1179656 | tf_op jit(solution)/shard_map/ppermute | solution.py:414
  31.9 0.5 collective-permute-start.10
  32.4 6.5 %shard_map.63.refs_2_ = f32[128,4096]{1,0:T(8,128)S(1)} custom-call(bf16[128,2048]{1,0:T(8,128)(2,1)S(1)} %collective-permute-done.3.refs_4_.refs_0_, bf16[6656,4096]{1,0:T(8,128)(2,1)} %refs_1_.7, f32[128,4096]{1,0:T(8,128)S(1)} %get-tuple-element.43.refs_2_, bf16[64,2048]{1,0:T(8,128)(2,1)S(1)} %get-tuple-element.42.refs_3_), custom_call_target="tpu_custom_call" | custom-call | flops 1 | bytes 1 | tf_op jit(solution)/shard_map/pallas_call | solution.py:139
  39.0 2.7 %collective-permute-start.5 = (bf16[32,2048]{1,0:T(8,128)(2,1)S(1)}, bf16[32,2048]{1,0:T(8,128)(2,1)S(1)}, u32[]{:S(2)}, u32[]{:S(2)}) collective-permute-start(bf16[32,2048]{1,0:T(8,128)(2,1)S(1)} %get-tuple-element.45.refs_3_), channel_id=1, source_target_pairs={{0,8},{4,12},{8,0},{12,4},{1,9},{5,13},{9,1},{13,5},{2,10},{6,14},... | collective-permute-start | bytes 393224 | tf_op jit(solution)/shard_map/ppermute | solution.py:385
  41.7 0.8 collective-permute-done.6.refs_0_
  42.5 5.2 %shard_map.65.refs_0_.refs_2_ = f32[128,4096]{1,0:T(8,128)S(1)} custom-call(bf16[128,1536]{1,0:T(8,128)(2,1)S(1)} %collective-permute-done.6.refs_0_, bf16[6656,4096]{1,0:T(8,128)(2,1)} %refs_1_.7, f32[128,4096]{1,0:T(8,128)S(1)} %shard_map.63.refs_2_, bf16[32,2048]{1,0:T(8,128)(2,1)S(1)} %get-tuple-element.45.refs_3_), custom_call_target="tpu_custom_call" | custom-call | flops 1 | bytes 1 | tf_op jit(solution)/shard_map/pallas_call | solution.py:139
  47.6 1.0 %shard_map.66 = (bf16[32,2048]{1,0:T(8,128)(2,1)S(1)}, f32[32,128]{1,0:T(8,128)S(1)}) custom-call(f32[32,2048]{1,0:T(8,128)S(1)} %get-tuple-element.44.kept_ref, bf16[32,2048]{1,0:T(8,128)(2,1)S(1)} %collective-permute-done.5.came_ref, f32[32,128]{1,0:T(8,128)S(1)} %broadcast_in_dim.6.scales_ref, f32[1,4096]{1,0:T(1,128)S(1)} %bitcast.2, ...), custom_call_target="tpu_custom_call" | custom-call | flops 1 | bytes 1 | tf_op jit(solution)/shard_map/pallas_call | solution.py:237
  48.7 0.3 collective-permute-start.7
  49.0 2.8 %collective-permute-start.8 = (bf16[32,2048]{1,0:T(8,128)(2,1)S(1)}, bf16[32,2048]{1,0:T(8,128)(2,1)S(1)}, u32[]{:S(2)}, u32[]{:S(2)}) collective-permute-start(bf16[32,2048]{1,0:T(8,128)(2,1)S(1)} %get-tuple-element.46.refs_3_.refs_0_), channel_id=1, source_target_pairs={{0,8},{4,12},{8,0},{12,4},{1,9},{5,13},{9,1},{13,5},{2,10},{6,14},... | collective-permute-start | bytes 393224 | tf_op jit(solution)/shard_map/ppermute | solution.py:385
  51.8 2.5 %shard_map.67 = (bf16[128,1024]{1,0:T(8,128)(2,1)S(1)}, f32[128,1024]{1,0:T(8,128)S(1)}) custom-call(bf16[128,1024]{1,0:T(8,128)(2,1)S(1)} %collective-permute-done.10.refs_0_, bf16[6656,4096]{1,0:T(8,128)(2,1)} %refs_1_.7, f32[128,4096]{1,0:T(8,128)S(1)} %shard_map.65.refs_0_.refs_2_, bf16[32,2048]{1,0:T(8,128)(2,1)S(1)} %get-tuple-element.46.refs_3_.refs_0_), custom_call_target="tpu_custom_call" | custom-call | flops 1 | bytes 1 | tf_op jit(solution)/shard_map/pallas_call | solution.py:139
  54.3 0.1 collective-permute-start.11
  54.4 2.6 %shard_map.69 = (bf16[128,1024]{1,0:T(8,128)(2,1)S(1)}, f32[128,1024]{1,0:T(8,128)S(1)}) custom-call(bf16[128,1024]{1,0:T(8,128)(2,1)S(1)} %collective-permute-done.10.refs_0_, bf16[6656,4096]{1,0:T(8,128)(2,1)} %refs_1_.7, f32[128,4096]{1,0:T(8,128)S(1)} %shard_map.65.refs_0_.refs_2_, bf16[128,1024]{1,0:T(8,128)(2,1)S(1)} %get-tuple-element.48.refs_3_), custom_call_target="tpu_custom_call" | custom-call | flops 1 | bytes 1 | tf_op jit(solution)/shard_map/pallas_call | solution.py:139
  57.0 0.5 collective-permute-start.13
  57.6 1.6 %collective-permute-start.12 = (bf16[64,1024]{1,0:T(8,128)(2,1)S(1)}, bf16[64,1024]{1,0:T(8,128)(2,1)S(1)}, u32[]{:S(2)}, u32[]{:S(2)}) collective-permute-start(bf16[64,1024]{1,0:T(8,128)(2,1)S(1)} %get-tuple-element.50), channel_id=1, source_target_pairs={{0,4},{4,0},{8,12},{12,8},{1,5},{5,1},{9,13},{13,9},{2,6},{6,2},{1... | collective-permute-start | bytes 393224 | tf_op jit(solution)/shard_map/ppermute | solution.py:385
  59.3 1.1 %collective-permute-start.15 = (bf16[64,1024]{1,0:T(8,128)(2,1)S(1)}, bf16[64,1024]{1,0:T(8,128)(2,1)S(1)}, u32[]{:S(2)}, u32[]{:S(2)}) collective-permute-start(bf16[64,1024]{1,0:T(8,128)(2,1)S(1)} %get-tuple-element.53.refs_2_), channel_id=1, source_target_pairs={{0,4},{4,0},{8,12},{12,8},{1,5},{5,1},{9,13},{13,9},{2,6},{6,2},{1... | collective-permute-start | bytes 393224 | tf_op jit(solution)/shard_map/ppermute | solution.py:385
  60.4 3.6 %collective-permute-done.12.refs_1_ = bf16[64,1024]{1,0:T(8,128)(2,1)S(1)} collective-permute-done((bf16[64,1024]{1,0:T(8,128)(2,1)S(1)}, bf16[64,1024]{1,0:T(8,128)(2,1)S(1)}, u32[]{:S(2)}, u32[]{:S(2)}) %collective-permute-start.12) | collective-permute-done | bytes 131104 | tf_op jit(solution)/shard_map/ppermute | solution.py:385
  64.1 1.0 %collective-permute-start.14 = (bf16[32,1024]{1,0:T(8,128)(2,1)S(1)}, bf16[32,1024]{1,0:T(8,128)(2,1)S(1)}, u32[]{:S(2)}, u32[]{:S(2)}) collective-permute-start(bf16[32,1024]{1,0:T(8,128)(2,1)S(1)} %get-tuple-element.55), channel_id=1, source_target_pairs={{0,8},{4,12},{8,0},{12,4},{1,9},{5,13},{9,1},{13,5},{2,10},{6,14},... | collective-permute-start | bytes 196616 | tf_op jit(solution)/shard_map/ppermute | solution.py:385
  65.1 1.9 %collective-permute-start.9 = (bf16[32,2048]{1,0:T(8,128)(2,1)S(1)}, bf16[32,2048]{1,0:T(8,128)(2,1)S(1)}, u32[]{:S(2)}, u32[]{:S(2)}) collective-permute-start(bf16[32,2048]{1,0:T(8,128)(2,1)S(1)} %collective-permute-done.8.refs_2_.refs_1_), channel_id=1, source_target_pairs={{0,4},{4,0},{8,12},{12,8},{1,5},{5,1},{9,13},{13,9},{2,6},{6,2},{1... | collective-permute-start | bytes 393224 | tf_op jit(solution)/shard_map/ppermute | solution.py:385
  67.1 2.3 %collective-permute-done.14.came_ref = bf16[32,1024]{1,0:T(8,128)(2,1)S(1)} collective-permute-done((bf16[32,1024]{1,0:T(8,128)(2,1)S(1)}, bf16[32,1024]{1,0:T(8,128)(2,1)S(1)}, u32[]{:S(2)}, u32[]{:S(2)}) %collective-permute-start.14) | collective-permute-done | bytes 65568 | tf_op jit(solution)/shard_map/ppermute | solution.py:385
  69.4 0.6 shard_map.74
  70.0 1.7 %collective-permute-start.17 = (bf16[32,1024]{1,0:T(8,128)(2,1)S(1)}, bf16[32,1024]{1,0:T(8,128)(2,1)S(1)}, u32[]{:S(2)}, u32[]{:S(2)}) collective-permute-start(bf16[32,1024]{1,0:T(8,128)(2,1)S(1)} %get-tuple-element.59.refs_4_), channel_id=1, source_target_pairs={{0,8},{4,12},{8,0},{12,4},{1,9},{5,13},{9,1},{13,5},{2,10},{6,14},... | collective-permute-start | bytes 196616 | tf_op jit(solution)/shard_map/ppermute | solution.py:385
  71.7 1.7 %collective-permute-start.16 = (bf16[32,1024]{1,0:T(8,128)(2,1)S(1)}, bf16[32,1024]{1,0:T(8,128)(2,1)S(1)}, u32[]{:S(2)}, u32[]{:S(2)}) collective-permute-start(bf16[32,1024]{1,0:T(8,128)(2,1)S(1)} %get-tuple-element.59.refs_4_), channel_id=1, source_target_pairs={{0,4},{4,0},{8,12},{12,8},{1,5},{5,1},{9,13},{13,9},{2,6},{6,2},{1... | collective-permute-start | bytes 196616 | tf_op jit(solution)/shard_map/ppermute | solution.py:385
  73.4 2.0 %collective-permute-done.17.refs_6_.refs_2_ = bf16[32,1024]{1,0:T(8,128)(2,1)S(1)} collective-permute-done((bf16[32,1024]{1,0:T(8,128)(2,1)S(1)}, bf16[32,1024]{1,0:T(8,128)(2,1)S(1)}, u32[]{:S(2)}, u32[]{:S(2)}) %collective-permute-start.17) | collective-permute-done | bytes 65568 | tf_op jit(solution)/shard_map/ppermute | solution.py:385
  75.3 1.4 %collective-permute-start.18 = (bf16[32,1024]{1,0:T(8,128)(2,1)S(1)}, bf16[32,1024]{1,0:T(8,128)(2,1)S(1)}, u32[]{:S(2)}, u32[]{:S(2)}) collective-permute-start(bf16[32,1024]{1,0:T(8,128)(2,1)S(1)} %collective-permute-done.17.refs_6_.refs_2_), channel_id=1, source_target_pairs={{0,4},{4,0},{8,12},{12,8},{1,5},{5,1},{9,13},{13,9},{2,6},{6,2},{1... | collective-permute-start | bytes 196616 | tf_op jit(solution)/shard_map/ppermute | solution.py:385
  76.8 2.9 %collective-permute-done.18.refs_7_ = bf16[32,1024]{1,0:T(8,128)(2,1)S(1)} collective-permute-done((bf16[32,1024]{1,0:T(8,128)(2,1)S(1)}, bf16[32,1024]{1,0:T(8,128)(2,1)S(1)}, u32[]{:S(2)}, u32[]{:S(2)}) %collective-permute-start.18) | collective-permute-done | bytes 65568 | tf_op jit(solution)/shard_map/ppermute | solution.py:385
  79.7 1.8 %collective-permute-start.19 = (bf16[32,1024]{1,0:T(8,128)(2,1)S(1)}, bf16[32,1024]{1,0:T(8,128)(2,1)S(1)}, u32[]{:S(2)}, u32[]{:S(2)}) collective-permute-start(bf16[32,1024]{1,0:T(8,128)(2,1)S(1)} %get-tuple-element.58.refs_0_), channel_id=1, source_target_pairs={{0,8},{4,12},{8,0},{12,4},{1,9},{5,13},{9,1},{13,5},{2,10},{6,14},... | collective-permute-start | bytes 196616 | tf_op jit(solution)/shard_map/ppermute | solution.py:385
  81.5 5.0 %collective-permute-done.19.came_ref = bf16[32,1024]{1,0:T(8,128)(2,1)S(1)} collective-permute-done((bf16[32,1024]{1,0:T(8,128)(2,1)S(1)}, bf16[32,1024]{1,0:T(8,128)(2,1)S(1)}, u32[]{:S(2)}, u32[]{:S(2)}) %collective-permute-start.19) | collective-permute-done | bytes 65568 | tf_op jit(solution)/shard_map/ppermute | solution.py:385
  86.5 0.6 shard_map.76.refs_0_
  87.2 0.5 collective-permute-start.21
  87.6 2.8 %collective-permute-start.20 = (bf16[32,1152]{1,0:T(8,128)(2,1)S(1)}, bf16[32,1152]{1,0:T(8,128)(2,1)S(1)}, u32[]{:S(2)}, u32[]{:S(2)}) collective-permute-start(bf16[32,1152]{1,0:T(8,128)(2,1)S(1)} %shard_map.77.refs_4_.refs_8_), channel_id=1, source_target_pairs={{0,4},{4,0},{8,12},{12,8},{1,5},{5,1},{9,13},{13,9},{2,6},{6,2},{1... | collective-permute-start | bytes 221192 | tf_op jit(solution)/shard_map/ppermute | solution.py:385
  90.4 3.2 %collective-permute-done.21.refs_6_.refs_10_ = bf16[32,1152]{1,0:T(8,128)(2,1)S(1)} collective-permute-done((bf16[32,1152]{1,0:T(8,128)(2,1)S(1)}, bf16[32,1152]{1,0:T(8,128)(2,1)S(1)}, u32[]{:S(2)}, u32[]{:S(2)}) %collective-permute-start.21) | collective-permute-done | bytes 73760 | tf_op jit(solution)/shard_map/ppermute | solution.py:385
  93.6 0.2 collective-permute-done.20.refs_5_.refs_9_
  93.8 4.2 %collective-permute-done.22.refs_7_.refs_11_ = bf16[32,1152]{1,0:T(8,128)(2,1)S(1)} collective-permute-done((bf16[32,1152]{1,0:T(8,128)(2,1)S(1)}, bf16[32,1152]{1,0:T(8,128)(2,1)S(1)}, u32[]{:S(2)}, u32[]{:S(2)}) %collective-permute-start.22) | collective-permute-done | bytes 73760 | tf_op jit(solution)/shard_map/ppermute | solution.py:385
  98.0 0.1 shard_map.82
  98.3 0.8 shard_map.79.refs_0_
  99.1 0.7 shard_map.81.refs_0_
  99.8 1.3 %shard_map.83 = (bf16[128,4096]{1,0:T(8,128)(2,1)}, bf16[32,128]{1,0:T(8,128)(2,1)}) custom-call(bf16[128,4096]{1,0:T(8,128)(2,1)} %shard_map.81.refs_0_, bf16[128,1152]{1,0:T(8,128)(2,1)S(1)} %collective-permute-done.24.refs_1_, bf16[128,1152]{1,0:T(8,128)(2,1)S(1)} %shard_map.78.refs_1_.refs_2_), custom_call_target="tpu_custom_call", output_to_operand_aliasing={{0}: (0, {})} | custom-call | flops 1 | bytes 1 | tf_op jit(solution)/shard_map/pallas_call | solution.py:349
  (35 shorter events, 0.5 us)
Async XLA Ops:
  0.6 1.5 %copy-start = (bf16[128,6656]{1,0:T(8,128)(2,1)S(1)}, bf16[128,6656]{1,0:T(8,128)(2,1)}, u32[]{:S(2)}) copy-start(bf16[128,6656]{1,0:T(8,128)(2,1)} %in_ref.1) | copy-start | bytes 5111812
  2.2 15.8 %collective-permute-start = (bf16[128,2048]{1,0:T(8,128)(2,1)S(1)}, bf16[128,2048]{1,0:T(8,128)(2,1)S(1)}, u32[]{:S(2)}, u32[]{:S(2)}) collective-permute-start(bf16[128,2048]{1,0:T(8,128)(2,1)S(1)} %get-tuple-element.33.refs_4_.refs_0_), channel_id=1, source_target_pairs={{0,2},{2,0},{1,3},{3,1},{4,6},{6,4},{5,7},{7,5},{8,10},{10,8},{9,1... | collective-permute-start | bytes 1572872 | tf_op jit(solution)/shard_map/ppermute | solution.py:414
  5.3 23.2 %collective-permute-start.3 = (bf16[128,2048]{1,0:T(8,128)(2,1)S(1)}, bf16[128,2048]{1,0:T(8,128)(2,1)S(1)}, u32[]{:S(2)}, u32[]{:S(2)}) collective-permute-start(bf16[128,2048]{1,0:T(8,128)(2,1)S(1)} %get-tuple-element.34.refs_0_), channel_id=1, source_target_pairs={{0,2},{2,0},{1,3},{3,1},{4,6},{6,4},{5,7},{7,5},{8,10},{10,8},{9,1... | collective-permute-start | bytes 1572872 | tf_op jit(solution)/shard_map/ppermute | solution.py:414
  25.4 3.0 %collective-permute-start.1 = (bf16[128,1024]{1,0:T(8,128)(2,1)S(1)}, bf16[128,1024]{1,0:T(8,128)(2,1)S(1)}, u32[]{:S(2)}, u32[]{:S(2)}) collective-permute-start(bf16[128,1024]{1,0:T(8,128)(2,1)S(1)} %get-tuple-element.39), channel_id=1, source_target_pairs={{0,1},{1,0},{2,3},{3,2},{4,5},{5,4},{6,7},{7,6},{8,9},{9,8},{10,11... | collective-permute-start | bytes 786440 | tf_op jit(solution)/shard_map/ppermute | solution.py:382
  25.5 3.0 %collective-permute-start.2 = (bf16[128,1024]{1,0:T(8,128)(2,1)S(1)}, bf16[128,1024]{1,0:T(8,128)(2,1)S(1)}, u32[]{:S(2)}, u32[]{:S(2)}) collective-permute-start(bf16[128,1024]{1,0:T(8,128)(2,1)S(1)} %get-tuple-element.40), channel_id=1, source_target_pairs={{0,1},{1,0},{2,3},{3,2},{4,5},{5,4},{6,7},{7,6},{8,9},{9,8},{10,11... | collective-permute-start | bytes 786440 | tf_op jit(solution)/shard_map/ppermute | solution.py:382
  28.5 10.4 %collective-permute-start.4 = (bf16[64,2048]{1,0:T(8,128)(2,1)S(1)}, bf16[64,2048]{1,0:T(8,128)(2,1)S(1)}, u32[]{:S(2)}, u32[]{:S(2)}) collective-permute-start(bf16[64,2048]{1,0:T(8,128)(2,1)S(1)} %get-tuple-element.42.refs_3_), channel_id=1, source_target_pairs={{0,4},{4,0},{8,12},{12,8},{1,5},{5,1},{9,13},{13,9},{2,6},{6,2},{1... | collective-permute-start | bytes 786440 | tf_op jit(solution)/shard_map/ppermute | solution.py:385
  30.4 12.1 %collective-permute-start.6 = (bf16[128,1536]{1,0:T(8,128)(2,1)S(1)}, bf16[128,1536]{1,0:T(8,128)(2,1)S(1)}, u32[]{:S(2)}, u32[]{:S(2)}) collective-permute-start(bf16[128,1536]{1,0:T(8,128)(2,1)S(1)} %get-tuple-element.35.refs_1_), channel_id=1, source_target_pairs={{0,2},{2,0},{1,3},{3,1},{4,6},{6,4},{5,7},{7,5},{8,10},{10,8},{9,1... | collective-permute-start | bytes 1179656 | tf_op jit(solution)/shard_map/ppermute | solution.py:414
  31.9 19.9 %collective-permute-start.10 = (bf16[128,1024]{1,0:T(8,128)(2,1)S(1)}, bf16[128,1024]{1,0:T(8,128)(2,1)S(1)}, u32[]{:S(2)}, u32[]{:S(2)}) collective-permute-start(bf16[128,1024]{1,0:T(8,128)(2,1)S(1)} %get-tuple-element.36.refs_2_), channel_id=1, source_target_pairs={{0,2},{2,0},{1,3},{3,1},{4,6},{6,4},{5,7},{7,5},{8,10},{10,8},{9,1... | collective-permute-start | bytes 786440 | tf_op jit(solution)/shard_map/ppermute | solution.py:414
  38.9 2.7 %copy-start.2 = (s32[4096]{0:T(1024)S(1)}, s32[4096]{0:T(1024)}, u32[]{:S(2)}) copy-start(s32[4096]{0:T(1024)} %param.6) | copy-start | bytes 49156
  39.0 8.6 %collective-permute-start.5 = (bf16[32,2048]{1,0:T(8,128)(2,1)S(1)}, bf16[32,2048]{1,0:T(8,128)(2,1)S(1)}, u32[]{:S(2)}, u32[]{:S(2)}) collective-permute-start(bf16[32,2048]{1,0:T(8,128)(2,1)S(1)} %get-tuple-element.45.refs_3_), channel_id=1, source_target_pairs={{0,8},{4,12},{8,0},{12,4},{1,9},{5,13},{9,1},{13,5},{2,10},{6,14},... | collective-permute-start | bytes 393224 | tf_op jit(solution)/shard_map/ppermute | solution.py:385
  41.7 6.0 %copy-start.1 = (f32[128,128]{1,0:T(8,128)S(1)}, f32[128,128]{1,0:T(8,128)}, u32[]{:S(2)}) copy-start(f32[128,128]{1,0:T(8,128)} %constant.9.clone.rotation_ref) | copy-start | bytes 196612
  48.7 8.3 %collective-permute-start.7 = (bf16[32,2048]{1,0:T(8,128)(2,1)S(1)}, bf16[32,2048]{1,0:T(8,128)(2,1)S(1)}, u32[]{:S(2)}, u32[]{:S(2)}) collective-permute-start(bf16[32,2048]{1,0:T(8,128)(2,1)S(1)} %get-tuple-element.46.refs_3_.refs_0_), channel_id=1, source_target_pairs={{0,4},{4,0},{8,12},{12,8},{1,5},{5,1},{9,13},{13,9},{2,6},{6,2},{1... | collective-permute-start | bytes 393224 | tf_op jit(solution)/shard_map/ppermute | solution.py:385
  49.0 8.0 %collective-permute-start.8 = (bf16[32,2048]{1,0:T(8,128)(2,1)S(1)}, bf16[32,2048]{1,0:T(8,128)(2,1)S(1)}, u32[]{:S(2)}, u32[]{:S(2)}) collective-permute-start(bf16[32,2048]{1,0:T(8,128)(2,1)S(1)} %get-tuple-element.46.refs_3_.refs_0_), channel_id=1, source_target_pairs={{0,8},{4,12},{8,0},{12,4},{1,9},{5,13},{9,1},{13,5},{2,10},{6,14},... | collective-permute-start | bytes 393224 | tf_op jit(solution)/shard_map/ppermute | solution.py:385
  54.3 3.2 %collective-permute-start.11 = (bf16[128,1024]{1,0:T(8,128)(2,1)S(1)}, bf16[128,1024]{1,0:T(8,128)(2,1)S(1)}, u32[]{:S(2)}, u32[]{:S(2)}) collective-permute-start(bf16[128,1024]{1,0:T(8,128)(2,1)S(1)} %get-tuple-element.48.refs_3_), channel_id=1, source_target_pairs={{0,1},{1,0},{2,3},{3,2},{4,5},{5,4},{6,7},{7,6},{8,9},{9,8},{10,11... | collective-permute-start | bytes 786440 | tf_op jit(solution)/shard_map/ppermute | solution.py:382
  57.0 2.2 %collective-permute-start.13 = (bf16[128,1024]{1,0:T(8,128)(2,1)S(1)}, bf16[128,1024]{1,0:T(8,128)(2,1)S(1)}, u32[]{:S(2)}, u32[]{:S(2)}) collective-permute-start(bf16[128,1024]{1,0:T(8,128)(2,1)S(1)} %shard_map.70), channel_id=1, source_target_pairs={{0,1},{1,0},{2,3},{3,2},{4,5},{5,4},{6,7},{7,6},{8,9},{9,8},{10,11... | collective-permute-start | bytes 786440 | tf_op jit(solution)/shard_map/ppermute | solution.py:382
  57.6 6.4 %collective-permute-start.12 = (bf16[64,1024]{1,0:T(8,128)(2,1)S(1)}, bf16[64,1024]{1,0:T(8,128)(2,1)S(1)}, u32[]{:S(2)}, u32[]{:S(2)}) collective-permute-start(bf16[64,1024]{1,0:T(8,128)(2,1)S(1)} %get-tuple-element.50), channel_id=1, source_target_pairs={{0,4},{4,0},{8,12},{12,8},{1,5},{5,1},{9,13},{13,9},{2,6},{6,2},{1... | collective-permute-start | bytes 393224 | tf_op jit(solution)/shard_map/ppermute | solution.py:385
  59.3 7.7 %collective-permute-start.15 = (bf16[64,1024]{1,0:T(8,128)(2,1)S(1)}, bf16[64,1024]{1,0:T(8,128)(2,1)S(1)}, u32[]{:S(2)}, u32[]{:S(2)}) collective-permute-start(bf16[64,1024]{1,0:T(8,128)(2,1)S(1)} %get-tuple-element.53.refs_2_), channel_id=1, source_target_pairs={{0,4},{4,0},{8,12},{12,8},{1,5},{5,1},{9,13},{13,9},{2,6},{6,2},{1... | collective-permute-start | bytes 393224 | tf_op jit(solution)/shard_map/ppermute | solution.py:385
  64.1 5.3 %collective-permute-start.14 = (bf16[32,1024]{1,0:T(8,128)(2,1)S(1)}, bf16[32,1024]{1,0:T(8,128)(2,1)S(1)}, u32[]{:S(2)}, u32[]{:S(2)}) collective-permute-start(bf16[32,1024]{1,0:T(8,128)(2,1)S(1)} %get-tuple-element.55), channel_id=1, source_target_pairs={{0,8},{4,12},{8,0},{12,4},{1,9},{5,13},{9,1},{13,5},{2,10},{6,14},... | collective-permute-start | bytes 196616 | tf_op jit(solution)/shard_map/ppermute | solution.py:385
  65.1 11.6 %collective-permute-start.9 = (bf16[32,2048]{1,0:T(8,128)(2,1)S(1)}, bf16[32,2048]{1,0:T(8,128)(2,1)S(1)}, u32[]{:S(2)}, u32[]{:S(2)}) collective-permute-start(bf16[32,2048]{1,0:T(8,128)(2,1)S(1)} %collective-permute-done.8.refs_2_.refs_1_), channel_id=1, source_target_pairs={{0,4},{4,0},{8,12},{12,8},{1,5},{5,1},{9,13},{13,9},{2,6},{6,2},{1... | collective-permute-start | bytes 393224 | tf_op jit(solution)/shard_map/ppermute | solution.py:385
  70.0 5.3 %collective-permute-start.17 = (bf16[32,1024]{1,0:T(8,128)(2,1)S(1)}, bf16[32,1024]{1,0:T(8,128)(2,1)S(1)}, u32[]{:S(2)}, u32[]{:S(2)}) collective-permute-start(bf16[32,1024]{1,0:T(8,128)(2,1)S(1)} %get-tuple-element.59.refs_4_), channel_id=1, source_target_pairs={{0,8},{4,12},{8,0},{12,4},{1,9},{5,13},{9,1},{13,5},{2,10},{6,14},... | collective-permute-start | bytes 196616 | tf_op jit(solution)/shard_map/ppermute | solution.py:385
  71.7 5.1 %collective-permute-start.16 = (bf16[32,1024]{1,0:T(8,128)(2,1)S(1)}, bf16[32,1024]{1,0:T(8,128)(2,1)S(1)}, u32[]{:S(2)}, u32[]{:S(2)}) collective-permute-start(bf16[32,1024]{1,0:T(8,128)(2,1)S(1)} %get-tuple-element.59.refs_4_), channel_id=1, source_target_pairs={{0,4},{4,0},{8,12},{12,8},{1,5},{5,1},{9,13},{13,9},{2,6},{6,2},{1... | collective-permute-start | bytes 196616 | tf_op jit(solution)/shard_map/ppermute | solution.py:385
  75.3 4.3 %collective-permute-start.18 = (bf16[32,1024]{1,0:T(8,128)(2,1)S(1)}, bf16[32,1024]{1,0:T(8,128)(2,1)S(1)}, u32[]{:S(2)}, u32[]{:S(2)}) collective-permute-start(bf16[32,1024]{1,0:T(8,128)(2,1)S(1)} %collective-permute-done.17.refs_6_.refs_2_), channel_id=1, source_target_pairs={{0,4},{4,0},{8,12},{12,8},{1,5},{5,1},{9,13},{13,9},{2,6},{6,2},{1... | collective-permute-start | bytes 196616 | tf_op jit(solution)/shard_map/ppermute | solution.py:385
  79.6 18.4 %collective-permute-start.23 = (bf16[128,1024]{1,0:T(8,128)(2,1)S(1)}, bf16[128,1024]{1,0:T(8,128)(2,1)S(1)}, u32[]{:S(2)}, u32[]{:S(2)}) collective-permute-start(bf16[128,1024]{1,0:T(8,128)(2,1)S(1)} %shard_map.80), channel_id=1, source_target_pairs={{0,1},{1,0},{2,3},{3,2},{4,5},{5,4},{6,7},{7,6},{8,9},{9,8},{10,11... | collective-permute-start | bytes 786440 | tf_op jit(solution)/shard_map/ppermute | solution.py:382
  79.7 6.8 %collective-permute-start.19 = (bf16[32,1024]{1,0:T(8,128)(2,1)S(1)}, bf16[32,1024]{1,0:T(8,128)(2,1)S(1)}, u32[]{:S(2)}, u32[]{:S(2)}) collective-permute-start(bf16[32,1024]{1,0:T(8,128)(2,1)S(1)} %get-tuple-element.58.refs_0_), channel_id=1, source_target_pairs={{0,8},{4,12},{8,0},{12,4},{1,9},{5,13},{9,1},{13,5},{2,10},{6,14},... | collective-permute-start | bytes 196616 | tf_op jit(solution)/shard_map/ppermute | solution.py:385
  87.2 6.5 %collective-permute-start.21 = (bf16[32,1152]{1,0:T(8,128)(2,1)S(1)}, bf16[32,1152]{1,0:T(8,128)(2,1)S(1)}, u32[]{:S(2)}, u32[]{:S(2)}) collective-permute-start(bf16[32,1152]{1,0:T(8,128)(2,1)S(1)} %shard_map.77.refs_4_.refs_8_), channel_id=1, source_target_pairs={{0,8},{4,12},{8,0},{12,4},{1,9},{5,13},{9,1},{13,5},{2,10},{6,14},... | collective-permute-start | bytes 221192 | tf_op jit(solution)/shard_map/ppermute | solution.py:385
  87.6 6.2 %collective-permute-start.20 = (bf16[32,1152]{1,0:T(8,128)(2,1)S(1)}, bf16[32,1152]{1,0:T(8,128)(2,1)S(1)}, u32[]{:S(2)}, u32[]{:S(2)}) collective-permute-start(bf16[32,1152]{1,0:T(8,128)(2,1)S(1)} %shard_map.77.refs_4_.refs_8_), channel_id=1, source_target_pairs={{0,4},{4,0},{8,12},{12,8},{1,5},{5,1},{9,13},{13,9},{2,6},{6,2},{1... | collective-permute-start | bytes 221192 | tf_op jit(solution)/shard_map/ppermute | solution.py:385
  93.6 4.4 %collective-permute-start.22 = (bf16[32,1152]{1,0:T(8,128)(2,1)S(1)}, bf16[32,1152]{1,0:T(8,128)(2,1)S(1)}, u32[]{:S(2)}, u32[]{:S(2)}) collective-permute-start(bf16[32,1152]{1,0:T(8,128)(2,1)S(1)} %collective-permute-done.21.refs_6_.refs_10_), channel_id=1, source_target_pairs={{0,4},{4,0},{8,12},{12,8},{1,5},{5,1},{9,13},{13,9},{2,6},{6,2},{1... | collective-permute-start | bytes 221192 | tf_op jit(solution)/shard_map/ppermute | solution.py:385
  98.1 1.7 %collective-permute-start.24 = (bf16[128,1152]{1,0:T(8,128)(2,1)S(1)}, bf16[128,1152]{1,0:T(8,128)(2,1)S(1)}, u32[]{:S(2)}, u32[]{:S(2)}) collective-permute-start(bf16[128,1152]{1,0:T(8,128)(2,1)S(1)} %shard_map.82), channel_id=1, source_target_pairs={{0,1},{1,0},{2,3},{3,2},{4,5},{5,4},{6,7},{7,6},{8,9},{9,8},{10,11... | collective-permute-start | bytes 884744 | tf_op jit(solution)/shard_map/ppermute | solution.py:382

commit v12 on v11

--- a/solution.py
+++ b/solution.py
@@ -202,6 +202,7 @@
 
 
 def encode_body(begin, lane, last, kept_ref, came_ref, scales_ref, flips_ref, rotation_ref, *refs):
+    out_ref = refs[-1 if last else -2]
     rows, columns = kept_ref.shape
     half = flips_ref.shape[1] // 2
     rotation = rotation_ref[...]
@@ -217,23 +218,19 @@
         )
         largest = jnp.max(jnp.abs(rotated), axis=1, keepdims=True)
         scale = (largest + epsilon).astype(jnp.bfloat16).astype(jnp.float32)
-        refs[-1 if last else -2][:, at] = (rotated / scale).astype(jnp.bfloat16)
+        out_ref[:, at] = (rotated / scale).astype(jnp.bfloat16)
         scales = jnp.where(lanes == lane + block, scale, scales)
     if last:
-        refs[-1][:, columns:] = scales.astype(jnp.bfloat16)
+        out_ref[:, columns:] = scales.astype(jnp.bfloat16)
     else:
         refs[-1][...] = scales
 
 
 def encode(kept, came, begin, scales, lane, last, flips, rotation, tokens=()):
     rows, columns = kept.shape
-    if last:
-        out_shape = [jax.ShapeDtypeStruct((rows, columns + BLOCK), jnp.bfloat16)]
-    else:
-        out_shape = [
-            jax.ShapeDtypeStruct((rows, columns), jnp.bfloat16),
-            jax.ShapeDtypeStruct((rows, BLOCK), jnp.float32),
-        ]
+    out_shape = [jax.ShapeDtypeStruct((rows, columns + (BLOCK if last else 0)), jnp.bfloat16)]
+    if not last:
+        out_shape.append(jax.ShapeDtypeStruct((rows, BLOCK), jnp.float32))
     return pl.pallas_call(
         functools.partial(encode_body, begin, lane, last),
         out_shape=out_shape,
@@ -255,7 +252,7 @@
     return lax.rem(lax.axis_index("seq") - (sub * places + place) + blocks, blocks)
 
 
-def choose_body(blocks, count, width, begins, other, places, scales, *refs):
+def choose_body(blocks, count, width, begins, other, places, scales, lane, *refs):
     out_ref = refs[-1]
     rows = refs[0].shape[0]
 
@@ -265,70 +262,68 @@
             here = pl.ds(pl.multiple_of(row, rows), rows)
             begin = begins[block]
             out_ref[here, :width] = refs[block * count + piece][:, begin : begin + width]
-            if scales:
-                ref = refs[blocks * count + piece]
-                at = ref.shape[1] - BLOCK + block * scales
-                out_ref[here, width : width + scales] = ref[:, at : at + scales]
+            ref = refs[(blocks - 1) * count + piece]
+            at = ref.shape[1] - BLOCK + block * scales + lane
+            out_ref[here, width : width + width // BLOCK] = ref[:, at : at + width // BLOCK]
 
     for place in range(places):
         for block in range(blocks):
             pl.when(block_of(other, place, places, blocks) == block)(functools.partial(put, block, place))
 
 
-def choose(results, group, width, other, places, scales, tokens):
+def choose(results, group, width, other, places, scales):
     picked = [result[0] if len(result) == 1 else result[group] for result in results]
     begins = [group * width if len(result) == 1 else 0 for result in results]
-    last = results[-1][-1] if scales else []
+    lane = group * (width // BLOCK)
     rows, count = picked[0][0].shape[0], len(picked[0])
-    columns = width + (BLOCK if scales else 0)
+    columns = width + BLOCK
     if rows % 16:
         blocks = []
         for block, (pieces, begin) in enumerate(zip(picked, begins)):
             held = jnp.zeros((count * rows, columns), jnp.bfloat16)
             for index, piece in enumerate(pieces):
                 part = piece[:, begin : begin + width]
-                if scales:
-                    at = last[index].shape[1] - BLOCK + block * scales
-                    scale = jnp.pad(last[index][:, at : at + scales], ((0, 0), (0, BLOCK - scales)))
-                    part = jnp.concatenate([part, scale], axis=1)
+                at = picked[-1][index].shape[1] - BLOCK + block * scales + lane
+                scale = picked[-1][index][:, at : at + width // BLOCK]
+                part = jnp.concatenate([part, jnp.pad(scale, ((0, 0), (0, BLOCK - width // BLOCK)))], axis=1)
                 row = rank_of(lax.axis_index("tensor") ^ index, count) * rows
                 held = lax.dynamic_update_slice_in_dim(held, part, row, 0)
             blocks.append(held)
         stacked = jnp.stack(blocks)
         return jnp.concatenate([stacked[block_of(other, place, places, len(blocks))] for place in range(places)])
-    operands = [piece for pieces in picked for piece in pieces] + last
-    return pl.pallas_call(
-        functools.partial(choose_body, len(picked), count, width, begins, other, places, scales),
+    operands = [piece for pieces in picked for piece in pieces]
+    return pl.pallas_call(
+        functools.partial(choose_body, len(picked), count, width, begins, other, places, scales, lane),
         out_shape=jax.ShapeDtypeStruct((places * count * rows, columns), jnp.bfloat16),
-        in_specs=[VMEM] * len(operands) + [ANY] * len(tokens),
+        in_specs=[VMEM] * len(operands),
         out_specs=VMEM,
         compiler_params=PARAMS,
         cost_estimate=SMALL,
-    )(*operands, *tokens)
-
-
-def place_body(mine, half, widths, groups, scales, held, *refs):
+    )(*operands)
+
+
+def place_body(mine, half, width, count, held, *refs):
     refs = refs[held:]
-    codes_ref, sems = refs[-3] if scales else refs[-2], refs[-1]
+    scaled = len(refs) > count + 2
+    codes_ref, sems = refs[-3 if scaled else -2], refs[-1]
     sub = lax.axis_index("sub")
     side = sub if mine else 1 - sub
 
     def copies(core):
         return [
             pltpu.make_async_copy(
-                ref.at[:, :width], codes_ref.at[:, pl.ds(core * half + group * width, width)], sems.at[index]
+                refs[group].at[:, :width], codes_ref.at[:, pl.ds(core * half + group * width, width)], sems.at[group]
             )
-            for index, (ref, width, group) in enumerate(zip(refs, widths, groups))
+            for group in range(count)
         ]
 
     def put(core):
         for copy in copies(core):
             copy.start()
-        if scales:
-            pair = [ref[:, width : width + scales] for ref, width in ((refs[len(widths)], widths[-1]), (refs[len(widths) - 1], widths[-1]))]
-            pair = pair if core == 1 else pair[::-1]
-            held = jnp.concatenate([value.astype(jnp.float32) for value in pair], axis=1)
-            refs[-2][...] = held.T.astype(jnp.bfloat16)
+        if scaled:
+            order = refs[count : 2 * count] + refs[:count] if core else refs[: 2 * count]
+            scales = [ref[:, width : width + width // BLOCK].astype(jnp.float32) for ref in order]
+            refs[-2][...] = jnp.concatenate(scales, axis=1).T.astype(jnp.bfloat16)
         for copy in copies(core):
             copy.wait()
 
@@ -336,18 +331,17 @@
         pl.when(side == core)(functools.partial(put, core))
 
 
-def put_codes(arrays, groups, width, half, mine, codes=None, scales_of=None):
+def put_codes(arrays, width, half, mine, codes=None, mine_too=()):
     rows = arrays[0].shape[0]
-    scales = half // BLOCK if scales_of is not None else 0
-    operands = list(arrays) + ([scales_of] if scales else [])
+    operands = list(arrays) + list(mine_too)
     out_shape = [jax.ShapeDtypeStruct((rows, 2 * half), jnp.bfloat16)]
     out_specs = [HBM]
-    if scales:
-        out_shape.append(jax.ShapeDtypeStruct((2 * scales, rows), jnp.bfloat16))
+    if mine_too:
+        out_shape.append(jax.ShapeDtypeStruct((2 * half // BLOCK, rows), jnp.bfloat16))
         out_specs.append(VMEM)
     held = [] if codes is None else [codes]
     return pl.pallas_call(
-        functools.partial(place_body, mine, half, [width] * len(arrays), groups, scales, len(held)),
+        functools.partial(place_body, mine, half, width, len(arrays), len(held)),
         out_shape=out_shape,
         in_specs=[HBM] * len(held) + [VMEM] * len(operands),
         out_specs=out_specs,
@@ -384,17 +378,16 @@
     def exchange(values, level):
         return lax.ppermute(values, "tensor", [(t, t ^ 1 << level) for t in range(tensor_count)])
 
-    def reduce(halves, begin, block, last):
+    def reduce(halves, begin, block, base, last):
         tokens = (yield None) or []
         kept, came = halves[1::2], [swap(sent) for sent in halves[::2]]
         for level in range(levels):
             sent, held = halve(kept, came, level, tokens)
             tokens = (yield sent) or []
             kept, came = [held], [exchange(sent, level)]
-        packed, *rest = encode(
-            kept[0], came[0], begin, scales[-1], (block * half + begin) // BLOCK, last, flips, rotation, tokens
+        packed, *base[:] = encode(
+            kept[0], came[0], begin, base[0], (block * half + begin) // BLOCK, last, flips, rotation, tokens
         )
-        scales.extend(rest)
         yield packed
 
     def spread(packed):
@@ -404,7 +397,7 @@
                 pieces[index ^ 1 << level] = exchange(pieces[index], level)
         return [pieces[index] for index in range(tensor_count)]
 
-    scales = [jnp.zeros((hidden.shape[0] // tensor_count, BLOCK), jnp.float32)]
+    zeros = jnp.zeros((hidden.shape[0] // tensor_count, BLOCK), jnp.float32)
     sizes = cut(depth)
     places = [sum(sizes[:index]) for index in range(len(sizes))]
     parts = slices_of(hidden, list(zip(places, sizes)))
@@ -415,17 +408,19 @@
 
     if len(sizes) == 1:
         outs = multiply([[parts[0]], [arrivals[0][0]]], down_weight, 0, [None, None], [True, True], wide_chunk)
-        reduced = [list(reduce(outs[:2], 0, 0, False))[-1], list(reduce(outs[2:], 0, 1, seq_count == 2))[-1]]
+        base = [zeros]
+        reduced = [list(reduce(outs[:2], 0, 0, base, False))[-1], list(reduce(outs[2:], 0, 1, base, seq_count == 2))[-1]]
         for block, arrived in enumerate(arrivals[1:], 2):
             outs = multiply([[arrived[0]]], down_weight, 0, [None], [True], wide_chunk)
-            reduced.append(list(reduce(outs, 0, block, block == seq_count - 1))[-1])
+            reduced.append(list(reduce(outs, 0, block, base, block == seq_count - 1))[-1])
         results = [[spread(packed)] for packed in reduced]
     else:
         (own,) = multiply([parts[1:]], down_weight, sizes[0], [None], [False], wide, tokens=parts[:1])
         *halves, total = multiply(
             [[parts[0]], [arrivals[0][0]]], down_weight, 0, [own, None], [True, False], wide_chunk, groups=GROUPS
         )
-        own_steps = reduce(halves, 0, 0, False)
+        own_base = [zeros]
+        own_steps = reduce(halves, 0, 0, own_base, False)
         next(own_steps)
         tokens = [own_steps.send([arrivals[0][1]])]
         results = []
@@ -439,10 +434,12 @@
                 if not results:
                     step = own_steps.send([total])
                     tokens = [step]
-                    if step.shape[0] * tensor_count == hidden.shape[0] and len(scales) > 1:
+                    if own_base[0] is not zeros:
                         results.append([spread(step)])
             if not results:
                 results.append([spread(list(own_steps)[-1])])
+            if shift == 0:
+                bases = [list(own_base) for _ in range(GROUPS)]
             remote, all_steps = [], []
             for group in range(GROUPS):
                 sent, kept = multiply(
@@ -452,7 +449,7 @@
                 tokens = [sent]
                 if group == GROUPS - 1 and shift == 0 and levels > 1:
                     sent = gate(sent, [results[0][0][1], results[0][0][1 << levels - 1]])
-                all_steps.append(reduce([sent, kept], group * half // GROUPS, shift + 1, shift == seq_count - 2 and group == GROUPS - 1))
+                all_steps.append(reduce([sent, kept], group * half // GROUPS, shift + 1, bases[group], shift == seq_count - 2))
                 next(all_steps[-1])
             last = []
             for level in range(levels + 1):
@@ -462,8 +459,6 @@
                         wait += results[0][0][1:]
                     step = steps.send(wait)
                     if level == levels:
-                        if remote and levels > 1:
-                            step = gate(step, [remote[-1][1], remote[-1][1 << levels - 1]])
                         remote.append(spread(step))
                 last = [step]
             results.append(remote)
@@ -471,19 +466,14 @@
 
     groups = max(len(result) for result in results)
     width = half // groups
-    last = groups - 1
-
-    def chosen(group, other, tokens):
-        return choose(results, group, width, other, per_sub, half // BLOCK if group == last else 0, tokens)
-
-    came = []
-    for group in range(groups):
-        came.append(swap(chosen(group, True, came[-1:])))
-    mine = [chosen(group, False, []) for group in range(groups)]
-    (codes,) = put_codes(mine, list(range(groups)), width, half, True)
-    if last:
-        (codes,) = put_codes(came[:last], list(range(last)), width, half, False, codes)
-    codes, flat = put_codes(came[last:], [last], width, half, False, codes, mine[last])
+
+    def chosen(other):
+        return [choose(results, group, width, other, per_sub, half // BLOCK) for group in range(groups)]
+
+    came = [swap(values) for values in chosen(True)]
+    mine = chosen(False)
+    (codes,) = put_codes(mine, width, half, True)
+    codes, flat = put_codes(came, width, half, False, codes, mine)
     return codes, flat.T
 
 

time: 101 us -> 89.9 us (0.89)
  waiting for transfers between devices: 26.6 us -> 18.3 us
  starting transfers between devices: 29.6 us -> 27 us
    ppermute x15, waiting for transfers between devices: 23.3 us -> 14.5 us  [exchange(): lax.ppermute(values, 'tensor', [(t, t ^ 1 << level) for t in range(tensor...]
    ppermute x15, starting transfers between devices: 23.2 us -> 20.6 us  [exchange(): lax.ppermute(values, 'tensor', [(t, t ^ 1 << level) for t in range(tensor...]
    pallas_call x3 -> x2, Pallas kernels: 2.88 us -> 2.22 us  [put_codes(): pl.pallas_call(functools.partial(place_body, mine, half, width, len(array...]
  transfers between devices with their start and end apart: 25 -> 25, of which waited for: 10 -> 10; matrix products, arithmetic and copies ran while one was open for 0% -> 0% of each run, Pallas kernels for 40% -> 45%
where the time goes in v12:
time: 89.9 us; the launch traced here: 89.7 us
  Pallas kernels  42 us (47%)
  starting transfers between devices  27 us (30%)
  waiting for transfers between devices  18.3 us (20%)
  local copies, waits for them, and re-layouts  1.46 us (2%)
  between operations  0.92 us (1%)
    pallas_call x6, Pallas kernels, multiply(): pl.pallas_call(body, out_shape=out_shape, in_specs=[VMEM] * spans[-1][1]...  36.8 us
    ppermute x15, starting transfers between devices, exchange(): lax.ppermute(values, 'tensor', [(t, t ^ 1 << level) for t in range(tensor...  20.6 us
    ppermute x15, waiting for transfers between devices, exchange(): lax.ppermute(values, 'tensor', [(t, t ^ 1 << level) for t in range(tensor...  14.5 us
    ppermute x4, starting transfers between devices, shards(): arrivals.append([lax.ppermute(part, 'seq', pairs) for part in parts])  5.11 us
    ppermute x4, waiting for transfers between devices, shards(): arrivals.append([lax.ppermute(part, 'seq', pairs) for part in parts])  3.22 us
    pallas_call x3, Pallas kernels, encode(): pl.pallas_call(functools.partial(encode_body, begin, lane, last), out_sha...  2.25 us
    pallas_call x2, Pallas kernels, put_codes(): pl.pallas_call(functools.partial(place_body, mine, half, width, len(array...  2.22 us
  transfers between devices with their start and end apart: 25, of which 10 were waited for; matrix products, arithmetic and copies ran while one was open for 0% of the time, Pallas kernels for 45%

profile of v12, /device:TPU:0, one launch (start us, length us, event | category | flops | bytes accessed | tf_op | source)
XLA Modules:
  0.0 89.7 jit_solution(10633256483874552573)
XLA Ops:
  0.6 1.4 %copy-done = bf16[128,6656]{1,0:T(8,128)(2,1)S(1)} copy-done((bf16[128,6656]{1,0:T(8,128)(2,1)S(1)}, bf16[128,6656]{1,0:T(8,128)(2,1)}, u32[]{:S(2)}) %copy-start) | copy-done | bytes 1703960
  2.1 0.2 shard_map.59
  2.2 3.0 %collective-permute-start = (bf16[128,2048]{1,0:T(8,128)(2,1)S(1)}, bf16[128,2048]{1,0:T(8,128)(2,1)S(1)}, u32[]{:S(2)}, u32[]{:S(2)}) collective-permute-start(bf16[128,2048]{1,0:T(8,128)(2,1)S(1)} %get-tuple-element.31.refs_4_.refs_0_), channel_id=1, source_target_pairs={{0,2},{2,0},{1,3},{3,1},{4,6},{6,4},{5,7},{7,5},{8,10},{10,8},{9,1... | collective-permute-start | bytes 1572872 | tf_op jit(solution)/shard_map/ppermute | solution.py:407
  5.3 0.1 collective-permute-start.3
  5.3 12.7 %shard_map.60.refs_3_ = f32[128,4096]{1,0:T(8,128)S(1)} custom-call(bf16[128,2048]{1,0:T(8,128)(2,1)S(1)} %get-tuple-element.32.refs_0_, bf16[128,1536]{1,0:T(8,128)(2,1)S(1)} %get-tuple-element.33.refs_1_, bf16[128,1024]{1,0:T(8,128)(2,1)S(1)} %get-tuple-element.34.refs_2_, bf16[6656,4096]{1,0:T(8,128)(2,1)} %refs_1_.7, ...), custom_call_target="tpu_custom_call" | custom-call | flops 1 | bytes 1 | tf_op jit(solution)/shard_map/pallas_call | solution.py:139
  18.0 7.3 %shard_map.61 = (bf16[128,1024]{1,0:T(8,128)(2,1)S(1)}, f32[128,1024]{1,0:T(8,128)S(1)}, bf16[128,1024]{1,0:T(8,128)(2,1)S(1)}, f32[128,1024]{1,0:T(8,128)S(1)}, f32[128,4096]{1,0:T(8,128)S(1)}) custom-call(bf16[128,2048]{1,0:T(8,128)(2,1)S(1)} %get-tuple-element.31.refs_4_.refs_0_, bf16[128,2048]{1,0:T(8,128)(2,1)S(1)} %collective-permute-done.refs_1_, ...), custom_call_target="tpu_custom_call" | custom-call | flops 1 | bytes 1 | tf_op jit(solution)/shard_map/pallas_call | solution.py:139
  25.4 0.1 collective-permute-start.1
  25.5 0.5 collective-permute-start.2
  26.0 2.5 %collective-permute-done.3.refs_4_.refs_0_ = bf16[128,2048]{1,0:T(8,128)(2,1)S(1)} collective-permute-done((bf16[128,2048]{1,0:T(8,128)(2,1)S(1)}, bf16[128,2048]{1,0:T(8,128)(2,1)S(1)}, u32[]{:S(2)}, u32[]{:S(2)}) %collective-permute-start.3) | collective-permute-done | bytes 524320 | tf_op jit(solution)/shard_map/ppermute | solution.py:407
  28.4 0.1 shard_map.62
  28.5 1.9 %collective-permute-start.4 = (bf16[64,2048]{1,0:T(8,128)(2,1)S(1)}, bf16[64,2048]{1,0:T(8,128)(2,1)S(1)}, u32[]{:S(2)}, u32[]{:S(2)}) collective-permute-start(bf16[64,2048]{1,0:T(8,128)(2,1)S(1)} %get-tuple-element.40.refs_3_), channel_id=1, source_target_pairs={{0,4},{4,0},{8,12},{12,8},{1,5},{5,1},{9,13},{13,9},{2,6},{6,2},{1... | collective-permute-start | bytes 786440 | tf_op jit(solution)/shard_map/ppermute | solution.py:379
  30.4 1.5 %collective-permute-start.6 = (bf16[128,1536]{1,0:T(8,128)(2,1)S(1)}, bf16[128,1536]{1,0:T(8,128)(2,1)S(1)}, u32[]{:S(2)}, u32[]{:S(2)}) collective-permute-start(bf16[128,1536]{1,0:T(8,128)(2,1)S(1)} %get-tuple-element.33.refs_1_), channel_id=1, source_target_pairs={{0,2},{2,0},{1,3},{3,1},{4,6},{6,4},{5,7},{7,5},{8,10},{10,8},{9,1... | collective-permute-start | bytes 1179656 | tf_op jit(solution)/shard_map/ppermute | solution.py:407
  31.9 0.5 collective-permute-start.10
  32.4 6.5 %shard_map.63.refs_2_ = f32[128,4096]{1,0:T(8,128)S(1)} custom-call(bf16[128,2048]{1,0:T(8,128)(2,1)S(1)} %collective-permute-done.3.refs_4_.refs_0_, bf16[6656,4096]{1,0:T(8,128)(2,1)} %refs_1_.7, f32[128,4096]{1,0:T(8,128)S(1)} %get-tuple-element.41.refs_2_, bf16[64,2048]{1,0:T(8,128)(2,1)S(1)} %get-tuple-element.40.refs_3_), custom_call_target="tpu_custom_call" | custom-call | flops 1 | bytes 1 | tf_op jit(solution)/shard_map/pallas_call | solution.py:139
  39.0 2.7 %collective-permute-start.5 = (bf16[32,2048]{1,0:T(8,128)(2,1)S(1)}, bf16[32,2048]{1,0:T(8,128)(2,1)S(1)}, u32[]{:S(2)}, u32[]{:S(2)}) collective-permute-start(bf16[32,2048]{1,0:T(8,128)(2,1)S(1)} %get-tuple-element.43.refs_3_), channel_id=1, source_target_pairs={{0,8},{4,12},{8,0},{12,4},{1,9},{5,13},{9,1},{13,5},{2,10},{6,14},... | collective-permute-start | bytes 393224 | tf_op jit(solution)/shard_map/ppermute | solution.py:379
  41.7 0.8 collective-permute-done.6.refs_0_
  42.5 5.2 %shard_map.65.refs_0_.refs_2_ = f32[128,4096]{1,0:T(8,128)S(1)} custom-call(bf16[128,1536]{1,0:T(8,128)(2,1)S(1)} %collective-permute-done.6.refs_0_, bf16[6656,4096]{1,0:T(8,128)(2,1)} %refs_1_.7, f32[128,4096]{1,0:T(8,128)S(1)} %shard_map.63.refs_2_, bf16[32,2048]{1,0:T(8,128)(2,1)S(1)} %get-tuple-element.43.refs_3_), custom_call_target="tpu_custom_call" | custom-call | flops 1 | bytes 1 | tf_op jit(solution)/shard_map/pallas_call | solution.py:139
  47.6 1.0 %shard_map.66 = (bf16[32,2048]{1,0:T(8,128)(2,1)S(1)}, f32[32,128]{1,0:T(8,128)S(1)}) custom-call(f32[32,2048]{1,0:T(8,128)S(1)} %get-tuple-element.42.kept_ref, bf16[32,2048]{1,0:T(8,128)(2,1)S(1)} %collective-permute-done.5.came_ref, f32[32,128]{1,0:T(8,128)S(1)} %broadcast_in_dim.6.scales_ref, f32[1,4096]{1,0:T(1,128)S(1)} %bitcast.2, ...), custom_call_target="tpu_custom_call" | custom-call | flops 1 | bytes 1 | tf_op jit(solution)/shard_map/pallas_call | solution.py:234
  48.7 0.3 collective-permute-start.7
  49.0 2.8 %collective-permute-start.8 = (bf16[32,2048]{1,0:T(8,128)(2,1)S(1)}, bf16[32,2048]{1,0:T(8,128)(2,1)S(1)}, u32[]{:S(2)}, u32[]{:S(2)}) collective-permute-start(bf16[32,2048]{1,0:T(8,128)(2,1)S(1)} %get-tuple-element.44.refs_3_.refs_0_), channel_id=1, source_target_pairs={{0,8},{4,12},{8,0},{12,4},{1,9},{5,13},{9,1},{13,5},{2,10},{6,14},... | collective-permute-start | bytes 393224 | tf_op jit(solution)/shard_map/ppermute | solution.py:379
  51.8 2.5 %shard_map.67 = (bf16[128,1024]{1,0:T(8,128)(2,1)S(1)}, f32[128,1024]{1,0:T(8,128)S(1)}) custom-call(bf16[128,1024]{1,0:T(8,128)(2,1)S(1)} %collective-permute-done.10.refs_0_, bf16[6656,4096]{1,0:T(8,128)(2,1)} %refs_1_.7, f32[128,4096]{1,0:T(8,128)S(1)} %shard_map.65.refs_0_.refs_2_, bf16[32,2048]{1,0:T(8,128)(2,1)S(1)} %get-tuple-element.44.refs_3_.refs_0_), custom_call_target="tpu_custom_call" | custom-call | flops 1 | bytes 1 | tf_op jit(solution)/shard_map/pallas_call | solution.py:139
  54.3 0.1 collective-permute-start.11
  54.4 2.6 %shard_map.69 = (bf16[128,1024]{1,0:T(8,128)(2,1)S(1)}, f32[128,1024]{1,0:T(8,128)S(1)}) custom-call(bf16[128,1024]{1,0:T(8,128)(2,1)S(1)} %collective-permute-done.10.refs_0_, bf16[6656,4096]{1,0:T(8,128)(2,1)} %refs_1_.7, f32[128,4096]{1,0:T(8,128)S(1)} %shard_map.65.refs_0_.refs_2_, bf16[128,1024]{1,0:T(8,128)(2,1)S(1)} %get-tuple-element.46.refs_3_), custom_call_target="tpu_custom_call" | custom-call | flops 1 | bytes 1 | tf_op jit(solution)/shard_map/pallas_call | solution.py:139
  57.0 0.5 collective-permute-start.13
  57.6 1.6 %collective-permute-start.12 = (bf16[64,1024]{1,0:T(8,128)(2,1)S(1)}, bf16[64,1024]{1,0:T(8,128)(2,1)S(1)}, u32[]{:S(2)}, u32[]{:S(2)}) collective-permute-start(bf16[64,1024]{1,0:T(8,128)(2,1)S(1)} %get-tuple-element.48), channel_id=1, source_target_pairs={{0,4},{4,0},{8,12},{12,8},{1,5},{5,1},{9,13},{13,9},{2,6},{6,2},{1... | collective-permute-start | bytes 393224 | tf_op jit(solution)/shard_map/ppermute | solution.py:379
  59.3 1.1 %collective-permute-start.15 = (bf16[64,1024]{1,0:T(8,128)(2,1)S(1)}, bf16[64,1024]{1,0:T(8,128)(2,1)S(1)}, u32[]{:S(2)}, u32[]{:S(2)}) collective-permute-start(bf16[64,1024]{1,0:T(8,128)(2,1)S(1)} %get-tuple-element.51.refs_2_), channel_id=1, source_target_pairs={{0,4},{4,0},{8,12},{12,8},{1,5},{5,1},{9,13},{13,9},{2,6},{6,2},{1... | collective-permute-start | bytes 393224 | tf_op jit(solution)/shard_map/ppermute | solution.py:379
  60.4 1.0 %collective-permute-start.9 = (bf16[32,2048]{1,0:T(8,128)(2,1)S(1)}, bf16[32,2048]{1,0:T(8,128)(2,1)S(1)}, u32[]{:S(2)}, u32[]{:S(2)}) collective-permute-start(bf16[32,2048]{1,0:T(8,128)(2,1)S(1)} %collective-permute-done.8.refs_2_.refs_1_), channel_id=1, source_target_pairs={{0,4},{4,0},{8,12},{12,8},{1,5},{5,1},{9,13},{13,9},{2,6},{6,2},{1... | collective-permute-start | bytes 393224 | tf_op jit(solution)/shard_map/ppermute | solution.py:379
  61.4 2.6 %collective-permute-done.12.refs_1_ = bf16[64,1024]{1,0:T(8,128)(2,1)S(1)} collective-permute-done((bf16[64,1024]{1,0:T(8,128)(2,1)S(1)}, bf16[64,1024]{1,0:T(8,128)(2,1)S(1)}, u32[]{:S(2)}, u32[]{:S(2)}) %collective-permute-start.12) | collective-permute-done | bytes 131104 | tf_op jit(solution)/shard_map/ppermute | solution.py:379
  64.1 1.0 %collective-permute-start.14 = (bf16[32,1024]{1,0:T(8,128)(2,1)S(1)}, bf16[32,1024]{1,0:T(8,128)(2,1)S(1)}, u32[]{:S(2)}, u32[]{:S(2)}) collective-permute-start(bf16[32,1024]{1,0:T(8,128)(2,1)S(1)} %get-tuple-element.53), channel_id=1, source_target_pairs={{0,8},{4,12},{8,0},{12,4},{1,9},{5,13},{9,1},{13,5},{2,10},{6,14},... | collective-permute-start | bytes 196616 | tf_op jit(solution)/shard_map/ppermute | solution.py:379
  65.1 2.5 %collective-permute-done.15.refs_1_ = bf16[64,1024]{1,0:T(8,128)(2,1)S(1)} collective-permute-done((bf16[64,1024]{1,0:T(8,128)(2,1)S(1)}, bf16[64,1024]{1,0:T(8,128)(2,1)S(1)}, u32[]{:S(2)}, u32[]{:S(2)}) %collective-permute-start.15) | collective-permute-done | bytes 131104 | tf_op jit(solution)/shard_map/ppermute | solution.py:379
  67.6 0.3 collective-permute-start.19
  67.9 2.3 %collective-permute-done.14.came_ref = bf16[32,1024]{1,0:T(8,128)(2,1)S(1)} collective-permute-done((bf16[32,1024]{1,0:T(8,128)(2,1)S(1)}, bf16[32,1024]{1,0:T(8,128)(2,1)S(1)}, u32[]{:S(2)}, u32[]{:S(2)}) %collective-permute-start.14) | collective-permute-done | bytes 65568 | tf_op jit(solution)/shard_map/ppermute | solution.py:379
  70.2 0.6 shard_map.74.refs_4_
  70.8 3.3 %collective-permute-start.17 = (bf16[32,1152]{1,0:T(8,128)(2,1)S(1)}, bf16[32,1152]{1,0:T(8,128)(2,1)S(1)}, u32[]{:S(2)}, u32[]{:S(2)}) collective-permute-start(bf16[32,1152]{1,0:T(8,128)(2,1)S(1)} %shard_map.74.refs_4_), channel_id=1, source_target_pairs={{0,8},{4,12},{8,0},{12,4},{1,9},{5,13},{9,1},{13,5},{2,10},{6,14},... | collective-permute-start | bytes 221192 | tf_op jit(solution)/shard_map/ppermute | solution.py:379
  74.1 0.6 shard_map.76.refs_4_
  74.7 0.1 collective-permute-start.21
  74.8 2.4 %collective-permute-start.16 = (bf16[32,1152]{1,0:T(8,128)(2,1)S(1)}, bf16[32,1152]{1,0:T(8,128)(2,1)S(1)}, u32[]{:S(2)}, u32[]{:S(2)}) collective-permute-start(bf16[32,1152]{1,0:T(8,128)(2,1)S(1)} %shard_map.74.refs_4_), channel_id=1, source_target_pairs={{0,4},{4,0},{8,12},{12,8},{1,5},{5,1},{9,13},{13,9},{2,6},{6,2},{1... | collective-permute-start | bytes 221192 | tf_op jit(solution)/shard_map/ppermute | solution.py:379
  77.2 3.0 %collective-permute-done.17.refs_6_ = bf16[32,1152]{1,0:T(8,128)(2,1)S(1)} collective-permute-done((bf16[32,1152]{1,0:T(8,128)(2,1)S(1)}, bf16[32,1152]{1,0:T(8,128)(2,1)S(1)}, u32[]{:S(2)}, u32[]{:S(2)}) %collective-permute-start.17) | collective-permute-done | bytes 73760 | tf_op jit(solution)/shard_map/ppermute | solution.py:379
  80.2 2.0 %collective-permute-start.20 = (bf16[32,1152]{1,0:T(8,128)(2,1)S(1)}, bf16[32,1152]{1,0:T(8,128)(2,1)S(1)}, u32[]{:S(2)}, u32[]{:S(2)}) collective-permute-start(bf16[32,1152]{1,0:T(8,128)(2,1)S(1)} %shard_map.76.refs_4_), channel_id=1, source_target_pairs={{0,4},{4,0},{8,12},{12,8},{1,5},{5,1},{9,13},{13,9},{2,6},{6,2},{1... | collective-permute-start | bytes 221192 | tf_op jit(solution)/shard_map/ppermute | solution.py:379
  82.3 2.3 %collective-permute-done.18.refs_7_ = bf16[32,1152]{1,0:T(8,128)(2,1)S(1)} collective-permute-done((bf16[32,1152]{1,0:T(8,128)(2,1)S(1)}, bf16[32,1152]{1,0:T(8,128)(2,1)S(1)}, u32[]{:S(2)}, u32[]{:S(2)}) %collective-permute-start.18) | collective-permute-done | bytes 73760 | tf_op jit(solution)/shard_map/ppermute | solution.py:379
  84.6 0.1 shard_map.79
  84.7 0.7 collective-permute-done.20.refs_5_
  85.3 1.2 %collective-permute-done.22.refs_7_ = bf16[32,1152]{1,0:T(8,128)(2,1)S(1)} collective-permute-done((bf16[32,1152]{1,0:T(8,128)(2,1)S(1)}, bf16[32,1152]{1,0:T(8,128)(2,1)S(1)}, u32[]{:S(2)}, u32[]{:S(2)}) %collective-permute-start.22) | collective-permute-done | bytes 73760 | tf_op jit(solution)/shard_map/ppermute | solution.py:379
  86.6 0.1 shard_map.80
  86.8 0.1 shard_map.77.refs_1_.refs_4_
  86.9 0.8 shard_map.78.refs_0_
  87.7 0.6 collective-permute-done.24.refs_2_
  88.3 1.4 %shard_map.81 = (bf16[128,4096]{1,0:T(8,128)(2,1)}, bf16[32,128]{1,0:T(8,128)(2,1)}) custom-call(bf16[128,4096]{1,0:T(8,128)(2,1)} %shard_map.78.refs_0_, bf16[128,1152]{1,0:T(8,128)(2,1)S(1)} %collective-permute-done.23.refs_1_, bf16[128,1152]{1,0:T(8,128)(2,1)S(1)} %collective-permute-done.24.refs_2_, ...), custom_call_target="tpu_custom_call", output_to_operand_aliasing={{0}: (0, {})} | custom-call | flops 1 | bytes 1 | tf_op jit(solution)/shard_map/pallas_call | solution.py:343
  (33 shorter events, 0.5 us)
Async XLA Ops:
  0.6 1.5 %copy-start = (bf16[128,6656]{1,0:T(8,128)(2,1)S(1)}, bf16[128,6656]{1,0:T(8,128)(2,1)}, u32[]{:S(2)}) copy-start(bf16[128,6656]{1,0:T(8,128)(2,1)} %in_ref.1) | copy-start | bytes 5111812
  2.2 15.8 %collective-permute-start = (bf16[128,2048]{1,0:T(8,128)(2,1)S(1)}, bf16[128,2048]{1,0:T(8,128)(2,1)S(1)}, u32[]{:S(2)}, u32[]{:S(2)}) collective-permute-start(bf16[128,2048]{1,0:T(8,128)(2,1)S(1)} %get-tuple-element.31.refs_4_.refs_0_), channel_id=1, source_target_pairs={{0,2},{2,0},{1,3},{3,1},{4,6},{6,4},{5,7},{7,5},{8,10},{10,8},{9,1... | collective-permute-start | bytes 1572872 | tf_op jit(solution)/shard_map/ppermute | solution.py:407
  5.3 23.2 %collective-permute-start.3 = (bf16[128,2048]{1,0:T(8,128)(2,1)S(1)}, bf16[128,2048]{1,0:T(8,128)(2,1)S(1)}, u32[]{:S(2)}, u32[]{:S(2)}) collective-permute-start(bf16[128,2048]{1,0:T(8,128)(2,1)S(1)} %get-tuple-element.32.refs_0_), channel_id=1, source_target_pairs={{0,2},{2,0},{1,3},{3,1},{4,6},{6,4},{5,7},{7,5},{8,10},{10,8},{9,1... | collective-permute-start | bytes 1572872 | tf_op jit(solution)/shard_map/ppermute | solution.py:407
  25.4 3.0 %collective-permute-start.1 = (bf16[128,1024]{1,0:T(8,128)(2,1)S(1)}, bf16[128,1024]{1,0:T(8,128)(2,1)S(1)}, u32[]{:S(2)}, u32[]{:S(2)}) collective-permute-start(bf16[128,1024]{1,0:T(8,128)(2,1)S(1)} %get-tuple-element.37), channel_id=1, source_target_pairs={{0,1},{1,0},{2,3},{3,2},{4,5},{5,4},{6,7},{7,6},{8,9},{9,8},{10,11... | collective-permute-start | bytes 786440 | tf_op jit(solution)/shard_map/ppermute | solution.py:376
  25.5 3.0 %collective-permute-start.2 = (bf16[128,1024]{1,0:T(8,128)(2,1)S(1)}, bf16[128,1024]{1,0:T(8,128)(2,1)S(1)}, u32[]{:S(2)}, u32[]{:S(2)}) collective-permute-start(bf16[128,1024]{1,0:T(8,128)(2,1)S(1)} %get-tuple-element.38), channel_id=1, source_target_pairs={{0,1},{1,0},{2,3},{3,2},{4,5},{5,4},{6,7},{7,6},{8,9},{9,8},{10,11... | collective-permute-start | bytes 786440 | tf_op jit(solution)/shard_map/ppermute | solution.py:376
  28.5 10.4 %collective-permute-start.4 = (bf16[64,2048]{1,0:T(8,128)(2,1)S(1)}, bf16[64,2048]{1,0:T(8,128)(2,1)S(1)}, u32[]{:S(2)}, u32[]{:S(2)}) collective-permute-start(bf16[64,2048]{1,0:T(8,128)(2,1)S(1)} %get-tuple-element.40.refs_3_), channel_id=1, source_target_pairs={{0,4},{4,0},{8,12},{12,8},{1,5},{5,1},{9,13},{13,9},{2,6},{6,2},{1... | collective-permute-start | bytes 786440 | tf_op jit(solution)/shard_map/ppermute | solution.py:379
  30.4 12.1 %collective-permute-start.6 = (bf16[128,1536]{1,0:T(8,128)(2,1)S(1)}, bf16[128,1536]{1,0:T(8,128)(2,1)S(1)}, u32[]{:S(2)}, u32[]{:S(2)}) collective-permute-start(bf16[128,1536]{1,0:T(8,128)(2,1)S(1)} %get-tuple-element.33.refs_1_), channel_id=1, source_target_pairs={{0,2},{2,0},{1,3},{3,1},{4,6},{6,4},{5,7},{7,5},{8,10},{10,8},{9,1... | collective-permute-start | bytes 1179656 | tf_op jit(solution)/shard_map/ppermute | solution.py:407
  31.9 19.9 %collective-permute-start.10 = (bf16[128,1024]{1,0:T(8,128)(2,1)S(1)}, bf16[128,1024]{1,0:T(8,128)(2,1)S(1)}, u32[]{:S(2)}, u32[]{:S(2)}) collective-permute-start(bf16[128,1024]{1,0:T(8,128)(2,1)S(1)} %get-tuple-element.34.refs_2_), channel_id=1, source_target_pairs={{0,2},{2,0},{1,3},{3,1},{4,6},{6,4},{5,7},{7,5},{8,10},{10,8},{9,1... | collective-permute-start | bytes 786440 | tf_op jit(solution)/shard_map/ppermute | solution.py:407
  38.9 2.7 %copy-start.2 = (s32[4096]{0:T(1024)S(1)}, s32[4096]{0:T(1024)}, u32[]{:S(2)}) copy-start(s32[4096]{0:T(1024)} %param.6) | copy-start | bytes 49156
  39.0 8.6 %collective-permute-start.5 = (bf16[32,2048]{1,0:T(8,128)(2,1)S(1)}, bf16[32,2048]{1,0:T(8,128)(2,1)S(1)}, u32[]{:S(2)}, u32[]{:S(2)}) collective-permute-start(bf16[32,2048]{1,0:T(8,128)(2,1)S(1)} %get-tuple-element.43.refs_3_), channel_id=1, source_target_pairs={{0,8},{4,12},{8,0},{12,4},{1,9},{5,13},{9,1},{13,5},{2,10},{6,14},... | collective-permute-start | bytes 393224 | tf_op jit(solution)/shard_map/ppermute | solution.py:379
  41.7 6.0 %copy-start.1 = (f32[128,128]{1,0:T(8,128)S(1)}, f32[128,128]{1,0:T(8,128)}, u32[]{:S(2)}) copy-start(f32[128,128]{1,0:T(8,128)} %constant.9.clone.rotation_ref) | copy-start | bytes 196612
  48.7 8.3 %collective-permute-start.7 = (bf16[32,2048]{1,0:T(8,128)(2,1)S(1)}, bf16[32,2048]{1,0:T(8,128)(2,1)S(1)}, u32[]{:S(2)}, u32[]{:S(2)}) collective-permute-start(bf16[32,2048]{1,0:T(8,128)(2,1)S(1)} %get-tuple-element.44.refs_3_.refs_0_), channel_id=1, source_target_pairs={{0,4},{4,0},{8,12},{12,8},{1,5},{5,1},{9,13},{13,9},{2,6},{6,2},{1... | collective-permute-start | bytes 393224 | tf_op jit(solution)/shard_map/ppermute | solution.py:379
  49.0 8.0 %collective-permute-start.8 = (bf16[32,2048]{1,0:T(8,128)(2,1)S(1)}, bf16[32,2048]{1,0:T(8,128)(2,1)S(1)}, u32[]{:S(2)}, u32[]{:S(2)}) collective-permute-start(bf16[32,2048]{1,0:T(8,128)(2,1)S(1)} %get-tuple-element.44.refs_3_.refs_0_), channel_id=1, source_target_pairs={{0,8},{4,12},{8,0},{12,4},{1,9},{5,13},{9,1},{13,5},{2,10},{6,14},... | collective-permute-start | bytes 393224 | tf_op jit(solution)/shard_map/ppermute | solution.py:379
  54.3 3.2 %collective-permute-start.11 = (bf16[128,1024]{1,0:T(8,128)(2,1)S(1)}, bf16[128,1024]{1,0:T(8,128)(2,1)S(1)}, u32[]{:S(2)}, u32[]{:S(2)}) collective-permute-start(bf16[128,1024]{1,0:T(8,128)(2,1)S(1)} %get-tuple-element.46.refs_3_), channel_id=1, source_target_pairs={{0,1},{1,0},{2,3},{3,2},{4,5},{5,4},{6,7},{7,6},{8,9},{9,8},{10,11... | collective-permute-start | bytes 786440 | tf_op jit(solution)/shard_map/ppermute | solution.py:376
  57.0 2.2 %collective-permute-start.13 = (bf16[128,1024]{1,0:T(8,128)(2,1)S(1)}, bf16[128,1024]{1,0:T(8,128)(2,1)S(1)}, u32[]{:S(2)}, u32[]{:S(2)}) collective-permute-start(bf16[128,1024]{1,0:T(8,128)(2,1)S(1)} %shard_map.70), channel_id=1, source_target_pairs={{0,1},{1,0},{2,3},{3,2},{4,5},{5,4},{6,7},{7,6},{8,9},{9,8},{10,11... | collective-permute-start | bytes 786440 | tf_op jit(solution)/shard_map/ppermute | solution.py:376
  57.6 6.4 %collective-permute-start.12 = (bf16[64,1024]{1,0:T(8,128)(2,1)S(1)}, bf16[64,1024]{1,0:T(8,128)(2,1)S(1)}, u32[]{:S(2)}, u32[]{:S(2)}) collective-permute-start(bf16[64,1024]{1,0:T(8,128)(2,1)S(1)} %get-tuple-element.48), channel_id=1, source_target_pairs={{0,4},{4,0},{8,12},{12,8},{1,5},{5,1},{9,13},{13,9},{2,6},{6,2},{1... | collective-permute-start | bytes 393224 | tf_op jit(solution)/shard_map/ppermute | solution.py:379
  59.3 8.2 %collective-permute-start.15 = (bf16[64,1024]{1,0:T(8,128)(2,1)S(1)}, bf16[64,1024]{1,0:T(8,128)(2,1)S(1)}, u32[]{:S(2)}, u32[]{:S(2)}) collective-permute-start(bf16[64,1024]{1,0:T(8,128)(2,1)S(1)} %get-tuple-element.51.refs_2_), channel_id=1, source_target_pairs={{0,4},{4,0},{8,12},{12,8},{1,5},{5,1},{9,13},{13,9},{2,6},{6,2},{1... | collective-permute-start | bytes 393224 | tf_op jit(solution)/shard_map/ppermute | solution.py:379
  60.4 13.7 %collective-permute-start.9 = (bf16[32,2048]{1,0:T(8,128)(2,1)S(1)}, bf16[32,2048]{1,0:T(8,128)(2,1)S(1)}, u32[]{:S(2)}, u32[]{:S(2)}) collective-permute-start(bf16[32,2048]{1,0:T(8,128)(2,1)S(1)} %collective-permute-done.8.refs_2_.refs_1_), channel_id=1, source_target_pairs={{0,4},{4,0},{8,12},{12,8},{1,5},{5,1},{9,13},{13,9},{2,6},{6,2},{1... | collective-permute-start | bytes 393224 | tf_op jit(solution)/shard_map/ppermute | solution.py:379
  64.1 6.1 %collective-permute-start.14 = (bf16[32,1024]{1,0:T(8,128)(2,1)S(1)}, bf16[32,1024]{1,0:T(8,128)(2,1)S(1)}, u32[]{:S(2)}, u32[]{:S(2)}) collective-permute-start(bf16[32,1024]{1,0:T(8,128)(2,1)S(1)} %get-tuple-element.53), channel_id=1, source_target_pairs={{0,8},{4,12},{8,0},{12,4},{1,9},{5,13},{9,1},{13,5},{2,10},{6,14},... | collective-permute-start | bytes 196616 | tf_op jit(solution)/shard_map/ppermute | solution.py:379
  67.6 6.5 %collective-permute-start.19 = (bf16[32,1024]{1,0:T(8,128)(2,1)S(1)}, bf16[32,1024]{1,0:T(8,128)(2,1)S(1)}, u32[]{:S(2)}, u32[]{:S(2)}) collective-permute-start(bf16[32,1024]{1,0:T(8,128)(2,1)S(1)} %get-tuple-element.56.refs_0_), channel_id=1, source_target_pairs={{0,8},{4,12},{8,0},{12,4},{1,9},{5,13},{9,1},{13,5},{2,10},{6,14},... | collective-permute-start | bytes 196616 | tf_op jit(solution)/shard_map/ppermute | solution.py:379
  70.8 9.4 %collective-permute-start.17 = (bf16[32,1152]{1,0:T(8,128)(2,1)S(1)}, bf16[32,1152]{1,0:T(8,128)(2,1)S(1)}, u32[]{:S(2)}, u32[]{:S(2)}) collective-permute-start(bf16[32,1152]{1,0:T(8,128)(2,1)S(1)} %shard_map.74.refs_4_), channel_id=1, source_target_pairs={{0,8},{4,12},{8,0},{12,4},{1,9},{5,13},{9,1},{13,5},{2,10},{6,14},... | collective-permute-start | bytes 221192 | tf_op jit(solution)/shard_map/ppermute | solution.py:379
  74.7 7.5 %collective-permute-start.21 = (bf16[32,1152]{1,0:T(8,128)(2,1)S(1)}, bf16[32,1152]{1,0:T(8,128)(2,1)S(1)}, u32[]{:S(2)}, u32[]{:S(2)}) collective-permute-start(bf16[32,1152]{1,0:T(8,128)(2,1)S(1)} %shard_map.76.refs_4_), channel_id=1, source_target_pairs={{0,8},{4,12},{8,0},{12,4},{1,9},{5,13},{9,1},{13,5},{2,10},{6,14},... | collective-permute-start | bytes 221192 | tf_op jit(solution)/shard_map/ppermute | solution.py:379
  74.8 7.4 %collective-permute-start.16 = (bf16[32,1152]{1,0:T(8,128)(2,1)S(1)}, bf16[32,1152]{1,0:T(8,128)(2,1)S(1)}, u32[]{:S(2)}, u32[]{:S(2)}) collective-permute-start(bf16[32,1152]{1,0:T(8,128)(2,1)S(1)} %shard_map.74.refs_4_), channel_id=1, source_target_pairs={{0,4},{4,0},{8,12},{12,8},{1,5},{5,1},{9,13},{13,9},{2,6},{6,2},{1... | collective-permute-start | bytes 221192 | tf_op jit(solution)/shard_map/ppermute | solution.py:379
  80.2 4.4 %collective-permute-start.18 = (bf16[32,1152]{1,0:T(8,128)(2,1)S(1)}, bf16[32,1152]{1,0:T(8,128)(2,1)S(1)}, u32[]{:S(2)}, u32[]{:S(2)}) collective-permute-start(bf16[32,1152]{1,0:T(8,128)(2,1)S(1)} %collective-permute-done.17.refs_6_), channel_id=1, source_target_pairs={{0,4},{4,0},{8,12},{12,8},{1,5},{5,1},{9,13},{13,9},{2,6},{6,2},{1... | collective-permute-start | bytes 221192 | tf_op jit(solution)/shard_map/ppermute | solution.py:379
  80.2 5.1 %collective-permute-start.20 = (bf16[32,1152]{1,0:T(8,128)(2,1)S(1)}, bf16[32,1152]{1,0:T(8,128)(2,1)S(1)}, u32[]{:S(2)}, u32[]{:S(2)}) collective-permute-start(bf16[32,1152]{1,0:T(8,128)(2,1)S(1)} %shard_map.76.refs_4_), channel_id=1, source_target_pairs={{0,4},{4,0},{8,12},{12,8},{1,5},{5,1},{9,13},{13,9},{2,6},{6,2},{1... | collective-permute-start | bytes 221192 | tf_op jit(solution)/shard_map/ppermute | solution.py:379
  82.2 4.4 %collective-permute-start.22 = (bf16[32,1152]{1,0:T(8,128)(2,1)S(1)}, bf16[32,1152]{1,0:T(8,128)(2,1)S(1)}, u32[]{:S(2)}, u32[]{:S(2)}) collective-permute-start(bf16[32,1152]{1,0:T(8,128)(2,1)S(1)} %collective-permute-done.21.refs_6_), channel_id=1, source_target_pairs={{0,4},{4,0},{8,12},{12,8},{1,5},{5,1},{9,13},{13,9},{2,6},{6,2},{1... | collective-permute-start | bytes 221192 | tf_op jit(solution)/shard_map/ppermute | solution.py:379
  84.6 3.1 %collective-permute-start.23 = (bf16[128,1152]{1,0:T(8,128)(2,1)S(1)}, bf16[128,1152]{1,0:T(8,128)(2,1)S(1)}, u32[]{:S(2)}, u32[]{:S(2)}) collective-permute-start(bf16[128,1152]{1,0:T(8,128)(2,1)S(1)} %shard_map.79), channel_id=1, source_target_pairs={{0,1},{1,0},{2,3},{3,2},{4,5},{5,4},{6,7},{7,6},{8,9},{9,8},{10,11... | collective-permute-start | bytes 884744 | tf_op jit(solution)/shard_map/ppermute | solution.py:376
  86.7 1.6 %collective-permute-start.24 = (bf16[128,1152]{1,0:T(8,128)(2,1)S(1)}, bf16[128,1152]{1,0:T(8,128)(2,1)S(1)}, u32[]{:S(2)}, u32[]{:S(2)}) collective-permute-start(bf16[128,1152]{1,0:T(8,128)(2,1)S(1)} %shard_map.80), channel_id=1, source_target_pairs={{0,1},{1,0},{2,3},{3,2},{4,5},{5,4},{6,7},{7,6},{8,9},{9,8},{10,11... | collective-permute-start | bytes 884744 | tf_op jit(solution)/shard_map/ppermute | solution.py:376

commit v13 on v12

--- a/solution.py
+++ b/solution.py
@@ -13,6 +13,7 @@
 UNIT = 512
 GROUPS = 2
 VMEM_LIMIT = 6 * 2**20
+SLICE_LIMIT = 61 * 2**20 + 2**19
 SHARES = (4, 4, 3)
 epsilon = 1e-06
 
@@ -50,7 +51,7 @@
         in_specs=[HBM],
         out_specs=[VMEM] * len(places),
         scratch_shapes=[pltpu.SemaphoreType.DMA((len(places),))],
-        compiler_params=PARAMS,
+        compiler_params=pltpu.CompilerParams(vmem_limit_bytes=SLICE_LIMIT),
         cost_estimate=SMALL,
     )(values)
 
@@ -205,21 +206,28 @@
     out_ref = refs[-1 if last else -2]
     rows, columns = kept_ref.shape
     half = flips_ref.shape[1] // 2
-    rotation = rotation_ref[...]
+    blocks = columns // BLOCK
     lanes = lax.broadcasted_iota(jnp.int32, (rows, BLOCK), 1)
     scales = scales_ref[...]
-    for block in range(columns // BLOCK):
+    totals = []
+    for block in range(blocks):
         at = slice(block * BLOCK, (block + 1) * BLOCK)
         place = lax.axis_index("sub") * half + begin + block * BLOCK
         flips = flips_ref[:, pl.ds(pl.multiple_of(place, BLOCK), BLOCK)]
-        total = (kept_ref[:, at] + came_ref[:, at].astype(jnp.float32)) * flips
-        rotated = jnp.dot(
-            total, rotation, precision=lax.Precision.HIGHEST, preferred_element_type=jnp.float32
-        )
-        largest = jnp.max(jnp.abs(rotated), axis=1, keepdims=True)
-        scale = (largest + epsilon).astype(jnp.bfloat16).astype(jnp.float32)
-        out_ref[:, at] = (rotated / scale).astype(jnp.bfloat16)
-        scales = jnp.where(lanes == lane + block, scale, scales)
+        totals.append((kept_ref[:, at] + came_ref[:, at].astype(jnp.float32)) * flips)
+    rotated = jnp.dot(
+        jnp.concatenate(totals, axis=0),
+        rotation_ref[...],
+        precision=lax.Precision.HIGHEST,
+        preferred_element_type=jnp.float32,
+    )
+    largest = jnp.max(jnp.abs(rotated), axis=1, keepdims=True)
+    scale = (largest + epsilon).astype(jnp.bfloat16).astype(jnp.float32)
+    codes = rotated / scale
+    for block in range(blocks):
+        part = slice(block * rows, (block + 1) * rows)
+        out_ref[:, block * BLOCK : (block + 1) * BLOCK] = codes[part].astype(jnp.bfloat16)
+        scales = jnp.where(lanes == lane + block, scale[part], scales)
     if last:
         out_ref[:, columns:] = scales.astype(jnp.bfloat16)
     else:
@@ -368,7 +376,7 @@
     half = down_weight.shape[1] // sub_count
     per_sub = seq_count // sub_count
     levels = tensor_count.bit_length() - 1
-    wide, wide_chunk = min(256, half // GROUPS), min(512, half // GROUPS)
+    wide, wide_chunk, wide_merged = (min(size, half // GROUPS) for size in (256, 512, 1024))
     flips = (2 * sign_bits - 1).astype(jnp.float32)[None, :]
     rotation = jnp.asarray(hadamard(BLOCK))
 
@@ -417,7 +425,7 @@
     else:
         (own,) = multiply([parts[1:]], down_weight, sizes[0], [None], [False], wide, tokens=parts[:1])
         *halves, total = multiply(
-            [[parts[0]], [arrivals[0][0]]], down_weight, 0, [own, None], [True, False], wide_chunk, groups=GROUPS
+            [[parts[0]], [arrivals[0][0]]], down_weight, 0, [own, None], [True, False], wide_merged, groups=GROUPS
         )
         own_base = [zeros]
         own_steps = reduce(halves, 0, 0, own_base, False)

time: 89.9 us -> 93.2 us (1.037)
  local copies, waits for them, and re-layouts: 1.46 us -> 4.05 us
  waiting for transfers between devices: 18.3 us -> 17 us
  Pallas kernels: 42 us -> 43.3 us
    unnamed x6 -> x14, local copies, waits for them, and re-layouts: 1.46 us -> 4.04 us
    ppermute x4, waiting for transfers between devices: 3.22 us -> 0.72 us  [shards(): arrivals.append([lax.ppermute(part, 'seq', pairs) for part in parts])]
    pallas_call x1, Pallas kernels: 0.16 us -> 2.6 us  [slices_of(): pl.pallas_call(functools.partial(slice_body, places), out_shape=[jax.Shap...]
    ppermute x6, waiting for transfers between devices: 0.6 us -> 2.03 us  [swap(): return lax.ppermute(values, 'sub', [(0, 1), (1, 0)])]
    ppermute x15, starting transfers between devices: 20.6 us -> 21.8 us  [exchange(): lax.ppermute(values, 'tensor', [(t, t ^ 1 << level) for t in range(tensor...]
    pallas_call x3, Pallas kernels: 2.25 us -> 1.16 us  [encode(): pl.pallas_call(functools.partial(encode_body, begin, lane, last), out_sha...]
  transfers between devices with their start and end apart: 25 -> 25, of which waited for: 10 -> 14; matrix products, arithmetic and copies ran while one was open for 0% -> 0% of each run, Pallas kernels for 45% -> 42%
where the time goes in v13:
time: 93.2 us; the launch traced here: 92.9 us
  Pallas kernels  43.3 us (46%)
  starting transfers between devices  27.6 us (30%)
  waiting for transfers between devices  17 us (18%)
  local copies, waits for them, and re-layouts  4.05 us (4%)
    pallas_call x6, Pallas kernels, multiply(): pl.pallas_call(body, out_shape=out_shape, in_specs=[VMEM] * spans[-1][1]...  36.7 us
    ppermute x15, starting transfers between devices, exchange(): lax.ppermute(values, 'tensor', [(t, t ^ 1 << level) for t in range(tensor...  21.8 us
    ppermute x15, waiting for transfers between devices, exchange(): lax.ppermute(values, 'tensor', [(t, t ^ 1 << level) for t in range(tensor...  14.2 us
    ppermute x4, starting transfers between devices, shards(): arrivals.append([lax.ppermute(part, 'seq', pairs) for part in parts])  5.11 us
    unnamed x14, local copies, waits for them, and re-layouts  4.04 us
    pallas_call x1, Pallas kernels, slices_of(): pl.pallas_call(functools.partial(slice_body, places), out_shape=[jax.Shap...  2.6 us
    pallas_call x2, Pallas kernels, put_codes(): pl.pallas_call(functools.partial(place_body, mine, half, width, len(array...  2.22 us
    ppermute x6, waiting for transfers between devices, swap(): return lax.ppermute(values, 'sub', [(0, 1), (1, 0)])  2.03 us
  transfers between devices with their start and end apart: 25, of which 14 were waited for; matrix products, arithmetic and copies ran while one was open for 0% of the time, Pallas kernels for 42%

profile of v13, /device:TPU:0, one launch (start us, length us, event | category | flops | bytes accessed | tf_op | source)
XLA Modules:
  0.0 92.9 jit_solution(11861773644798214936)
XLA Ops:
  0.6 2.6 %shard_map.59 = (bf16[128,2048]{1,0:T(8,128)(2,1)}, bf16[128,2048]{1,0:T(8,128)(2,1)}, bf16[128,1536]{1,0:T(8,128)(2,1)}, bf16[128,1024]{1,0:T(8,128)(2,1)}) custom-call(bf16[128,6656]{1,0:T(8,128)(2,1)} %in_ref.1), custom_call_target="tpu_custom_call" | custom-call | flops 1 | bytes 1 | tf_op jit(solution)/shard_map/pallas_call | solution.py:48
  3.2 3.0 %collective-permute-start = (bf16[128,2048]{1,0:T(8,128)(2,1)}, bf16[128,2048]{1,0:T(8,128)(2,1)S(1)}, u32[]{:S(2)}, u32[]{:S(2)}) collective-permute-start(bf16[128,2048]{1,0:T(8,128)(2,1)} %get-tuple-element.31.refs_4_.refs_0_), channel_id=1, source_target_pairs={{0,2},{2,0},{1,3},{3,1},{4,6},{6,4},{5,7},{7,5},{8,10},{10,8},{9,1... | collective-permute-start | bytes 1572872 | tf_op jit(solution)/shard_map/ppermute | solution.py:415
  6.3 1.0 %copy-done = bf16[128,2048]{1,0:T(8,128)(2,1)S(1)} copy-done((bf16[128,2048]{1,0:T(8,128)(2,1)S(1)}, bf16[128,2048]{1,0:T(8,128)(2,1)}, u32[]{:S(2)}) %copy-start) | copy-done | bytes 524312
  7.4 1.0 %copy-done.2 = bf16[128,2048]{1,0:T(8,128)(2,1)S(1)} copy-done((bf16[128,2048]{1,0:T(8,128)(2,1)S(1)}, bf16[128,2048]{1,0:T(8,128)(2,1)}, u32[]{:S(2)}) %copy-start.2) | copy-done | bytes 524312
  8.4 1.0 %copy-done.3 = bf16[128,1536]{1,0:T(8,128)(2,1)S(1)} copy-done((bf16[128,1536]{1,0:T(8,128)(2,1)S(1)}, bf16[128,1536]{1,0:T(8,128)(2,1)}, u32[]{:S(2)}) %copy-start.3) | copy-done | bytes 393240
  9.4 0.9 %copy-done.4 = bf16[128,1024]{1,0:T(8,128)(2,1)S(1)} copy-done((bf16[128,1024]{1,0:T(8,128)(2,1)S(1)}, bf16[128,1024]{1,0:T(8,128)(2,1)}, u32[]{:S(2)}) %copy-start.4) | copy-done | bytes 262168
  10.4 12.7 %shard_map.60.refs_3_ = f32[128,4096]{1,0:T(8,128)S(1)} custom-call(bf16[128,2048]{1,0:T(8,128)(2,1)S(1)} %copy-done.2, bf16[128,1536]{1,0:T(8,128)(2,1)S(1)} %copy-done.3, bf16[128,1024]{1,0:T(8,128)(2,1)S(1)} %copy-done.4, bf16[6656,4096]{1,0:T(8,128)(2,1)} %refs_1_.7, bf16[128,2048]{1,0:T(8,128)(2,1)S(1)} %copy-done), custom_call_target="tpu_custom_call" | custom-call | flops 1 | bytes 1 | tf_op jit(solution)/shard_map/pallas_call | solution.py:140
  23.1 7.3 %shard_map.61 = (bf16[128,1024]{1,0:T(8,128)(2,1)S(1)}, f32[128,1024]{1,0:T(8,128)S(1)}, bf16[128,1024]{1,0:T(8,128)(2,1)S(1)}, f32[128,1024]{1,0:T(8,128)S(1)}, f32[128,4096]{1,0:T(8,128)S(1)}) custom-call(bf16[128,2048]{1,0:T(8,128)(2,1)S(1)} %copy-done, bf16[128,2048]{1,0:T(8,128)(2,1)S(1)} %collective-permute-done.refs_1_, bf16[6656,4096]{1,0:T(8,128)(2,1)} %refs_1_.7, ...), custom_call_target="tpu_custom_call" | custom-call | flops 1 | bytes 1 | tf_op jit(solution)/shard_map/pallas_call | solution.py:140
  30.4 0.5 collective-permute-start.2
  30.9 1.0 %collective-permute-done.1.refs_2_ = bf16[128,1024]{1,0:T(8,128)(2,1)S(1)} collective-permute-done((bf16[128,1024]{1,0:T(8,128)(2,1)S(1)}, bf16[128,1024]{1,0:T(8,128)(2,1)S(1)}, u32[]{:S(2)}, u32[]{:S(2)}) %collective-permute-start.1) | collective-permute-done | bytes 262176 | tf_op jit(solution)/shard_map/ppermute | solution.py:384
  32.0 0.4 collective-permute-done.2.refs_3_
  32.3 0.1 shard_map.62
  32.4 2.1 %collective-permute-start.4 = (bf16[64,2048]{1,0:T(8,128)(2,1)S(1)}, bf16[64,2048]{1,0:T(8,128)(2,1)S(1)}, u32[]{:S(2)}, u32[]{:S(2)}) collective-permute-start(bf16[64,2048]{1,0:T(8,128)(2,1)S(1)} %get-tuple-element.40.refs_3_), channel_id=1, source_target_pairs={{0,4},{4,0},{8,12},{12,8},{1,5},{5,1},{9,13},{13,9},{2,6},{6,2},{1... | collective-permute-start | bytes 786440 | tf_op jit(solution)/shard_map/ppermute | solution.py:387
  34.5 1.5 %collective-permute-start.6 = (bf16[128,1536]{1,0:T(8,128)(2,1)S(1)}, bf16[128,1536]{1,0:T(8,128)(2,1)S(1)}, u32[]{:S(2)}, u32[]{:S(2)}) collective-permute-start(bf16[128,1536]{1,0:T(8,128)(2,1)S(1)} %copy-done.3), channel_id=1, source_target_pairs={{0,2},{2,0},{1,3},{3,1},{4,6},{6,4},{5,7},{7,5},{8,10},{10,8},{9,1... | collective-permute-start | bytes 1179656 | tf_op jit(solution)/shard_map/ppermute | solution.py:415
  36.0 0.5 collective-permute-start.10
  36.5 6.5 %shard_map.63.refs_2_ = f32[128,4096]{1,0:T(8,128)S(1)} custom-call(bf16[128,2048]{1,0:T(8,128)(2,1)S(1)} %collective-permute-done.3.refs_4_.refs_0_, bf16[6656,4096]{1,0:T(8,128)(2,1)} %refs_1_.7, f32[128,4096]{1,0:T(8,128)S(1)} %get-tuple-element.41.refs_2_, bf16[64,2048]{1,0:T(8,128)(2,1)S(1)} %get-tuple-element.40.refs_3_), custom_call_target="tpu_custom_call" | custom-call | flops 1 | bytes 1 | tf_op jit(solution)/shard_map/pallas_call | solution.py:140
  43.1 2.6 %collective-permute-start.5 = (bf16[32,2048]{1,0:T(8,128)(2,1)S(1)}, bf16[32,2048]{1,0:T(8,128)(2,1)S(1)}, u32[]{:S(2)}, u32[]{:S(2)}) collective-permute-start(bf16[32,2048]{1,0:T(8,128)(2,1)S(1)} %get-tuple-element.43.refs_3_), channel_id=1, source_target_pairs={{0,8},{4,12},{8,0},{12,4},{1,9},{5,13},{9,1},{13,5},{2,10},{6,14},... | collective-permute-start | bytes 393224 | tf_op jit(solution)/shard_map/ppermute | solution.py:387
  45.8 0.7 collective-permute-done.6.refs_0_
  46.5 5.2 %shard_map.65.refs_0_.refs_2_ = f32[128,4096]{1,0:T(8,128)S(1)} custom-call(bf16[128,1536]{1,0:T(8,128)(2,1)S(1)} %collective-permute-done.6.refs_0_, bf16[6656,4096]{1,0:T(8,128)(2,1)} %refs_1_.7, f32[128,4096]{1,0:T(8,128)S(1)} %shard_map.63.refs_2_, bf16[32,2048]{1,0:T(8,128)(2,1)S(1)} %get-tuple-element.43.refs_3_), custom_call_target="tpu_custom_call" | custom-call | flops 1 | bytes 1 | tf_op jit(solution)/shard_map/pallas_call | solution.py:140
  51.7 0.5 shard_map.66
  52.2 0.1 collective-permute-start.7
  52.3 3.0 %collective-permute-start.8 = (bf16[32,2048]{1,0:T(8,128)(2,1)S(1)}, bf16[32,2048]{1,0:T(8,128)(2,1)S(1)}, u32[]{:S(2)}, u32[]{:S(2)}) collective-permute-start(bf16[32,2048]{1,0:T(8,128)(2,1)S(1)} %get-tuple-element.44.refs_3_.refs_0_), channel_id=1, source_target_pairs={{0,8},{4,12},{8,0},{12,4},{1,9},{5,13},{9,1},{13,5},{2,10},{6,14},... | collective-permute-start | bytes 393224 | tf_op jit(solution)/shard_map/ppermute | solution.py:387
  55.3 2.5 %shard_map.67 = (bf16[128,1024]{1,0:T(8,128)(2,1)S(1)}, f32[128,1024]{1,0:T(8,128)S(1)}) custom-call(bf16[128,1024]{1,0:T(8,128)(2,1)S(1)} %collective-permute-done.10.refs_0_, bf16[6656,4096]{1,0:T(8,128)(2,1)} %refs_1_.7, f32[128,4096]{1,0:T(8,128)S(1)} %shard_map.65.refs_0_.refs_2_, bf16[32,2048]{1,0:T(8,128)(2,1)S(1)} %get-tuple-element.44.refs_3_.refs_0_), custom_call_target="tpu_custom_call" | custom-call | flops 1 | bytes 1 | tf_op jit(solution)/shard_map/pallas_call | solution.py:140
  57.9 2.6 %shard_map.69 = (bf16[128,1024]{1,0:T(8,128)(2,1)S(1)}, f32[128,1024]{1,0:T(8,128)S(1)}) custom-call(bf16[128,1024]{1,0:T(8,128)(2,1)S(1)} %collective-permute-done.10.refs_0_, bf16[6656,4096]{1,0:T(8,128)(2,1)} %refs_1_.7, f32[128,4096]{1,0:T(8,128)S(1)} %shard_map.65.refs_0_.refs_2_, bf16[128,1024]{1,0:T(8,128)(2,1)S(1)} %get-tuple-element.46.refs_3_), custom_call_target="tpu_custom_call" | custom-call | flops 1 | bytes 1 | tf_op jit(solution)/shard_map/pallas_call | solution.py:140
  60.5 0.8 collective-permute-done.8.refs_2_.refs_1_
  61.4 1.4 %collective-permute-start.12 = (bf16[64,1024]{1,0:T(8,128)(2,1)S(1)}, bf16[64,1024]{1,0:T(8,128)(2,1)S(1)}, u32[]{:S(2)}, u32[]{:S(2)}) collective-permute-start(bf16[64,1024]{1,0:T(8,128)(2,1)S(1)} %get-tuple-element.48), channel_id=1, source_target_pairs={{0,4},{4,0},{8,12},{12,8},{1,5},{5,1},{9,13},{13,9},{2,6},{6,2},{1... | collective-permute-start | bytes 393224 | tf_op jit(solution)/shard_map/ppermute | solution.py:387
  62.9 1.1 %collective-permute-start.15 = (bf16[64,1024]{1,0:T(8,128)(2,1)S(1)}, bf16[64,1024]{1,0:T(8,128)(2,1)S(1)}, u32[]{:S(2)}, u32[]{:S(2)}) collective-permute-start(bf16[64,1024]{1,0:T(8,128)(2,1)S(1)} %get-tuple-element.51.refs_2_), channel_id=1, source_target_pairs={{0,4},{4,0},{8,12},{12,8},{1,5},{5,1},{9,13},{13,9},{2,6},{6,2},{1... | collective-permute-start | bytes 393224 | tf_op jit(solution)/shard_map/ppermute | solution.py:387
  63.9 1.0 %collective-permute-start.9 = (bf16[32,2048]{1,0:T(8,128)(2,1)S(1)}, bf16[32,2048]{1,0:T(8,128)(2,1)S(1)}, u32[]{:S(2)}, u32[]{:S(2)}) collective-permute-start(bf16[32,2048]{1,0:T(8,128)(2,1)S(1)} %collective-permute-done.8.refs_2_.refs_1_), channel_id=1, source_target_pairs={{0,4},{4,0},{8,12},{12,8},{1,5},{5,1},{9,13},{13,9},{2,6},{6,2},{1... | collective-permute-start | bytes 393224 | tf_op jit(solution)/shard_map/ppermute | solution.py:387
  65.0 2.7 %collective-permute-done.12.refs_1_ = bf16[64,1024]{1,0:T(8,128)(2,1)S(1)} collective-permute-done((bf16[64,1024]{1,0:T(8,128)(2,1)S(1)}, bf16[64,1024]{1,0:T(8,128)(2,1)S(1)}, u32[]{:S(2)}, u32[]{:S(2)}) %collective-permute-start.12) | collective-permute-done | bytes 131104 | tf_op jit(solution)/shard_map/ppermute | solution.py:387
  67.7 1.1 %collective-permute-start.14 = (bf16[32,1024]{1,0:T(8,128)(2,1)S(1)}, bf16[32,1024]{1,0:T(8,128)(2,1)S(1)}, u32[]{:S(2)}, u32[]{:S(2)}) collective-permute-start(bf16[32,1024]{1,0:T(8,128)(2,1)S(1)} %get-tuple-element.53), channel_id=1, source_target_pairs={{0,8},{4,12},{8,0},{12,4},{1,9},{5,13},{9,1},{13,5},{2,10},{6,14},... | collective-permute-start | bytes 196616 | tf_op jit(solution)/shard_map/ppermute | solution.py:387
  68.8 1.7 %collective-permute-done.15.refs_1_ = bf16[64,1024]{1,0:T(8,128)(2,1)S(1)} collective-permute-done((bf16[64,1024]{1,0:T(8,128)(2,1)S(1)}, bf16[64,1024]{1,0:T(8,128)(2,1)S(1)}, u32[]{:S(2)}, u32[]{:S(2)}) %collective-permute-start.15) | collective-permute-done | bytes 131104 | tf_op jit(solution)/shard_map/ppermute | solution.py:387
  70.6 1.1 %collective-permute-start.19 = (bf16[32,1024]{1,0:T(8,128)(2,1)S(1)}, bf16[32,1024]{1,0:T(8,128)(2,1)S(1)}, u32[]{:S(2)}, u32[]{:S(2)}) collective-permute-start(bf16[32,1024]{1,0:T(8,128)(2,1)S(1)} %get-tuple-element.56.refs_0_), channel_id=1, source_target_pairs={{0,8},{4,12},{8,0},{12,4},{1,9},{5,13},{9,1},{13,5},{2,10},{6,14},... | collective-permute-start | bytes 196616 | tf_op jit(solution)/shard_map/ppermute | solution.py:387
  71.7 1.8 %collective-permute-done.14.came_ref = bf16[32,1024]{1,0:T(8,128)(2,1)S(1)} collective-permute-done((bf16[32,1024]{1,0:T(8,128)(2,1)S(1)}, bf16[32,1024]{1,0:T(8,128)(2,1)S(1)}, u32[]{:S(2)}, u32[]{:S(2)}) %collective-permute-start.14) | collective-permute-done | bytes 65568 | tf_op jit(solution)/shard_map/ppermute | solution.py:387
  73.5 0.3 shard_map.74.refs_4_
  73.9 3.5 %collective-permute-start.17 = (bf16[32,1152]{1,0:T(8,128)(2,1)S(1)}, bf16[32,1152]{1,0:T(8,128)(2,1)S(1)}, u32[]{:S(2)}, u32[]{:S(2)}) collective-permute-start(bf16[32,1152]{1,0:T(8,128)(2,1)S(1)} %shard_map.74.refs_4_), channel_id=1, source_target_pairs={{0,8},{4,12},{8,0},{12,4},{1,9},{5,13},{9,1},{13,5},{2,10},{6,14},... | collective-permute-start | bytes 221192 | tf_op jit(solution)/shard_map/ppermute | solution.py:387
  77.3 0.6 collective-permute-done.19.came_ref
  77.9 0.3 shard_map.76.refs_4_
  78.4 2.6 %collective-permute-start.16 = (bf16[32,1152]{1,0:T(8,128)(2,1)S(1)}, bf16[32,1152]{1,0:T(8,128)(2,1)S(1)}, u32[]{:S(2)}, u32[]{:S(2)}) collective-permute-start(bf16[32,1152]{1,0:T(8,128)(2,1)S(1)} %shard_map.74.refs_4_), channel_id=1, source_target_pairs={{0,4},{4,0},{8,12},{12,8},{1,5},{5,1},{9,13},{13,9},{2,6},{6,2},{1... | collective-permute-start | bytes 221192 | tf_op jit(solution)/shard_map/ppermute | solution.py:387
  80.9 2.1 %collective-permute-done.17.refs_6_ = bf16[32,1152]{1,0:T(8,128)(2,1)S(1)} collective-permute-done((bf16[32,1152]{1,0:T(8,128)(2,1)S(1)}, bf16[32,1152]{1,0:T(8,128)(2,1)S(1)}, u32[]{:S(2)}, u32[]{:S(2)}) %collective-permute-start.17) | collective-permute-done | bytes 73760 | tf_op jit(solution)/shard_map/ppermute | solution.py:387
  83.0 2.0 %collective-permute-start.20 = (bf16[32,1152]{1,0:T(8,128)(2,1)S(1)}, bf16[32,1152]{1,0:T(8,128)(2,1)S(1)}, u32[]{:S(2)}, u32[]{:S(2)}) collective-permute-start(bf16[32,1152]{1,0:T(8,128)(2,1)S(1)} %shard_map.76.refs_4_), channel_id=1, source_target_pairs={{0,4},{4,0},{8,12},{12,8},{1,5},{5,1},{9,13},{13,9},{2,6},{6,2},{1... | collective-permute-start | bytes 221192 | tf_op jit(solution)/shard_map/ppermute | solution.py:387
  85.1 0.6 collective-permute-done.16.refs_5_
  85.8 2.1 %collective-permute-done.18.refs_7_ = bf16[32,1152]{1,0:T(8,128)(2,1)S(1)} collective-permute-done((bf16[32,1152]{1,0:T(8,128)(2,1)S(1)}, bf16[32,1152]{1,0:T(8,128)(2,1)S(1)}, u32[]{:S(2)}, u32[]{:S(2)}) %collective-permute-start.18) | collective-permute-done | bytes 73760 | tf_op jit(solution)/shard_map/ppermute | solution.py:387
  88.0 1.0 %collective-permute-done.20.refs_5_ = bf16[32,1152]{1,0:T(8,128)(2,1)S(1)} collective-permute-done((bf16[32,1152]{1,0:T(8,128)(2,1)S(1)}, bf16[32,1152]{1,0:T(8,128)(2,1)S(1)}, u32[]{:S(2)}, u32[]{:S(2)}) %collective-permute-start.20) | collective-permute-done | bytes 73760 | tf_op jit(solution)/shard_map/ppermute | solution.py:387
  89.0 0.8 collective-permute-done.22.refs_7_
  90.0 0.1 shard_map.77.refs_1_.refs_4_
  90.1 0.8 shard_map.78.refs_0_
  90.9 0.6 collective-permute-done.24.refs_2_
  91.5 1.4 %shard_map.81 = (bf16[128,4096]{1,0:T(8,128)(2,1)}, bf16[32,128]{1,0:T(8,128)(2,1)}) custom-call(bf16[128,4096]{1,0:T(8,128)(2,1)} %shard_map.78.refs_0_, bf16[128,1152]{1,0:T(8,128)(2,1)S(1)} %collective-permute-done.23.refs_1_, bf16[128,1152]{1,0:T(8,128)(2,1)S(1)} %collective-permute-done.24.refs_2_, ...), custom_call_target="tpu_custom_call", output_to_operand_aliasing={{0}: (0, {})} | custom-call | flops 1 | bytes 1 | tf_op jit(solution)/shard_map/pallas_call | solution.py:351
  (41 shorter events, 1.0 us)
Async XLA Ops:
  3.2 19.8 %collective-permute-start = (bf16[128,2048]{1,0:T(8,128)(2,1)}, bf16[128,2048]{1,0:T(8,128)(2,1)S(1)}, u32[]{:S(2)}, u32[]{:S(2)}) collective-permute-start(bf16[128,2048]{1,0:T(8,128)(2,1)} %get-tuple-element.31.refs_4_.refs_0_), channel_id=1, source_target_pairs={{0,2},{2,0},{1,3},{3,1},{4,6},{6,4},{5,7},{7,5},{8,10},{10,8},{9,1... | collective-permute-start | bytes 1572872 | tf_op jit(solution)/shard_map/ppermute | solution.py:415
  6.2 24.7 %collective-permute-start.3 = (bf16[128,2048]{1,0:T(8,128)(2,1)}, bf16[128,2048]{1,0:T(8,128)(2,1)S(1)}, u32[]{:S(2)}, u32[]{:S(2)}) collective-permute-start(bf16[128,2048]{1,0:T(8,128)(2,1)} %get-tuple-element.32.refs_0_), channel_id=1, source_target_pairs={{0,2},{2,0},{1,3},{3,1},{4,6},{6,4},{5,7},{7,5},{8,10},{10,8},{9,1... | collective-permute-start | bytes 1572872 | tf_op jit(solution)/shard_map/ppermute | solution.py:415
  6.3 1.0 %copy-start = (bf16[128,2048]{1,0:T(8,128)(2,1)S(1)}, bf16[128,2048]{1,0:T(8,128)(2,1)}, u32[]{:S(2)}) copy-start(bf16[128,2048]{1,0:T(8,128)(2,1)} %get-tuple-element.31.refs_4_.refs_0_) | copy-start | bytes 1572868
  7.4 1.0 %copy-start.2 = (bf16[128,2048]{1,0:T(8,128)(2,1)S(1)}, bf16[128,2048]{1,0:T(8,128)(2,1)}, u32[]{:S(2)}) copy-start(bf16[128,2048]{1,0:T(8,128)(2,1)} %get-tuple-element.32.refs_0_) | copy-start | bytes 1572868
  8.4 1.0 %copy-start.3 = (bf16[128,1536]{1,0:T(8,128)(2,1)S(1)}, bf16[128,1536]{1,0:T(8,128)(2,1)}, u32[]{:S(2)}) copy-start(bf16[128,1536]{1,0:T(8,128)(2,1)} %get-tuple-element.33.refs_1_) | copy-start | bytes 1179652
  9.4 0.9 %copy-start.4 = (bf16[128,1024]{1,0:T(8,128)(2,1)S(1)}, bf16[128,1024]{1,0:T(8,128)(2,1)}, u32[]{:S(2)}) copy-start(bf16[128,1024]{1,0:T(8,128)(2,1)} %get-tuple-element.34.refs_2_) | copy-start | bytes 786436
  30.3 5.7 %copy-start.5 = (bf16[128,1024]{1,0:T(8,128)(2,1)S(1)}, bf16[128,1024]{1,0:T(8,128)(2,1)}, u32[]{:S(2)}) copy-start(bf16[128,1024]{1,0:T(8,128)(2,1)} %get-tuple-element.34.refs_2_) | copy-start | bytes 786436
  30.4 1.6 %collective-permute-start.1 = (bf16[128,1024]{1,0:T(8,128)(2,1)S(1)}, bf16[128,1024]{1,0:T(8,128)(2,1)S(1)}, u32[]{:S(2)}, u32[]{:S(2)}) collective-permute-start(bf16[128,1024]{1,0:T(8,128)(2,1)S(1)} %get-tuple-element.37), channel_id=1, source_target_pairs={{0,1},{1,0},{2,3},{3,2},{4,5},{5,4},{6,7},{7,6},{8,9},{9,8},{10,11... | collective-permute-start | bytes 786440 | tf_op jit(solution)/shard_map/ppermute | solution.py:384
  30.4 1.9 %collective-permute-start.2 = (bf16[128,1024]{1,0:T(8,128)(2,1)S(1)}, bf16[128,1024]{1,0:T(8,128)(2,1)S(1)}, u32[]{:S(2)}, u32[]{:S(2)}) collective-permute-start(bf16[128,1024]{1,0:T(8,128)(2,1)S(1)} %get-tuple-element.38), channel_id=1, source_target_pairs={{0,1},{1,0},{2,3},{3,2},{4,5},{5,4},{6,7},{7,6},{8,9},{9,8},{10,11... | collective-permute-start | bytes 786440 | tf_op jit(solution)/shard_map/ppermute | solution.py:384
  32.4 10.6 %collective-permute-start.4 = (bf16[64,2048]{1,0:T(8,128)(2,1)S(1)}, bf16[64,2048]{1,0:T(8,128)(2,1)S(1)}, u32[]{:S(2)}, u32[]{:S(2)}) collective-permute-start(bf16[64,2048]{1,0:T(8,128)(2,1)S(1)} %get-tuple-element.40.refs_3_), channel_id=1, source_target_pairs={{0,4},{4,0},{8,12},{12,8},{1,5},{5,1},{9,13},{13,9},{2,6},{6,2},{1... | collective-permute-start | bytes 786440 | tf_op jit(solution)/shard_map/ppermute | solution.py:387
  34.5 12.0 %collective-permute-start.6 = (bf16[128,1536]{1,0:T(8,128)(2,1)S(1)}, bf16[128,1536]{1,0:T(8,128)(2,1)S(1)}, u32[]{:S(2)}, u32[]{:S(2)}) collective-permute-start(bf16[128,1536]{1,0:T(8,128)(2,1)S(1)} %copy-done.3), channel_id=1, source_target_pairs={{0,2},{2,0},{1,3},{3,1},{4,6},{6,4},{5,7},{7,5},{8,10},{10,8},{9,1... | collective-permute-start | bytes 1179656 | tf_op jit(solution)/shard_map/ppermute | solution.py:415
  36.0 19.3 %collective-permute-start.10 = (bf16[128,1024]{1,0:T(8,128)(2,1)S(1)}, bf16[128,1024]{1,0:T(8,128)(2,1)S(1)}, u32[]{:S(2)}, u32[]{:S(2)}) collective-permute-start(bf16[128,1024]{1,0:T(8,128)(2,1)S(1)} %copy-done.5), channel_id=1, source_target_pairs={{0,2},{2,0},{1,3},{3,1},{4,6},{6,4},{5,7},{7,5},{8,10},{10,8},{9,1... | collective-permute-start | bytes 786440 | tf_op jit(solution)/shard_map/ppermute | solution.py:415
  43.0 2.7 %copy-start.6 = (s32[4096]{0:T(1024)S(1)}, s32[4096]{0:T(1024)}, u32[]{:S(2)}) copy-start(s32[4096]{0:T(1024)} %param.6) | copy-start | bytes 49156
  43.1 8.6 %collective-permute-start.5 = (bf16[32,2048]{1,0:T(8,128)(2,1)S(1)}, bf16[32,2048]{1,0:T(8,128)(2,1)S(1)}, u32[]{:S(2)}, u32[]{:S(2)}) collective-permute-start(bf16[32,2048]{1,0:T(8,128)(2,1)S(1)} %get-tuple-element.43.refs_3_), channel_id=1, source_target_pairs={{0,8},{4,12},{8,0},{12,4},{1,9},{5,13},{9,1},{13,5},{2,10},{6,14},... | collective-permute-start | bytes 393224 | tf_op jit(solution)/shard_map/ppermute | solution.py:387
  45.8 5.9 %copy-start.1 = (f32[128,128]{1,0:T(8,128)S(1)}, f32[128,128]{1,0:T(8,128)}, u32[]{:S(2)}) copy-start(f32[128,128]{1,0:T(8,128)} %constant.9.clone.rotation_ref) | copy-start | bytes 196612
  52.2 8.3 %collective-permute-start.7 = (bf16[32,2048]{1,0:T(8,128)(2,1)S(1)}, bf16[32,2048]{1,0:T(8,128)(2,1)S(1)}, u32[]{:S(2)}, u32[]{:S(2)}) collective-permute-start(bf16[32,2048]{1,0:T(8,128)(2,1)S(1)} %get-tuple-element.44.refs_3_.refs_0_), channel_id=1, source_target_pairs={{0,4},{4,0},{8,12},{12,8},{1,5},{5,1},{9,13},{13,9},{2,6},{6,2},{1... | collective-permute-start | bytes 393224 | tf_op jit(solution)/shard_map/ppermute | solution.py:387
  52.3 9.0 %collective-permute-start.8 = (bf16[32,2048]{1,0:T(8,128)(2,1)S(1)}, bf16[32,2048]{1,0:T(8,128)(2,1)S(1)}, u32[]{:S(2)}, u32[]{:S(2)}) collective-permute-start(bf16[32,2048]{1,0:T(8,128)(2,1)S(1)} %get-tuple-element.44.refs_3_.refs_0_), channel_id=1, source_target_pairs={{0,8},{4,12},{8,0},{12,4},{1,9},{5,13},{9,1},{13,5},{2,10},{6,14},... | collective-permute-start | bytes 393224 | tf_op jit(solution)/shard_map/ppermute | solution.py:387
  57.8 3.4 %collective-permute-start.11 = (bf16[128,1024]{1,0:T(8,128)(2,1)S(1)}, bf16[128,1024]{1,0:T(8,128)(2,1)S(1)}, u32[]{:S(2)}, u32[]{:S(2)}) collective-permute-start(bf16[128,1024]{1,0:T(8,128)(2,1)S(1)} %get-tuple-element.46.refs_3_), channel_id=1, source_target_pairs={{0,1},{1,0},{2,3},{3,2},{4,5},{5,4},{6,7},{7,6},{8,9},{9,8},{10,11... | collective-permute-start | bytes 786440 | tf_op jit(solution)/shard_map/ppermute | solution.py:384
  61.3 1.5 %collective-permute-start.13 = (bf16[128,1024]{1,0:T(8,128)(2,1)S(1)}, bf16[128,1024]{1,0:T(8,128)(2,1)S(1)}, u32[]{:S(2)}, u32[]{:S(2)}) collective-permute-start(bf16[128,1024]{1,0:T(8,128)(2,1)S(1)} %shard_map.70), channel_id=1, source_target_pairs={{0,1},{1,0},{2,3},{3,2},{4,5},{5,4},{6,7},{7,6},{8,9},{9,8},{10,11... | collective-permute-start | bytes 786440 | tf_op jit(solution)/shard_map/ppermute | solution.py:384
  61.4 6.4 %collective-permute-start.12 = (bf16[64,1024]{1,0:T(8,128)(2,1)S(1)}, bf16[64,1024]{1,0:T(8,128)(2,1)S(1)}, u32[]{:S(2)}, u32[]{:S(2)}) collective-permute-start(bf16[64,1024]{1,0:T(8,128)(2,1)S(1)} %get-tuple-element.48), channel_id=1, source_target_pairs={{0,4},{4,0},{8,12},{12,8},{1,5},{5,1},{9,13},{13,9},{2,6},{6,2},{1... | collective-permute-start | bytes 393224 | tf_op jit(solution)/shard_map/ppermute | solution.py:387
  62.9 7.6 %collective-permute-start.15 = (bf16[64,1024]{1,0:T(8,128)(2,1)S(1)}, bf16[64,1024]{1,0:T(8,128)(2,1)S(1)}, u32[]{:S(2)}, u32[]{:S(2)}) collective-permute-start(bf16[64,1024]{1,0:T(8,128)(2,1)S(1)} %get-tuple-element.51.refs_2_), channel_id=1, source_target_pairs={{0,4},{4,0},{8,12},{12,8},{1,5},{5,1},{9,13},{13,9},{2,6},{6,2},{1... | collective-permute-start | bytes 393224 | tf_op jit(solution)/shard_map/ppermute | solution.py:387
  63.9 13.4 %collective-permute-start.9 = (bf16[32,2048]{1,0:T(8,128)(2,1)S(1)}, bf16[32,2048]{1,0:T(8,128)(2,1)S(1)}, u32[]{:S(2)}, u32[]{:S(2)}) collective-permute-start(bf16[32,2048]{1,0:T(8,128)(2,1)S(1)} %collective-permute-done.8.refs_2_.refs_1_), channel_id=1, source_target_pairs={{0,4},{4,0},{8,12},{12,8},{1,5},{5,1},{9,13},{13,9},{2,6},{6,2},{1... | collective-permute-start | bytes 393224 | tf_op jit(solution)/shard_map/ppermute | solution.py:387
  67.7 5.8 %collective-permute-start.14 = (bf16[32,1024]{1,0:T(8,128)(2,1)S(1)}, bf16[32,1024]{1,0:T(8,128)(2,1)S(1)}, u32[]{:S(2)}, u32[]{:S(2)}) collective-permute-start(bf16[32,1024]{1,0:T(8,128)(2,1)S(1)} %get-tuple-element.53), channel_id=1, source_target_pairs={{0,8},{4,12},{8,0},{12,4},{1,9},{5,13},{9,1},{13,5},{2,10},{6,14},... | collective-permute-start | bytes 196616 | tf_op jit(solution)/shard_map/ppermute | solution.py:387
  70.6 7.4 %collective-permute-start.19 = (bf16[32,1024]{1,0:T(8,128)(2,1)S(1)}, bf16[32,1024]{1,0:T(8,128)(2,1)S(1)}, u32[]{:S(2)}, u32[]{:S(2)}) collective-permute-start(bf16[32,1024]{1,0:T(8,128)(2,1)S(1)} %get-tuple-element.56.refs_0_), channel_id=1, source_target_pairs={{0,8},{4,12},{8,0},{12,4},{1,9},{5,13},{9,1},{13,5},{2,10},{6,14},... | collective-permute-start | bytes 196616 | tf_op jit(solution)/shard_map/ppermute | solution.py:387
  73.9 9.2 %collective-permute-start.17 = (bf16[32,1152]{1,0:T(8,128)(2,1)S(1)}, bf16[32,1152]{1,0:T(8,128)(2,1)S(1)}, u32[]{:S(2)}, u32[]{:S(2)}) collective-permute-start(bf16[32,1152]{1,0:T(8,128)(2,1)S(1)} %shard_map.74.refs_4_), channel_id=1, source_target_pairs={{0,8},{4,12},{8,0},{12,4},{1,9},{5,13},{9,1},{13,5},{2,10},{6,14},... | collective-permute-start | bytes 221192 | tf_op jit(solution)/shard_map/ppermute | solution.py:387
  78.3 6.8 %collective-permute-start.21 = (bf16[32,1152]{1,0:T(8,128)(2,1)S(1)}, bf16[32,1152]{1,0:T(8,128)(2,1)S(1)}, u32[]{:S(2)}, u32[]{:S(2)}) collective-permute-start(bf16[32,1152]{1,0:T(8,128)(2,1)S(1)} %shard_map.76.refs_4_), channel_id=1, source_target_pairs={{0,8},{4,12},{8,0},{12,4},{1,9},{5,13},{9,1},{13,5},{2,10},{6,14},... | collective-permute-start | bytes 221192 | tf_op jit(solution)/shard_map/ppermute | solution.py:387
  78.4 7.4 %collective-permute-start.16 = (bf16[32,1152]{1,0:T(8,128)(2,1)S(1)}, bf16[32,1152]{1,0:T(8,128)(2,1)S(1)}, u32[]{:S(2)}, u32[]{:S(2)}) collective-permute-start(bf16[32,1152]{1,0:T(8,128)(2,1)S(1)} %shard_map.74.refs_4_), channel_id=1, source_target_pairs={{0,4},{4,0},{8,12},{12,8},{1,5},{5,1},{9,13},{13,9},{2,6},{6,2},{1... | collective-permute-start | bytes 221192 | tf_op jit(solution)/shard_map/ppermute | solution.py:387
  83.0 4.8 %collective-permute-start.18 = (bf16[32,1152]{1,0:T(8,128)(2,1)S(1)}, bf16[32,1152]{1,0:T(8,128)(2,1)S(1)}, u32[]{:S(2)}, u32[]{:S(2)}) collective-permute-start(bf16[32,1152]{1,0:T(8,128)(2,1)S(1)} %collective-permute-done.17.refs_6_), channel_id=1, source_target_pairs={{0,4},{4,0},{8,12},{12,8},{1,5},{5,1},{9,13},{13,9},{2,6},{6,2},{1... | collective-permute-start | bytes 221192 | tf_op jit(solution)/shard_map/ppermute | solution.py:387
  83.0 5.9 %collective-permute-start.20 = (bf16[32,1152]{1,0:T(8,128)(2,1)S(1)}, bf16[32,1152]{1,0:T(8,128)(2,1)S(1)}, u32[]{:S(2)}, u32[]{:S(2)}) collective-permute-start(bf16[32,1152]{1,0:T(8,128)(2,1)S(1)} %shard_map.76.refs_4_), channel_id=1, source_target_pairs={{0,4},{4,0},{8,12},{12,8},{1,5},{5,1},{9,13},{13,9},{2,6},{6,2},{1... | collective-permute-start | bytes 221192 | tf_op jit(solution)/shard_map/ppermute | solution.py:387
  85.1 4.7 %collective-permute-start.22 = (bf16[32,1152]{1,0:T(8,128)(2,1)S(1)}, bf16[32,1152]{1,0:T(8,128)(2,1)S(1)}, u32[]{:S(2)}, u32[]{:S(2)}) collective-permute-start(bf16[32,1152]{1,0:T(8,128)(2,1)S(1)} %collective-permute-done.21.refs_6_), channel_id=1, source_target_pairs={{0,4},{4,0},{8,12},{12,8},{1,5},{5,1},{9,13},{13,9},{2,6},{6,2},{1... | collective-permute-start | bytes 221192 | tf_op jit(solution)/shard_map/ppermute | solution.py:387
  88.0 2.9 %collective-permute-start.23 = (bf16[128,1152]{1,0:T(8,128)(2,1)S(1)}, bf16[128,1152]{1,0:T(8,128)(2,1)S(1)}, u32[]{:S(2)}, u32[]{:S(2)}) collective-permute-start(bf16[128,1152]{1,0:T(8,128)(2,1)S(1)} %shard_map.79), channel_id=1, source_target_pairs={{0,1},{1,0},{2,3},{3,2},{4,5},{5,4},{6,7},{7,6},{8,9},{9,8},{10,11... | collective-permute-start | bytes 884744 | tf_op jit(solution)/shard_map/ppermute | solution.py:384
  89.9 1.6 %collective-permute-start.24 = (bf16[128,1152]{1,0:T(8,128)(2,1)S(1)}, bf16[128,1152]{1,0:T(8,128)(2,1)S(1)}, u32[]{:S(2)}, u32[]{:S(2)}) collective-permute-start(bf16[128,1152]{1,0:T(8,128)(2,1)S(1)} %shard_map.80), channel_id=1, source_target_pairs={{0,1},{1,0},{2,3},{3,2},{4,5},{5,4},{6,7},{7,6},{8,9},{9,8},{10,11... | collective-permute-start | bytes 884744 | tf_op jit(solution)/shard_map/ppermute | solution.py:384

commit v14 on v13

--- a/solution.py
+++ b/solution.py
@@ -10,11 +10,10 @@
 from jax.sharding import PartitionSpec as P
 
 BLOCK = 128
-UNIT = 512
+UNIT = 256
 GROUPS = 2
 VMEM_LIMIT = 6 * 2**20
-SLICE_LIMIT = 61 * 2**20 + 2**19
-SHARES = (4, 4, 3)
+SHARES = (8, 7, 6)
 epsilon = 1e-06
 
 SMALL = pl.CostEstimate(flops=1, bytes_accessed=1, transcendentals=0)
@@ -51,7 +50,7 @@
         in_specs=[HBM],
         out_specs=[VMEM] * len(places),
         scratch_shapes=[pltpu.SemaphoreType.DMA((len(places),))],
-        compiler_params=pltpu.CompilerParams(vmem_limit_bytes=SLICE_LIMIT),
+        compiler_params=PARAMS,
         cost_estimate=SMALL,
     )(values)
 
@@ -313,26 +312,27 @@
 def place_body(mine, half, width, count, held, *refs):
     refs = refs[held:]
     scaled = len(refs) > count + 2
-    codes_ref, sems = refs[-3 if scaled else -2], refs[-1]
+    codes_ref, sems = refs[2 * count if scaled else count], refs[-1]
     sub = lax.axis_index("sub")
     side = sub if mine else 1 - sub
 
-    def copies(core):
-        return [
+    def put(core):
+        copies = [
             pltpu.make_async_copy(
                 refs[group].at[:, :width], codes_ref.at[:, pl.ds(core * half + group * width, width)], sems.at[group]
             )
             for group in range(count)
         ]
-
-    def put(core):
-        for copy in copies(core):
+        for copy in copies:
             copy.start()
         if scaled:
+            out_ref, flat = refs[2 * count + 1 : 2 * count + 3]
             order = refs[count : 2 * count] + refs[:count] if core else refs[: 2 * count]
             scales = [ref[:, width : width + width // BLOCK].astype(jnp.float32) for ref in order]
-            refs[-2][...] = jnp.concatenate(scales, axis=1).T.astype(jnp.bfloat16)
-        for copy in copies(core):
+            flat[...] = jnp.concatenate(scales, axis=1).T.astype(jnp.bfloat16)
+            copies.append(pltpu.make_async_copy(flat, out_ref, sems.at[count]))
+            copies[-1].start()
+        for copy in copies:
             copy.wait()
 
     for core in range(2):
@@ -343,28 +343,28 @@
     rows = arrays[0].shape[0]
     operands = list(arrays) + list(mine_too)
     out_shape = [jax.ShapeDtypeStruct((rows, 2 * half), jnp.bfloat16)]
-    out_specs = [HBM]
+    scratch = [pltpu.SemaphoreType.DMA((len(arrays) + 1,))]
     if mine_too:
         out_shape.append(jax.ShapeDtypeStruct((2 * half // BLOCK, rows), jnp.bfloat16))
-        out_specs.append(VMEM)
+        scratch.insert(0, pltpu.VMEM((2 * half // BLOCK, rows), jnp.bfloat16))
     held = [] if codes is None else [codes]
     return pl.pallas_call(
         functools.partial(place_body, mine, half, width, len(arrays), len(held)),
         out_shape=out_shape,
         in_specs=[HBM] * len(held) + [VMEM] * len(operands),
-        out_specs=out_specs,
+        out_specs=[HBM] * len(out_shape),
         input_output_aliases={0: 0} if held else {},
-        scratch_shapes=[pltpu.SemaphoreType.DMA((len(arrays),))],
+        scratch_shapes=scratch,
         compiler_params=PARAMS,
         cost_estimate=SMALL,
     )(*held, *operands)
 
 
 def cut(depth):
-    if depth % UNIT or depth < 8 * UNIT:
+    if depth % UNIT or depth < 16 * UNIT:
         return [depth]
     units = depth // UNIT
-    sizes = [max(1, units * share // 13) for share in SHARES]
+    sizes = [max(1, units * share // 26) for share in SHARES]
     return [size * UNIT for size in sizes + [units - sum(sizes)]]
 
 

time: 93.2 us -> 87.1 us (0.935)
  Pallas kernels: 43.3 us -> 40.3 us
  starting transfers between devices: 27.6 us -> 24.9 us
  local copies, waits for them, and re-layouts: 4.05 us -> 1.46 us
  waiting for transfers between devices: 17 us -> 19.3 us
    ppermute x15, starting transfers between devices: 21.8 us -> 18.5 us  [exchange(): lax.ppermute(values, 'tensor', [(t, t ^ 1 << level) for t in range(tensor...]
    unnamed x14 -> x6, local copies, waits for them, and re-layouts: 4.04 us -> 1.46 us
    pallas_call x1, Pallas kernels: 2.6 us -> 0.16 us  [slices_of(): pl.pallas_call(functools.partial(slice_body, places), out_shape=[jax.Shap...]
    ppermute x4, waiting for transfers between devices: 0.72 us -> 2.5 us  [shards(): arrivals.append([lax.ppermute(part, 'seq', pairs) for part in parts])]
    ppermute x15, waiting for transfers between devices: 14.2 us -> 16 us  [exchange(): lax.ppermute(values, 'tensor', [(t, t ^ 1 << level) for t in range(tensor...]
    ppermute x6, waiting for transfers between devices: 2.03 us -> 0.87 us  [swap(): return lax.ppermute(values, 'sub', [(0, 1), (1, 0)])]
  transfers between devices with their start and end apart: 25 -> 25, of which waited for: 14 -> 13; matrix products, arithmetic and copies ran while one was open for 0% -> 0% of each run, Pallas kernels for 42% -> 45%
where the time goes in v14:
time: 87.1 us; the launch traced here: 87 us
  Pallas kernels  40.3 us (46%)
  starting transfers between devices  24.9 us (29%)
  waiting for transfers between devices  19.3 us (22%)
  local copies, waits for them, and re-layouts  1.46 us (2%)
  between operations  0.93 us (1%)
    pallas_call x6, Pallas kernels, multiply(): pl.pallas_call(body, out_shape=out_shape, in_specs=[VMEM] * spans[-1][1]...  36.8 us
    ppermute x15, starting transfers between devices, exchange(): lax.ppermute(values, 'tensor', [(t, t ^ 1 << level) for t in range(tensor...  18.5 us
    ppermute x15, waiting for transfers between devices, exchange(): lax.ppermute(values, 'tensor', [(t, t ^ 1 << level) for t in range(tensor...  16 us
    ppermute x4, starting transfers between devices, shards(): arrivals.append([lax.ppermute(part, 'seq', pairs) for part in parts])  5.11 us
    ppermute x4, waiting for transfers between devices, shards(): arrivals.append([lax.ppermute(part, 'seq', pairs) for part in parts])  2.5 us
  transfers between devices with their start and end apart: 25, of which 13 were waited for; matrix products, arithmetic and copies ran while one was open for 0% of the time, Pallas kernels for 45%

profile of v14, /device:TPU:0, one launch (start us, length us, event | category | flops | bytes accessed | tf_op | source)
XLA Modules:
  0.0 87.0 jit_solution(14550565250267230267)
XLA Ops:
  0.6 1.4 %copy-done = bf16[128,6656]{1,0:T(8,128)(2,1)S(1)} copy-done((bf16[128,6656]{1,0:T(8,128)(2,1)S(1)}, bf16[128,6656]{1,0:T(8,128)(2,1)}, u32[]{:S(2)}) %copy-start) | copy-done | bytes 1703960
  2.1 0.2 shard_map.59
  2.3 3.0 %collective-permute-start = (bf16[128,2048]{1,0:T(8,128)(2,1)S(1)}, bf16[128,2048]{1,0:T(8,128)(2,1)S(1)}, u32[]{:S(2)}, u32[]{:S(2)}) collective-permute-start(bf16[128,2048]{1,0:T(8,128)(2,1)S(1)} %get-tuple-element.31.refs_4_.refs_0_), channel_id=1, source_target_pairs={{0,2},{2,0},{1,3},{3,1},{4,6},{6,4},{5,7},{7,5},{8,10},{10,8},{9,1... | collective-permute-start | bytes 1572872 | tf_op jit(solution)/shard_map/ppermute | solution.py:415
  5.3 0.1 collective-permute-start.3
  5.3 12.7 %shard_map.60.refs_3_ = f32[128,4096]{1,0:T(8,128)S(1)} custom-call(bf16[128,1792]{1,0:T(8,128)(2,1)S(1)} %get-tuple-element.32.refs_0_, bf16[128,1536]{1,0:T(8,128)(2,1)S(1)} %get-tuple-element.33.refs_1_, bf16[128,1280]{1,0:T(8,128)(2,1)S(1)} %get-tuple-element.34.refs_2_, bf16[6656,4096]{1,0:T(8,128)(2,1)} %refs_1_.7, ...), custom_call_target="tpu_custom_call" | custom-call | flops 1 | bytes 1 | tf_op jit(solution)/shard_map/pallas_call | solution.py:139
  18.0 7.3 %shard_map.61 = (bf16[128,1024]{1,0:T(8,128)(2,1)S(1)}, f32[128,1024]{1,0:T(8,128)S(1)}, bf16[128,1024]{1,0:T(8,128)(2,1)S(1)}, f32[128,1024]{1,0:T(8,128)S(1)}, f32[128,4096]{1,0:T(8,128)S(1)}) custom-call(bf16[128,2048]{1,0:T(8,128)(2,1)S(1)} %get-tuple-element.31.refs_4_.refs_0_, bf16[128,2048]{1,0:T(8,128)(2,1)S(1)} %collective-permute-done.refs_1_, ...), custom_call_target="tpu_custom_call" | custom-call | flops 1 | bytes 1 | tf_op jit(solution)/shard_map/pallas_call | solution.py:139
  25.4 0.5 collective-permute-start.2
  25.9 1.1 %collective-permute-done.3.refs_4_.refs_0_ = bf16[128,1792]{1,0:T(8,128)(2,1)S(1)} collective-permute-done((bf16[128,1792]{1,0:T(8,128)(2,1)S(1)}, bf16[128,1792]{1,0:T(8,128)(2,1)S(1)}, u32[]{:S(2)}, u32[]{:S(2)}) %collective-permute-start.3) | collective-permute-done | bytes 458784 | tf_op jit(solution)/shard_map/ppermute | solution.py:415
  27.0 0.3 collective-permute-done.2.refs_3_
  27.3 0.1 shard_map.62
  27.4 2.2 %collective-permute-start.4 = (bf16[64,2048]{1,0:T(8,128)(2,1)S(1)}, bf16[64,2048]{1,0:T(8,128)(2,1)S(1)}, u32[]{:S(2)}, u32[]{:S(2)}) collective-permute-start(bf16[64,2048]{1,0:T(8,128)(2,1)S(1)} %get-tuple-element.40.refs_3_), channel_id=1, source_target_pairs={{0,4},{4,0},{8,12},{12,8},{1,5},{5,1},{9,13},{13,9},{2,6},{6,2},{1... | collective-permute-start | bytes 786440 | tf_op jit(solution)/shard_map/ppermute | solution.py:387
  29.6 1.5 %collective-permute-start.6 = (bf16[128,1536]{1,0:T(8,128)(2,1)S(1)}, bf16[128,1536]{1,0:T(8,128)(2,1)S(1)}, u32[]{:S(2)}, u32[]{:S(2)}) collective-permute-start(bf16[128,1536]{1,0:T(8,128)(2,1)S(1)} %get-tuple-element.33.refs_1_), channel_id=1, source_target_pairs={{0,2},{2,0},{1,3},{3,1},{4,6},{6,4},{5,7},{7,5},{8,10},{10,8},{9,1... | collective-permute-start | bytes 1179656 | tf_op jit(solution)/shard_map/ppermute | solution.py:415
  31.0 0.5 collective-permute-start.10
  31.6 5.8 %shard_map.63.refs_2_ = f32[128,4096]{1,0:T(8,128)S(1)} custom-call(bf16[128,1792]{1,0:T(8,128)(2,1)S(1)} %collective-permute-done.3.refs_4_.refs_0_, bf16[6656,4096]{1,0:T(8,128)(2,1)} %refs_1_.7, f32[128,4096]{1,0:T(8,128)S(1)} %get-tuple-element.41.refs_2_, bf16[64,2048]{1,0:T(8,128)(2,1)S(1)} %get-tuple-element.40.refs_3_), custom_call_target="tpu_custom_call" | custom-call | flops 1 | bytes 1 | tf_op jit(solution)/shard_map/pallas_call | solution.py:139
  37.5 2.6 %collective-permute-start.5 = (bf16[32,2048]{1,0:T(8,128)(2,1)S(1)}, bf16[32,2048]{1,0:T(8,128)(2,1)S(1)}, u32[]{:S(2)}, u32[]{:S(2)}) collective-permute-start(bf16[32,2048]{1,0:T(8,128)(2,1)S(1)} %get-tuple-element.43.refs_3_), channel_id=1, source_target_pairs={{0,8},{4,12},{8,0},{12,4},{1,9},{5,13},{9,1},{13,5},{2,10},{6,14},... | collective-permute-start | bytes 393224 | tf_op jit(solution)/shard_map/ppermute | solution.py:387
  40.2 1.4 %collective-permute-done.6.refs_0_ = bf16[128,1536]{1,0:T(8,128)(2,1)S(1)} collective-permute-done((bf16[128,1536]{1,0:T(8,128)(2,1)S(1)}, bf16[128,1536]{1,0:T(8,128)(2,1)S(1)}, u32[]{:S(2)}, u32[]{:S(2)}) %collective-permute-start.6) | collective-permute-done | bytes 393248 | tf_op jit(solution)/shard_map/ppermute | solution.py:415
  41.6 5.2 %shard_map.65.refs_0_.refs_2_ = f32[128,4096]{1,0:T(8,128)S(1)} custom-call(bf16[128,1536]{1,0:T(8,128)(2,1)S(1)} %collective-permute-done.6.refs_0_, bf16[6656,4096]{1,0:T(8,128)(2,1)} %refs_1_.7, f32[128,4096]{1,0:T(8,128)S(1)} %shard_map.63.refs_2_, bf16[32,2048]{1,0:T(8,128)(2,1)S(1)} %get-tuple-element.43.refs_3_), custom_call_target="tpu_custom_call" | custom-call | flops 1 | bytes 1 | tf_op jit(solution)/shard_map/pallas_call | solution.py:139
  46.8 0.5 shard_map.66
  47.2 0.1 collective-permute-start.7
  47.3 3.0 %collective-permute-start.8 = (bf16[32,2048]{1,0:T(8,128)(2,1)S(1)}, bf16[32,2048]{1,0:T(8,128)(2,1)S(1)}, u32[]{:S(2)}, u32[]{:S(2)}) collective-permute-start(bf16[32,2048]{1,0:T(8,128)(2,1)S(1)} %get-tuple-element.44.refs_3_.refs_0_), channel_id=1, source_target_pairs={{0,8},{4,12},{8,0},{12,4},{1,9},{5,13},{9,1},{13,5},{2,10},{6,14},... | collective-permute-start | bytes 393224 | tf_op jit(solution)/shard_map/ppermute | solution.py:387
  50.3 2.9 %shard_map.67 = (bf16[128,1024]{1,0:T(8,128)(2,1)S(1)}, f32[128,1024]{1,0:T(8,128)S(1)}) custom-call(bf16[128,1280]{1,0:T(8,128)(2,1)S(1)} %collective-permute-done.10.refs_0_, bf16[6656,4096]{1,0:T(8,128)(2,1)} %refs_1_.7, f32[128,4096]{1,0:T(8,128)S(1)} %shard_map.65.refs_0_.refs_2_, bf16[32,2048]{1,0:T(8,128)(2,1)S(1)} %get-tuple-element.44.refs_3_.refs_0_), custom_call_target="tpu_custom_call" | custom-call | flops 1 | bytes 1 | tf_op jit(solution)/shard_map/pallas_call | solution.py:139
  53.2 0.1 collective-permute-start.11
  53.3 2.9 %shard_map.69 = (bf16[128,1024]{1,0:T(8,128)(2,1)S(1)}, f32[128,1024]{1,0:T(8,128)S(1)}) custom-call(bf16[128,1280]{1,0:T(8,128)(2,1)S(1)} %collective-permute-done.10.refs_0_, bf16[6656,4096]{1,0:T(8,128)(2,1)} %refs_1_.7, f32[128,4096]{1,0:T(8,128)S(1)} %shard_map.65.refs_0_.refs_2_, bf16[128,1024]{1,0:T(8,128)(2,1)S(1)} %get-tuple-element.46.refs_3_), custom_call_target="tpu_custom_call" | custom-call | flops 1 | bytes 1 | tf_op jit(solution)/shard_map/pallas_call | solution.py:139
  56.3 0.5 collective-permute-start.13
  56.9 1.6 %collective-permute-start.12 = (bf16[64,1024]{1,0:T(8,128)(2,1)S(1)}, bf16[64,1024]{1,0:T(8,128)(2,1)S(1)}, u32[]{:S(2)}, u32[]{:S(2)}) collective-permute-start(bf16[64,1024]{1,0:T(8,128)(2,1)S(1)} %get-tuple-element.48), channel_id=1, source_target_pairs={{0,4},{4,0},{8,12},{12,8},{1,5},{5,1},{9,13},{13,9},{2,6},{6,2},{1... | collective-permute-start | bytes 393224 | tf_op jit(solution)/shard_map/ppermute | solution.py:387
  58.6 1.1 %collective-permute-start.15 = (bf16[64,1024]{1,0:T(8,128)(2,1)S(1)}, bf16[64,1024]{1,0:T(8,128)(2,1)S(1)}, u32[]{:S(2)}, u32[]{:S(2)}) collective-permute-start(bf16[64,1024]{1,0:T(8,128)(2,1)S(1)} %get-tuple-element.51.refs_2_), channel_id=1, source_target_pairs={{0,4},{4,0},{8,12},{12,8},{1,5},{5,1},{9,13},{13,9},{2,6},{6,2},{1... | collective-permute-start | bytes 393224 | tf_op jit(solution)/shard_map/ppermute | solution.py:387
  59.7 1.0 %collective-permute-start.9 = (bf16[32,2048]{1,0:T(8,128)(2,1)S(1)}, bf16[32,2048]{1,0:T(8,128)(2,1)S(1)}, u32[]{:S(2)}, u32[]{:S(2)}) collective-permute-start(bf16[32,2048]{1,0:T(8,128)(2,1)S(1)} %collective-permute-done.8.refs_2_.refs_1_), channel_id=1, source_target_pairs={{0,4},{4,0},{8,12},{12,8},{1,5},{5,1},{9,13},{13,9},{2,6},{6,2},{1... | collective-permute-start | bytes 393224 | tf_op jit(solution)/shard_map/ppermute | solution.py:387
  60.7 2.7 %collective-permute-done.12.refs_1_ = bf16[64,1024]{1,0:T(8,128)(2,1)S(1)} collective-permute-done((bf16[64,1024]{1,0:T(8,128)(2,1)S(1)}, bf16[64,1024]{1,0:T(8,128)(2,1)S(1)}, u32[]{:S(2)}, u32[]{:S(2)}) %collective-permute-start.12) | collective-permute-done | bytes 131104 | tf_op jit(solution)/shard_map/ppermute | solution.py:387
  63.4 0.3 collective-permute-start.14
  63.7 3.2 %collective-permute-done.15.refs_1_ = bf16[64,1024]{1,0:T(8,128)(2,1)S(1)} collective-permute-done((bf16[64,1024]{1,0:T(8,128)(2,1)S(1)}, bf16[64,1024]{1,0:T(8,128)(2,1)S(1)}, u32[]{:S(2)}, u32[]{:S(2)}) %collective-permute-start.15) | collective-permute-done | bytes 131104 | tf_op jit(solution)/shard_map/ppermute | solution.py:387
  66.9 4.3 %collective-permute-done.14.came_ref = bf16[32,1024]{1,0:T(8,128)(2,1)S(1)} collective-permute-done((bf16[32,1024]{1,0:T(8,128)(2,1)S(1)}, bf16[32,1024]{1,0:T(8,128)(2,1)S(1)}, u32[]{:S(2)}, u32[]{:S(2)}) %collective-permute-start.14) | collective-permute-done | bytes 65568 | tf_op jit(solution)/shard_map/ppermute | solution.py:387
  71.3 0.3 shard_map.74.refs_4_
  71.6 1.5 %collective-permute-start.17 = (bf16[32,1152]{1,0:T(8,128)(2,1)S(1)}, bf16[32,1152]{1,0:T(8,128)(2,1)S(1)}, u32[]{:S(2)}, u32[]{:S(2)}) collective-permute-start(bf16[32,1152]{1,0:T(8,128)(2,1)S(1)} %shard_map.74.refs_4_), channel_id=1, source_target_pairs={{0,8},{4,12},{8,0},{12,4},{1,9},{5,13},{9,1},{13,5},{2,10},{6,14},... | collective-permute-start | bytes 221192 | tf_op jit(solution)/shard_map/ppermute | solution.py:387
  73.2 0.3 shard_map.76.refs_4_
  73.5 1.5 %collective-permute-start.21 = (bf16[32,1152]{1,0:T(8,128)(2,1)S(1)}, bf16[32,1152]{1,0:T(8,128)(2,1)S(1)}, u32[]{:S(2)}, u32[]{:S(2)}) collective-permute-start(bf16[32,1152]{1,0:T(8,128)(2,1)S(1)} %shard_map.76.refs_4_), channel_id=1, source_target_pairs={{0,8},{4,12},{8,0},{12,4},{1,9},{5,13},{9,1},{13,5},{2,10},{6,14},... | collective-permute-start | bytes 221192 | tf_op jit(solution)/shard_map/ppermute | solution.py:387
  75.1 1.4 %collective-permute-start.16 = (bf16[32,1152]{1,0:T(8,128)(2,1)S(1)}, bf16[32,1152]{1,0:T(8,128)(2,1)S(1)}, u32[]{:S(2)}, u32[]{:S(2)}) collective-permute-start(bf16[32,1152]{1,0:T(8,128)(2,1)S(1)} %shard_map.74.refs_4_), channel_id=1, source_target_pairs={{0,4},{4,0},{8,12},{12,8},{1,5},{5,1},{9,13},{13,9},{2,6},{6,2},{1... | collective-permute-start | bytes 221192 | tf_op jit(solution)/shard_map/ppermute | solution.py:387
  76.5 1.6 %collective-permute-done.17.refs_6_ = bf16[32,1152]{1,0:T(8,128)(2,1)S(1)} collective-permute-done((bf16[32,1152]{1,0:T(8,128)(2,1)S(1)}, bf16[32,1152]{1,0:T(8,128)(2,1)S(1)}, u32[]{:S(2)}, u32[]{:S(2)}) %collective-permute-start.17) | collective-permute-done | bytes 73760 | tf_op jit(solution)/shard_map/ppermute | solution.py:387
  78.1 2.0 %collective-permute-start.20 = (bf16[32,1152]{1,0:T(8,128)(2,1)S(1)}, bf16[32,1152]{1,0:T(8,128)(2,1)S(1)}, u32[]{:S(2)}, u32[]{:S(2)}) collective-permute-start(bf16[32,1152]{1,0:T(8,128)(2,1)S(1)} %shard_map.76.refs_4_), channel_id=1, source_target_pairs={{0,4},{4,0},{8,12},{12,8},{1,5},{5,1},{9,13},{13,9},{2,6},{6,2},{1... | collective-permute-start | bytes 221192 | tf_op jit(solution)/shard_map/ppermute | solution.py:387
  80.1 0.6 collective-permute-done.16.refs_5_
  80.8 1.6 %collective-permute-done.18.refs_7_ = bf16[32,1152]{1,0:T(8,128)(2,1)S(1)} collective-permute-done((bf16[32,1152]{1,0:T(8,128)(2,1)S(1)}, bf16[32,1152]{1,0:T(8,128)(2,1)S(1)}, u32[]{:S(2)}, u32[]{:S(2)}) %collective-permute-start.18) | collective-permute-done | bytes 73760 | tf_op jit(solution)/shard_map/ppermute | solution.py:387
  82.4 0.1 shard_map.79
  82.6 0.7 collective-permute-done.20.refs_5_
  83.2 1.2 %collective-permute-done.22.refs_7_ = bf16[32,1152]{1,0:T(8,128)(2,1)S(1)} collective-permute-done((bf16[32,1152]{1,0:T(8,128)(2,1)S(1)}, bf16[32,1152]{1,0:T(8,128)(2,1)S(1)}, u32[]{:S(2)}, u32[]{:S(2)}) %collective-permute-start.22) | collective-permute-done | bytes 73760 | tf_op jit(solution)/shard_map/ppermute | solution.py:387
  84.4 0.1 shard_map.80
  84.6 0.1 shard_map.77.refs_1_.refs_4_
  84.7 0.8 shard_map.78.refs_0_
  85.6 0.6 collective-permute-done.24.refs_2_
  86.2 0.8 shard_map.81
  (33 shorter events, 0.7 us)
Async XLA Ops:
  0.6 1.5 %copy-start = (bf16[128,6656]{1,0:T(8,128)(2,1)S(1)}, bf16[128,6656]{1,0:T(8,128)(2,1)}, u32[]{:S(2)}) copy-start(bf16[128,6656]{1,0:T(8,128)(2,1)} %in_ref.1) | copy-start | bytes 5111812
  2.3 15.8 %collective-permute-start = (bf16[128,2048]{1,0:T(8,128)(2,1)S(1)}, bf16[128,2048]{1,0:T(8,128)(2,1)S(1)}, u32[]{:S(2)}, u32[]{:S(2)}) collective-permute-start(bf16[128,2048]{1,0:T(8,128)(2,1)S(1)} %get-tuple-element.31.refs_4_.refs_0_), channel_id=1, source_target_pairs={{0,2},{2,0},{1,3},{3,1},{4,6},{6,4},{5,7},{7,5},{8,10},{10,8},{9,1... | collective-permute-start | bytes 1572872 | tf_op jit(solution)/shard_map/ppermute | solution.py:415
  5.3 21.8 %collective-permute-start.3 = (bf16[128,1792]{1,0:T(8,128)(2,1)S(1)}, bf16[128,1792]{1,0:T(8,128)(2,1)S(1)}, u32[]{:S(2)}, u32[]{:S(2)}) collective-permute-start(bf16[128,1792]{1,0:T(8,128)(2,1)S(1)} %get-tuple-element.32.refs_0_), channel_id=1, source_target_pairs={{0,2},{2,0},{1,3},{3,1},{4,6},{6,4},{5,7},{7,5},{8,10},{10,8},{9,1... | collective-permute-start | bytes 1376264 | tf_op jit(solution)/shard_map/ppermute | solution.py:415
  25.3 1.7 %collective-permute-start.1 = (bf16[128,1024]{1,0:T(8,128)(2,1)S(1)}, bf16[128,1024]{1,0:T(8,128)(2,1)S(1)}, u32[]{:S(2)}, u32[]{:S(2)}) collective-permute-start(bf16[128,1024]{1,0:T(8,128)(2,1)S(1)} %get-tuple-element.37), channel_id=1, source_target_pairs={{0,1},{1,0},{2,3},{3,2},{4,5},{5,4},{6,7},{7,6},{8,9},{9,8},{10,11... | collective-permute-start | bytes 786440 | tf_op jit(solution)/shard_map/ppermute | solution.py:384
  25.4 1.9 %collective-permute-start.2 = (bf16[128,1024]{1,0:T(8,128)(2,1)S(1)}, bf16[128,1024]{1,0:T(8,128)(2,1)S(1)}, u32[]{:S(2)}, u32[]{:S(2)}) collective-permute-start(bf16[128,1024]{1,0:T(8,128)(2,1)S(1)} %get-tuple-element.38), channel_id=1, source_target_pairs={{0,1},{1,0},{2,3},{3,2},{4,5},{5,4},{6,7},{7,6},{8,9},{9,8},{10,11... | collective-permute-start | bytes 786440 | tf_op jit(solution)/shard_map/ppermute | solution.py:384
  27.4 10.0 %collective-permute-start.4 = (bf16[64,2048]{1,0:T(8,128)(2,1)S(1)}, bf16[64,2048]{1,0:T(8,128)(2,1)S(1)}, u32[]{:S(2)}, u32[]{:S(2)}) collective-permute-start(bf16[64,2048]{1,0:T(8,128)(2,1)S(1)} %get-tuple-element.40.refs_3_), channel_id=1, source_target_pairs={{0,4},{4,0},{8,12},{12,8},{1,5},{5,1},{9,13},{13,9},{2,6},{6,2},{1... | collective-permute-start | bytes 786440 | tf_op jit(solution)/shard_map/ppermute | solution.py:387
  29.6 12.0 %collective-permute-start.6 = (bf16[128,1536]{1,0:T(8,128)(2,1)S(1)}, bf16[128,1536]{1,0:T(8,128)(2,1)S(1)}, u32[]{:S(2)}, u32[]{:S(2)}) collective-permute-start(bf16[128,1536]{1,0:T(8,128)(2,1)S(1)} %get-tuple-element.33.refs_1_), channel_id=1, source_target_pairs={{0,2},{2,0},{1,3},{3,1},{4,6},{6,4},{5,7},{7,5},{8,10},{10,8},{9,1... | collective-permute-start | bytes 1179656 | tf_op jit(solution)/shard_map/ppermute | solution.py:415
  31.0 19.3 %collective-permute-start.10 = (bf16[128,1280]{1,0:T(8,128)(2,1)S(1)}, bf16[128,1280]{1,0:T(8,128)(2,1)S(1)}, u32[]{:S(2)}, u32[]{:S(2)}) collective-permute-start(bf16[128,1280]{1,0:T(8,128)(2,1)S(1)} %get-tuple-element.34.refs_2_), channel_id=1, source_target_pairs={{0,2},{2,0},{1,3},{3,1},{4,6},{6,4},{5,7},{7,5},{8,10},{10,8},{9,1... | collective-permute-start | bytes 983048 | tf_op jit(solution)/shard_map/ppermute | solution.py:415
  37.4 2.7 %copy-start.2 = (s32[4096]{0:T(1024)S(1)}, s32[4096]{0:T(1024)}, u32[]{:S(2)}) copy-start(s32[4096]{0:T(1024)} %param.6) | copy-start | bytes 49156
  37.5 9.2 %collective-permute-start.5 = (bf16[32,2048]{1,0:T(8,128)(2,1)S(1)}, bf16[32,2048]{1,0:T(8,128)(2,1)S(1)}, u32[]{:S(2)}, u32[]{:S(2)}) collective-permute-start(bf16[32,2048]{1,0:T(8,128)(2,1)S(1)} %get-tuple-element.43.refs_3_), channel_id=1, source_target_pairs={{0,8},{4,12},{8,0},{12,4},{1,9},{5,13},{9,1},{13,5},{2,10},{6,14},... | collective-permute-start | bytes 393224 | tf_op jit(solution)/shard_map/ppermute | solution.py:387
  40.2 6.6 %copy-start.1 = (f32[128,128]{1,0:T(8,128)S(1)}, f32[128,128]{1,0:T(8,128)}, u32[]{:S(2)}) copy-start(f32[128,128]{1,0:T(8,128)} %constant.9.clone.rotation_ref) | copy-start | bytes 196612
  47.2 9.0 %collective-permute-start.7 = (bf16[32,2048]{1,0:T(8,128)(2,1)S(1)}, bf16[32,2048]{1,0:T(8,128)(2,1)S(1)}, u32[]{:S(2)}, u32[]{:S(2)}) collective-permute-start(bf16[32,2048]{1,0:T(8,128)(2,1)S(1)} %get-tuple-element.44.refs_3_.refs_0_), channel_id=1, source_target_pairs={{0,4},{4,0},{8,12},{12,8},{1,5},{5,1},{9,13},{13,9},{2,6},{6,2},{1... | collective-permute-start | bytes 393224 | tf_op jit(solution)/shard_map/ppermute | solution.py:387
  47.3 9.0 %collective-permute-start.8 = (bf16[32,2048]{1,0:T(8,128)(2,1)S(1)}, bf16[32,2048]{1,0:T(8,128)(2,1)S(1)}, u32[]{:S(2)}, u32[]{:S(2)}) collective-permute-start(bf16[32,2048]{1,0:T(8,128)(2,1)S(1)} %get-tuple-element.44.refs_3_.refs_0_), channel_id=1, source_target_pairs={{0,8},{4,12},{8,0},{12,4},{1,9},{5,13},{9,1},{13,5},{2,10},{6,14},... | collective-permute-start | bytes 393224 | tf_op jit(solution)/shard_map/ppermute | solution.py:387
  53.2 3.6 %collective-permute-start.11 = (bf16[128,1024]{1,0:T(8,128)(2,1)S(1)}, bf16[128,1024]{1,0:T(8,128)(2,1)S(1)}, u32[]{:S(2)}, u32[]{:S(2)}) collective-permute-start(bf16[128,1024]{1,0:T(8,128)(2,1)S(1)} %get-tuple-element.46.refs_3_), channel_id=1, source_target_pairs={{0,1},{1,0},{2,3},{3,2},{4,5},{5,4},{6,7},{7,6},{8,9},{9,8},{10,11... | collective-permute-start | bytes 786440 | tf_op jit(solution)/shard_map/ppermute | solution.py:384
  56.3 2.2 %collective-permute-start.13 = (bf16[128,1024]{1,0:T(8,128)(2,1)S(1)}, bf16[128,1024]{1,0:T(8,128)(2,1)S(1)}, u32[]{:S(2)}, u32[]{:S(2)}) collective-permute-start(bf16[128,1024]{1,0:T(8,128)(2,1)S(1)} %shard_map.70), channel_id=1, source_target_pairs={{0,1},{1,0},{2,3},{3,2},{4,5},{5,4},{6,7},{7,6},{8,9},{9,8},{10,11... | collective-permute-start | bytes 786440 | tf_op jit(solution)/shard_map/ppermute | solution.py:384
  56.9 6.4 %collective-permute-start.12 = (bf16[64,1024]{1,0:T(8,128)(2,1)S(1)}, bf16[64,1024]{1,0:T(8,128)(2,1)S(1)}, u32[]{:S(2)}, u32[]{:S(2)}) collective-permute-start(bf16[64,1024]{1,0:T(8,128)(2,1)S(1)} %get-tuple-element.48), channel_id=1, source_target_pairs={{0,4},{4,0},{8,12},{12,8},{1,5},{5,1},{9,13},{13,9},{2,6},{6,2},{1... | collective-permute-start | bytes 393224 | tf_op jit(solution)/shard_map/ppermute | solution.py:387
  58.6 8.3 %collective-permute-start.15 = (bf16[64,1024]{1,0:T(8,128)(2,1)S(1)}, bf16[64,1024]{1,0:T(8,128)(2,1)S(1)}, u32[]{:S(2)}, u32[]{:S(2)}) collective-permute-start(bf16[64,1024]{1,0:T(8,128)(2,1)S(1)} %get-tuple-element.51.refs_2_), channel_id=1, source_target_pairs={{0,4},{4,0},{8,12},{12,8},{1,5},{5,1},{9,13},{13,9},{2,6},{6,2},{1... | collective-permute-start | bytes 393224 | tf_op jit(solution)/shard_map/ppermute | solution.py:387
  59.7 13.4 %collective-permute-start.9 = (bf16[32,2048]{1,0:T(8,128)(2,1)S(1)}, bf16[32,2048]{1,0:T(8,128)(2,1)S(1)}, u32[]{:S(2)}, u32[]{:S(2)}) collective-permute-start(bf16[32,2048]{1,0:T(8,128)(2,1)S(1)} %collective-permute-done.8.refs_2_.refs_1_), channel_id=1, source_target_pairs={{0,4},{4,0},{8,12},{12,8},{1,5},{5,1},{9,13},{13,9},{2,6},{6,2},{1... | collective-permute-start | bytes 393224 | tf_op jit(solution)/shard_map/ppermute | solution.py:387
  63.4 7.9 %collective-permute-start.14 = (bf16[32,1024]{1,0:T(8,128)(2,1)S(1)}, bf16[32,1024]{1,0:T(8,128)(2,1)S(1)}, u32[]{:S(2)}, u32[]{:S(2)}) collective-permute-start(bf16[32,1024]{1,0:T(8,128)(2,1)S(1)} %get-tuple-element.53), channel_id=1, source_target_pairs={{0,8},{4,12},{8,0},{12,4},{1,9},{5,13},{9,1},{13,5},{2,10},{6,14},... | collective-permute-start | bytes 196616 | tf_op jit(solution)/shard_map/ppermute | solution.py:387
  66.9 6.3 %collective-permute-start.19 = (bf16[32,1024]{1,0:T(8,128)(2,1)S(1)}, bf16[32,1024]{1,0:T(8,128)(2,1)S(1)}, u32[]{:S(2)}, u32[]{:S(2)}) collective-permute-start(bf16[32,1024]{1,0:T(8,128)(2,1)S(1)} %get-tuple-element.56.refs_0_), channel_id=1, source_target_pairs={{0,8},{4,12},{8,0},{12,4},{1,9},{5,13},{9,1},{13,5},{2,10},{6,14},... | collective-permute-start | bytes 196616 | tf_op jit(solution)/shard_map/ppermute | solution.py:387
  71.6 6.4 %collective-permute-start.17 = (bf16[32,1152]{1,0:T(8,128)(2,1)S(1)}, bf16[32,1152]{1,0:T(8,128)(2,1)S(1)}, u32[]{:S(2)}, u32[]{:S(2)}) collective-permute-start(bf16[32,1152]{1,0:T(8,128)(2,1)S(1)} %shard_map.74.refs_4_), channel_id=1, source_target_pairs={{0,8},{4,12},{8,0},{12,4},{1,9},{5,13},{9,1},{13,5},{2,10},{6,14},... | collective-permute-start | bytes 221192 | tf_op jit(solution)/shard_map/ppermute | solution.py:387
  73.5 6.6 %collective-permute-start.21 = (bf16[32,1152]{1,0:T(8,128)(2,1)S(1)}, bf16[32,1152]{1,0:T(8,128)(2,1)S(1)}, u32[]{:S(2)}, u32[]{:S(2)}) collective-permute-start(bf16[32,1152]{1,0:T(8,128)(2,1)S(1)} %shard_map.76.refs_4_), channel_id=1, source_target_pairs={{0,8},{4,12},{8,0},{12,4},{1,9},{5,13},{9,1},{13,5},{2,10},{6,14},... | collective-permute-start | bytes 221192 | tf_op jit(solution)/shard_map/ppermute | solution.py:387
  75.1 5.7 %collective-permute-start.16 = (bf16[32,1152]{1,0:T(8,128)(2,1)S(1)}, bf16[32,1152]{1,0:T(8,128)(2,1)S(1)}, u32[]{:S(2)}, u32[]{:S(2)}) collective-permute-start(bf16[32,1152]{1,0:T(8,128)(2,1)S(1)} %shard_map.74.refs_4_), channel_id=1, source_target_pairs={{0,4},{4,0},{8,12},{12,8},{1,5},{5,1},{9,13},{13,9},{2,6},{6,2},{1... | collective-permute-start | bytes 221192 | tf_op jit(solution)/shard_map/ppermute | solution.py:387
  78.1 4.4 %collective-permute-start.18 = (bf16[32,1152]{1,0:T(8,128)(2,1)S(1)}, bf16[32,1152]{1,0:T(8,128)(2,1)S(1)}, u32[]{:S(2)}, u32[]{:S(2)}) collective-permute-start(bf16[32,1152]{1,0:T(8,128)(2,1)S(1)} %collective-permute-done.17.refs_6_), channel_id=1, source_target_pairs={{0,4},{4,0},{8,12},{12,8},{1,5},{5,1},{9,13},{13,9},{2,6},{6,2},{1... | collective-permute-start | bytes 221192 | tf_op jit(solution)/shard_map/ppermute | solution.py:387
  78.1 5.1 %collective-permute-start.20 = (bf16[32,1152]{1,0:T(8,128)(2,1)S(1)}, bf16[32,1152]{1,0:T(8,128)(2,1)S(1)}, u32[]{:S(2)}, u32[]{:S(2)}) collective-permute-start(bf16[32,1152]{1,0:T(8,128)(2,1)S(1)} %shard_map.76.refs_4_), channel_id=1, source_target_pairs={{0,4},{4,0},{8,12},{12,8},{1,5},{5,1},{9,13},{13,9},{2,6},{6,2},{1... | collective-permute-start | bytes 221192 | tf_op jit(solution)/shard_map/ppermute | solution.py:387
  80.1 4.4 %collective-permute-start.22 = (bf16[32,1152]{1,0:T(8,128)(2,1)S(1)}, bf16[32,1152]{1,0:T(8,128)(2,1)S(1)}, u32[]{:S(2)}, u32[]{:S(2)}) collective-permute-start(bf16[32,1152]{1,0:T(8,128)(2,1)S(1)} %collective-permute-done.21.refs_6_), channel_id=1, source_target_pairs={{0,4},{4,0},{8,12},{12,8},{1,5},{5,1},{9,13},{13,9},{2,6},{6,2},{1... | collective-permute-start | bytes 221192 | tf_op jit(solution)/shard_map/ppermute | solution.py:387
  82.5 3.1 %collective-permute-start.23 = (bf16[128,1152]{1,0:T(8,128)(2,1)S(1)}, bf16[128,1152]{1,0:T(8,128)(2,1)S(1)}, u32[]{:S(2)}, u32[]{:S(2)}) collective-permute-start(bf16[128,1152]{1,0:T(8,128)(2,1)S(1)} %shard_map.79), channel_id=1, source_target_pairs={{0,1},{1,0},{2,3},{3,2},{4,5},{5,4},{6,7},{7,6},{8,9},{9,8},{10,11... | collective-permute-start | bytes 884744 | tf_op jit(solution)/shard_map/ppermute | solution.py:384
  84.5 1.6 %collective-permute-start.24 = (bf16[128,1152]{1,0:T(8,128)(2,1)S(1)}, bf16[128,1152]{1,0:T(8,128)(2,1)S(1)}, u32[]{:S(2)}, u32[]{:S(2)}) collective-permute-start(bf16[128,1152]{1,0:T(8,128)(2,1)S(1)} %shard_map.80), channel_id=1, source_target_pairs={{0,1},{1,0},{2,3},{3,2},{4,5},{5,4},{6,7},{7,6},{8,9},{9,8},{10,11... | collective-permute-start | bytes 884744 | tf_op jit(solution)/shard_map/ppermute | solution.py:384

commit v15 on v14

--- a/solution.py
+++ b/solution.py
@@ -162,6 +162,23 @@
         compiler_params=PARAMS,
         cost_estimate=SMALL,
     )(values, *tokens)
+
+
+def join_body(first_ref, second_ref, out_ref):
+    rows = first_ref.shape[0]
+    out_ref[:rows] = first_ref[...]
+    out_ref[rows:] = second_ref[...]
+
+
+def join(first, second):
+    return pl.pallas_call(
+        join_body,
+        out_shape=jax.ShapeDtypeStruct((2 * first.shape[0], first.shape[1]), first.dtype),
+        in_specs=[VMEM, VMEM],
+        out_specs=VMEM,
+        compiler_params=PARAMS,
+        cost_estimate=SMALL,
+    )(first, second)
 
 
 def halve_body(level, count, *refs):
@@ -259,19 +276,19 @@
     return lax.rem(lax.axis_index("seq") - (sub * places + place) + blocks, blocks)
 
 
-def choose_body(blocks, count, width, begins, other, places, scales, lane, *refs):
+def choose_body(blocks, count, rows, tops, width, begins, other, places, scales, lane, *refs):
     out_ref = refs[-1]
-    rows = refs[0].shape[0]
 
     def put(block, place):
         for piece in range(count):
             row = (place * count + rank_of(lax.axis_index("tensor") ^ piece, count)) * rows
             here = pl.ds(pl.multiple_of(row, rows), rows)
             begin = begins[block]
-            out_ref[here, :width] = refs[block * count + piece][:, begin : begin + width]
-            ref = refs[(blocks - 1) * count + piece]
+            ref, top = refs[block * count + piece], tops[block * count + piece]
+            out_ref[here, :width] = ref[top : top + rows, begin : begin + width]
+            ref, top = refs[(blocks - 1) * count + piece], tops[(blocks - 1) * count + piece]
             at = ref.shape[1] - BLOCK + block * scales + lane
-            out_ref[here, width : width + width // BLOCK] = ref[:, at : at + width // BLOCK]
+            out_ref[here, width : width + width // BLOCK] = ref[top : top + rows, at : at + width // BLOCK]
 
     for place in range(places):
         for block in range(blocks):
@@ -282,25 +299,29 @@
     picked = [result[0] if len(result) == 1 else result[group] for result in results]
     begins = [group * width if len(result) == 1 else 0 for result in results]
     lane = group * (width // BLOCK)
-    rows, count = picked[0][0].shape[0], len(picked[0])
+    count = len(picked[0])
+    picked = [[piece if isinstance(piece, tuple) else (piece, 0) for piece in pieces] for pieces in picked]
+    rows = picked[0][0][0].shape[0]
     columns = width + BLOCK
     if rows % 16:
         blocks = []
         for block, (pieces, begin) in enumerate(zip(picked, begins)):
             held = jnp.zeros((count * rows, columns), jnp.bfloat16)
-            for index, piece in enumerate(pieces):
-                part = piece[:, begin : begin + width]
-                at = picked[-1][index].shape[1] - BLOCK + block * scales + lane
-                scale = picked[-1][index][:, at : at + width // BLOCK]
+            for index, (piece, top) in enumerate(pieces):
+                part = piece[top : top + rows, begin : begin + width]
+                scaled, top = picked[-1][index]
+                at = scaled.shape[1] - BLOCK + block * scales + lane
+                scale = scaled[top : top + rows, at : at + width // BLOCK]
                 part = jnp.concatenate([part, jnp.pad(scale, ((0, 0), (0, BLOCK - width // BLOCK)))], axis=1)
                 row = rank_of(lax.axis_index("tensor") ^ index, count) * rows
                 held = lax.dynamic_update_slice_in_dim(held, part, row, 0)
             blocks.append(held)
         stacked = jnp.stack(blocks)
         return jnp.concatenate([stacked[block_of(other, place, places, len(blocks))] for place in range(places)])
-    operands = [piece for pieces in picked for piece in pieces]
-    return pl.pallas_call(
-        functools.partial(choose_body, len(picked), count, width, begins, other, places, scales, lane),
+    operands = [piece for pieces in picked for piece, _ in pieces]
+    tops = [top for pieces in picked for _, top in pieces]
+    return pl.pallas_call(
+        functools.partial(choose_body, len(picked), count, rows, tops, width, begins, other, places, scales, lane),
         out_shape=jax.ShapeDtypeStruct((places * count * rows, columns), jnp.bfloat16),
         in_specs=[VMEM] * len(operands),
         out_specs=VMEM,
@@ -406,13 +427,27 @@
         return [pieces[index] for index in range(tensor_count)]
 
     zeros = jnp.zeros((hidden.shape[0] // tensor_count, BLOCK), jnp.float32)
+    def spread_joined(packed):
+        rows, here = packed.shape[0], packed
+        pieces = {0: (packed, 0)}
+        for level in reversed(range(levels)):
+            came = exchange(here, level)
+            order = list(pieces)
+            for place, index in enumerate(order):
+                pieces[index ^ 1 << level] = (came, place * rows)
+            if level:
+                here = join(here, came)
+        return [pieces[index] for index in range(tensor_count)]
+
     sizes = cut(depth)
     places = [sum(sizes[:index]) for index in range(len(sizes))]
     parts = slices_of(hidden, list(zip(places, sizes)))
-    arrivals = []
-    for shift in range(1, seq_count):
-        pairs = [(s, (s + shift) % seq_count) for s in range(seq_count)]
-        arrivals.append([lax.ppermute(part, "seq", pairs) for part in parts])
+
+    def from_seq(part, shift):
+        return lax.ppermute(part, "seq", [(s, (s + shift) % seq_count) for s in range(seq_count)])
+
+    early = max(1, len(sizes) - 1)
+    arrivals = [[from_seq(part, shift) for part in parts[:early]] for shift in range(1, seq_count)]
 
     if len(sizes) == 1:
         outs = multiply([[parts[0]], [arrivals[0][0]]], down_weight, 0, [None, None], [True, True], wide_chunk)
@@ -439,6 +474,8 @@
                 (total,) = multiply(
                     [[arrived[index]]], down_weight, places[index], [total], [False], wide_chunk, tokens=tokens
                 )
+                if index == 1 and shift == 0:
+                    late = gate(parts[-1], [total])
                 if not results:
                     step = own_steps.send([total])
                     tokens = [step]
@@ -448,13 +485,13 @@
                 results.append([spread(list(own_steps)[-1])])
             if shift == 0:
                 bases = [list(own_base) for _ in range(GROUPS)]
+            outs = multiply(
+                [[from_seq(late, shift + 1)]], down_weight, places[-1], [total], [True], wide_chunk,
+                groups=GROUPS, tokens=tokens,
+            )
             remote, all_steps = [], []
             for group in range(GROUPS):
-                sent, kept = multiply(
-                    [[arrived[-1]]], down_weight, places[-1], [total], [True], wide_chunk,
-                    groups=GROUPS, only=group, tokens=tokens,
-                )
-                tokens = [sent]
+                sent, kept = outs[2 * group : 2 * group + 2]
                 if group == GROUPS - 1 and shift == 0 and levels > 1:
                     sent = gate(sent, [results[0][0][1], results[0][0][1 << levels - 1]])
                 all_steps.append(reduce([sent, kept], group * half // GROUPS, shift + 1, bases[group], shift == seq_count - 2))
@@ -467,7 +504,7 @@
                         wait += results[0][0][1:]
                     step = steps.send(wait)
                     if level == levels:
-                        remote.append(spread(step))
+                        remote.append(spread_joined(step))
                 last = [step]
             results.append(remote)
             tokens = []

time: 87.1 us -> 88.2 us (1.013)
  waiting for transfers between devices: 19.3 us -> 23.7 us
  starting transfers between devices: 24.9 us -> 22.9 us
  Pallas kernels: 40.3 us -> 39 us
    ppermute x15 -> x13, waiting for transfers between devices: 16 us -> 19.4 us  [exchange(): lax.ppermute(values, 'tensor', [(t, t ^ 1 << level) for t in range(tensor...]
    ppermute x15 -> x13, starting transfers between devices: 18.5 us -> 16.5 us  [exchange(): lax.ppermute(values, 'tensor', [(t, t ^ 1 << level) for t in range(tensor...]
    pallas_call x6 -> x5, Pallas kernels: 36.8 us -> 35.4 us  [multiply(): pl.pallas_call(body, out_shape=out_shape, in_specs=[VMEM] * spans[-1][1]...]
    ppermute x6, waiting for transfers between devices: 0.87 us -> 1.88 us  [swap(): return lax.ppermute(values, 'sub', [(0, 1), (1, 0)])]
  transfers between devices with their start and end apart: 25 -> 23, of which waited for: 13 -> 12; matrix products, arithmetic and copies ran while one was open for 0% -> 0% of each run, Pallas kernels for 45% -> 43%
where the time goes in v15:
time: 88.2 us; the launch traced here: 88 us
  Pallas kernels  39 us (44%)
  waiting for transfers between devices  23.7 us (27%)
  starting transfers between devices  22.9 us (26%)
  local copies, waits for them, and re-layouts  1.46 us (2%)
  between operations  0.94 us (1%)
    pallas_call x5, Pallas kernels, multiply(): pl.pallas_call(body, out_shape=out_shape, in_specs=[VMEM] * spans[-1][1]...  35.4 us
    ppermute x13, waiting for transfers between devices, exchange(): lax.ppermute(values, 'tensor', [(t, t ^ 1 << level) for t in range(tensor...  19.4 us
    ppermute x13, starting transfers between devices, exchange(): lax.ppermute(values, 'tensor', [(t, t ^ 1 << level) for t in range(tensor...  16.5 us
    ppermute x4, starting transfers between devices, from_seq(): lax.ppermute(part, 'seq', [(s, (s + shift) % seq_count) for s in range(se...  5.17 us
    ppermute x4, waiting for transfers between devices, from_seq(): lax.ppermute(part, 'seq', [(s, (s + shift) % seq_count) for s in range(se...  2.44 us
    ppermute x6, waiting for transfers between devices, swap(): return lax.ppermute(values, 'sub', [(0, 1), (1, 0)])  1.88 us
  transfers between devices with their start and end apart: 23, of which 12 were waited for; matrix products, arithmetic and copies ran while one was open for 0% of the time, Pallas kernels for 43%

profile of v15, /device:TPU:0, one launch (start us, length us, event | category | flops | bytes accessed | tf_op | source)
XLA Modules:
  0.0 88.0 jit_solution(2670282267855565372)
XLA Ops:
  0.6 1.4 %copy-done = bf16[128,6656]{1,0:T(8,128)(2,1)S(1)} copy-done((bf16[128,6656]{1,0:T(8,128)(2,1)S(1)}, bf16[128,6656]{1,0:T(8,128)(2,1)}, u32[]{:S(2)}) %copy-start) | copy-done | bytes 1703960
  2.1 0.2 shard_map.59
  2.3 3.0 %collective-permute-start = (bf16[128,2048]{1,0:T(8,128)(2,1)S(1)}, bf16[128,2048]{1,0:T(8,128)(2,1)S(1)}, u32[]{:S(2)}, u32[]{:S(2)}) collective-permute-start(bf16[128,2048]{1,0:T(8,128)(2,1)S(1)} %get-tuple-element.31.refs_4_.refs_0_), channel_id=1, source_target_pairs={{0,2},{2,0},{1,3},{3,1},{4,6},{6,4},{5,7},{7,5},{8,10},{10,8},{9,1... | collective-permute-start | bytes 1572872 | tf_op jit(solution)/shard_map/ppermute | solution.py:447
  5.3 0.1 collective-permute-start.3
  5.3 12.7 %shard_map.60.refs_3_ = f32[128,4096]{1,0:T(8,128)S(1)} custom-call(bf16[128,1792]{1,0:T(8,128)(2,1)S(1)} %get-tuple-element.32.refs_0_, bf16[128,1536]{1,0:T(8,128)(2,1)S(1)} %get-tuple-element.33.refs_1_, bf16[128,1280]{1,0:T(8,128)(2,1)S(1)} %get-tuple-element.34.refs_2_.refs_0_, bf16[6656,4096]{1,0:T(8,128)(2,1)} %refs_1_.5, ...), custom_call_target="tpu_custom_call" | custom-call | flops 1 | bytes 1 | tf_op jit(solution)/shard_map/pallas_call | solution.py:139
  18.0 7.3 %shard_map.61 = (bf16[128,1024]{1,0:T(8,128)(2,1)S(1)}, f32[128,1024]{1,0:T(8,128)S(1)}, bf16[128,1024]{1,0:T(8,128)(2,1)S(1)}, f32[128,1024]{1,0:T(8,128)S(1)}, f32[128,4096]{1,0:T(8,128)S(1)}) custom-call(bf16[128,2048]{1,0:T(8,128)(2,1)S(1)} %get-tuple-element.31.refs_4_.refs_0_, bf16[128,2048]{1,0:T(8,128)(2,1)S(1)} %collective-permute-done.refs_1_, ...), custom_call_target="tpu_custom_call" | custom-call | flops 1 | bytes 1 | tf_op jit(solution)/shard_map/pallas_call | solution.py:139
  25.3 0.1 collective-permute-start.1
  25.4 0.5 collective-permute-start.2
  25.9 1.1 %collective-permute-done.3.refs_4_.refs_0_ = bf16[128,1792]{1,0:T(8,128)(2,1)S(1)} collective-permute-done((bf16[128,1792]{1,0:T(8,128)(2,1)S(1)}, bf16[128,1792]{1,0:T(8,128)(2,1)S(1)}, u32[]{:S(2)}, u32[]{:S(2)}) %collective-permute-start.3) | collective-permute-done | bytes 458784 | tf_op jit(solution)/shard_map/ppermute | solution.py:447
  27.0 0.3 collective-permute-done.2.refs_3_
  27.3 0.1 shard_map.62
  27.4 2.2 %collective-permute-start.4 = (bf16[64,2048]{1,0:T(8,128)(2,1)S(1)}, bf16[64,2048]{1,0:T(8,128)(2,1)S(1)}, u32[]{:S(2)}, u32[]{:S(2)}) collective-permute-start(bf16[64,2048]{1,0:T(8,128)(2,1)S(1)} %get-tuple-element.40.refs_3_), channel_id=1, source_target_pairs={{0,4},{4,0},{8,12},{12,8},{1,5},{5,1},{9,13},{13,9},{2,6},{6,2},{1... | collective-permute-start | bytes 786440 | tf_op jit(solution)/shard_map/ppermute | solution.py:408
  29.6 1.5 %collective-permute-start.6 = (bf16[128,1536]{1,0:T(8,128)(2,1)S(1)}, bf16[128,1536]{1,0:T(8,128)(2,1)S(1)}, u32[]{:S(2)}, u32[]{:S(2)}) collective-permute-start(bf16[128,1536]{1,0:T(8,128)(2,1)S(1)} %get-tuple-element.33.refs_1_), channel_id=1, source_target_pairs={{0,2},{2,0},{1,3},{3,1},{4,6},{6,4},{5,7},{7,5},{8,10},{10,8},{9,1... | collective-permute-start | bytes 1179656 | tf_op jit(solution)/shard_map/ppermute | solution.py:447
  31.0 5.8 %shard_map.63.refs_2_.refs_1_ = f32[128,4096]{1,0:T(8,128)S(1)} custom-call(bf16[128,1792]{1,0:T(8,128)(2,1)S(1)} %collective-permute-done.3.refs_4_.refs_0_, bf16[6656,4096]{1,0:T(8,128)(2,1)} %refs_1_.5, f32[128,4096]{1,0:T(8,128)S(1)} %get-tuple-element.41.refs_2_, bf16[64,2048]{1,0:T(8,128)(2,1)S(1)} %get-tuple-element.40.refs_3_), custom_call_target="tpu_custom_call" | custom-call | flops 1 | bytes 1 | tf_op jit(solution)/shard_map/pallas_call | solution.py:139
  36.9 0.6 collective-permute-start.10
  37.5 2.7 %collective-permute-start.5 = (bf16[32,2048]{1,0:T(8,128)(2,1)S(1)}, bf16[32,2048]{1,0:T(8,128)(2,1)S(1)}, u32[]{:S(2)}, u32[]{:S(2)}) collective-permute-start(bf16[32,2048]{1,0:T(8,128)(2,1)S(1)} %get-tuple-element.43.refs_3_), channel_id=1, source_target_pairs={{0,8},{4,12},{8,0},{12,4},{1,9},{5,13},{9,1},{13,5},{2,10},{6,14},... | collective-permute-start | bytes 393224 | tf_op jit(solution)/shard_map/ppermute | solution.py:408
  40.2 1.3 %collective-permute-done.6.refs_0_ = bf16[128,1536]{1,0:T(8,128)(2,1)S(1)} collective-permute-done((bf16[128,1536]{1,0:T(8,128)(2,1)S(1)}, bf16[128,1536]{1,0:T(8,128)(2,1)S(1)}, u32[]{:S(2)}, u32[]{:S(2)}) %collective-permute-start.6) | collective-permute-done | bytes 393248 | tf_op jit(solution)/shard_map/ppermute | solution.py:447
  41.6 5.2 %shard_map.65.refs_0_.refs_2_ = f32[128,4096]{1,0:T(8,128)S(1)} custom-call(bf16[128,1536]{1,0:T(8,128)(2,1)S(1)} %collective-permute-done.6.refs_0_, bf16[6656,4096]{1,0:T(8,128)(2,1)} %refs_1_.5, f32[128,4096]{1,0:T(8,128)S(1)} %shard_map.63.refs_2_.refs_1_, bf16[32,2048]{1,0:T(8,128)(2,1)S(1)} %get-tuple-element.43.refs_3_), custom_call_target="tpu_custom_call" | custom-call | flops 1 | bytes 1 | tf_op jit(solution)/shard_map/pallas_call | solution.py:139
  46.8 0.5 shard_map.66
  47.2 0.1 collective-permute-start.7
  47.3 3.0 %collective-permute-start.8 = (bf16[32,2048]{1,0:T(8,128)(2,1)S(1)}, bf16[32,2048]{1,0:T(8,128)(2,1)S(1)}, u32[]{:S(2)}, u32[]{:S(2)}) collective-permute-start(bf16[32,2048]{1,0:T(8,128)(2,1)S(1)} %get-tuple-element.44.refs_3_.refs_0_), channel_id=1, source_target_pairs={{0,8},{4,12},{8,0},{12,4},{1,9},{5,13},{9,1},{13,5},{2,10},{6,14},... | collective-permute-start | bytes 393224 | tf_op jit(solution)/shard_map/ppermute | solution.py:408
  50.3 4.5 %shard_map.68 = (bf16[128,1024]{1,0:T(8,128)(2,1)S(1)}, f32[128,1024]{1,0:T(8,128)S(1)}, bf16[128,1024]{1,0:T(8,128)(2,1)S(1)}, f32[128,1024]{1,0:T(8,128)S(1)}) custom-call(bf16[128,1280]{1,0:T(8,128)(2,1)S(1)} %collective-permute-done.10.refs_0_, bf16[6656,4096]{1,0:T(8,128)(2,1)} %refs_1_.5, f32[128,4096]{1,0:T(8,128)S(1)} %shard_map.65.refs_0_.refs_2_, ...), custom_call_target="tpu_custom_call" | custom-call | flops 1 | bytes 1 | tf_op jit(solution)/shard_map/pallas_call | solution.py:139
  54.8 0.1 collective-permute-start.11
  55.0 0.5 collective-permute-start.13
  55.4 1.0 %collective-permute-done.11.refs_1_ = bf16[128,1024]{1,0:T(8,128)(2,1)S(1)} collective-permute-done((bf16[128,1024]{1,0:T(8,128)(2,1)S(1)}, bf16[128,1024]{1,0:T(8,128)(2,1)S(1)}, u32[]{:S(2)}, u32[]{:S(2)}) %collective-permute-start.11) | collective-permute-done | bytes 262176 | tf_op jit(solution)/shard_map/ppermute | solution.py:405
  56.5 1.6 %collective-permute-start.12 = (bf16[64,1024]{1,0:T(8,128)(2,1)S(1)}, bf16[64,1024]{1,0:T(8,128)(2,1)S(1)}, u32[]{:S(2)}, u32[]{:S(2)}) collective-permute-start(bf16[64,1024]{1,0:T(8,128)(2,1)S(1)} %get-tuple-element.48), channel_id=1, source_target_pairs={{0,4},{4,0},{8,12},{12,8},{1,5},{5,1},{9,13},{13,9},{2,6},{6,2},{1... | collective-permute-start | bytes 393224 | tf_op jit(solution)/shard_map/ppermute | solution.py:408
  58.2 0.5 collective-permute-start.15
  58.7 1.6 %collective-permute-start.9 = (bf16[32,2048]{1,0:T(8,128)(2,1)S(1)}, bf16[32,2048]{1,0:T(8,128)(2,1)S(1)}, u32[]{:S(2)}, u32[]{:S(2)}) collective-permute-start(bf16[32,2048]{1,0:T(8,128)(2,1)S(1)} %collective-permute-done.8.refs_2_.refs_1_), channel_id=1, source_target_pairs={{0,4},{4,0},{8,12},{12,8},{1,5},{5,1},{9,13},{13,9},{2,6},{6,2},{1... | collective-permute-start | bytes 393224 | tf_op jit(solution)/shard_map/ppermute | solution.py:408
  60.3 2.6 %collective-permute-done.12.refs_1_ = bf16[64,1024]{1,0:T(8,128)(2,1)S(1)} collective-permute-done((bf16[64,1024]{1,0:T(8,128)(2,1)S(1)}, bf16[64,1024]{1,0:T(8,128)(2,1)S(1)}, u32[]{:S(2)}, u32[]{:S(2)}) %collective-permute-start.12) | collective-permute-done | bytes 131104 | tf_op jit(solution)/shard_map/ppermute | solution.py:408
  62.9 0.7 collective-permute-start.14
  63.7 2.8 %collective-permute-done.15.refs_1_ = bf16[64,1024]{1,0:T(8,128)(2,1)S(1)} collective-permute-done((bf16[64,1024]{1,0:T(8,128)(2,1)S(1)}, bf16[64,1024]{1,0:T(8,128)(2,1)S(1)}, u32[]{:S(2)}, u32[]{:S(2)}) %collective-permute-start.15) | collective-permute-done | bytes 131104 | tf_op jit(solution)/shard_map/ppermute | solution.py:408
  66.5 4.2 %collective-permute-done.14.came_ref = bf16[32,1024]{1,0:T(8,128)(2,1)S(1)} collective-permute-done((bf16[32,1024]{1,0:T(8,128)(2,1)S(1)}, bf16[32,1024]{1,0:T(8,128)(2,1)S(1)}, u32[]{:S(2)}, u32[]{:S(2)}) %collective-permute-start.14) | collective-permute-done | bytes 65568 | tf_op jit(solution)/shard_map/ppermute | solution.py:408
  70.7 0.3 shard_map.74.first_ref.refs_4_
  71.1 1.7 %collective-permute-start.16 = (bf16[32,1152]{1,0:T(8,128)(2,1)S(1)}, bf16[32,1152]{1,0:T(8,128)(2,1)S(1)}, u32[]{:S(2)}, u32[]{:S(2)}) collective-permute-start(bf16[32,1152]{1,0:T(8,128)(2,1)S(1)} %shard_map.74.first_ref.refs_4_), channel_id=1, source_target_pairs={{0,8},{4,12},{8,0},{12,4},{1,9},{5,13},{9,1},{13,5},{2,10},{6,14},... | collective-permute-start | bytes 221192 | tf_op jit(solution)/shard_map/ppermute | solution.py:408
  72.8 0.4 shard_map.77.first_ref.refs_4_
  73.2 1.3 %collective-permute-start.19 = (bf16[32,1152]{1,0:T(8,128)(2,1)S(1)}, bf16[32,1152]{1,0:T(8,128)(2,1)S(1)}, u32[]{:S(2)}, u32[]{:S(2)}) collective-permute-start(bf16[32,1152]{1,0:T(8,128)(2,1)S(1)} %shard_map.77.first_ref.refs_4_), channel_id=1, source_target_pairs={{0,8},{4,12},{8,0},{12,4},{1,9},{5,13},{9,1},{13,5},{2,10},{6,14},... | collective-permute-start | bytes 221192 | tf_op jit(solution)/shard_map/ppermute | solution.py:408
  74.5 3.6 %collective-permute-done.16.second_ref.refs_6_ = bf16[32,1152]{1,0:T(8,128)(2,1)S(1)} collective-permute-done((bf16[32,1152]{1,0:T(8,128)(2,1)S(1)}, bf16[32,1152]{1,0:T(8,128)(2,1)S(1)}, u32[]{:S(2)}, u32[]{:S(2)}) %collective-permute-start.16) | collective-permute-done | bytes 73760 | tf_op jit(solution)/shard_map/ppermute | solution.py:408
  78.1 0.1 collective-permute-start.17
  78.2 1.1 %collective-permute-done.19.second_ref.refs_6_ = bf16[32,1152]{1,0:T(8,128)(2,1)S(1)} collective-permute-done((bf16[32,1152]{1,0:T(8,128)(2,1)S(1)}, bf16[32,1152]{1,0:T(8,128)(2,1)S(1)}, u32[]{:S(2)}, u32[]{:S(2)}) %collective-permute-start.19) | collective-permute-done | bytes 73760 | tf_op jit(solution)/shard_map/ppermute | solution.py:408
  79.3 1.0 %collective-permute-start.20 = (bf16[64,1152]{1,0:T(8,128)(2,1)S(1)}, bf16[64,1152]{1,0:T(8,128)(2,1)S(1)}, u32[]{:S(2)}, u32[]{:S(2)}) collective-permute-start(bf16[64,1152]{1,0:T(8,128)(2,1)S(1)} %shard_map.78), channel_id=1, source_target_pairs={{0,4},{4,0},{8,12},{12,8},{1,5},{5,1},{9,13},{13,9},{2,6},{6,2},{1... | collective-permute-start | bytes 442376 | tf_op jit(solution)/shard_map/ppermute | solution.py:408
  80.3 3.6 %collective-permute-done.17.refs_5_.refs_7_ = bf16[64,1152]{1,0:T(8,128)(2,1)S(1)} collective-permute-done((bf16[64,1152]{1,0:T(8,128)(2,1)S(1)}, bf16[64,1152]{1,0:T(8,128)(2,1)S(1)}, u32[]{:S(2)}, u32[]{:S(2)}) %collective-permute-start.17) | collective-permute-done | bytes 147488 | tf_op jit(solution)/shard_map/ppermute | solution.py:408
  83.9 0.1 shard_map.81
  84.0 1.4 %collective-permute-done.20.refs_5_.refs_7_ = bf16[64,1152]{1,0:T(8,128)(2,1)S(1)} collective-permute-done((bf16[64,1152]{1,0:T(8,128)(2,1)S(1)}, bf16[64,1152]{1,0:T(8,128)(2,1)S(1)}, u32[]{:S(2)}, u32[]{:S(2)}) %collective-permute-start.20) | collective-permute-done | bytes 147488 | tf_op jit(solution)/shard_map/ppermute | solution.py:408
  85.5 0.1 shard_map.82
  85.7 0.1 shard_map.79.refs_1_.refs_4_
  85.8 0.8 shard_map.80.refs_0_
  86.6 0.6 collective-permute-done.22.refs_2_
  87.2 0.8 shard_map.83
  (31 shorter events, 0.5 us)
Async XLA Ops:
  0.6 1.5 %copy-start = (bf16[128,6656]{1,0:T(8,128)(2,1)S(1)}, bf16[128,6656]{1,0:T(8,128)(2,1)}, u32[]{:S(2)}) copy-start(bf16[128,6656]{1,0:T(8,128)(2,1)} %in_ref.1) | copy-start | bytes 5111812
  2.3 15.8 %collective-permute-start = (bf16[128,2048]{1,0:T(8,128)(2,1)S(1)}, bf16[128,2048]{1,0:T(8,128)(2,1)S(1)}, u32[]{:S(2)}, u32[]{:S(2)}) collective-permute-start(bf16[128,2048]{1,0:T(8,128)(2,1)S(1)} %get-tuple-element.31.refs_4_.refs_0_), channel_id=1, source_target_pairs={{0,2},{2,0},{1,3},{3,1},{4,6},{6,4},{5,7},{7,5},{8,10},{10,8},{9,1... | collective-permute-start | bytes 1572872 | tf_op jit(solution)/shard_map/ppermute | solution.py:447
  5.3 21.8 %collective-permute-start.3 = (bf16[128,1792]{1,0:T(8,128)(2,1)S(1)}, bf16[128,1792]{1,0:T(8,128)(2,1)S(1)}, u32[]{:S(2)}, u32[]{:S(2)}) collective-permute-start(bf16[128,1792]{1,0:T(8,128)(2,1)S(1)} %get-tuple-element.32.refs_0_), channel_id=1, source_target_pairs={{0,2},{2,0},{1,3},{3,1},{4,6},{6,4},{5,7},{7,5},{8,10},{10,8},{9,1... | collective-permute-start | bytes 1376264 | tf_op jit(solution)/shard_map/ppermute | solution.py:447
  25.3 1.7 %collective-permute-start.1 = (bf16[128,1024]{1,0:T(8,128)(2,1)S(1)}, bf16[128,1024]{1,0:T(8,128)(2,1)S(1)}, u32[]{:S(2)}, u32[]{:S(2)}) collective-permute-start(bf16[128,1024]{1,0:T(8,128)(2,1)S(1)} %get-tuple-element.37), channel_id=1, source_target_pairs={{0,1},{1,0},{2,3},{3,2},{4,5},{5,4},{6,7},{7,6},{8,9},{9,8},{10,11... | collective-permute-start | bytes 786440 | tf_op jit(solution)/shard_map/ppermute | solution.py:405
  25.4 1.9 %collective-permute-start.2 = (bf16[128,1024]{1,0:T(8,128)(2,1)S(1)}, bf16[128,1024]{1,0:T(8,128)(2,1)S(1)}, u32[]{:S(2)}, u32[]{:S(2)}) collective-permute-start(bf16[128,1024]{1,0:T(8,128)(2,1)S(1)} %get-tuple-element.38), channel_id=1, source_target_pairs={{0,1},{1,0},{2,3},{3,2},{4,5},{5,4},{6,7},{7,6},{8,9},{9,8},{10,11... | collective-permute-start | bytes 786440 | tf_op jit(solution)/shard_map/ppermute | solution.py:405
  27.4 10.1 %collective-permute-start.4 = (bf16[64,2048]{1,0:T(8,128)(2,1)S(1)}, bf16[64,2048]{1,0:T(8,128)(2,1)S(1)}, u32[]{:S(2)}, u32[]{:S(2)}) collective-permute-start(bf16[64,2048]{1,0:T(8,128)(2,1)S(1)} %get-tuple-element.40.refs_3_), channel_id=1, source_target_pairs={{0,4},{4,0},{8,12},{12,8},{1,5},{5,1},{9,13},{13,9},{2,6},{6,2},{1... | collective-permute-start | bytes 786440 | tf_op jit(solution)/shard_map/ppermute | solution.py:408
  29.6 12.0 %collective-permute-start.6 = (bf16[128,1536]{1,0:T(8,128)(2,1)S(1)}, bf16[128,1536]{1,0:T(8,128)(2,1)S(1)}, u32[]{:S(2)}, u32[]{:S(2)}) collective-permute-start(bf16[128,1536]{1,0:T(8,128)(2,1)S(1)} %get-tuple-element.33.refs_1_), channel_id=1, source_target_pairs={{0,2},{2,0},{1,3},{3,1},{4,6},{6,4},{5,7},{7,5},{8,10},{10,8},{9,1... | collective-permute-start | bytes 1179656 | tf_op jit(solution)/shard_map/ppermute | solution.py:447
  36.9 3.3 %copy-start.2 = (s32[4096]{0:T(1024)S(1)}, s32[4096]{0:T(1024)}, u32[]{:S(2)}) copy-start(s32[4096]{0:T(1024)} %param.6) | copy-start | bytes 49156
  36.9 13.4 %collective-permute-start.10 = (bf16[128,1280]{1,0:T(8,128)(2,1)S(1)}, bf16[128,1280]{1,0:T(8,128)(2,1)S(1)}, u32[]{:S(2)}, u32[]{:S(2)}) collective-permute-start(bf16[128,1280]{1,0:T(8,128)(2,1)S(1)} %shard_map.67), channel_id=1, source_target_pairs={{0,2},{2,0},{1,3},{3,1},{4,6},{6,4},{5,7},{7,5},{8,10},{10,8},{9,1... | collective-permute-start | bytes 983048 | tf_op jit(solution)/shard_map/ppermute | solution.py:447
  37.5 9.2 %collective-permute-start.5 = (bf16[32,2048]{1,0:T(8,128)(2,1)S(1)}, bf16[32,2048]{1,0:T(8,128)(2,1)S(1)}, u32[]{:S(2)}, u32[]{:S(2)}) collective-permute-start(bf16[32,2048]{1,0:T(8,128)(2,1)S(1)} %get-tuple-element.43.refs_3_), channel_id=1, source_target_pairs={{0,8},{4,12},{8,0},{12,4},{1,9},{5,13},{9,1},{13,5},{2,10},{6,14},... | collective-permute-start | bytes 393224 | tf_op jit(solution)/shard_map/ppermute | solution.py:408
  40.2 6.5 %copy-start.1 = (f32[128,128]{1,0:T(8,128)S(1)}, f32[128,128]{1,0:T(8,128)}, u32[]{:S(2)}) copy-start(f32[128,128]{1,0:T(8,128)} %constant.9.clone.rotation_ref) | copy-start | bytes 196612
  47.2 7.7 %collective-permute-start.7 = (bf16[32,2048]{1,0:T(8,128)(2,1)S(1)}, bf16[32,2048]{1,0:T(8,128)(2,1)S(1)}, u32[]{:S(2)}, u32[]{:S(2)}) collective-permute-start(bf16[32,2048]{1,0:T(8,128)(2,1)S(1)} %get-tuple-element.44.refs_3_.refs_0_), channel_id=1, source_target_pairs={{0,4},{4,0},{8,12},{12,8},{1,5},{5,1},{9,13},{13,9},{2,6},{6,2},{1... | collective-permute-start | bytes 393224 | tf_op jit(solution)/shard_map/ppermute | solution.py:408
  47.3 7.6 %collective-permute-start.8 = (bf16[32,2048]{1,0:T(8,128)(2,1)S(1)}, bf16[32,2048]{1,0:T(8,128)(2,1)S(1)}, u32[]{:S(2)}, u32[]{:S(2)}) collective-permute-start(bf16[32,2048]{1,0:T(8,128)(2,1)S(1)} %get-tuple-element.44.refs_3_.refs_0_), channel_id=1, source_target_pairs={{0,8},{4,12},{8,0},{12,4},{1,9},{5,13},{9,1},{13,5},{2,10},{6,14},... | collective-permute-start | bytes 393224 | tf_op jit(solution)/shard_map/ppermute | solution.py:408
  54.8 1.6 %collective-permute-start.11 = (bf16[128,1024]{1,0:T(8,128)(2,1)S(1)}, bf16[128,1024]{1,0:T(8,128)(2,1)S(1)}, u32[]{:S(2)}, u32[]{:S(2)}) collective-permute-start(bf16[128,1024]{1,0:T(8,128)(2,1)S(1)} %get-tuple-element.46), channel_id=1, source_target_pairs={{0,1},{1,0},{2,3},{3,2},{4,5},{5,4},{6,7},{7,6},{8,9},{9,8},{10,11... | collective-permute-start | bytes 786440 | tf_op jit(solution)/shard_map/ppermute | solution.py:405
  55.0 3.2 %collective-permute-start.13 = (bf16[128,1024]{1,0:T(8,128)(2,1)S(1)}, bf16[128,1024]{1,0:T(8,128)(2,1)S(1)}, u32[]{:S(2)}, u32[]{:S(2)}) collective-permute-start(bf16[128,1024]{1,0:T(8,128)(2,1)S(1)} %shard_map.70), channel_id=1, source_target_pairs={{0,1},{1,0},{2,3},{3,2},{4,5},{5,4},{6,7},{7,6},{8,9},{9,8},{10,11... | collective-permute-start | bytes 786440 | tf_op jit(solution)/shard_map/ppermute | solution.py:405
  56.5 6.4 %collective-permute-start.12 = (bf16[64,1024]{1,0:T(8,128)(2,1)S(1)}, bf16[64,1024]{1,0:T(8,128)(2,1)S(1)}, u32[]{:S(2)}, u32[]{:S(2)}) collective-permute-start(bf16[64,1024]{1,0:T(8,128)(2,1)S(1)} %get-tuple-element.48), channel_id=1, source_target_pairs={{0,4},{4,0},{8,12},{12,8},{1,5},{5,1},{9,13},{13,9},{2,6},{6,2},{1... | collective-permute-start | bytes 393224 | tf_op jit(solution)/shard_map/ppermute | solution.py:408
  58.2 8.2 %collective-permute-start.15 = (bf16[64,1024]{1,0:T(8,128)(2,1)S(1)}, bf16[64,1024]{1,0:T(8,128)(2,1)S(1)}, u32[]{:S(2)}, u32[]{:S(2)}) collective-permute-start(bf16[64,1024]{1,0:T(8,128)(2,1)S(1)} %get-tuple-element.51.refs_2_), channel_id=1, source_target_pairs={{0,4},{4,0},{8,12},{12,8},{1,5},{5,1},{9,13},{13,9},{2,6},{6,2},{1... | collective-permute-start | bytes 393224 | tf_op jit(solution)/shard_map/ppermute | solution.py:408
  58.7 14.1 %collective-permute-start.9 = (bf16[32,2048]{1,0:T(8,128)(2,1)S(1)}, bf16[32,2048]{1,0:T(8,128)(2,1)S(1)}, u32[]{:S(2)}, u32[]{:S(2)}) collective-permute-start(bf16[32,2048]{1,0:T(8,128)(2,1)S(1)} %collective-permute-done.8.refs_2_.refs_1_), channel_id=1, source_target_pairs={{0,4},{4,0},{8,12},{12,8},{1,5},{5,1},{9,13},{13,9},{2,6},{6,2},{1... | collective-permute-start | bytes 393224 | tf_op jit(solution)/shard_map/ppermute | solution.py:408
  62.9 7.8 %collective-permute-start.14 = (bf16[32,1024]{1,0:T(8,128)(2,1)S(1)}, bf16[32,1024]{1,0:T(8,128)(2,1)S(1)}, u32[]{:S(2)}, u32[]{:S(2)}) collective-permute-start(bf16[32,1024]{1,0:T(8,128)(2,1)S(1)} %get-tuple-element.53), channel_id=1, source_target_pairs={{0,8},{4,12},{8,0},{12,4},{1,9},{5,13},{9,1},{13,5},{2,10},{6,14},... | collective-permute-start | bytes 196616 | tf_op jit(solution)/shard_map/ppermute | solution.py:408
  66.4 6.4 %collective-permute-start.18 = (bf16[32,1024]{1,0:T(8,128)(2,1)S(1)}, bf16[32,1024]{1,0:T(8,128)(2,1)S(1)}, u32[]{:S(2)}, u32[]{:S(2)}) collective-permute-start(bf16[32,1024]{1,0:T(8,128)(2,1)S(1)} %get-tuple-element.56.refs_0_), channel_id=1, source_target_pairs={{0,8},{4,12},{8,0},{12,4},{1,9},{5,13},{9,1},{13,5},{2,10},{6,14},... | collective-permute-start | bytes 196616 | tf_op jit(solution)/shard_map/ppermute | solution.py:408
  71.1 7.1 %collective-permute-start.16 = (bf16[32,1152]{1,0:T(8,128)(2,1)S(1)}, bf16[32,1152]{1,0:T(8,128)(2,1)S(1)}, u32[]{:S(2)}, u32[]{:S(2)}) collective-permute-start(bf16[32,1152]{1,0:T(8,128)(2,1)S(1)} %shard_map.74.first_ref.refs_4_), channel_id=1, source_target_pairs={{0,8},{4,12},{8,0},{12,4},{1,9},{5,13},{9,1},{13,5},{2,10},{6,14},... | collective-permute-start | bytes 221192 | tf_op jit(solution)/shard_map/ppermute | solution.py:408
  73.2 6.1 %collective-permute-start.19 = (bf16[32,1152]{1,0:T(8,128)(2,1)S(1)}, bf16[32,1152]{1,0:T(8,128)(2,1)S(1)}, u32[]{:S(2)}, u32[]{:S(2)}) collective-permute-start(bf16[32,1152]{1,0:T(8,128)(2,1)S(1)} %shard_map.77.first_ref.refs_4_), channel_id=1, source_target_pairs={{0,8},{4,12},{8,0},{12,4},{1,9},{5,13},{9,1},{13,5},{2,10},{6,14},... | collective-permute-start | bytes 221192 | tf_op jit(solution)/shard_map/ppermute | solution.py:408
  78.1 5.8 %collective-permute-start.17 = (bf16[64,1152]{1,0:T(8,128)(2,1)S(1)}, bf16[64,1152]{1,0:T(8,128)(2,1)S(1)}, u32[]{:S(2)}, u32[]{:S(2)}) collective-permute-start(bf16[64,1152]{1,0:T(8,128)(2,1)S(1)} %shard_map.75), channel_id=1, source_target_pairs={{0,4},{4,0},{8,12},{12,8},{1,5},{5,1},{9,13},{13,9},{2,6},{6,2},{1... | collective-permute-start | bytes 442376 | tf_op jit(solution)/shard_map/ppermute | solution.py:408
  79.3 6.2 %collective-permute-start.20 = (bf16[64,1152]{1,0:T(8,128)(2,1)S(1)}, bf16[64,1152]{1,0:T(8,128)(2,1)S(1)}, u32[]{:S(2)}, u32[]{:S(2)}) collective-permute-start(bf16[64,1152]{1,0:T(8,128)(2,1)S(1)} %shard_map.78), channel_id=1, source_target_pairs={{0,4},{4,0},{8,12},{12,8},{1,5},{5,1},{9,13},{13,9},{2,6},{6,2},{1... | collective-permute-start | bytes 442376 | tf_op jit(solution)/shard_map/ppermute | solution.py:408
  84.0 2.6 %collective-permute-start.21 = (bf16[128,1152]{1,0:T(8,128)(2,1)S(1)}, bf16[128,1152]{1,0:T(8,128)(2,1)S(1)}, u32[]{:S(2)}, u32[]{:S(2)}) collective-permute-start(bf16[128,1152]{1,0:T(8,128)(2,1)S(1)} %shard_map.81), channel_id=1, source_target_pairs={{0,1},{1,0},{2,3},{3,2},{4,5},{5,4},{6,7},{7,6},{8,9},{9,8},{10,11... | collective-permute-start | bytes 884744 | tf_op jit(solution)/shard_map/ppermute | solution.py:405
  85.6 1.6 %collective-permute-start.22 = (bf16[128,1152]{1,0:T(8,128)(2,1)S(1)}, bf16[128,1152]{1,0:T(8,128)(2,1)S(1)}, u32[]{:S(2)}, u32[]{:S(2)}) collective-permute-start(bf16[128,1152]{1,0:T(8,128)(2,1)S(1)} %shard_map.82), channel_id=1, source_target_pairs={{0,1},{1,0},{2,3},{3,2},{4,5},{5,4},{6,7},{7,6},{8,9},{9,8},{10,11... | collective-permute-start | bytes 884744 | tf_op jit(solution)/shard_map/ppermute | solution.py:405

commit v16 on v15

--- a/solution.py
+++ b/solution.py
@@ -68,6 +68,7 @@
     rows = lefts[0][0].shape[0]
     in_half = w_ref.shape[1] // wide // 2
     first = in_half // groups
+    ahead = min(steps, max(2, steps // 2))
     here = lax.axis_index("sub")
 
     def column(n):
@@ -86,6 +87,11 @@
 
     def step(n):
         copy(n).wait()
+        if any(splits):
+            if n + ahead < steps:
+                copy(n + ahead).start()
+        else:
+            pl.when(n + ahead < steps)(lambda: copy(n + ahead).start())
         product, begin = None, 0
         for index in range(len(lefts[0])):
             parts = [left[index][...] for left in lefts]
@@ -108,7 +114,7 @@
             else:
                 outs.pop(0)[:, at(column(n))] = value
 
-    for n in range(steps):
+    for n in range(ahead):
         copy(n).start()
     if any(splits):
         for n in range(steps):
@@ -162,23 +168,6 @@
         compiler_params=PARAMS,
         cost_estimate=SMALL,
     )(values, *tokens)
-
-
-def join_body(first_ref, second_ref, out_ref):
-    rows = first_ref.shape[0]
-    out_ref[:rows] = first_ref[...]
-    out_ref[rows:] = second_ref[...]
-
-
-def join(first, second):
-    return pl.pallas_call(
-        join_body,
-        out_shape=jax.ShapeDtypeStruct((2 * first.shape[0], first.shape[1]), first.dtype),
-        in_specs=[VMEM, VMEM],
-        out_specs=VMEM,
-        compiler_params=PARAMS,
-        cost_estimate=SMALL,
-    )(first, second)
 
 
 def halve_body(level, count, *refs):
@@ -427,18 +416,6 @@
         return [pieces[index] for index in range(tensor_count)]
 
     zeros = jnp.zeros((hidden.shape[0] // tensor_count, BLOCK), jnp.float32)
-    def spread_joined(packed):
-        rows, here = packed.shape[0], packed
-        pieces = {0: (packed, 0)}
-        for level in reversed(range(levels)):
-            came = exchange(here, level)
-            order = list(pieces)
-            for place, index in enumerate(order):
-                pieces[index ^ 1 << level] = (came, place * rows)
-            if level:
-                here = join(here, came)
-        return [pieces[index] for index in range(tensor_count)]
-
     sizes = cut(depth)
     places = [sum(sizes[:index]) for index in range(len(sizes))]
     parts = slices_of(hidden, list(zip(places, sizes)))
@@ -446,8 +423,7 @@
     def from_seq(part, shift):
         return lax.ppermute(part, "seq", [(s, (s + shift) % seq_count) for s in range(seq_count)])
 
-    early = max(1, len(sizes) - 1)
-    arrivals = [[from_seq(part, shift) for part in parts[:early]] for shift in range(1, seq_count)]
+    arrivals = [[from_seq(part, shift) for part in parts] for shift in range(1, seq_count)]
 
     if len(sizes) == 1:
         outs = multiply([[parts[0]], [arrivals[0][0]]], down_weight, 0, [None, None], [True, True], wide_chunk)
@@ -474,8 +450,6 @@
                 (total,) = multiply(
                     [[arrived[index]]], down_weight, places[index], [total], [False], wide_chunk, tokens=tokens
                 )
-                if index == 1 and shift == 0:
-                    late = gate(parts[-1], [total])
                 if not results:
                     step = own_steps.send([total])
                     tokens = [step]
@@ -486,7 +460,7 @@
             if shift == 0:
                 bases = [list(own_base) for _ in range(GROUPS)]
             outs = multiply(
-                [[from_seq(late, shift + 1)]], down_weight, places[-1], [total], [True], wide_chunk,
+                [[arrived[-1]]], down_weight, places[-1], [total], [True], wide_chunk,
                 groups=GROUPS, tokens=tokens,
             )
             remote, all_steps = [], []
@@ -504,7 +478,7 @@
                         wait += results[0][0][1:]
                     step = steps.send(wait)
                     if level == levels:
-                        remote.append(spread_joined(step))
+                        remote.append(spread(step))
                 last = [step]
             results.append(remote)
             tokens = []

time: 88.2 us -> 87.4 us (level)
  waiting for transfers between devices: 23.7 us -> 19.7 us
  starting transfers between devices: 22.9 us -> 25.3 us
  Pallas kernels: 39 us -> 39.9 us
    ppermute x13 -> x15, waiting for transfers between devices: 19.4 us -> 15.5 us  [exchange(): lax.ppermute(values, 'tensor', [(t, t ^ 1 << level) for t in range(tensor...]
    ppermute x13 -> x15, starting transfers between devices: 16.5 us -> 19 us  [exchange(): lax.ppermute(values, 'tensor', [(t, t ^ 1 << level) for t in range(tensor...]
    pallas_call x5, Pallas kernels: 35.4 us -> 36.4 us  [multiply(): pl.pallas_call(body, out_shape=out_shape, in_specs=[VMEM] * spans[-1][1]...]
  transfers between devices with their start and end apart: 23 -> 25, of which waited for: 12 -> 14; matrix products, arithmetic and copies ran while one was open for 0% -> 0% of each run, Pallas kernels for 43% -> 45%
where the time goes in v16:
time: 87.4 us; the launch traced here: 87.3 us
  Pallas kernels  39.9 us (46%)
  starting transfers between devices  25.3 us (29%)
  waiting for transfers between devices  19.7 us (23%)
  local copies, waits for them, and re-layouts  1.46 us (2%)
  between operations  0.92 us (1%)
    pallas_call x5, Pallas kernels, multiply(): pl.pallas_call(body, out_shape=out_shape, in_specs=[VMEM] * spans[-1][1]...  36.4 us
    ppermute x15, starting transfers between devices, exchange(): lax.ppermute(values, 'tensor', [(t, t ^ 1 << level) for t in range(tensor...  19 us
    ppermute x15, waiting for transfers between devices, exchange(): lax.ppermute(values, 'tensor', [(t, t ^ 1 << level) for t in range(tensor...  15.5 us
    ppermute x4, starting transfers between devices, from_seq(): lax.ppermute(part, 'seq', [(s, (s + shift) % seq_count) for s in range(se...  5.11 us
    ppermute x6, waiting for transfers between devices, swap(): return lax.ppermute(values, 'sub', [(0, 1), (1, 0)])  2.22 us
    ppermute x4, waiting for transfers between devices, from_seq(): lax.ppermute(part, 'seq', [(s, (s + shift) % seq_count) for s in range(se...  1.98 us
  transfers between devices with their start and end apart: 25, of which 14 were waited for; matrix products, arithmetic and copies ran while one was open for 0% of the time, Pallas kernels for 45%

profile of v16, /device:TPU:0, one launch (start us, length us, event | category | flops | bytes accessed | tf_op | source)
XLA Modules:
  0.0 87.3 jit_solution(9610124732651770031)
XLA Ops:
  0.6 1.4 %copy-done = bf16[128,6656]{1,0:T(8,128)(2,1)S(1)} copy-done((bf16[128,6656]{1,0:T(8,128)(2,1)S(1)}, bf16[128,6656]{1,0:T(8,128)(2,1)}, u32[]{:S(2)}) %copy-start) | copy-done | bytes 1703960
  2.1 0.2 shard_map.59
  2.3 3.0 %collective-permute-start = (bf16[128,2048]{1,0:T(8,128)(2,1)S(1)}, bf16[128,2048]{1,0:T(8,128)(2,1)S(1)}, u32[]{:S(2)}, u32[]{:S(2)}) collective-permute-start(bf16[128,2048]{1,0:T(8,128)(2,1)S(1)} %get-tuple-element.31.refs_4_.refs_0_), channel_id=1, source_target_pairs={{0,2},{2,0},{1,3},{3,1},{4,6},{6,4},{5,7},{7,5},{8,10},{10,8},{9,1... | collective-permute-start | bytes 1572872 | tf_op jit(solution)/shard_map/ppermute | solution.py:424
  5.3 0.1 collective-permute-start.3
  5.3 12.9 %shard_map.60.refs_3_ = f32[128,4096]{1,0:T(8,128)S(1)} custom-call(bf16[128,1792]{1,0:T(8,128)(2,1)S(1)} %get-tuple-element.32.refs_0_, bf16[128,1536]{1,0:T(8,128)(2,1)S(1)} %get-tuple-element.33.refs_1_, bf16[128,1280]{1,0:T(8,128)(2,1)S(1)} %get-tuple-element.34.refs_2_, bf16[6656,4096]{1,0:T(8,128)(2,1)} %refs_1_.5, ...), custom_call_target="tpu_custom_call" | custom-call | flops 1 | bytes 1 | tf_op jit(solution)/shard_map/pallas_call | solution.py:145
  18.2 7.4 %shard_map.61 = (bf16[128,1024]{1,0:T(8,128)(2,1)S(1)}, f32[128,1024]{1,0:T(8,128)S(1)}, bf16[128,1024]{1,0:T(8,128)(2,1)S(1)}, f32[128,1024]{1,0:T(8,128)S(1)}, f32[128,4096]{1,0:T(8,128)S(1)}) custom-call(bf16[128,2048]{1,0:T(8,128)(2,1)S(1)} %get-tuple-element.31.refs_4_.refs_0_, bf16[128,2048]{1,0:T(8,128)(2,1)S(1)} %collective-permute-done.refs_1_, ...), custom_call_target="tpu_custom_call" | custom-call | flops 1 | bytes 1 | tf_op jit(solution)/shard_map/pallas_call | solution.py:145
  25.7 0.5 collective-permute-start.2
  26.2 0.8 collective-permute-done.3.refs_4_.refs_0_
  27.0 0.3 collective-permute-done.1.refs_2_
  27.3 0.4 collective-permute-done.2.refs_3_
  27.6 0.1 shard_map.62
  27.7 2.1 %collective-permute-start.4 = (bf16[64,2048]{1,0:T(8,128)(2,1)S(1)}, bf16[64,2048]{1,0:T(8,128)(2,1)S(1)}, u32[]{:S(2)}, u32[]{:S(2)}) collective-permute-start(bf16[64,2048]{1,0:T(8,128)(2,1)S(1)} %get-tuple-element.40.refs_3_), channel_id=1, source_target_pairs={{0,4},{4,0},{8,12},{12,8},{1,5},{5,1},{9,13},{13,9},{2,6},{6,2},{1... | collective-permute-start | bytes 786440 | tf_op jit(solution)/shard_map/ppermute | solution.py:397
  29.8 1.5 %collective-permute-start.6 = (bf16[128,1536]{1,0:T(8,128)(2,1)S(1)}, bf16[128,1536]{1,0:T(8,128)(2,1)S(1)}, u32[]{:S(2)}, u32[]{:S(2)}) collective-permute-start(bf16[128,1536]{1,0:T(8,128)(2,1)S(1)} %get-tuple-element.33.refs_1_), channel_id=1, source_target_pairs={{0,2},{2,0},{1,3},{3,1},{4,6},{6,4},{5,7},{7,5},{8,10},{10,8},{9,1... | collective-permute-start | bytes 1179656 | tf_op jit(solution)/shard_map/ppermute | solution.py:424
  31.3 0.5 collective-permute-start.10
  31.9 6.0 %shard_map.63.refs_2_ = f32[128,4096]{1,0:T(8,128)S(1)} custom-call(bf16[128,1792]{1,0:T(8,128)(2,1)S(1)} %collective-permute-done.3.refs_4_.refs_0_, bf16[6656,4096]{1,0:T(8,128)(2,1)} %refs_1_.5, f32[128,4096]{1,0:T(8,128)S(1)} %get-tuple-element.41.refs_2_, bf16[64,2048]{1,0:T(8,128)(2,1)S(1)} %get-tuple-element.40.refs_3_), custom_call_target="tpu_custom_call" | custom-call | flops 1 | bytes 1 | tf_op jit(solution)/shard_map/pallas_call | solution.py:145
  38.0 2.7 %collective-permute-start.5 = (bf16[32,2048]{1,0:T(8,128)(2,1)S(1)}, bf16[32,2048]{1,0:T(8,128)(2,1)S(1)}, u32[]{:S(2)}, u32[]{:S(2)}) collective-permute-start(bf16[32,2048]{1,0:T(8,128)(2,1)S(1)} %get-tuple-element.43.refs_3_), channel_id=1, source_target_pairs={{0,8},{4,12},{8,0},{12,4},{1,9},{5,13},{9,1},{13,5},{2,10},{6,14},... | collective-permute-start | bytes 393224 | tf_op jit(solution)/shard_map/ppermute | solution.py:397
  40.6 1.2 %collective-permute-done.6.refs_0_ = bf16[128,1536]{1,0:T(8,128)(2,1)S(1)} collective-permute-done((bf16[128,1536]{1,0:T(8,128)(2,1)S(1)}, bf16[128,1536]{1,0:T(8,128)(2,1)S(1)}, u32[]{:S(2)}, u32[]{:S(2)}) %collective-permute-start.6) | collective-permute-done | bytes 393248 | tf_op jit(solution)/shard_map/ppermute | solution.py:424
  41.8 5.4 %shard_map.65.refs_0_.refs_2_ = f32[128,4096]{1,0:T(8,128)S(1)} custom-call(bf16[128,1536]{1,0:T(8,128)(2,1)S(1)} %collective-permute-done.6.refs_0_, bf16[6656,4096]{1,0:T(8,128)(2,1)} %refs_1_.5, f32[128,4096]{1,0:T(8,128)S(1)} %shard_map.63.refs_2_, bf16[32,2048]{1,0:T(8,128)(2,1)S(1)} %get-tuple-element.43.refs_3_), custom_call_target="tpu_custom_call" | custom-call | flops 1 | bytes 1 | tf_op jit(solution)/shard_map/pallas_call | solution.py:145
  47.2 0.5 shard_map.66
  47.7 0.1 collective-permute-start.7
  47.8 3.0 %collective-permute-start.8 = (bf16[32,2048]{1,0:T(8,128)(2,1)S(1)}, bf16[32,2048]{1,0:T(8,128)(2,1)S(1)}, u32[]{:S(2)}, u32[]{:S(2)}) collective-permute-start(bf16[32,2048]{1,0:T(8,128)(2,1)S(1)} %get-tuple-element.44.refs_3_.refs_0_), channel_id=1, source_target_pairs={{0,8},{4,12},{8,0},{12,4},{1,9},{5,13},{9,1},{13,5},{2,10},{6,14},... | collective-permute-start | bytes 393224 | tf_op jit(solution)/shard_map/ppermute | solution.py:397
  50.8 4.7 %shard_map.67 = (bf16[128,1024]{1,0:T(8,128)(2,1)S(1)}, f32[128,1024]{1,0:T(8,128)S(1)}, bf16[128,1024]{1,0:T(8,128)(2,1)S(1)}, f32[128,1024]{1,0:T(8,128)S(1)}) custom-call(bf16[128,1280]{1,0:T(8,128)(2,1)S(1)} %collective-permute-done.10.refs_0_, bf16[6656,4096]{1,0:T(8,128)(2,1)} %refs_1_.5, f32[128,4096]{1,0:T(8,128)S(1)} %shard_map.65.refs_0_.refs_2_, ...), custom_call_target="tpu_custom_call" | custom-call | flops 1 | bytes 1 | tf_op jit(solution)/shard_map/pallas_call | solution.py:145
  55.6 0.5 collective-permute-start.13
  56.1 1.0 %collective-permute-done.11.refs_1_ = bf16[128,1024]{1,0:T(8,128)(2,1)S(1)} collective-permute-done((bf16[128,1024]{1,0:T(8,128)(2,1)S(1)}, bf16[128,1024]{1,0:T(8,128)(2,1)S(1)}, u32[]{:S(2)}, u32[]{:S(2)}) %collective-permute-start.11) | collective-permute-done | bytes 262176 | tf_op jit(solution)/shard_map/ppermute | solution.py:394
  57.2 1.6 %collective-permute-start.12 = (bf16[64,1024]{1,0:T(8,128)(2,1)S(1)}, bf16[64,1024]{1,0:T(8,128)(2,1)S(1)}, u32[]{:S(2)}, u32[]{:S(2)}) collective-permute-start(bf16[64,1024]{1,0:T(8,128)(2,1)S(1)} %get-tuple-element.48), channel_id=1, source_target_pairs={{0,4},{4,0},{8,12},{12,8},{1,5},{5,1},{9,13},{13,9},{2,6},{6,2},{1... | collective-permute-start | bytes 393224 | tf_op jit(solution)/shard_map/ppermute | solution.py:397
  58.9 0.5 collective-permute-start.15
  59.4 1.6 %collective-permute-start.9 = (bf16[32,2048]{1,0:T(8,128)(2,1)S(1)}, bf16[32,2048]{1,0:T(8,128)(2,1)S(1)}, u32[]{:S(2)}, u32[]{:S(2)}) collective-permute-start(bf16[32,2048]{1,0:T(8,128)(2,1)S(1)} %collective-permute-done.8.refs_2_.refs_1_), channel_id=1, source_target_pairs={{0,4},{4,0},{8,12},{12,8},{1,5},{5,1},{9,13},{13,9},{2,6},{6,2},{1... | collective-permute-start | bytes 393224 | tf_op jit(solution)/shard_map/ppermute | solution.py:397
  61.0 2.6 %collective-permute-done.12.refs_1_ = bf16[64,1024]{1,0:T(8,128)(2,1)S(1)} collective-permute-done((bf16[64,1024]{1,0:T(8,128)(2,1)S(1)}, bf16[64,1024]{1,0:T(8,128)(2,1)S(1)}, u32[]{:S(2)}, u32[]{:S(2)}) %collective-permute-start.12) | collective-permute-done | bytes 131104 | tf_op jit(solution)/shard_map/ppermute | solution.py:397
  63.6 0.5 collective-permute-start.14
  64.1 3.0 %collective-permute-done.15.refs_1_ = bf16[64,1024]{1,0:T(8,128)(2,1)S(1)} collective-permute-done((bf16[64,1024]{1,0:T(8,128)(2,1)S(1)}, bf16[64,1024]{1,0:T(8,128)(2,1)S(1)}, u32[]{:S(2)}, u32[]{:S(2)}) %collective-permute-start.15) | collective-permute-done | bytes 131104 | tf_op jit(solution)/shard_map/ppermute | solution.py:397
  67.2 4.2 %collective-permute-done.14.came_ref = bf16[32,1024]{1,0:T(8,128)(2,1)S(1)} collective-permute-done((bf16[32,1024]{1,0:T(8,128)(2,1)S(1)}, bf16[32,1024]{1,0:T(8,128)(2,1)S(1)}, u32[]{:S(2)}, u32[]{:S(2)}) %collective-permute-start.14) | collective-permute-done | bytes 65568 | tf_op jit(solution)/shard_map/ppermute | solution.py:397
  71.4 0.3 shard_map.73.refs_4_
  71.8 1.7 %collective-permute-start.17 = (bf16[32,1152]{1,0:T(8,128)(2,1)S(1)}, bf16[32,1152]{1,0:T(8,128)(2,1)S(1)}, u32[]{:S(2)}, u32[]{:S(2)}) collective-permute-start(bf16[32,1152]{1,0:T(8,128)(2,1)S(1)} %shard_map.73.refs_4_), channel_id=1, source_target_pairs={{0,8},{4,12},{8,0},{12,4},{1,9},{5,13},{9,1},{13,5},{2,10},{6,14},... | collective-permute-start | bytes 221192 | tf_op jit(solution)/shard_map/ppermute | solution.py:397
  73.5 0.4 shard_map.75.refs_4_
  73.9 1.3 %collective-permute-start.21 = (bf16[32,1152]{1,0:T(8,128)(2,1)S(1)}, bf16[32,1152]{1,0:T(8,128)(2,1)S(1)}, u32[]{:S(2)}, u32[]{:S(2)}) collective-permute-start(bf16[32,1152]{1,0:T(8,128)(2,1)S(1)} %shard_map.75.refs_4_), channel_id=1, source_target_pairs={{0,8},{4,12},{8,0},{12,4},{1,9},{5,13},{9,1},{13,5},{2,10},{6,14},... | collective-permute-start | bytes 221192 | tf_op jit(solution)/shard_map/ppermute | solution.py:397
  75.2 1.7 %collective-permute-start.16 = (bf16[32,1152]{1,0:T(8,128)(2,1)S(1)}, bf16[32,1152]{1,0:T(8,128)(2,1)S(1)}, u32[]{:S(2)}, u32[]{:S(2)}) collective-permute-start(bf16[32,1152]{1,0:T(8,128)(2,1)S(1)} %shard_map.73.refs_4_), channel_id=1, source_target_pairs={{0,4},{4,0},{8,12},{12,8},{1,5},{5,1},{9,13},{13,9},{2,6},{6,2},{1... | collective-permute-start | bytes 221192 | tf_op jit(solution)/shard_map/ppermute | solution.py:397
  76.9 1.5 %collective-permute-done.17.refs_6_ = bf16[32,1152]{1,0:T(8,128)(2,1)S(1)} collective-permute-done((bf16[32,1152]{1,0:T(8,128)(2,1)S(1)}, bf16[32,1152]{1,0:T(8,128)(2,1)S(1)}, u32[]{:S(2)}, u32[]{:S(2)}) %collective-permute-start.17) | collective-permute-done | bytes 73760 | tf_op jit(solution)/shard_map/ppermute | solution.py:397
  78.4 2.0 %collective-permute-start.20 = (bf16[32,1152]{1,0:T(8,128)(2,1)S(1)}, bf16[32,1152]{1,0:T(8,128)(2,1)S(1)}, u32[]{:S(2)}, u32[]{:S(2)}) collective-permute-start(bf16[32,1152]{1,0:T(8,128)(2,1)S(1)} %shard_map.75.refs_4_), channel_id=1, source_target_pairs={{0,4},{4,0},{8,12},{12,8},{1,5},{5,1},{9,13},{13,9},{2,6},{6,2},{1... | collective-permute-start | bytes 221192 | tf_op jit(solution)/shard_map/ppermute | solution.py:397
  80.4 0.6 collective-permute-done.16.refs_5_
  81.0 1.8 %collective-permute-done.18.refs_7_ = bf16[32,1152]{1,0:T(8,128)(2,1)S(1)} collective-permute-done((bf16[32,1152]{1,0:T(8,128)(2,1)S(1)}, bf16[32,1152]{1,0:T(8,128)(2,1)S(1)}, u32[]{:S(2)}, u32[]{:S(2)}) %collective-permute-start.18) | collective-permute-done | bytes 73760 | tf_op jit(solution)/shard_map/ppermute | solution.py:397
  82.8 0.1 shard_map.78
  82.9 0.7 collective-permute-done.20.refs_5_
  83.6 1.1 %collective-permute-done.22.refs_7_ = bf16[32,1152]{1,0:T(8,128)(2,1)S(1)} collective-permute-done((bf16[32,1152]{1,0:T(8,128)(2,1)S(1)}, bf16[32,1152]{1,0:T(8,128)(2,1)S(1)}, u32[]{:S(2)}, u32[]{:S(2)}) %collective-permute-start.22) | collective-permute-done | bytes 73760 | tf_op jit(solution)/shard_map/ppermute | solution.py:397
  84.7 0.1 shard_map.79
  84.9 0.1 shard_map.76.refs_1_.refs_4_
  85.0 0.8 shard_map.77.refs_0_
  85.9 0.6 collective-permute-done.24.refs_2_
  86.4 0.8 shard_map.80
  (32 shorter events, 0.7 us)
Async XLA Ops:
  0.6 1.5 %copy-start = (bf16[128,6656]{1,0:T(8,128)(2,1)S(1)}, bf16[128,6656]{1,0:T(8,128)(2,1)}, u32[]{:S(2)}) copy-start(bf16[128,6656]{1,0:T(8,128)(2,1)} %in_ref.1) | copy-start | bytes 5111812
  2.3 16.0 %collective-permute-start = (bf16[128,2048]{1,0:T(8,128)(2,1)S(1)}, bf16[128,2048]{1,0:T(8,128)(2,1)S(1)}, u32[]{:S(2)}, u32[]{:S(2)}) collective-permute-start(bf16[128,2048]{1,0:T(8,128)(2,1)S(1)} %get-tuple-element.31.refs_4_.refs_0_), channel_id=1, source_target_pairs={{0,2},{2,0},{1,3},{3,1},{4,6},{6,4},{5,7},{7,5},{8,10},{10,8},{9,1... | collective-permute-start | bytes 1572872 | tf_op jit(solution)/shard_map/ppermute | solution.py:424
  5.3 21.8 %collective-permute-start.3 = (bf16[128,1792]{1,0:T(8,128)(2,1)S(1)}, bf16[128,1792]{1,0:T(8,128)(2,1)S(1)}, u32[]{:S(2)}, u32[]{:S(2)}) collective-permute-start(bf16[128,1792]{1,0:T(8,128)(2,1)S(1)} %get-tuple-element.32.refs_0_), channel_id=1, source_target_pairs={{0,2},{2,0},{1,3},{3,1},{4,6},{6,4},{5,7},{7,5},{8,10},{10,8},{9,1... | collective-permute-start | bytes 1376264 | tf_op jit(solution)/shard_map/ppermute | solution.py:424
  25.7 1.6 %collective-permute-start.1 = (bf16[128,1024]{1,0:T(8,128)(2,1)S(1)}, bf16[128,1024]{1,0:T(8,128)(2,1)S(1)}, u32[]{:S(2)}, u32[]{:S(2)}) collective-permute-start(bf16[128,1024]{1,0:T(8,128)(2,1)S(1)} %get-tuple-element.37), channel_id=1, source_target_pairs={{0,1},{1,0},{2,3},{3,2},{4,5},{5,4},{6,7},{7,6},{8,9},{9,8},{10,11... | collective-permute-start | bytes 786440 | tf_op jit(solution)/shard_map/ppermute | solution.py:394
  25.7 1.9 %collective-permute-start.2 = (bf16[128,1024]{1,0:T(8,128)(2,1)S(1)}, bf16[128,1024]{1,0:T(8,128)(2,1)S(1)}, u32[]{:S(2)}, u32[]{:S(2)}) collective-permute-start(bf16[128,1024]{1,0:T(8,128)(2,1)S(1)} %get-tuple-element.38), channel_id=1, source_target_pairs={{0,1},{1,0},{2,3},{3,2},{4,5},{5,4},{6,7},{7,6},{8,9},{9,8},{10,11... | collective-permute-start | bytes 786440 | tf_op jit(solution)/shard_map/ppermute | solution.py:394
  27.7 10.1 %collective-permute-start.4 = (bf16[64,2048]{1,0:T(8,128)(2,1)S(1)}, bf16[64,2048]{1,0:T(8,128)(2,1)S(1)}, u32[]{:S(2)}, u32[]{:S(2)}) collective-permute-start(bf16[64,2048]{1,0:T(8,128)(2,1)S(1)} %get-tuple-element.40.refs_3_), channel_id=1, source_target_pairs={{0,4},{4,0},{8,12},{12,8},{1,5},{5,1},{9,13},{13,9},{2,6},{6,2},{1... | collective-permute-start | bytes 786440 | tf_op jit(solution)/shard_map/ppermute | solution.py:397
  29.8 12.0 %collective-permute-start.6 = (bf16[128,1536]{1,0:T(8,128)(2,1)S(1)}, bf16[128,1536]{1,0:T(8,128)(2,1)S(1)}, u32[]{:S(2)}, u32[]{:S(2)}) collective-permute-start(bf16[128,1536]{1,0:T(8,128)(2,1)S(1)} %get-tuple-element.33.refs_1_), channel_id=1, source_target_pairs={{0,2},{2,0},{1,3},{3,1},{4,6},{6,4},{5,7},{7,5},{8,10},{10,8},{9,1... | collective-permute-start | bytes 1179656 | tf_op jit(solution)/shard_map/ppermute | solution.py:424
  31.3 19.5 %collective-permute-start.10 = (bf16[128,1280]{1,0:T(8,128)(2,1)S(1)}, bf16[128,1280]{1,0:T(8,128)(2,1)S(1)}, u32[]{:S(2)}, u32[]{:S(2)}) collective-permute-start(bf16[128,1280]{1,0:T(8,128)(2,1)S(1)} %get-tuple-element.34.refs_2_), channel_id=1, source_target_pairs={{0,2},{2,0},{1,3},{3,1},{4,6},{6,4},{5,7},{7,5},{8,10},{10,8},{9,1... | collective-permute-start | bytes 983048 | tf_op jit(solution)/shard_map/ppermute | solution.py:424
  37.9 2.7 %copy-start.2 = (s32[4096]{0:T(1024)S(1)}, s32[4096]{0:T(1024)}, u32[]{:S(2)}) copy-start(s32[4096]{0:T(1024)} %param.6) | copy-start | bytes 49156
  38.0 9.2 %collective-permute-start.5 = (bf16[32,2048]{1,0:T(8,128)(2,1)S(1)}, bf16[32,2048]{1,0:T(8,128)(2,1)S(1)}, u32[]{:S(2)}, u32[]{:S(2)}) collective-permute-start(bf16[32,2048]{1,0:T(8,128)(2,1)S(1)} %get-tuple-element.43.refs_3_), channel_id=1, source_target_pairs={{0,8},{4,12},{8,0},{12,4},{1,9},{5,13},{9,1},{13,5},{2,10},{6,14},... | collective-permute-start | bytes 393224 | tf_op jit(solution)/shard_map/ppermute | solution.py:397
  40.6 6.6 %copy-start.1 = (f32[128,128]{1,0:T(8,128)S(1)}, f32[128,128]{1,0:T(8,128)}, u32[]{:S(2)}) copy-start(f32[128,128]{1,0:T(8,128)} %constant.9.clone.rotation_ref) | copy-start | bytes 196612
  47.7 7.9 %collective-permute-start.7 = (bf16[32,2048]{1,0:T(8,128)(2,1)S(1)}, bf16[32,2048]{1,0:T(8,128)(2,1)S(1)}, u32[]{:S(2)}, u32[]{:S(2)}) collective-permute-start(bf16[32,2048]{1,0:T(8,128)(2,1)S(1)} %get-tuple-element.44.refs_3_.refs_0_), channel_id=1, source_target_pairs={{0,4},{4,0},{8,12},{12,8},{1,5},{5,1},{9,13},{13,9},{2,6},{6,2},{1... | collective-permute-start | bytes 393224 | tf_op jit(solution)/shard_map/ppermute | solution.py:397
  47.8 7.8 %collective-permute-start.8 = (bf16[32,2048]{1,0:T(8,128)(2,1)S(1)}, bf16[32,2048]{1,0:T(8,128)(2,1)S(1)}, u32[]{:S(2)}, u32[]{:S(2)}) collective-permute-start(bf16[32,2048]{1,0:T(8,128)(2,1)S(1)} %get-tuple-element.44.refs_3_.refs_0_), channel_id=1, source_target_pairs={{0,8},{4,12},{8,0},{12,4},{1,9},{5,13},{9,1},{13,5},{2,10},{6,14},... | collective-permute-start | bytes 393224 | tf_op jit(solution)/shard_map/ppermute | solution.py:397
  55.5 1.6 %collective-permute-start.11 = (bf16[128,1024]{1,0:T(8,128)(2,1)S(1)}, bf16[128,1024]{1,0:T(8,128)(2,1)S(1)}, u32[]{:S(2)}, u32[]{:S(2)}) collective-permute-start(bf16[128,1024]{1,0:T(8,128)(2,1)S(1)} %get-tuple-element.46), channel_id=1, source_target_pairs={{0,1},{1,0},{2,3},{3,2},{4,5},{5,4},{6,7},{7,6},{8,9},{9,8},{10,11... | collective-permute-start | bytes 786440 | tf_op jit(solution)/shard_map/ppermute | solution.py:394
  55.6 3.2 %collective-permute-start.13 = (bf16[128,1024]{1,0:T(8,128)(2,1)S(1)}, bf16[128,1024]{1,0:T(8,128)(2,1)S(1)}, u32[]{:S(2)}, u32[]{:S(2)}) collective-permute-start(bf16[128,1024]{1,0:T(8,128)(2,1)S(1)} %shard_map.69), channel_id=1, source_target_pairs={{0,1},{1,0},{2,3},{3,2},{4,5},{5,4},{6,7},{7,6},{8,9},{9,8},{10,11... | collective-permute-start | bytes 786440 | tf_op jit(solution)/shard_map/ppermute | solution.py:394
  57.2 6.4 %collective-permute-start.12 = (bf16[64,1024]{1,0:T(8,128)(2,1)S(1)}, bf16[64,1024]{1,0:T(8,128)(2,1)S(1)}, u32[]{:S(2)}, u32[]{:S(2)}) collective-permute-start(bf16[64,1024]{1,0:T(8,128)(2,1)S(1)} %get-tuple-element.48), channel_id=1, source_target_pairs={{0,4},{4,0},{8,12},{12,8},{1,5},{5,1},{9,13},{13,9},{2,6},{6,2},{1... | collective-permute-start | bytes 393224 | tf_op jit(solution)/shard_map/ppermute | solution.py:397
  58.9 8.2 %collective-permute-start.15 = (bf16[64,1024]{1,0:T(8,128)(2,1)S(1)}, bf16[64,1024]{1,0:T(8,128)(2,1)S(1)}, u32[]{:S(2)}, u32[]{:S(2)}) collective-permute-start(bf16[64,1024]{1,0:T(8,128)(2,1)S(1)} %get-tuple-element.51.refs_2_), channel_id=1, source_target_pairs={{0,4},{4,0},{8,12},{12,8},{1,5},{5,1},{9,13},{13,9},{2,6},{6,2},{1... | collective-permute-start | bytes 393224 | tf_op jit(solution)/shard_map/ppermute | solution.py:397
  59.4 14.1 %collective-permute-start.9 = (bf16[32,2048]{1,0:T(8,128)(2,1)S(1)}, bf16[32,2048]{1,0:T(8,128)(2,1)S(1)}, u32[]{:S(2)}, u32[]{:S(2)}) collective-permute-start(bf16[32,2048]{1,0:T(8,128)(2,1)S(1)} %collective-permute-done.8.refs_2_.refs_1_), channel_id=1, source_target_pairs={{0,4},{4,0},{8,12},{12,8},{1,5},{5,1},{9,13},{13,9},{2,6},{6,2},{1... | collective-permute-start | bytes 393224 | tf_op jit(solution)/shard_map/ppermute | solution.py:397
  63.6 7.8 %collective-permute-start.14 = (bf16[32,1024]{1,0:T(8,128)(2,1)S(1)}, bf16[32,1024]{1,0:T(8,128)(2,1)S(1)}, u32[]{:S(2)}, u32[]{:S(2)}) collective-permute-start(bf16[32,1024]{1,0:T(8,128)(2,1)S(1)} %get-tuple-element.53), channel_id=1, source_target_pairs={{0,8},{4,12},{8,0},{12,4},{1,9},{5,13},{9,1},{13,5},{2,10},{6,14},... | collective-permute-start | bytes 196616 | tf_op jit(solution)/shard_map/ppermute | solution.py:397
  67.1 6.4 %collective-permute-start.19 = (bf16[32,1024]{1,0:T(8,128)(2,1)S(1)}, bf16[32,1024]{1,0:T(8,128)(2,1)S(1)}, u32[]{:S(2)}, u32[]{:S(2)}) collective-permute-start(bf16[32,1024]{1,0:T(8,128)(2,1)S(1)} %get-tuple-element.56.refs_0_), channel_id=1, source_target_pairs={{0,8},{4,12},{8,0},{12,4},{1,9},{5,13},{9,1},{13,5},{2,10},{6,14},... | collective-permute-start | bytes 196616 | tf_op jit(solution)/shard_map/ppermute | solution.py:397
  71.8 6.6 %collective-permute-start.17 = (bf16[32,1152]{1,0:T(8,128)(2,1)S(1)}, bf16[32,1152]{1,0:T(8,128)(2,1)S(1)}, u32[]{:S(2)}, u32[]{:S(2)}) collective-permute-start(bf16[32,1152]{1,0:T(8,128)(2,1)S(1)} %shard_map.73.refs_4_), channel_id=1, source_target_pairs={{0,8},{4,12},{8,0},{12,4},{1,9},{5,13},{9,1},{13,5},{2,10},{6,14},... | collective-permute-start | bytes 221192 | tf_op jit(solution)/shard_map/ppermute | solution.py:397
  73.9 6.5 %collective-permute-start.21 = (bf16[32,1152]{1,0:T(8,128)(2,1)S(1)}, bf16[32,1152]{1,0:T(8,128)(2,1)S(1)}, u32[]{:S(2)}, u32[]{:S(2)}) collective-permute-start(bf16[32,1152]{1,0:T(8,128)(2,1)S(1)} %shard_map.75.refs_4_), channel_id=1, source_target_pairs={{0,8},{4,12},{8,0},{12,4},{1,9},{5,13},{9,1},{13,5},{2,10},{6,14},... | collective-permute-start | bytes 221192 | tf_op jit(solution)/shard_map/ppermute | solution.py:397
  75.2 5.8 %collective-permute-start.16 = (bf16[32,1152]{1,0:T(8,128)(2,1)S(1)}, bf16[32,1152]{1,0:T(8,128)(2,1)S(1)}, u32[]{:S(2)}, u32[]{:S(2)}) collective-permute-start(bf16[32,1152]{1,0:T(8,128)(2,1)S(1)} %shard_map.73.refs_4_), channel_id=1, source_target_pairs={{0,4},{4,0},{8,12},{12,8},{1,5},{5,1},{9,13},{13,9},{2,6},{6,2},{1... | collective-permute-start | bytes 221192 | tf_op jit(solution)/shard_map/ppermute | solution.py:397
  78.4 4.4 %collective-permute-start.18 = (bf16[32,1152]{1,0:T(8,128)(2,1)S(1)}, bf16[32,1152]{1,0:T(8,128)(2,1)S(1)}, u32[]{:S(2)}, u32[]{:S(2)}) collective-permute-start(bf16[32,1152]{1,0:T(8,128)(2,1)S(1)} %collective-permute-done.17.refs_6_), channel_id=1, source_target_pairs={{0,4},{4,0},{8,12},{12,8},{1,5},{5,1},{9,13},{13,9},{2,6},{6,2},{1... | collective-permute-start | bytes 221192 | tf_op jit(solution)/shard_map/ppermute | solution.py:397
  78.4 5.2 %collective-permute-start.20 = (bf16[32,1152]{1,0:T(8,128)(2,1)S(1)}, bf16[32,1152]{1,0:T(8,128)(2,1)S(1)}, u32[]{:S(2)}, u32[]{:S(2)}) collective-permute-start(bf16[32,1152]{1,0:T(8,128)(2,1)S(1)} %shard_map.75.refs_4_), channel_id=1, source_target_pairs={{0,4},{4,0},{8,12},{12,8},{1,5},{5,1},{9,13},{13,9},{2,6},{6,2},{1... | collective-permute-start | bytes 221192 | tf_op jit(solution)/shard_map/ppermute | solution.py:397
  80.4 4.4 %collective-permute-start.22 = (bf16[32,1152]{1,0:T(8,128)(2,1)S(1)}, bf16[32,1152]{1,0:T(8,128)(2,1)S(1)}, u32[]{:S(2)}, u32[]{:S(2)}) collective-permute-start(bf16[32,1152]{1,0:T(8,128)(2,1)S(1)} %collective-permute-done.21.refs_6_), channel_id=1, source_target_pairs={{0,4},{4,0},{8,12},{12,8},{1,5},{5,1},{9,13},{13,9},{2,6},{6,2},{1... | collective-permute-start | bytes 221192 | tf_op jit(solution)/shard_map/ppermute | solution.py:397
  82.9 3.0 %collective-permute-start.23 = (bf16[128,1152]{1,0:T(8,128)(2,1)S(1)}, bf16[128,1152]{1,0:T(8,128)(2,1)S(1)}, u32[]{:S(2)}, u32[]{:S(2)}) collective-permute-start(bf16[128,1152]{1,0:T(8,128)(2,1)S(1)} %shard_map.78), channel_id=1, source_target_pairs={{0,1},{1,0},{2,3},{3,2},{4,5},{5,4},{6,7},{7,6},{8,9},{9,8},{10,11... | collective-permute-start | bytes 884744 | tf_op jit(solution)/shard_map/ppermute | solution.py:394
  84.8 1.6 %collective-permute-start.24 = (bf16[128,1152]{1,0:T(8,128)(2,1)S(1)}, bf16[128,1152]{1,0:T(8,128)(2,1)S(1)}, u32[]{:S(2)}, u32[]{:S(2)}) collective-permute-start(bf16[128,1152]{1,0:T(8,128)(2,1)S(1)} %shard_map.79), channel_id=1, source_target_pairs={{0,1},{1,0},{2,3},{3,2},{4,5},{5,4},{6,7},{7,6},{8,9},{9,8},{10,11... | collective-permute-start | bytes 884744 | tf_op jit(solution)/shard_map/ppermute | solution.py:394

commit v17 on v16

--- a/solution.py
+++ b/solution.py
@@ -68,7 +68,6 @@
     rows = lefts[0][0].shape[0]
     in_half = w_ref.shape[1] // wide // 2
     first = in_half // groups
-    ahead = min(steps, max(2, steps // 2))
     here = lax.axis_index("sub")
 
     def column(n):
@@ -87,11 +86,6 @@
 
     def step(n):
         copy(n).wait()
-        if any(splits):
-            if n + ahead < steps:
-                copy(n + ahead).start()
-        else:
-            pl.when(n + ahead < steps)(lambda: copy(n + ahead).start())
         product, begin = None, 0
         for index in range(len(lefts[0])):
             parts = [left[index][...] for left in lefts]
@@ -114,7 +108,7 @@
             else:
                 outs.pop(0)[:, at(column(n))] = value
 
-    for n in range(ahead):
+    for n in range(steps):
         copy(n).start()
     if any(splits):
         for n in range(steps):

time: 87.4 us -> 87.1 us (level)
  Pallas kernels: 39.9 us -> 39 us
    pallas_call x5, Pallas kernels: 36.4 us -> 35.4 us  [multiply(): pl.pallas_call(body, out_shape=out_shape, in_specs=[VMEM] * spans[-1][1]...]
  transfers between devices with their start and end apart: 25 -> 25, of which waited for: 14 -> 13; matrix products, arithmetic and copies ran while one was open for 0% -> 0% of each run, Pallas kernels for 45% -> 44%
where the time goes in v17:
time: 87.1 us; the launch traced here: 87 us
  Pallas kernels  39 us (45%)
  starting transfers between devices  25.7 us (30%)
  waiting for transfers between devices  19.9 us (23%)
  local copies, waits for them, and re-layouts  1.46 us (2%)
  between operations  0.92 us (1%)
    pallas_call x5, Pallas kernels, multiply(): pl.pallas_call(body, out_shape=out_shape, in_specs=[VMEM] * spans[-1][1]...  35.4 us
    ppermute x15, starting transfers between devices, exchange(): lax.ppermute(values, 'tensor', [(t, t ^ 1 << level) for t in range(tensor...  19.4 us
    ppermute x15, waiting for transfers between devices, exchange(): lax.ppermute(values, 'tensor', [(t, t ^ 1 << level) for t in range(tensor...  15.5 us
    ppermute x4, starting transfers between devices, from_seq(): lax.ppermute(part, 'seq', [(s, (s + shift) % seq_count) for s in range(se...  5.11 us
    ppermute x4, waiting for transfers between devices, from_seq(): lax.ppermute(part, 'seq', [(s, (s + shift) % seq_count) for s in range(se...  2.5 us
    ppermute x6, waiting for transfers between devices, swap(): return lax.ppermute(values, 'sub', [(0, 1), (1, 0)])  1.88 us
  transfers between devices with their start and end apart: 25, of which 13 were waited for; matrix products, arithmetic and copies ran while one was open for 0% of the time, Pallas kernels for 44%

profile of v17, /device:TPU:0, one launch (start us, length us, event | category | flops | bytes accessed | tf_op | source)
XLA Modules:
  0.0 87.0 jit_solution(6995002298749232951)
XLA Ops:
  0.6 1.4 %copy-done = bf16[128,6656]{1,0:T(8,128)(2,1)S(1)} copy-done((bf16[128,6656]{1,0:T(8,128)(2,1)S(1)}, bf16[128,6656]{1,0:T(8,128)(2,1)}, u32[]{:S(2)}) %copy-start) | copy-done | bytes 1703960
  2.1 0.2 shard_map.59
  2.3 3.0 %collective-permute-start = (bf16[128,2048]{1,0:T(8,128)(2,1)S(1)}, bf16[128,2048]{1,0:T(8,128)(2,1)S(1)}, u32[]{:S(2)}, u32[]{:S(2)}) collective-permute-start(bf16[128,2048]{1,0:T(8,128)(2,1)S(1)} %get-tuple-element.31.refs_4_.refs_0_), channel_id=1, source_target_pairs={{0,2},{2,0},{1,3},{3,1},{4,6},{6,4},{5,7},{7,5},{8,10},{10,8},{9,1... | collective-permute-start | bytes 1572872 | tf_op jit(solution)/shard_map/ppermute | solution.py:418
  5.3 0.1 collective-permute-start.3
  5.3 12.7 %shard_map.60.refs_3_ = f32[128,4096]{1,0:T(8,128)S(1)} custom-call(bf16[128,1792]{1,0:T(8,128)(2,1)S(1)} %get-tuple-element.32.refs_0_, bf16[128,1536]{1,0:T(8,128)(2,1)S(1)} %get-tuple-element.33.refs_1_, bf16[128,1280]{1,0:T(8,128)(2,1)S(1)} %get-tuple-element.34.refs_2_, bf16[6656,4096]{1,0:T(8,128)(2,1)} %refs_1_.5, ...), custom_call_target="tpu_custom_call" | custom-call | flops 1 | bytes 1 | tf_op jit(solution)/shard_map/pallas_call | solution.py:139
  18.0 7.3 %shard_map.61 = (bf16[128,1024]{1,0:T(8,128)(2,1)S(1)}, f32[128,1024]{1,0:T(8,128)S(1)}, bf16[128,1024]{1,0:T(8,128)(2,1)S(1)}, f32[128,1024]{1,0:T(8,128)S(1)}, f32[128,4096]{1,0:T(8,128)S(1)}) custom-call(bf16[128,2048]{1,0:T(8,128)(2,1)S(1)} %get-tuple-element.31.refs_4_.refs_0_, bf16[128,2048]{1,0:T(8,128)(2,1)S(1)} %collective-permute-done.refs_1_, ...), custom_call_target="tpu_custom_call" | custom-call | flops 1 | bytes 1 | tf_op jit(solution)/shard_map/pallas_call | solution.py:139
  25.4 0.5 collective-permute-start.2
  25.9 1.1 %collective-permute-done.3.refs_4_.refs_0_ = bf16[128,1792]{1,0:T(8,128)(2,1)S(1)} collective-permute-done((bf16[128,1792]{1,0:T(8,128)(2,1)S(1)}, bf16[128,1792]{1,0:T(8,128)(2,1)S(1)}, u32[]{:S(2)}, u32[]{:S(2)}) %collective-permute-start.3) | collective-permute-done | bytes 458784 | tf_op jit(solution)/shard_map/ppermute | solution.py:418
  27.0 0.3 collective-permute-done.2.refs_3_
  27.3 0.1 shard_map.62
  27.4 2.2 %collective-permute-start.4 = (bf16[64,2048]{1,0:T(8,128)(2,1)S(1)}, bf16[64,2048]{1,0:T(8,128)(2,1)S(1)}, u32[]{:S(2)}, u32[]{:S(2)}) collective-permute-start(bf16[64,2048]{1,0:T(8,128)(2,1)S(1)} %get-tuple-element.40.refs_3_), channel_id=1, source_target_pairs={{0,4},{4,0},{8,12},{12,8},{1,5},{5,1},{9,13},{13,9},{2,6},{6,2},{1... | collective-permute-start | bytes 786440 | tf_op jit(solution)/shard_map/ppermute | solution.py:391
  29.6 1.5 %collective-permute-start.6 = (bf16[128,1536]{1,0:T(8,128)(2,1)S(1)}, bf16[128,1536]{1,0:T(8,128)(2,1)S(1)}, u32[]{:S(2)}, u32[]{:S(2)}) collective-permute-start(bf16[128,1536]{1,0:T(8,128)(2,1)S(1)} %get-tuple-element.33.refs_1_), channel_id=1, source_target_pairs={{0,2},{2,0},{1,3},{3,1},{4,6},{6,4},{5,7},{7,5},{8,10},{10,8},{9,1... | collective-permute-start | bytes 1179656 | tf_op jit(solution)/shard_map/ppermute | solution.py:418
  31.0 0.5 collective-permute-start.10
  31.6 5.8 %shard_map.63.refs_2_ = f32[128,4096]{1,0:T(8,128)S(1)} custom-call(bf16[128,1792]{1,0:T(8,128)(2,1)S(1)} %collective-permute-done.3.refs_4_.refs_0_, bf16[6656,4096]{1,0:T(8,128)(2,1)} %refs_1_.5, f32[128,4096]{1,0:T(8,128)S(1)} %get-tuple-element.41.refs_2_, bf16[64,2048]{1,0:T(8,128)(2,1)S(1)} %get-tuple-element.40.refs_3_), custom_call_target="tpu_custom_call" | custom-call | flops 1 | bytes 1 | tf_op jit(solution)/shard_map/pallas_call | solution.py:139
  37.5 2.6 %collective-permute-start.5 = (bf16[32,2048]{1,0:T(8,128)(2,1)S(1)}, bf16[32,2048]{1,0:T(8,128)(2,1)S(1)}, u32[]{:S(2)}, u32[]{:S(2)}) collective-permute-start(bf16[32,2048]{1,0:T(8,128)(2,1)S(1)} %get-tuple-element.43.refs_3_), channel_id=1, source_target_pairs={{0,8},{4,12},{8,0},{12,4},{1,9},{5,13},{9,1},{13,5},{2,10},{6,14},... | collective-permute-start | bytes 393224 | tf_op jit(solution)/shard_map/ppermute | solution.py:391
  40.2 1.4 %collective-permute-done.6.refs_0_ = bf16[128,1536]{1,0:T(8,128)(2,1)S(1)} collective-permute-done((bf16[128,1536]{1,0:T(8,128)(2,1)S(1)}, bf16[128,1536]{1,0:T(8,128)(2,1)S(1)}, u32[]{:S(2)}, u32[]{:S(2)}) %collective-permute-start.6) | collective-permute-done | bytes 393248 | tf_op jit(solution)/shard_map/ppermute | solution.py:418
  41.6 5.2 %shard_map.65.refs_0_.refs_2_ = f32[128,4096]{1,0:T(8,128)S(1)} custom-call(bf16[128,1536]{1,0:T(8,128)(2,1)S(1)} %collective-permute-done.6.refs_0_, bf16[6656,4096]{1,0:T(8,128)(2,1)} %refs_1_.5, f32[128,4096]{1,0:T(8,128)S(1)} %shard_map.63.refs_2_, bf16[32,2048]{1,0:T(8,128)(2,1)S(1)} %get-tuple-element.43.refs_3_), custom_call_target="tpu_custom_call" | custom-call | flops 1 | bytes 1 | tf_op jit(solution)/shard_map/pallas_call | solution.py:139
  46.8 0.5 shard_map.66
  47.2 0.1 collective-permute-start.7
  47.3 3.0 %collective-permute-start.8 = (bf16[32,2048]{1,0:T(8,128)(2,1)S(1)}, bf16[32,2048]{1,0:T(8,128)(2,1)S(1)}, u32[]{:S(2)}, u32[]{:S(2)}) collective-permute-start(bf16[32,2048]{1,0:T(8,128)(2,1)S(1)} %get-tuple-element.44.refs_3_.refs_0_), channel_id=1, source_target_pairs={{0,8},{4,12},{8,0},{12,4},{1,9},{5,13},{9,1},{13,5},{2,10},{6,14},... | collective-permute-start | bytes 393224 | tf_op jit(solution)/shard_map/ppermute | solution.py:391
  50.3 4.5 %shard_map.67 = (bf16[128,1024]{1,0:T(8,128)(2,1)S(1)}, f32[128,1024]{1,0:T(8,128)S(1)}, bf16[128,1024]{1,0:T(8,128)(2,1)S(1)}, f32[128,1024]{1,0:T(8,128)S(1)}) custom-call(bf16[128,1280]{1,0:T(8,128)(2,1)S(1)} %collective-permute-done.10.refs_0_, bf16[6656,4096]{1,0:T(8,128)(2,1)} %refs_1_.5, f32[128,4096]{1,0:T(8,128)S(1)} %shard_map.65.refs_0_.refs_2_, ...), custom_call_target="tpu_custom_call" | custom-call | flops 1 | bytes 1 | tf_op jit(solution)/shard_map/pallas_call | solution.py:139
  54.8 0.1 collective-permute-start.11
  55.0 0.5 collective-permute-start.13
  55.4 1.0 %collective-permute-done.11.refs_1_ = bf16[128,1024]{1,0:T(8,128)(2,1)S(1)} collective-permute-done((bf16[128,1024]{1,0:T(8,128)(2,1)S(1)}, bf16[128,1024]{1,0:T(8,128)(2,1)S(1)}, u32[]{:S(2)}, u32[]{:S(2)}) %collective-permute-start.11) | collective-permute-done | bytes 262176 | tf_op jit(solution)/shard_map/ppermute | solution.py:388
  56.5 1.6 %collective-permute-start.12 = (bf16[64,1024]{1,0:T(8,128)(2,1)S(1)}, bf16[64,1024]{1,0:T(8,128)(2,1)S(1)}, u32[]{:S(2)}, u32[]{:S(2)}) collective-permute-start(bf16[64,1024]{1,0:T(8,128)(2,1)S(1)} %get-tuple-element.48), channel_id=1, source_target_pairs={{0,4},{4,0},{8,12},{12,8},{1,5},{5,1},{9,13},{13,9},{2,6},{6,2},{1... | collective-permute-start | bytes 393224 | tf_op jit(solution)/shard_map/ppermute | solution.py:391
  58.2 0.5 collective-permute-start.15
  58.7 1.6 %collective-permute-start.9 = (bf16[32,2048]{1,0:T(8,128)(2,1)S(1)}, bf16[32,2048]{1,0:T(8,128)(2,1)S(1)}, u32[]{:S(2)}, u32[]{:S(2)}) collective-permute-start(bf16[32,2048]{1,0:T(8,128)(2,1)S(1)} %collective-permute-done.8.refs_2_.refs_1_), channel_id=1, source_target_pairs={{0,4},{4,0},{8,12},{12,8},{1,5},{5,1},{9,13},{13,9},{2,6},{6,2},{1... | collective-permute-start | bytes 393224 | tf_op jit(solution)/shard_map/ppermute | solution.py:391
  60.3 2.6 %collective-permute-done.12.refs_1_ = bf16[64,1024]{1,0:T(8,128)(2,1)S(1)} collective-permute-done((bf16[64,1024]{1,0:T(8,128)(2,1)S(1)}, bf16[64,1024]{1,0:T(8,128)(2,1)S(1)}, u32[]{:S(2)}, u32[]{:S(2)}) %collective-permute-start.12) | collective-permute-done | bytes 131104 | tf_op jit(solution)/shard_map/ppermute | solution.py:391
  62.9 0.7 collective-permute-start.14
  63.7 2.8 %collective-permute-done.15.refs_1_ = bf16[64,1024]{1,0:T(8,128)(2,1)S(1)} collective-permute-done((bf16[64,1024]{1,0:T(8,128)(2,1)S(1)}, bf16[64,1024]{1,0:T(8,128)(2,1)S(1)}, u32[]{:S(2)}, u32[]{:S(2)}) %collective-permute-start.15) | collective-permute-done | bytes 131104 | tf_op jit(solution)/shard_map/ppermute | solution.py:391
  66.5 4.2 %collective-permute-done.14.came_ref = bf16[32,1024]{1,0:T(8,128)(2,1)S(1)} collective-permute-done((bf16[32,1024]{1,0:T(8,128)(2,1)S(1)}, bf16[32,1024]{1,0:T(8,128)(2,1)S(1)}, u32[]{:S(2)}, u32[]{:S(2)}) %collective-permute-start.14) | collective-permute-done | bytes 65568 | tf_op jit(solution)/shard_map/ppermute | solution.py:391
  70.7 0.3 shard_map.73.refs_4_
  71.1 1.7 %collective-permute-start.17 = (bf16[32,1152]{1,0:T(8,128)(2,1)S(1)}, bf16[32,1152]{1,0:T(8,128)(2,1)S(1)}, u32[]{:S(2)}, u32[]{:S(2)}) collective-permute-start(bf16[32,1152]{1,0:T(8,128)(2,1)S(1)} %shard_map.73.refs_4_), channel_id=1, source_target_pairs={{0,8},{4,12},{8,0},{12,4},{1,9},{5,13},{9,1},{13,5},{2,10},{6,14},... | collective-permute-start | bytes 221192 | tf_op jit(solution)/shard_map/ppermute | solution.py:391
  72.8 0.4 shard_map.75.refs_4_
  73.2 1.3 %collective-permute-start.21 = (bf16[32,1152]{1,0:T(8,128)(2,1)S(1)}, bf16[32,1152]{1,0:T(8,128)(2,1)S(1)}, u32[]{:S(2)}, u32[]{:S(2)}) collective-permute-start(bf16[32,1152]{1,0:T(8,128)(2,1)S(1)} %shard_map.75.refs_4_), channel_id=1, source_target_pairs={{0,8},{4,12},{8,0},{12,4},{1,9},{5,13},{9,1},{13,5},{2,10},{6,14},... | collective-permute-start | bytes 221192 | tf_op jit(solution)/shard_map/ppermute | solution.py:391
  74.5 1.8 %collective-permute-start.16 = (bf16[32,1152]{1,0:T(8,128)(2,1)S(1)}, bf16[32,1152]{1,0:T(8,128)(2,1)S(1)}, u32[]{:S(2)}, u32[]{:S(2)}) collective-permute-start(bf16[32,1152]{1,0:T(8,128)(2,1)S(1)} %shard_map.73.refs_4_), channel_id=1, source_target_pairs={{0,4},{4,0},{8,12},{12,8},{1,5},{5,1},{9,13},{13,9},{2,6},{6,2},{1... | collective-permute-start | bytes 221192 | tf_op jit(solution)/shard_map/ppermute | solution.py:391
  76.3 1.7 %collective-permute-done.17.refs_6_ = bf16[32,1152]{1,0:T(8,128)(2,1)S(1)} collective-permute-done((bf16[32,1152]{1,0:T(8,128)(2,1)S(1)}, bf16[32,1152]{1,0:T(8,128)(2,1)S(1)}, u32[]{:S(2)}, u32[]{:S(2)}) %collective-permute-start.17) | collective-permute-done | bytes 73760 | tf_op jit(solution)/shard_map/ppermute | solution.py:391
  78.1 2.0 %collective-permute-start.20 = (bf16[32,1152]{1,0:T(8,128)(2,1)S(1)}, bf16[32,1152]{1,0:T(8,128)(2,1)S(1)}, u32[]{:S(2)}, u32[]{:S(2)}) collective-permute-start(bf16[32,1152]{1,0:T(8,128)(2,1)S(1)} %shard_map.75.refs_4_), channel_id=1, source_target_pairs={{0,4},{4,0},{8,12},{12,8},{1,5},{5,1},{9,13},{13,9},{2,6},{6,2},{1... | collective-permute-start | bytes 221192 | tf_op jit(solution)/shard_map/ppermute | solution.py:391
  80.1 0.4 collective-permute-done.16.refs_5_
  80.5 1.9 %collective-permute-done.18.refs_7_ = bf16[32,1152]{1,0:T(8,128)(2,1)S(1)} collective-permute-done((bf16[32,1152]{1,0:T(8,128)(2,1)S(1)}, bf16[32,1152]{1,0:T(8,128)(2,1)S(1)}, u32[]{:S(2)}, u32[]{:S(2)}) %collective-permute-start.18) | collective-permute-done | bytes 73760 | tf_op jit(solution)/shard_map/ppermute | solution.py:391
  82.4 0.1 shard_map.78
  82.5 0.7 collective-permute-done.20.refs_5_
  83.2 1.2 %collective-permute-done.22.refs_7_ = bf16[32,1152]{1,0:T(8,128)(2,1)S(1)} collective-permute-done((bf16[32,1152]{1,0:T(8,128)(2,1)S(1)}, bf16[32,1152]{1,0:T(8,128)(2,1)S(1)}, u32[]{:S(2)}, u32[]{:S(2)}) %collective-permute-start.22) | collective-permute-done | bytes 73760 | tf_op jit(solution)/shard_map/ppermute | solution.py:391
  84.4 0.1 shard_map.79
  84.6 0.1 shard_map.76.refs_1_.refs_4_
  84.7 0.8 shard_map.77.refs_0_
  85.6 0.6 collective-permute-done.24.refs_2_
  86.1 0.8 shard_map.80
  (32 shorter events, 0.6 us)
Async XLA Ops:
  0.6 1.5 %copy-start = (bf16[128,6656]{1,0:T(8,128)(2,1)S(1)}, bf16[128,6656]{1,0:T(8,128)(2,1)}, u32[]{:S(2)}) copy-start(bf16[128,6656]{1,0:T(8,128)(2,1)} %in_ref.1) | copy-start | bytes 5111812
  2.3 15.8 %collective-permute-start = (bf16[128,2048]{1,0:T(8,128)(2,1)S(1)}, bf16[128,2048]{1,0:T(8,128)(2,1)S(1)}, u32[]{:S(2)}, u32[]{:S(2)}) collective-permute-start(bf16[128,2048]{1,0:T(8,128)(2,1)S(1)} %get-tuple-element.31.refs_4_.refs_0_), channel_id=1, source_target_pairs={{0,2},{2,0},{1,3},{3,1},{4,6},{6,4},{5,7},{7,5},{8,10},{10,8},{9,1... | collective-permute-start | bytes 1572872 | tf_op jit(solution)/shard_map/ppermute | solution.py:418
  5.3 21.8 %collective-permute-start.3 = (bf16[128,1792]{1,0:T(8,128)(2,1)S(1)}, bf16[128,1792]{1,0:T(8,128)(2,1)S(1)}, u32[]{:S(2)}, u32[]{:S(2)}) collective-permute-start(bf16[128,1792]{1,0:T(8,128)(2,1)S(1)} %get-tuple-element.32.refs_0_), channel_id=1, source_target_pairs={{0,2},{2,0},{1,3},{3,1},{4,6},{6,4},{5,7},{7,5},{8,10},{10,8},{9,1... | collective-permute-start | bytes 1376264 | tf_op jit(solution)/shard_map/ppermute | solution.py:418
  25.3 1.7 %collective-permute-start.1 = (bf16[128,1024]{1,0:T(8,128)(2,1)S(1)}, bf16[128,1024]{1,0:T(8,128)(2,1)S(1)}, u32[]{:S(2)}, u32[]{:S(2)}) collective-permute-start(bf16[128,1024]{1,0:T(8,128)(2,1)S(1)} %get-tuple-element.37), channel_id=1, source_target_pairs={{0,1},{1,0},{2,3},{3,2},{4,5},{5,4},{6,7},{7,6},{8,9},{9,8},{10,11... | collective-permute-start | bytes 786440 | tf_op jit(solution)/shard_map/ppermute | solution.py:388
  25.4 1.9 %collective-permute-start.2 = (bf16[128,1024]{1,0:T(8,128)(2,1)S(1)}, bf16[128,1024]{1,0:T(8,128)(2,1)S(1)}, u32[]{:S(2)}, u32[]{:S(2)}) collective-permute-start(bf16[128,1024]{1,0:T(8,128)(2,1)S(1)} %get-tuple-element.38), channel_id=1, source_target_pairs={{0,1},{1,0},{2,3},{3,2},{4,5},{5,4},{6,7},{7,6},{8,9},{9,8},{10,11... | collective-permute-start | bytes 786440 | tf_op jit(solution)/shard_map/ppermute | solution.py:388
  27.4 10.0 %collective-permute-start.4 = (bf16[64,2048]{1,0:T(8,128)(2,1)S(1)}, bf16[64,2048]{1,0:T(8,128)(2,1)S(1)}, u32[]{:S(2)}, u32[]{:S(2)}) collective-permute-start(bf16[64,2048]{1,0:T(8,128)(2,1)S(1)} %get-tuple-element.40.refs_3_), channel_id=1, source_target_pairs={{0,4},{4,0},{8,12},{12,8},{1,5},{5,1},{9,13},{13,9},{2,6},{6,2},{1... | collective-permute-start | bytes 786440 | tf_op jit(solution)/shard_map/ppermute | solution.py:391
  29.6 12.0 %collective-permute-start.6 = (bf16[128,1536]{1,0:T(8,128)(2,1)S(1)}, bf16[128,1536]{1,0:T(8,128)(2,1)S(1)}, u32[]{:S(2)}, u32[]{:S(2)}) collective-permute-start(bf16[128,1536]{1,0:T(8,128)(2,1)S(1)} %get-tuple-element.33.refs_1_), channel_id=1, source_target_pairs={{0,2},{2,0},{1,3},{3,1},{4,6},{6,4},{5,7},{7,5},{8,10},{10,8},{9,1... | collective-permute-start | bytes 1179656 | tf_op jit(solution)/shard_map/ppermute | solution.py:418
  31.0 19.3 %collective-permute-start.10 = (bf16[128,1280]{1,0:T(8,128)(2,1)S(1)}, bf16[128,1280]{1,0:T(8,128)(2,1)S(1)}, u32[]{:S(2)}, u32[]{:S(2)}) collective-permute-start(bf16[128,1280]{1,0:T(8,128)(2,1)S(1)} %get-tuple-element.34.refs_2_), channel_id=1, source_target_pairs={{0,2},{2,0},{1,3},{3,1},{4,6},{6,4},{5,7},{7,5},{8,10},{10,8},{9,1... | collective-permute-start | bytes 983048 | tf_op jit(solution)/shard_map/ppermute | solution.py:418
  37.4 2.7 %copy-start.2 = (s32[4096]{0:T(1024)S(1)}, s32[4096]{0:T(1024)}, u32[]{:S(2)}) copy-start(s32[4096]{0:T(1024)} %param.6) | copy-start | bytes 49156
  37.5 9.2 %collective-permute-start.5 = (bf16[32,2048]{1,0:T(8,128)(2,1)S(1)}, bf16[32,2048]{1,0:T(8,128)(2,1)S(1)}, u32[]{:S(2)}, u32[]{:S(2)}) collective-permute-start(bf16[32,2048]{1,0:T(8,128)(2,1)S(1)} %get-tuple-element.43.refs_3_), channel_id=1, source_target_pairs={{0,8},{4,12},{8,0},{12,4},{1,9},{5,13},{9,1},{13,5},{2,10},{6,14},... | collective-permute-start | bytes 393224 | tf_op jit(solution)/shard_map/ppermute | solution.py:391
  40.2 6.6 %copy-start.1 = (f32[128,128]{1,0:T(8,128)S(1)}, f32[128,128]{1,0:T(8,128)}, u32[]{:S(2)}) copy-start(f32[128,128]{1,0:T(8,128)} %constant.9.clone.rotation_ref) | copy-start | bytes 196612
  47.2 7.7 %collective-permute-start.7 = (bf16[32,2048]{1,0:T(8,128)(2,1)S(1)}, bf16[32,2048]{1,0:T(8,128)(2,1)S(1)}, u32[]{:S(2)}, u32[]{:S(2)}) collective-permute-start(bf16[32,2048]{1,0:T(8,128)(2,1)S(1)} %get-tuple-element.44.refs_3_.refs_0_), channel_id=1, source_target_pairs={{0,4},{4,0},{8,12},{12,8},{1,5},{5,1},{9,13},{13,9},{2,6},{6,2},{1... | collective-permute-start | bytes 393224 | tf_op jit(solution)/shard_map/ppermute | solution.py:391
  47.3 7.6 %collective-permute-start.8 = (bf16[32,2048]{1,0:T(8,128)(2,1)S(1)}, bf16[32,2048]{1,0:T(8,128)(2,1)S(1)}, u32[]{:S(2)}, u32[]{:S(2)}) collective-permute-start(bf16[32,2048]{1,0:T(8,128)(2,1)S(1)} %get-tuple-element.44.refs_3_.refs_0_), channel_id=1, source_target_pairs={{0,8},{4,12},{8,0},{12,4},{1,9},{5,13},{9,1},{13,5},{2,10},{6,14},... | collective-permute-start | bytes 393224 | tf_op jit(solution)/shard_map/ppermute | solution.py:391
  54.8 1.6 %collective-permute-start.11 = (bf16[128,1024]{1,0:T(8,128)(2,1)S(1)}, bf16[128,1024]{1,0:T(8,128)(2,1)S(1)}, u32[]{:S(2)}, u32[]{:S(2)}) collective-permute-start(bf16[128,1024]{1,0:T(8,128)(2,1)S(1)} %get-tuple-element.46), channel_id=1, source_target_pairs={{0,1},{1,0},{2,3},{3,2},{4,5},{5,4},{6,7},{7,6},{8,9},{9,8},{10,11... | collective-permute-start | bytes 786440 | tf_op jit(solution)/shard_map/ppermute | solution.py:388
  55.0 3.2 %collective-permute-start.13 = (bf16[128,1024]{1,0:T(8,128)(2,1)S(1)}, bf16[128,1024]{1,0:T(8,128)(2,1)S(1)}, u32[]{:S(2)}, u32[]{:S(2)}) collective-permute-start(bf16[128,1024]{1,0:T(8,128)(2,1)S(1)} %shard_map.69), channel_id=1, source_target_pairs={{0,1},{1,0},{2,3},{3,2},{4,5},{5,4},{6,7},{7,6},{8,9},{9,8},{10,11... | collective-permute-start | bytes 786440 | tf_op jit(solution)/shard_map/ppermute | solution.py:388
  56.5 6.4 %collective-permute-start.12 = (bf16[64,1024]{1,0:T(8,128)(2,1)S(1)}, bf16[64,1024]{1,0:T(8,128)(2,1)S(1)}, u32[]{:S(2)}, u32[]{:S(2)}) collective-permute-start(bf16[64,1024]{1,0:T(8,128)(2,1)S(1)} %get-tuple-element.48), channel_id=1, source_target_pairs={{0,4},{4,0},{8,12},{12,8},{1,5},{5,1},{9,13},{13,9},{2,6},{6,2},{1... | collective-permute-start | bytes 393224 | tf_op jit(solution)/shard_map/ppermute | solution.py:391
  58.2 8.2 %collective-permute-start.15 = (bf16[64,1024]{1,0:T(8,128)(2,1)S(1)}, bf16[64,1024]{1,0:T(8,128)(2,1)S(1)}, u32[]{:S(2)}, u32[]{:S(2)}) collective-permute-start(bf16[64,1024]{1,0:T(8,128)(2,1)S(1)} %get-tuple-element.51.refs_2_), channel_id=1, source_target_pairs={{0,4},{4,0},{8,12},{12,8},{1,5},{5,1},{9,13},{13,9},{2,6},{6,2},{1... | collective-permute-start | bytes 393224 | tf_op jit(solution)/shard_map/ppermute | solution.py:391
  58.7 14.1 %collective-permute-start.9 = (bf16[32,2048]{1,0:T(8,128)(2,1)S(1)}, bf16[32,2048]{1,0:T(8,128)(2,1)S(1)}, u32[]{:S(2)}, u32[]{:S(2)}) collective-permute-start(bf16[32,2048]{1,0:T(8,128)(2,1)S(1)} %collective-permute-done.8.refs_2_.refs_1_), channel_id=1, source_target_pairs={{0,4},{4,0},{8,12},{12,8},{1,5},{5,1},{9,13},{13,9},{2,6},{6,2},{1... | collective-permute-start | bytes 393224 | tf_op jit(solution)/shard_map/ppermute | solution.py:391
  62.9 7.8 %collective-permute-start.14 = (bf16[32,1024]{1,0:T(8,128)(2,1)S(1)}, bf16[32,1024]{1,0:T(8,128)(2,1)S(1)}, u32[]{:S(2)}, u32[]{:S(2)}) collective-permute-start(bf16[32,1024]{1,0:T(8,128)(2,1)S(1)} %get-tuple-element.53), channel_id=1, source_target_pairs={{0,8},{4,12},{8,0},{12,4},{1,9},{5,13},{9,1},{13,5},{2,10},{6,14},... | collective-permute-start | bytes 196616 | tf_op jit(solution)/shard_map/ppermute | solution.py:391
  66.4 6.4 %collective-permute-start.19 = (bf16[32,1024]{1,0:T(8,128)(2,1)S(1)}, bf16[32,1024]{1,0:T(8,128)(2,1)S(1)}, u32[]{:S(2)}, u32[]{:S(2)}) collective-permute-start(bf16[32,1024]{1,0:T(8,128)(2,1)S(1)} %get-tuple-element.56.refs_0_), channel_id=1, source_target_pairs={{0,8},{4,12},{8,0},{12,4},{1,9},{5,13},{9,1},{13,5},{2,10},{6,14},... | collective-permute-start | bytes 196616 | tf_op jit(solution)/shard_map/ppermute | solution.py:391
  71.1 7.0 %collective-permute-start.17 = (bf16[32,1152]{1,0:T(8,128)(2,1)S(1)}, bf16[32,1152]{1,0:T(8,128)(2,1)S(1)}, u32[]{:S(2)}, u32[]{:S(2)}) collective-permute-start(bf16[32,1152]{1,0:T(8,128)(2,1)S(1)} %shard_map.73.refs_4_), channel_id=1, source_target_pairs={{0,8},{4,12},{8,0},{12,4},{1,9},{5,13},{9,1},{13,5},{2,10},{6,14},... | collective-permute-start | bytes 221192 | tf_op jit(solution)/shard_map/ppermute | solution.py:391
  73.2 6.9 %collective-permute-start.21 = (bf16[32,1152]{1,0:T(8,128)(2,1)S(1)}, bf16[32,1152]{1,0:T(8,128)(2,1)S(1)}, u32[]{:S(2)}, u32[]{:S(2)}) collective-permute-start(bf16[32,1152]{1,0:T(8,128)(2,1)S(1)} %shard_map.75.refs_4_), channel_id=1, source_target_pairs={{0,8},{4,12},{8,0},{12,4},{1,9},{5,13},{9,1},{13,5},{2,10},{6,14},... | collective-permute-start | bytes 221192 | tf_op jit(solution)/shard_map/ppermute | solution.py:391
  74.5 6.0 %collective-permute-start.16 = (bf16[32,1152]{1,0:T(8,128)(2,1)S(1)}, bf16[32,1152]{1,0:T(8,128)(2,1)S(1)}, u32[]{:S(2)}, u32[]{:S(2)}) collective-permute-start(bf16[32,1152]{1,0:T(8,128)(2,1)S(1)} %shard_map.73.refs_4_), channel_id=1, source_target_pairs={{0,4},{4,0},{8,12},{12,8},{1,5},{5,1},{9,13},{13,9},{2,6},{6,2},{1... | collective-permute-start | bytes 221192 | tf_op jit(solution)/shard_map/ppermute | solution.py:391
  78.1 4.4 %collective-permute-start.18 = (bf16[32,1152]{1,0:T(8,128)(2,1)S(1)}, bf16[32,1152]{1,0:T(8,128)(2,1)S(1)}, u32[]{:S(2)}, u32[]{:S(2)}) collective-permute-start(bf16[32,1152]{1,0:T(8,128)(2,1)S(1)} %collective-permute-done.17.refs_6_), channel_id=1, source_target_pairs={{0,4},{4,0},{8,12},{12,8},{1,5},{5,1},{9,13},{13,9},{2,6},{6,2},{1... | collective-permute-start | bytes 221192 | tf_op jit(solution)/shard_map/ppermute | solution.py:391
  78.1 5.1 %collective-permute-start.20 = (bf16[32,1152]{1,0:T(8,128)(2,1)S(1)}, bf16[32,1152]{1,0:T(8,128)(2,1)S(1)}, u32[]{:S(2)}, u32[]{:S(2)}) collective-permute-start(bf16[32,1152]{1,0:T(8,128)(2,1)S(1)} %shard_map.75.refs_4_), channel_id=1, source_target_pairs={{0,4},{4,0},{8,12},{12,8},{1,5},{5,1},{9,13},{13,9},{2,6},{6,2},{1... | collective-permute-start | bytes 221192 | tf_op jit(solution)/shard_map/ppermute | solution.py:391
  80.1 4.4 %collective-permute-start.22 = (bf16[32,1152]{1,0:T(8,128)(2,1)S(1)}, bf16[32,1152]{1,0:T(8,128)(2,1)S(1)}, u32[]{:S(2)}, u32[]{:S(2)}) collective-permute-start(bf16[32,1152]{1,0:T(8,128)(2,1)S(1)} %collective-permute-done.21.refs_6_), channel_id=1, source_target_pairs={{0,4},{4,0},{8,12},{12,8},{1,5},{5,1},{9,13},{13,9},{2,6},{6,2},{1... | collective-permute-start | bytes 221192 | tf_op jit(solution)/shard_map/ppermute | solution.py:391
  82.5 3.1 %collective-permute-start.23 = (bf16[128,1152]{1,0:T(8,128)(2,1)S(1)}, bf16[128,1152]{1,0:T(8,128)(2,1)S(1)}, u32[]{:S(2)}, u32[]{:S(2)}) collective-permute-start(bf16[128,1152]{1,0:T(8,128)(2,1)S(1)} %shard_map.78), channel_id=1, source_target_pairs={{0,1},{1,0},{2,3},{3,2},{4,5},{5,4},{6,7},{7,6},{8,9},{9,8},{10,11... | collective-permute-start | bytes 884744 | tf_op jit(solution)/shard_map/ppermute | solution.py:388
  84.5 1.6 %collective-permute-start.24 = (bf16[128,1152]{1,0:T(8,128)(2,1)S(1)}, bf16[128,1152]{1,0:T(8,128)(2,1)S(1)}, u32[]{:S(2)}, u32[]{:S(2)}) collective-permute-start(bf16[128,1152]{1,0:T(8,128)(2,1)S(1)} %shard_map.79), channel_id=1, source_target_pairs={{0,1},{1,0},{2,3},{3,2},{4,5},{5,4},{6,7},{7,6},{8,9},{9,8},{10,11... | collective-permute-start | bytes 884744 | tf_op jit(solution)/shard_map/ppermute | solution.py:388

commit v18 on v17

--- a/solution.py
+++ b/solution.py
@@ -460,16 +460,14 @@
             remote, all_steps = [], []
             for group in range(GROUPS):
                 sent, kept = outs[2 * group : 2 * group + 2]
-                if group == GROUPS - 1 and shift == 0 and levels > 1:
-                    sent = gate(sent, [results[0][0][1], results[0][0][1 << levels - 1]])
                 all_steps.append(reduce([sent, kept], group * half // GROUPS, shift + 1, bases[group], shift == seq_count - 2))
                 next(all_steps[-1])
             last = []
             for level in range(levels + 1):
                 for group, steps in enumerate(all_steps):
                     wait = list(last) if group == 0 else []
-                    if group == GROUPS - 1 and level == levels and shift == 0:
-                        wait += results[0][0][1:]
+                    if group == 0 and level == levels and shift == 0:
+                        wait += [results[0][0][1 << place] for place in range(levels)]
                     step = steps.send(wait)
                     if level == levels:
                         remote.append(spread(step))

time: 87.1 us -> 89 us (1.022)
  waiting for transfers between devices: 19.9 us -> 24 us
  starting transfers between devices: 25.7 us -> 23.4 us
    ppermute x15, waiting for transfers between devices: 15.5 us -> 19.4 us  [exchange(): lax.ppermute(values, 'tensor', [(t, t ^ 1 << level) for t in range(tensor...]
    ppermute x15, starting transfers between devices: 19.4 us -> 17.1 us  [exchange(): lax.ppermute(values, 'tensor', [(t, t ^ 1 << level) for t in range(tensor...]
  transfers between devices with their start and end apart: 25 -> 25, of which waited for: 13 -> 17; matrix products, arithmetic and copies ran while one was open for 0% -> 0% of each run, Pallas kernels for 44% -> 38%
where the time goes in v18:
time: 89 us; the launch traced here: 88.8 us
  Pallas kernels  39 us (44%)
  waiting for transfers between devices  24 us (27%)
  starting transfers between devices  23.4 us (26%)
  local copies, waits for them, and re-layouts  1.46 us (2%)
  between operations  0.91 us (1%)
    pallas_call x5, Pallas kernels, multiply(): pl.pallas_call(body, out_shape=out_shape, in_specs=[VMEM] * spans[-1][1]...  35.4 us
    ppermute x15, waiting for transfers between devices, exchange(): lax.ppermute(values, 'tensor', [(t, t ^ 1 << level) for t in range(tensor...  19.4 us
    ppermute x15, starting transfers between devices, exchange(): lax.ppermute(values, 'tensor', [(t, t ^ 1 << level) for t in range(tensor...  17.1 us
    ppermute x4, starting transfers between devices, from_seq(): lax.ppermute(part, 'seq', [(s, (s + shift) % seq_count) for s in range(se...  5.11 us
    ppermute x4, waiting for transfers between devices, from_seq(): lax.ppermute(part, 'seq', [(s, (s + shift) % seq_count) for s in range(se...  2.73 us
    ppermute x6, waiting for transfers between devices, swap(): return lax.ppermute(values, 'sub', [(0, 1), (1, 0)])  1.9 us
  transfers between devices with their start and end apart: 25, of which 17 were waited for; matrix products, arithmetic and copies ran while one was open for 0% of the time, Pallas kernels for 38%

profile of v18, /device:TPU:0, one launch (start us, length us, event | category | flops | bytes accessed | tf_op | source)
XLA Modules:
  0.0 88.8 jit_solution(9631199064646046187)
XLA Ops:
  0.6 1.4 %copy-done = bf16[128,6656]{1,0:T(8,128)(2,1)S(1)} copy-done((bf16[128,6656]{1,0:T(8,128)(2,1)S(1)}, bf16[128,6656]{1,0:T(8,128)(2,1)}, u32[]{:S(2)}) %copy-start) | copy-done | bytes 1703960
  2.1 0.2 shard_map.59
  2.3 3.0 %collective-permute-start = (bf16[128,2048]{1,0:T(8,128)(2,1)S(1)}, bf16[128,2048]{1,0:T(8,128)(2,1)S(1)}, u32[]{:S(2)}, u32[]{:S(2)}) collective-permute-start(bf16[128,2048]{1,0:T(8,128)(2,1)S(1)} %get-tuple-element.31.refs_4_.refs_0_), channel_id=1, source_target_pairs={{0,2},{2,0},{1,3},{3,1},{4,6},{6,4},{5,7},{7,5},{8,10},{10,8},{9,1... | collective-permute-start | bytes 1572872 | tf_op jit(solution)/shard_map/ppermute | solution.py:418
  5.3 12.7 %shard_map.60.refs_3_ = f32[128,4096]{1,0:T(8,128)S(1)} custom-call(bf16[128,1792]{1,0:T(8,128)(2,1)S(1)} %get-tuple-element.32.refs_0_, bf16[128,1536]{1,0:T(8,128)(2,1)S(1)} %get-tuple-element.33.refs_1_, bf16[128,1280]{1,0:T(8,128)(2,1)S(1)} %get-tuple-element.34.refs_2_, bf16[6656,4096]{1,0:T(8,128)(2,1)} %refs_1_.5, ...), custom_call_target="tpu_custom_call" | custom-call | flops 1 | bytes 1 | tf_op jit(solution)/shard_map/pallas_call | solution.py:139
  18.0 7.3 %shard_map.61 = (bf16[128,1024]{1,0:T(8,128)(2,1)S(1)}, f32[128,1024]{1,0:T(8,128)S(1)}, bf16[128,1024]{1,0:T(8,128)(2,1)S(1)}, f32[128,1024]{1,0:T(8,128)S(1)}, f32[128,4096]{1,0:T(8,128)S(1)}) custom-call(bf16[128,2048]{1,0:T(8,128)(2,1)S(1)} %get-tuple-element.31.refs_4_.refs_0_, bf16[128,2048]{1,0:T(8,128)(2,1)S(1)} %collective-permute-done.refs_1_, ...), custom_call_target="tpu_custom_call" | custom-call | flops 1 | bytes 1 | tf_op jit(solution)/shard_map/pallas_call | solution.py:139
  25.4 0.5 collective-permute-start.2
  25.9 1.1 %collective-permute-done.3.refs_4_.refs_0_ = bf16[128,1792]{1,0:T(8,128)(2,1)S(1)} collective-permute-done((bf16[128,1792]{1,0:T(8,128)(2,1)S(1)}, bf16[128,1792]{1,0:T(8,128)(2,1)S(1)}, u32[]{:S(2)}, u32[]{:S(2)}) %collective-permute-start.3) | collective-permute-done | bytes 458784 | tf_op jit(solution)/shard_map/ppermute | solution.py:418
  27.0 0.3 collective-permute-done.2.refs_3_
  27.4 2.2 %collective-permute-start.4 = (bf16[64,2048]{1,0:T(8,128)(2,1)S(1)}, bf16[64,2048]{1,0:T(8,128)(2,1)S(1)}, u32[]{:S(2)}, u32[]{:S(2)}) collective-permute-start(bf16[64,2048]{1,0:T(8,128)(2,1)S(1)} %get-tuple-element.40.refs_3_), channel_id=1, source_target_pairs={{0,4},{4,0},{8,12},{12,8},{1,5},{5,1},{9,13},{13,9},{2,6},{6,2},{1... | collective-permute-start | bytes 786440 | tf_op jit(solution)/shard_map/ppermute | solution.py:391
  29.6 1.5 %collective-permute-start.6 = (bf16[128,1536]{1,0:T(8,128)(2,1)S(1)}, bf16[128,1536]{1,0:T(8,128)(2,1)S(1)}, u32[]{:S(2)}, u32[]{:S(2)}) collective-permute-start(bf16[128,1536]{1,0:T(8,128)(2,1)S(1)} %get-tuple-element.33.refs_1_), channel_id=1, source_target_pairs={{0,2},{2,0},{1,3},{3,1},{4,6},{6,4},{5,7},{7,5},{8,10},{10,8},{9,1... | collective-permute-start | bytes 1179656 | tf_op jit(solution)/shard_map/ppermute | solution.py:418
  31.0 0.5 collective-permute-start.10
  31.6 5.8 %shard_map.63.refs_2_ = f32[128,4096]{1,0:T(8,128)S(1)} custom-call(bf16[128,1792]{1,0:T(8,128)(2,1)S(1)} %collective-permute-done.3.refs_4_.refs_0_, bf16[6656,4096]{1,0:T(8,128)(2,1)} %refs_1_.5, f32[128,4096]{1,0:T(8,128)S(1)} %get-tuple-element.41.refs_2_, bf16[64,2048]{1,0:T(8,128)(2,1)S(1)} %get-tuple-element.40.refs_3_), custom_call_target="tpu_custom_call" | custom-call | flops 1 | bytes 1 | tf_op jit(solution)/shard_map/pallas_call | solution.py:139
  37.5 2.6 %collective-permute-start.5 = (bf16[32,2048]{1,0:T(8,128)(2,1)S(1)}, bf16[32,2048]{1,0:T(8,128)(2,1)S(1)}, u32[]{:S(2)}, u32[]{:S(2)}) collective-permute-start(bf16[32,2048]{1,0:T(8,128)(2,1)S(1)} %get-tuple-element.43.refs_3_), channel_id=1, source_target_pairs={{0,8},{4,12},{8,0},{12,4},{1,9},{5,13},{9,1},{13,5},{2,10},{6,14},... | collective-permute-start | bytes 393224 | tf_op jit(solution)/shard_map/ppermute | solution.py:391
  40.2 1.4 %collective-permute-done.6.refs_0_ = bf16[128,1536]{1,0:T(8,128)(2,1)S(1)} collective-permute-done((bf16[128,1536]{1,0:T(8,128)(2,1)S(1)}, bf16[128,1536]{1,0:T(8,128)(2,1)S(1)}, u32[]{:S(2)}, u32[]{:S(2)}) %collective-permute-start.6) | collective-permute-done | bytes 393248 | tf_op jit(solution)/shard_map/ppermute | solution.py:418
  41.6 5.2 %shard_map.65.refs_0_.refs_2_ = f32[128,4096]{1,0:T(8,128)S(1)} custom-call(bf16[128,1536]{1,0:T(8,128)(2,1)S(1)} %collective-permute-done.6.refs_0_, bf16[6656,4096]{1,0:T(8,128)(2,1)} %refs_1_.5, f32[128,4096]{1,0:T(8,128)S(1)} %shard_map.63.refs_2_, bf16[32,2048]{1,0:T(8,128)(2,1)S(1)} %get-tuple-element.43.refs_3_), custom_call_target="tpu_custom_call" | custom-call | flops 1 | bytes 1 | tf_op jit(solution)/shard_map/pallas_call | solution.py:139
  46.8 0.5 shard_map.66
  47.2 0.2 collective-permute-done.10.refs_0_
  47.5 4.5 %shard_map.67 = (bf16[128,1024]{1,0:T(8,128)(2,1)S(1)}, f32[128,1024]{1,0:T(8,128)S(1)}, bf16[128,1024]{1,0:T(8,128)(2,1)S(1)}, f32[128,1024]{1,0:T(8,128)S(1)}) custom-call(bf16[128,1280]{1,0:T(8,128)(2,1)S(1)} %collective-permute-done.10.refs_0_, bf16[6656,4096]{1,0:T(8,128)(2,1)} %refs_1_.5, f32[128,4096]{1,0:T(8,128)S(1)} %shard_map.65.refs_0_.refs_2_, ...), custom_call_target="tpu_custom_call" | custom-call | flops 1 | bytes 1 | tf_op jit(solution)/shard_map/pallas_call | solution.py:139
  52.0 0.5 collective-permute-start.11
  52.5 1.0 %collective-permute-done.13.refs_1_ = bf16[128,1024]{1,0:T(8,128)(2,1)S(1)} collective-permute-done((bf16[128,1024]{1,0:T(8,128)(2,1)S(1)}, bf16[128,1024]{1,0:T(8,128)(2,1)S(1)}, u32[]{:S(2)}, u32[]{:S(2)}) %collective-permute-start.13) | collective-permute-done | bytes 262176 | tf_op jit(solution)/shard_map/ppermute | solution.py:388
  53.6 0.4 collective-permute-start.15
  54.1 1.7 %collective-permute-start.12 = (bf16[64,1024]{1,0:T(8,128)(2,1)S(1)}, bf16[64,1024]{1,0:T(8,128)(2,1)S(1)}, u32[]{:S(2)}, u32[]{:S(2)}) collective-permute-start(bf16[64,1024]{1,0:T(8,128)(2,1)S(1)} %get-tuple-element.48), channel_id=1, source_target_pairs={{0,4},{4,0},{8,12},{12,8},{1,5},{5,1},{9,13},{13,9},{2,6},{6,2},{1... | collective-permute-start | bytes 393224 | tf_op jit(solution)/shard_map/ppermute | solution.py:391
  55.8 2.6 %collective-permute-start.8 = (bf16[32,2048]{1,0:T(8,128)(2,1)S(1)}, bf16[32,2048]{1,0:T(8,128)(2,1)S(1)}, u32[]{:S(2)}, u32[]{:S(2)}) collective-permute-start(bf16[32,2048]{1,0:T(8,128)(2,1)S(1)} %get-tuple-element.44.refs_3_.refs_0_), channel_id=1, source_target_pairs={{0,8},{4,12},{8,0},{12,4},{1,9},{5,13},{9,1},{13,5},{2,10},{6,14},... | collective-permute-start | bytes 393224 | tf_op jit(solution)/shard_map/ppermute | solution.py:391
  58.4 0.5 collective-permute-start.7
  58.9 4.7 %collective-permute-done.15.refs_1_ = bf16[64,1024]{1,0:T(8,128)(2,1)S(1)} collective-permute-done((bf16[64,1024]{1,0:T(8,128)(2,1)S(1)}, bf16[64,1024]{1,0:T(8,128)(2,1)S(1)}, u32[]{:S(2)}, u32[]{:S(2)}) %collective-permute-start.15) | collective-permute-done | bytes 131104 | tf_op jit(solution)/shard_map/ppermute | solution.py:391
  63.6 2.7 %collective-permute-done.12.refs_1_ = bf16[64,1024]{1,0:T(8,128)(2,1)S(1)} collective-permute-done((bf16[64,1024]{1,0:T(8,128)(2,1)S(1)}, bf16[64,1024]{1,0:T(8,128)(2,1)S(1)}, u32[]{:S(2)}, u32[]{:S(2)}) %collective-permute-start.12) | collective-permute-done | bytes 131104 | tf_op jit(solution)/shard_map/ppermute | solution.py:391
  66.4 0.6 collective-permute-start.14
  67.0 2.6 %collective-permute-done.19.came_ref = bf16[32,1024]{1,0:T(8,128)(2,1)S(1)} collective-permute-done((bf16[32,1024]{1,0:T(8,128)(2,1)S(1)}, bf16[32,1024]{1,0:T(8,128)(2,1)S(1)}, u32[]{:S(2)}, u32[]{:S(2)}) %collective-permute-start.19) | collective-permute-done | bytes 65568 | tf_op jit(solution)/shard_map/ppermute | solution.py:391
  69.6 0.3 shard_map.74.refs_4_
  70.0 1.6 %collective-permute-start.21 = (bf16[32,1152]{1,0:T(8,128)(2,1)S(1)}, bf16[32,1152]{1,0:T(8,128)(2,1)S(1)}, u32[]{:S(2)}, u32[]{:S(2)}) collective-permute-start(bf16[32,1152]{1,0:T(8,128)(2,1)S(1)} %shard_map.74.refs_4_), channel_id=1, source_target_pairs={{0,8},{4,12},{8,0},{12,4},{1,9},{5,13},{9,1},{13,5},{2,10},{6,14},... | collective-permute-start | bytes 221192 | tf_op jit(solution)/shard_map/ppermute | solution.py:391
  71.6 2.3 %collective-permute-done.14.came_ref = bf16[32,1024]{1,0:T(8,128)(2,1)S(1)} collective-permute-done((bf16[32,1024]{1,0:T(8,128)(2,1)S(1)}, bf16[32,1024]{1,0:T(8,128)(2,1)S(1)}, u32[]{:S(2)}, u32[]{:S(2)}) %collective-permute-start.14) | collective-permute-done | bytes 65568 | tf_op jit(solution)/shard_map/ppermute | solution.py:391
  73.9 0.3 shard_map.72.refs_4_
  74.3 1.9 %collective-permute-start.9 = (bf16[32,2048]{1,0:T(8,128)(2,1)S(1)}, bf16[32,2048]{1,0:T(8,128)(2,1)S(1)}, u32[]{:S(2)}, u32[]{:S(2)}) collective-permute-start(bf16[32,2048]{1,0:T(8,128)(2,1)S(1)} %collective-permute-done.8.refs_2_), channel_id=1, source_target_pairs={{0,4},{4,0},{8,12},{12,8},{1,5},{5,1},{9,13},{13,9},{2,6},{6,2},{1... | collective-permute-start | bytes 393224 | tf_op jit(solution)/shard_map/ppermute | solution.py:391
  76.2 0.2 collective-permute-start.20
  76.4 1.1 %collective-permute-done.21.refs_6_ = bf16[32,1152]{1,0:T(8,128)(2,1)S(1)} collective-permute-done((bf16[32,1152]{1,0:T(8,128)(2,1)S(1)}, bf16[32,1152]{1,0:T(8,128)(2,1)S(1)}, u32[]{:S(2)}, u32[]{:S(2)}) %collective-permute-start.21) | collective-permute-done | bytes 73760 | tf_op jit(solution)/shard_map/ppermute | solution.py:391
  77.5 1.4 %collective-permute-start.22 = (bf16[32,1152]{1,0:T(8,128)(2,1)S(1)}, bf16[32,1152]{1,0:T(8,128)(2,1)S(1)}, u32[]{:S(2)}, u32[]{:S(2)}) collective-permute-start(bf16[32,1152]{1,0:T(8,128)(2,1)S(1)} %collective-permute-done.21.refs_6_), channel_id=1, source_target_pairs={{0,4},{4,0},{8,12},{12,8},{1,5},{5,1},{9,13},{13,9},{2,6},{6,2},{1... | collective-permute-start | bytes 221192 | tf_op jit(solution)/shard_map/ppermute | solution.py:391
  78.9 0.6 collective-permute-start.16
  79.5 0.8 collective-permute-done.17.refs_6_
  80.3 0.6 collective-permute-start.18
  80.9 0.7 collective-permute-done.9.refs_3_
  81.6 1.6 %collective-permute-done.20.refs_5_ = bf16[32,1152]{1,0:T(8,128)(2,1)S(1)} collective-permute-done((bf16[32,1152]{1,0:T(8,128)(2,1)S(1)}, bf16[32,1152]{1,0:T(8,128)(2,1)S(1)}, u32[]{:S(2)}, u32[]{:S(2)}) %collective-permute-start.20) | collective-permute-done | bytes 73760 | tf_op jit(solution)/shard_map/ppermute | solution.py:391
  83.2 1.5 %collective-permute-done.22.refs_7_ = bf16[32,1152]{1,0:T(8,128)(2,1)S(1)} collective-permute-done((bf16[32,1152]{1,0:T(8,128)(2,1)S(1)}, bf16[32,1152]{1,0:T(8,128)(2,1)S(1)}, u32[]{:S(2)}, u32[]{:S(2)}) %collective-permute-start.22) | collective-permute-done | bytes 73760 | tf_op jit(solution)/shard_map/ppermute | solution.py:391
  84.8 0.7 collective-permute-done.16.refs_5_
  85.5 0.8 collective-permute-done.18.refs_7_
  86.4 0.1 shard_map.75.refs_1_.refs_4_
  86.5 0.8 shard_map.76.refs_0_
  87.4 0.6 collective-permute-done.23.refs_1_
  88.0 0.8 shard_map.79
  (31 shorter events, 1.0 us)
Async XLA Ops:
  0.6 1.5 %copy-start = (bf16[128,6656]{1,0:T(8,128)(2,1)S(1)}, bf16[128,6656]{1,0:T(8,128)(2,1)}, u32[]{:S(2)}) copy-start(bf16[128,6656]{1,0:T(8,128)(2,1)} %in_ref.1) | copy-start | bytes 5111812
  2.3 15.8 %collective-permute-start = (bf16[128,2048]{1,0:T(8,128)(2,1)S(1)}, bf16[128,2048]{1,0:T(8,128)(2,1)S(1)}, u32[]{:S(2)}, u32[]{:S(2)}) collective-permute-start(bf16[128,2048]{1,0:T(8,128)(2,1)S(1)} %get-tuple-element.31.refs_4_.refs_0_), channel_id=1, source_target_pairs={{0,2},{2,0},{1,3},{3,1},{4,6},{6,4},{5,7},{7,5},{8,10},{10,8},{9,1... | collective-permute-start | bytes 1572872 | tf_op jit(solution)/shard_map/ppermute | solution.py:418
  5.3 21.8 %collective-permute-start.3 = (bf16[128,1792]{1,0:T(8,128)(2,1)S(1)}, bf16[128,1792]{1,0:T(8,128)(2,1)S(1)}, u32[]{:S(2)}, u32[]{:S(2)}) collective-permute-start(bf16[128,1792]{1,0:T(8,128)(2,1)S(1)} %get-tuple-element.32.refs_0_), channel_id=1, source_target_pairs={{0,2},{2,0},{1,3},{3,1},{4,6},{6,4},{5,7},{7,5},{8,10},{10,8},{9,1... | collective-permute-start | bytes 1376264 | tf_op jit(solution)/shard_map/ppermute | solution.py:418
  25.3 1.7 %collective-permute-start.1 = (bf16[128,1024]{1,0:T(8,128)(2,1)S(1)}, bf16[128,1024]{1,0:T(8,128)(2,1)S(1)}, u32[]{:S(2)}, u32[]{:S(2)}) collective-permute-start(bf16[128,1024]{1,0:T(8,128)(2,1)S(1)} %get-tuple-element.37), channel_id=1, source_target_pairs={{0,1},{1,0},{2,3},{3,2},{4,5},{5,4},{6,7},{7,6},{8,9},{9,8},{10,11... | collective-permute-start | bytes 786440 | tf_op jit(solution)/shard_map/ppermute | solution.py:388
  25.4 1.9 %collective-permute-start.2 = (bf16[128,1024]{1,0:T(8,128)(2,1)S(1)}, bf16[128,1024]{1,0:T(8,128)(2,1)S(1)}, u32[]{:S(2)}, u32[]{:S(2)}) collective-permute-start(bf16[128,1024]{1,0:T(8,128)(2,1)S(1)} %get-tuple-element.38), channel_id=1, source_target_pairs={{0,1},{1,0},{2,3},{3,2},{4,5},{5,4},{6,7},{7,6},{8,9},{9,8},{10,11... | collective-permute-start | bytes 786440 | tf_op jit(solution)/shard_map/ppermute | solution.py:388
  27.4 10.0 %collective-permute-start.4 = (bf16[64,2048]{1,0:T(8,128)(2,1)S(1)}, bf16[64,2048]{1,0:T(8,128)(2,1)S(1)}, u32[]{:S(2)}, u32[]{:S(2)}) collective-permute-start(bf16[64,2048]{1,0:T(8,128)(2,1)S(1)} %get-tuple-element.40.refs_3_), channel_id=1, source_target_pairs={{0,4},{4,0},{8,12},{12,8},{1,5},{5,1},{9,13},{13,9},{2,6},{6,2},{1... | collective-permute-start | bytes 786440 | tf_op jit(solution)/shard_map/ppermute | solution.py:391
  29.6 12.0 %collective-permute-start.6 = (bf16[128,1536]{1,0:T(8,128)(2,1)S(1)}, bf16[128,1536]{1,0:T(8,128)(2,1)S(1)}, u32[]{:S(2)}, u32[]{:S(2)}) collective-permute-start(bf16[128,1536]{1,0:T(8,128)(2,1)S(1)} %get-tuple-element.33.refs_1_), channel_id=1, source_target_pairs={{0,2},{2,0},{1,3},{3,1},{4,6},{6,4},{5,7},{7,5},{8,10},{10,8},{9,1... | collective-permute-start | bytes 1179656 | tf_op jit(solution)/shard_map/ppermute | solution.py:418
  31.0 16.4 %collective-permute-start.10 = (bf16[128,1280]{1,0:T(8,128)(2,1)S(1)}, bf16[128,1280]{1,0:T(8,128)(2,1)S(1)}, u32[]{:S(2)}, u32[]{:S(2)}) collective-permute-start(bf16[128,1280]{1,0:T(8,128)(2,1)S(1)} %get-tuple-element.34.refs_2_), channel_id=1, source_target_pairs={{0,2},{2,0},{1,3},{3,1},{4,6},{6,4},{5,7},{7,5},{8,10},{10,8},{9,1... | collective-permute-start | bytes 983048 | tf_op jit(solution)/shard_map/ppermute | solution.py:418
  37.4 2.7 %copy-start.2 = (s32[4096]{0:T(1024)S(1)}, s32[4096]{0:T(1024)}, u32[]{:S(2)}) copy-start(s32[4096]{0:T(1024)} %param.6) | copy-start | bytes 49156
  37.5 9.2 %collective-permute-start.5 = (bf16[32,2048]{1,0:T(8,128)(2,1)S(1)}, bf16[32,2048]{1,0:T(8,128)(2,1)S(1)}, u32[]{:S(2)}, u32[]{:S(2)}) collective-permute-start(bf16[32,2048]{1,0:T(8,128)(2,1)S(1)} %get-tuple-element.43.refs_3_), channel_id=1, source_target_pairs={{0,8},{4,12},{8,0},{12,4},{1,9},{5,13},{9,1},{13,5},{2,10},{6,14},... | collective-permute-start | bytes 393224 | tf_op jit(solution)/shard_map/ppermute | solution.py:391
  40.2 6.6 %copy-start.1 = (f32[128,128]{1,0:T(8,128)S(1)}, f32[128,128]{1,0:T(8,128)}, u32[]{:S(2)}) copy-start(f32[128,128]{1,0:T(8,128)} %constant.9.clone.rotation_ref) | copy-start | bytes 196612
  52.0 1.6 %collective-permute-start.13 = (bf16[128,1024]{1,0:T(8,128)(2,1)S(1)}, bf16[128,1024]{1,0:T(8,128)(2,1)S(1)}, u32[]{:S(2)}, u32[]{:S(2)}) collective-permute-start(bf16[128,1024]{1,0:T(8,128)(2,1)S(1)} %get-tuple-element.50), channel_id=1, source_target_pairs={{0,1},{1,0},{2,3},{3,2},{4,5},{5,4},{6,7},{7,6},{8,9},{9,8},{10,11... | collective-permute-start | bytes 786440 | tf_op jit(solution)/shard_map/ppermute | solution.py:388
  52.0 2.0 %collective-permute-start.11 = (bf16[128,1024]{1,0:T(8,128)(2,1)S(1)}, bf16[128,1024]{1,0:T(8,128)(2,1)S(1)}, u32[]{:S(2)}, u32[]{:S(2)}) collective-permute-start(bf16[128,1024]{1,0:T(8,128)(2,1)S(1)} %get-tuple-element.46), channel_id=1, source_target_pairs={{0,1},{1,0},{2,3},{3,2},{4,5},{5,4},{6,7},{7,6},{8,9},{9,8},{10,11... | collective-permute-start | bytes 786440 | tf_op jit(solution)/shard_map/ppermute | solution.py:388
  53.6 9.9 %collective-permute-start.15 = (bf16[64,1024]{1,0:T(8,128)(2,1)S(1)}, bf16[64,1024]{1,0:T(8,128)(2,1)S(1)}, u32[]{:S(2)}, u32[]{:S(2)}) collective-permute-start(bf16[64,1024]{1,0:T(8,128)(2,1)S(1)} %get-tuple-element.51.refs_2_), channel_id=1, source_target_pairs={{0,4},{4,0},{8,12},{12,8},{1,5},{5,1},{9,13},{13,9},{2,6},{6,2},{1... | collective-permute-start | bytes 393224 | tf_op jit(solution)/shard_map/ppermute | solution.py:391
  54.1 12.3 %collective-permute-start.12 = (bf16[64,1024]{1,0:T(8,128)(2,1)S(1)}, bf16[64,1024]{1,0:T(8,128)(2,1)S(1)}, u32[]{:S(2)}, u32[]{:S(2)}) collective-permute-start(bf16[64,1024]{1,0:T(8,128)(2,1)S(1)} %get-tuple-element.48), channel_id=1, source_target_pairs={{0,4},{4,0},{8,12},{12,8},{1,5},{5,1},{9,13},{13,9},{2,6},{6,2},{1... | collective-permute-start | bytes 393224 | tf_op jit(solution)/shard_map/ppermute | solution.py:391
  55.8 15.7 %collective-permute-start.8 = (bf16[32,2048]{1,0:T(8,128)(2,1)S(1)}, bf16[32,2048]{1,0:T(8,128)(2,1)S(1)}, u32[]{:S(2)}, u32[]{:S(2)}) collective-permute-start(bf16[32,2048]{1,0:T(8,128)(2,1)S(1)} %get-tuple-element.44.refs_3_.refs_0_), channel_id=1, source_target_pairs={{0,8},{4,12},{8,0},{12,4},{1,9},{5,13},{9,1},{13,5},{2,10},{6,14},... | collective-permute-start | bytes 393224 | tf_op jit(solution)/shard_map/ppermute | solution.py:391
  58.4 13.2 %collective-permute-start.7 = (bf16[32,2048]{1,0:T(8,128)(2,1)S(1)}, bf16[32,2048]{1,0:T(8,128)(2,1)S(1)}, u32[]{:S(2)}, u32[]{:S(2)}) collective-permute-start(bf16[32,2048]{1,0:T(8,128)(2,1)S(1)} %get-tuple-element.44.refs_3_.refs_0_), channel_id=1, source_target_pairs={{0,4},{4,0},{8,12},{12,8},{1,5},{5,1},{9,13},{13,9},{2,6},{6,2},{1... | collective-permute-start | bytes 393224 | tf_op jit(solution)/shard_map/ppermute | solution.py:391
  63.6 6.0 %collective-permute-start.19 = (bf16[32,1024]{1,0:T(8,128)(2,1)S(1)}, bf16[32,1024]{1,0:T(8,128)(2,1)S(1)}, u32[]{:S(2)}, u32[]{:S(2)}) collective-permute-start(bf16[32,1024]{1,0:T(8,128)(2,1)S(1)} %get-tuple-element.56.refs_0_), channel_id=1, source_target_pairs={{0,8},{4,12},{8,0},{12,4},{1,9},{5,13},{9,1},{13,5},{2,10},{6,14},... | collective-permute-start | bytes 196616 | tf_op jit(solution)/shard_map/ppermute | solution.py:391
  66.4 7.5 %collective-permute-start.14 = (bf16[32,1024]{1,0:T(8,128)(2,1)S(1)}, bf16[32,1024]{1,0:T(8,128)(2,1)S(1)}, u32[]{:S(2)}, u32[]{:S(2)}) collective-permute-start(bf16[32,1024]{1,0:T(8,128)(2,1)S(1)} %get-tuple-element.53), channel_id=1, source_target_pairs={{0,8},{4,12},{8,0},{12,4},{1,9},{5,13},{9,1},{13,5},{2,10},{6,14},... | collective-permute-start | bytes 196616 | tf_op jit(solution)/shard_map/ppermute | solution.py:391
  70.0 7.5 %collective-permute-start.21 = (bf16[32,1152]{1,0:T(8,128)(2,1)S(1)}, bf16[32,1152]{1,0:T(8,128)(2,1)S(1)}, u32[]{:S(2)}, u32[]{:S(2)}) collective-permute-start(bf16[32,1152]{1,0:T(8,128)(2,1)S(1)} %shard_map.74.refs_4_), channel_id=1, source_target_pairs={{0,8},{4,12},{8,0},{12,4},{1,9},{5,13},{9,1},{13,5},{2,10},{6,14},... | collective-permute-start | bytes 221192 | tf_op jit(solution)/shard_map/ppermute | solution.py:391
  74.2 6.1 %collective-permute-start.17 = (bf16[32,1152]{1,0:T(8,128)(2,1)S(1)}, bf16[32,1152]{1,0:T(8,128)(2,1)S(1)}, u32[]{:S(2)}, u32[]{:S(2)}) collective-permute-start(bf16[32,1152]{1,0:T(8,128)(2,1)S(1)} %shard_map.72.refs_4_), channel_id=1, source_target_pairs={{0,8},{4,12},{8,0},{12,4},{1,9},{5,13},{9,1},{13,5},{2,10},{6,14},... | collective-permute-start | bytes 221192 | tf_op jit(solution)/shard_map/ppermute | solution.py:391
  74.3 7.3 %collective-permute-start.9 = (bf16[32,2048]{1,0:T(8,128)(2,1)S(1)}, bf16[32,2048]{1,0:T(8,128)(2,1)S(1)}, u32[]{:S(2)}, u32[]{:S(2)}) collective-permute-start(bf16[32,2048]{1,0:T(8,128)(2,1)S(1)} %collective-permute-done.8.refs_2_), channel_id=1, source_target_pairs={{0,4},{4,0},{8,12},{12,8},{1,5},{5,1},{9,13},{13,9},{2,6},{6,2},{1... | collective-permute-start | bytes 393224 | tf_op jit(solution)/shard_map/ppermute | solution.py:391
  76.2 7.0 %collective-permute-start.20 = (bf16[32,1152]{1,0:T(8,128)(2,1)S(1)}, bf16[32,1152]{1,0:T(8,128)(2,1)S(1)}, u32[]{:S(2)}, u32[]{:S(2)}) collective-permute-start(bf16[32,1152]{1,0:T(8,128)(2,1)S(1)} %shard_map.74.refs_4_), channel_id=1, source_target_pairs={{0,4},{4,0},{8,12},{12,8},{1,5},{5,1},{9,13},{13,9},{2,6},{6,2},{1... | collective-permute-start | bytes 221192 | tf_op jit(solution)/shard_map/ppermute | solution.py:391
  77.5 7.2 %collective-permute-start.22 = (bf16[32,1152]{1,0:T(8,128)(2,1)S(1)}, bf16[32,1152]{1,0:T(8,128)(2,1)S(1)}, u32[]{:S(2)}, u32[]{:S(2)}) collective-permute-start(bf16[32,1152]{1,0:T(8,128)(2,1)S(1)} %collective-permute-done.21.refs_6_), channel_id=1, source_target_pairs={{0,4},{4,0},{8,12},{12,8},{1,5},{5,1},{9,13},{13,9},{2,6},{6,2},{1... | collective-permute-start | bytes 221192 | tf_op jit(solution)/shard_map/ppermute | solution.py:391
  78.9 6.6 %collective-permute-start.16 = (bf16[32,1152]{1,0:T(8,128)(2,1)S(1)}, bf16[32,1152]{1,0:T(8,128)(2,1)S(1)}, u32[]{:S(2)}, u32[]{:S(2)}) collective-permute-start(bf16[32,1152]{1,0:T(8,128)(2,1)S(1)} %shard_map.72.refs_4_), channel_id=1, source_target_pairs={{0,4},{4,0},{8,12},{12,8},{1,5},{5,1},{9,13},{13,9},{2,6},{6,2},{1... | collective-permute-start | bytes 221192 | tf_op jit(solution)/shard_map/ppermute | solution.py:391
  80.3 5.9 %collective-permute-start.18 = (bf16[32,1152]{1,0:T(8,128)(2,1)S(1)}, bf16[32,1152]{1,0:T(8,128)(2,1)S(1)}, u32[]{:S(2)}, u32[]{:S(2)}) collective-permute-start(bf16[32,1152]{1,0:T(8,128)(2,1)S(1)} %collective-permute-done.17.refs_6_), channel_id=1, source_target_pairs={{0,4},{4,0},{8,12},{12,8},{1,5},{5,1},{9,13},{13,9},{2,6},{6,2},{1... | collective-permute-start | bytes 221192 | tf_op jit(solution)/shard_map/ppermute | solution.py:391
  84.8 2.6 %collective-permute-start.24 = (bf16[128,1152]{1,0:T(8,128)(2,1)S(1)}, bf16[128,1152]{1,0:T(8,128)(2,1)S(1)}, u32[]{:S(2)}, u32[]{:S(2)}) collective-permute-start(bf16[128,1152]{1,0:T(8,128)(2,1)S(1)} %shard_map.78), channel_id=1, source_target_pairs={{0,1},{1,0},{2,3},{3,2},{4,5},{5,4},{6,7},{7,6},{8,9},{9,8},{10,11... | collective-permute-start | bytes 884744 | tf_op jit(solution)/shard_map/ppermute | solution.py:388
  86.3 1.6 %collective-permute-start.23 = (bf16[128,1152]{1,0:T(8,128)(2,1)S(1)}, bf16[128,1152]{1,0:T(8,128)(2,1)S(1)}, u32[]{:S(2)}, u32[]{:S(2)}) collective-permute-start(bf16[128,1152]{1,0:T(8,128)(2,1)S(1)} %shard_map.77), channel_id=1, source_target_pairs={{0,1},{1,0},{2,3},{3,2},{4,5},{5,4},{6,7},{7,6},{8,9},{9,8},{10,11... | collective-permute-start | bytes 884744 | tf_op jit(solution)/shard_map/ppermute | solution.py:388

commit v19 on v17

--- a/solution.py
+++ b/solution.py
@@ -380,7 +380,7 @@
     half = down_weight.shape[1] // sub_count
     per_sub = seq_count // sub_count
     levels = tensor_count.bit_length() - 1
-    wide, wide_chunk, wide_merged = (min(size, half // GROUPS) for size in (256, 512, 1024))
+    wide, wide_chunk, wide_merged = (min(size, half // GROUPS) for size in (256, 256, 1024))
     flips = (2 * sign_bits - 1).astype(jnp.float32)[None, :]
     rotation = jnp.asarray(hadamard(BLOCK))
 

time: 87.1 us -> 89.3 us (1.025)
  Pallas kernels: 39 us -> 41.6 us
  starting transfers between devices: 25.7 us -> 24.6 us
    pallas_call x5, Pallas kernels: 35.4 us -> 38.1 us  [multiply(): pl.pallas_call(body, out_shape=out_shape, in_specs=[VMEM] * spans[-1][1]...]
    ppermute x15, starting transfers between devices: 19.4 us -> 18.3 us  [exchange(): lax.ppermute(values, 'tensor', [(t, t ^ 1 << level) for t in range(tensor...]
  transfers between devices with their start and end apart: 25 -> 25, of which waited for: 13 -> 15; matrix products, arithmetic and copies ran while one was open for 0% -> 0% of each run, Pallas kernels for 44% -> 46%
where the time goes in v19:
time: 89.3 us; the launch traced here: 89.1 us
  Pallas kernels  41.6 us (47%)
  starting transfers between devices  24.6 us (28%)
  waiting for transfers between devices  20.4 us (23%)
  local copies, waits for them, and re-layouts  1.46 us (2%)
  between operations  0.93 us (1%)
    pallas_call x5, Pallas kernels, multiply(): pl.pallas_call(body, out_shape=out_shape, in_specs=[VMEM] * spans[-1][1]...  38.1 us
    ppermute x15, starting transfers between devices, exchange(): lax.ppermute(values, 'tensor', [(t, t ^ 1 << level) for t in range(tensor...  18.3 us
    ppermute x15, waiting for transfers between devices, exchange(): lax.ppermute(values, 'tensor', [(t, t ^ 1 << level) for t in range(tensor...  16.3 us
    ppermute x4, starting transfers between devices, from_seq(): lax.ppermute(part, 'seq', [(s, (s + shift) % seq_count) for s in range(se...  5.11 us
    ppermute x4, waiting for transfers between devices, from_seq(): lax.ppermute(part, 'seq', [(s, (s + shift) % seq_count) for s in range(se...  2.28 us
    ppermute x6, waiting for transfers between devices, swap(): return lax.ppermute(values, 'sub', [(0, 1), (1, 0)])  1.88 us
  transfers between devices with their start and end apart: 25, of which 15 were waited for; matrix products, arithmetic and copies ran while one was open for 0% of the time, Pallas kernels for 46%

profile of v19, /device:TPU:0, one launch (start us, length us, event | category | flops | bytes accessed | tf_op | source)
XLA Modules:
  0.0 89.1 jit_solution(15403284886841362737)
XLA Ops:
  0.6 1.4 %copy-done = bf16[128,6656]{1,0:T(8,128)(2,1)S(1)} copy-done((bf16[128,6656]{1,0:T(8,128)(2,1)S(1)}, bf16[128,6656]{1,0:T(8,128)(2,1)}, u32[]{:S(2)}) %copy-start) | copy-done | bytes 1703960
  2.1 0.2 shard_map.59
  2.3 3.0 %collective-permute-start = (bf16[128,2048]{1,0:T(8,128)(2,1)S(1)}, bf16[128,2048]{1,0:T(8,128)(2,1)S(1)}, u32[]{:S(2)}, u32[]{:S(2)}) collective-permute-start(bf16[128,2048]{1,0:T(8,128)(2,1)S(1)} %get-tuple-element.31.refs_4_.refs_0_), channel_id=1, source_target_pairs={{0,2},{2,0},{1,3},{3,1},{4,6},{6,4},{5,7},{7,5},{8,10},{10,8},{9,1... | collective-permute-start | bytes 1572872 | tf_op jit(solution)/shard_map/ppermute | solution.py:418
  5.3 0.1 collective-permute-start.3
  5.3 12.7 %shard_map.60.refs_3_ = f32[128,4096]{1,0:T(8,128)S(1)} custom-call(bf16[128,1792]{1,0:T(8,128)(2,1)S(1)} %get-tuple-element.32.refs_0_, bf16[128,1536]{1,0:T(8,128)(2,1)S(1)} %get-tuple-element.33.refs_1_, bf16[128,1280]{1,0:T(8,128)(2,1)S(1)} %get-tuple-element.34.refs_2_, bf16[6656,4096]{1,0:T(8,128)(2,1)} %refs_1_.5, ...), custom_call_target="tpu_custom_call" | custom-call | flops 1 | bytes 1 | tf_op jit(solution)/shard_map/pallas_call | solution.py:139
  18.0 7.3 %shard_map.61 = (bf16[128,1024]{1,0:T(8,128)(2,1)S(1)}, f32[128,1024]{1,0:T(8,128)S(1)}, bf16[128,1024]{1,0:T(8,128)(2,1)S(1)}, f32[128,1024]{1,0:T(8,128)S(1)}, f32[128,4096]{1,0:T(8,128)S(1)}) custom-call(bf16[128,2048]{1,0:T(8,128)(2,1)S(1)} %get-tuple-element.31.refs_4_.refs_0_, bf16[128,2048]{1,0:T(8,128)(2,1)S(1)} %collective-permute-done.refs_1_, ...), custom_call_target="tpu_custom_call" | custom-call | flops 1 | bytes 1 | tf_op jit(solution)/shard_map/pallas_call | solution.py:139
  25.4 0.5 collective-permute-start.2
  25.9 1.1 %collective-permute-done.3.refs_4_.refs_0_ = bf16[128,1792]{1,0:T(8,128)(2,1)S(1)} collective-permute-done((bf16[128,1792]{1,0:T(8,128)(2,1)S(1)}, bf16[128,1792]{1,0:T(8,128)(2,1)S(1)}, u32[]{:S(2)}, u32[]{:S(2)}) %collective-permute-start.3) | collective-permute-done | bytes 458784 | tf_op jit(solution)/shard_map/ppermute | solution.py:418
  27.0 0.3 collective-permute-done.2.refs_3_
  27.3 0.1 shard_map.62
  27.4 2.2 %collective-permute-start.4 = (bf16[64,2048]{1,0:T(8,128)(2,1)S(1)}, bf16[64,2048]{1,0:T(8,128)(2,1)S(1)}, u32[]{:S(2)}, u32[]{:S(2)}) collective-permute-start(bf16[64,2048]{1,0:T(8,128)(2,1)S(1)} %get-tuple-element.40.refs_3_), channel_id=1, source_target_pairs={{0,4},{4,0},{8,12},{12,8},{1,5},{5,1},{9,13},{13,9},{2,6},{6,2},{1... | collective-permute-start | bytes 786440 | tf_op jit(solution)/shard_map/ppermute | solution.py:391
  29.6 1.5 %collective-permute-start.6 = (bf16[128,1536]{1,0:T(8,128)(2,1)S(1)}, bf16[128,1536]{1,0:T(8,128)(2,1)S(1)}, u32[]{:S(2)}, u32[]{:S(2)}) collective-permute-start(bf16[128,1536]{1,0:T(8,128)(2,1)S(1)} %get-tuple-element.33.refs_1_), channel_id=1, source_target_pairs={{0,2},{2,0},{1,3},{3,1},{4,6},{6,4},{5,7},{7,5},{8,10},{10,8},{9,1... | collective-permute-start | bytes 1179656 | tf_op jit(solution)/shard_map/ppermute | solution.py:418
  31.0 0.5 collective-permute-start.10
  31.6 6.0 %shard_map.63.refs_2_ = f32[128,4096]{1,0:T(8,128)S(1)} custom-call(bf16[128,1792]{1,0:T(8,128)(2,1)S(1)} %collective-permute-done.3.refs_4_.refs_0_, bf16[6656,4096]{1,0:T(8,128)(2,1)} %refs_1_.5, f32[128,4096]{1,0:T(8,128)S(1)} %get-tuple-element.41.refs_2_, bf16[64,2048]{1,0:T(8,128)(2,1)S(1)} %get-tuple-element.40.refs_3_), custom_call_target="tpu_custom_call" | custom-call | flops 1 | bytes 1 | tf_op jit(solution)/shard_map/pallas_call | solution.py:139
  37.7 2.7 %collective-permute-start.5 = (bf16[32,2048]{1,0:T(8,128)(2,1)S(1)}, bf16[32,2048]{1,0:T(8,128)(2,1)S(1)}, u32[]{:S(2)}, u32[]{:S(2)}) collective-permute-start(bf16[32,2048]{1,0:T(8,128)(2,1)S(1)} %get-tuple-element.43.refs_3_), channel_id=1, source_target_pairs={{0,8},{4,12},{8,0},{12,4},{1,9},{5,13},{9,1},{13,5},{2,10},{6,14},... | collective-permute-start | bytes 393224 | tf_op jit(solution)/shard_map/ppermute | solution.py:391
  40.4 1.2 %collective-permute-done.6.refs_0_ = bf16[128,1536]{1,0:T(8,128)(2,1)S(1)} collective-permute-done((bf16[128,1536]{1,0:T(8,128)(2,1)S(1)}, bf16[128,1536]{1,0:T(8,128)(2,1)S(1)}, u32[]{:S(2)}, u32[]{:S(2)}) %collective-permute-start.6) | collective-permute-done | bytes 393248 | tf_op jit(solution)/shard_map/ppermute | solution.py:418
  41.6 5.7 %shard_map.65.refs_0_.refs_2_ = f32[128,4096]{1,0:T(8,128)S(1)} custom-call(bf16[128,1536]{1,0:T(8,128)(2,1)S(1)} %collective-permute-done.6.refs_0_, bf16[6656,4096]{1,0:T(8,128)(2,1)} %refs_1_.5, f32[128,4096]{1,0:T(8,128)S(1)} %shard_map.63.refs_2_, bf16[32,2048]{1,0:T(8,128)(2,1)S(1)} %get-tuple-element.43.refs_3_), custom_call_target="tpu_custom_call" | custom-call | flops 1 | bytes 1 | tf_op jit(solution)/shard_map/pallas_call | solution.py:139
  47.3 0.5 shard_map.66
  47.8 0.1 collective-permute-start.7
  47.9 3.0 %collective-permute-start.8 = (bf16[32,2048]{1,0:T(8,128)(2,1)S(1)}, bf16[32,2048]{1,0:T(8,128)(2,1)S(1)}, u32[]{:S(2)}, u32[]{:S(2)}) collective-permute-start(bf16[32,2048]{1,0:T(8,128)(2,1)S(1)} %get-tuple-element.44.refs_3_.refs_0_), channel_id=1, source_target_pairs={{0,8},{4,12},{8,0},{12,4},{1,9},{5,13},{9,1},{13,5},{2,10},{6,14},... | collective-permute-start | bytes 393224 | tf_op jit(solution)/shard_map/ppermute | solution.py:391
  50.9 6.3 %shard_map.67 = (bf16[128,1024]{1,0:T(8,128)(2,1)S(1)}, f32[128,1024]{1,0:T(8,128)S(1)}, bf16[128,1024]{1,0:T(8,128)(2,1)S(1)}, f32[128,1024]{1,0:T(8,128)S(1)}) custom-call(bf16[128,1280]{1,0:T(8,128)(2,1)S(1)} %collective-permute-done.10.refs_0_, bf16[6656,4096]{1,0:T(8,128)(2,1)} %refs_1_.5, f32[128,4096]{1,0:T(8,128)S(1)} %shard_map.65.refs_0_.refs_2_, ...), custom_call_target="tpu_custom_call" | custom-call | flops 1 | bytes 1 | tf_op jit(solution)/shard_map/pallas_call | solution.py:139
  57.4 0.5 collective-permute-start.13
  57.8 1.0 %collective-permute-done.11.refs_1_ = bf16[128,1024]{1,0:T(8,128)(2,1)S(1)} collective-permute-done((bf16[128,1024]{1,0:T(8,128)(2,1)S(1)}, bf16[128,1024]{1,0:T(8,128)(2,1)S(1)}, u32[]{:S(2)}, u32[]{:S(2)}) %collective-permute-start.11) | collective-permute-done | bytes 262176 | tf_op jit(solution)/shard_map/ppermute | solution.py:388
  58.9 1.6 %collective-permute-start.12 = (bf16[64,1024]{1,0:T(8,128)(2,1)S(1)}, bf16[64,1024]{1,0:T(8,128)(2,1)S(1)}, u32[]{:S(2)}, u32[]{:S(2)}) collective-permute-start(bf16[64,1024]{1,0:T(8,128)(2,1)S(1)} %get-tuple-element.48), channel_id=1, source_target_pairs={{0,4},{4,0},{8,12},{12,8},{1,5},{5,1},{9,13},{13,9},{2,6},{6,2},{1... | collective-permute-start | bytes 393224 | tf_op jit(solution)/shard_map/ppermute | solution.py:391
  60.6 0.5 collective-permute-start.15
  61.1 1.6 %collective-permute-start.9 = (bf16[32,2048]{1,0:T(8,128)(2,1)S(1)}, bf16[32,2048]{1,0:T(8,128)(2,1)S(1)}, u32[]{:S(2)}, u32[]{:S(2)}) collective-permute-start(bf16[32,2048]{1,0:T(8,128)(2,1)S(1)} %collective-permute-done.8.refs_2_.refs_1_), channel_id=1, source_target_pairs={{0,4},{4,0},{8,12},{12,8},{1,5},{5,1},{9,13},{13,9},{2,6},{6,2},{1... | collective-permute-start | bytes 393224 | tf_op jit(solution)/shard_map/ppermute | solution.py:391
  62.7 2.6 %collective-permute-done.12.refs_1_ = bf16[64,1024]{1,0:T(8,128)(2,1)S(1)} collective-permute-done((bf16[64,1024]{1,0:T(8,128)(2,1)S(1)}, bf16[64,1024]{1,0:T(8,128)(2,1)S(1)}, u32[]{:S(2)}, u32[]{:S(2)}) %collective-permute-start.12) | collective-permute-done | bytes 131104 | tf_op jit(solution)/shard_map/ppermute | solution.py:391
  65.4 3.4 %collective-permute-done.15.refs_1_ = bf16[64,1024]{1,0:T(8,128)(2,1)S(1)} collective-permute-done((bf16[64,1024]{1,0:T(8,128)(2,1)S(1)}, bf16[64,1024]{1,0:T(8,128)(2,1)S(1)}, u32[]{:S(2)}, u32[]{:S(2)}) %collective-permute-start.15) | collective-permute-done | bytes 131104 | tf_op jit(solution)/shard_map/ppermute | solution.py:391
  68.9 3.9 %collective-permute-done.14.came_ref = bf16[32,1024]{1,0:T(8,128)(2,1)S(1)} collective-permute-done((bf16[32,1024]{1,0:T(8,128)(2,1)S(1)}, bf16[32,1024]{1,0:T(8,128)(2,1)S(1)}, u32[]{:S(2)}, u32[]{:S(2)}) %collective-permute-start.14) | collective-permute-done | bytes 65568 | tf_op jit(solution)/shard_map/ppermute | solution.py:391
  72.8 0.3 shard_map.73.refs_4_
  73.2 2.0 %collective-permute-start.17 = (bf16[32,1152]{1,0:T(8,128)(2,1)S(1)}, bf16[32,1152]{1,0:T(8,128)(2,1)S(1)}, u32[]{:S(2)}, u32[]{:S(2)}) collective-permute-start(bf16[32,1152]{1,0:T(8,128)(2,1)S(1)} %shard_map.73.refs_4_), channel_id=1, source_target_pairs={{0,8},{4,12},{8,0},{12,4},{1,9},{5,13},{9,1},{13,5},{2,10},{6,14},... | collective-permute-start | bytes 221192 | tf_op jit(solution)/shard_map/ppermute | solution.py:391
  75.2 0.7 collective-permute-done.19.came_ref
  75.9 0.3 shard_map.75.refs_4_
  76.3 0.3 collective-permute-start.21
  76.6 2.1 %collective-permute-start.16 = (bf16[32,1152]{1,0:T(8,128)(2,1)S(1)}, bf16[32,1152]{1,0:T(8,128)(2,1)S(1)}, u32[]{:S(2)}, u32[]{:S(2)}) collective-permute-start(bf16[32,1152]{1,0:T(8,128)(2,1)S(1)} %shard_map.73.refs_4_), channel_id=1, source_target_pairs={{0,4},{4,0},{8,12},{12,8},{1,5},{5,1},{9,13},{13,9},{2,6},{6,2},{1... | collective-permute-start | bytes 221192 | tf_op jit(solution)/shard_map/ppermute | solution.py:391
  78.7 0.8 collective-permute-done.17.refs_6_
  79.5 2.0 %collective-permute-start.20 = (bf16[32,1152]{1,0:T(8,128)(2,1)S(1)}, bf16[32,1152]{1,0:T(8,128)(2,1)S(1)}, u32[]{:S(2)}, u32[]{:S(2)}) collective-permute-start(bf16[32,1152]{1,0:T(8,128)(2,1)S(1)} %shard_map.75.refs_4_), channel_id=1, source_target_pairs={{0,4},{4,0},{8,12},{12,8},{1,5},{5,1},{9,13},{13,9},{2,6},{6,2},{1... | collective-permute-start | bytes 221192 | tf_op jit(solution)/shard_map/ppermute | solution.py:391
  81.5 0.4 collective-permute-done.21.refs_6_
  81.9 0.2 collective-permute-done.16.refs_5_
  82.1 2.6 %collective-permute-done.18.refs_7_ = bf16[32,1152]{1,0:T(8,128)(2,1)S(1)} collective-permute-done((bf16[32,1152]{1,0:T(8,128)(2,1)S(1)}, bf16[32,1152]{1,0:T(8,128)(2,1)S(1)}, u32[]{:S(2)}, u32[]{:S(2)}) %collective-permute-start.18) | collective-permute-done | bytes 73760 | tf_op jit(solution)/shard_map/ppermute | solution.py:391
  84.7 0.1 shard_map.78
  84.8 1.0 %collective-permute-done.20.refs_5_ = bf16[32,1152]{1,0:T(8,128)(2,1)S(1)} collective-permute-done((bf16[32,1152]{1,0:T(8,128)(2,1)S(1)}, bf16[32,1152]{1,0:T(8,128)(2,1)S(1)}, u32[]{:S(2)}, u32[]{:S(2)}) %collective-permute-start.20) | collective-permute-done | bytes 73760 | tf_op jit(solution)/shard_map/ppermute | solution.py:391
  85.8 0.8 collective-permute-done.22.refs_7_
  86.6 0.1 shard_map.79
  86.8 0.1 shard_map.76.refs_1_.refs_4_
  86.9 0.8 shard_map.77.refs_0_
  87.7 0.6 collective-permute-done.24.refs_2_
  88.3 0.8 shard_map.80
  (32 shorter events, 0.7 us)
Async XLA Ops:
  0.6 1.5 %copy-start = (bf16[128,6656]{1,0:T(8,128)(2,1)S(1)}, bf16[128,6656]{1,0:T(8,128)(2,1)}, u32[]{:S(2)}) copy-start(bf16[128,6656]{1,0:T(8,128)(2,1)} %in_ref.1) | copy-start | bytes 5111812
  2.3 15.8 %collective-permute-start = (bf16[128,2048]{1,0:T(8,128)(2,1)S(1)}, bf16[128,2048]{1,0:T(8,128)(2,1)S(1)}, u32[]{:S(2)}, u32[]{:S(2)}) collective-permute-start(bf16[128,2048]{1,0:T(8,128)(2,1)S(1)} %get-tuple-element.31.refs_4_.refs_0_), channel_id=1, source_target_pairs={{0,2},{2,0},{1,3},{3,1},{4,6},{6,4},{5,7},{7,5},{8,10},{10,8},{9,1... | collective-permute-start | bytes 1572872 | tf_op jit(solution)/shard_map/ppermute | solution.py:418
  5.3 21.8 %collective-permute-start.3 = (bf16[128,1792]{1,0:T(8,128)(2,1)S(1)}, bf16[128,1792]{1,0:T(8,128)(2,1)S(1)}, u32[]{:S(2)}, u32[]{:S(2)}) collective-permute-start(bf16[128,1792]{1,0:T(8,128)(2,1)S(1)} %get-tuple-element.32.refs_0_), channel_id=1, source_target_pairs={{0,2},{2,0},{1,3},{3,1},{4,6},{6,4},{5,7},{7,5},{8,10},{10,8},{9,1... | collective-permute-start | bytes 1376264 | tf_op jit(solution)/shard_map/ppermute | solution.py:418
  25.3 1.7 %collective-permute-start.1 = (bf16[128,1024]{1,0:T(8,128)(2,1)S(1)}, bf16[128,1024]{1,0:T(8,128)(2,1)S(1)}, u32[]{:S(2)}, u32[]{:S(2)}) collective-permute-start(bf16[128,1024]{1,0:T(8,128)(2,1)S(1)} %get-tuple-element.37), channel_id=1, source_target_pairs={{0,1},{1,0},{2,3},{3,2},{4,5},{5,4},{6,7},{7,6},{8,9},{9,8},{10,11... | collective-permute-start | bytes 786440 | tf_op jit(solution)/shard_map/ppermute | solution.py:388
  25.4 1.9 %collective-permute-start.2 = (bf16[128,1024]{1,0:T(8,128)(2,1)S(1)}, bf16[128,1024]{1,0:T(8,128)(2,1)S(1)}, u32[]{:S(2)}, u32[]{:S(2)}) collective-permute-start(bf16[128,1024]{1,0:T(8,128)(2,1)S(1)} %get-tuple-element.38), channel_id=1, source_target_pairs={{0,1},{1,0},{2,3},{3,2},{4,5},{5,4},{6,7},{7,6},{8,9},{9,8},{10,11... | collective-permute-start | bytes 786440 | tf_op jit(solution)/shard_map/ppermute | solution.py:388
  27.4 10.2 %collective-permute-start.4 = (bf16[64,2048]{1,0:T(8,128)(2,1)S(1)}, bf16[64,2048]{1,0:T(8,128)(2,1)S(1)}, u32[]{:S(2)}, u32[]{:S(2)}) collective-permute-start(bf16[64,2048]{1,0:T(8,128)(2,1)S(1)} %get-tuple-element.40.refs_3_), channel_id=1, source_target_pairs={{0,4},{4,0},{8,12},{12,8},{1,5},{5,1},{9,13},{13,9},{2,6},{6,2},{1... | collective-permute-start | bytes 786440 | tf_op jit(solution)/shard_map/ppermute | solution.py:391
  29.6 12.0 %collective-permute-start.6 = (bf16[128,1536]{1,0:T(8,128)(2,1)S(1)}, bf16[128,1536]{1,0:T(8,128)(2,1)S(1)}, u32[]{:S(2)}, u32[]{:S(2)}) collective-permute-start(bf16[128,1536]{1,0:T(8,128)(2,1)S(1)} %get-tuple-element.33.refs_1_), channel_id=1, source_target_pairs={{0,2},{2,0},{1,3},{3,1},{4,6},{6,4},{5,7},{7,5},{8,10},{10,8},{9,1... | collective-permute-start | bytes 1179656 | tf_op jit(solution)/shard_map/ppermute | solution.py:418
  31.0 19.8 %collective-permute-start.10 = (bf16[128,1280]{1,0:T(8,128)(2,1)S(1)}, bf16[128,1280]{1,0:T(8,128)(2,1)S(1)}, u32[]{:S(2)}, u32[]{:S(2)}) collective-permute-start(bf16[128,1280]{1,0:T(8,128)(2,1)S(1)} %get-tuple-element.34.refs_2_), channel_id=1, source_target_pairs={{0,2},{2,0},{1,3},{3,1},{4,6},{6,4},{5,7},{7,5},{8,10},{10,8},{9,1... | collective-permute-start | bytes 983048 | tf_op jit(solution)/shard_map/ppermute | solution.py:418
  37.6 2.8 %copy-start.2 = (s32[4096]{0:T(1024)S(1)}, s32[4096]{0:T(1024)}, u32[]{:S(2)}) copy-start(s32[4096]{0:T(1024)} %param.6) | copy-start | bytes 49156
  37.7 9.6 %collective-permute-start.5 = (bf16[32,2048]{1,0:T(8,128)(2,1)S(1)}, bf16[32,2048]{1,0:T(8,128)(2,1)S(1)}, u32[]{:S(2)}, u32[]{:S(2)}) collective-permute-start(bf16[32,2048]{1,0:T(8,128)(2,1)S(1)} %get-tuple-element.43.refs_3_), channel_id=1, source_target_pairs={{0,8},{4,12},{8,0},{12,4},{1,9},{5,13},{9,1},{13,5},{2,10},{6,14},... | collective-permute-start | bytes 393224 | tf_op jit(solution)/shard_map/ppermute | solution.py:391
  40.4 6.9 %copy-start.1 = (f32[128,128]{1,0:T(8,128)S(1)}, f32[128,128]{1,0:T(8,128)}, u32[]{:S(2)}) copy-start(f32[128,128]{1,0:T(8,128)} %constant.9.clone.rotation_ref) | copy-start | bytes 196612
  47.8 9.6 %collective-permute-start.7 = (bf16[32,2048]{1,0:T(8,128)(2,1)S(1)}, bf16[32,2048]{1,0:T(8,128)(2,1)S(1)}, u32[]{:S(2)}, u32[]{:S(2)}) collective-permute-start(bf16[32,2048]{1,0:T(8,128)(2,1)S(1)} %get-tuple-element.44.refs_3_.refs_0_), channel_id=1, source_target_pairs={{0,4},{4,0},{8,12},{12,8},{1,5},{5,1},{9,13},{13,9},{2,6},{6,2},{1... | collective-permute-start | bytes 393224 | tf_op jit(solution)/shard_map/ppermute | solution.py:391
  47.9 9.5 %collective-permute-start.8 = (bf16[32,2048]{1,0:T(8,128)(2,1)S(1)}, bf16[32,2048]{1,0:T(8,128)(2,1)S(1)}, u32[]{:S(2)}, u32[]{:S(2)}) collective-permute-start(bf16[32,2048]{1,0:T(8,128)(2,1)S(1)} %get-tuple-element.44.refs_3_.refs_0_), channel_id=1, source_target_pairs={{0,8},{4,12},{8,0},{12,4},{1,9},{5,13},{9,1},{13,5},{2,10},{6,14},... | collective-permute-start | bytes 393224 | tf_op jit(solution)/shard_map/ppermute | solution.py:391
  57.2 1.6 %collective-permute-start.11 = (bf16[128,1024]{1,0:T(8,128)(2,1)S(1)}, bf16[128,1024]{1,0:T(8,128)(2,1)S(1)}, u32[]{:S(2)}, u32[]{:S(2)}) collective-permute-start(bf16[128,1024]{1,0:T(8,128)(2,1)S(1)} %get-tuple-element.46), channel_id=1, source_target_pairs={{0,1},{1,0},{2,3},{3,2},{4,5},{5,4},{6,7},{7,6},{8,9},{9,8},{10,11... | collective-permute-start | bytes 786440 | tf_op jit(solution)/shard_map/ppermute | solution.py:388
  57.4 3.2 %collective-permute-start.13 = (bf16[128,1024]{1,0:T(8,128)(2,1)S(1)}, bf16[128,1024]{1,0:T(8,128)(2,1)S(1)}, u32[]{:S(2)}, u32[]{:S(2)}) collective-permute-start(bf16[128,1024]{1,0:T(8,128)(2,1)S(1)} %shard_map.69), channel_id=1, source_target_pairs={{0,1},{1,0},{2,3},{3,2},{4,5},{5,4},{6,7},{7,6},{8,9},{9,8},{10,11... | collective-permute-start | bytes 786440 | tf_op jit(solution)/shard_map/ppermute | solution.py:388
  58.9 6.4 %collective-permute-start.12 = (bf16[64,1024]{1,0:T(8,128)(2,1)S(1)}, bf16[64,1024]{1,0:T(8,128)(2,1)S(1)}, u32[]{:S(2)}, u32[]{:S(2)}) collective-permute-start(bf16[64,1024]{1,0:T(8,128)(2,1)S(1)} %get-tuple-element.48), channel_id=1, source_target_pairs={{0,4},{4,0},{8,12},{12,8},{1,5},{5,1},{9,13},{13,9},{2,6},{6,2},{1... | collective-permute-start | bytes 393224 | tf_op jit(solution)/shard_map/ppermute | solution.py:391
  60.6 8.2 %collective-permute-start.15 = (bf16[64,1024]{1,0:T(8,128)(2,1)S(1)}, bf16[64,1024]{1,0:T(8,128)(2,1)S(1)}, u32[]{:S(2)}, u32[]{:S(2)}) collective-permute-start(bf16[64,1024]{1,0:T(8,128)(2,1)S(1)} %get-tuple-element.51.refs_2_), channel_id=1, source_target_pairs={{0,4},{4,0},{8,12},{12,8},{1,5},{5,1},{9,13},{13,9},{2,6},{6,2},{1... | collective-permute-start | bytes 393224 | tf_op jit(solution)/shard_map/ppermute | solution.py:391
  61.1 14.1 %collective-permute-start.9 = (bf16[32,2048]{1,0:T(8,128)(2,1)S(1)}, bf16[32,2048]{1,0:T(8,128)(2,1)S(1)}, u32[]{:S(2)}, u32[]{:S(2)}) collective-permute-start(bf16[32,2048]{1,0:T(8,128)(2,1)S(1)} %collective-permute-done.8.refs_2_.refs_1_), channel_id=1, source_target_pairs={{0,4},{4,0},{8,12},{12,8},{1,5},{5,1},{9,13},{13,9},{2,6},{6,2},{1... | collective-permute-start | bytes 393224 | tf_op jit(solution)/shard_map/ppermute | solution.py:391
  65.3 7.5 %collective-permute-start.14 = (bf16[32,1024]{1,0:T(8,128)(2,1)S(1)}, bf16[32,1024]{1,0:T(8,128)(2,1)S(1)}, u32[]{:S(2)}, u32[]{:S(2)}) collective-permute-start(bf16[32,1024]{1,0:T(8,128)(2,1)S(1)} %get-tuple-element.53), channel_id=1, source_target_pairs={{0,8},{4,12},{8,0},{12,4},{1,9},{5,13},{9,1},{13,5},{2,10},{6,14},... | collective-permute-start | bytes 196616 | tf_op jit(solution)/shard_map/ppermute | solution.py:391
  68.9 7.0 %collective-permute-start.19 = (bf16[32,1024]{1,0:T(8,128)(2,1)S(1)}, bf16[32,1024]{1,0:T(8,128)(2,1)S(1)}, u32[]{:S(2)}, u32[]{:S(2)}) collective-permute-start(bf16[32,1024]{1,0:T(8,128)(2,1)S(1)} %get-tuple-element.56.refs_0_), channel_id=1, source_target_pairs={{0,8},{4,12},{8,0},{12,4},{1,9},{5,13},{9,1},{13,5},{2,10},{6,14},... | collective-permute-start | bytes 196616 | tf_op jit(solution)/shard_map/ppermute | solution.py:391
  73.2 6.3 %collective-permute-start.17 = (bf16[32,1152]{1,0:T(8,128)(2,1)S(1)}, bf16[32,1152]{1,0:T(8,128)(2,1)S(1)}, u32[]{:S(2)}, u32[]{:S(2)}) collective-permute-start(bf16[32,1152]{1,0:T(8,128)(2,1)S(1)} %shard_map.73.refs_4_), channel_id=1, source_target_pairs={{0,8},{4,12},{8,0},{12,4},{1,9},{5,13},{9,1},{13,5},{2,10},{6,14},... | collective-permute-start | bytes 221192 | tf_op jit(solution)/shard_map/ppermute | solution.py:391
  76.3 5.7 %collective-permute-start.21 = (bf16[32,1152]{1,0:T(8,128)(2,1)S(1)}, bf16[32,1152]{1,0:T(8,128)(2,1)S(1)}, u32[]{:S(2)}, u32[]{:S(2)}) collective-permute-start(bf16[32,1152]{1,0:T(8,128)(2,1)S(1)} %shard_map.75.refs_4_), channel_id=1, source_target_pairs={{0,8},{4,12},{8,0},{12,4},{1,9},{5,13},{9,1},{13,5},{2,10},{6,14},... | collective-permute-start | bytes 221192 | tf_op jit(solution)/shard_map/ppermute | solution.py:391
  76.6 5.5 %collective-permute-start.16 = (bf16[32,1152]{1,0:T(8,128)(2,1)S(1)}, bf16[32,1152]{1,0:T(8,128)(2,1)S(1)}, u32[]{:S(2)}, u32[]{:S(2)}) collective-permute-start(bf16[32,1152]{1,0:T(8,128)(2,1)S(1)} %shard_map.73.refs_4_), channel_id=1, source_target_pairs={{0,4},{4,0},{8,12},{12,8},{1,5},{5,1},{9,13},{13,9},{2,6},{6,2},{1... | collective-permute-start | bytes 221192 | tf_op jit(solution)/shard_map/ppermute | solution.py:391
  79.5 5.2 %collective-permute-start.18 = (bf16[32,1152]{1,0:T(8,128)(2,1)S(1)}, bf16[32,1152]{1,0:T(8,128)(2,1)S(1)}, u32[]{:S(2)}, u32[]{:S(2)}) collective-permute-start(bf16[32,1152]{1,0:T(8,128)(2,1)S(1)} %collective-permute-done.17.refs_6_), channel_id=1, source_target_pairs={{0,4},{4,0},{8,12},{12,8},{1,5},{5,1},{9,13},{13,9},{2,6},{6,2},{1... | collective-permute-start | bytes 221192 | tf_op jit(solution)/shard_map/ppermute | solution.py:391
  79.5 6.3 %collective-permute-start.20 = (bf16[32,1152]{1,0:T(8,128)(2,1)S(1)}, bf16[32,1152]{1,0:T(8,128)(2,1)S(1)}, u32[]{:S(2)}, u32[]{:S(2)}) collective-permute-start(bf16[32,1152]{1,0:T(8,128)(2,1)S(1)} %shard_map.75.refs_4_), channel_id=1, source_target_pairs={{0,4},{4,0},{8,12},{12,8},{1,5},{5,1},{9,13},{13,9},{2,6},{6,2},{1... | collective-permute-start | bytes 221192 | tf_op jit(solution)/shard_map/ppermute | solution.py:391
  81.9 4.6 %collective-permute-start.22 = (bf16[32,1152]{1,0:T(8,128)(2,1)S(1)}, bf16[32,1152]{1,0:T(8,128)(2,1)S(1)}, u32[]{:S(2)}, u32[]{:S(2)}) collective-permute-start(bf16[32,1152]{1,0:T(8,128)(2,1)S(1)} %collective-permute-done.21.refs_6_), channel_id=1, source_target_pairs={{0,4},{4,0},{8,12},{12,8},{1,5},{5,1},{9,13},{13,9},{2,6},{6,2},{1... | collective-permute-start | bytes 221192 | tf_op jit(solution)/shard_map/ppermute | solution.py:391
  84.8 2.9 %collective-permute-start.23 = (bf16[128,1152]{1,0:T(8,128)(2,1)S(1)}, bf16[128,1152]{1,0:T(8,128)(2,1)S(1)}, u32[]{:S(2)}, u32[]{:S(2)}) collective-permute-start(bf16[128,1152]{1,0:T(8,128)(2,1)S(1)} %shard_map.78), channel_id=1, source_target_pairs={{0,1},{1,0},{2,3},{3,2},{4,5},{5,4},{6,7},{7,6},{8,9},{9,8},{10,11... | collective-permute-start | bytes 884744 | tf_op jit(solution)/shard_map/ppermute | solution.py:388
  86.6 1.6 %collective-permute-start.24 = (bf16[128,1152]{1,0:T(8,128)(2,1)S(1)}, bf16[128,1152]{1,0:T(8,128)(2,1)S(1)}, u32[]{:S(2)}, u32[]{:S(2)}) collective-permute-start(bf16[128,1152]{1,0:T(8,128)(2,1)S(1)} %shard_map.79), channel_id=1, source_target_pairs={{0,1},{1,0},{2,3},{3,2},{4,5},{5,4},{6,7},{7,6},{8,9},{9,8},{10,11... | collective-permute-start | bytes 884744 | tf_op jit(solution)/shard_map/ppermute | solution.py:388
